TPU v7x, 32 devices: a whole 2x2x4 slice. The times are simulated.
32 devices in a mesh: row: 4 (over y, core), col: 8 (over z, x).
Axes of the slice: x: 2, y: 2, z: 4, core: 2. Of those that a mesh axis runs over, the one named last changes fastest.
Arguments:
- operator_blocks: float32 [256, 64, 512], P(('row', 'col')), may hold values from -0.75 to 0.75
- operator_count: int32 [256], P(('row', 'col')), may hold values from 1 to 8
- operator_slot: int32 [256, 8], P(('row', 'col')), may hold values from 0 to 31
- fetch_lists: int32 [4, 8, 8, 4], P('row', 'col'), may hold values from 0 to 255, as said below
- prolong_blocks: float32 [256, 64, 128], P(('row', 'col')), may hold values from -0.75 to 0.75
- prolong_cols: int32 [256, 2], P(('row', 'col')), may hold values from 0 to 7
- restrict_blocks: float32 [256, 64, 128], P(('row', 'col')), may hold values from -0.09375 to 0.09375
- restrict_rows: int32 [256, 2], P(('row', 'col')), may hold values from 0 to 1
Outputs:
- coarse_operator: float32 [512, 512], P('row', 'col')
Inputs may be any that keep to these rules, and one draw needn't show every extreme that they name: fetch_lists[r, c, p, s] names a fine block held by the device with column index p and row index r2 = (r + c + p * 4 + s + h) mod 4, for one whole number h of the draw; that device holds fine blocks (r2 * 8 + p) * 8 to (r2 * 8 + p + 1) * 8 - 1.
All inputs are finite; a program needn't handle non-finite values.
Results may differ from a plain program's by a relative error of at most 0.0003.
Values sent between devices are 32-bit elements; how exact they have to be, the bound alone decides.
No kernel may reach another device: no remote copies, remote signals or barrier semaphores. Data moves between devices by JAX's collectives and lax.ppermute only.
A program may use at most 64 MiB of HBM per device.

v0:
```python
import jax
import jax.numpy as jnp
from jax import lax
from jax.sharding import PartitionSpec as P

NCR = 2


def contract(form, left, right):
    return jnp.einsum(form, left, right, precision=lax.Precision.HIGHEST)


def gather_panel(prolong_blocks, prolong_cols):
    return (
        lax.all_gather(prolong_blocks, "row", axis=0, tiled=True),
        lax.all_gather(prolong_cols, "row", axis=0, tiled=True),
    )


def local(
    operator_blocks,
    operator_count,
    operator_slot,
    fetch_lists,
    prolong_blocks,
    prolong_cols,
    restrict_blocks,
    restrict_rows,
):
    fine_rows = operator_blocks.shape[0]
    block_size = operator_blocks.shape[1]
    row_entries = operator_slot.shape[1]
    prolong_entries = prolong_cols.shape[1]
    restrict_entries = restrict_rows.shape[1]
    columns = lax.axis_size("col")
    slot_count = fetch_lists.shape[3]
    total_slots = columns * slot_count
    coarse_all = NCR * lax.axis_size("row")
    live_mask = (
        jnp.arange(row_entries, dtype=jnp.int32)[None, :] < operator_count[:, None]
    ).astype(jnp.float32)
    blocks = operator_blocks.reshape(fine_rows, block_size, row_entries, block_size)
    restrict_hot = (restrict_rows[..., None] == jnp.arange(NCR, dtype=jnp.int32)).astype(
        jnp.float32
    )
    restrict_dense = contract(
        "iaqb,iqQ->iaQb",
        restrict_blocks.reshape(fine_rows, block_size, restrict_entries, block_size),
        restrict_hot,
    )
    requests = fetch_lists.reshape(columns, slot_count)
    panel_blocks, panel_columns = gather_panel(prolong_blocks, prolong_cols)
    wanted = lax.all_to_all(requests, "col", split_axis=0, concat_axis=0, tiled=True)
    position = wanted // (fine_rows * columns) * fine_rows + wanted % fine_rows
    fetched = panel_blocks[position]
    fetched_columns = panel_columns[position]
    got_blocks = lax.all_to_all(fetched, "col", split_axis=0, concat_axis=0, tiled=True)
    got_columns = lax.all_to_all(fetched_columns, "col", split_axis=0, concat_axis=0, tiled=True)
    got_blocks = got_blocks.reshape(total_slots, block_size, prolong_entries * block_size)
    got_columns = got_columns.reshape(total_slots, prolong_entries)
    picked = got_blocks[operator_slot]
    picked_columns = got_columns[operator_slot]
    products = contract("iakb,ikbn->ikan", blocks, picked)
    prolong_hot = (picked_columns[..., None] == jnp.arange(coarse_all, dtype=jnp.int32)).astype(
        jnp.float32
    ) * live_mask[:, :, None, None]
    product_dense = contract(
        "ikamc,ikmJ->iaJc",
        products.reshape(fine_rows, row_entries, block_size, prolong_entries, block_size),
        prolong_hot,
    )
    partial_value = contract("iaQb,iaJc->QbJc", restrict_dense, product_dense)
    partial_value = partial_value.reshape(NCR * block_size, coarse_all * block_size)
    return lax.psum_scatter(partial_value, "col", scatter_dimension=1, tiled=True)


def solution(mesh):
    return jax.shard_map(
        local,
        mesh=mesh,
        in_specs=(
            P(("row", "col"), None, None),
            P(("row", "col")),
            P(("row", "col"), None),
            P("row", "col", None, None),
            P(("row", "col"), None, None),
            P(("row", "col"), None),
            P(("row", "col"), None, None),
            P(("row", "col"), None),
        ),
        out_specs=P("row", "col"),
        check_vma=False,
    )
```

profile of v0, /device:TPU:0, one launch (start us, length us, event | category | flops | bytes accessed | tf_op | source)
XLA Modules:
  0.0 153.1 jit_solution(4006413540117789112)
XLA Ops:
  6.5 0.7 all-gather.3.cloned.1.call-update
  7.3 1.3 copy.31
  8.6 7.3 %all-to-all-start = ((s32[8,1,4]{2,1,0:T(1,128)}), s32[8,1,4]{2,1,0:T(1,128)S(1)}, u32[]{:S(2)}, u32[]{:S(2)}) async-start(s32[8,1,4]{2,1,0:T(1,128)} %copy.31), calls=%async_computation | async-start | bytes 8192 | tf_op jit(solution)/shard_map/all_to_all | solution.py:53
  15.9 5.3 %all-gather = s32[4,8,2]{1,2,0:T(2,128)S(1)} all-gather(s32[1,8,2]{1,2,0:T(2,128)} %bitcast.74), channel_id=1, replica_groups=mesh['row'=4,'col'=8] {'row'}, dimensions={0}, use_global_device_ids=true | all-gather | bytes 320 | tf_op jit(solution)/shard_map/all_gather | solution.py:16
  21.2 1.0 all-to-all-done
  22.5 0.6 gather_fusion
  23.1 0.7 copy.36
  23.8 5.0 %all-to-all-start.1 = ((s32[8,4,2]{1,2,0:T(2,128)}), s32[8,4,2]{1,2,0:T(2,128)S(1)}, u32[]{:S(2)}, u32[]{:S(2)}) async-start(s32[8,4,2]{1,2,0:T(2,128)} %copy.36), calls=%async_computation.1 | async-start | bytes 16384 | tf_op jit(solution)/shard_map/all_to_all | solution.py:58
  28.8 2.9 %gather_fusion.2 = f32[32,64,128]{2,1,0:T(8,128)} fusion(f32[32,64,128]{2,1,0:T(8,128)} %all-gather.3.cloned.1.call-done, s32[1024]{0:T(1024)S(1)} %pad_clamp_fusion.1), kind=kCustom, calls=%fused_computation.2 | custom fusion | bytes 2097280 | tf_op jit(solution)/shard_map/gather | solution.py:55
  31.7 3.6 %all-to-all-done.1 = s32[8,4,2]{1,2,0:T(2,128)S(1)} async-done(((s32[8,4,2]{1,2,0:T(2,128)}), s32[8,4,2]{1,2,0:T(2,128)S(1)}, u32[]{:S(2)}, u32[]{:S(2)}) %all-to-all-start.1) | async-done | bytes 288 | tf_op jit(solution)/shard_map/all_to_all | solution.py:58
  35.3 3.6 %all-to-all-start.2 = ((f32[8,4,64,128]{3,2,1,0:T(8,128)}), f32[8,4,64,128]{3,2,1,0:T(8,128)S(1)}, u32[]{:S(2)}, u32[]{:S(2)}) async-start(f32[8,4,64,128]{3,2,1,0:T(8,128)} %bitcast.13), calls=%async_computation.2 | async-start | bytes 2097152 | tf_op jit(solution)/shard_map/all_to_all | solution.py:57
  39.1 1.8 %reshape.167 = f32[8,64,8,64]{3,2,1,0:T(8,128)} reshape(f32[8,64,512]{2,1,0:T(8,128)S(1)} %copy-done.1) | data formatting | bytes 2097152 | tf_op jit(solution)/shard_map/reshape | solution.py:42
  40.8 0.3 reshape.164
  41.3 1.9 %convolution_bitcast_fusion = f32[8,64,2,64,1]{3,2,1,0,4:T(2,128)} fusion(f32[8,64,2,64]{3,2,1,0:T(2,128)S(1)} %reshape.164, s32[8,2]{1,0:T(8,128)S(1)} %copy.29), kind=kOutput, calls=%fused_computation.14 | convolution fusion | flops 1572896 | bytes 524352 | tf_op jit(solution)/shard_map/iaqb,iqQ->iaQb/dot_general | solution.py:10
  43.4 0.6 gather_fusion.1
  44.1 20.0 %all-to-all-done.2 = f32[8,4,64,128]{3,2,1,0:T(8,128)S(1)} async-done(((f32[8,4,64,128]{3,2,1,0:T(8,128)}), f32[8,4,64,128]{3,2,1,0:T(8,128)S(1)}, u32[]{:S(2)}, u32[]{:S(2)}) %all-to-all-start.2) | async-done | bytes 1048608 | tf_op jit(solution)/shard_map/all_to_all | solution.py:57
  64.1 0.7 gather_fusion.3
  64.8 5.2 %fusion.7 = f32[8,8,64,128]{3,2,1,0:T(8,128)} fusion(f32[8,8,64,128]{3,2,1,0:T(8,128)S(1)} %bitcast.67, f32[8,64,8,64]{3,2,1,0:T(8,128)} %reshape.167), kind=kOutput, calls=%fused_computation.11 | convolution fusion | flops 402653184 | bytes 5242880 | tf_op jit(solution)/shard_map/iakb,ikbn->ikan/dot_general | solution.py:10
  70.0 5.6 %reshape.168 = f32[8,8,64,2,64]{4,3,2,1,0:T(2,128)} reshape(f32[8,8,64,128]{3,2,1,0:T(8,128)} %fusion.7) | data formatting | bytes 4194304 | tf_op jit(solution)/shard_map/reshape | solution.py:69
  75.6 6.7 %fusion.10 = f32[8,64,8,64]{3,2,1,0:T(8,128)S(1)} fusion(f32[8,8,64,2,64]{4,3,2,1,0:T(2,128)} %reshape.168, f32[8,8]{1,0:T(8,128)S(1)} %fusion.26, s32[8,8,2]{1,2,0:T(2,128)S(1)} %copy.40), kind=kOutput, calls=%fused_computation.12 | convolution fusion | flops 50333696 | bytes 3146496 | tf_op jit(solution)/shard_map/ikamc,ikmJ->iaJc/dot_general | solution.py:10
  82.4 1.7 %fusion.13 = f32[2,64,8,64]{3,1,2,0:T(8,128)S(1)} fusion(f32[8,64,8,64]{3,2,1,0:T(8,128)S(1)} %fusion.10, f32[8,64,2,64,1]{3,2,1,0,4:T(2,128)S(1)} %copy-done), kind=kOutput, calls=%fused_computation.13 | convolution fusion | flops 402653184 | bytes 1572864 | tf_op jit(solution)/shard_map/iaQb,iaJc->QbJc/dot_general | solution.py:10
  84.1 0.3 copy.64
  84.4 1.0 reshape.218
  85.4 60.8 %reduce-scatter.4.cloned.1.call-done = f32[64,128]{1,0:T(8,128)} async-done(((f32[512,128]{1,0:T(8,128)}), f32[64,128]{1,0:T(8,128)}) %reduce-scatter.4.cloned.1.call-update) | async-done | bytes 32784
  (29 shorter events, 1.0 us)
Async XLA Ops:
  6.5 22.3 %all-gather.3.cloned.1.call-start = ((), (), s32[]{:S(2)}) async-start(), calls=%async_computation.4 | async-start | bytes 1310720 | tf_op jit(solution)/shard_map/all_gather | solution.py:15
  8.6 13.6 %all-to-all-start = ((s32[8,1,4]{2,1,0:T(1,128)}), s32[8,1,4]{2,1,0:T(1,128)S(1)}, u32[]{:S(2)}, u32[]{:S(2)}) async-start(s32[8,1,4]{2,1,0:T(1,128)} %copy.31), calls=%async_computation | async-start | bytes 8192 | tf_op jit(solution)/shard_map/all_to_all | solution.py:53
  23.8 11.5 %all-to-all-start.1 = ((s32[8,4,2]{1,2,0:T(2,128)}), s32[8,4,2]{1,2,0:T(2,128)S(1)}, u32[]{:S(2)}, u32[]{:S(2)}) async-start(s32[8,4,2]{1,2,0:T(2,128)} %copy.36), calls=%async_computation.1 | async-start | bytes 16384 | tf_op jit(solution)/shard_map/all_to_all | solution.py:58
  28.8 10.2 %copy-start.3 = (s32[8,8]{1,0:T(8,128)S(1)}, s32[8,8]{1,0:T(8,128)}, u32[]{:S(2)}) copy-start(s32[8,8]{1,0:T(8,128)} %param.10) | copy-start | bytes 772
  28.8 10.3 %copy-start.1 = (f32[8,64,512]{2,1,0:T(8,128)S(1)}, f32[8,64,512]{2,1,0:T(8,128)}, u32[]{:S(2)}) copy-start(f32[8,64,512]{2,1,0:T(8,128)} %param.8) | copy-start | bytes 3145732
  35.3 28.8 %all-to-all-start.2 = ((f32[8,4,64,128]{3,2,1,0:T(8,128)}), f32[8,4,64,128]{3,2,1,0:T(8,128)S(1)}, u32[]{:S(2)}, u32[]{:S(2)}) async-start(f32[8,4,64,128]{3,2,1,0:T(8,128)} %bitcast.13), calls=%async_computation.2 | async-start | bytes 2097152 | tf_op jit(solution)/shard_map/all_to_all | solution.py:57
  38.9 1.9 %copy-start.2 = (f32[8,64,128]{2,1,0:T(8,128)S(1)}, f32[8,64,128]{2,1,0:T(8,128)}, u32[]{:S(2)}) copy-start(f32[8,64,128]{2,1,0:T(8,128)} %param.14) | copy-start | bytes 786436
  38.9 2.3 %copy-start.4 = (s32[8,2]{0,1:T(2,128)S(1)}, s32[8,2]{0,1:T(2,128)}, u32[]{:S(2)}) copy-start(s32[8,2]{0,1:T(2,128)} %param.15) | copy-start | bytes 196
  38.9 107.3 %reduce-scatter.4.cloned.1.call-start = ((), (), s32[]{:S(2)}) async-start(), calls=%async_computation.5 | async-start | bytes 294912
  39.1 4.1 %copy-start.5 = (s32[8]{0:T(128)S(1)}, s32[8]{0:T(128)}, u32[]{:S(2)}) copy-start(s32[8]{0:T(128)} %param.9) | copy-start | bytes 100
  75.6 6.8 %copy-start = (f32[8,64,2,64,1]{3,2,1,0,4:T(2,128)S(1)}, f32[8,64,2,64,1]{3,2,1,0,4:T(2,128)}, u32[]{:S(2)}) copy-start(f32[8,64,2,64,1]{3,2,1,0,4:T(2,128)} %convolution_bitcast_fusion) | copy-start | bytes 786436
Sparse Core Ops, SparseCore 0:
  8.9 19.4 all-gather.2
  85.5 60.6 reduce-scatter.3
where the time goes:
time: 153 us
  waiting for transfers between devices  86.2 us (56%)
  local copies, waits for them, and re-layouts  16.6 us (11%)
  starting transfers between devices  15.8 us (10%)
  matrix products  15.5 us (10%)
  between operations  13.5 us (9%)
  blocking collectives  5.27 us (3%)
    unnamed x3, waiting for transfers between devices  61.5 us
    all_to_all x1, waiting for transfers between devices, local(): lax.all_to_all(fetched, 'col', split_axis=0, concat_axis=0, tiled=True)  20 us
    dot_general x4, matrix products, contract(): return jnp.einsum(form, left, right, precision=lax.Precision.HIGHEST)  15.5 us
    all_to_all x1, starting transfers between devices, local(): lax.all_to_all(requests, 'col', split_axis=0, concat_axis=0, tiled=True)  7.25 us
    reshape x1, local copies, waits for them, and re-layouts, local(): products.reshape(fine_rows, row_entries, block_size, prolong_entries, blo...  5.63 us
    all_gather x1, blocking collectives, gather_panel(): lax.all_gather(prolong_cols, 'row', axis=0, tiled=True)  5.27 us
    all_to_all x1, starting transfers between devices, local(): lax.all_to_all(fetched_columns, 'col', split_axis=0, concat_axis=0, tiled...  4.98 us
    all_to_all x1, waiting for transfers between devices, local(): lax.all_to_all(fetched_columns, 'col', split_axis=0, concat_axis=0, tiled...  3.58 us
  transfers between devices with their start and end apart: 5, of which 4 were waited for; matrix products, arithmetic and copies ran while one was open for 7% of the time, Pallas kernels for 0%

commit v1 on v0

v1 whole, which is shorter than its diff:
```python
import functools

import jax
import jax.numpy as jnp
from jax import lax
from jax.experimental import pallas as pl
from jax.experimental.pallas import tpu as pltpu
from jax.sharding import PartitionSpec as P

NCR = 2
LANES = 128
AXES = ("row", "col")
VMEM_LIMIT = 48 * 1024 * 1024


def split3(x, order):
    high = x.astype(jnp.bfloat16)
    low = (x - high.astype(jnp.float32)).astype(jnp.bfloat16)
    parts = {"left": (high, low, high), "right": (high, high, low)}[order]
    return jnp.concatenate(parts, axis=0)


def transposed_dot(left, right):
    return lax.dot_general(left, right, (((0,), (0,)), ((), ())), preferred_element_type=jnp.float32)


def restrict_kernel(count_ref, slot_ref, rows_ref, operator_ref, restrict_ref, out_ref, sums_ref):
    fine_rows, block_size, _ = operator_ref.shape
    entries = slot_ref.shape[1]
    sums_ref[...] = jnp.zeros_like(sums_ref)
    lane = lax.broadcasted_iota(jnp.int32, (block_size, NCR * block_size), 1)
    second = (lane >= block_size).astype(jnp.int32)

    for i in range(fine_rows):
        value = restrict_ref[i]
        swapped = pltpu.roll(value, block_size, 1)
        own_row = jnp.where(second == 0, rows_ref[i, 0], rows_ref[i, 1])
        other_row = jnp.where(second == 0, rows_ref[i, 1], rows_ref[i, 0])
        dense = jnp.where(own_row == second, value, 0.0) + jnp.where(other_row == second, swapped, 0.0)
        product = transposed_dot(split3(operator_ref[i], "left"), split3(dense, "right"))
        for k in range(entries):
            part = product[k * block_size : (k + 1) * block_size]
            slot = slot_ref[i, k]
            sums_ref[slot] += jnp.where(k < count_ref[i], part, 0.0)

    def finish(slot, carry):
        out_ref[slot] = split3(sums_ref[slot], "right")
        return carry

    lax.fori_loop(0, out_ref.shape[0], finish, 0, unroll=8)


def restrict_operator(operator_count, operator_slot, restrict_rows, operator_blocks, restrict_blocks, slots):
    fine_rows, block_size, width = operator_blocks.shape
    wide = NCR * block_size
    return pl.pallas_call(
        restrict_kernel,
        out_shape=jax.ShapeDtypeStruct((slots, 3 * block_size, wide), jnp.bfloat16),
        in_specs=[pl.BlockSpec(memory_space=pltpu.SMEM)] * 3 + [pl.BlockSpec(memory_space=pltpu.VMEM)] * 2,
        out_specs=pl.BlockSpec(memory_space=pltpu.VMEM),
        scratch_shapes=[pltpu.VMEM((slots, block_size, wide), jnp.float32)],
        compiler_params=pltpu.CompilerParams(vmem_limit_bytes=VMEM_LIMIT),
        cost_estimate=pl.CostEstimate(
            flops=6 * fine_rows * block_size * width * wide, bytes_accessed=4 << 20, transcendentals=0
        ),
        name="restrict_operator",
    )(operator_count, operator_slot, restrict_rows, operator_blocks, restrict_blocks)


def combine_kernel(sizes, fetch_ref, table_ref, restricted_ref, blocks_ref, out_ref):
    slots = restricted_ref.shape[0]
    block_size = out_ref.shape[1]
    slot_count = fetch_ref.shape[1]
    fine_rows, columns, prolong_entries = sizes
    out_ref[...] = jnp.zeros_like(out_ref)

    def step(slot, carry):
        peer = lax.div(slot, slot_count)
        wanted = fetch_ref[peer, lax.rem(slot, slot_count)]
        inside = lax.rem(wanted, fine_rows)
        group = lax.div(wanted, fine_rows * columns)
        place = group * columns + peer
        product = transposed_dot(split3(blocks_ref[place], "left"), restricted_ref[slot])
        for m in range(prolong_entries):
            column = table_ref[place, 1 + prolong_entries * inside + m]
            out_ref[column] += product[m * block_size : (m + 1) * block_size]
        return carry

    lax.fori_loop(0, slots, step, 0, unroll=8)


def combine(sizes, fetch, table, restricted, blocks, coarse_all):
    block_size = blocks.shape[1]
    wide = restricted.shape[2]
    return pl.pallas_call(
        functools.partial(combine_kernel, sizes),
        out_shape=jax.ShapeDtypeStruct((coarse_all, block_size, wide), jnp.float32),
        in_specs=[pl.BlockSpec(memory_space=pltpu.SMEM)] * 2 + [pl.BlockSpec(memory_space=pltpu.VMEM)] * 2,
        out_specs=pl.BlockSpec(memory_space=pltpu.VMEM),
        compiler_params=pltpu.CompilerParams(vmem_limit_bytes=VMEM_LIMIT),
        cost_estimate=pl.CostEstimate(flops=1 << 28, bytes_accessed=4 << 20, transcendentals=0),
        name="combine",
    )(fetch, table, restricted, blocks)


def pick_kernel(table_ref, blocks_ref, out_ref):
    def step(place, carry):
        out_ref[place] = blocks_ref[table_ref[place, 0]]
        return carry

    lax.fori_loop(0, out_ref.shape[0], step, 0, unroll=8)


def pick(table, blocks):
    return pl.pallas_call(
        pick_kernel,
        out_shape=jax.ShapeDtypeStruct((table.shape[0],) + blocks.shape[1:], blocks.dtype),
        in_specs=[pl.BlockSpec(memory_space=pltpu.SMEM), pl.BlockSpec(memory_space=pltpu.VMEM)],
        out_specs=pl.BlockSpec(memory_space=pltpu.VMEM),
        compiler_params=pltpu.CompilerParams(vmem_limit_bytes=VMEM_LIMIT),
        cost_estimate=pl.CostEstimate(flops=0, bytes_accessed=2 << 20, transcendentals=0),
        name="pick",
    )(table, blocks)


def add_kernel(parts_ref, out_ref):
    total = parts_ref[0]
    for i in range(1, parts_ref.shape[0]):
        total = total + parts_ref[i]
    out_ref[...] = total.T


def add_up(parts):
    return pl.pallas_call(
        add_kernel,
        out_shape=jax.ShapeDtypeStruct((parts.shape[2], parts.shape[1]), parts.dtype),
        in_specs=[pl.BlockSpec(memory_space=pltpu.VMEM)],
        out_specs=pl.BlockSpec(memory_space=pltpu.VMEM),
        compiler_params=pltpu.CompilerParams(vmem_limit_bytes=VMEM_LIMIT),
        name="add_up",
    )(parts)


def local(
    operator_blocks,
    operator_count,
    operator_slot,
    fetch_lists,
    prolong_blocks,
    prolong_cols,
    restrict_blocks,
    restrict_rows,
):
    fine_rows = operator_blocks.shape[0]
    prolong_entries = prolong_cols.shape[1]
    rows, columns = lax.axis_size("row"), lax.axis_size("col")
    devices = rows * columns
    slot_count = fetch_lists.shape[3]
    fetch = fetch_lists.reshape(columns, slot_count)

    owner_row = fetch // (fine_rows * columns)
    inside = fetch % fine_rows
    mine = owner_row[None] == jnp.arange(rows, dtype=jnp.int32)[:, None, None]
    request = jnp.sum(jnp.where(mine, inside[None], 0), axis=2).reshape(devices, 1)
    own_columns = jnp.broadcast_to(prolong_cols.reshape(1, -1), (devices, prolong_cols.size))
    message = jnp.concatenate([request, own_columns], axis=1)
    message = jnp.pad(message, ((0, 0), (0, LANES - message.shape[1])))
    table = lax.all_to_all(message[:, None, :], AXES, split_axis=0, concat_axis=0, tiled=True)[:, 0, :]

    restricted = restrict_operator(
        operator_count, operator_slot, restrict_rows, operator_blocks, restrict_blocks, columns * slot_count
    )
    picked = pick(table, prolong_blocks)
    blocks = lax.all_to_all(picked, AXES, split_axis=0, concat_axis=0, tiled=True)
    partial_sums = combine((fine_rows, columns, prolong_entries), fetch, table, restricted, blocks, NCR * rows)
    parts = lax.all_to_all(partial_sums, "col", split_axis=0, concat_axis=0, tiled=True)
    return add_up(parts)


def solution(mesh):
    return jax.shard_map(
        local,
        mesh=mesh,
        in_specs=(
            P(("row", "col"), None, None),
            P(("row", "col")),
            P(("row", "col"), None),
            P("row", "col", None, None),
            P(("row", "col"), None, None),
            P(("row", "col"), None),
            P(("row", "col"), None, None),
            P(("row", "col"), None),
        ),
        out_specs=P("row", "col"),
        check_vma=False,
    )
```

time: 153 us -> 64 us (0.42)
  waiting for transfers between devices: 86.2 us -> 24.4 us
  blocking collectives: 5.27 us -> 25.7 us
  matrix products: 15.5 us -> 0 us
  between operations: 13.5 us -> 0.06 us
  starting transfers between devices: 15.8 us -> 2.64 us
  local copies, waits for them, and re-layouts: 16.6 us -> 4.05 us
  Pallas kernels: 0 us -> 6.07 us
    unnamed x3 -> x0, waiting for transfers between devices: 61.5 us -> none
    all_to_all x0 -> x2, blocking collectives: none -> 25.7 us  [the longest x1 14.2 us: local(): lax.all_to_all(message[:, None, :], AXES, split_axis=0, concat_axis=0, ti...]
    dot_general x4 -> x0, matrix products: 15.5 us -> none  [contract(): return jnp.einsum(form, left, right, precision=lax.Precision.HIGHEST)]
    all_to_all x3 -> x1, starting transfers between devices: 15.8 us -> 2.64 us  [local(): lax.all_to_all(picked, AXES, split_axis=0, concat_axis=0, tiled=True)]
    reshape x4 -> x2, local copies, waits for them, and re-layouts: 7.84 us -> 0.16 us  [the longest x1 0.08 us: local(): fetch = fetch_lists.reshape(columns, slot_count)]
    pallas_call x0 -> x4, Pallas kernels: none -> 6.07 us  [the longest x1 2.33 us: combine(): pl.pallas_call(functools.partial(combine_kernel, sizes), out_shape=jax.Sh...]
    gather x6 -> x0, local copies, waits for them, and re-layouts: 5.59 us -> none  [the longest x1 2.89 us: local(): fetched = panel_blocks[position]]
    all_gather x1 -> x0, blocking collectives: 5.27 us -> none  [gather_panel(): lax.all_gather(prolong_cols, 'row', axis=0, tiled=True)]
  transfers between devices with their start and end apart: 5 -> 1, of which waited for: 4 -> 1; matrix products, arithmetic and copies ran while one was open for 7% -> 0% of each run, Pallas kernels for 0% -> 3%
where the time goes in v1:
time: 64 us; the launch traced here: 63.6 us
  blocking collectives  25.7 us (40%)
  waiting for transfers between devices  24.4 us (38%)
  Pallas kernels  6.07 us (9%)
  local copies, waits for them, and re-layouts  4.05 us (6%)
  starting transfers between devices  2.64 us (4%)
  other arithmetic  0.72 us (1%)
    all_to_all x1, waiting for transfers between devices, local(): lax.all_to_all(picked, AXES, split_axis=0, concat_axis=0, tiled=True)  24.4 us
    all_to_all x1, blocking collectives, local(): lax.all_to_all(message[:, None, :], AXES, split_axis=0, concat_axis=0, ti...  14.2 us
    all_to_all x1, blocking collectives, local(): lax.all_to_all(partial_sums, 'col', split_axis=0, concat_axis=0, tiled=True)  11.4 us
    unnamed x16, local copies, waits for them, and re-layouts  3.03 us
    all_to_all x1, starting transfers between devices, local(): lax.all_to_all(picked, AXES, split_axis=0, concat_axis=0, tiled=True)  2.64 us
    pallas_call x1, Pallas kernels, combine(): pl.pallas_call(functools.partial(combine_kernel, sizes), out_shape=jax.Sh...  2.33 us
    pallas_call x1, Pallas kernels, pick(): pl.pallas_call(pick_kernel, out_shape=jax.ShapeDtypeStruct((table.shape[0...  1.86 us
    pallas_call x1, Pallas kernels, restrict_operator(): pl.pallas_call(restrict_kernel, out_shape=jax.ShapeDtypeStruct((slots, 3...  1.78 us
  transfers between devices with their start and end apart: 1, of which 1 were waited for; matrix products, arithmetic and copies ran while one was open for 0% of the time, Pallas kernels for 3%

profile of v1, /device:TPU:0, one launch (start us, length us, event | category | flops | bytes accessed | tf_op | source)
XLA Modules:
  0.0 63.6 jit_solution(11323793592393557597)
XLA Ops:
  0.0 0.8 %copy.30 = s32[8,2]{1,0:T(8,128)S(1)} copy(s32[8,2]{0,1:T(2,128)} %param.13) | data formatting | bytes 128 | tf_op args[5]
  0.8 0.1 reshape.60
  0.8 0.7 %add_select_fusion.1 = (s32[8,4]{0,1:T(4,128)S(1)}, s32[8,4]{0,1:T(4,128)S(1)}) fusion(s32[1,1,8,4]{2,3,1,0:T(4,128)} %param.11), kind=kLoop, calls=%fused_computation.5 | loop fusion | flops 736 | bytes 384 | tf_op jit(solution)/shard_map/jit(floor_divide)/jit(_where)/select_n | solution.py:161
  1.6 0.1 reshape.59
  1.6 0.1 pad.6.clone
  1.7 14.2 %all_to_all.15 = s32[32,1,128]{2,1,0:T(1,128)S(1)} all-to-all(s32[32,1,128]{2,1,0:T(1,128)S(1)} %bitcast.7), channel_id=1, replica_groups=mesh['row'=4,'col'=8] {'row','col'}, dimensions={0} | all-to-all | bytes 32768 | tf_op jit(solution)/shard_map/all_to_all | solution.py:168
  15.9 0.9 %copy-done.2 = f32[8,64,128]{2,1,0:T(8,128)S(1)} copy-done((f32[8,64,128]{2,1,0:T(8,128)S(1)}, f32[8,64,128]{2,1,0:T(8,128)}, u32[]{:S(2)}) %copy-start.2) | copy-done | bytes 262168
  16.9 0.0 copy-start.4
  16.9 1.9 %pick.1 = f32[32,64,128]{2,1,0:T(8,128)} custom-call(s32[32,128]{1,0:T(8,128)S(1)} %bitcast.5, f32[8,64,128]{2,1,0:T(8,128)S(1)} %copy-done.2), custom_call_target="tpu_custom_call" | custom-call | bytes 2097152 | tf_op jit(solution)/shard_map/pick/pallas_call | solution.py:115
  18.8 2.6 %all-to-all-start.1 = ((f32[32,64,128]{2,1,0:T(8,128)}), f32[32,64,128]{2,1,0:T(8,128)S(1)}, u32[]{:S(2)}, u32[]{:S(2)}) async-start(f32[32,64,128]{2,1,0:T(8,128)} %pick.1), calls=%async_computation.1 | async-start | bytes 2097152 | tf_op jit(solution)/shard_map/all_to_all | solution.py:174
  21.4 0.0 copy-done.6
  21.4 0.1 copy.32.rows_ref
  21.5 0.0 copy-done.5
  21.5 0.1 copy.33.fetch_ref
  21.6 0.0 copy-done.1
  21.6 0.0 copy-done.3
  21.6 0.0 copy-done.4
  21.6 1.2 %copy-done = f32[8,64,512]{2,1,0:T(8,128)S(1)} copy-done((f32[8,64,512]{2,1,0:T(8,128)S(1)}, f32[8,64,512]{2,1,0:T(8,128)}, u32[]{:S(2)}) %copy-start) | copy-done | bytes 1048600
  22.8 1.8 %restrict_operator.1.restricted_ref = bf16[32,192,128]{2,1,0:T(8,128)(2,1)S(1)} custom-call(s32[8]{0:T(128)S(1)} %copy-done.4, s32[8,8]{1,0:T(8,128)S(1)} %copy-done.3, s32[8,2]{1,0:T(8,128)S(1)} %copy.32.rows_ref, f32[8,64,512]{2,1,0:T(8,128)S(1)} %copy-done, f32[8,64,128]{2,1,0:T(8,128)S(1)} %copy-done.1), custom_call_target="tpu_custom_call" | custom-call | flops 201326592 | bytes 4194304 | tf_op jit(solution)/shard_map/restrict_operator/pallas_call | solution.py:56
  24.6 24.4 %all-to-all-done.1.blocks_ref = f32[32,64,128]{2,1,0:T(8,128)S(1)} async-done(((f32[32,64,128]{2,1,0:T(8,128)}), f32[32,64,128]{2,1,0:T(8,128)S(1)}, u32[]{:S(2)}, u32[]{:S(2)}) %all-to-all-start.1) | async-done | bytes 1048608 | tf_op jit(solution)/shard_map/all_to_all | solution.py:174
  49.0 2.3 %combine.1 = f32[8,64,128]{2,1,0:T(8,128)S(1)} custom-call(s32[8,4]{1,0:T(8,128)S(1)} %copy.33.fetch_ref, s32[32,128]{1,0:T(8,128)S(1)} %bitcast.6, bf16[32,192,128]{2,1,0:T(8,128)(2,1)S(1)} %restrict_operator.1.restricted_ref, f32[32,64,128]{2,1,0:T(8,128)S(1)} %all-to-all-done.1.blocks_ref), custom_call_target="tpu_custom_call" | custom-call | flops 268435456 | bytes 4194304 | tf_op jit(solution)/shard_map/combine/pallas_call | solution.py:95
  51.4 11.4 %all_to_all.16.parts_ref = f32[8,64,128]{2,1,0:T(8,128)S(1)} all-to-all(f32[8,64,128]{2,1,0:T(8,128)S(1)} %combine.1), channel_id=1, replica_groups=mesh['row'=4,'col'=8] {'col'}, dimensions={0} | all-to-all | bytes 524288 | tf_op jit(solution)/shard_map/all_to_all | solution.py:176
  62.8 0.1 add_up.1
  62.9 0.7 %copy.34 = f32[128,64]{0,1:T(8,128)} copy(f32[128,64]{1,0:T(8,128)S(1)} %add_up.1) | data formatting | bytes 65536 | tf_op jit(solution)/shard_map/add_up/pallas_call | solution.py:134
  (9 shorter events, 0.0 us)
Async XLA Ops:
  15.9 1.0 %copy-start.2 = (f32[8,64,128]{2,1,0:T(8,128)S(1)}, f32[8,64,128]{2,1,0:T(8,128)}, u32[]{:S(2)}) copy-start(f32[8,64,128]{2,1,0:T(8,128)} %blocks_ref.1) | copy-start | bytes 786436
  16.9 4.5 %copy-start.6 = (s32[8,2]{0,1:T(2,128)S(1)}, s32[8,2]{0,1:T(2,128)}, u32[]{:S(2)}) copy-start(s32[8,2]{0,1:T(2,128)} %param.15) | copy-start | bytes 196
  16.9 4.6 %copy-start.5 = (s32[1,1,8,4]{2,3,1,0:T(4,128)S(1)}, s32[1,1,8,4]{2,3,1,0:T(4,128)}, u32[]{:S(2)}) copy-start(s32[1,1,8,4]{2,3,1,0:T(4,128)} %param.11) | copy-start | bytes 388
  16.9 4.7 %copy-start.1 = (f32[8,64,128]{2,1,0:T(8,128)S(1)}, f32[8,64,128]{2,1,0:T(8,128)}, u32[]{:S(2)}) copy-start(f32[8,64,128]{2,1,0:T(8,128)} %restrict_ref.1) | copy-start | bytes 786436
  16.9 4.7 %copy-start.3 = (s32[8,8]{1,0:T(8,128)S(1)}, s32[8,8]{1,0:T(8,128)}, u32[]{:S(2)}) copy-start(s32[8,8]{1,0:T(8,128)} %slot_ref.1) | copy-start | bytes 772
  16.9 4.7 %copy-start.4 = (s32[8]{0:T(128)S(1)}, s32[8]{0:T(128)}, u32[]{:S(2)}) copy-start(s32[8]{0:T(128)} %count_ref.1) | copy-start | bytes 100
  18.8 30.2 %all-to-all-start.1 = ((f32[32,64,128]{2,1,0:T(8,128)}), f32[32,64,128]{2,1,0:T(8,128)S(1)}, u32[]{:S(2)}, u32[]{:S(2)}) async-start(f32[32,64,128]{2,1,0:T(8,128)} %pick.1), calls=%async_computation.1 | async-start | bytes 2097152 | tf_op jit(solution)/shard_map/all_to_all | solution.py:174
  21.6 1.2 %copy-start = (f32[8,64,512]{2,1,0:T(8,128)S(1)}, f32[8,64,512]{2,1,0:T(8,128)}, u32[]{:S(2)}) copy-start(f32[8,64,512]{2,1,0:T(8,128)} %operator_ref.1) | copy-start | bytes 3145732

commit v2 on v1

v2 whole, which is shorter than its diff:
```python
import functools

import jax
import jax.numpy as jnp
from jax import lax
from jax.experimental import pallas as pl
from jax.experimental.pallas import tpu as pltpu
from jax.sharding import Mesh
from jax.sharding import PartitionSpec as P

NCR = 2
LANES = 128
VMEM_LIMIT = 48 * 1024 * 1024


def split3(x, order):
    high = x.astype(jnp.bfloat16)
    low = (x - high.astype(jnp.float32)).astype(jnp.bfloat16)
    parts = {"left": (high, low, high), "right": (high, high, low)}[order]
    return jnp.concatenate(parts, axis=0)


def transposed_dot(left, right):
    return lax.dot_general(left, right, (((0,), (0,)), ((), ())), preferred_element_type=jnp.float32)


def restrict_kernel(count_ref, slot_ref, rows_ref, operator_ref, restrict_ref, out_ref, sums_ref):
    fine_rows, block_size, _ = operator_ref.shape
    entries = slot_ref.shape[1]
    sums_ref[...] = jnp.zeros_like(sums_ref)
    lane = lax.broadcasted_iota(jnp.int32, (block_size, NCR * block_size), 1)
    second = (lane >= block_size).astype(jnp.int32)

    for i in range(fine_rows):
        value = restrict_ref[i]
        swapped = pltpu.roll(value, block_size, 1)
        own_row = jnp.where(second == 0, rows_ref[0, i], rows_ref[1, i])
        other_row = jnp.where(second == 0, rows_ref[1, i], rows_ref[0, i])
        dense = jnp.where(own_row == second, value, 0.0) + jnp.where(other_row == second, swapped, 0.0)
        product = transposed_dot(split3(operator_ref[i], "left"), split3(dense, "right"))
        for k in range(entries):
            part = product[k * block_size : (k + 1) * block_size]
            slot = slot_ref[i, k]
            sums_ref[slot] += jnp.where(k < count_ref[i], part, 0.0)

    def finish(slot, carry):
        out_ref[slot] = split3(sums_ref[slot], "right")
        return carry

    lax.fori_loop(0, out_ref.shape[0], finish, 0, unroll=8)


def restrict_operator(operator_count, operator_slot, restrict_rows, operator_blocks, restrict_blocks, slots):
    fine_rows, block_size, width = operator_blocks.shape
    wide = NCR * block_size
    return pl.pallas_call(
        restrict_kernel,
        out_shape=jax.ShapeDtypeStruct((slots, 3 * block_size, wide), jnp.bfloat16),
        in_specs=[pl.BlockSpec(memory_space=pltpu.SMEM)] * 3 + [pl.BlockSpec(memory_space=pltpu.VMEM)] * 2,
        out_specs=pl.BlockSpec(memory_space=pltpu.VMEM),
        scratch_shapes=[pltpu.VMEM((slots, block_size, wide), jnp.float32)],
        compiler_params=pltpu.CompilerParams(vmem_limit_bytes=VMEM_LIMIT),
        cost_estimate=pl.CostEstimate(
            flops=6 * fine_rows * block_size * width * wide, bytes_accessed=4 << 20, transcendentals=0
        ),
        name="restrict_operator",
    )(operator_count, operator_slot, restrict_rows, operator_blocks, restrict_blocks)


def lookup_kernel(half_ref, fetch_ref, table_ref, out_ref, *, fine_rows, rows, columns, entries):
    slot_count = fetch_ref.shape[0]
    half = columns // 2
    own_half = half_ref[0]

    for peer in range(columns):
        for s in range(slot_count):
            slot = peer * slot_count + s
            wanted = fetch_ref[s, peer]
            group = lax.div(wanted, fine_rows * columns)
            inside = lax.rem(wanted, fine_rows)
            far = jnp.where(own_half == peer // half, 0, 1)
            out_ref[0, slot] = 2 * (group * half + peer % half) + far
            holder = (group * 2 + peer // half) * half + peer % half
            for m in range(entries):
                out_ref[1 + m, slot] = table_ref[holder, 2 + entries * inside + m]


def lookup(fetch, table, **sizes):
    slots = fetch.size
    return pl.pallas_call(
        functools.partial(lookup_kernel, **sizes),
        out_shape=jax.ShapeDtypeStruct((1 + sizes["entries"], slots), jnp.int32),
        in_specs=[pl.BlockSpec(memory_space=pltpu.SMEM)] * 3,
        out_specs=pl.BlockSpec(memory_space=pltpu.SMEM),
        cost_estimate=pl.CostEstimate(flops=1 << 20, bytes_accessed=1 << 20, transcendentals=0),
        name="lookup",
    )(lax.axis_index("half").reshape(1), fetch, table)


def combine_kernel(where_ref, restricted_ref, blocks_ref, out_ref):
    slots = restricted_ref.shape[0]
    block_size = out_ref.shape[1]
    out_ref[...] = jnp.zeros_like(out_ref)

    def step(slot, carry):
        block = blocks_ref[where_ref[0, slot]]
        product = transposed_dot(split3(block, "left"), restricted_ref[slot])
        for m in range(where_ref.shape[0] - 1):
            out_ref[where_ref[1 + m, slot]] += product[m * block_size : (m + 1) * block_size]
        return carry

    lax.fori_loop(0, slots, step, 0, unroll=8)


def combine(where, restricted, blocks, coarse_all):
    block_size = blocks.shape[1]
    wide = restricted.shape[2]
    return pl.pallas_call(
        combine_kernel,
        out_shape=jax.ShapeDtypeStruct((coarse_all, block_size, wide), jnp.float32),
        in_specs=[pl.BlockSpec(memory_space=pltpu.SMEM)] + [pl.BlockSpec(memory_space=pltpu.VMEM)] * 2,
        out_specs=pl.BlockSpec(memory_space=pltpu.VMEM),
        compiler_params=pltpu.CompilerParams(vmem_limit_bytes=VMEM_LIMIT),
        cost_estimate=pl.CostEstimate(flops=1 << 28, bytes_accessed=4 << 20, transcendentals=0),
        name="combine",
    )(where, restricted, blocks)


def pick_kernel(request_ref, near_ref, far_ref, out_ref):
    def step(place, carry):
        out_ref[2 * place] = near_ref[request_ref[0, place]]
        out_ref[2 * place + 1] = far_ref[request_ref[1, place]]
        return carry

    lax.fori_loop(0, request_ref.shape[1], step, 0, unroll=8)


def pick(request, near, far):
    return pl.pallas_call(
        pick_kernel,
        out_shape=jax.ShapeDtypeStruct((2 * request.shape[1],) + near.shape[1:], near.dtype),
        in_specs=[pl.BlockSpec(memory_space=pltpu.SMEM)] + [pl.BlockSpec(memory_space=pltpu.VMEM)] * 2,
        out_specs=pl.BlockSpec(memory_space=pltpu.VMEM),
        compiler_params=pltpu.CompilerParams(vmem_limit_bytes=VMEM_LIMIT),
        cost_estimate=pl.CostEstimate(flops=0, bytes_accessed=2 << 20, transcendentals=0),
        name="pick",
    )(request, near, far)


def add_kernel(parts_ref, out_ref):
    total = parts_ref[0]
    for i in range(1, parts_ref.shape[0]):
        total = total + parts_ref[i]
    out_ref[...] = total


def add_up(parts):
    return pl.pallas_call(
        add_kernel,
        out_shape=jax.ShapeDtypeStruct(parts.shape[1:], parts.dtype),
        in_specs=[pl.BlockSpec(memory_space=pltpu.VMEM)],
        out_specs=pl.BlockSpec(memory_space=pltpu.VMEM),
        compiler_params=pltpu.CompilerParams(vmem_limit_bytes=VMEM_LIMIT),
        name="add_up",
    )(parts)


def requests(fetch, prolong_cols, fine_rows, rows, columns):
    half = columns // 2
    own_half = lax.axis_index("half")
    owner_row = fetch // (fine_rows * columns)
    inside = fetch % fine_rows
    mine = owner_row[None] == jnp.arange(rows, dtype=jnp.int32)[:, None, None]
    wanted = jnp.sum(jnp.where(mine, inside[None], 0), axis=1)
    first, second = wanted[:, :half], wanted[:, half:]
    near = jnp.where(own_half == 0, first, second)
    far = jnp.where(own_half == 0, second, first)
    pair = jnp.stack([near, far], axis=-1)[:, None]
    pair = jnp.broadcast_to(pair, (rows, 2, half, 2)).reshape(rows * columns, 2)
    own_columns = jnp.broadcast_to(prolong_cols.reshape(1, -1), (rows * columns, prolong_cols.size))
    message = jnp.concatenate([pair, own_columns], axis=1)
    return jnp.pad(message, ((0, 0), (0, LANES - message.shape[1])))


def local(
    operator_blocks,
    operator_count,
    operator_slot,
    fetch_lists,
    prolong_blocks,
    prolong_cols,
    restrict_blocks,
    restrict_rows,
):
    fine_rows = operator_blocks.shape[0]
    entries = prolong_cols.shape[1]
    rows, half = lax.axis_size("row"), lax.axis_size("near")
    columns = 2 * half
    fetch = fetch_lists.reshape(columns, fetch_lists.shape[3]).T

    far_blocks = lax.ppermute(prolong_blocks, "half", [(0, 1), (1, 0)])
    message = requests(fetch, prolong_cols, fine_rows, rows, columns)
    table = lax.all_to_all(message[:, None, :], ("row", "half", "near"), split_axis=0, concat_axis=0, tiled=True)[:, 0]
    here = lax.dynamic_index_in_dim(table.reshape(rows, 2, half, LANES), lax.axis_index("half"), 1, False)
    request = here[..., :2].reshape(rows * half, 2).T

    restricted = restrict_operator(
        operator_count, operator_slot, restrict_rows.T, operator_blocks, restrict_blocks, fetch.size
    )
    picked = pick(request, prolong_blocks, far_blocks)
    pairs = picked.reshape((rows * half, 2) + picked.shape[1:])
    blocks = lax.all_to_all(pairs, ("row", "near"), split_axis=0, concat_axis=0, tiled=True)
    where = lookup(fetch, table, fine_rows=fine_rows, rows=rows, columns=columns, entries=entries)
    partial_sums = combine(where, restricted, blocks.reshape(picked.shape), NCR * rows)
    parts = lax.all_to_all(partial_sums, ("half", "near"), split_axis=0, concat_axis=0, tiled=True)
    return add_up(parts).T


def solution(mesh):
    rows, columns = mesh.shape["row"], mesh.shape["col"]
    split = Mesh(mesh.devices.reshape(rows, 2, columns // 2), ("row", "half", "near"))
    flat = ("row", "half", "near")
    return jax.shard_map(
        local,
        mesh=split,
        in_specs=(
            P(flat, None, None),
            P(flat),
            P(flat, None),
            P("row", ("half", "near"), None, None),
            P(flat, None, None),
            P(flat, None),
            P(flat, None, None),
            P(flat, None),
        ),
        out_specs=P("row", ("half", "near")),
        check_vma=False,
    )
```

time: 64 us -> 57.3 us (0.90)
  blocking collectives: 25.7 us -> 13.9 us
  starting transfers between devices: 2.64 us -> 11.5 us
  waiting for transfers between devices: 24.4 us -> 18 us
  Pallas kernels: 6.07 us -> 7.79 us
  local copies, waits for them, and re-layouts: 4.05 us -> 4.76 us
    all_to_all x2 -> x1, blocking collectives: 25.7 us -> 13.9 us  [local(): lax.all_to_all(partial_sums, ('half', 'near'), split_axis=0, concat_axis=...]
    all_to_all x1 -> x2, waiting for transfers between devices: 24.4 us -> 18 us  [the longest x1 9.93 us: local(): lax.all_to_all(pairs, ('row', 'near'), split_axis=0, concat_axis=0, tiled...]
    all_to_all x1 -> x2, starting transfers between devices: 2.64 us -> 7.48 us  [the longest x1 3.82 us: local(): lax.all_to_all(message[:, None, :], ('row', 'half', 'near'), split_axis=0...]
    ppermute x0 -> x1, starting transfers between devices: none -> 4.04 us  [local(): far_blocks = lax.ppermute(prolong_blocks, 'half', [(0, 1), (1, 0)])]
    pallas_call x3 -> x4, Pallas kernels: 4.29 us -> 6.06 us  [the longest x1 2.01 us: combine(): pl.pallas_call(combine_kernel, out_shape=jax.ShapeDtypeStruct((coarse_all...]
    pallas_call x1 -> x0, local copies, waits for them, and re-layouts: 0.7 us -> none  [add_up(): pl.pallas_call(add_kernel, out_shape=jax.ShapeDtypeStruct((parts.shape[2]...]
    unnamed x16 -> x18, local copies, waits for them, and re-layouts: 3.03 us -> 3.73 us
  transfers between devices with their start and end apart: 1 -> 3, of which waited for: 1 -> 2; matrix products, arithmetic and copies ran while one was open for 0% -> 5% of each run, Pallas kernels for 3% -> 6%
where the time goes in v2:
time: 57.3 us; the launch traced here: 56.9 us
  waiting for transfers between devices  18 us (31%)
  blocking collectives  13.9 us (24%)
  starting transfers between devices  11.5 us (20%)
  Pallas kernels  7.79 us (14%)
  local copies, waits for them, and re-layouts  4.76 us (8%)
  other arithmetic  0.81 us (1%)
    all_to_all x1, blocking collectives, local(): lax.all_to_all(partial_sums, ('half', 'near'), split_axis=0, concat_axis=...  13.9 us
    all_to_all x1, waiting for transfers between devices, local(): lax.all_to_all(pairs, ('row', 'near'), split_axis=0, concat_axis=0, tiled...  9.93 us
    all_to_all x1, waiting for transfers between devices, local(): lax.all_to_all(message[:, None, :], ('row', 'half', 'near'), split_axis=0...  8.06 us
    ppermute x1, starting transfers between devices, local(): far_blocks = lax.ppermute(prolong_blocks, 'half', [(0, 1), (1, 0)])  4.04 us
    all_to_all x1, starting transfers between devices, local(): lax.all_to_all(message[:, None, :], ('row', 'half', 'near'), split_axis=0...  3.82 us
    unnamed x18, local copies, waits for them, and re-layouts  3.73 us
    all_to_all x1, starting transfers between devices, local(): lax.all_to_all(pairs, ('row', 'near'), split_axis=0, concat_axis=0, tiled...  3.65 us
    pallas_call x1, Pallas kernels, combine(): pl.pallas_call(combine_kernel, out_shape=jax.ShapeDtypeStruct((coarse_all...  2.01 us
  transfers between devices with their start and end apart: 3, of which 2 were waited for; matrix products, arithmetic and copies ran while one was open for 5% of the time, Pallas kernels for 6%

profile of v2, /device:TPU:0, one launch (start us, length us, event | category | flops | bytes accessed | tf_op | source)
XLA Modules:
  0.0 56.9 jit_solution(9671222157436370221)
XLA Ops:
  0.0 4.0 %collective-permute-start = (f32[8,64,128]{2,1,0:T(8,128)}, f32[8,64,128]{2,1,0:T(8,128)S(1)}, u32[]{:S(2)}, u32[]{:S(2)}) collective-permute-start(f32[8,64,128]{2,1,0:T(8,128)} %near_ref.1), channel_id=1, source_target_pairs={{0,4},{4,0},{1,5},{5,1},{2,6},{6,2},{3,7},{7,3},{8,12},{12,8},{9,1... | collective-permute-start | bytes 786440 | tf_op jit(solution)/shard_map/ppermute | solution.py:201
  4.0 0.8 %copy.18 = s32[8,2]{1,0:T(8,128)S(1)} copy(s32[8,2]{0,1:T(2,128)} %param.13) | data formatting | bytes 128 | tf_op args[5]
  4.8 0.1 reshape.29
  4.9 0.1 pad.6.clone
  4.9 0.7 %add_select_fusion.1 = (s32[4,8]{1,0:T(4,128)S(1)}, s32[4,8]{1,0:T(4,128)S(1)}) fusion(s32[1,1,8,4]{2,3,1,0:T(4,128)} %param.11), kind=kLoop, calls=%fused_computation.6 | loop fusion | flops 736 | bytes 384 | tf_op jit(solution)/shard_map/jit(floor_divide)/jit(_where)/select_n | solution.py:171
  5.7 0.1 select_bitcast_fusion.1
  5.7 0.1 copy.22
  5.9 0.6 %pad.4 = s32[32,128]{1,0:T(8,128)} pad(s32[32,18]{1,0:T(8,128)S(1)} %pad_add_fusion, s32[]{:T(128)} %constant.34.clone.1), padding=0_0x0_110 | pad | bytes 18692 | tf_op jit(solution)/shard_map/jit(_pad)/pad | solution.py:182
  6.5 3.8 %all-to-all-start = ((s32[32,1,128]{2,1,0:T(1,128)}), s32[32,1,128]{2,1,0:T(1,128)S(1)}, u32[]{:S(2)}, u32[]{:S(2)}) async-start(s32[32,1,128]{2,1,0:T(1,128)} %bitcast.7), calls=%async_computation | async-start | bytes 32768 | tf_op jit(solution)/shard_map/all_to_all | solution.py:203
  10.3 8.1 %all-to-all-done = s32[32,1,128]{2,1,0:T(1,128)S(1)} async-done(((s32[32,1,128]{2,1,0:T(1,128)}), s32[32,1,128]{2,1,0:T(1,128)S(1)}, u32[]{:S(2)}, u32[]{:S(2)}) %all-to-all-start) | async-done | bytes 16416 | tf_op jit(solution)/shard_map/all_to_all | solution.py:203
  18.4 0.2 copy.20
  18.6 0.1 reshape.26
  18.7 1.0 %copy-done.2 = f32[8,64,128]{2,1,0:T(8,128)S(1)} copy-done((f32[8,64,128]{2,1,0:T(8,128)S(1)}, f32[8,64,128]{2,1,0:T(8,128)}, u32[]{:S(2)}) %copy-start.2) | copy-done | bytes 262168
  19.6 1.6 %pick.1 = f32[32,64,128]{2,1,0:T(8,128)} custom-call(s32[2,16]{1,0:T(2,128)S(1)} %bitcast.23, f32[8,64,128]{2,1,0:T(8,128)S(1)} %copy-done.2, f32[8,64,128]{2,1,0:T(8,128)S(1)} %collective-permute-done.far_ref), custom_call_target="tpu_custom_call" | custom-call | bytes 2097152 | tf_op jit(solution)/shard_map/pick/pallas_call | solution.py:139
  21.2 3.7 %all-to-all-start.1 = ((f32[16,2,64,128]{3,2,1,0:T(8,128)}), f32[16,2,64,128]{3,2,1,0:T(8,128)S(1)}, u32[]{:S(2)}, u32[]{:S(2)}) async-start(f32[16,2,64,128]{3,2,1,0:T(8,128)} %bitcast.13), calls=%async_computation.1 | async-start | bytes 2097152 | tf_op jit(solution)/shard_map/all_to_all | solution.py:212
  24.9 0.0 copy-start
  25.0 1.2 %copy-done = f32[8,64,512]{2,1,0:T(8,128)S(1)} copy-done((f32[8,64,512]{2,1,0:T(8,128)S(1)}, f32[8,64,512]{2,1,0:T(8,128)}, u32[]{:S(2)}) %copy-start) | copy-done | bytes 1048600
  26.2 1.7 %restrict_operator.1.restricted_ref = bf16[32,192,128]{2,1,0:T(8,128)(2,1)S(1)} custom-call(s32[8]{0:T(128)S(1)} %copy-done.6, s32[8,8]{1,0:T(8,128)S(1)} %copy-done.4, s32[2,8]{1,0:T(2,128)S(1)} %bitcast.24, f32[8,64,512]{2,1,0:T(8,128)S(1)} %copy-done, f32[8,64,128]{2,1,0:T(8,128)S(1)} %copy-done.1), custom_call_target="tpu_custom_call" | custom-call | flops 201326592 | bytes 4194304 | tf_op jit(solution)/shard_map/restrict_operator/pallas_call | solution.py:56
  27.9 1.8 %lookup.1.where_ref = s32[3,32]{1,0:T(4,128)} custom-call(s32[1]{0:T(128)} %bitcast.half_ref, s32[4,8]{1,0:T(4,128)} %bitcast.29, s32[32,128]{1,0:T(8,128)} %bitcast.27), custom_call_target="tpu_custom_call" | custom-call | flops 1048576 | bytes 1048576 | tf_op jit(solution)/shard_map/lookup/pallas_call | solution.py:90
  29.7 9.9 %all-to-all-done.1 = f32[16,2,64,128]{3,2,1,0:T(8,128)S(1)} async-done(((f32[16,2,64,128]{3,2,1,0:T(8,128)}), f32[16,2,64,128]{3,2,1,0:T(8,128)S(1)}, u32[]{:S(2)}, u32[]{:S(2)}) %all-to-all-start.1) | async-done | bytes 1048608 | tf_op jit(solution)/shard_map/all_to_all | solution.py:212
  39.7 0.7 %copy-done.3 = s32[3,32]{1,0:T(4,128)S(1)} copy-done((s32[3,32]{1,0:T(4,128)S(1)}, s32[3,32]{1,0:T(4,128)}, u32[]{:S(2)}) %copy-start.3) | copy-done | bytes 408
  40.3 2.0 %combine.1 = f32[8,64,128]{2,1,0:T(8,128)S(1)} custom-call(s32[3,32]{1,0:T(4,128)S(1)} %copy-done.3, bf16[32,192,128]{2,1,0:T(8,128)(2,1)S(1)} %restrict_operator.1.restricted_ref, f32[32,64,128]{2,1,0:T(8,128)S(1)} %bitcast.22), custom_call_target="tpu_custom_call" | custom-call | flops 268435456 | bytes 4194304 | tf_op jit(solution)/shard_map/combine/pallas_call | solution.py:118
  42.3 13.9 %all_to_all.15.parts_ref = f32[8,64,128]{2,1,0:T(8,128)S(1)} all-to-all(f32[8,64,128]{2,1,0:T(8,128)S(1)} %combine.1), channel_id=1, replica_groups=mesh['row'=4,'half'=2,'near'=4] {'half','near'}, dimensions={0} | all-to-all | bytes 524288 | tf_op jit(solution)/shard_map/all_to_all | solution.py:215
  56.3 0.6 %add_up.1 = f32[64,128]{1,0:T(8,128)} custom-call(f32[8,64,128]{2,1,0:T(8,128)S(1)} %all_to_all.15.parts_ref), custom_call_target="tpu_custom_call" | custom-call | tf_op jit(solution)/shard_map/add_up/pallas_call | solution.py:158
  (19 shorter events, 0.1 us)
Async XLA Ops:
  0.0 18.7 %collective-permute-start = (f32[8,64,128]{2,1,0:T(8,128)}, f32[8,64,128]{2,1,0:T(8,128)S(1)}, u32[]{:S(2)}, u32[]{:S(2)}) collective-permute-start(f32[8,64,128]{2,1,0:T(8,128)} %near_ref.1), channel_id=1, source_target_pairs={{0,4},{4,0},{1,5},{5,1},{2,6},{6,2},{3,7},{7,3},{8,12},{12,8},{9,1... | collective-permute-start | bytes 786440 | tf_op jit(solution)/shard_map/ppermute | solution.py:201
  6.5 11.9 %all-to-all-start = ((s32[32,1,128]{2,1,0:T(1,128)}), s32[32,1,128]{2,1,0:T(1,128)S(1)}, u32[]{:S(2)}, u32[]{:S(2)}) async-start(s32[32,1,128]{2,1,0:T(1,128)} %bitcast.7), calls=%async_computation | async-start | bytes 32768 | tf_op jit(solution)/shard_map/all_to_all | solution.py:203
  18.4 2.9 %copy-start.7 = (s32[32,1,128]{2,1,0:T(1,128)}, s32[32,1,128]{2,1,0:T(1,128)S(1)}, u32[]{:S(2)}) copy-start(s32[32,1,128]{2,1,0:T(1,128)S(1)} %all-to-all-done) | copy-start | bytes 49156
  18.7 1.0 %copy-start.2 = (f32[8,64,128]{2,1,0:T(8,128)S(1)}, f32[8,64,128]{2,1,0:T(8,128)}, u32[]{:S(2)}) copy-start(f32[8,64,128]{2,1,0:T(8,128)} %near_ref.1) | copy-start | bytes 786436
  19.6 5.3 %copy-start.1 = (f32[8,64,128]{2,1,0:T(8,128)S(1)}, f32[8,64,128]{2,1,0:T(8,128)}, u32[]{:S(2)}) copy-start(f32[8,64,128]{2,1,0:T(8,128)} %restrict_ref.1) | copy-start | bytes 786436
  19.6 5.3 %copy-start.4 = (s32[8,8]{1,0:T(8,128)S(1)}, s32[8,8]{1,0:T(8,128)}, u32[]{:S(2)}) copy-start(s32[8,8]{1,0:T(8,128)} %slot_ref.1) | copy-start | bytes 772
  19.6 5.3 %copy-start.5 = (s32[8,2]{0,1:T(2,128)S(1)}, s32[8,2]{0,1:T(2,128)}, u32[]{:S(2)}) copy-start(s32[8,2]{0,1:T(2,128)} %param.15) | copy-start | bytes 196
  19.6 5.3 %copy-start.6 = (s32[8]{0:T(128)S(1)}, s32[8]{0:T(128)}, u32[]{:S(2)}) copy-start(s32[8]{0:T(128)} %count_ref.1) | copy-start | bytes 100
  21.2 18.4 %all-to-all-start.1 = ((f32[16,2,64,128]{3,2,1,0:T(8,128)}), f32[16,2,64,128]{3,2,1,0:T(8,128)S(1)}, u32[]{:S(2)}, u32[]{:S(2)}) async-start(f32[16,2,64,128]{3,2,1,0:T(8,128)} %bitcast.13), calls=%async_computation.1 | async-start | bytes 2097152 | tf_op jit(solution)/shard_map/all_to_all | solution.py:212
  24.9 1.2 %copy-start = (f32[8,64,512]{2,1,0:T(8,128)S(1)}, f32[8,64,512]{2,1,0:T(8,128)}, u32[]{:S(2)}) copy-start(f32[8,64,512]{2,1,0:T(8,128)} %operator_ref.1) | copy-start | bytes 3145732
  39.7 0.7 %copy-start.3 = (s32[3,32]{1,0:T(4,128)S(1)}, s32[3,32]{1,0:T(4,128)}, u32[]{:S(2)}) copy-start(s32[3,32]{1,0:T(4,128)} %lookup.1.where_ref) | copy-start | bytes 1156

commit v3 on v2

v3 whole, which is shorter than its diff:
```python
import functools

import jax
import jax.numpy as jnp
from jax import lax
from jax.experimental import pallas as pl
from jax.experimental.pallas import tpu as pltpu
from jax.sharding import Mesh
from jax.sharding import PartitionSpec as P

NCR = 2
LANES = 128
VMEM_LIMIT = 48 * 1024 * 1024


def split3(x, order):
    high = x.astype(jnp.bfloat16)
    low = (x - high.astype(jnp.float32)).astype(jnp.bfloat16)
    parts = {"left": (high, low, high), "right": (high, high, low)}[order]
    return jnp.concatenate(parts, axis=0)


def transposed_dot(left, right):
    return lax.dot_general(left, right, (((0,), (0,)), ((), ())), preferred_element_type=jnp.float32)


def restrict_kernel(count_ref, slot_ref, rows_ref, operator_ref, restrict_ref, out_ref, sums_ref):
    fine_rows, block_size, _ = operator_ref.shape
    entries = slot_ref.shape[1]
    sums_ref[...] = jnp.zeros_like(sums_ref)
    lane = lax.broadcasted_iota(jnp.int32, (block_size, NCR * block_size), 1)
    second = (lane >= block_size).astype(jnp.int32)

    for i in range(fine_rows):
        value = restrict_ref[i]
        swapped = pltpu.roll(value, block_size, 1)
        own_row = jnp.where(second == 0, rows_ref[0, i], rows_ref[1, i])
        other_row = jnp.where(second == 0, rows_ref[1, i], rows_ref[0, i])
        dense = jnp.where(own_row == second, value, 0.0) + jnp.where(other_row == second, swapped, 0.0)
        product = transposed_dot(split3(operator_ref[i], "left"), split3(dense, "right"))
        for k in range(entries):
            part = product[k * block_size : (k + 1) * block_size]
            slot = slot_ref[i, k]
            sums_ref[slot] += jnp.where(k < count_ref[i], part, 0.0)

    def finish(slot, carry):
        out_ref[slot] = split3(sums_ref[slot], "right")
        return carry

    lax.fori_loop(0, out_ref.shape[0], finish, 0, unroll=8)


def restrict_operator(operator_count, operator_slot, restrict_rows, operator_blocks, restrict_blocks, slots):
    fine_rows, block_size, width = operator_blocks.shape
    wide = NCR * block_size
    return pl.pallas_call(
        restrict_kernel,
        out_shape=jax.ShapeDtypeStruct((slots, 3 * block_size, wide), jnp.bfloat16),
        in_specs=[pl.BlockSpec(memory_space=pltpu.SMEM)] * 3 + [pl.BlockSpec(memory_space=pltpu.VMEM)] * 2,
        out_specs=pl.BlockSpec(memory_space=pltpu.VMEM),
        scratch_shapes=[pltpu.VMEM((slots, block_size, wide), jnp.float32)],
        compiler_params=pltpu.CompilerParams(vmem_limit_bytes=VMEM_LIMIT),
        cost_estimate=pl.CostEstimate(
            flops=6 * fine_rows * block_size * width * wide, bytes_accessed=4 << 20, transcendentals=0
        ),
        name="restrict_operator",
    )(operator_count, operator_slot, restrict_rows, operator_blocks, restrict_blocks)


def message_kernel(half_ref, fetch_ref, columns_ref, out_ref, *, fine_rows):
    slot_count, columns = fetch_ref.shape
    entries = columns_ref.shape[0]
    half = columns // 2
    own_half = half_ref[0]
    row = lax.broadcasted_iota(jnp.int32, out_ref.shape, 0)
    lane = lax.broadcasted_iota(jnp.int32, out_ref.shape, 1)
    value = jnp.zeros(out_ref.shape, jnp.int32)
    for i in range(fine_rows):
        for m in range(entries):
            value = jnp.where(lane == 2 + entries * i + m, columns_ref[m, i], value)
    for peer in range(columns):
        far = jnp.where(own_half == peer // half, 0, 1)
        for s in range(slot_count):
            wanted = fetch_ref[s, peer]
            place = lax.div(wanted, fine_rows * columns) * half + peer % half
            value = jnp.where((row == place) & (lane == far), lax.rem(wanted, fine_rows), value)
    out_ref[...] = value


def build_message(own_half, fetch, columns, rows, fine_rows):
    return pl.pallas_call(
        functools.partial(message_kernel, fine_rows=fine_rows),
        out_shape=jax.ShapeDtypeStruct((rows, LANES), jnp.int32),
        in_specs=[pl.BlockSpec(memory_space=pltpu.SMEM)] * 3,
        out_specs=pl.BlockSpec(memory_space=pltpu.VMEM),
        cost_estimate=pl.CostEstimate(flops=0, bytes_accessed=1 << 14, transcendentals=0),
        name="build_message",
    )(own_half, fetch, columns)


def pick_kernel(table_ref, blocks_ref, out_ref, sems, *, far):
    places = out_ref.shape[0]

    def copy(place):
        return pltpu.make_async_copy(blocks_ref.at[table_ref[place, far]], out_ref.at[place], sems.at[place])

    def start(place, carry):
        copy(place).start()
        return carry

    def wait(place, carry):
        copy(place).wait()
        return carry

    lax.fori_loop(0, places, start, 0, unroll=16)
    lax.fori_loop(0, places, wait, 0, unroll=16)


def pick(table, blocks, far):
    places = table.shape[0]
    return pl.pallas_call(
        functools.partial(pick_kernel, far=far),
        out_shape=jax.ShapeDtypeStruct((places,) + blocks.shape[1:], blocks.dtype),
        in_specs=[pl.BlockSpec(memory_space=pltpu.SMEM), pl.BlockSpec(memory_space=pltpu.HBM)],
        out_specs=pl.BlockSpec(memory_space=pltpu.HBM),
        scratch_shapes=[pltpu.SemaphoreType.DMA((places,))],
        cost_estimate=pl.CostEstimate(flops=0, bytes_accessed=1 << 20, transcendentals=0),
        name="pick_far" if far else "pick_near",
    )(table, blocks)


def combine_kernel(half_ref, fetch_ref, table_ref, restricted_ref, blocks_ref, *rest, fine_rows, entries):
    out_ref = rest[-1]
    far = len(rest) - 1
    slot_count, columns = fetch_ref.shape
    half = columns // 2
    block_size = out_ref.shape[1]
    first_peer = half * (half_ref[0] if far == 0 else 1 - half_ref[0])
    first_slot = far * half * slot_count
    out_ref[...] = rest[0][...] if far else jnp.zeros_like(out_ref)

    def step(j, carry):
        near_peer = lax.div(j, slot_count)
        wanted = fetch_ref[lax.rem(j, slot_count), first_peer + near_peer]
        place = lax.div(wanted, fine_rows * columns) * half + near_peer
        inside = lax.rem(wanted, fine_rows)
        product = transposed_dot(split3(blocks_ref[place], "left"), restricted_ref[first_slot + j])
        for m in range(entries):
            column = table_ref[place, 2 + entries * inside + m]
            out_ref[column] += product[m * block_size : (m + 1) * block_size]
        return carry

    lax.fori_loop(0, half * slot_count, step, 0, unroll=16)


def combine(own_half, fetch, table, restricted, blocks, so_far, coarse_all, fine_rows, entries):
    block_size = blocks.shape[1]
    wide = restricted.shape[2]
    return pl.pallas_call(
        functools.partial(combine_kernel, fine_rows=fine_rows, entries=entries),
        out_shape=jax.ShapeDtypeStruct((coarse_all, block_size, wide), jnp.float32),
        in_specs=[pl.BlockSpec(memory_space=pltpu.SMEM)] * 3
        + [pl.BlockSpec(memory_space=pltpu.VMEM)] * (2 + len(so_far)),
        out_specs=pl.BlockSpec(memory_space=pltpu.VMEM),
        compiler_params=pltpu.CompilerParams(vmem_limit_bytes=VMEM_LIMIT),
        cost_estimate=pl.CostEstimate(flops=1 << 27, bytes_accessed=2 << 20, transcendentals=0),
        name="combine_far" if so_far else "combine_near",
    )(own_half, fetch, table, restricted, blocks, *so_far)


def add_kernel(parts_ref, out_ref):
    total = parts_ref[0]
    for i in range(1, parts_ref.shape[0]):
        total = total + parts_ref[i]
    out_ref[...] = total


def add_up(parts):
    return pl.pallas_call(
        add_kernel,
        out_shape=jax.ShapeDtypeStruct(parts.shape[1:], parts.dtype),
        in_specs=[pl.BlockSpec(memory_space=pltpu.VMEM)],
        out_specs=pl.BlockSpec(memory_space=pltpu.VMEM),
        compiler_params=pltpu.CompilerParams(vmem_limit_bytes=VMEM_LIMIT),
        name="add_up",
    )(parts)


def local(
    operator_blocks,
    operator_count,
    operator_slot,
    fetch_lists,
    prolong_blocks,
    prolong_cols,
    restrict_blocks,
    restrict_rows,
):
    fine_rows = operator_blocks.shape[0]
    entries = prolong_cols.shape[1]
    rows, half = lax.axis_size("row"), lax.axis_size("near")
    fetch = fetch_lists.reshape(2 * half, fetch_lists.shape[3]).T
    own_half = lax.axis_index("half").reshape(1)
    swap = [(0, 1), (1, 0)]

    far_blocks = lax.ppermute(prolong_blocks, "half", swap)
    message = build_message(own_half, fetch, prolong_cols.T, rows * half, fine_rows)
    table = lax.all_to_all(message[:, None], ("row", "near"), split_axis=0, concat_axis=0, tiled=True)[:, 0]
    far_table = lax.ppermute(table, "half", swap)
    near = lax.all_to_all(pick(table, prolong_blocks, 0), ("row", "near"), split_axis=0, concat_axis=0, tiled=True)
    far = lax.all_to_all(pick(table, far_blocks, 1), ("row", "near"), split_axis=0, concat_axis=0, tiled=True)

    slot = (operator_slot + own_half * (fetch.size // 2)) % fetch.size
    restricted = restrict_operator(
        operator_count, slot, restrict_rows.T, operator_blocks, restrict_blocks, fetch.size
    )
    sizes = (NCR * rows, fine_rows, entries)
    sums = combine(own_half, fetch, table, restricted, near, (), *sizes)
    sums = combine(own_half, fetch, far_table, restricted, far, (sums,), *sizes)
    parts = lax.all_to_all(sums, ("half", "near"), split_axis=0, concat_axis=0, tiled=True)
    return add_up(parts).T


def solution(mesh):
    rows, columns = mesh.shape["row"], mesh.shape["col"]
    split = Mesh(mesh.devices.reshape(rows, 2, columns // 2), ("row", "half", "near"))
    flat = ("row", "half", "near")
    return jax.shard_map(
        local,
        mesh=split,
        in_specs=(
            P(flat, None, None),
            P(flat),
            P(flat, None),
            P("row", ("half", "near"), None, None),
            P(flat, None, None),
            P(flat, None),
            P(flat, None, None),
            P(flat, None),
        ),
        out_specs=P("row", ("half", "near")),
        check_vma=False,
    )
```

time: 57.3 us -> 99.1 us (1.73)
  Pallas kernels: 7.79 us -> 42.2 us
  blocking collectives: 13.9 us -> 25.2 us
  waiting for transfers between devices: 18 us -> 12.2 us
  starting transfers between devices: 11.5 us -> 16.9 us
  local copies, waits for them, and re-layouts: 4.76 us -> 1.98 us
    pallas_call x3 -> x5, Pallas kernels: 5.43 us -> 39.8 us  [the longest x2 35.8 us: pick(): pl.pallas_call(functools.partial(pick_kernel, far=far), out_shape=jax.Sha...]
    all_to_all x2, waiting for transfers between devices: 18 us -> 1.8 us  [the longest x1 1.79 us: local(): lax.all_to_all(pick(table, far_blocks, 1), ('row', 'near'), split_axis=0,...]
    all_to_all x1 -> x2, blocking collectives: 13.9 us -> 25.2 us  [the longest x1 13.6 us: local(): lax.all_to_all(sums, ('half', 'near'), split_axis=0, concat_axis=0, tiled...]
    ppermute x1 -> x2, waiting for transfers between devices: 0.01 us -> 10.4 us  [the longest x1 9.57 us: local(): far_blocks = lax.ppermute(prolong_blocks, 'half', swap)]
    all_to_all x2, starting transfers between devices: 7.48 us -> 11.6 us  [the longest x1 7.87 us: local(): lax.all_to_all(pick(table, far_blocks, 1), ('row', 'near'), split_axis=0,...]
    unnamed x18, local copies, waits for them, and re-layouts: 3.73 us -> 1.98 us
    ppermute x1 -> x2, starting transfers between devices: 4.04 us -> 5.27 us  [the longest x1 2.65 us: local(): far_blocks = lax.ppermute(prolong_blocks, 'half', swap)]
  transfers between devices with their start and end apart: 3 -> 4, of which waited for: 2 -> 3; matrix products, arithmetic and copies ran while one was open for 5% -> 0% of each run, Pallas kernels for 6% -> 21%
where the time goes in v3:
time: 99.1 us; the launch traced here: 98.6 us
  Pallas kernels  42.2 us (43%)
  blocking collectives  25.2 us (25%)
  starting transfers between devices  16.9 us (17%)
  waiting for transfers between devices  12.2 us (12%)
  local copies, waits for them, and re-layouts  1.98 us (2%)
    pallas_call x2, Pallas kernels, pick(): pl.pallas_call(functools.partial(pick_kernel, far=far), out_shape=jax.Sha...  35.8 us
    all_to_all x1, blocking collectives, local(): lax.all_to_all(sums, ('half', 'near'), split_axis=0, concat_axis=0, tiled...  13.6 us
    all_to_all x1, blocking collectives, local(): lax.all_to_all(message[:, None], ('row', 'near'), split_axis=0, concat_ax...  11.6 us
    ppermute x1, waiting for transfers between devices, local(): far_blocks = lax.ppermute(prolong_blocks, 'half', swap)  9.57 us
    all_to_all x1, starting transfers between devices, local(): lax.all_to_all(pick(table, far_blocks, 1), ('row', 'near'), split_axis=0,...  7.87 us
    all_to_all x1, starting transfers between devices, local(): lax.all_to_all(pick(table, prolong_blocks, 0), ('row', 'near'), split_axi...  3.71 us
    ppermute x1, starting transfers between devices, local(): far_blocks = lax.ppermute(prolong_blocks, 'half', swap)  2.65 us
    ppermute x1, starting transfers between devices, local(): far_table = lax.ppermute(table, 'half', swap)  2.62 us
  transfers between devices with their start and end apart: 4, of which 3 were waited for; matrix products, arithmetic and copies ran while one was open for 0% of the time, Pallas kernels for 21%

profile of v3, /device:TPU:0, one launch (start us, length us, event | category | flops | bytes accessed | tf_op | source)
XLA Modules:
  0.0 98.6 jit_solution(14064082802315413002)
XLA Ops:
  0.0 1.6 %build_message.1 = s32[16,128]{1,0:T(8,128)} custom-call(s32[1]{0:T(128)} %bitcast.half_ref, s32[4,8]{1,0:T(4,128)} %bitcast.16, s32[2,8]{1,0:T(2,128)} %bitcast.21), custom_call_target="tpu_custom_call" | custom-call | bytes 16384 | tf_op jit(solution)/shard_map/build_message/pallas_call | solution.py:91
  1.6 11.6 %all_to_all.20 = s32[16,1,128]{2,1,0:T(1,128)} all-to-all(s32[16,1,128]{2,1,0:T(1,128)} %bitcast.20), channel_id=1, replica_groups=mesh['row'=4,'half'=2,'near'=4] {'row','near'}, dimensions={0} | all-to-all | bytes 16384 | tf_op jit(solution)/shard_map/all_to_all | solution.py:208
  13.2 17.9 %pick_near.1 = f32[16,64,128]{2,1,0:T(8,128)} custom-call(s32[16,128]{1,0:T(8,128)} %bitcast.12, f32[8,64,128]{2,1,0:T(8,128)} %blocks_ref.1), custom_call_target="tpu_custom_call" | custom-call | bytes 1048576 | tf_op jit(solution)/shard_map/pick_near/pallas_call | solution.py:121
  31.1 0.0 copy-start.8
  31.1 0.0 copy-start.1
  31.1 0.0 copy-start.4
  31.2 0.0 copy-start.5
  31.2 3.7 %all-to-all-start.2 = ((f32[16,64,128]{2,1,0:T(8,128)}), f32[16,64,128]{2,1,0:T(8,128)S(1)}, u32[]{:S(2)}, u32[]{:S(2)}) async-start(f32[16,64,128]{2,1,0:T(8,128)} %pick_near.1), calls=%async_computation.2 | async-start | bytes 1048576 | tf_op jit(solution)/shard_map/all_to_all | solution.py:210
  34.9 2.7 %collective-permute-start.1 = (f32[8,64,128]{2,1,0:T(8,128)S(1)}, f32[8,64,128]{2,1,0:T(8,128)S(1)}, u32[]{:S(2)}, u32[]{:S(2)}) collective-permute-start(f32[8,64,128]{2,1,0:T(8,128)S(1)} %copy-done.6), channel_id=1, source_target_pairs={{0,4},{4,0},{1,5},{5,1},{2,6},{6,2},{3,7},{7,3},{8,12},{12,8},{9,1... | collective-permute-start | bytes 786440 | tf_op jit(solution)/shard_map/ppermute | solution.py:206
  37.6 9.6 %collective-permute-done.1.blocks_ref = f32[8,64,128]{2,1,0:T(8,128)S(1)} collective-permute-done((f32[8,64,128]{2,1,0:T(8,128)S(1)}, f32[8,64,128]{2,1,0:T(8,128)S(1)}, u32[]{:S(2)}, u32[]{:S(2)}) %collective-permute-start.1) | collective-permute-done | bytes 262176 | tf_op jit(solution)/shard_map/ppermute | solution.py:206
  47.1 0.7 copy-done.7
  47.8 17.9 %pick_far.1 = f32[16,64,128]{2,1,0:T(8,128)} custom-call(s32[16,128]{1,0:T(8,128)} %bitcast.13, f32[8,64,128]{2,1,0:T(8,128)} %copy-done.7), custom_call_target="tpu_custom_call" | custom-call | bytes 1048576 | tf_op jit(solution)/shard_map/pick_far/pallas_call | solution.py:121
  65.8 7.9 %all-to-all-start.1 = ((f32[16,64,128]{2,1,0:T(8,128)}), f32[16,64,128]{2,1,0:T(8,128)S(1)}, u32[]{:S(2)}, u32[]{:S(2)}) async-start(f32[16,64,128]{2,1,0:T(8,128)} %pick_far.1), calls=%async_computation.1 | async-start | bytes 1048576 | tf_op jit(solution)/shard_map/all_to_all | solution.py:211
  73.7 0.0 copy-start.3
  73.7 0.0 copy-start
  73.7 1.2 %copy-done = f32[8,64,512]{2,1,0:T(8,128)S(1)} copy-done((f32[8,64,512]{2,1,0:T(8,128)S(1)}, f32[8,64,512]{2,1,0:T(8,128)}, u32[]{:S(2)}) %copy-start) | copy-done | bytes 1048600
  75.0 1.7 %restrict_operator.1.restricted_ref = bf16[32,192,128]{2,1,0:T(8,128)(2,1)S(1)} custom-call(s32[8]{0:T(128)S(1)} %copy-done.5, s32[8,8]{1,0:T(8,128)S(1)} %add_select_fusion.slot_ref, s32[2,8]{1,0:T(2,128)S(1)} %bitcast.19, f32[8,64,512]{2,1,0:T(8,128)S(1)} %copy-done, f32[8,64,128]{2,1,0:T(8,128)S(1)} %copy-done.1), custom_call_target="tpu_custom_call" | custom-call | flops 201326592 | bytes 4194304 | tf_op jit(solution)/shard_map/restrict_operator/pallas_call | solution.py:56
  76.7 2.6 %collective-permute-start = (s32[16,128]{1,0:T(8,128)S(1)}, s32[16,128]{1,0:T(8,128)S(1)}, u32[]{:S(2)}, u32[]{:S(2)}) collective-permute-start(s32[16,128]{1,0:T(8,128)S(1)} %bitcast.14), channel_id=1, source_target_pairs={{0,4},{4,0},{1,5},{5,1},{2,6},{6,2},{3,7},{7,3},{8,12},{12,8},{9,1... | collective-permute-start | bytes 24584 | tf_op jit(solution)/shard_map/ppermute | solution.py:209
  79.3 1.2 %combine_near.1.rest_0_ = f32[8,64,128]{2,1,0:T(8,128)S(1)} custom-call(s32[1]{0:T(128)} %bitcast.half_ref, s32[4,8]{1,0:T(4,128)S(1)} %bitcast.17, s32[16,128]{1,0:T(8,128)S(1)} %bitcast.15, bf16[32,192,128]{2,1,0:T(8,128)(2,1)S(1)} %restrict_operator.1.restricted_ref, f32[16,64,128]{2,1,0:T(8,128)S(1)} %all-to-all-done.2.blocks_ref), custom_call_target="tpu_custom_call" | custom-call | flops 134217728 | bytes 2097152 | tf_op jit(solution)/shard_map/combine_near/pallas_call | solution.py:159
  80.5 0.8 collective-permute-done.table_ref
  81.3 1.8 %all-to-all-done.1.blocks_ref = f32[16,64,128]{2,1,0:T(8,128)S(1)} async-done(((f32[16,64,128]{2,1,0:T(8,128)}), f32[16,64,128]{2,1,0:T(8,128)S(1)}, u32[]{:S(2)}, u32[]{:S(2)}) %all-to-all-start.1) | async-done | bytes 524320 | tf_op jit(solution)/shard_map/all_to_all | solution.py:211
  83.1 1.2 %combine_far.1 = f32[8,64,128]{2,1,0:T(8,128)S(1)} custom-call(s32[1]{0:T(128)} %bitcast.half_ref, s32[4,8]{1,0:T(4,128)S(1)} %bitcast.18, s32[16,128]{1,0:T(8,128)S(1)} %collective-permute-done.table_ref, bf16[32,192,128]{2,1,0:T(8,128)(2,1)S(1)} %restrict_operator.1.restricted_ref, f32[16,64,128]{2,1,0:T(8,128)S(1)} %all-to-all-done.1.blocks_ref, ...), custom_call_target="tpu_custom_call" | custom-call | flops 134217728 | bytes 2097152 | tf_op jit(solution)/shard_map/combine_far/pallas_call | solution.py:159
  84.3 13.6 %all_to_all.21.parts_ref = f32[8,64,128]{2,1,0:T(8,128)S(1)} all-to-all(f32[8,64,128]{2,1,0:T(8,128)S(1)} %combine_far.1), channel_id=1, replica_groups=mesh['row'=4,'half'=2,'near'=4] {'half','near'}, dimensions={0} | all-to-all | bytes 524288 | tf_op jit(solution)/shard_map/all_to_all | solution.py:220
  97.9 0.6 add_up.1
  (12 shorter events, 0.0 us)
Async XLA Ops:
  0.0 34.9 %copy-start.6 = (f32[8,64,128]{2,1,0:T(8,128)S(1)}, f32[8,64,128]{2,1,0:T(8,128)}, u32[]{:S(2)}) copy-start(f32[8,64,128]{2,1,0:T(8,128)} %blocks_ref.1) | copy-start | bytes 786436
  31.1 42.6 %copy-start.8 = (s32[8,8]{1,0:T(8,128)S(1)}, s32[8,8]{1,0:T(8,128)}, u32[]{:S(2)}) copy-start(s32[8,8]{1,0:T(8,128)} %param.10) | copy-start | bytes 772
  31.1 42.6 %copy-start.1 = (f32[8,64,128]{2,1,0:T(8,128)S(1)}, f32[8,64,128]{2,1,0:T(8,128)}, u32[]{:S(2)}) copy-start(f32[8,64,128]{2,1,0:T(8,128)} %restrict_ref.1) | copy-start | bytes 786436
  31.1 42.6 %copy-start.4 = (s32[8,2]{0,1:T(2,128)S(1)}, s32[8,2]{0,1:T(2,128)}, u32[]{:S(2)}) copy-start(s32[8,2]{0,1:T(2,128)} %param.15) | copy-start | bytes 196
  31.2 42.6 %copy-start.5 = (s32[8]{0:T(128)S(1)}, s32[8]{0:T(128)}, u32[]{:S(2)}) copy-start(s32[8]{0:T(128)} %count_ref.1) | copy-start | bytes 100
  31.2 34.6 %all-to-all-start.2 = ((f32[16,64,128]{2,1,0:T(8,128)}), f32[16,64,128]{2,1,0:T(8,128)S(1)}, u32[]{:S(2)}, u32[]{:S(2)}) async-start(f32[16,64,128]{2,1,0:T(8,128)} %pick_near.1), calls=%async_computation.2 | async-start | bytes 1048576 | tf_op jit(solution)/shard_map/all_to_all | solution.py:210
  34.9 12.2 %collective-permute-start.1 = (f32[8,64,128]{2,1,0:T(8,128)S(1)}, f32[8,64,128]{2,1,0:T(8,128)S(1)}, u32[]{:S(2)}, u32[]{:S(2)}) collective-permute-start(f32[8,64,128]{2,1,0:T(8,128)S(1)} %copy-done.6), channel_id=1, source_target_pairs={{0,4},{4,0},{1,5},{5,1},{2,6},{6,2},{3,7},{7,3},{8,12},{12,8},{9,1... | collective-permute-start | bytes 786440 | tf_op jit(solution)/shard_map/ppermute | solution.py:206
  47.1 0.7 copy-start.7
  65.8 17.3 %all-to-all-start.1 = ((f32[16,64,128]{2,1,0:T(8,128)}), f32[16,64,128]{2,1,0:T(8,128)S(1)}, u32[]{:S(2)}, u32[]{:S(2)}) async-start(f32[16,64,128]{2,1,0:T(8,128)} %pick_far.1), calls=%async_computation.1 | async-start | bytes 1048576 | tf_op jit(solution)/shard_map/all_to_all | solution.py:211
  73.7 3.0 %copy-start.2 = (s32[16,1,128]{2,1,0:T(1,128)S(1)}, s32[16,1,128]{2,1,0:T(1,128)}, u32[]{:S(2)}) copy-start(s32[16,1,128]{2,1,0:T(1,128)} %all_to_all.20) | copy-start | bytes 24580
  73.7 5.7 %copy-start.3 = (s32[1,1,8,4]{2,3,1,0:T(4,128)S(1)}, s32[1,1,8,4]{2,3,1,0:T(4,128)}, u32[]{:S(2)}) copy-start(s32[1,1,8,4]{2,3,1,0:T(4,128)} %param.11) | copy-start | bytes 388
  73.7 1.2 %copy-start = (f32[8,64,512]{2,1,0:T(8,128)S(1)}, f32[8,64,512]{2,1,0:T(8,128)}, u32[]{:S(2)}) copy-start(f32[8,64,512]{2,1,0:T(8,128)} %operator_ref.1) | copy-start | bytes 3145732
  76.7 4.6 %collective-permute-start = (s32[16,128]{1,0:T(8,128)S(1)}, s32[16,128]{1,0:T(8,128)S(1)}, u32[]{:S(2)}, u32[]{:S(2)}) collective-permute-start(s32[16,128]{1,0:T(8,128)S(1)} %bitcast.14), channel_id=1, source_target_pairs={{0,4},{4,0},{1,5},{5,1},{2,6},{6,2},{3,7},{7,3},{8,12},{12,8},{9,1... | collective-permute-start | bytes 24584 | tf_op jit(solution)/shard_map/ppermute | solution.py:209

commit v4 on v1

v4 whole, which is shorter than its diff:
```python
import functools

import jax
import jax.numpy as jnp
from jax import lax
from jax.experimental import pallas as pl
from jax.experimental.pallas import tpu as pltpu
from jax.sharding import Mesh
from jax.sharding import PartitionSpec as P

NCR = 2
LANES = 128
EXTRA = 8
VMEM_LIMIT = 48 * 1024 * 1024


def split3(x, order):
    high = x.astype(jnp.bfloat16)
    low = (x - high.astype(jnp.float32)).astype(jnp.bfloat16)
    parts = {"left": (high, low, high), "right": (high, high, low)}[order]
    return jnp.concatenate(parts, axis=0)


def transposed_dot(left, right):
    return lax.dot_general(left, right, (((0,), (0,)), ((), ())), preferred_element_type=jnp.float32)


def extend_kernel(columns_ref, blocks_ref, out_ref):
    fine_rows, block_size, width = blocks_ref.shape
    entries = columns_ref.shape[0]
    used = fine_rows * block_size
    out_ref[:used] = blocks_ref[...].reshape(used, width)
    lane = lax.broadcasted_iota(jnp.int32, (EXTRA, width), 1)
    value = jnp.zeros((EXTRA, width), jnp.int32)
    for i in range(fine_rows):
        for m in range(entries):
            value = jnp.where(lane == entries * i + m, columns_ref[m, i], value)
    out_ref[used:] = value.astype(jnp.float32)


def extend(columns, blocks):
    fine_rows, block_size, width = blocks.shape
    return pl.pallas_call(
        extend_kernel,
        out_shape=jax.ShapeDtypeStruct((fine_rows * block_size + EXTRA, width), blocks.dtype),
        in_specs=[pl.BlockSpec(memory_space=pltpu.SMEM), pl.BlockSpec(memory_space=pltpu.VMEM)],
        out_specs=pl.BlockSpec(memory_space=pltpu.VMEM),
        cost_estimate=pl.CostEstimate(flops=0, bytes_accessed=1 << 19, transcendentals=0),
        name="extend",
    )(columns, blocks)


def restrict_kernel(count_ref, slot_ref, rows_ref, fetch_ref, operator_ref, restrict_ref, out_ref):
    fine_rows, block_size, _ = operator_ref.shape
    entries = slot_ref.shape[1]
    slot_count, columns = fetch_ref.shape
    half = columns // 2
    used = 2 * slot_count * block_size
    wide = NCR * block_size
    lane = lax.broadcasted_iota(jnp.int32, (block_size, wide), 1)
    second = (lane >= block_size).astype(jnp.int32)
    short_lane = lax.broadcasted_iota(jnp.int32, (EXTRA, wide), 1)

    for near in range(half):
        out_ref[near, :used] = jnp.zeros((used, wide), jnp.float32)
        value = jnp.zeros((EXTRA, wide), jnp.int32)
        for side in range(2):
            for s in range(slot_count):
                wanted = fetch_ref[s, side * half + near]
                value = jnp.where(short_lane == side * slot_count + s, wanted, value)
        out_ref[near, used:] = value.astype(jnp.float32)

    for i in range(fine_rows):
        value = restrict_ref[i]
        swapped = pltpu.roll(value, block_size, 1)
        own_row = jnp.where(second == 0, rows_ref[0, i], rows_ref[1, i])
        other_row = jnp.where(second == 0, rows_ref[1, i], rows_ref[0, i])
        dense = jnp.where(own_row == second, value, 0.0) + jnp.where(other_row == second, swapped, 0.0)
        product = transposed_dot(split3(operator_ref[i], "left"), split3(dense, "right"))
        for k in range(entries):
            part = jnp.where(k < count_ref[i], product[k * block_size : (k + 1) * block_size], 0.0)
            peer = lax.div(slot_ref[i, k], slot_count)
            place = lax.div(peer, half) * slot_count + lax.rem(slot_ref[i, k], slot_count)
            start = pl.multiple_of(place * block_size, block_size)
            out_ref[lax.rem(peer, half), pl.ds(start, block_size)] += part


def restrict_operator(operator_count, operator_slot, restrict_rows, fetch, operator_blocks, restrict_blocks):
    fine_rows, block_size, width = operator_blocks.shape
    slot_count, columns = fetch.shape
    wide = NCR * block_size
    rows = 2 * slot_count * block_size + EXTRA
    return pl.pallas_call(
        restrict_kernel,
        out_shape=jax.ShapeDtypeStruct((columns // 2, rows, wide), jnp.float32),
        in_specs=[pl.BlockSpec(memory_space=pltpu.SMEM)] * 4 + [pl.BlockSpec(memory_space=pltpu.VMEM)] * 2,
        out_specs=pl.BlockSpec(memory_space=pltpu.VMEM),
        compiler_params=pltpu.CompilerParams(vmem_limit_bytes=VMEM_LIMIT),
        cost_estimate=pl.CostEstimate(
            flops=6 * fine_rows * block_size * width * wide, bytes_accessed=4 << 20, transcendentals=0
        ),
        name="restrict_operator",
    )(operator_count, operator_slot, restrict_rows, fetch, operator_blocks, restrict_blocks)


def combine_kernel(own_ref, restricted_ref, *rest, slot_count, fine_rows, entries):
    pieces, (out_ref, held_ref, table_ref, index_ref, sem) = rest[:-5], rest[-5:]
    half = restricted_ref.shape[0]
    block_size = out_ref.shape[1]
    rows = len(pieces) // 2
    columns = 2 * half
    used = 2 * slot_count * block_size
    held = fine_rows * block_size

    table_ref[...] = jnp.zeros_like(table_ref)
    for near in range(half):
        table_ref[near : near + 1] = restricted_ref[near, used : used + 1].astype(jnp.int32)
    for i, piece in enumerate(pieces):
        table_ref[half + i : half + i + 1] = piece[held : held + 1].astype(jnp.int32)
    copy = pltpu.make_async_copy(table_ref, index_ref, sem)
    copy.start()
    for i, piece in enumerate(pieces):
        held_ref[i] = piece[:held]
    out_ref[...] = jnp.zeros_like(out_ref)
    copy.wait()

    def step(i, carry):
        near = lax.div(i, 2 * slot_count)
        place = lax.rem(i, 2 * slot_count)
        wanted = index_ref[near, place]
        far = lax.div(place, slot_count) ^ own_ref[1]
        inside = lax.rem(wanted, fine_rows)
        piece = far * rows + (lax.div(wanted, fine_rows * columns) ^ own_ref[0])
        block = held_ref[piece, pl.ds(pl.multiple_of(inside * block_size, block_size), block_size)]
        restricted = restricted_ref[near, pl.ds(pl.multiple_of(place * block_size, block_size), block_size)]
        product = transposed_dot(split3(block, "left"), split3(restricted, "right"))
        for m in range(entries):
            column = index_ref[half + piece, entries * inside + m]
            out_ref[column] += product[m * block_size : (m + 1) * block_size]
        return carry

    lax.fori_loop(0, half * 2 * slot_count, step, 0, unroll=16)


def combine(own, restricted, pieces, coarse_all, block_size, slot_count, fine_rows, entries):
    half, _, wide = restricted.shape
    table_rows = -(-(half + len(pieces)) // 8) * 8
    return pl.pallas_call(
        functools.partial(combine_kernel, slot_count=slot_count, fine_rows=fine_rows, entries=entries),
        out_shape=jax.ShapeDtypeStruct((coarse_all, block_size, wide), jnp.float32),
        in_specs=[pl.BlockSpec(memory_space=pltpu.SMEM)]
        + [pl.BlockSpec(memory_space=pltpu.VMEM)] * (1 + len(pieces)),
        out_specs=pl.BlockSpec(memory_space=pltpu.VMEM),
        scratch_shapes=[
            pltpu.VMEM((len(pieces), fine_rows * block_size, entries * block_size), jnp.float32),
            pltpu.VMEM((table_rows, LANES), jnp.int32),
            pltpu.SMEM((table_rows, LANES), jnp.int32),
            pltpu.SemaphoreType.DMA,
        ],
        compiler_params=pltpu.CompilerParams(vmem_limit_bytes=VMEM_LIMIT),
        cost_estimate=pl.CostEstimate(flops=1 << 28, bytes_accessed=4 << 20, transcendentals=0),
        name="combine",
    )(own, restricted, *pieces)


def add_kernel(parts_ref, out_ref):
    total = parts_ref[0]
    for i in range(1, parts_ref.shape[0]):
        total = total + parts_ref[i]
    out_ref[...] = total


def add_up(parts):
    return pl.pallas_call(
        add_kernel,
        out_shape=jax.ShapeDtypeStruct(parts.shape[1:], parts.dtype),
        in_specs=[pl.BlockSpec(memory_space=pltpu.VMEM)],
        out_specs=pl.BlockSpec(memory_space=pltpu.VMEM),
        compiler_params=pltpu.CompilerParams(vmem_limit_bytes=VMEM_LIMIT),
        name="add_up",
    )(parts)


def spread_over_rows(blocks, rows):
    pieces = {0: blocks}
    bit = rows // 2
    while bit:
        for mask in list(pieces):
            pieces[mask ^ bit] = lax.ppermute(pieces[mask], "row", [(r, r ^ bit) for r in range(rows)])
        bit //= 2
    return [pieces[mask] for mask in range(rows)]


def local(
    operator_blocks,
    operator_count,
    operator_slot,
    fetch_lists,
    prolong_blocks,
    prolong_cols,
    restrict_blocks,
    restrict_rows,
):
    fine_rows, block_size, _ = operator_blocks.shape
    entries = prolong_cols.shape[1]
    rows, half = lax.axis_size("row"), lax.axis_size("near")
    slot_count = fetch_lists.shape[3]
    fetch = fetch_lists.reshape(2 * half, slot_count).T
    own = jnp.stack([lax.axis_index("row"), lax.axis_index("half")])

    near_blocks = extend(prolong_cols.T, prolong_blocks)
    far_blocks = lax.ppermute(near_blocks, "half", [(0, 1), (1, 0)])
    restricted = restrict_operator(
        operator_count, operator_slot, restrict_rows.T, fetch, operator_blocks, restrict_blocks
    )
    restricted = lax.all_to_all(restricted, "near", split_axis=0, concat_axis=0, tiled=True)
    pieces = spread_over_rows(near_blocks, rows) + spread_over_rows(far_blocks, rows)
    sums = combine(own, restricted, pieces, NCR * rows, block_size, slot_count, fine_rows, entries)
    parts = lax.all_to_all(sums, ("half", "near"), split_axis=0, concat_axis=0, tiled=True)
    return add_up(parts).T


def solution(mesh):
    rows, columns = mesh.shape["row"], mesh.shape["col"]
    split = Mesh(mesh.devices.reshape(rows, 2, columns // 2), ("row", "half", "near"))
    flat = ("row", "half", "near")
    return jax.shard_map(
        local,
        mesh=split,
        in_specs=(
            P(flat, None, None),
            P(flat),
            P(flat, None),
            P("row", ("half", "near"), None, None),
            P(flat, None, None),
            P(flat, None),
            P(flat, None, None),
            P(flat, None),
        ),
        out_specs=P("row", ("half", "near")),
        check_vma=False,
    )
```

time: 64 us -> 58.8 us (0.919)
  blocking collectives: 25.7 us -> 15.6 us
  starting transfers between devices: 2.64 us -> 11.4 us
  waiting for transfers between devices: 24.4 us -> 18.3 us
  local copies, waits for them, and re-layouts: 4.05 us -> 5.83 us
  Pallas kernels: 6.07 us -> 7.23 us
  other arithmetic: 0.72 us -> 0.07 us
    all_to_all x1, waiting for transfers between devices: 24.4 us -> 0.01 us  [local(): lax.all_to_all(restricted, 'near', split_axis=0, concat_axis=0, tiled=True)]
    ppermute x0 -> x7, waiting for transfers between devices: none -> 18.3 us  [the longest x1 11.6 us: local(): far_blocks = lax.ppermute(near_blocks, 'half', [(0, 1), (1, 0)])]
    all_to_all x2 -> x1, blocking collectives: 25.7 us -> 15.6 us  [local(): lax.all_to_all(sums, ('half', 'near'), split_axis=0, concat_axis=0, tiled...]
    ppermute x0 -> x7, starting transfers between devices: none -> 6.16 us  [the longest x6 3.58 us: spread_over_rows(): lax.ppermute(pieces[mask], 'row', [(r, r ^ bit) for r in range(rows)])]
    unnamed x16 -> x14, local copies, waits for them, and re-layouts: 3.03 us -> 5.83 us
    all_to_all x1, starting transfers between devices: 2.64 us -> 5.22 us  [local(): lax.all_to_all(restricted, 'near', split_axis=0, concat_axis=0, tiled=True)]
    pallas_call x4, Pallas kernels: 6.07 us -> 7.23 us  [the longest x1 2.61 us: restrict_operator(): pl.pallas_call(restrict_kernel, out_shape=jax.ShapeDtypeStruct((columns /...]
    pallas_call x1 -> x0, local copies, waits for them, and re-layouts: 0.7 us -> none  [add_up(): pl.pallas_call(add_kernel, out_shape=jax.ShapeDtypeStruct((parts.shape[2]...]
  transfers between devices with their start and end apart: 1 -> 8, of which waited for: 1 -> 3; matrix products, arithmetic and copies ran while one was open for 0% -> 0% of each run, Pallas kernels for 3% -> 3%
where the time goes in v4:
time: 58.8 us; the launch traced here: 58.4 us
  waiting for transfers between devices  18.3 us (31%)
  blocking collectives  15.6 us (27%)
  starting transfers between devices  11.4 us (19%)
  Pallas kernels  7.23 us (12%)
  local copies, waits for them, and re-layouts  5.83 us (10%)
    all_to_all x1, blocking collectives, local(): lax.all_to_all(sums, ('half', 'near'), split_axis=0, concat_axis=0, tiled...  15.6 us
    ppermute x1, waiting for transfers between devices, local(): far_blocks = lax.ppermute(near_blocks, 'half', [(0, 1), (1, 0)])  11.6 us
    ppermute x6, waiting for transfers between devices, spread_over_rows(): lax.ppermute(pieces[mask], 'row', [(r, r ^ bit) for r in range(rows)])  6.65 us
    unnamed x14, local copies, waits for them, and re-layouts  5.83 us
    all_to_all x1, starting transfers between devices, local(): lax.all_to_all(restricted, 'near', split_axis=0, concat_axis=0, tiled=True)  5.22 us
    ppermute x6, starting transfers between devices, spread_over_rows(): lax.ppermute(pieces[mask], 'row', [(r, r ^ bit) for r in range(rows)])  3.58 us
    pallas_call x1, Pallas kernels, restrict_operator(): pl.pallas_call(restrict_kernel, out_shape=jax.ShapeDtypeStruct((columns /...  2.61 us
    ppermute x1, starting transfers between devices, local(): far_blocks = lax.ppermute(near_blocks, 'half', [(0, 1), (1, 0)])  2.58 us
  transfers between devices with their start and end apart: 8, of which 3 were waited for; matrix products, arithmetic and copies ran while one was open for 0% of the time, Pallas kernels for 3%

profile of v4, /device:TPU:0, one launch (start us, length us, event | category | flops | bytes accessed | tf_op | source)
XLA Modules:
  0.0 58.4 jit_solution(16055092823279375584)
XLA Ops:
  0.0 1.2 %copy-done.1 = f32[8,64,512]{2,1,0:T(8,128)S(1)} copy-done((f32[8,64,512]{2,1,0:T(8,128)S(1)}, f32[8,64,512]{2,1,0:T(8,128)}, u32[]{:S(2)}) %copy-start.1) | copy-done | bytes 1048600
  1.2 0.9 %copy-done.2 = f32[8,64,128]{2,1,0:T(8,128)S(1)} copy-done((f32[8,64,128]{2,1,0:T(8,128)S(1)}, f32[8,64,128]{2,1,0:T(8,128)}, u32[]{:S(2)}) %copy-start.2) | copy-done | bytes 262168
  2.2 0.7 %copy-done.3 = s32[8,8]{1,0:T(8,128)S(1)} copy-done((s32[8,8]{1,0:T(8,128)S(1)}, s32[8,8]{1,0:T(8,128)}, u32[]{:S(2)}) %copy-start.3) | copy-done | bytes 280
  2.9 0.7 %copy-done.4 = s32[1,1,8,4]{2,3,1,0:T(4,128)S(1)} copy-done((s32[1,1,8,4]{2,3,1,0:T(4,128)S(1)}, s32[1,1,8,4]{2,3,1,0:T(4,128)}, u32[]{:S(2)}) %copy-start.4) | copy-done | bytes 152
  3.5 0.7 %copy-done.5 = s32[8,2]{0,1:T(2,128)S(1)} copy-done((s32[8,2]{0,1:T(2,128)S(1)}, s32[8,2]{0,1:T(2,128)}, u32[]{:S(2)}) %copy-start.5) | copy-done | bytes 88
  4.2 0.7 %copy-done.6 = s32[8]{0:T(128)S(1)} copy-done((s32[8]{0:T(128)S(1)}, s32[8]{0:T(128)}, u32[]{:S(2)}) %copy-start.6) | copy-done | bytes 56
  4.9 2.6 %restrict_operator.1 = f32[4,520,128]{2,1,0:T(8,128)} custom-call(s32[8]{0:T(128)S(1)} %copy-done.6, s32[8,8]{1,0:T(8,128)S(1)} %copy-done.3, s32[2,8]{1,0:T(2,128)S(1)} %bitcast.9, s32[4,8]{1,0:T(4,128)S(1)} %bitcast.8, f32[8,64,512]{2,1,0:T(8,128)S(1)} %copy-done.1, f32[8,64,128]{2,1,0:T(8,128)S(1)} %copy-done.2), custom_call_target="tpu_custom_call" | custom-call | flops 201326592 | bytes 4194304 | tf_op jit(solution)/shard_map/restrict_operator/pallas_call | solution.py:93
  7.5 5.2 %all-to-all-start = ((f32[4,520,128]{2,1,0:T(8,128)}), f32[4,520,128]{2,1,0:T(8,128)S(1)}, u32[]{:S(2)}, u32[]{:S(2)}) async-start(f32[4,520,128]{2,1,0:T(8,128)} %restrict_operator.1), calls=%async_computation | async-start | bytes 2129920 | tf_op jit(solution)/shard_map/all_to_all | solution.py:216
  12.7 1.7 %extend.1.rest_0_ = f32[520,128]{1,0:T(8,128)} custom-call(s32[2,8]{1,0:T(2,128)} %bitcast.10, f32[8,64,128]{2,1,0:T(8,128)} %blocks_ref.1), custom_call_target="tpu_custom_call" | custom-call | bytes 524288 | tf_op jit(solution)/shard_map/extend/pallas_call | solution.py:43
  14.4 2.6 %collective-permute-start.3 = (f32[520,128]{1,0:T(8,128)}, f32[520,128]{1,0:T(8,128)S(1)}, u32[]{:S(2)}, u32[]{:S(2)}) collective-permute-start(f32[520,128]{1,0:T(8,128)} %extend.1.rest_0_), channel_id=1, source_target_pairs={{0,4},{4,0},{1,5},{5,1},{2,6},{6,2},{3,7},{7,3},{8,12},{12,8},{9,1... | collective-permute-start | bytes 798728 | tf_op jit(solution)/shard_map/ppermute | solution.py:212
  17.0 1.5 %collective-permute-start.1 = (f32[520,128]{1,0:T(8,128)}, f32[520,128]{1,0:T(8,128)S(1)}, u32[]{:S(2)}, u32[]{:S(2)}) collective-permute-start(f32[520,128]{1,0:T(8,128)} %extend.1.rest_0_), channel_id=1, source_target_pairs={{0,16},{8,24},{16,0},{24,8},{1,17},{9,25},{17,1},{25,9},{2,18},{10... | collective-permute-start | bytes 798728 | tf_op jit(solution)/shard_map/ppermute | solution.py:189
  18.5 11.6 %collective-permute-done.3.rest_4_ = f32[520,128]{1,0:T(8,128)S(1)} collective-permute-done((f32[520,128]{1,0:T(8,128)}, f32[520,128]{1,0:T(8,128)S(1)}, u32[]{:S(2)}, u32[]{:S(2)}) %collective-permute-start.3) | collective-permute-done | bytes 266272 | tf_op jit(solution)/shard_map/ppermute | solution.py:212
  30.1 1.5 %collective-permute-start.5 = (f32[520,128]{1,0:T(8,128)S(1)}, f32[520,128]{1,0:T(8,128)S(1)}, u32[]{:S(2)}, u32[]{:S(2)}) collective-permute-start(f32[520,128]{1,0:T(8,128)S(1)} %collective-permute-done.3.rest_4_), channel_id=1, source_target_pairs={{0,16},{8,24},{16,0},{24,8},{1,17},{9,25},{17,1},{25,9},{2,18},{10... | collective-permute-start | bytes 798728 | tf_op jit(solution)/shard_map/ppermute | solution.py:189
  31.7 0.0 collective-permute-start
  31.7 0.5 collective-permute-start.4
  32.2 0.0 collective-permute-start.2
  32.2 5.2 %collective-permute-done.5.rest_6_ = f32[520,128]{1,0:T(8,128)S(1)} collective-permute-done((f32[520,128]{1,0:T(8,128)S(1)}, f32[520,128]{1,0:T(8,128)S(1)}, u32[]{:S(2)}, u32[]{:S(2)}) %collective-permute-start.5) | collective-permute-done | bytes 266272 | tf_op jit(solution)/shard_map/ppermute | solution.py:189
  37.4 0.1 pad_add_fusion.own_ref
  37.5 1.4 %collective-permute-done.6.rest_7_ = f32[520,128]{1,0:T(8,128)S(1)} collective-permute-done((f32[520,128]{1,0:T(8,128)S(1)}, f32[520,128]{1,0:T(8,128)S(1)}, u32[]{:S(2)}, u32[]{:S(2)}) %collective-permute-start.6) | collective-permute-done | bytes 266272 | tf_op jit(solution)/shard_map/ppermute | solution.py:189
  38.9 0.0 all-to-all-done.restricted_ref
  38.9 1.0 %copy-done = f32[520,128]{1,0:T(8,128)S(1)} copy-done((f32[520,128]{1,0:T(8,128)S(1)}, f32[520,128]{1,0:T(8,128)}, u32[]{:S(2)}) %copy-start) | copy-done | bytes 266264
  39.9 2.3 %combine.1 = f32[8,64,128]{2,1,0:T(8,128)S(1)} custom-call(s32[2]{0:T(128)S(1)} %pad_add_fusion.own_ref, f32[4,520,128]{2,1,0:T(8,128)S(1)} %all-to-all-done.restricted_ref, f32[520,128]{1,0:T(8,128)S(1)} %copy-done, f32[520,128]{1,0:T(8,128)S(1)} %collective-permute-done.rest_1_, f32[520,128]{1,0:T(8,128)S(1)} %collective-permute-done.1.rest_2_, ...), custom_call_target="tpu_custom_call" | custom-call | flops 268435456 | bytes 4194304 | tf_op jit(solution)/shard_map/combine/pallas_call | solution.py:148
  42.2 15.6 %all_to_all.10.parts_ref = f32[8,64,128]{2,1,0:T(8,128)S(1)} all-to-all(f32[8,64,128]{2,1,0:T(8,128)S(1)} %combine.1), channel_id=1, replica_groups=mesh['row'=4,'half'=2,'near'=4] {'half','near'}, dimensions={0} | all-to-all | bytes 524288 | tf_op jit(solution)/shard_map/all_to_all | solution.py:219
  57.8 0.6 %add_up.1 = f32[64,128]{1,0:T(8,128)} custom-call(f32[8,64,128]{2,1,0:T(8,128)S(1)} %all_to_all.10.parts_ref), custom_call_target="tpu_custom_call" | custom-call | tf_op jit(solution)/shard_map/add_up/pallas_call | solution.py:174
  (12 shorter events, 0.0 us)
Async XLA Ops:
  0.0 1.2 %copy-start.1 = (f32[8,64,512]{2,1,0:T(8,128)S(1)}, f32[8,64,512]{2,1,0:T(8,128)}, u32[]{:S(2)}) copy-start(f32[8,64,512]{2,1,0:T(8,128)} %operator_ref.1) | copy-start | bytes 3145732
  1.2 0.9 %copy-start.2 = (f32[8,64,128]{2,1,0:T(8,128)S(1)}, f32[8,64,128]{2,1,0:T(8,128)}, u32[]{:S(2)}) copy-start(f32[8,64,128]{2,1,0:T(8,128)} %restrict_ref.1) | copy-start | bytes 786436
  2.2 0.7 %copy-start.3 = (s32[8,8]{1,0:T(8,128)S(1)}, s32[8,8]{1,0:T(8,128)}, u32[]{:S(2)}) copy-start(s32[8,8]{1,0:T(8,128)} %slot_ref.1) | copy-start | bytes 772
  2.9 0.7 %copy-start.4 = (s32[1,1,8,4]{2,3,1,0:T(4,128)S(1)}, s32[1,1,8,4]{2,3,1,0:T(4,128)}, u32[]{:S(2)}) copy-start(s32[1,1,8,4]{2,3,1,0:T(4,128)} %param.11) | copy-start | bytes 388
  3.5 0.7 %copy-start.5 = (s32[8,2]{0,1:T(2,128)S(1)}, s32[8,2]{0,1:T(2,128)}, u32[]{:S(2)}) copy-start(s32[8,2]{0,1:T(2,128)} %param.15) | copy-start | bytes 196
  4.2 0.7 %copy-start.6 = (s32[8]{0:T(128)S(1)}, s32[8]{0:T(128)}, u32[]{:S(2)}) copy-start(s32[8]{0:T(128)} %count_ref.1) | copy-start | bytes 100
  7.5 31.4 %all-to-all-start = ((f32[4,520,128]{2,1,0:T(8,128)}), f32[4,520,128]{2,1,0:T(8,128)S(1)}, u32[]{:S(2)}, u32[]{:S(2)}) async-start(f32[4,520,128]{2,1,0:T(8,128)} %restrict_operator.1), calls=%async_computation | async-start | bytes 2129920 | tf_op jit(solution)/shard_map/all_to_all | solution.py:216
  14.4 15.7 %collective-permute-start.3 = (f32[520,128]{1,0:T(8,128)}, f32[520,128]{1,0:T(8,128)S(1)}, u32[]{:S(2)}, u32[]{:S(2)}) collective-permute-start(f32[520,128]{1,0:T(8,128)} %extend.1.rest_0_), channel_id=1, source_target_pairs={{0,4},{4,0},{1,5},{5,1},{2,6},{6,2},{3,7},{7,3},{8,12},{12,8},{9,1... | collective-permute-start | bytes 798728 | tf_op jit(solution)/shard_map/ppermute | solution.py:212
  17.0 15.2 %collective-permute-start.1 = (f32[520,128]{1,0:T(8,128)}, f32[520,128]{1,0:T(8,128)S(1)}, u32[]{:S(2)}, u32[]{:S(2)}) collective-permute-start(f32[520,128]{1,0:T(8,128)} %extend.1.rest_0_), channel_id=1, source_target_pairs={{0,16},{8,24},{16,0},{24,8},{1,17},{9,25},{17,1},{25,9},{2,18},{10... | collective-permute-start | bytes 798728 | tf_op jit(solution)/shard_map/ppermute | solution.py:189
  30.1 7.3 %collective-permute-start.5 = (f32[520,128]{1,0:T(8,128)S(1)}, f32[520,128]{1,0:T(8,128)S(1)}, u32[]{:S(2)}, u32[]{:S(2)}) collective-permute-start(f32[520,128]{1,0:T(8,128)S(1)} %collective-permute-done.3.rest_4_), channel_id=1, source_target_pairs={{0,16},{8,24},{16,0},{24,8},{1,17},{9,25},{17,1},{25,9},{2,18},{10... | collective-permute-start | bytes 798728 | tf_op jit(solution)/shard_map/ppermute | solution.py:189
  31.7 5.8 %collective-permute-start = (f32[520,128]{1,0:T(8,128)}, f32[520,128]{1,0:T(8,128)S(1)}, u32[]{:S(2)}, u32[]{:S(2)}) collective-permute-start(f32[520,128]{1,0:T(8,128)} %extend.1.rest_0_), channel_id=1, source_target_pairs={{0,8},{8,0},{16,24},{24,16},{1,9},{9,1},{17,25},{25,17},{2,10},{10... | collective-permute-start | bytes 798728 | tf_op jit(solution)/shard_map/ppermute | solution.py:189
  31.7 5.8 %collective-permute-start.4 = (f32[520,128]{1,0:T(8,128)S(1)}, f32[520,128]{1,0:T(8,128)S(1)}, u32[]{:S(2)}, u32[]{:S(2)}) collective-permute-start(f32[520,128]{1,0:T(8,128)S(1)} %collective-permute-done.3.rest_4_), channel_id=1, source_target_pairs={{0,8},{8,0},{16,24},{24,16},{1,9},{9,1},{17,25},{25,17},{2,10},{10... | collective-permute-start | bytes 798728 | tf_op jit(solution)/shard_map/ppermute | solution.py:189
  32.2 5.3 %collective-permute-start.2 = (f32[520,128]{1,0:T(8,128)S(1)}, f32[520,128]{1,0:T(8,128)S(1)}, u32[]{:S(2)}, u32[]{:S(2)}) collective-permute-start(f32[520,128]{1,0:T(8,128)S(1)} %collective-permute-done.1.rest_2_), channel_id=1, source_target_pairs={{0,8},{8,0},{16,24},{24,16},{1,9},{9,1},{17,25},{25,17},{2,10},{10... | collective-permute-start | bytes 798728 | tf_op jit(solution)/shard_map/ppermute | solution.py:189
  37.4 1.5 %collective-permute-start.6 = (f32[520,128]{1,0:T(8,128)S(1)}, f32[520,128]{1,0:T(8,128)S(1)}, u32[]{:S(2)}, u32[]{:S(2)}) collective-permute-start(f32[520,128]{1,0:T(8,128)S(1)} %collective-permute-done.5.rest_6_), channel_id=1, source_target_pairs={{0,8},{8,0},{16,24},{24,16},{1,9},{9,1},{17,25},{25,17},{2,10},{10... | collective-permute-start | bytes 798728 | tf_op jit(solution)/shard_map/ppermute | solution.py:189
  38.9 1.0 %copy-start = (f32[520,128]{1,0:T(8,128)S(1)}, f32[520,128]{1,0:T(8,128)}, u32[]{:S(2)}) copy-start(f32[520,128]{1,0:T(8,128)} %extend.1.rest_0_) | copy-start | bytes 798724

commit v5 on v4

v5 whole, which is shorter than its diff:
```python
import functools

import jax
import jax.numpy as jnp
from jax import lax
from jax.experimental import pallas as pl
from jax.experimental.pallas import tpu as pltpu
from jax.sharding import Mesh
from jax.sharding import PartitionSpec as P

NCR = 2
LANES = 128
EXTRA = 8
VMEM_LIMIT = 48 * 1024 * 1024


def split3(x, order):
    high = x.astype(jnp.bfloat16)
    low = (x - high.astype(jnp.float32)).astype(jnp.bfloat16)
    parts = {"left": (high, low, high), "right": (high, high, low)}[order]
    return jnp.concatenate(parts, axis=0)


def transposed_dot(left, right):
    return lax.dot_general(left, right, (((0,), (0,)), ((), ())), preferred_element_type=jnp.float32)


def restrict_kernel(
    count_any, slot_any, rows_any, fetch_any, restrict_any, operator_any, out_ref,
    count_ref, slot_ref, rows_ref, fetch_ref, restrict_ref, operator_ref, sems, operator_sems,
):
    fine_rows, block_size, _ = operator_ref.shape
    entries = slot_ref.shape[1]
    slot_count, columns = fetch_ref.shape
    half = columns // 2
    used = 2 * slot_count * block_size
    wide = NCR * block_size

    pairs = [
        (count_any, count_ref), (slot_any, slot_ref), (rows_any, rows_ref),
        (fetch_any, fetch_ref), (restrict_any, restrict_ref),
    ]
    copies = [pltpu.make_async_copy(a, b, sems.at[i]) for i, (a, b) in enumerate(pairs)]
    operators = [
        pltpu.make_async_copy(operator_any.at[i], operator_ref.at[i], operator_sems.at[i]) for i in range(fine_rows)
    ]
    for copy in copies + operators:
        copy.start()

    lane = lax.broadcasted_iota(jnp.int32, (block_size, wide), 1)
    second = (lane >= block_size).astype(jnp.int32)
    short_lane = lax.broadcasted_iota(jnp.int32, (EXTRA, wide), 1)
    for near in range(half):
        out_ref[near, :used] = jnp.zeros((used, wide), jnp.float32)
    for copy in copies:
        copy.wait()

    for near in range(half):
        value = jnp.zeros((EXTRA, wide), jnp.int32)
        for side in range(2):
            for s in range(slot_count):
                wanted = fetch_ref[s, side * half + near]
                value = jnp.where(short_lane == side * slot_count + s, wanted, value)
        out_ref[near, used:] = value.astype(jnp.float32)

    for i in range(fine_rows):
        value = restrict_ref[i]
        swapped = pltpu.roll(value, block_size, 1)
        own_row = jnp.where(second == 0, rows_ref[0, i], rows_ref[1, i])
        other_row = jnp.where(second == 0, rows_ref[1, i], rows_ref[0, i])
        dense = jnp.where(own_row == second, value, 0.0) + jnp.where(other_row == second, swapped, 0.0)
        operators[i].wait()
        product = transposed_dot(split3(operator_ref[i], "left"), split3(dense, "right"))
        for k in range(entries):
            part = jnp.where(k < count_ref[i], product[k * block_size : (k + 1) * block_size], 0.0)
            peer = lax.div(slot_ref[i, k], slot_count)
            place = lax.div(peer, half) * slot_count + lax.rem(slot_ref[i, k], slot_count)
            start = pl.multiple_of(place * block_size, block_size)
            out_ref[lax.rem(peer, half), pl.ds(start, block_size)] += part


def restrict_operator(operator_count, operator_slot, restrict_rows, fetch, operator_blocks, restrict_blocks):
    fine_rows, block_size, width = operator_blocks.shape
    slot_count, columns = fetch.shape
    wide = NCR * block_size
    rows = 2 * slot_count * block_size + EXTRA
    small = (operator_count, operator_slot, restrict_rows, fetch)
    return pl.pallas_call(
        restrict_kernel,
        out_shape=jax.ShapeDtypeStruct((columns // 2, rows, wide), jnp.float32),
        in_specs=[pl.BlockSpec(memory_space=pltpu.HBM)] * 6,
        out_specs=pl.BlockSpec(memory_space=pltpu.VMEM),
        scratch_shapes=[pltpu.SMEM(x.shape, x.dtype) for x in small]
        + [pltpu.VMEM(x.shape, x.dtype) for x in (restrict_blocks, operator_blocks)]
        + [pltpu.SemaphoreType.DMA((5,)), pltpu.SemaphoreType.DMA((fine_rows,))],
        compiler_params=pltpu.CompilerParams(vmem_limit_bytes=VMEM_LIMIT),
        cost_estimate=pl.CostEstimate(
            flops=6 * fine_rows * block_size * width * wide, bytes_accessed=4 << 20, transcendentals=0
        ),
        name="restrict_operator",
    )(*small, restrict_blocks, operator_blocks)


def combine_kernel(own_ref, columns_ref, restricted_ref, *rest, far, slot_count, fine_rows, entries):
    out_ref, held_ref, table_ref, index_ref, sem, held_sem = rest[-6:]
    pieces, so_far = (rest[:-7], rest[-7]) if far else (rest[:-6], None)
    half = restricted_ref.shape[0]
    block_size = out_ref.shape[1]
    columns = 2 * half
    used = 2 * slot_count * block_size
    side = 1 - own_ref[1] if far else own_ref[1]

    if not far:
        own_copy = pltpu.make_async_copy(pieces[0], held_ref.at[0], held_sem)
        own_copy.start()
    table_ref[...] = jnp.zeros_like(table_ref)
    for near in range(half):
        table_ref[near : near + 1] = restricted_ref[near, used : used + 1].astype(jnp.int32)
    copy = pltpu.make_async_copy(table_ref, index_ref, sem)
    copy.start()
    for i, piece in enumerate(pieces):
        if far or i:
            held_ref[i] = piece[...]
    out_ref[...] = so_far[...] if far else jnp.zeros_like(out_ref)
    copy.wait()
    if not far:
        own_copy.wait()

    def step(i, carry):
        near = lax.div(i, slot_count)
        place = side * slot_count + lax.rem(i, slot_count)
        wanted = index_ref[near, place]
        inside = lax.rem(wanted, fine_rows)
        piece = lax.div(wanted, fine_rows * columns) ^ own_ref[0]
        restricted = restricted_ref[near, pl.ds(pl.multiple_of(place * block_size, block_size), block_size)]
        product = transposed_dot(split3(held_ref[piece, inside], "left"), split3(restricted, "right"))
        for m in range(entries):
            column = columns_ref[entries * piece + m, inside]
            out_ref[column] += product[m * block_size : (m + 1) * block_size]
        return carry

    lax.fori_loop(0, half * slot_count, step, 0, unroll=16)


def combine(own, columns, restricted, pieces, so_far, coarse_all, slot_count):
    half, _, wide = restricted.shape
    fine_rows, block_size, width = pieces[0].shape
    table_rows = -(-half // 8) * 8
    far = len(so_far)
    first = pl.BlockSpec(memory_space=pltpu.VMEM if far else pltpu.HBM)
    return pl.pallas_call(
        functools.partial(
            combine_kernel, far=far, slot_count=slot_count, fine_rows=fine_rows, entries=width // block_size
        ),
        out_shape=jax.ShapeDtypeStruct((coarse_all, block_size, wide), jnp.float32),
        in_specs=[pl.BlockSpec(memory_space=pltpu.SMEM)] * 2
        + [pl.BlockSpec(memory_space=pltpu.VMEM), first]
        + [pl.BlockSpec(memory_space=pltpu.VMEM)] * (len(pieces) - 1 + far),
        out_specs=pl.BlockSpec(memory_space=pltpu.VMEM),
        scratch_shapes=[
            pltpu.VMEM((len(pieces), fine_rows, block_size, width), jnp.float32),
            pltpu.VMEM((table_rows, LANES), jnp.int32),
            pltpu.SMEM((table_rows, LANES), jnp.int32),
            pltpu.SemaphoreType.DMA,
            pltpu.SemaphoreType.DMA,
        ],
        compiler_params=pltpu.CompilerParams(vmem_limit_bytes=VMEM_LIMIT),
        cost_estimate=pl.CostEstimate(flops=1 << 27, bytes_accessed=2 << 20, transcendentals=0),
        name="combine_far" if far else "combine_near",
    )(own, columns, restricted, *pieces, *so_far)


def add_kernel(parts_ref, out_ref):
    total = parts_ref[0]
    for i in range(1, parts_ref.shape[0]):
        total = total + parts_ref[i]
    out_ref[...] = total


def add_up(parts):
    return pl.pallas_call(
        add_kernel,
        out_shape=jax.ShapeDtypeStruct(parts.shape[1:], parts.dtype),
        in_specs=[pl.BlockSpec(memory_space=pltpu.VMEM)],
        out_specs=pl.BlockSpec(memory_space=pltpu.VMEM),
        compiler_params=pltpu.CompilerParams(vmem_limit_bytes=VMEM_LIMIT),
        name="add_up",
    )(parts)


def row_swap(x, bit):
    return lax.ppermute(x, "row", [(r, r ^ bit) for r in range(lax.axis_size("row"))])


def half_swap(x):
    return lax.ppermute(x, "half", [(0, 1), (1, 0)])


def spread_over_rows(blocks, rows):
    pieces = {0: blocks}
    bit = rows // 2
    while bit:
        for mask in list(pieces):
            pieces[mask ^ bit] = row_swap(pieces[mask], bit)
        bit //= 2
    return [pieces[mask] for mask in range(rows)]


def columns_of_rows(columns, rows):
    bit = 1
    while bit < rows:
        columns = jnp.concatenate([columns, row_swap(columns, bit)], axis=0)
        bit *= 2
    return columns


def local(
    operator_blocks,
    operator_count,
    operator_slot,
    fetch_lists,
    prolong_blocks,
    prolong_cols,
    restrict_blocks,
    restrict_rows,
):
    rows, half = lax.axis_size("row"), lax.axis_size("near")
    slot_count = fetch_lists.shape[3]
    fetch = fetch_lists.reshape(2 * half, slot_count).T
    own = jnp.stack([lax.axis_index("row"), lax.axis_index("half")])

    far_blocks = half_swap(prolong_blocks)
    restricted = restrict_operator(
        operator_count, operator_slot, restrict_rows.T, fetch, operator_blocks, restrict_blocks
    )
    restricted = lax.all_to_all(restricted, "near", split_axis=0, concat_axis=0, tiled=True)
    near_columns = columns_of_rows(prolong_cols.T, rows)
    far_columns = half_swap(near_columns)
    near_pieces = spread_over_rows(prolong_blocks, rows)
    far_pieces = spread_over_rows(far_blocks, rows)
    sums = combine(own, near_columns, restricted, near_pieces, (), NCR * rows, slot_count)
    sums = combine(own, far_columns, restricted, far_pieces, (sums,), NCR * rows, slot_count)
    parts = lax.all_to_all(sums, ("half", "near"), split_axis=0, concat_axis=0, tiled=True)
    return add_up(parts).T


def solution(mesh):
    rows, columns = mesh.shape["row"], mesh.shape["col"]
    split = Mesh(mesh.devices.reshape(rows, 2, columns // 2), ("row", "half", "near"))
    flat = ("row", "half", "near")
    return jax.shard_map(
        local,
        mesh=split,
        in_specs=(
            P(flat, None, None),
            P(flat),
            P(flat, None),
            P("row", ("half", "near"), None, None),
            P(flat, None, None),
            P(flat, None),
            P(flat, None, None),
            P(flat, None),
        ),
        out_specs=P("row", ("half", "near")),
        check_vma=False,
    )
```

time: 58.8 us -> 65.6 us (1.12)
  starting transfers between devices: 11.4 us -> 17.1 us
  Pallas kernels: 7.23 us -> 9.29 us
  blocking collectives: 15.6 us -> 14 us
  waiting for transfers between devices: 18.3 us -> 19.7 us
  local copies, waits for them, and re-layouts: 5.83 us -> 4.89 us
    ppermute x7 -> x10, starting transfers between devices: 6.16 us -> 11.7 us  [the longest x2 6.03 us: half_swap(): return lax.ppermute(x, 'half', [(0, 1), (1, 0)])]
    pallas_call x1, Pallas kernels: 2.61 us -> 5.16 us  [restrict_operator(): pl.pallas_call(restrict_kernel, out_shape=jax.ShapeDtypeStruct((columns /...]
    all_to_all x1, blocking collectives: 15.6 us -> 14 us  [local(): lax.all_to_all(sums, ('half', 'near'), split_axis=0, concat_axis=0, tiled...]
    ppermute x7 -> x10, waiting for transfers between devices: 18.3 us -> 19.7 us  [the longest x2 13.1 us: half_swap(): return lax.ppermute(x, 'half', [(0, 1), (1, 0)])]
    unnamed x14 -> x16, local copies, waits for them, and re-layouts: 5.83 us -> 4.89 us
  transfers between devices with their start and end apart: 8 -> 11, of which waited for: 3 -> 3; matrix products, arithmetic and copies ran while one was open for 0% -> 0% of each run, Pallas kernels for 3% -> 3%
where the time goes in v5:
time: 65.6 us; the launch traced here: 65.2 us
  waiting for transfers between devices  19.7 us (30%)
  starting transfers between devices  17.1 us (26%)
  blocking collectives  14 us (21%)
  Pallas kernels  9.29 us (14%)
  local copies, waits for them, and re-layouts  4.89 us (7%)
    all_to_all x1, blocking collectives, local(): lax.all_to_all(sums, ('half', 'near'), split_axis=0, concat_axis=0, tiled...  14 us
    ppermute x2, waiting for transfers between devices, half_swap(): return lax.ppermute(x, 'half', [(0, 1), (1, 0)])  13.1 us
    ppermute x8, waiting for transfers between devices, row_swap(): lax.ppermute(x, 'row', [(r, r ^ bit) for r in range(lax.axis_size('row'))])  6.58 us
    ppermute x2, starting transfers between devices, half_swap(): return lax.ppermute(x, 'half', [(0, 1), (1, 0)])  6.03 us
    ppermute x8, starting transfers between devices, row_swap(): lax.ppermute(x, 'row', [(r, r ^ bit) for r in range(lax.axis_size('row'))])  5.7 us
    all_to_all x1, starting transfers between devices, local(): lax.all_to_all(restricted, 'near', split_axis=0, concat_axis=0, tiled=True)  5.36 us
    pallas_call x1, Pallas kernels, restrict_operator(): pl.pallas_call(restrict_kernel, out_shape=jax.ShapeDtypeStruct((columns /...  5.16 us
    unnamed x16, local copies, waits for them, and re-layouts  4.89 us
  transfers between devices with their start and end apart: 11, of which 3 were waited for; matrix products, arithmetic and copies ran while one was open for 0% of the time, Pallas kernels for 3%

profile of v5, /device:TPU:0, one launch (start us, length us, event | category | flops | bytes accessed | tf_op | source)
XLA Modules:
  0.0 65.2 jit_solution(14777265861397278382)
XLA Ops:
  0.0 1.2 %copy-done = f32[8,64,512]{2,1,0:T(8,128)S(1)} copy-done((f32[8,64,512]{2,1,0:T(8,128)S(1)}, f32[8,64,512]{2,1,0:T(8,128)}, u32[]{:S(2)}) %copy-start) | copy-done | bytes 1048600
  1.2 0.9 %copy-done.1 = f32[8,64,128]{2,1,0:T(8,128)S(1)} copy-done((f32[8,64,128]{2,1,0:T(8,128)S(1)}, f32[8,64,128]{2,1,0:T(8,128)}, u32[]{:S(2)}) %copy-start.1) | copy-done | bytes 262168
  2.2 0.7 %copy-done.3 = s32[8,8]{1,0:T(8,128)S(1)} copy-done((s32[8,8]{1,0:T(8,128)S(1)}, s32[8,8]{1,0:T(8,128)}, u32[]{:S(2)}) %copy-start.3) | copy-done | bytes 280
  2.9 0.7 %copy-done.4 = s32[1,1,8,4]{2,3,1,0:T(4,128)S(1)} copy-done((s32[1,1,8,4]{2,3,1,0:T(4,128)S(1)}, s32[1,1,8,4]{2,3,1,0:T(4,128)}, u32[]{:S(2)}) %copy-start.4) | copy-done | bytes 152
  3.5 0.7 %copy-done.5 = s32[8,2]{0,1:T(2,128)S(1)} copy-done((s32[8,2]{0,1:T(2,128)S(1)}, s32[8,2]{0,1:T(2,128)}, u32[]{:S(2)}) %copy-start.5) | copy-done | bytes 88
  4.2 0.7 %copy-done.6 = s32[8]{0:T(128)S(1)} copy-done((s32[8]{0:T(128)S(1)}, s32[8]{0:T(128)}, u32[]{:S(2)}) %copy-start.6) | copy-done | bytes 56
  4.9 5.2 %restrict_operator.1 = f32[4,520,128]{2,1,0:T(8,128)} custom-call(s32[8]{0:T(128)S(1)} %copy-done.6, s32[8,8]{1,0:T(8,128)S(1)} %copy-done.3, s32[2,8]{1,0:T(2,128)S(1)} %bitcast.9, s32[4,8]{1,0:T(4,128)S(1)} %bitcast.8, f32[8,64,128]{2,1,0:T(8,128)S(1)} %copy-done.1, f32[8,64,512]{2,1,0:T(8,128)S(1)} %copy-done), custom_call_target="tpu_custom_call" | custom-call | flops 201326592 | bytes 4194304 | tf_op jit(solution)/shard_map/restrict_operator/pallas_call | solution.py:88
  10.1 0.0 copy-start.7
  10.1 5.4 %all-to-all-start = ((f32[4,520,128]{2,1,0:T(8,128)}), f32[4,520,128]{2,1,0:T(8,128)S(1)}, u32[]{:S(2)}, u32[]{:S(2)}) async-start(f32[4,520,128]{2,1,0:T(8,128)} %restrict_operator.1), calls=%async_computation | async-start | bytes 2129920 | tf_op jit(solution)/shard_map/all_to_all | solution.py:236
  15.4 2.6 %collective-permute-start.3 = (f32[8,64,128]{2,1,0:T(8,128)S(1)}, f32[8,64,128]{2,1,0:T(8,128)S(1)}, u32[]{:S(2)}, u32[]{:S(2)}) collective-permute-start(f32[8,64,128]{2,1,0:T(8,128)S(1)} %copy-done.2), channel_id=1, source_target_pairs={{0,4},{4,0},{1,5},{5,1},{2,6},{6,2},{3,7},{7,3},{8,12},{12,8},{9,1... | collective-permute-start | bytes 786440 | tf_op jit(solution)/shard_map/ppermute | solution.py:196
  18.0 1.5 %collective-permute-start.8 = (f32[8,64,128]{2,1,0:T(8,128)S(1)}, f32[8,64,128]{2,1,0:T(8,128)S(1)}, u32[]{:S(2)}, u32[]{:S(2)}) collective-permute-start(f32[8,64,128]{2,1,0:T(8,128)S(1)} %copy-done.2), channel_id=1, source_target_pairs={{0,16},{8,24},{16,0},{24,8},{1,17},{9,25},{17,1},{25,9},{2,18},{10... | collective-permute-start | bytes 786440 | tf_op jit(solution)/shard_map/ppermute | solution.py:192
  19.6 13.1 %collective-permute-done.3.rest_0_ = f32[8,64,128]{2,1,0:T(8,128)S(1)} collective-permute-done((f32[8,64,128]{2,1,0:T(8,128)S(1)}, f32[8,64,128]{2,1,0:T(8,128)S(1)}, u32[]{:S(2)}, u32[]{:S(2)}) %collective-permute-start.3) | collective-permute-done | bytes 262176 | tf_op jit(solution)/shard_map/ppermute | solution.py:196
  32.7 1.5 %collective-permute-start.5 = (f32[8,64,128]{2,1,0:T(8,128)S(1)}, f32[8,64,128]{2,1,0:T(8,128)S(1)}, u32[]{:S(2)}, u32[]{:S(2)}) collective-permute-start(f32[8,64,128]{2,1,0:T(8,128)S(1)} %collective-permute-done.3.rest_0_), channel_id=1, source_target_pairs={{0,16},{8,24},{16,0},{24,8},{1,17},{9,25},{17,1},{25,9},{2,18},{10... | collective-permute-start | bytes 786440 | tf_op jit(solution)/shard_map/ppermute | solution.py:192
  34.2 0.5 collective-permute-start
  34.7 0.5 collective-permute-start.9
  35.2 4.6 %collective-permute-done.5.rest_2_ = f32[8,64,128]{2,1,0:T(8,128)S(1)} collective-permute-done((f32[8,64,128]{2,1,0:T(8,128)S(1)}, f32[8,64,128]{2,1,0:T(8,128)S(1)}, u32[]{:S(2)}, u32[]{:S(2)}) %collective-permute-start.5) | collective-permute-done | bytes 262176 | tf_op jit(solution)/shard_map/ppermute | solution.py:192
  39.9 1.6 %collective-permute-start.1 = (s32[4,8]{1,0:T(4,128)S(1)}, s32[4,8]{1,0:T(4,128)S(1)}, u32[]{:S(2)}, u32[]{:S(2)}) collective-permute-start(s32[4,8]{1,0:T(4,128)S(1)} %pad_add_fusion.1), channel_id=1, source_target_pairs={{0,16},{8,24},{16,0},{24,8},{1,17},{9,25},{17,1},{25,9},{2,18},{10... | collective-permute-start | bytes 392 | tf_op jit(solution)/shard_map/ppermute | solution.py:192
  41.5 0.1 pad_add_fusion.2.own_ref
  41.6 2.0 %collective-permute-done.1 = s32[4,8]{1,0:T(4,128)S(1)} collective-permute-done((s32[4,8]{1,0:T(4,128)S(1)}, s32[4,8]{1,0:T(4,128)S(1)}, u32[]{:S(2)}, u32[]{:S(2)}) %collective-permute-start.1) | collective-permute-done | bytes 160 | tf_op jit(solution)/shard_map/ppermute | solution.py:192
  43.5 3.4 %collective-permute-start.2 = (s32[8,8]{1,0:T(8,128)S(1)}, s32[8,8]{1,0:T(8,128)S(1)}, u32[]{:S(2)}, u32[]{:S(2)}) collective-permute-start(s32[8,8]{1,0:T(8,128)S(1)} %pad_add_fusion.columns_ref), channel_id=1, source_target_pairs={{0,4},{4,0},{1,5},{5,1},{2,6},{6,2},{3,7},{7,3},{8,12},{12,8},{9,1... | collective-permute-start | bytes 776 | tf_op jit(solution)/shard_map/ppermute | solution.py:196
  47.0 1.8 %combine_near.1.rest_4_ = f32[8,64,128]{2,1,0:T(8,128)S(1)} custom-call(s32[2]{0:T(128)S(1)} %pad_add_fusion.2.own_ref, s32[8,8]{1,0:T(8,128)S(1)} %pad_add_fusion.columns_ref, f32[4,520,128]{2,1,0:T(8,128)S(1)} %all-to-all-done.restricted_ref, f32[8,64,128]{2,1,0:T(8,128)S(1)} %copy-done.2, f32[8,64,128]{2,1,0:T(8,128)S(1)} %collective-permute-done.7.rest_1_, ...), custom_call_target="tpu_custom_call" | custom-call | flops 134217728 | bytes 2097152 | tf_op jit(solution)/shard_map/combine_near/pallas_call | solution.py:151
  48.8 1.7 %combine_far.1 = f32[8,64,128]{2,1,0:T(8,128)S(1)} custom-call(s32[2]{0:T(128)S(1)} %pad_add_fusion.2.own_ref, s32[8,8]{1,0:T(8,128)S(1)} %collective-permute-done.2.columns_ref, f32[4,520,128]{2,1,0:T(8,128)S(1)} %all-to-all-done.restricted_ref, f32[8,64,128]{2,1,0:T(8,128)S(1)} %collective-permute-done.3.rest_0_, ...), custom_call_target="tpu_custom_call" | custom-call | flops 134217728 | bytes 2097152 | tf_op jit(solution)/shard_map/combine_far/pallas_call | solution.py:151
  50.5 14.0 %all_to_all.10.parts_ref = f32[8,64,128]{2,1,0:T(8,128)S(1)} all-to-all(f32[8,64,128]{2,1,0:T(8,128)S(1)} %combine_far.1), channel_id=1, replica_groups=mesh['row'=4,'half'=2,'near'=4] {'half','near'}, dimensions={0} | all-to-all | bytes 524288 | tf_op jit(solution)/shard_map/all_to_all | solution.py:243
  64.6 0.6 add_up.1
  (22 shorter events, 0.1 us)
Async XLA Ops:
  0.0 1.2 %copy-start = (f32[8,64,512]{2,1,0:T(8,128)S(1)}, f32[8,64,512]{2,1,0:T(8,128)}, u32[]{:S(2)}) copy-start(f32[8,64,512]{2,1,0:T(8,128)} %operator_any.1) | copy-start | bytes 3145732
  1.2 0.9 %copy-start.1 = (f32[8,64,128]{2,1,0:T(8,128)S(1)}, f32[8,64,128]{2,1,0:T(8,128)}, u32[]{:S(2)}) copy-start(f32[8,64,128]{2,1,0:T(8,128)} %restrict_any.1) | copy-start | bytes 786436
  2.2 0.7 %copy-start.3 = (s32[8,8]{1,0:T(8,128)S(1)}, s32[8,8]{1,0:T(8,128)}, u32[]{:S(2)}) copy-start(s32[8,8]{1,0:T(8,128)} %slot_any.1) | copy-start | bytes 772
  2.9 0.7 %copy-start.4 = (s32[1,1,8,4]{2,3,1,0:T(4,128)S(1)}, s32[1,1,8,4]{2,3,1,0:T(4,128)}, u32[]{:S(2)}) copy-start(s32[1,1,8,4]{2,3,1,0:T(4,128)} %param.11) | copy-start | bytes 388
  3.5 0.7 %copy-start.5 = (s32[8,2]{0,1:T(2,128)S(1)}, s32[8,2]{0,1:T(2,128)}, u32[]{:S(2)}) copy-start(s32[8,2]{0,1:T(2,128)} %param.15) | copy-start | bytes 196
  4.2 0.7 %copy-start.6 = (s32[8]{0:T(128)S(1)}, s32[8]{0:T(128)}, u32[]{:S(2)}) copy-start(s32[8]{0:T(128)} %count_any.1) | copy-start | bytes 100
  10.1 5.4 %copy-start.2 = (f32[8,64,128]{2,1,0:T(8,128)S(1)}, f32[8,64,128]{2,1,0:T(8,128)}, u32[]{:S(2)}) copy-start(f32[8,64,128]{2,1,0:T(8,128)} %rest_0_.1) | copy-start | bytes 786436
  10.1 24.1 %copy-start.7 = (s32[8,2]{0,1:T(2,128)S(1)}, s32[8,2]{0,1:T(2,128)}, u32[]{:S(2)}) copy-start(s32[8,2]{0,1:T(2,128)} %param.13) | copy-start | bytes 196
  10.1 36.9 %all-to-all-start = ((f32[4,520,128]{2,1,0:T(8,128)}), f32[4,520,128]{2,1,0:T(8,128)S(1)}, u32[]{:S(2)}, u32[]{:S(2)}) async-start(f32[4,520,128]{2,1,0:T(8,128)} %restrict_operator.1), calls=%async_computation | async-start | bytes 2129920 | tf_op jit(solution)/shard_map/all_to_all | solution.py:236
  15.4 17.2 %collective-permute-start.3 = (f32[8,64,128]{2,1,0:T(8,128)S(1)}, f32[8,64,128]{2,1,0:T(8,128)S(1)}, u32[]{:S(2)}, u32[]{:S(2)}) collective-permute-start(f32[8,64,128]{2,1,0:T(8,128)S(1)} %copy-done.2), channel_id=1, source_target_pairs={{0,4},{4,0},{1,5},{5,1},{2,6},{6,2},{3,7},{7,3},{8,12},{12,8},{9,1... | collective-permute-start | bytes 786440 | tf_op jit(solution)/shard_map/ppermute | solution.py:196
  18.0 16.7 %collective-permute-start.8 = (f32[8,64,128]{2,1,0:T(8,128)S(1)}, f32[8,64,128]{2,1,0:T(8,128)S(1)}, u32[]{:S(2)}, u32[]{:S(2)}) collective-permute-start(f32[8,64,128]{2,1,0:T(8,128)S(1)} %copy-done.2), channel_id=1, source_target_pairs={{0,16},{8,24},{16,0},{24,8},{1,17},{9,25},{17,1},{25,9},{2,18},{10... | collective-permute-start | bytes 786440 | tf_op jit(solution)/shard_map/ppermute | solution.py:192
  32.7 7.2 %collective-permute-start.5 = (f32[8,64,128]{2,1,0:T(8,128)S(1)}, f32[8,64,128]{2,1,0:T(8,128)S(1)}, u32[]{:S(2)}, u32[]{:S(2)}) collective-permute-start(f32[8,64,128]{2,1,0:T(8,128)S(1)} %collective-permute-done.3.rest_0_), channel_id=1, source_target_pairs={{0,16},{8,24},{16,0},{24,8},{1,17},{9,25},{17,1},{25,9},{2,18},{10... | collective-permute-start | bytes 786440 | tf_op jit(solution)/shard_map/ppermute | solution.py:192
  34.2 12.8 %collective-permute-start.7 = (f32[8,64,128]{2,1,0:T(8,128)S(1)}, f32[8,64,128]{2,1,0:T(8,128)S(1)}, u32[]{:S(2)}, u32[]{:S(2)}) collective-permute-start(f32[8,64,128]{2,1,0:T(8,128)S(1)} %copy-done.2), channel_id=1, source_target_pairs={{0,8},{8,0},{16,24},{24,16},{1,9},{9,1},{17,25},{25,17},{2,10},{10... | collective-permute-start | bytes 786440 | tf_op jit(solution)/shard_map/ppermute | solution.py:192
  34.2 5.6 %collective-permute-start = (s32[2,8]{1,0:T(2,128)S(1)}, s32[2,8]{1,0:T(2,128)S(1)}, u32[]{:S(2)}, u32[]{:S(2)}) collective-permute-start(s32[2,8]{1,0:T(2,128)S(1)} %bitcast.10), channel_id=1, source_target_pairs={{0,8},{8,0},{16,24},{24,16},{1,9},{9,1},{17,25},{25,17},{2,10},{10... | collective-permute-start | bytes 200 | tf_op jit(solution)/shard_map/ppermute | solution.py:192
  34.7 14.1 %collective-permute-start.4 = (f32[8,64,128]{2,1,0:T(8,128)S(1)}, f32[8,64,128]{2,1,0:T(8,128)S(1)}, u32[]{:S(2)}, u32[]{:S(2)}) collective-permute-start(f32[8,64,128]{2,1,0:T(8,128)S(1)} %collective-permute-done.3.rest_0_), channel_id=1, source_target_pairs={{0,8},{8,0},{16,24},{24,16},{1,9},{9,1},{17,25},{25,17},{2,10},{10... | collective-permute-start | bytes 786440 | tf_op jit(solution)/shard_map/ppermute | solution.py:192
  34.7 12.2 %collective-permute-start.9 = (f32[8,64,128]{2,1,0:T(8,128)S(1)}, f32[8,64,128]{2,1,0:T(8,128)S(1)}, u32[]{:S(2)}, u32[]{:S(2)}) collective-permute-start(f32[8,64,128]{2,1,0:T(8,128)S(1)} %collective-permute-done.8.rest_2_), channel_id=1, source_target_pairs={{0,8},{8,0},{16,24},{24,16},{1,9},{9,1},{17,25},{25,17},{2,10},{10... | collective-permute-start | bytes 786440 | tf_op jit(solution)/shard_map/ppermute | solution.py:192
  39.8 8.9 %collective-permute-start.6 = (f32[8,64,128]{2,1,0:T(8,128)S(1)}, f32[8,64,128]{2,1,0:T(8,128)S(1)}, u32[]{:S(2)}, u32[]{:S(2)}) collective-permute-start(f32[8,64,128]{2,1,0:T(8,128)S(1)} %collective-permute-done.5.rest_2_), channel_id=1, source_target_pairs={{0,8},{8,0},{16,24},{24,16},{1,9},{9,1},{17,25},{25,17},{2,10},{10... | collective-permute-start | bytes 786440 | tf_op jit(solution)/shard_map/ppermute | solution.py:192
  39.9 3.7 %collective-permute-start.1 = (s32[4,8]{1,0:T(4,128)S(1)}, s32[4,8]{1,0:T(4,128)S(1)}, u32[]{:S(2)}, u32[]{:S(2)}) collective-permute-start(s32[4,8]{1,0:T(4,128)S(1)} %pad_add_fusion.1), channel_id=1, source_target_pairs={{0,16},{8,24},{16,0},{24,8},{1,17},{9,25},{17,1},{25,9},{2,18},{10... | collective-permute-start | bytes 392 | tf_op jit(solution)/shard_map/ppermute | solution.py:192
  43.5 5.2 %collective-permute-start.2 = (s32[8,8]{1,0:T(8,128)S(1)}, s32[8,8]{1,0:T(8,128)S(1)}, u32[]{:S(2)}, u32[]{:S(2)}) collective-permute-start(s32[8,8]{1,0:T(8,128)S(1)} %pad_add_fusion.columns_ref), channel_id=1, source_target_pairs={{0,4},{4,0},{1,5},{5,1},{2,6},{6,2},{3,7},{7,3},{8,12},{12,8},{9,1... | collective-permute-start | bytes 776 | tf_op jit(solution)/shard_map/ppermute | solution.py:196

commit v6 on v5

--- a/solution.py
+++ b/solution.py
@@ -11,6 +11,8 @@
 NCR = 2
 LANES = 128
 EXTRA = 8
+HOLD_FLOPS = 4 << 30
+HOLD_BYTES = 12 << 20
 VMEM_LIMIT = 48 * 1024 * 1024
 
 
@@ -25,8 +27,24 @@
     return lax.dot_general(left, right, (((0,), (0,)), ((), ())), preferred_element_type=jnp.float32)
 
 
+def hold_kernel(columns_ref, mark_ref, blocks_ref, out_ref):
+    out_ref[...] = blocks_ref[...]
+
+
+def hold_until(columns, mark, blocks):
+    return pl.pallas_call(
+        hold_kernel,
+        out_shape=jax.ShapeDtypeStruct(blocks.shape, blocks.dtype),
+        in_specs=[pl.BlockSpec(memory_space=pltpu.VMEM)] * 3,
+        out_specs=pl.BlockSpec(memory_space=pltpu.VMEM),
+        compiler_params=pltpu.CompilerParams(vmem_limit_bytes=VMEM_LIMIT),
+        cost_estimate=pl.CostEstimate(flops=HOLD_FLOPS, bytes_accessed=HOLD_BYTES, transcendentals=0),
+        name="hold_until",
+    )(columns, mark, blocks)
+
+
 def restrict_kernel(
-    count_any, slot_any, rows_any, fetch_any, restrict_any, operator_any, out_ref,
+    count_any, slot_any, rows_any, fetch_any, restrict_any, operator_any, out_ref, mark_ref,
     count_ref, slot_ref, rows_ref, fetch_ref, restrict_ref, operator_ref, sems, operator_sems,
 ):
     fine_rows, block_size, _ = operator_ref.shape
@@ -62,6 +80,7 @@
                 wanted = fetch_ref[s, side * half + near]
                 value = jnp.where(short_lane == side * slot_count + s, wanted, value)
         out_ref[near, used:] = value.astype(jnp.float32)
+    mark_ref[...] = out_ref[0, used:]
 
     for i in range(fine_rows):
         value = restrict_ref[i]
@@ -87,13 +106,15 @@
     small = (operator_count, operator_slot, restrict_rows, fetch)
     return pl.pallas_call(
         restrict_kernel,
-        out_shape=jax.ShapeDtypeStruct((columns // 2, rows, wide), jnp.float32),
+        out_shape=(
+            jax.ShapeDtypeStruct((columns // 2, rows, wide), jnp.float32),
+            jax.ShapeDtypeStruct((EXTRA, wide), jnp.float32),
+        ),
         in_specs=[pl.BlockSpec(memory_space=pltpu.HBM)] * 6,
-        out_specs=pl.BlockSpec(memory_space=pltpu.VMEM),
+        out_specs=[pl.BlockSpec(memory_space=pltpu.VMEM)] * 2,
         scratch_shapes=[pltpu.SMEM(x.shape, x.dtype) for x in small]
         + [pltpu.VMEM(x.shape, x.dtype) for x in (restrict_blocks, operator_blocks)]
         + [pltpu.SemaphoreType.DMA((5,)), pltpu.SemaphoreType.DMA((fine_rows,))],
-        compiler_params=pltpu.CompilerParams(vmem_limit_bytes=VMEM_LIMIT),
         cost_estimate=pl.CostEstimate(
             flops=6 * fine_rows * block_size * width * wide, bytes_accessed=4 << 20, transcendentals=0
         ),
@@ -230,12 +251,13 @@
     own = jnp.stack([lax.axis_index("row"), lax.axis_index("half")])
 
     far_blocks = half_swap(prolong_blocks)
-    restricted = restrict_operator(
+    restricted, mark = restrict_operator(
         operator_count, operator_slot, restrict_rows.T, fetch, operator_blocks, restrict_blocks
     )
     restricted = lax.all_to_all(restricted, "near", split_axis=0, concat_axis=0, tiled=True)
     near_columns = columns_of_rows(prolong_cols.T, rows)
     far_columns = half_swap(near_columns)
+    far_blocks = hold_until(near_columns, mark, far_blocks)
     near_pieces = spread_over_rows(prolong_blocks, rows)
     far_pieces = spread_over_rows(far_blocks, rows)
     sums = combine(own, near_columns, restricted, near_pieces, (), NCR * rows, slot_count)

time: 65.6 us -> 57.6 us (0.88)
  local copies, waits for them, and re-layouts: 4.89 us -> 0.02 us
  waiting for transfers between devices: 19.7 us -> 17.7 us
  starting transfers between devices: 17.1 us -> 15.5 us
  blocking collectives: 14 us -> 14.8 us
    unnamed x16 -> x6, local copies, waits for them, and re-layouts: 4.89 us -> 0.02 us
    ppermute x2, waiting for transfers between devices: 13.1 us -> 9.83 us  [half_swap(): return lax.ppermute(x, 'half', [(0, 1), (1, 0)])]
    ppermute x8, starting transfers between devices: 5.7 us -> 4.21 us  [row_swap(): lax.ppermute(x, 'row', [(r, r ^ bit) for r in range(lax.axis_size('row'))])]
    ppermute x8, waiting for transfers between devices: 6.58 us -> 7.83 us  [row_swap(): lax.ppermute(x, 'row', [(r, r ^ bit) for r in range(lax.axis_size('row'))])]
    all_to_all x1, blocking collectives: 14 us -> 14.8 us  [local(): lax.all_to_all(sums, ('half', 'near'), split_axis=0, concat_axis=0, tiled...]
    pallas_call x1 -> x2, Pallas kernels: 5.16 us -> 5.02 us  [the longest x1 5.01 us: restrict_operator(): pl.pallas_call(restrict_kernel, out_shape=(jax.ShapeDtypeStruct((columns...]
  transfers between devices with their start and end apart: 11 -> 11, of which waited for: 3 -> 4; matrix products, arithmetic and copies ran while one was open for 0% -> 0% of each run, Pallas kernels for 3% -> 3%
where the time goes in v6:
time: 57.6 us; the launch traced here: 57.3 us
  waiting for transfers between devices  17.7 us (31%)
  starting transfers between devices  15.5 us (27%)
  blocking collectives  14.8 us (26%)
  Pallas kernels  9.15 us (16%)
    all_to_all x1, blocking collectives, local(): lax.all_to_all(sums, ('half', 'near'), split_axis=0, concat_axis=0, tiled...  14.8 us
    ppermute x2, waiting for transfers between devices, half_swap(): return lax.ppermute(x, 'half', [(0, 1), (1, 0)])  9.83 us
    ppermute x8, waiting for transfers between devices, row_swap(): lax.ppermute(x, 'row', [(r, r ^ bit) for r in range(lax.axis_size('row'))])  7.83 us
    ppermute x2, starting transfers between devices, half_swap(): return lax.ppermute(x, 'half', [(0, 1), (1, 0)])  5.97 us
    all_to_all x1, starting transfers between devices, local(): lax.all_to_all(restricted, 'near', split_axis=0, concat_axis=0, tiled=True)  5.36 us
    pallas_call x1, Pallas kernels, restrict_operator(): pl.pallas_call(restrict_kernel, out_shape=(jax.ShapeDtypeStruct((columns...  5.01 us
    ppermute x8, starting transfers between devices, row_swap(): lax.ppermute(x, 'row', [(r, r ^ bit) for r in range(lax.axis_size('row'))])  4.21 us
    pallas_call x2, Pallas kernels, combine(): pl.pallas_call(functools.partial(combine_kernel, far=far, slot_count=slot...  3.5 us
  transfers between devices with their start and end apart: 11, of which 4 were waited for; matrix products, arithmetic and copies ran while one was open for 0% of the time, Pallas kernels for 3%

profile of v6, /device:TPU:0, one launch (start us, length us, event | category | flops | bytes accessed | tf_op | source)
XLA Modules:
  0.0 57.3 jit_solution(14502228748032333058)
XLA Ops:
  0.0 5.0 %restrict_operator.1 = (f32[4,520,128]{2,1,0:T(8,128)}, f32[8,128]{1,0:T(8,128)}) custom-call(s32[8]{0:T(128)} %count_any.1, s32[8,8]{1,0:T(8,128)} %slot_any.1, s32[2,8]{1,0:T(2,128)} %bitcast.12, s32[4,8]{1,0:T(4,128)} %bitcast.11, f32[8,64,128]{2,1,0:T(8,128)} %restrict_any.1, f32[8,64,512]{2,1,0:T(8,128)} %operator_any.1), custom_call_target="tpu_custom_call" | custom-call | flops 201326592 | bytes 4194304 | tf_op jit(solution)/shard_map/restrict_operator/pallas_call | solution.py:107
  5.0 0.0 copy-start
  5.0 0.0 copy-start.2
  5.0 0.0 copy-start.1
  5.1 5.4 %all-to-all-start = ((f32[4,520,128]{2,1,0:T(8,128)}), f32[4,520,128]{2,1,0:T(8,128)S(1)}, u32[]{:S(2)}, u32[]{:S(2)}) async-start(f32[4,520,128]{2,1,0:T(8,128)} %get-tuple-element.7), calls=%async_computation | async-start | bytes 2129920 | tf_op jit(solution)/shard_map/all_to_all | solution.py:257
  10.4 2.6 %collective-permute-start.3 = (f32[8,64,128]{2,1,0:T(8,128)S(1)}, f32[8,64,128]{2,1,0:T(8,128)S(1)}, u32[]{:S(2)}, u32[]{:S(2)}) collective-permute-start(f32[8,64,128]{2,1,0:T(8,128)S(1)} %copy-done), channel_id=1, source_target_pairs={{0,4},{4,0},{1,5},{5,1},{2,6},{6,2},{3,7},{7,3},{8,12},{12,8},{9,1... | collective-permute-start | bytes 786440 | tf_op jit(solution)/shard_map/ppermute | solution.py:217
  13.0 1.1 %collective-permute-done = s32[2,8]{1,0:T(2,128)S(1)} collective-permute-done((s32[2,8]{1,0:T(2,128)S(1)}, s32[2,8]{1,0:T(2,128)S(1)}, u32[]{:S(2)}, u32[]{:S(2)}) %collective-permute-start) | collective-permute-done | bytes 96 | tf_op jit(solution)/shard_map/ppermute | solution.py:213
  14.2 1.6 %collective-permute-start.1 = (s32[4,8]{1,0:T(4,128)S(1)}, s32[4,8]{1,0:T(4,128)S(1)}, u32[]{:S(2)}, u32[]{:S(2)}) collective-permute-start(s32[4,8]{1,0:T(4,128)S(1)} %pad_add_fusion.1), channel_id=1, source_target_pairs={{0,16},{8,24},{16,0},{24,8},{1,17},{9,25},{17,1},{25,9},{2,18},{10... | collective-permute-start | bytes 392 | tf_op jit(solution)/shard_map/ppermute | solution.py:213
  15.8 0.5 collective-permute-start.8
  16.2 1.6 %collective-permute-done.1 = s32[4,8]{1,0:T(4,128)S(1)} collective-permute-done((s32[4,8]{1,0:T(4,128)S(1)}, s32[4,8]{1,0:T(4,128)S(1)}, u32[]{:S(2)}, u32[]{:S(2)}) %collective-permute-start.1) | collective-permute-done | bytes 160 | tf_op jit(solution)/shard_map/ppermute | solution.py:213
  17.8 9.8 %collective-permute-done.3.blocks_ref = f32[8,64,128]{2,1,0:T(8,128)S(1)} collective-permute-done((f32[8,64,128]{2,1,0:T(8,128)S(1)}, f32[8,64,128]{2,1,0:T(8,128)S(1)}, u32[]{:S(2)}, u32[]{:S(2)}) %collective-permute-start.3) | collective-permute-done | bytes 262176 | tf_op jit(solution)/shard_map/ppermute | solution.py:217
  27.7 1.6 %collective-permute-start.5 = (f32[8,64,128]{2,1,0:T(8,128)S(1)}, f32[8,64,128]{2,1,0:T(8,128)S(1)}, u32[]{:S(2)}, u32[]{:S(2)}) collective-permute-start(f32[8,64,128]{2,1,0:T(8,128)S(1)} %hold_until.1.rest_0_), channel_id=1, source_target_pairs={{0,16},{8,24},{16,0},{24,8},{1,17},{9,25},{17,1},{25,9},{2,18},{10... | collective-permute-start | bytes 786440 | tf_op jit(solution)/shard_map/ppermute | solution.py:213
  29.3 0.5 collective-permute-start.9
  29.8 0.0 collective-permute-start.4
  29.8 5.1 %collective-permute-done.5.rest_2_ = f32[8,64,128]{2,1,0:T(8,128)S(1)} collective-permute-done((f32[8,64,128]{2,1,0:T(8,128)S(1)}, f32[8,64,128]{2,1,0:T(8,128)S(1)}, u32[]{:S(2)}, u32[]{:S(2)}) %collective-permute-start.5) | collective-permute-done | bytes 262176 | tf_op jit(solution)/shard_map/ppermute | solution.py:213
  34.9 0.1 pad_add_fusion.2.own_ref
  35.0 3.4 %collective-permute-start.2 = (s32[8,8]{1,0:T(8,128)S(1)}, s32[8,8]{1,0:T(8,128)S(1)}, u32[]{:S(2)}, u32[]{:S(2)}) collective-permute-start(s32[8,8]{1,0:T(8,128)S(1)} %pad_add_fusion.columns_ref), channel_id=1, source_target_pairs={{0,4},{4,0},{1,5},{5,1},{2,6},{6,2},{3,7},{7,3},{8,12},{12,8},{9,1... | collective-permute-start | bytes 776 | tf_op jit(solution)/shard_map/ppermute | solution.py:217
  38.4 0.0 collective-permute-done.7.rest_1_
  38.4 0.0 collective-permute-done.9.rest_3_
  38.4 0.0 all-to-all-done.restricted_ref
  38.4 1.8 %combine_near.1.rest_4_ = f32[8,64,128]{2,1,0:T(8,128)S(1)} custom-call(s32[2]{0:T(128)S(1)} %pad_add_fusion.2.own_ref, s32[8,8]{1,0:T(8,128)S(1)} %pad_add_fusion.columns_ref, f32[4,520,128]{2,1,0:T(8,128)S(1)} %all-to-all-done.restricted_ref, f32[8,64,128]{2,1,0:T(8,128)S(1)} %copy-done, f32[8,64,128]{2,1,0:T(8,128)S(1)} %collective-permute-done.7.rest_1_, ...), custom_call_target="tpu_custom_call" | custom-call | flops 134217728 | bytes 2097152 | tf_op jit(solution)/shard_map/combine_near/pallas_call | solution.py:172
  40.2 1.7 %combine_far.1 = f32[8,64,128]{2,1,0:T(8,128)S(1)} custom-call(s32[2]{0:T(128)S(1)} %pad_add_fusion.2.own_ref, s32[8,8]{1,0:T(8,128)S(1)} %collective-permute-done.2.columns_ref, f32[4,520,128]{2,1,0:T(8,128)S(1)} %all-to-all-done.restricted_ref, f32[8,64,128]{2,1,0:T(8,128)S(1)} %hold_until.1.rest_0_, f32[8,64,128]{2,1,0:T(8,128)S(1)} %collective-permute-done.4.rest_1_, ...), custom_call_target="tpu_custom_call" | custom-call | flops 134217728 | bytes 2097152 | tf_op jit(solution)/shard_map/combine_far/pallas_call | solution.py:172
  41.9 14.8 %all_to_all.10.parts_ref = f32[8,64,128]{2,1,0:T(8,128)S(1)} all-to-all(f32[8,64,128]{2,1,0:T(8,128)S(1)} %combine_far.1), channel_id=1, replica_groups=mesh['row'=4,'half'=2,'near'=4] {'half','near'}, dimensions={0} | all-to-all | bytes 524288 | tf_op jit(solution)/shard_map/all_to_all | solution.py:265
  56.7 0.6 %add_up.1 = f32[64,128]{1,0:T(8,128)} custom-call(f32[8,64,128]{2,1,0:T(8,128)S(1)} %all_to_all.10.parts_ref), custom_call_target="tpu_custom_call" | custom-call | tf_op jit(solution)/shard_map/add_up/pallas_call | solution.py:202
  (13 shorter events, 0.1 us)
Async XLA Ops:
  5.0 5.4 %copy-start = (f32[8,64,128]{2,1,0:T(8,128)S(1)}, f32[8,64,128]{2,1,0:T(8,128)}, u32[]{:S(2)}) copy-start(f32[8,64,128]{2,1,0:T(8,128)} %rest_0_.1) | copy-start | bytes 786436
  5.0 8.0 %copy-start.2 = (s32[8,2]{0,1:T(2,128)S(1)}, s32[8,2]{0,1:T(2,128)}, u32[]{:S(2)}) copy-start(s32[8,2]{0,1:T(2,128)} %param.13) | copy-start | bytes 196
  5.0 22.6 %copy-start.1 = (f32[8,128]{1,0:T(8,128)S(1)}, f32[8,128]{1,0:T(8,128)}, u32[]{:S(2)}) copy-start(f32[8,128]{1,0:T(8,128)} %get-tuple-element.8.mark_ref) | copy-start | bytes 12292
  5.1 33.3 %all-to-all-start = ((f32[4,520,128]{2,1,0:T(8,128)}), f32[4,520,128]{2,1,0:T(8,128)S(1)}, u32[]{:S(2)}, u32[]{:S(2)}) async-start(f32[4,520,128]{2,1,0:T(8,128)} %get-tuple-element.7), calls=%async_computation | async-start | bytes 2129920 | tf_op jit(solution)/shard_map/all_to_all | solution.py:257
  10.4 17.2 %collective-permute-start.3 = (f32[8,64,128]{2,1,0:T(8,128)S(1)}, f32[8,64,128]{2,1,0:T(8,128)S(1)}, u32[]{:S(2)}, u32[]{:S(2)}) collective-permute-start(f32[8,64,128]{2,1,0:T(8,128)S(1)} %copy-done), channel_id=1, source_target_pairs={{0,4},{4,0},{1,5},{5,1},{2,6},{6,2},{3,7},{7,3},{8,12},{12,8},{9,1... | collective-permute-start | bytes 786440 | tf_op jit(solution)/shard_map/ppermute | solution.py:217
  13.0 1.1 %collective-permute-start = (s32[2,8]{1,0:T(2,128)S(1)}, s32[2,8]{1,0:T(2,128)S(1)}, u32[]{:S(2)}, u32[]{:S(2)}) collective-permute-start(s32[2,8]{1,0:T(2,128)S(1)} %bitcast.8), channel_id=1, source_target_pairs={{0,8},{8,0},{16,24},{24,16},{1,9},{9,1},{17,25},{25,17},{2,10},{10... | collective-permute-start | bytes 200 | tf_op jit(solution)/shard_map/ppermute | solution.py:213
  14.2 3.6 %collective-permute-start.1 = (s32[4,8]{1,0:T(4,128)S(1)}, s32[4,8]{1,0:T(4,128)S(1)}, u32[]{:S(2)}, u32[]{:S(2)}) collective-permute-start(s32[4,8]{1,0:T(4,128)S(1)} %pad_add_fusion.1), channel_id=1, source_target_pairs={{0,16},{8,24},{16,0},{24,8},{1,17},{9,25},{17,1},{25,9},{2,18},{10... | collective-permute-start | bytes 392 | tf_op jit(solution)/shard_map/ppermute | solution.py:213
  15.8 13.5 %collective-permute-start.8 = (f32[8,64,128]{2,1,0:T(8,128)S(1)}, f32[8,64,128]{2,1,0:T(8,128)S(1)}, u32[]{:S(2)}, u32[]{:S(2)}) collective-permute-start(f32[8,64,128]{2,1,0:T(8,128)S(1)} %copy-done), channel_id=1, source_target_pairs={{0,16},{8,24},{16,0},{24,8},{1,17},{9,25},{17,1},{25,9},{2,18},{10... | collective-permute-start | bytes 786440 | tf_op jit(solution)/shard_map/ppermute | solution.py:213
  27.7 7.2 %collective-permute-start.5 = (f32[8,64,128]{2,1,0:T(8,128)S(1)}, f32[8,64,128]{2,1,0:T(8,128)S(1)}, u32[]{:S(2)}, u32[]{:S(2)}) collective-permute-start(f32[8,64,128]{2,1,0:T(8,128)S(1)} %hold_until.1.rest_0_), channel_id=1, source_target_pairs={{0,16},{8,24},{16,0},{24,8},{1,17},{9,25},{17,1},{25,9},{2,18},{10... | collective-permute-start | bytes 786440 | tf_op jit(solution)/shard_map/ppermute | solution.py:213
  29.3 9.1 %collective-permute-start.7 = (f32[8,64,128]{2,1,0:T(8,128)S(1)}, f32[8,64,128]{2,1,0:T(8,128)S(1)}, u32[]{:S(2)}, u32[]{:S(2)}) collective-permute-start(f32[8,64,128]{2,1,0:T(8,128)S(1)} %copy-done), channel_id=1, source_target_pairs={{0,8},{8,0},{16,24},{24,16},{1,9},{9,1},{17,25},{25,17},{2,10},{10... | collective-permute-start | bytes 786440 | tf_op jit(solution)/shard_map/ppermute | solution.py:213
  29.3 9.1 %collective-permute-start.9 = (f32[8,64,128]{2,1,0:T(8,128)S(1)}, f32[8,64,128]{2,1,0:T(8,128)S(1)}, u32[]{:S(2)}, u32[]{:S(2)}) collective-permute-start(f32[8,64,128]{2,1,0:T(8,128)S(1)} %collective-permute-done.8.rest_2_), channel_id=1, source_target_pairs={{0,8},{8,0},{16,24},{24,16},{1,9},{9,1},{17,25},{25,17},{2,10},{10... | collective-permute-start | bytes 786440 | tf_op jit(solution)/shard_map/ppermute | solution.py:213
  29.8 10.4 %collective-permute-start.4 = (f32[8,64,128]{2,1,0:T(8,128)S(1)}, f32[8,64,128]{2,1,0:T(8,128)S(1)}, u32[]{:S(2)}, u32[]{:S(2)}) collective-permute-start(f32[8,64,128]{2,1,0:T(8,128)S(1)} %hold_until.1.rest_0_), channel_id=1, source_target_pairs={{0,8},{8,0},{16,24},{24,16},{1,9},{9,1},{17,25},{25,17},{2,10},{10... | collective-permute-start | bytes 786440 | tf_op jit(solution)/shard_map/ppermute | solution.py:213
  34.9 5.3 %collective-permute-start.6 = (f32[8,64,128]{2,1,0:T(8,128)S(1)}, f32[8,64,128]{2,1,0:T(8,128)S(1)}, u32[]{:S(2)}, u32[]{:S(2)}) collective-permute-start(f32[8,64,128]{2,1,0:T(8,128)S(1)} %collective-permute-done.5.rest_2_), channel_id=1, source_target_pairs={{0,8},{8,0},{16,24},{24,16},{1,9},{9,1},{17,25},{25,17},{2,10},{10... | collective-permute-start | bytes 786440 | tf_op jit(solution)/shard_map/ppermute | solution.py:213
  35.0 5.2 %collective-permute-start.2 = (s32[8,8]{1,0:T(8,128)S(1)}, s32[8,8]{1,0:T(8,128)S(1)}, u32[]{:S(2)}, u32[]{:S(2)}) collective-permute-start(s32[8,8]{1,0:T(8,128)S(1)} %pad_add_fusion.columns_ref), channel_id=1, source_target_pairs={{0,4},{4,0},{1,5},{5,1},{2,6},{6,2},{3,7},{7,3},{8,12},{12,8},{9,1... | collective-permute-start | bytes 776 | tf_op jit(solution)/shard_map/ppermute | solution.py:217

commit v7 on v6

--- a/solution.py
+++ b/solution.py
@@ -11,8 +11,8 @@
 NCR = 2
 LANES = 128
 EXTRA = 8
-HOLD_FLOPS = 4 << 30
-HOLD_BYTES = 12 << 20
+HOLD_FLOPS = 16 << 30
+HOLD_BYTES = 48 << 20
 VMEM_LIMIT = 48 * 1024 * 1024
 
 
@@ -70,7 +70,7 @@
     short_lane = lax.broadcasted_iota(jnp.int32, (EXTRA, wide), 1)
     for near in range(half):
         out_ref[near, :used] = jnp.zeros((used, wide), jnp.float32)
-    for copy in copies:
+    for copy in copies + operators:
         copy.wait()
 
     for near in range(half):
@@ -88,7 +88,6 @@
         own_row = jnp.where(second == 0, rows_ref[0, i], rows_ref[1, i])
         other_row = jnp.where(second == 0, rows_ref[1, i], rows_ref[0, i])
         dense = jnp.where(own_row == second, value, 0.0) + jnp.where(other_row == second, swapped, 0.0)
-        operators[i].wait()
         product = transposed_dot(split3(operator_ref[i], "left"), split3(dense, "right"))
         for k in range(entries):
             part = jnp.where(k < count_ref[i], product[k * block_size : (k + 1) * block_size], 0.0)

time: 57.6 us -> 46.7 us (0.81)
  waiting for transfers between devices: 17.7 us -> 11.8 us
  starting transfers between devices: 15.5 us -> 12.3 us
  Pallas kernels: 9.15 us -> 7.54 us
    ppermute x2, waiting for transfers between devices: 9.83 us -> 2.67 us  [half_swap(): return lax.ppermute(x, 'half', [(0, 1), (1, 0)])]
    all_to_all x1, waiting for transfers between devices: 0.01 us -> 3.82 us  [local(): lax.all_to_all(restricted, 'near', split_axis=0, concat_axis=0, tiled=True)]
    ppermute x8, waiting for transfers between devices: 7.83 us -> 5.35 us  [row_swap(): lax.ppermute(x, 'row', [(r, r ^ bit) for r in range(lax.axis_size('row'))])]
    ppermute x2, starting transfers between devices: 5.97 us -> 4.04 us  [half_swap(): return lax.ppermute(x, 'half', [(0, 1), (1, 0)])]
    pallas_call x1, Pallas kernels: 5.01 us -> 3.4 us  [restrict_operator(): pl.pallas_call(restrict_kernel, out_shape=(jax.ShapeDtypeStruct((columns...]
    all_to_all x1, starting transfers between devices: 5.36 us -> 3.91 us  [local(): lax.all_to_all(restricted, 'near', split_axis=0, concat_axis=0, tiled=True)]
  transfers between devices with their start and end apart: 11 -> 11, of which waited for: 4 -> 3; matrix products, arithmetic and copies ran while one was open for 0% -> 0% of each run, Pallas kernels for 3% -> 11%
where the time goes in v7:
time: 46.7 us; the launch traced here: 46.5 us
  blocking collectives  14.6 us (31%)
  starting transfers between devices  12.3 us (26%)
  waiting for transfers between devices  11.8 us (25%)
  Pallas kernels  7.54 us (16%)
    all_to_all x1, blocking collectives, local(): lax.all_to_all(sums, ('half', 'near'), split_axis=0, concat_axis=0, tiled...  14.6 us
    ppermute x8, waiting for transfers between devices, row_swap(): lax.ppermute(x, 'row', [(r, r ^ bit) for r in range(lax.axis_size('row'))])  5.35 us
    ppermute x8, starting transfers between devices, row_swap(): lax.ppermute(x, 'row', [(r, r ^ bit) for r in range(lax.axis_size('row'))])  4.31 us
    ppermute x2, starting transfers between devices, half_swap(): return lax.ppermute(x, 'half', [(0, 1), (1, 0)])  4.04 us
    all_to_all x1, starting transfers between devices, local(): lax.all_to_all(restricted, 'near', split_axis=0, concat_axis=0, tiled=True)  3.91 us
    all_to_all x1, waiting for transfers between devices, local(): lax.all_to_all(restricted, 'near', split_axis=0, concat_axis=0, tiled=True)  3.82 us
    pallas_call x2, Pallas kernels, combine(): pl.pallas_call(functools.partial(combine_kernel, far=far, slot_count=slot...  3.49 us
    pallas_call x1, Pallas kernels, restrict_operator(): pl.pallas_call(restrict_kernel, out_shape=(jax.ShapeDtypeStruct((columns...  3.4 us
  transfers between devices with their start and end apart: 11, of which 3 were waited for; matrix products, arithmetic and copies ran while one was open for 0% of the time, Pallas kernels for 11%

profile of v7, /device:TPU:0, one launch (start us, length us, event | category | flops | bytes accessed | tf_op | source)
XLA Modules:
  0.0 46.5 jit_solution(16079442668325211514)
XLA Ops:
  0.0 4.0 %collective-permute-start.3 = (f32[8,64,128]{2,1,0:T(8,128)}, f32[8,64,128]{2,1,0:T(8,128)S(1)}, u32[]{:S(2)}, u32[]{:S(2)}) collective-permute-start(f32[8,64,128]{2,1,0:T(8,128)} %rest_0_.1), channel_id=1, source_target_pairs={{0,4},{4,0},{1,5},{5,1},{2,6},{6,2},{3,7},{7,3},{8,12},{12,8},{9,1... | collective-permute-start | bytes 786440 | tf_op jit(solution)/shard_map/ppermute | solution.py:216
  4.0 1.5 %collective-permute-start.8 = (f32[8,64,128]{2,1,0:T(8,128)}, f32[8,64,128]{2,1,0:T(8,128)S(1)}, u32[]{:S(2)}, u32[]{:S(2)}) collective-permute-start(f32[8,64,128]{2,1,0:T(8,128)} %rest_0_.1), channel_id=1, source_target_pairs={{0,16},{8,24},{16,0},{24,8},{1,17},{9,25},{17,1},{25,9},{2,18},{10... | collective-permute-start | bytes 786440 | tf_op jit(solution)/shard_map/ppermute | solution.py:212
  5.6 0.0 collective-permute-start
  5.6 3.4 %restrict_operator.1 = (f32[4,520,128]{2,1,0:T(8,128)}, f32[8,128]{1,0:T(8,128)}) custom-call(s32[8]{0:T(128)} %count_any.1, s32[8,8]{1,0:T(8,128)} %slot_any.1, s32[2,8]{1,0:T(2,128)} %bitcast.12, s32[4,8]{1,0:T(4,128)} %bitcast.11, f32[8,64,128]{2,1,0:T(8,128)} %restrict_any.1, f32[8,64,512]{2,1,0:T(8,128)} %operator_any.1), custom_call_target="tpu_custom_call" | custom-call | flops 201326592 | bytes 4194304 | tf_op jit(solution)/shard_map/restrict_operator/pallas_call | solution.py:106
  9.0 0.0 collective-permute-done
  9.0 0.6 %collective-permute-start.1 = (s32[4,8]{1,0:T(4,128)S(1)}, s32[4,8]{1,0:T(4,128)S(1)}, u32[]{:S(2)}, u32[]{:S(2)}) collective-permute-start(s32[4,8]{1,0:T(4,128)S(1)} %pad_add_fusion.1), channel_id=1, source_target_pairs={{0,16},{8,24},{16,0},{24,8},{1,17},{9,25},{17,1},{25,9},{2,18},{10... | collective-permute-start | bytes 392 | tf_op jit(solution)/shard_map/ppermute | solution.py:212
  9.6 3.9 %all-to-all-start = ((f32[4,520,128]{2,1,0:T(8,128)}), f32[4,520,128]{2,1,0:T(8,128)S(1)}, u32[]{:S(2)}, u32[]{:S(2)}) async-start(f32[4,520,128]{2,1,0:T(8,128)} %get-tuple-element.7), calls=%async_computation | async-start | bytes 2129920 | tf_op jit(solution)/shard_map/all_to_all | solution.py:256
  13.5 2.7 %collective-permute-done.3.blocks_ref = f32[8,64,128]{2,1,0:T(8,128)S(1)} collective-permute-done((f32[8,64,128]{2,1,0:T(8,128)}, f32[8,64,128]{2,1,0:T(8,128)S(1)}, u32[]{:S(2)}, u32[]{:S(2)}) %collective-permute-start.3) | collective-permute-done | bytes 262176 | tf_op jit(solution)/shard_map/ppermute | solution.py:216
  16.2 1.6 %collective-permute-start.5 = (f32[8,64,128]{2,1,0:T(8,128)S(1)}, f32[8,64,128]{2,1,0:T(8,128)S(1)}, u32[]{:S(2)}, u32[]{:S(2)}) collective-permute-start(f32[8,64,128]{2,1,0:T(8,128)S(1)} %hold_until.1.rest_0_), channel_id=1, source_target_pairs={{0,16},{8,24},{16,0},{24,8},{1,17},{9,25},{17,1},{25,9},{2,18},{10... | collective-permute-start | bytes 786440 | tf_op jit(solution)/shard_map/ppermute | solution.py:212
  17.8 0.0 collective-permute-start.7
  17.8 0.0 collective-permute-done.8.rest_2_
  17.8 0.5 %collective-permute-start.9 = (f32[8,64,128]{2,1,0:T(8,128)S(1)}, f32[8,64,128]{2,1,0:T(8,128)S(1)}, u32[]{:S(2)}, u32[]{:S(2)}) collective-permute-start(f32[8,64,128]{2,1,0:T(8,128)S(1)} %collective-permute-done.8.rest_2_), channel_id=1, source_target_pairs={{0,8},{8,0},{16,24},{24,16},{1,9},{9,1},{17,25},{25,17},{2,10},{10... | collective-permute-start | bytes 786440 | tf_op jit(solution)/shard_map/ppermute | solution.py:212
  18.4 0.1 collective-permute-start.4
  18.4 5.3 %collective-permute-done.5.rest_2_ = f32[8,64,128]{2,1,0:T(8,128)S(1)} collective-permute-done((f32[8,64,128]{2,1,0:T(8,128)S(1)}, f32[8,64,128]{2,1,0:T(8,128)S(1)}, u32[]{:S(2)}, u32[]{:S(2)}) %collective-permute-start.5) | collective-permute-done | bytes 262176 | tf_op jit(solution)/shard_map/ppermute | solution.py:212
  23.8 0.1 pad_add_fusion.2.own_ref
  23.8 0.0 collective-permute-start.2
  23.8 0.0 collective-permute-done.7.rest_1_
  23.9 3.8 %all-to-all-done.restricted_ref = f32[4,520,128]{2,1,0:T(8,128)S(1)} async-done(((f32[4,520,128]{2,1,0:T(8,128)}), f32[4,520,128]{2,1,0:T(8,128)S(1)}, u32[]{:S(2)}, u32[]{:S(2)}) %all-to-all-start) | async-done | bytes 1064992 | tf_op jit(solution)/shard_map/all_to_all | solution.py:256
  27.7 1.8 %combine_near.1.rest_4_ = f32[8,64,128]{2,1,0:T(8,128)S(1)} custom-call(s32[2]{0:T(128)S(1)} %pad_add_fusion.2.own_ref, s32[8,8]{1,0:T(8,128)S(1)} %pad_add_fusion.columns_ref, f32[4,520,128]{2,1,0:T(8,128)S(1)} %all-to-all-done.restricted_ref, f32[8,64,128]{2,1,0:T(8,128)S(1)} %copy-done, f32[8,64,128]{2,1,0:T(8,128)S(1)} %collective-permute-done.7.rest_1_, ...), custom_call_target="tpu_custom_call" | custom-call | flops 134217728 | bytes 2097152 | tf_op jit(solution)/shard_map/combine_near/pallas_call | solution.py:171
  29.5 0.0 collective-permute-done.2.columns_ref
  29.5 0.0 collective-permute-done.6.rest_3_
  29.5 1.7 %combine_far.1 = f32[8,64,128]{2,1,0:T(8,128)S(1)} custom-call(s32[2]{0:T(128)S(1)} %pad_add_fusion.2.own_ref, s32[8,8]{1,0:T(8,128)S(1)} %collective-permute-done.2.columns_ref, f32[4,520,128]{2,1,0:T(8,128)S(1)} %all-to-all-done.restricted_ref, f32[8,64,128]{2,1,0:T(8,128)S(1)} %hold_until.1.rest_0_, f32[8,64,128]{2,1,0:T(8,128)S(1)} %collective-permute-done.4.rest_1_, ...), custom_call_target="tpu_custom_call" | custom-call | flops 134217728 | bytes 2097152 | tf_op jit(solution)/shard_map/combine_far/pallas_call | solution.py:171
  31.2 14.6 %all_to_all.10.parts_ref = f32[8,64,128]{2,1,0:T(8,128)S(1)} all-to-all(f32[8,64,128]{2,1,0:T(8,128)S(1)} %combine_far.1), channel_id=1, replica_groups=mesh['row'=4,'half'=2,'near'=4] {'half','near'}, dimensions={0} | all-to-all | bytes 524288 | tf_op jit(solution)/shard_map/all_to_all | solution.py:264
  45.8 0.6 %add_up.1 = f32[64,128]{1,0:T(8,128)} custom-call(f32[8,64,128]{2,1,0:T(8,128)S(1)} %all_to_all.10.parts_ref), custom_call_target="tpu_custom_call" | custom-call | tf_op jit(solution)/shard_map/add_up/pallas_call | solution.py:201
  (13 shorter events, 0.1 us)
Async XLA Ops:
  0.0 9.0 %copy-start.2 = (s32[8,2]{0,1:T(2,128)S(1)}, s32[8,2]{0,1:T(2,128)}, u32[]{:S(2)}) copy-start(s32[8,2]{0,1:T(2,128)} %param.13) | copy-start | bytes 196
  0.0 16.2 %collective-permute-start.3 = (f32[8,64,128]{2,1,0:T(8,128)}, f32[8,64,128]{2,1,0:T(8,128)S(1)}, u32[]{:S(2)}, u32[]{:S(2)}) collective-permute-start(f32[8,64,128]{2,1,0:T(8,128)} %rest_0_.1), channel_id=1, source_target_pairs={{0,4},{4,0},{1,5},{5,1},{2,6},{6,2},{3,7},{7,3},{8,12},{12,8},{9,1... | collective-permute-start | bytes 786440 | tf_op jit(solution)/shard_map/ppermute | solution.py:216
  4.0 13.8 %collective-permute-start.8 = (f32[8,64,128]{2,1,0:T(8,128)}, f32[8,64,128]{2,1,0:T(8,128)S(1)}, u32[]{:S(2)}, u32[]{:S(2)}) collective-permute-start(f32[8,64,128]{2,1,0:T(8,128)} %rest_0_.1), channel_id=1, source_target_pairs={{0,16},{8,24},{16,0},{24,8},{1,17},{9,25},{17,1},{25,9},{2,18},{10... | collective-permute-start | bytes 786440 | tf_op jit(solution)/shard_map/ppermute | solution.py:212
  5.6 3.4 %collective-permute-start = (s32[2,8]{1,0:T(2,128)}, s32[2,8]{1,0:T(2,128)S(1)}, u32[]{:S(2)}, u32[]{:S(2)}) collective-permute-start(s32[2,8]{1,0:T(2,128)} %bitcast.8), channel_id=1, source_target_pairs={{0,8},{8,0},{16,24},{24,16},{1,9},{9,1},{17,25},{25,17},{2,10},{10... | collective-permute-start | bytes 200 | tf_op jit(solution)/shard_map/ppermute | solution.py:212
  9.0 4.5 %collective-permute-start.1 = (s32[4,8]{1,0:T(4,128)S(1)}, s32[4,8]{1,0:T(4,128)S(1)}, u32[]{:S(2)}, u32[]{:S(2)}) collective-permute-start(s32[4,8]{1,0:T(4,128)S(1)} %pad_add_fusion.1), channel_id=1, source_target_pairs={{0,16},{8,24},{16,0},{24,8},{1,17},{9,25},{17,1},{25,9},{2,18},{10... | collective-permute-start | bytes 392 | tf_op jit(solution)/shard_map/ppermute | solution.py:212
  9.6 6.6 %copy-start.1 = (f32[8,128]{1,0:T(8,128)S(1)}, f32[8,128]{1,0:T(8,128)}, u32[]{:S(2)}) copy-start(f32[8,128]{1,0:T(8,128)} %get-tuple-element.8.mark_ref) | copy-start | bytes 12292
  9.6 18.1 %all-to-all-start = ((f32[4,520,128]{2,1,0:T(8,128)}), f32[4,520,128]{2,1,0:T(8,128)S(1)}, u32[]{:S(2)}, u32[]{:S(2)}) async-start(f32[4,520,128]{2,1,0:T(8,128)} %get-tuple-element.7), calls=%async_computation | async-start | bytes 2129920 | tf_op jit(solution)/shard_map/all_to_all | solution.py:256
  16.2 1.7 %copy-start = (f32[8,64,128]{2,1,0:T(8,128)S(1)}, f32[8,64,128]{2,1,0:T(8,128)}, u32[]{:S(2)}) copy-start(f32[8,64,128]{2,1,0:T(8,128)} %rest_0_.1) | copy-start | bytes 786436
  16.2 7.6 %collective-permute-start.5 = (f32[8,64,128]{2,1,0:T(8,128)S(1)}, f32[8,64,128]{2,1,0:T(8,128)S(1)}, u32[]{:S(2)}, u32[]{:S(2)}) collective-permute-start(f32[8,64,128]{2,1,0:T(8,128)S(1)} %hold_until.1.rest_0_), channel_id=1, source_target_pairs={{0,16},{8,24},{16,0},{24,8},{1,17},{9,25},{17,1},{25,9},{2,18},{10... | collective-permute-start | bytes 786440 | tf_op jit(solution)/shard_map/ppermute | solution.py:212
  17.8 6.0 %collective-permute-start.7 = (f32[8,64,128]{2,1,0:T(8,128)S(1)}, f32[8,64,128]{2,1,0:T(8,128)S(1)}, u32[]{:S(2)}, u32[]{:S(2)}) collective-permute-start(f32[8,64,128]{2,1,0:T(8,128)S(1)} %copy-done), channel_id=1, source_target_pairs={{0,8},{8,0},{16,24},{24,16},{1,9},{9,1},{17,25},{25,17},{2,10},{10... | collective-permute-start | bytes 786440 | tf_op jit(solution)/shard_map/ppermute | solution.py:212
  17.8 6.0 %collective-permute-start.9 = (f32[8,64,128]{2,1,0:T(8,128)S(1)}, f32[8,64,128]{2,1,0:T(8,128)S(1)}, u32[]{:S(2)}, u32[]{:S(2)}) collective-permute-start(f32[8,64,128]{2,1,0:T(8,128)S(1)} %collective-permute-done.8.rest_2_), channel_id=1, source_target_pairs={{0,8},{8,0},{16,24},{24,16},{1,9},{9,1},{17,25},{25,17},{2,10},{10... | collective-permute-start | bytes 786440 | tf_op jit(solution)/shard_map/ppermute | solution.py:212
  18.4 11.1 %collective-permute-start.4 = (f32[8,64,128]{2,1,0:T(8,128)S(1)}, f32[8,64,128]{2,1,0:T(8,128)S(1)}, u32[]{:S(2)}, u32[]{:S(2)}) collective-permute-start(f32[8,64,128]{2,1,0:T(8,128)S(1)} %hold_until.1.rest_0_), channel_id=1, source_target_pairs={{0,8},{8,0},{16,24},{24,16},{1,9},{9,1},{17,25},{25,17},{2,10},{10... | collective-permute-start | bytes 786440 | tf_op jit(solution)/shard_map/ppermute | solution.py:212
  23.8 5.7 %collective-permute-start.6 = (f32[8,64,128]{2,1,0:T(8,128)S(1)}, f32[8,64,128]{2,1,0:T(8,128)S(1)}, u32[]{:S(2)}, u32[]{:S(2)}) collective-permute-start(f32[8,64,128]{2,1,0:T(8,128)S(1)} %collective-permute-done.5.rest_2_), channel_id=1, source_target_pairs={{0,8},{8,0},{16,24},{24,16},{1,9},{9,1},{17,25},{25,17},{2,10},{10... | collective-permute-start | bytes 786440 | tf_op jit(solution)/shard_map/ppermute | solution.py:212
  23.8 5.6 %collective-permute-start.2 = (s32[8,8]{1,0:T(8,128)S(1)}, s32[8,8]{1,0:T(8,128)S(1)}, u32[]{:S(2)}, u32[]{:S(2)}) collective-permute-start(s32[8,8]{1,0:T(8,128)S(1)} %pad_add_fusion.columns_ref), channel_id=1, source_target_pairs={{0,4},{4,0},{1,5},{5,1},{2,6},{6,2},{3,7},{7,3},{8,12},{12,8},{9,1... | collective-permute-start | bytes 776 | tf_op jit(solution)/shard_map/ppermute | solution.py:216

commit v8 on v7

--- a/solution.py
+++ b/solution.py
@@ -12,7 +12,6 @@
 LANES = 128
 EXTRA = 8
 HOLD_FLOPS = 16 << 30
-HOLD_BYTES = 48 << 20
 VMEM_LIMIT = 48 * 1024 * 1024
 
 
@@ -27,24 +26,24 @@
     return lax.dot_general(left, right, (((0,), (0,)), ((), ())), preferred_element_type=jnp.float32)
 
 
-def hold_kernel(columns_ref, mark_ref, blocks_ref, out_ref):
+def hold_kernel(mark_ref, blocks_ref, out_ref):
     out_ref[...] = blocks_ref[...]
 
 
-def hold_until(columns, mark, blocks):
+def hold_until(mark, blocks, flops):
     return pl.pallas_call(
         hold_kernel,
         out_shape=jax.ShapeDtypeStruct(blocks.shape, blocks.dtype),
-        in_specs=[pl.BlockSpec(memory_space=pltpu.VMEM)] * 3,
+        in_specs=[pl.BlockSpec(memory_space=pltpu.VMEM)] * 2,
         out_specs=pl.BlockSpec(memory_space=pltpu.VMEM),
         compiler_params=pltpu.CompilerParams(vmem_limit_bytes=VMEM_LIMIT),
-        cost_estimate=pl.CostEstimate(flops=HOLD_FLOPS, bytes_accessed=HOLD_BYTES, transcendentals=0),
+        cost_estimate=pl.CostEstimate(flops=flops, bytes_accessed=flops >> 8, transcendentals=0),
         name="hold_until",
-    )(columns, mark, blocks)
+    )(mark, blocks)
 
 
 def restrict_kernel(
-    count_any, slot_any, rows_any, fetch_any, restrict_any, operator_any, out_ref, mark_ref,
+    count_any, slot_any, rows_any, fetch_any, restrict_any, operator_any, columns_ref, out_ref, mark_ref,
     count_ref, slot_ref, rows_ref, fetch_ref, restrict_ref, operator_ref, sems, operator_sems,
 ):
     fine_rows, block_size, _ = operator_ref.shape
@@ -80,7 +79,7 @@
                 wanted = fetch_ref[s, side * half + near]
                 value = jnp.where(short_lane == side * slot_count + s, wanted, value)
         out_ref[near, used:] = value.astype(jnp.float32)
-    mark_ref[...] = out_ref[0, used:]
+    mark_ref[...] = columns_ref[...]
 
     for i in range(fine_rows):
         value = restrict_ref[i]
@@ -97,7 +96,9 @@
             out_ref[lax.rem(peer, half), pl.ds(start, block_size)] += part
 
 
-def restrict_operator(operator_count, operator_slot, restrict_rows, fetch, operator_blocks, restrict_blocks):
+def restrict_operator(
+    operator_count, operator_slot, restrict_rows, fetch, operator_blocks, restrict_blocks, prolong_columns
+):
     fine_rows, block_size, width = operator_blocks.shape
     slot_count, columns = fetch.shape
     wide = NCR * block_size
@@ -107,9 +108,9 @@
         restrict_kernel,
         out_shape=(
             jax.ShapeDtypeStruct((columns // 2, rows, wide), jnp.float32),
-            jax.ShapeDtypeStruct((EXTRA, wide), jnp.float32),
-        ),
-        in_specs=[pl.BlockSpec(memory_space=pltpu.HBM)] * 6,
+            jax.ShapeDtypeStruct(prolong_columns.shape, prolong_columns.dtype),
+        ),
+        in_specs=[pl.BlockSpec(memory_space=pltpu.HBM)] * 6 + [pl.BlockSpec(memory_space=pltpu.VMEM)],
         out_specs=[pl.BlockSpec(memory_space=pltpu.VMEM)] * 2,
         scratch_shapes=[pltpu.SMEM(x.shape, x.dtype) for x in small]
         + [pltpu.VMEM(x.shape, x.dtype) for x in (restrict_blocks, operator_blocks)]
@@ -118,40 +119,33 @@
             flops=6 * fine_rows * block_size * width * wide, bytes_accessed=4 << 20, transcendentals=0
         ),
         name="restrict_operator",
-    )(*small, restrict_blocks, operator_blocks)
-
-
-def combine_kernel(own_ref, columns_ref, restricted_ref, *rest, far, slot_count, fine_rows, entries):
-    out_ref, held_ref, table_ref, index_ref, sem, held_sem = rest[-6:]
-    pieces, so_far = (rest[:-7], rest[-7]) if far else (rest[:-6], None)
+    )(*small, restrict_blocks, operator_blocks, prolong_columns)
+
+
+def combine_kernel(own_ref, columns_ref, restricted_ref, *rest, slot_count, fine_rows, entries):
+    pieces, (out_ref, held_ref, table_ref, index_ref, sem) = rest[:-5], rest[-5:]
     half = restricted_ref.shape[0]
+    rows = len(pieces) // 2
     block_size = out_ref.shape[1]
     columns = 2 * half
     used = 2 * slot_count * block_size
-    side = 1 - own_ref[1] if far else own_ref[1]
-
-    if not far:
-        own_copy = pltpu.make_async_copy(pieces[0], held_ref.at[0], held_sem)
-        own_copy.start()
-    table_ref[...] = jnp.zeros_like(table_ref)
+
     for near in range(half):
         table_ref[near : near + 1] = restricted_ref[near, used : used + 1].astype(jnp.int32)
     copy = pltpu.make_async_copy(table_ref, index_ref, sem)
     copy.start()
     for i, piece in enumerate(pieces):
-        if far or i:
-            held_ref[i] = piece[...]
-    out_ref[...] = so_far[...] if far else jnp.zeros_like(out_ref)
+        held_ref[i] = piece[...]
+    out_ref[...] = jnp.zeros_like(out_ref)
     copy.wait()
-    if not far:
-        own_copy.wait()
 
     def step(i, carry):
-        near = lax.div(i, slot_count)
-        place = side * slot_count + lax.rem(i, slot_count)
+        near = lax.div(i, 2 * slot_count)
+        place = lax.rem(i, 2 * slot_count)
         wanted = index_ref[near, place]
         inside = lax.rem(wanted, fine_rows)
-        piece = lax.div(wanted, fine_rows * columns) ^ own_ref[0]
+        far = lax.div(place, slot_count) ^ own_ref[1]
+        piece = far * rows + (lax.div(wanted, fine_rows * columns) ^ own_ref[0])
         restricted = restricted_ref[near, pl.ds(pl.multiple_of(place * block_size, block_size), block_size)]
         product = transposed_dot(split3(held_ref[piece, inside], "left"), split3(restricted, "right"))
         for m in range(entries):
@@ -159,35 +153,31 @@
             out_ref[column] += product[m * block_size : (m + 1) * block_size]
         return carry
 
-    lax.fori_loop(0, half * slot_count, step, 0, unroll=16)
-
-
-def combine(own, columns, restricted, pieces, so_far, coarse_all, slot_count):
+    lax.fori_loop(0, half * 2 * slot_count, step, 0, unroll=16)
+
+
+def combine(own, columns, restricted, pieces, coarse_all, slot_count):
     half, _, wide = restricted.shape
     fine_rows, block_size, width = pieces[0].shape
     table_rows = -(-half // 8) * 8
-    far = len(so_far)
-    first = pl.BlockSpec(memory_space=pltpu.VMEM if far else pltpu.HBM)
     return pl.pallas_call(
         functools.partial(
-            combine_kernel, far=far, slot_count=slot_count, fine_rows=fine_rows, entries=width // block_size
+            combine_kernel, slot_count=slot_count, fine_rows=fine_rows, entries=width // block_size
         ),
         out_shape=jax.ShapeDtypeStruct((coarse_all, block_size, wide), jnp.float32),
         in_specs=[pl.BlockSpec(memory_space=pltpu.SMEM)] * 2
-        + [pl.BlockSpec(memory_space=pltpu.VMEM), first]
-        + [pl.BlockSpec(memory_space=pltpu.VMEM)] * (len(pieces) - 1 + far),
+        + [pl.BlockSpec(memory_space=pltpu.VMEM)] * (1 + len(pieces)),
         out_specs=pl.BlockSpec(memory_space=pltpu.VMEM),
         scratch_shapes=[
             pltpu.VMEM((len(pieces), fine_rows, block_size, width), jnp.float32),
             pltpu.VMEM((table_rows, LANES), jnp.int32),
             pltpu.SMEM((table_rows, LANES), jnp.int32),
             pltpu.SemaphoreType.DMA,
-            pltpu.SemaphoreType.DMA,
         ],
         compiler_params=pltpu.CompilerParams(vmem_limit_bytes=VMEM_LIMIT),
-        cost_estimate=pl.CostEstimate(flops=1 << 27, bytes_accessed=2 << 20, transcendentals=0),
-        name="combine_far" if far else "combine_near",
-    )(own, columns, restricted, *pieces, *so_far)
+        cost_estimate=pl.CostEstimate(flops=1 << 28, bytes_accessed=4 << 20, transcendentals=0),
+        name="combine",
+    )(own, columns, restricted, *pieces)
 
 
 def add_kernel(parts_ref, out_ref):
@@ -216,12 +206,14 @@
     return lax.ppermute(x, "half", [(0, 1), (1, 0)])
 
 
-def spread_over_rows(blocks, rows):
+def spread_over_rows(blocks, rows, mark=None):
     pieces = {0: blocks}
     bit = rows // 2
     while bit:
         for mask in list(pieces):
             pieces[mask ^ bit] = row_swap(pieces[mask], bit)
+        if mark is not None and bit == rows // 2:
+            pieces[bit] = hold_until(mark, pieces[bit], 1 << 20)
         bit //= 2
     return [pieces[mask] for mask in range(rows)]
 
@@ -250,17 +242,22 @@
     own = jnp.stack([lax.axis_index("row"), lax.axis_index("half")])
 
     far_blocks = half_swap(prolong_blocks)
-    restricted, mark = restrict_operator(
-        operator_count, operator_slot, restrict_rows.T, fetch, operator_blocks, restrict_blocks
+    restricted, own_columns = restrict_operator(
+        operator_count,
+        operator_slot,
+        restrict_rows.T,
+        fetch,
+        operator_blocks,
+        restrict_blocks,
+        prolong_cols.T,
     )
-    restricted = lax.all_to_all(restricted, "near", split_axis=0, concat_axis=0, tiled=True)
-    near_columns = columns_of_rows(prolong_cols.T, rows)
-    far_columns = half_swap(near_columns)
-    far_blocks = hold_until(near_columns, mark, far_blocks)
+    restricted_here = lax.all_to_all(restricted, "near", split_axis=0, concat_axis=0, tiled=True)
+    near_columns = columns_of_rows(own_columns, rows)
+    all_columns = jnp.concatenate([near_columns, half_swap(near_columns)], axis=0)
+    far_blocks = hold_until(own_columns, far_blocks, HOLD_FLOPS)
     near_pieces = spread_over_rows(prolong_blocks, rows)
-    far_pieces = spread_over_rows(far_blocks, rows)
-    sums = combine(own, near_columns, restricted, near_pieces, (), NCR * rows, slot_count)
-    sums = combine(own, far_columns, restricted, far_pieces, (sums,), NCR * rows, slot_count)
+    far_pieces = spread_over_rows(far_blocks, rows, all_columns)
+    sums = combine(own, all_columns, restricted_here, near_pieces + far_pieces, NCR * rows, slot_count)
     parts = lax.all_to_all(sums, ("half", "near"), split_axis=0, concat_axis=0, tiled=True)
     return add_up(parts).T
 

time: 46.7 us -> 49.5 us (1.060)
  waiting for transfers between devices: 11.8 us -> 14 us
  blocking collectives: 14.6 us -> 15.5 us
    ppermute x2, waiting for transfers between devices: 2.67 us -> 7.04 us  [half_swap(): return lax.ppermute(x, 'half', [(0, 1), (1, 0)])]
    all_to_all x1, waiting for transfers between devices: 3.82 us -> 0.01 us  [local(): lax.all_to_all(restricted, 'near', split_axis=0, concat_axis=0, tiled=True)]
    ppermute x8, waiting for transfers between devices: 5.35 us -> 6.94 us  [row_swap(): lax.ppermute(x, 'row', [(r, r ^ bit) for r in range(lax.axis_size('row'))])]
    pallas_call x2 -> x1, Pallas kernels: 3.49 us -> 2.32 us  [combine(): pl.pallas_call(functools.partial(combine_kernel, slot_count=slot_count, f...]
    all_to_all x1, blocking collectives: 14.6 us -> 15.5 us  [local(): lax.all_to_all(sums, ('half', 'near'), split_axis=0, concat_axis=0, tiled...]
    pallas_call x1, Pallas kernels: 3.4 us -> 4.09 us  [restrict_operator(): pl.pallas_call(restrict_kernel, out_shape=(jax.ShapeDtypeStruct((columns...]
  transfers between devices with their start and end apart: 11 -> 11, of which waited for: 3 -> 5; matrix products, arithmetic and copies ran while one was open for 0% -> 0% of each run, Pallas kernels for 11% -> 8%
where the time goes in v8:
time: 49.5 us; the launch traced here: 49.2 us
  blocking collectives  15.5 us (31%)
  waiting for transfers between devices  14 us (28%)
  starting transfers between devices  12.4 us (25%)
  Pallas kernels  7.07 us (14%)
    all_to_all x1, blocking collectives, local(): lax.all_to_all(sums, ('half', 'near'), split_axis=0, concat_axis=0, tiled...  15.5 us
    ppermute x2, waiting for transfers between devices, half_swap(): return lax.ppermute(x, 'half', [(0, 1), (1, 0)])  7.04 us
    ppermute x8, waiting for transfers between devices, row_swap(): lax.ppermute(x, 'row', [(r, r ^ bit) for r in range(lax.axis_size('row'))])  6.94 us
    ppermute x8, starting transfers between devices, row_swap(): lax.ppermute(x, 'row', [(r, r ^ bit) for r in range(lax.axis_size('row'))])  4.54 us
    ppermute x2, starting transfers between devices, half_swap(): return lax.ppermute(x, 'half', [(0, 1), (1, 0)])  4.11 us
    pallas_call x1, Pallas kernels, restrict_operator(): pl.pallas_call(restrict_kernel, out_shape=(jax.ShapeDtypeStruct((columns...  4.09 us
    all_to_all x1, starting transfers between devices, local(): lax.all_to_all(restricted, 'near', split_axis=0, concat_axis=0, tiled=True)  3.78 us
    pallas_call x1, Pallas kernels, combine(): pl.pallas_call(functools.partial(combine_kernel, slot_count=slot_count, f...  2.32 us
  transfers between devices with their start and end apart: 11, of which 5 were waited for; matrix products, arithmetic and copies ran while one was open for 0% of the time, Pallas kernels for 8%

profile of v8, /device:TPU:0, one launch (start us, length us, event | category | flops | bytes accessed | tf_op | source)
XLA Modules:
  0.0 49.2 jit_solution(16584910250554269542)
XLA Ops:
  0.0 4.0 %collective-permute-start.6 = (f32[8,64,128]{2,1,0:T(8,128)}, f32[8,64,128]{2,1,0:T(8,128)S(1)}, u32[]{:S(2)}, u32[]{:S(2)}) collective-permute-start(f32[8,64,128]{2,1,0:T(8,128)} %rest_0_.1), channel_id=1, source_target_pairs={{0,4},{4,0},{1,5},{5,1},{2,6},{6,2},{3,7},{7,3},{8,12},{12,8},{9,1... | collective-permute-start | bytes 786440 | tf_op jit(solution)/shard_map/ppermute | solution.py:206
  4.0 1.5 %collective-permute-start.4 = (f32[8,64,128]{2,1,0:T(8,128)}, f32[8,64,128]{2,1,0:T(8,128)S(1)}, u32[]{:S(2)}, u32[]{:S(2)}) collective-permute-start(f32[8,64,128]{2,1,0:T(8,128)} %rest_0_.1), channel_id=1, source_target_pairs={{0,16},{8,24},{16,0},{24,8},{1,17},{9,25},{17,1},{25,9},{2,18},{10... | collective-permute-start | bytes 786440 | tf_op jit(solution)/shard_map/ppermute | solution.py:202
  5.6 4.1 %restrict_operator.1 = (f32[4,520,128]{2,1,0:T(8,128)}, s32[2,8]{1,0:T(2,128)}) custom-call(s32[8]{0:T(128)} %count_any.1, s32[8,8]{1,0:T(8,128)} %slot_any.1, s32[2,8]{1,0:T(2,128)} %bitcast.9, s32[4,8]{1,0:T(4,128)} %bitcast.8, f32[8,64,128]{2,1,0:T(8,128)} %restrict_any.1, f32[8,64,512]{2,1,0:T(8,128)} %operator_any.1, s32[2,8]{1,0:T(2,128)} %bitcast.10), custom_call_target="tpu_custom_call" | custom-call | flops 201326592 | bytes 4194304 | tf_op jit(solution)/shard_map/restrict_operator/pallas_call | solution.py:107
  9.7 0.1 collective-permute-start
  9.7 3.8 %all-to-all-start = ((f32[4,520,128]{2,1,0:T(8,128)}), f32[4,520,128]{2,1,0:T(8,128)S(1)}, u32[]{:S(2)}, u32[]{:S(2)}) async-start(f32[4,520,128]{2,1,0:T(8,128)} %get-tuple-element.8), calls=%async_computation | async-start | bytes 2129920 | tf_op jit(solution)/shard_map/all_to_all | solution.py:254
  13.5 2.6 %collective-permute-done.6.blocks_ref = f32[8,64,128]{2,1,0:T(8,128)S(1)} collective-permute-done((f32[8,64,128]{2,1,0:T(8,128)}, f32[8,64,128]{2,1,0:T(8,128)S(1)}, u32[]{:S(2)}, u32[]{:S(2)}) %collective-permute-start.6) | collective-permute-done | bytes 262176 | tf_op jit(solution)/shard_map/ppermute | solution.py:206
  16.2 1.7 %collective-permute-start.8 = (f32[8,64,128]{2,1,0:T(8,128)S(1)}, f32[8,64,128]{2,1,0:T(8,128)S(1)}, u32[]{:S(2)}, u32[]{:S(2)}) collective-permute-start(f32[8,64,128]{2,1,0:T(8,128)S(1)} %hold_until.2.rest_4_), channel_id=1, source_target_pairs={{0,16},{8,24},{16,0},{24,8},{1,17},{9,25},{17,1},{25,9},{2,18},{10... | collective-permute-start | bytes 786440 | tf_op jit(solution)/shard_map/ppermute | solution.py:202
  17.9 0.0 collective-permute-done
  17.9 0.5 collective-permute-start.1
  18.4 5.4 %collective-permute-done.1 = s32[4,8]{1,0:T(4,128)S(1)} collective-permute-done((s32[4,8]{1,0:T(4,128)S(1)}, s32[4,8]{1,0:T(4,128)S(1)}, u32[]{:S(2)}, u32[]{:S(2)}) %collective-permute-start.1) | collective-permute-done | bytes 160 | tf_op jit(solution)/shard_map/ppermute | solution.py:202
  23.8 0.1 collective-permute-start.2
  23.9 0.1 collective-permute-start.3
  24.0 4.4 %collective-permute-done.2 = s32[8,8]{1,0:T(8,128)S(1)} collective-permute-done((s32[8,8]{1,0:T(8,128)S(1)}, s32[8,8]{1,0:T(8,128)S(1)}, u32[]{:S(2)}, u32[]{:S(2)}) %collective-permute-start.2) | collective-permute-done | bytes 288 | tf_op jit(solution)/shard_map/ppermute | solution.py:206
  28.4 0.1 collective-permute-start.7
  28.5 0.0 collective-permute-done.4.rest_2_
  28.5 0.5 collective-permute-start.5
  29.0 0.0 collective-permute-done.8.blocks_ref
  29.0 0.2 collective-permute-start.9
  29.1 0.1 pad_add_fusion.3.own_ref
  29.2 1.1 %collective-permute-done.5.rest_3_ = f32[8,64,128]{2,1,0:T(8,128)S(1)} collective-permute-done((f32[8,64,128]{2,1,0:T(8,128)S(1)}, f32[8,64,128]{2,1,0:T(8,128)S(1)}, u32[]{:S(2)}, u32[]{:S(2)}) %collective-permute-start.5) | collective-permute-done | bytes 262176 | tf_op jit(solution)/shard_map/ppermute | solution.py:202
  30.4 0.4 collective-permute-done.9.rest_7_
  30.7 2.3 %combine.1 = f32[8,64,128]{2,1,0:T(8,128)S(1)} custom-call(s32[2]{0:T(128)S(1)} %pad_add_fusion.3.own_ref, s32[16,8]{1,0:T(8,128)S(1)} %pad_add_fusion.mark_ref.columns_ref, f32[4,520,128]{2,1,0:T(8,128)S(1)} %all-to-all-done.restricted_ref, f32[8,64,128]{2,1,0:T(8,128)S(1)} %copy-done, f32[8,64,128]{2,1,0:T(8,128)S(1)} %collective-permute-done.3.rest_1_, ...), custom_call_target="tpu_custom_call" | custom-call | flops 268435456 | bytes 4194304 | tf_op jit(solution)/shard_map/combine/pallas_call | solution.py:163
  33.1 15.5 %all_to_all.10.parts_ref = f32[8,64,128]{2,1,0:T(8,128)S(1)} all-to-all(f32[8,64,128]{2,1,0:T(8,128)S(1)} %combine.1), channel_id=1, replica_groups=mesh['row'=4,'half'=2,'near'=4] {'half','near'}, dimensions={0} | all-to-all | bytes 524288 | tf_op jit(solution)/shard_map/all_to_all | solution.py:261
  48.6 0.6 %add_up.1 = f32[64,128]{1,0:T(8,128)} custom-call(f32[8,64,128]{2,1,0:T(8,128)S(1)} %all_to_all.10.parts_ref), custom_call_target="tpu_custom_call" | custom-call | tf_op jit(solution)/shard_map/add_up/pallas_call | solution.py:191
  (12 shorter events, 0.1 us)
Async XLA Ops:
  0.0 16.2 %collective-permute-start.6 = (f32[8,64,128]{2,1,0:T(8,128)}, f32[8,64,128]{2,1,0:T(8,128)S(1)}, u32[]{:S(2)}, u32[]{:S(2)}) collective-permute-start(f32[8,64,128]{2,1,0:T(8,128)} %rest_0_.1), channel_id=1, source_target_pairs={{0,4},{4,0},{1,5},{5,1},{2,6},{6,2},{3,7},{7,3},{8,12},{12,8},{9,1... | collective-permute-start | bytes 786440 | tf_op jit(solution)/shard_map/ppermute | solution.py:206
  4.0 24.4 %collective-permute-start.4 = (f32[8,64,128]{2,1,0:T(8,128)}, f32[8,64,128]{2,1,0:T(8,128)S(1)}, u32[]{:S(2)}, u32[]{:S(2)}) collective-permute-start(f32[8,64,128]{2,1,0:T(8,128)} %rest_0_.1), channel_id=1, source_target_pairs={{0,16},{8,24},{16,0},{24,8},{1,17},{9,25},{17,1},{25,9},{2,18},{10... | collective-permute-start | bytes 786440 | tf_op jit(solution)/shard_map/ppermute | solution.py:202
  9.7 8.2 %collective-permute-start = (s32[2,8]{1,0:T(2,128)}, s32[2,8]{1,0:T(2,128)S(1)}, u32[]{:S(2)}, u32[]{:S(2)}) collective-permute-start(s32[2,8]{1,0:T(2,128)} %get-tuple-element.7.mark_ref), channel_id=1, source_target_pairs={{0,8},{8,0},{16,24},{24,16},{1,9},{9,1},{17,25},{25,17},{2,10},{10... | collective-permute-start | bytes 200 | tf_op jit(solution)/shard_map/ppermute | solution.py:202
  9.7 6.4 %copy-start.1 = (s32[2,8]{1,0:T(2,128)S(1)}, s32[2,8]{1,0:T(2,128)}, u32[]{:S(2)}) copy-start(s32[2,8]{1,0:T(2,128)} %get-tuple-element.7.mark_ref) | copy-start | bytes 196
  9.7 21.0 %all-to-all-start = ((f32[4,520,128]{2,1,0:T(8,128)}), f32[4,520,128]{2,1,0:T(8,128)S(1)}, u32[]{:S(2)}, u32[]{:S(2)}) async-start(f32[4,520,128]{2,1,0:T(8,128)} %get-tuple-element.8), calls=%async_computation | async-start | bytes 2129920 | tf_op jit(solution)/shard_map/all_to_all | solution.py:254
  13.5 10.4 %copy-start = (f32[8,64,128]{2,1,0:T(8,128)S(1)}, f32[8,64,128]{2,1,0:T(8,128)}, u32[]{:S(2)}) copy-start(f32[8,64,128]{2,1,0:T(8,128)} %rest_0_.1) | copy-start | bytes 786436
  16.2 12.8 %collective-permute-start.8 = (f32[8,64,128]{2,1,0:T(8,128)S(1)}, f32[8,64,128]{2,1,0:T(8,128)S(1)}, u32[]{:S(2)}, u32[]{:S(2)}) collective-permute-start(f32[8,64,128]{2,1,0:T(8,128)S(1)} %hold_until.2.rest_4_), channel_id=1, source_target_pairs={{0,16},{8,24},{16,0},{24,8},{1,17},{9,25},{17,1},{25,9},{2,18},{10... | collective-permute-start | bytes 786440 | tf_op jit(solution)/shard_map/ppermute | solution.py:202
  17.9 5.9 %collective-permute-start.1 = (s32[4,8]{1,0:T(4,128)S(1)}, s32[4,8]{1,0:T(4,128)S(1)}, u32[]{:S(2)}, u32[]{:S(2)}) collective-permute-start(s32[4,8]{1,0:T(4,128)S(1)} %pad_add_fusion.2), channel_id=1, source_target_pairs={{0,16},{8,24},{16,0},{24,8},{1,17},{9,25},{17,1},{25,9},{2,18},{10... | collective-permute-start | bytes 392 | tf_op jit(solution)/shard_map/ppermute | solution.py:202
  23.8 4.6 %collective-permute-start.2 = (s32[8,8]{1,0:T(8,128)S(1)}, s32[8,8]{1,0:T(8,128)S(1)}, u32[]{:S(2)}, u32[]{:S(2)}) collective-permute-start(s32[8,8]{1,0:T(8,128)S(1)} %pad_add_fusion.1), channel_id=1, source_target_pairs={{0,4},{4,0},{1,5},{5,1},{2,6},{6,2},{3,7},{7,3},{8,12},{12,8},{9,1... | collective-permute-start | bytes 776 | tf_op jit(solution)/shard_map/ppermute | solution.py:206
  23.9 5.3 %collective-permute-start.3 = (f32[8,64,128]{2,1,0:T(8,128)S(1)}, f32[8,64,128]{2,1,0:T(8,128)S(1)}, u32[]{:S(2)}, u32[]{:S(2)}) collective-permute-start(f32[8,64,128]{2,1,0:T(8,128)S(1)} %copy-done), channel_id=1, source_target_pairs={{0,8},{8,0},{16,24},{24,16},{1,9},{9,1},{17,25},{25,17},{2,10},{10... | collective-permute-start | bytes 786440 | tf_op jit(solution)/shard_map/ppermute | solution.py:202
  28.4 2.0 %collective-permute-start.7 = (f32[8,64,128]{2,1,0:T(8,128)S(1)}, f32[8,64,128]{2,1,0:T(8,128)S(1)}, u32[]{:S(2)}, u32[]{:S(2)}) collective-permute-start(f32[8,64,128]{2,1,0:T(8,128)S(1)} %hold_until.2.rest_4_), channel_id=1, source_target_pairs={{0,8},{8,0},{16,24},{24,16},{1,9},{9,1},{17,25},{25,17},{2,10},{10... | collective-permute-start | bytes 786440 | tf_op jit(solution)/shard_map/ppermute | solution.py:202
  28.5 1.9 %collective-permute-start.5 = (f32[8,64,128]{2,1,0:T(8,128)S(1)}, f32[8,64,128]{2,1,0:T(8,128)S(1)}, u32[]{:S(2)}, u32[]{:S(2)}) collective-permute-start(f32[8,64,128]{2,1,0:T(8,128)S(1)} %collective-permute-done.4.rest_2_), channel_id=1, source_target_pairs={{0,8},{8,0},{16,24},{24,16},{1,9},{9,1},{17,25},{25,17},{2,10},{10... | collective-permute-start | bytes 786440 | tf_op jit(solution)/shard_map/ppermute | solution.py:202
  29.0 1.7 %collective-permute-start.9 = (f32[8,64,128]{2,1,0:T(8,128)S(1)}, f32[8,64,128]{2,1,0:T(8,128)S(1)}, u32[]{:S(2)}, u32[]{:S(2)}) collective-permute-start(f32[8,64,128]{2,1,0:T(8,128)S(1)} %hold_until.3.rest_6_), channel_id=1, source_target_pairs={{0,8},{8,0},{16,24},{24,16},{1,9},{9,1},{17,25},{25,17},{2,10},{10... | collective-permute-start | bytes 786440 | tf_op jit(solution)/shard_map/ppermute | solution.py:202

commit v9 on v8

--- a/solution.py
+++ b/solution.py
@@ -24,6 +24,29 @@
 
 def transposed_dot(left, right):
     return lax.dot_general(left, right, (((0,), (0,)), ((), ())), preferred_element_type=jnp.float32)
+
+
+def extend_kernel(columns_ref, blocks_any, out_ref, sem):
+    used = blocks_any.shape[0]
+    entries, fine_rows = columns_ref.shape
+    copy = pltpu.make_async_copy(blocks_any, out_ref.at[pl.ds(0, used)], sem)
+    copy.start()
+    out_ref[used:] = jnp.zeros((EXTRA, out_ref.shape[1]), jnp.float32)
+    out_ref[used : used + entries, :fine_rows] = columns_ref[...].astype(jnp.float32)
+    copy.wait()
+
+
+def extend(columns, blocks):
+    used, width = blocks.shape
+    return pl.pallas_call(
+        extend_kernel,
+        out_shape=jax.ShapeDtypeStruct((used + EXTRA, width), blocks.dtype),
+        in_specs=[pl.BlockSpec(memory_space=pltpu.VMEM), pl.BlockSpec(memory_space=pltpu.HBM)],
+        out_specs=pl.BlockSpec(memory_space=pltpu.VMEM),
+        scratch_shapes=[pltpu.SemaphoreType.DMA],
+        cost_estimate=pl.CostEstimate(flops=0, bytes_accessed=1 << 19, transcendentals=0),
+        name="extend",
+    )(columns, blocks)
 
 
 def hold_kernel(mark_ref, blocks_ref, out_ref):
@@ -43,7 +66,7 @@
 
 
 def restrict_kernel(
-    count_any, slot_any, rows_any, fetch_any, restrict_any, operator_any, columns_ref, out_ref, mark_ref,
+    count_any, slot_any, rows_any, fetch_any, restrict_any, operator_any, out_ref, mark_ref,
     count_ref, slot_ref, rows_ref, fetch_ref, restrict_ref, operator_ref, sems, operator_sems,
 ):
     fine_rows, block_size, _ = operator_ref.shape
@@ -79,7 +102,7 @@
                 wanted = fetch_ref[s, side * half + near]
                 value = jnp.where(short_lane == side * slot_count + s, wanted, value)
         out_ref[near, used:] = value.astype(jnp.float32)
-    mark_ref[...] = columns_ref[...]
+    mark_ref[...] = out_ref[0, used:]
 
     for i in range(fine_rows):
         value = restrict_ref[i]
@@ -96,9 +119,7 @@
             out_ref[lax.rem(peer, half), pl.ds(start, block_size)] += part
 
 
-def restrict_operator(
-    operator_count, operator_slot, restrict_rows, fetch, operator_blocks, restrict_blocks, prolong_columns
-):
+def restrict_operator(operator_count, operator_slot, restrict_rows, fetch, operator_blocks, restrict_blocks):
     fine_rows, block_size, width = operator_blocks.shape
     slot_count, columns = fetch.shape
     wide = NCR * block_size
@@ -108,9 +129,9 @@
         restrict_kernel,
         out_shape=(
             jax.ShapeDtypeStruct((columns // 2, rows, wide), jnp.float32),
-            jax.ShapeDtypeStruct(prolong_columns.shape, prolong_columns.dtype),
+            jax.ShapeDtypeStruct((EXTRA, wide), jnp.float32),
         ),
-        in_specs=[pl.BlockSpec(memory_space=pltpu.HBM)] * 6 + [pl.BlockSpec(memory_space=pltpu.VMEM)],
+        in_specs=[pl.BlockSpec(memory_space=pltpu.HBM)] * 6,
         out_specs=[pl.BlockSpec(memory_space=pltpu.VMEM)] * 2,
         scratch_shapes=[pltpu.SMEM(x.shape, x.dtype) for x in small]
         + [pltpu.VMEM(x.shape, x.dtype) for x in (restrict_blocks, operator_blocks)]
@@ -119,23 +140,27 @@
             flops=6 * fine_rows * block_size * width * wide, bytes_accessed=4 << 20, transcendentals=0
         ),
         name="restrict_operator",
-    )(*small, restrict_blocks, operator_blocks, prolong_columns)
-
-
-def combine_kernel(own_ref, columns_ref, restricted_ref, *rest, slot_count, fine_rows, entries):
+    )(*small, restrict_blocks, operator_blocks)
+
+
+def combine_kernel(own_ref, restricted_ref, *rest, slot_count, fine_rows, entries):
     pieces, (out_ref, held_ref, table_ref, index_ref, sem) = rest[:-5], rest[-5:]
     half = restricted_ref.shape[0]
     rows = len(pieces) // 2
     block_size = out_ref.shape[1]
     columns = 2 * half
     used = 2 * slot_count * block_size
+    held = fine_rows * block_size
 
     for near in range(half):
         table_ref[near : near + 1] = restricted_ref[near, used : used + 1].astype(jnp.int32)
+    for i, piece in enumerate(pieces):
+        first = half + entries * i
+        table_ref[first : first + entries] = piece[held : held + entries].astype(jnp.int32)
     copy = pltpu.make_async_copy(table_ref, index_ref, sem)
     copy.start()
     for i, piece in enumerate(pieces):
-        held_ref[i] = piece[...]
+        held_ref[i] = piece[:held]
     out_ref[...] = jnp.zeros_like(out_ref)
     copy.wait()
 
@@ -146,30 +171,30 @@
         inside = lax.rem(wanted, fine_rows)
         far = lax.div(place, slot_count) ^ own_ref[1]
         piece = far * rows + (lax.div(wanted, fine_rows * columns) ^ own_ref[0])
+        block = held_ref[piece, pl.ds(pl.multiple_of(inside * block_size, block_size), block_size)]
         restricted = restricted_ref[near, pl.ds(pl.multiple_of(place * block_size, block_size), block_size)]
-        product = transposed_dot(split3(held_ref[piece, inside], "left"), split3(restricted, "right"))
+        product = transposed_dot(split3(block, "left"), split3(restricted, "right"))
         for m in range(entries):
-            column = columns_ref[entries * piece + m, inside]
+            column = own_ref[2 + index_ref[half + entries * piece + m, inside]]
             out_ref[column] += product[m * block_size : (m + 1) * block_size]
         return carry
 
     lax.fori_loop(0, half * 2 * slot_count, step, 0, unroll=16)
 
 
-def combine(own, columns, restricted, pieces, coarse_all, slot_count):
+def combine(own, restricted, pieces, coarse_all, slot_count, fine_rows, block_size):
     half, _, wide = restricted.shape
-    fine_rows, block_size, width = pieces[0].shape
-    table_rows = -(-half // 8) * 8
-    return pl.pallas_call(
-        functools.partial(
-            combine_kernel, slot_count=slot_count, fine_rows=fine_rows, entries=width // block_size
-        ),
+    width = pieces[0].shape[1]
+    entries = width // block_size
+    table_rows = -(-(half + entries * len(pieces)) // 8) * 8
+    return pl.pallas_call(
+        functools.partial(combine_kernel, slot_count=slot_count, fine_rows=fine_rows, entries=entries),
         out_shape=jax.ShapeDtypeStruct((coarse_all, block_size, wide), jnp.float32),
-        in_specs=[pl.BlockSpec(memory_space=pltpu.SMEM)] * 2
+        in_specs=[pl.BlockSpec(memory_space=pltpu.SMEM)]
         + [pl.BlockSpec(memory_space=pltpu.VMEM)] * (1 + len(pieces)),
         out_specs=pl.BlockSpec(memory_space=pltpu.VMEM),
         scratch_shapes=[
-            pltpu.VMEM((len(pieces), fine_rows, block_size, width), jnp.float32),
+            pltpu.VMEM((len(pieces), fine_rows * block_size, width), jnp.float32),
             pltpu.VMEM((table_rows, LANES), jnp.int32),
             pltpu.SMEM((table_rows, LANES), jnp.int32),
             pltpu.SemaphoreType.DMA,
@@ -177,25 +202,7 @@
         compiler_params=pltpu.CompilerParams(vmem_limit_bytes=VMEM_LIMIT),
         cost_estimate=pl.CostEstimate(flops=1 << 28, bytes_accessed=4 << 20, transcendentals=0),
         name="combine",
-    )(own, columns, restricted, *pieces)
-
-
-def add_kernel(parts_ref, out_ref):
-    total = parts_ref[0]
-    for i in range(1, parts_ref.shape[0]):
-        total = total + parts_ref[i]
-    out_ref[...] = total
-
-
-def add_up(parts):
-    return pl.pallas_call(
-        add_kernel,
-        out_shape=jax.ShapeDtypeStruct(parts.shape[1:], parts.dtype),
-        in_specs=[pl.BlockSpec(memory_space=pltpu.VMEM)],
-        out_specs=pl.BlockSpec(memory_space=pltpu.VMEM),
-        compiler_params=pltpu.CompilerParams(vmem_limit_bytes=VMEM_LIMIT),
-        name="add_up",
-    )(parts)
+    )(own, restricted, *pieces)
 
 
 def row_swap(x, bit):
@@ -206,24 +213,34 @@
     return lax.ppermute(x, "half", [(0, 1), (1, 0)])
 
 
-def spread_over_rows(blocks, rows, mark=None):
+def spread_over_rows(blocks, rows):
     pieces = {0: blocks}
     bit = rows // 2
     while bit:
         for mask in list(pieces):
             pieces[mask ^ bit] = row_swap(pieces[mask], bit)
-        if mark is not None and bit == rows // 2:
-            pieces[bit] = hold_until(mark, pieces[bit], 1 << 20)
         bit //= 2
     return [pieces[mask] for mask in range(rows)]
 
 
-def columns_of_rows(columns, rows):
+def place_of_columns(columns):
+    ahead = jnp.arange(columns, dtype=jnp.int32) ^ (lax.axis_index("half") * (columns // 2) + lax.axis_index("near"))
+    place = jnp.zeros_like(ahead)
+    low, high = 1, columns // 2
+    while high:
+        place = place + jnp.where(ahead & low != 0, high, 0)
+        low, high = low * 2, high // 2
+    return place
+
+
+def add_over_columns(sums, half):
     bit = 1
-    while bit < rows:
-        columns = jnp.concatenate([columns, row_swap(columns, bit)], axis=0)
+    while bit < half:
+        kept, sent = jnp.split(sums, 2)
+        sums = kept + lax.ppermute(sent, "near", [(n, n ^ bit) for n in range(half)])
         bit *= 2
-    return columns
+    kept, sent = jnp.split(sums, 2)
+    return kept[0] + half_swap(sent)[0]
 
 
 def local(
@@ -238,28 +255,21 @@
 ):
     rows, half = lax.axis_size("row"), lax.axis_size("near")
     slot_count = fetch_lists.shape[3]
+    fine_rows, block_size, width = prolong_blocks.shape
     fetch = fetch_lists.reshape(2 * half, slot_count).T
     own = jnp.stack([lax.axis_index("row"), lax.axis_index("half")])
-
-    far_blocks = half_swap(prolong_blocks)
-    restricted, own_columns = restrict_operator(
-        operator_count,
-        operator_slot,
-        restrict_rows.T,
-        fetch,
-        operator_blocks,
-        restrict_blocks,
-        prolong_cols.T,
+    own = jnp.concatenate([own, place_of_columns(2 * half)])
+
+    near_blocks = extend(prolong_cols.T, prolong_blocks.reshape(fine_rows * block_size, width))
+    far_blocks = half_swap(near_blocks)
+    restricted, mark = restrict_operator(
+        operator_count, operator_slot, restrict_rows.T, fetch, operator_blocks, restrict_blocks
     )
-    restricted_here = lax.all_to_all(restricted, "near", split_axis=0, concat_axis=0, tiled=True)
-    near_columns = columns_of_rows(own_columns, rows)
-    all_columns = jnp.concatenate([near_columns, half_swap(near_columns)], axis=0)
-    far_blocks = hold_until(own_columns, far_blocks, HOLD_FLOPS)
-    near_pieces = spread_over_rows(prolong_blocks, rows)
-    far_pieces = spread_over_rows(far_blocks, rows, all_columns)
-    sums = combine(own, all_columns, restricted_here, near_pieces + far_pieces, NCR * rows, slot_count)
-    parts = lax.all_to_all(sums, ("half", "near"), split_axis=0, concat_axis=0, tiled=True)
-    return add_up(parts).T
+    restricted = lax.all_to_all(restricted, "near", split_axis=0, concat_axis=0, tiled=True)
+    far_blocks = hold_until(mark, far_blocks, HOLD_FLOPS)
+    pieces = spread_over_rows(near_blocks, rows) + spread_over_rows(far_blocks, rows)
+    sums = combine(own, restricted, pieces, NCR * rows, slot_count, fine_rows, block_size)
+    return add_over_columns(sums, half).T
 
 
 def solution(mesh):

time: 49.5 us -> 48.2 us (0.974)
  blocking collectives: 15.5 us -> 0 us
  waiting for transfers between devices: 14 us -> 23.4 us
  starting transfers between devices: 12.4 us -> 15.5 us
  Pallas kernels: 7.07 us -> 8.14 us
  other arithmetic: 0.1 us -> 0.74 us
    all_to_all x1 -> x0, blocking collectives: 15.5 us -> none  [local(): lax.all_to_all(sums, ('half', 'near'), split_axis=0, concat_axis=0, tiled...]
    ppermute x0 -> x2, waiting for transfers between devices: none -> 8.04 us  [add_over_columns(): lax.ppermute(sent, 'near', [(n, n ^ bit) for n in range(half)])]
    all_to_all x1, waiting for transfers between devices: 0.01 us -> 2.24 us  [local(): lax.all_to_all(restricted, 'near', split_axis=0, concat_axis=0, tiled=True)]
    ppermute x2, starting transfers between devices: 4.11 us -> 6.34 us  [half_swap(): return lax.ppermute(x, 'half', [(0, 1), (1, 0)])]
    pallas_call x1, Pallas kernels: 0.63 us -> 2.35 us  [extend(): pl.pallas_call(extend_kernel, out_shape=jax.ShapeDtypeStruct((used + EXTR...]
    ppermute x0 -> x2, starting transfers between devices: none -> 1.67 us  [add_over_columns(): lax.ppermute(sent, 'near', [(n, n ^ bit) for n in range(half)])]
    ppermute x8 -> x6, starting transfers between devices: 4.54 us -> 3.67 us  [row_swap(): lax.ppermute(x, 'row', [(r, r ^ bit) for r in range(lax.axis_size('row'))])]
    ppermute x2, waiting for transfers between devices: 7.04 us -> 6.32 us  [half_swap(): return lax.ppermute(x, 'half', [(0, 1), (1, 0)])]
  transfers between devices with their start and end apart: 11 -> 11, of which waited for: 5 -> 7; matrix products, arithmetic and copies ran while one was open for 0% -> 0% of each run, Pallas kernels for 8% -> 7%
where the time goes in v9:
time: 48.2 us; the launch traced here: 47.9 us
  waiting for transfers between devices  23.4 us (49%)
  starting transfers between devices  15.5 us (32%)
  Pallas kernels  8.14 us (17%)
  other arithmetic  0.74 us (2%)
    ppermute x2, waiting for transfers between devices, add_over_columns(): lax.ppermute(sent, 'near', [(n, n ^ bit) for n in range(half)])  8.04 us
    ppermute x6, waiting for transfers between devices, row_swap(): lax.ppermute(x, 'row', [(r, r ^ bit) for r in range(lax.axis_size('row'))])  6.84 us
    ppermute x2, starting transfers between devices, half_swap(): return lax.ppermute(x, 'half', [(0, 1), (1, 0)])  6.34 us
    ppermute x2, waiting for transfers between devices, half_swap(): return lax.ppermute(x, 'half', [(0, 1), (1, 0)])  6.32 us
    all_to_all x1, starting transfers between devices, local(): lax.all_to_all(restricted, 'near', split_axis=0, concat_axis=0, tiled=True)  3.78 us
    ppermute x6, starting transfers between devices, row_swap(): lax.ppermute(x, 'row', [(r, r ^ bit) for r in range(lax.axis_size('row'))])  3.67 us
    pallas_call x1, Pallas kernels, restrict_operator(): pl.pallas_call(restrict_kernel, out_shape=(jax.ShapeDtypeStruct((columns...  3.4 us
    pallas_call x1, Pallas kernels, combine(): pl.pallas_call(functools.partial(combine_kernel, slot_count=slot_count, f...  2.36 us
  transfers between devices with their start and end apart: 11, of which 7 were waited for; matrix products, arithmetic and copies ran while one was open for 0% of the time, Pallas kernels for 7%

profile of v9, /device:TPU:0, one launch (start us, length us, event | category | flops | bytes accessed | tf_op | source)
XLA Modules:
  0.0 47.9 jit_solution(1962832712161061878)
XLA Ops:
  0.0 2.4 %extend.1.rest_0_ = f32[520,128]{1,0:T(8,128)} custom-call(s32[2,8]{1,0:T(2,128)} %bitcast.14, f32[512,128]{1,0:T(8,128)} %bitcast.12), custom_call_target="tpu_custom_call" | custom-call | bytes 524288 | tf_op jit(solution)/shard_map/extend/pallas_call | solution.py:41
  2.4 4.1 %collective-permute-start.3 = (f32[520,128]{1,0:T(8,128)}, f32[520,128]{1,0:T(8,128)S(1)}, u32[]{:S(2)}, u32[]{:S(2)}) collective-permute-start(f32[520,128]{1,0:T(8,128)} %extend.1.rest_0_), channel_id=1, source_target_pairs={{0,4},{4,0},{1,5},{5,1},{2,6},{6,2},{3,7},{7,3},{8,12},{12,8},{9,1... | collective-permute-start | bytes 798728 | tf_op jit(solution)/shard_map/ppermute | solution.py:213
  6.5 1.5 %collective-permute-start.1 = (f32[520,128]{1,0:T(8,128)}, f32[520,128]{1,0:T(8,128)S(1)}, u32[]{:S(2)}, u32[]{:S(2)}) collective-permute-start(f32[520,128]{1,0:T(8,128)} %extend.1.rest_0_), channel_id=1, source_target_pairs={{0,16},{8,24},{16,0},{24,8},{1,17},{9,25},{17,1},{25,9},{2,18},{10... | collective-permute-start | bytes 798728 | tf_op jit(solution)/shard_map/ppermute | solution.py:209
  8.0 3.4 %restrict_operator.1 = (f32[4,520,128]{2,1,0:T(8,128)}, f32[8,128]{1,0:T(8,128)}) custom-call(s32[8]{0:T(128)} %count_any.1, s32[8,8]{1,0:T(8,128)} %slot_any.1, s32[2,8]{1,0:T(2,128)} %bitcast.15, s32[4,8]{1,0:T(4,128)} %bitcast.13, f32[8,64,128]{2,1,0:T(8,128)} %restrict_any.1, f32[8,64,512]{2,1,0:T(8,128)} %operator_any.1), custom_call_target="tpu_custom_call" | custom-call | flops 201326592 | bytes 4194304 | tf_op jit(solution)/shard_map/restrict_operator/pallas_call | solution.py:128
  11.4 0.0 copy-start.1
  11.4 3.8 %all-to-all-start = ((f32[4,520,128]{2,1,0:T(8,128)}), f32[4,520,128]{2,1,0:T(8,128)S(1)}, u32[]{:S(2)}, u32[]{:S(2)}) async-start(f32[4,520,128]{2,1,0:T(8,128)} %get-tuple-element.7), calls=%async_computation | async-start | bytes 2129920 | tf_op jit(solution)/shard_map/all_to_all | solution.py:268
  15.2 3.7 %collective-permute-done.3.blocks_ref = f32[520,128]{1,0:T(8,128)S(1)} collective-permute-done((f32[520,128]{1,0:T(8,128)}, f32[520,128]{1,0:T(8,128)S(1)}, u32[]{:S(2)}, u32[]{:S(2)}) %collective-permute-start.3) | collective-permute-done | bytes 266272 | tf_op jit(solution)/shard_map/ppermute | solution.py:213
  18.9 1.6 %collective-permute-start.5 = (f32[520,128]{1,0:T(8,128)S(1)}, f32[520,128]{1,0:T(8,128)S(1)}, u32[]{:S(2)}, u32[]{:S(2)}) collective-permute-start(f32[520,128]{1,0:T(8,128)S(1)} %hold_until.1.rest_4_), channel_id=1, source_target_pairs={{0,16},{8,24},{16,0},{24,8},{1,17},{9,25},{17,1},{25,9},{2,18},{10... | collective-permute-start | bytes 798728 | tf_op jit(solution)/shard_map/ppermute | solution.py:209
  20.5 0.5 %collective-permute-start.4 = (f32[520,128]{1,0:T(8,128)S(1)}, f32[520,128]{1,0:T(8,128)S(1)}, u32[]{:S(2)}, u32[]{:S(2)}) collective-permute-start(f32[520,128]{1,0:T(8,128)S(1)} %hold_until.1.rest_4_), channel_id=1, source_target_pairs={{0,8},{8,0},{16,24},{24,16},{1,9},{9,1},{17,25},{25,17},{2,10},{10... | collective-permute-start | bytes 798728 | tf_op jit(solution)/shard_map/ppermute | solution.py:209
  21.0 0.0 collective-permute-done.1.rest_2_
  21.1 0.0 collective-permute-start.2
  21.1 5.4 %collective-permute-done.5.rest_6_ = f32[520,128]{1,0:T(8,128)S(1)} collective-permute-done((f32[520,128]{1,0:T(8,128)S(1)}, f32[520,128]{1,0:T(8,128)S(1)}, u32[]{:S(2)}, u32[]{:S(2)}) %collective-permute-start.5) | collective-permute-done | bytes 266272 | tf_op jit(solution)/shard_map/ppermute | solution.py:209
  26.4 0.0 collective-permute-start.6
  26.5 0.1 pad_add_fusion.own_ref
  26.6 1.4 %collective-permute-done.6.rest_7_ = f32[520,128]{1,0:T(8,128)S(1)} collective-permute-done((f32[520,128]{1,0:T(8,128)S(1)}, f32[520,128]{1,0:T(8,128)S(1)}, u32[]{:S(2)}, u32[]{:S(2)}) %collective-permute-start.6) | collective-permute-done | bytes 266272 | tf_op jit(solution)/shard_map/ppermute | solution.py:209
  28.0 2.2 %all-to-all-done.restricted_ref = f32[4,520,128]{2,1,0:T(8,128)S(1)} async-done(((f32[4,520,128]{2,1,0:T(8,128)}), f32[4,520,128]{2,1,0:T(8,128)S(1)}, u32[]{:S(2)}, u32[]{:S(2)}) %all-to-all-start) | async-done | bytes 1064992 | tf_op jit(solution)/shard_map/all_to_all | solution.py:268
  30.2 2.4 %combine.1 = f32[8,64,128]{2,1,0:T(8,128)S(1)} custom-call(s32[10]{0:T(128)S(1)} %pad_add_fusion.own_ref, f32[4,520,128]{2,1,0:T(8,128)S(1)} %all-to-all-done.restricted_ref, f32[520,128]{1,0:T(8,128)S(1)} %copy-done, f32[520,128]{1,0:T(8,128)S(1)} %collective-permute-done.rest_1_, f32[520,128]{1,0:T(8,128)S(1)} %collective-permute-done.1.rest_2_, ...), custom_call_target="tpu_custom_call" | custom-call | flops 268435456 | bytes 4194304 | tf_op jit(solution)/shard_map/combine/pallas_call | solution.py:190
  32.6 1.6 %collective-permute-start.7 = (f32[4,64,128]{2,1,0:T(8,128)S(1)}, f32[4,64,128]{2,1,0:T(8,128)S(1)}, u32[]{:S(2)}, u32[]{:S(2)}) collective-permute-start(f32[4,64,128]{2,1,0:T(8,128)S(1)} %split.25), channel_id=1, source_target_pairs={{0,1},{1,0},{2,3},{3,2},{4,5},{5,4},{6,7},{7,6},{8,9},{9,8},{10,11... | collective-permute-start | bytes 393224 | tf_op jit(solution)/shard_map/ppermute | solution.py:240
  34.2 3.8 %collective-permute-done.7 = f32[4,64,128]{2,1,0:T(8,128)S(1)} collective-permute-done((f32[4,64,128]{2,1,0:T(8,128)S(1)}, f32[4,64,128]{2,1,0:T(8,128)S(1)}, u32[]{:S(2)}, u32[]{:S(2)}) %collective-permute-start.7) | collective-permute-done | bytes 131104 | tf_op jit(solution)/shard_map/ppermute | solution.py:240
  38.0 0.1 collective-permute-start.8
  38.1 4.3 %collective-permute-done.8 = f32[2,64,128]{2,1,0:T(8,128)S(1)} collective-permute-done((f32[2,64,128]{2,1,0:T(8,128)S(1)}, f32[2,64,128]{2,1,0:T(8,128)S(1)}, u32[]{:S(2)}, u32[]{:S(2)}) %collective-permute-start.8) | collective-permute-done | bytes 65568 | tf_op jit(solution)/shard_map/ppermute | solution.py:240
  42.4 2.2 %collective-permute-start.9 = (f32[1,64,128]{2,1,0:T(8,128)S(1)}, f32[1,64,128]{2,1,0:T(8,128)S(1)}, u32[]{:S(2)}, u32[]{:S(2)}) collective-permute-start(f32[1,64,128]{2,1,0:T(8,128)S(1)} %split.29), channel_id=1, source_target_pairs={{0,4},{4,0},{1,5},{5,1},{2,6},{6,2},{3,7},{7,3},{8,12},{12,8},{9,1... | collective-permute-start | bytes 98312 | tf_op jit(solution)/shard_map/ppermute | solution.py:213
  44.6 2.6 %collective-permute-done.9 = f32[1,64,128]{2,1,0:T(8,128)S(1)} collective-permute-done((f32[1,64,128]{2,1,0:T(8,128)S(1)}, f32[1,64,128]{2,1,0:T(8,128)S(1)}, u32[]{:S(2)}, u32[]{:S(2)}) %collective-permute-start.9) | collective-permute-done | bytes 32800 | tf_op jit(solution)/shard_map/ppermute | solution.py:213
  47.3 0.6 %fusion = f32[128,64]{0,1:T(8,128)} fusion(f32[1,64,128]{2,1,0:T(8,128)S(1)} %collective-permute-done.9, f32[2,64,128]{2,1,0:T(8,128)S(1)} %slice_add_fusion.1), kind=kLoop, calls=%fused_computation.3 | loop fusion | flops 8192 | bytes 98304 | tf_op jit(solution)/shard_map/transpose | solution.py:272
  (14 shorter events, 0.1 us)
Async XLA Ops:
  2.4 16.5 %collective-permute-start.3 = (f32[520,128]{1,0:T(8,128)}, f32[520,128]{1,0:T(8,128)S(1)}, u32[]{:S(2)}, u32[]{:S(2)}) collective-permute-start(f32[520,128]{1,0:T(8,128)} %extend.1.rest_0_), channel_id=1, source_target_pairs={{0,4},{4,0},{1,5},{5,1},{2,6},{6,2},{3,7},{7,3},{8,12},{12,8},{9,1... | collective-permute-start | bytes 798728 | tf_op jit(solution)/shard_map/ppermute | solution.py:213
  6.5 14.6 %collective-permute-start.1 = (f32[520,128]{1,0:T(8,128)}, f32[520,128]{1,0:T(8,128)S(1)}, u32[]{:S(2)}, u32[]{:S(2)}) collective-permute-start(f32[520,128]{1,0:T(8,128)} %extend.1.rest_0_), channel_id=1, source_target_pairs={{0,16},{8,24},{16,0},{24,8},{1,17},{9,25},{17,1},{25,9},{2,18},{10... | collective-permute-start | bytes 798728 | tf_op jit(solution)/shard_map/ppermute | solution.py:209
  11.4 7.5 %copy-start.1 = (f32[8,128]{1,0:T(8,128)S(1)}, f32[8,128]{1,0:T(8,128)}, u32[]{:S(2)}) copy-start(f32[8,128]{1,0:T(8,128)} %get-tuple-element.8.mark_ref) | copy-start | bytes 12292
  11.4 18.8 %all-to-all-start = ((f32[4,520,128]{2,1,0:T(8,128)}), f32[4,520,128]{2,1,0:T(8,128)S(1)}, u32[]{:S(2)}, u32[]{:S(2)}) async-start(f32[4,520,128]{2,1,0:T(8,128)} %get-tuple-element.7), calls=%async_computation | async-start | bytes 2129920 | tf_op jit(solution)/shard_map/all_to_all | solution.py:268
  18.9 1.7 %copy-start = (f32[520,128]{1,0:T(8,128)S(1)}, f32[520,128]{1,0:T(8,128)}, u32[]{:S(2)}) copy-start(f32[520,128]{1,0:T(8,128)} %extend.1.rest_0_) | copy-start | bytes 798724
  18.9 7.5 %collective-permute-start.5 = (f32[520,128]{1,0:T(8,128)S(1)}, f32[520,128]{1,0:T(8,128)S(1)}, u32[]{:S(2)}, u32[]{:S(2)}) collective-permute-start(f32[520,128]{1,0:T(8,128)S(1)} %hold_until.1.rest_4_), channel_id=1, source_target_pairs={{0,16},{8,24},{16,0},{24,8},{1,17},{9,25},{17,1},{25,9},{2,18},{10... | collective-permute-start | bytes 798728 | tf_op jit(solution)/shard_map/ppermute | solution.py:209
  20.5 6.0 %collective-permute-start = (f32[520,128]{1,0:T(8,128)S(1)}, f32[520,128]{1,0:T(8,128)S(1)}, u32[]{:S(2)}, u32[]{:S(2)}) collective-permute-start(f32[520,128]{1,0:T(8,128)S(1)} %copy-done), channel_id=1, source_target_pairs={{0,8},{8,0},{16,24},{24,16},{1,9},{9,1},{17,25},{25,17},{2,10},{10... | collective-permute-start | bytes 798728 | tf_op jit(solution)/shard_map/ppermute | solution.py:209
  20.5 6.0 %collective-permute-start.4 = (f32[520,128]{1,0:T(8,128)S(1)}, f32[520,128]{1,0:T(8,128)S(1)}, u32[]{:S(2)}, u32[]{:S(2)}) collective-permute-start(f32[520,128]{1,0:T(8,128)S(1)} %hold_until.1.rest_4_), channel_id=1, source_target_pairs={{0,8},{8,0},{16,24},{24,16},{1,9},{9,1},{17,25},{25,17},{2,10},{10... | collective-permute-start | bytes 798728 | tf_op jit(solution)/shard_map/ppermute | solution.py:209
  21.1 5.5 %collective-permute-start.2 = (f32[520,128]{1,0:T(8,128)S(1)}, f32[520,128]{1,0:T(8,128)S(1)}, u32[]{:S(2)}, u32[]{:S(2)}) collective-permute-start(f32[520,128]{1,0:T(8,128)S(1)} %collective-permute-done.1.rest_2_), channel_id=1, source_target_pairs={{0,8},{8,0},{16,24},{24,16},{1,9},{9,1},{17,25},{25,17},{2,10},{10... | collective-permute-start | bytes 798728 | tf_op jit(solution)/shard_map/ppermute | solution.py:209
  26.4 1.5 %collective-permute-start.6 = (f32[520,128]{1,0:T(8,128)S(1)}, f32[520,128]{1,0:T(8,128)S(1)}, u32[]{:S(2)}, u32[]{:S(2)}) collective-permute-start(f32[520,128]{1,0:T(8,128)S(1)} %collective-permute-done.5.rest_6_), channel_id=1, source_target_pairs={{0,8},{8,0},{16,24},{24,16},{1,9},{9,1},{17,25},{25,17},{2,10},{10... | collective-permute-start | bytes 798728 | tf_op jit(solution)/shard_map/ppermute | solution.py:209
  32.6 5.4 %collective-permute-start.7 = (f32[4,64,128]{2,1,0:T(8,128)S(1)}, f32[4,64,128]{2,1,0:T(8,128)S(1)}, u32[]{:S(2)}, u32[]{:S(2)}) collective-permute-start(f32[4,64,128]{2,1,0:T(8,128)S(1)} %split.25), channel_id=1, source_target_pairs={{0,1},{1,0},{2,3},{3,2},{4,5},{5,4},{6,7},{7,6},{8,9},{9,8},{10,11... | collective-permute-start | bytes 393224 | tf_op jit(solution)/shard_map/ppermute | solution.py:240
  38.0 4.3 %collective-permute-start.8 = (f32[2,64,128]{2,1,0:T(8,128)S(1)}, f32[2,64,128]{2,1,0:T(8,128)S(1)}, u32[]{:S(2)}, u32[]{:S(2)}) collective-permute-start(f32[2,64,128]{2,1,0:T(8,128)S(1)} %split.27), channel_id=1, source_target_pairs={{0,2},{1,3},{2,0},{3,1},{4,6},{5,7},{6,4},{7,5},{8,10},{9,11},{10,... | collective-permute-start | bytes 196616 | tf_op jit(solution)/shard_map/ppermute | solution.py:240
  42.4 4.9 %collective-permute-start.9 = (f32[1,64,128]{2,1,0:T(8,128)S(1)}, f32[1,64,128]{2,1,0:T(8,128)S(1)}, u32[]{:S(2)}, u32[]{:S(2)}) collective-permute-start(f32[1,64,128]{2,1,0:T(8,128)S(1)} %split.29), channel_id=1, source_target_pairs={{0,4},{4,0},{1,5},{5,1},{2,6},{6,2},{3,7},{7,3},{8,12},{12,8},{9,1... | collective-permute-start | bytes 98312 | tf_op jit(solution)/shard_map/ppermute | solution.py:213

commit v10 on v9

--- a/solution.py
+++ b/solution.py
@@ -26,43 +26,26 @@
     return lax.dot_general(left, right, (((0,), (0,)), ((), ())), preferred_element_type=jnp.float32)
 
 
-def extend_kernel(columns_ref, blocks_any, out_ref, sem):
-    used = blocks_any.shape[0]
-    entries, fine_rows = columns_ref.shape
-    copy = pltpu.make_async_copy(blocks_any, out_ref.at[pl.ds(0, used)], sem)
-    copy.start()
+def append_kernel(mark_ref, far_columns_ref, own_columns_ref, blocks_ref, out_ref):
+    used = blocks_ref.shape[0]
+    entries, fine_rows = own_columns_ref.shape
+    out_ref[:used] = blocks_ref[...]
     out_ref[used:] = jnp.zeros((EXTRA, out_ref.shape[1]), jnp.float32)
-    out_ref[used : used + entries, :fine_rows] = columns_ref[...].astype(jnp.float32)
-    copy.wait()
-
-
-def extend(columns, blocks):
+    out_ref[used : used + entries, :fine_rows] = far_columns_ref[...].astype(jnp.float32)
+    out_ref[used + entries : used + 2 * entries, :fine_rows] = own_columns_ref[...].astype(jnp.float32)
+
+
+def append_columns(mark, far_columns, own_columns, blocks):
     used, width = blocks.shape
     return pl.pallas_call(
-        extend_kernel,
+        append_kernel,
         out_shape=jax.ShapeDtypeStruct((used + EXTRA, width), blocks.dtype),
-        in_specs=[pl.BlockSpec(memory_space=pltpu.VMEM), pl.BlockSpec(memory_space=pltpu.HBM)],
-        out_specs=pl.BlockSpec(memory_space=pltpu.VMEM),
-        scratch_shapes=[pltpu.SemaphoreType.DMA],
-        cost_estimate=pl.CostEstimate(flops=0, bytes_accessed=1 << 19, transcendentals=0),
-        name="extend",
-    )(columns, blocks)
-
-
-def hold_kernel(mark_ref, blocks_ref, out_ref):
-    out_ref[...] = blocks_ref[...]
-
-
-def hold_until(mark, blocks, flops):
-    return pl.pallas_call(
-        hold_kernel,
-        out_shape=jax.ShapeDtypeStruct(blocks.shape, blocks.dtype),
-        in_specs=[pl.BlockSpec(memory_space=pltpu.VMEM)] * 2,
+        in_specs=[pl.BlockSpec(memory_space=pltpu.VMEM)] * 4,
         out_specs=pl.BlockSpec(memory_space=pltpu.VMEM),
         compiler_params=pltpu.CompilerParams(vmem_limit_bytes=VMEM_LIMIT),
-        cost_estimate=pl.CostEstimate(flops=flops, bytes_accessed=flops >> 8, transcendentals=0),
-        name="hold_until",
-    )(mark, blocks)
+        cost_estimate=pl.CostEstimate(flops=HOLD_FLOPS, bytes_accessed=HOLD_FLOPS >> 8, transcendentals=0),
+        name="append_columns",
+    )(mark, far_columns, own_columns, blocks)
 
 
 def restrict_kernel(
@@ -154,13 +137,15 @@
 
     for near in range(half):
         table_ref[near : near + 1] = restricted_ref[near, used : used + 1].astype(jnp.int32)
-    for i, piece in enumerate(pieces):
-        first = half + entries * i
-        table_ref[first : first + entries] = piece[held : held + entries].astype(jnp.int32)
+    for i, piece in enumerate(pieces[rows:]):
+        for far in range(2):
+            first = half + entries * (far * rows + i)
+            row = held + entries * (1 - far)
+            table_ref[first : first + entries] = piece[row : row + entries].astype(jnp.int32)
     copy = pltpu.make_async_copy(table_ref, index_ref, sem)
     copy.start()
     for i, piece in enumerate(pieces):
-        held_ref[i] = piece[:held]
+        held_ref[i] = piece[...] if i < rows else piece[:held]
     out_ref[...] = jnp.zeros_like(out_ref)
     copy.wait()
 
@@ -175,7 +160,7 @@
         restricted = restricted_ref[near, pl.ds(pl.multiple_of(place * block_size, block_size), block_size)]
         product = transposed_dot(split3(block, "left"), split3(restricted, "right"))
         for m in range(entries):
-            column = own_ref[2 + index_ref[half + entries * piece + m, inside]]
+            column = index_ref[half + entries * piece + m, inside]
             out_ref[column] += product[m * block_size : (m + 1) * block_size]
         return carry
 
@@ -205,6 +190,24 @@
     )(own, restricted, *pieces)
 
 
+def add_kernel(parts_ref, out_ref):
+    total = parts_ref[0]
+    for i in range(1, parts_ref.shape[0]):
+        total = total + parts_ref[i]
+    out_ref[...] = total
+
+
+def add_up(parts):
+    return pl.pallas_call(
+        add_kernel,
+        out_shape=jax.ShapeDtypeStruct(parts.shape[1:], parts.dtype),
+        in_specs=[pl.BlockSpec(memory_space=pltpu.VMEM)],
+        out_specs=pl.BlockSpec(memory_space=pltpu.VMEM),
+        compiler_params=pltpu.CompilerParams(vmem_limit_bytes=VMEM_LIMIT),
+        name="add_up",
+    )(parts)
+
+
 def row_swap(x, bit):
     return lax.ppermute(x, "row", [(r, r ^ bit) for r in range(lax.axis_size("row"))])
 
@@ -221,26 +224,6 @@
             pieces[mask ^ bit] = row_swap(pieces[mask], bit)
         bit //= 2
     return [pieces[mask] for mask in range(rows)]
-
-
-def place_of_columns(columns):
-    ahead = jnp.arange(columns, dtype=jnp.int32) ^ (lax.axis_index("half") * (columns // 2) + lax.axis_index("near"))
-    place = jnp.zeros_like(ahead)
-    low, high = 1, columns // 2
-    while high:
-        place = place + jnp.where(ahead & low != 0, high, 0)
-        low, high = low * 2, high // 2
-    return place
-
-
-def add_over_columns(sums, half):
-    bit = 1
-    while bit < half:
-        kept, sent = jnp.split(sums, 2)
-        sums = kept + lax.ppermute(sent, "near", [(n, n ^ bit) for n in range(half)])
-        bit *= 2
-    kept, sent = jnp.split(sums, 2)
-    return kept[0] + half_swap(sent)[0]
 
 
 def local(
@@ -258,18 +241,20 @@
     fine_rows, block_size, width = prolong_blocks.shape
     fetch = fetch_lists.reshape(2 * half, slot_count).T
     own = jnp.stack([lax.axis_index("row"), lax.axis_index("half")])
-    own = jnp.concatenate([own, place_of_columns(2 * half)])
-
-    near_blocks = extend(prolong_cols.T, prolong_blocks.reshape(fine_rows * block_size, width))
+    own_columns = prolong_cols.T
+
+    near_blocks = prolong_blocks.reshape(fine_rows * block_size, width)
     far_blocks = half_swap(near_blocks)
+    far_columns = half_swap(own_columns)
     restricted, mark = restrict_operator(
         operator_count, operator_slot, restrict_rows.T, fetch, operator_blocks, restrict_blocks
     )
     restricted = lax.all_to_all(restricted, "near", split_axis=0, concat_axis=0, tiled=True)
-    far_blocks = hold_until(mark, far_blocks, HOLD_FLOPS)
+    far_blocks = append_columns(mark, far_columns, own_columns, far_blocks)
     pieces = spread_over_rows(near_blocks, rows) + spread_over_rows(far_blocks, rows)
     sums = combine(own, restricted, pieces, NCR * rows, slot_count, fine_rows, block_size)
-    return add_over_columns(sums, half).T
+    parts = lax.all_to_all(sums, ("half", "near"), split_axis=0, concat_axis=0, tiled=True)
+    return add_up(parts).T
 
 
 def solution(mesh):

time: 48.2 us -> 49.9 us (1.035)
  blocking collectives: 0 us -> 15.5 us
  waiting for transfers between devices: 23.4 us -> 16.4 us
  starting transfers between devices: 15.5 us -> 11.2 us
  Pallas kernels: 8.14 us -> 6.41 us
  other arithmetic: 0.74 us -> 0.07 us
    all_to_all x0 -> x1, blocking collectives: none -> 15.5 us  [local(): lax.all_to_all(sums, ('half', 'near'), split_axis=0, concat_axis=0, tiled...]
    ppermute x2 -> x0, waiting for transfers between devices: 8.04 us -> none  [add_over_columns(): lax.ppermute(sent, 'near', [(n, n ^ bit) for n in range(half)])]
    ppermute x6, waiting for transfers between devices: 6.84 us -> 11.6 us  [row_swap(): lax.ppermute(x, 'row', [(r, r ^ bit) for r in range(lax.axis_size('row'))])]
    ppermute x2, starting transfers between devices: 6.34 us -> 4.07 us  [half_swap(): return lax.ppermute(x, 'half', [(0, 1), (1, 0)])]
    all_to_all x1, waiting for transfers between devices: 2.24 us -> 0.01 us  [local(): lax.all_to_all(restricted, 'near', split_axis=0, concat_axis=0, tiled=True)]
    pallas_call x2, Pallas kernels: 2.37 us -> 0.65 us  [the longest x1 0.63 us: add_up(): pl.pallas_call(add_kernel, out_shape=jax.ShapeDtypeStruct(parts.shape[1:]...]
    ppermute x2 -> x0, starting transfers between devices: 1.67 us -> none  [add_over_columns(): lax.ppermute(sent, 'near', [(n, n ^ bit) for n in range(half)])]
    ppermute x2, waiting for transfers between devices: 6.32 us -> 4.75 us  [half_swap(): return lax.ppermute(x, 'half', [(0, 1), (1, 0)])]
  transfers between devices with their start and end apart: 11 -> 9, of which waited for: 7 -> 4; matrix products, arithmetic and copies ran while one was open for 0% -> 0% of each run, Pallas kernels for 7% -> 7%
where the time goes in v10:
time: 49.9 us; the launch traced here: 49.6 us
  waiting for transfers between devices  16.4 us (33%)
  blocking collectives  15.5 us (31%)
  starting transfers between devices  11.2 us (22%)
  Pallas kernels  6.41 us (13%)
    all_to_all x1, blocking collectives, local(): lax.all_to_all(sums, ('half', 'near'), split_axis=0, concat_axis=0, tiled...  15.5 us
    ppermute x6, waiting for transfers between devices, row_swap(): lax.ppermute(x, 'row', [(r, r ^ bit) for r in range(lax.axis_size('row'))])  11.6 us
    ppermute x2, waiting for transfers between devices, half_swap(): return lax.ppermute(x, 'half', [(0, 1), (1, 0)])  4.75 us
    all_to_all x1, starting transfers between devices, local(): lax.all_to_all(restricted, 'near', split_axis=0, concat_axis=0, tiled=True)  4.09 us
    ppermute x2, starting transfers between devices, half_swap(): return lax.ppermute(x, 'half', [(0, 1), (1, 0)])  4.07 us
    pallas_call x1, Pallas kernels, restrict_operator(): pl.pallas_call(restrict_kernel, out_shape=(jax.ShapeDtypeStruct((columns...  3.41 us
    ppermute x6, starting transfers between devices, row_swap(): lax.ppermute(x, 'row', [(r, r ^ bit) for r in range(lax.axis_size('row'))])  3 us
    pallas_call x1, Pallas kernels, combine(): pl.pallas_call(functools.partial(combine_kernel, slot_count=slot_count, f...  2.35 us
  transfers between devices with their start and end apart: 9, of which 4 were waited for; matrix products, arithmetic and copies ran while one was open for 0% of the time, Pallas kernels for 7%

profile of v10, /device:TPU:0, one launch (start us, length us, event | category | flops | bytes accessed | tf_op | source)
XLA Modules:
  0.0 49.6 jit_solution(11754041304330989712)
XLA Ops:
  0.0 4.0 %collective-permute-start.4 = (f32[512,128]{1,0:T(8,128)}, f32[512,128]{1,0:T(8,128)S(1)}, u32[]{:S(2)}, u32[]{:S(2)}) collective-permute-start(f32[512,128]{1,0:T(8,128)} %bitcast.9), channel_id=1, source_target_pairs={{0,4},{4,0},{1,5},{5,1},{2,6},{6,2},{3,7},{7,3},{8,12},{12,8},{9,1... | collective-permute-start | bytes 786440 | tf_op jit(solution)/shard_map/ppermute | solution.py:216
  4.0 0.0 collective-permute-start.3
  4.1 3.4 %restrict_operator.1 = (f32[4,520,128]{2,1,0:T(8,128)}, f32[8,128]{1,0:T(8,128)}) custom-call(s32[8]{0:T(128)} %count_any.1, s32[8,8]{1,0:T(8,128)} %slot_any.1, s32[2,8]{1,0:T(2,128)} %bitcast.16, s32[4,8]{1,0:T(4,128)} %bitcast.15, f32[8,64,128]{2,1,0:T(8,128)} %restrict_any.1, f32[8,64,512]{2,1,0:T(8,128)} %operator_any.1), custom_call_target="tpu_custom_call" | custom-call | flops 201326592 | bytes 4194304 | tf_op jit(solution)/shard_map/restrict_operator/pallas_call | solution.py:111
  7.5 0.0 copy-start.1
  7.5 0.0 copy-start.2
  7.5 4.1 %all-to-all-start = ((f32[4,520,128]{2,1,0:T(8,128)}), f32[4,520,128]{2,1,0:T(8,128)S(1)}, u32[]{:S(2)}, u32[]{:S(2)}) async-start(f32[4,520,128]{2,1,0:T(8,128)} %get-tuple-element.7), calls=%async_computation | async-start | bytes 2129920 | tf_op jit(solution)/shard_map/all_to_all | solution.py:252
  11.6 4.7 %collective-permute-done.3.far_columns_ref = s32[2,8]{1,0:T(2,128)S(1)} collective-permute-done((s32[2,8]{1,0:T(2,128)}, s32[2,8]{1,0:T(2,128)S(1)}, u32[]{:S(2)}, u32[]{:S(2)}) %collective-permute-start.3) | collective-permute-done | bytes 96 | tf_op jit(solution)/shard_map/ppermute | solution.py:216
  16.3 0.0 collective-permute-done.4.blocks_ref
  16.4 0.0 copy-start
  16.4 1.6 %collective-permute-start.6 = (f32[520,128]{1,0:T(8,128)S(1)}, f32[520,128]{1,0:T(8,128)S(1)}, u32[]{:S(2)}, u32[]{:S(2)}) collective-permute-start(f32[520,128]{1,0:T(8,128)S(1)} %append_columns.1.rest_4_), channel_id=1, source_target_pairs={{0,16},{8,24},{16,0},{24,8},{1,17},{9,25},{17,1},{25,9},{2,18},{10... | collective-permute-start | bytes 798728 | tf_op jit(solution)/shard_map/ppermute | solution.py:212
  18.0 0.8 %collective-permute-start.1 = (f32[512,128]{1,0:T(8,128)S(1)}, f32[512,128]{1,0:T(8,128)S(1)}, u32[]{:S(2)}, u32[]{:S(2)}) collective-permute-start(f32[512,128]{1,0:T(8,128)S(1)} %bitcast.10), channel_id=1, source_target_pairs={{0,16},{8,24},{16,0},{24,8},{1,17},{9,25},{17,1},{25,9},{2,18},{10... | collective-permute-start | bytes 786440 | tf_op jit(solution)/shard_map/ppermute | solution.py:212
  18.9 6.9 %collective-permute-done.6.rest_6_ = f32[520,128]{1,0:T(8,128)S(1)} collective-permute-done((f32[520,128]{1,0:T(8,128)S(1)}, f32[520,128]{1,0:T(8,128)S(1)}, u32[]{:S(2)}, u32[]{:S(2)}) %collective-permute-start.6) | collective-permute-done | bytes 266272 | tf_op jit(solution)/shard_map/ppermute | solution.py:212
  25.8 0.0 collective-permute-start.7
  25.8 0.5 %collective-permute-start = (f32[512,128]{1,0:T(8,128)S(1)}, f32[512,128]{1,0:T(8,128)S(1)}, u32[]{:S(2)}, u32[]{:S(2)}) collective-permute-start(f32[512,128]{1,0:T(8,128)S(1)} %bitcast.11), channel_id=1, source_target_pairs={{0,8},{8,0},{16,24},{24,16},{1,9},{9,1},{17,25},{25,17},{2,10},{10... | collective-permute-start | bytes 786440 | tf_op jit(solution)/shard_map/ppermute | solution.py:212
  26.3 3.3 %collective-permute-done.1.rest_2_ = f32[512,128]{1,0:T(8,128)S(1)} collective-permute-done((f32[512,128]{1,0:T(8,128)S(1)}, f32[512,128]{1,0:T(8,128)S(1)}, u32[]{:S(2)}, u32[]{:S(2)}) %collective-permute-start.1) | collective-permute-done | bytes 262176 | tf_op jit(solution)/shard_map/ppermute | solution.py:212
  29.6 0.0 collective-permute-start.2
  29.6 0.1 pad_add_fusion.own_ref
  29.6 0.0 collective-permute-done.rest_1_
  29.6 1.5 %collective-permute-done.2.rest_3_ = f32[512,128]{1,0:T(8,128)S(1)} collective-permute-done((f32[512,128]{1,0:T(8,128)S(1)}, f32[512,128]{1,0:T(8,128)S(1)}, u32[]{:S(2)}, u32[]{:S(2)}) %collective-permute-start.2) | collective-permute-done | bytes 262176 | tf_op jit(solution)/shard_map/ppermute | solution.py:212
  31.1 0.0 collective-permute-done.5.rest_5_
  31.1 0.0 collective-permute-done.7.rest_7_
  31.1 2.3 %combine.1 = f32[8,64,128]{2,1,0:T(8,128)S(1)} custom-call(s32[2]{0:T(128)S(1)} %pad_add_fusion.own_ref, f32[4,520,128]{2,1,0:T(8,128)S(1)} %all-to-all-done.restricted_ref, f32[512,128]{1,0:T(8,128)S(1)} %bitcast.12, f32[512,128]{1,0:T(8,128)S(1)} %collective-permute-done.rest_1_, f32[512,128]{1,0:T(8,128)S(1)} %collective-permute-done.1.rest_2_, ...), custom_call_target="tpu_custom_call" | custom-call | flops 268435456 | bytes 4194304 | tf_op jit(solution)/shard_map/combine/pallas_call | solution.py:175
  33.5 15.5 %all_to_all.10.parts_ref = f32[8,64,128]{2,1,0:T(8,128)S(1)} all-to-all(f32[8,64,128]{2,1,0:T(8,128)S(1)} %combine.1), channel_id=1, replica_groups=mesh['row'=4,'half'=2,'near'=4] {'half','near'}, dimensions={0} | all-to-all | bytes 524288 | tf_op jit(solution)/shard_map/all_to_all | solution.py:256
  49.0 0.6 %add_up.1 = f32[64,128]{1,0:T(8,128)} custom-call(f32[8,64,128]{2,1,0:T(8,128)S(1)} %all_to_all.10.parts_ref), custom_call_target="tpu_custom_call" | custom-call | tf_op jit(solution)/shard_map/add_up/pallas_call | solution.py:201
  (6 shorter events, 0.0 us)
Async XLA Ops:
  0.0 16.4 %collective-permute-start.4 = (f32[512,128]{1,0:T(8,128)}, f32[512,128]{1,0:T(8,128)S(1)}, u32[]{:S(2)}, u32[]{:S(2)}) collective-permute-start(f32[512,128]{1,0:T(8,128)} %bitcast.9), channel_id=1, source_target_pairs={{0,4},{4,0},{1,5},{5,1},{2,6},{6,2},{3,7},{7,3},{8,12},{12,8},{9,1... | collective-permute-start | bytes 786440 | tf_op jit(solution)/shard_map/ppermute | solution.py:216
  4.0 12.3 %collective-permute-start.3 = (s32[2,8]{1,0:T(2,128)}, s32[2,8]{1,0:T(2,128)S(1)}, u32[]{:S(2)}, u32[]{:S(2)}) collective-permute-start(s32[2,8]{1,0:T(2,128)} %bitcast.13), channel_id=1, source_target_pairs={{0,4},{4,0},{1,5},{5,1},{2,6},{6,2},{3,7},{7,3},{8,12},{12,8},{9,1... | collective-permute-start | bytes 200 | tf_op jit(solution)/shard_map/ppermute | solution.py:216
  7.5 8.9 %copy-start.1 = (f32[8,128]{1,0:T(8,128)S(1)}, f32[8,128]{1,0:T(8,128)}, u32[]{:S(2)}) copy-start(f32[8,128]{1,0:T(8,128)} %get-tuple-element.8.mark_ref) | copy-start | bytes 12292
  7.5 8.9 %copy-start.2 = (s32[8,2]{0,1:T(2,128)S(1)}, s32[8,2]{0,1:T(2,128)}, u32[]{:S(2)}) copy-start(s32[8,2]{0,1:T(2,128)} %param.13) | copy-start | bytes 196
  7.5 23.6 %all-to-all-start = ((f32[4,520,128]{2,1,0:T(8,128)}), f32[4,520,128]{2,1,0:T(8,128)S(1)}, u32[]{:S(2)}, u32[]{:S(2)}) async-start(f32[4,520,128]{2,1,0:T(8,128)} %get-tuple-element.7), calls=%async_computation | async-start | bytes 2129920 | tf_op jit(solution)/shard_map/all_to_all | solution.py:252
  16.4 1.7 %copy-start = (f32[8,64,128]{2,1,0:T(8,128)S(1)}, f32[8,64,128]{2,1,0:T(8,128)}, u32[]{:S(2)}) copy-start(f32[8,64,128]{2,1,0:T(8,128)} %param.12) | copy-start | bytes 786436
  16.4 9.4 %collective-permute-start.6 = (f32[520,128]{1,0:T(8,128)S(1)}, f32[520,128]{1,0:T(8,128)S(1)}, u32[]{:S(2)}, u32[]{:S(2)}) collective-permute-start(f32[520,128]{1,0:T(8,128)S(1)} %append_columns.1.rest_4_), channel_id=1, source_target_pairs={{0,16},{8,24},{16,0},{24,8},{1,17},{9,25},{17,1},{25,9},{2,18},{10... | collective-permute-start | bytes 798728 | tf_op jit(solution)/shard_map/ppermute | solution.py:212
  18.0 11.5 %collective-permute-start.1 = (f32[512,128]{1,0:T(8,128)S(1)}, f32[512,128]{1,0:T(8,128)S(1)}, u32[]{:S(2)}, u32[]{:S(2)}) collective-permute-start(f32[512,128]{1,0:T(8,128)S(1)} %bitcast.10), channel_id=1, source_target_pairs={{0,16},{8,24},{16,0},{24,8},{1,17},{9,25},{17,1},{25,9},{2,18},{10... | collective-permute-start | bytes 786440 | tf_op jit(solution)/shard_map/ppermute | solution.py:212
  18.9 12.2 %collective-permute-start.5 = (f32[520,128]{1,0:T(8,128)S(1)}, f32[520,128]{1,0:T(8,128)S(1)}, u32[]{:S(2)}, u32[]{:S(2)}) collective-permute-start(f32[520,128]{1,0:T(8,128)S(1)} %append_columns.1.rest_4_), channel_id=1, source_target_pairs={{0,8},{8,0},{16,24},{24,16},{1,9},{9,1},{17,25},{25,17},{2,10},{10... | collective-permute-start | bytes 798728 | tf_op jit(solution)/shard_map/ppermute | solution.py:212
  25.8 5.3 %collective-permute-start.7 = (f32[520,128]{1,0:T(8,128)S(1)}, f32[520,128]{1,0:T(8,128)S(1)}, u32[]{:S(2)}, u32[]{:S(2)}) collective-permute-start(f32[520,128]{1,0:T(8,128)S(1)} %collective-permute-done.6.rest_6_), channel_id=1, source_target_pairs={{0,8},{8,0},{16,24},{24,16},{1,9},{9,1},{17,25},{25,17},{2,10},{10... | collective-permute-start | bytes 798728 | tf_op jit(solution)/shard_map/ppermute | solution.py:212
  25.8 3.8 %collective-permute-start = (f32[512,128]{1,0:T(8,128)S(1)}, f32[512,128]{1,0:T(8,128)S(1)}, u32[]{:S(2)}, u32[]{:S(2)}) collective-permute-start(f32[512,128]{1,0:T(8,128)S(1)} %bitcast.11), channel_id=1, source_target_pairs={{0,8},{8,0},{16,24},{24,16},{1,9},{9,1},{17,25},{25,17},{2,10},{10... | collective-permute-start | bytes 786440 | tf_op jit(solution)/shard_map/ppermute | solution.py:212
  29.6 1.5 %collective-permute-start.2 = (f32[512,128]{1,0:T(8,128)S(1)}, f32[512,128]{1,0:T(8,128)S(1)}, u32[]{:S(2)}, u32[]{:S(2)}) collective-permute-start(f32[512,128]{1,0:T(8,128)S(1)} %collective-permute-done.1.rest_2_), channel_id=1, source_target_pairs={{0,8},{8,0},{16,24},{24,16},{1,9},{9,1},{17,25},{25,17},{2,10},{10... | collective-permute-start | bytes 786440 | tf_op jit(solution)/shard_map/ppermute | solution.py:212

commit v11 on v10

--- a/solution.py
+++ b/solution.py
@@ -26,7 +26,23 @@
     return lax.dot_general(left, right, (((0,), (0,)), ((), ())), preferred_element_type=jnp.float32)
 
 
-def append_kernel(mark_ref, far_columns_ref, own_columns_ref, blocks_ref, out_ref):
+def hold_kernel(mark_ref, blocks_ref, out_ref):
+    out_ref[...] = blocks_ref[...]
+
+
+def hold_until(mark, blocks):
+    return pl.pallas_call(
+        hold_kernel,
+        out_shape=jax.ShapeDtypeStruct(blocks.shape, blocks.dtype),
+        in_specs=[pl.BlockSpec(memory_space=pltpu.VMEM)] * 2,
+        out_specs=pl.BlockSpec(memory_space=pltpu.VMEM),
+        compiler_params=pltpu.CompilerParams(vmem_limit_bytes=VMEM_LIMIT),
+        cost_estimate=pl.CostEstimate(flops=HOLD_FLOPS, bytes_accessed=HOLD_FLOPS >> 8, transcendentals=0),
+        name="hold_until",
+    )(mark, blocks)
+
+
+def append_kernel(far_columns_ref, own_columns_ref, next_ref, blocks_ref, out_ref):
     used = blocks_ref.shape[0]
     entries, fine_rows = own_columns_ref.shape
     out_ref[:used] = blocks_ref[...]
@@ -35,7 +51,7 @@
     out_ref[used + entries : used + 2 * entries, :fine_rows] = own_columns_ref[...].astype(jnp.float32)
 
 
-def append_columns(mark, far_columns, own_columns, blocks):
+def append_columns(far_columns, own_columns, next_blocks, blocks):
     used, width = blocks.shape
     return pl.pallas_call(
         append_kernel,
@@ -43,13 +59,13 @@
         in_specs=[pl.BlockSpec(memory_space=pltpu.VMEM)] * 4,
         out_specs=pl.BlockSpec(memory_space=pltpu.VMEM),
         compiler_params=pltpu.CompilerParams(vmem_limit_bytes=VMEM_LIMIT),
-        cost_estimate=pl.CostEstimate(flops=HOLD_FLOPS, bytes_accessed=HOLD_FLOPS >> 8, transcendentals=0),
+        cost_estimate=pl.CostEstimate(flops=0, bytes_accessed=1 << 19, transcendentals=0),
         name="append_columns",
-    )(mark, far_columns, own_columns, blocks)
+    )(far_columns, own_columns, next_blocks, blocks)
 
 
 def restrict_kernel(
-    count_any, slot_any, rows_any, fetch_any, restrict_any, operator_any, out_ref, mark_ref,
+    count_any, slot_any, rows_any, fetch_any, restrict_any, operator_any, columns_any, out_ref, mark_ref,
     count_ref, slot_ref, rows_ref, fetch_ref, restrict_ref, operator_ref, sems, operator_sems,
 ):
     fine_rows, block_size, _ = operator_ref.shape
@@ -61,7 +77,7 @@
 
     pairs = [
         (count_any, count_ref), (slot_any, slot_ref), (rows_any, rows_ref),
-        (fetch_any, fetch_ref), (restrict_any, restrict_ref),
+        (fetch_any, fetch_ref), (restrict_any, restrict_ref), (columns_any, mark_ref),
     ]
     copies = [pltpu.make_async_copy(a, b, sems.at[i]) for i, (a, b) in enumerate(pairs)]
     operators = [
@@ -85,7 +101,6 @@
                 wanted = fetch_ref[s, side * half + near]
                 value = jnp.where(short_lane == side * slot_count + s, wanted, value)
         out_ref[near, used:] = value.astype(jnp.float32)
-    mark_ref[...] = out_ref[0, used:]
 
     for i in range(fine_rows):
         value = restrict_ref[i]
@@ -102,7 +117,9 @@
             out_ref[lax.rem(peer, half), pl.ds(start, block_size)] += part
 
 
-def restrict_operator(operator_count, operator_slot, restrict_rows, fetch, operator_blocks, restrict_blocks):
+def restrict_operator(
+    operator_count, operator_slot, restrict_rows, fetch, operator_blocks, restrict_blocks, prolong_columns
+):
     fine_rows, block_size, width = operator_blocks.shape
     slot_count, columns = fetch.shape
     wide = NCR * block_size
@@ -112,18 +129,18 @@
         restrict_kernel,
         out_shape=(
             jax.ShapeDtypeStruct((columns // 2, rows, wide), jnp.float32),
-            jax.ShapeDtypeStruct((EXTRA, wide), jnp.float32),
+            jax.ShapeDtypeStruct(prolong_columns.shape, prolong_columns.dtype),
         ),
-        in_specs=[pl.BlockSpec(memory_space=pltpu.HBM)] * 6,
+        in_specs=[pl.BlockSpec(memory_space=pltpu.HBM)] * 7,
         out_specs=[pl.BlockSpec(memory_space=pltpu.VMEM)] * 2,
         scratch_shapes=[pltpu.SMEM(x.shape, x.dtype) for x in small]
         + [pltpu.VMEM(x.shape, x.dtype) for x in (restrict_blocks, operator_blocks)]
-        + [pltpu.SemaphoreType.DMA((5,)), pltpu.SemaphoreType.DMA((fine_rows,))],
+        + [pltpu.SemaphoreType.DMA((6,)), pltpu.SemaphoreType.DMA((fine_rows,))],
         cost_estimate=pl.CostEstimate(
             flops=6 * fine_rows * block_size * width * wide, bytes_accessed=4 << 20, transcendentals=0
         ),
         name="restrict_operator",
-    )(*small, restrict_blocks, operator_blocks)
+    )(*small, restrict_blocks, operator_blocks, prolong_columns)
 
 
 def combine_kernel(own_ref, restricted_ref, *rest, slot_count, fine_rows, entries):
@@ -241,17 +258,18 @@
     fine_rows, block_size, width = prolong_blocks.shape
     fetch = fetch_lists.reshape(2 * half, slot_count).T
     own = jnp.stack([lax.axis_index("row"), lax.axis_index("half")])
-    own_columns = prolong_cols.T
 
     near_blocks = prolong_blocks.reshape(fine_rows * block_size, width)
     far_blocks = half_swap(near_blocks)
-    far_columns = half_swap(own_columns)
-    restricted, mark = restrict_operator(
-        operator_count, operator_slot, restrict_rows.T, fetch, operator_blocks, restrict_blocks
+    restricted, own_columns = restrict_operator(
+        operator_count, operator_slot, restrict_rows.T, fetch, operator_blocks, restrict_blocks, prolong_cols.T
     )
     restricted = lax.all_to_all(restricted, "near", split_axis=0, concat_axis=0, tiled=True)
-    far_blocks = append_columns(mark, far_columns, own_columns, far_blocks)
-    pieces = spread_over_rows(near_blocks, rows) + spread_over_rows(far_blocks, rows)
+    far_columns = half_swap(own_columns)
+    near_pieces = spread_over_rows(near_blocks, rows)
+    far_blocks = hold_until(own_columns, far_blocks)
+    far_blocks = append_columns(far_columns, own_columns, near_pieces[rows // 2], far_blocks)
+    pieces = near_pieces + spread_over_rows(far_blocks, rows)
     sums = combine(own, restricted, pieces, NCR * rows, slot_count, fine_rows, block_size)
     parts = lax.all_to_all(sums, ("half", "near"), split_axis=0, concat_axis=0, tiled=True)
     return add_up(parts).T

time: 49.9 us -> 50.7 us (1.016)
  waiting for transfers between devices: 16.4 us -> 18.7 us
  blocking collectives: 15.5 us -> 14.5 us
    ppermute x2, waiting for transfers between devices: 4.75 us -> 10.8 us  [half_swap(): return lax.ppermute(x, 'half', [(0, 1), (1, 0)])]
    ppermute x6, waiting for transfers between devices: 11.6 us -> 7.86 us  [row_swap(): lax.ppermute(x, 'row', [(r, r ^ bit) for r in range(lax.axis_size('row'))])]
    all_to_all x1, blocking collectives: 15.5 us -> 14.5 us  [local(): lax.all_to_all(sums, ('half', 'near'), split_axis=0, concat_axis=0, tiled...]
  transfers between devices with their start and end apart: 9 -> 9, of which waited for: 4 -> 5; matrix products, arithmetic and copies ran while one was open for 0% -> 0% of each run, Pallas kernels for 7% -> 7%
where the time goes in v11:
time: 50.7 us; the launch traced here: 50.5 us
  waiting for transfers between devices  18.7 us (37%)
  blocking collectives  14.5 us (29%)
  starting transfers between devices  10.8 us (21%)
  Pallas kernels  6.44 us (13%)
    all_to_all x1, blocking collectives, local(): lax.all_to_all(sums, ('half', 'near'), split_axis=0, concat_axis=0, tiled...  14.5 us
    ppermute x2, waiting for transfers between devices, half_swap(): return lax.ppermute(x, 'half', [(0, 1), (1, 0)])  10.8 us
    ppermute x6, waiting for transfers between devices, row_swap(): lax.ppermute(x, 'row', [(r, r ^ bit) for r in range(lax.axis_size('row'))])  7.86 us
    ppermute x2, starting transfers between devices, half_swap(): return lax.ppermute(x, 'half', [(0, 1), (1, 0)])  4.37 us
    all_to_all x1, starting transfers between devices, local(): lax.all_to_all(restricted, 'near', split_axis=0, concat_axis=0, tiled=True)  3.78 us
    pallas_call x1, Pallas kernels, restrict_operator(): pl.pallas_call(restrict_kernel, out_shape=(jax.ShapeDtypeStruct((columns...  3.42 us
    ppermute x6, starting transfers between devices, row_swap(): lax.ppermute(x, 'row', [(r, r ^ bit) for r in range(lax.axis_size('row'))])  2.6 us
    pallas_call x1, Pallas kernels, combine(): pl.pallas_call(functools.partial(combine_kernel, slot_count=slot_count, f...  2.35 us
  transfers between devices with their start and end apart: 9, of which 5 were waited for; matrix products, arithmetic and copies ran while one was open for 0% of the time, Pallas kernels for 7%

profile of v11, /device:TPU:0, one launch (start us, length us, event | category | flops | bytes accessed | tf_op | source)
XLA Modules:
  0.0 50.5 jit_solution(8495451337680273515)
XLA Ops:
  0.0 4.0 %collective-permute-start.4 = (f32[512,128]{1,0:T(8,128)}, f32[512,128]{1,0:T(8,128)S(1)}, u32[]{:S(2)}, u32[]{:S(2)}) collective-permute-start(f32[512,128]{1,0:T(8,128)} %bitcast.9), channel_id=1, source_target_pairs={{0,4},{4,0},{1,5},{5,1},{2,6},{6,2},{3,7},{7,3},{8,12},{12,8},{9,1... | collective-permute-start | bytes 786440 | tf_op jit(solution)/shard_map/ppermute | solution.py:233
  4.0 1.5 %collective-permute-start.1 = (f32[512,128]{1,0:T(8,128)}, f32[512,128]{1,0:T(8,128)S(1)}, u32[]{:S(2)}, u32[]{:S(2)}) collective-permute-start(f32[512,128]{1,0:T(8,128)} %bitcast.10), channel_id=1, source_target_pairs={{0,16},{8,24},{16,0},{24,8},{1,17},{9,25},{17,1},{25,9},{2,18},{10... | collective-permute-start | bytes 786440 | tf_op jit(solution)/shard_map/ppermute | solution.py:229
  5.6 3.4 %restrict_operator.1 = (f32[4,520,128]{2,1,0:T(8,128)}, s32[2,8]{1,0:T(2,128)}) custom-call(s32[8]{0:T(128)} %count_any.1, s32[8,8]{1,0:T(8,128)} %slot_any.1, s32[2,8]{1,0:T(2,128)} %bitcast.14, s32[4,8]{1,0:T(4,128)} %bitcast.13, f32[8,64,128]{2,1,0:T(8,128)} %restrict_any.1, f32[8,64,512]{2,1,0:T(8,128)} %operator_any.1, s32[2,8]{1,0:T(2,128)} %bitcast.15), custom_call_target="tpu_custom_call" | custom-call | flops 201326592 | bytes 4194304 | tf_op jit(solution)/shard_map/restrict_operator/pallas_call | solution.py:128
  9.0 0.0 copy-start.1
  9.0 3.8 %all-to-all-start = ((f32[4,520,128]{2,1,0:T(8,128)}), f32[4,520,128]{2,1,0:T(8,128)S(1)}, u32[]{:S(2)}, u32[]{:S(2)}) async-start(f32[4,520,128]{2,1,0:T(8,128)} %get-tuple-element.7), calls=%async_computation | async-start | bytes 2129920 | tf_op jit(solution)/shard_map/all_to_all | solution.py:267
  12.8 0.3 collective-permute-start.3
  13.1 3.2 %collective-permute-done.4.blocks_ref = f32[512,128]{1,0:T(8,128)S(1)} collective-permute-done((f32[512,128]{1,0:T(8,128)}, f32[512,128]{1,0:T(8,128)S(1)}, u32[]{:S(2)}, u32[]{:S(2)}) %collective-permute-start.4) | collective-permute-done | bytes 262176 | tf_op jit(solution)/shard_map/ppermute | solution.py:233
  16.3 7.7 %collective-permute-done.3.far_columns_ref = s32[2,8]{1,0:T(2,128)S(1)} collective-permute-done((s32[2,8]{1,0:T(2,128)S(1)}, s32[2,8]{1,0:T(2,128)S(1)}, u32[]{:S(2)}, u32[]{:S(2)}) %collective-permute-start.3) | collective-permute-done | bytes 96 | tf_op jit(solution)/shard_map/ppermute | solution.py:233
  24.0 0.0 collective-permute-done.1.next_ref.rest_2_
  24.0 0.6 %collective-permute-start.6 = (f32[520,128]{1,0:T(8,128)S(1)}, f32[520,128]{1,0:T(8,128)S(1)}, u32[]{:S(2)}, u32[]{:S(2)}) collective-permute-start(f32[520,128]{1,0:T(8,128)S(1)} %append_columns.1.rest_4_), channel_id=1, source_target_pairs={{0,16},{8,24},{16,0},{24,8},{1,17},{9,25},{17,1},{25,9},{2,18},{10... | collective-permute-start | bytes 798728 | tf_op jit(solution)/shard_map/ppermute | solution.py:229
  24.6 0.0 collective-permute-start.5
  24.6 6.2 %collective-permute-done.6.rest_6_ = f32[520,128]{1,0:T(8,128)S(1)} collective-permute-done((f32[520,128]{1,0:T(8,128)S(1)}, f32[520,128]{1,0:T(8,128)S(1)}, u32[]{:S(2)}, u32[]{:S(2)}) %collective-permute-start.6) | collective-permute-done | bytes 266272 | tf_op jit(solution)/shard_map/ppermute | solution.py:229
  30.7 0.0 collective-permute-start.7
  30.7 0.5 %collective-permute-start = (f32[512,128]{1,0:T(8,128)S(1)}, f32[512,128]{1,0:T(8,128)S(1)}, u32[]{:S(2)}, u32[]{:S(2)}) collective-permute-start(f32[512,128]{1,0:T(8,128)S(1)} %bitcast.11), channel_id=1, source_target_pairs={{0,8},{8,0},{16,24},{24,16},{1,9},{9,1},{17,25},{25,17},{2,10},{10... | collective-permute-start | bytes 786440 | tf_op jit(solution)/shard_map/ppermute | solution.py:229
  31.2 0.0 collective-permute-start.2
  31.2 0.1 pad_add_fusion.own_ref
  31.3 1.3 %collective-permute-done.rest_1_ = f32[512,128]{1,0:T(8,128)S(1)} collective-permute-done((f32[512,128]{1,0:T(8,128)S(1)}, f32[512,128]{1,0:T(8,128)S(1)}, u32[]{:S(2)}, u32[]{:S(2)}) %collective-permute-start) | collective-permute-done | bytes 262176 | tf_op jit(solution)/shard_map/ppermute | solution.py:229
  32.6 0.4 collective-permute-done.2.rest_3_
  33.0 0.0 collective-permute-done.5.rest_5_
  33.0 0.0 collective-permute-done.7.rest_7_
  33.0 0.0 all-to-all-done.restricted_ref
  33.0 2.3 %combine.1 = f32[8,64,128]{2,1,0:T(8,128)S(1)} custom-call(s32[2]{0:T(128)S(1)} %pad_add_fusion.own_ref, f32[4,520,128]{2,1,0:T(8,128)S(1)} %all-to-all-done.restricted_ref, f32[512,128]{1,0:T(8,128)S(1)} %bitcast.12, f32[512,128]{1,0:T(8,128)S(1)} %collective-permute-done.rest_1_, f32[512,128]{1,0:T(8,128)S(1)} %collective-permute-done.1.next_ref.rest_2_, ...), custom_call_target="tpu_custom_call" | custom-call | flops 268435456 | bytes 4194304 | tf_op jit(solution)/shard_map/combine/pallas_call | solution.py:192
  35.4 14.5 %all_to_all.10.parts_ref = f32[8,64,128]{2,1,0:T(8,128)S(1)} all-to-all(f32[8,64,128]{2,1,0:T(8,128)S(1)} %combine.1), channel_id=1, replica_groups=mesh['row'=4,'half'=2,'near'=4] {'half','near'}, dimensions={0} | all-to-all | bytes 524288 | tf_op jit(solution)/shard_map/all_to_all | solution.py:274
  49.9 0.6 %add_up.1 = f32[64,128]{1,0:T(8,128)} custom-call(f32[8,64,128]{2,1,0:T(8,128)S(1)} %all_to_all.10.parts_ref), custom_call_target="tpu_custom_call" | custom-call | tf_op jit(solution)/shard_map/add_up/pallas_call | solution.py:218
  (5 shorter events, 0.0 us)
Async XLA Ops:
  0.0 16.3 %collective-permute-start.4 = (f32[512,128]{1,0:T(8,128)}, f32[512,128]{1,0:T(8,128)S(1)}, u32[]{:S(2)}, u32[]{:S(2)}) collective-permute-start(f32[512,128]{1,0:T(8,128)} %bitcast.9), channel_id=1, source_target_pairs={{0,4},{4,0},{1,5},{5,1},{2,6},{6,2},{3,7},{7,3},{8,12},{12,8},{9,1... | collective-permute-start | bytes 786440 | tf_op jit(solution)/shard_map/ppermute | solution.py:233
  4.0 19.9 %collective-permute-start.1 = (f32[512,128]{1,0:T(8,128)}, f32[512,128]{1,0:T(8,128)S(1)}, u32[]{:S(2)}, u32[]{:S(2)}) collective-permute-start(f32[512,128]{1,0:T(8,128)} %bitcast.10), channel_id=1, source_target_pairs={{0,16},{8,24},{16,0},{24,8},{1,17},{9,25},{17,1},{25,9},{2,18},{10... | collective-permute-start | bytes 786440 | tf_op jit(solution)/shard_map/ppermute | solution.py:229
  9.0 3.8 %copy-start.1 = (s32[2,8]{1,0:T(2,128)S(1)}, s32[2,8]{1,0:T(2,128)}, u32[]{:S(2)}) copy-start(s32[2,8]{1,0:T(2,128)} %get-tuple-element.8.mark_ref.own_columns_ref) | copy-start | bytes 196
  9.0 24.0 %all-to-all-start = ((f32[4,520,128]{2,1,0:T(8,128)}), f32[4,520,128]{2,1,0:T(8,128)S(1)}, u32[]{:S(2)}, u32[]{:S(2)}) async-start(f32[4,520,128]{2,1,0:T(8,128)} %get-tuple-element.7), calls=%async_computation | async-start | bytes 2129920 | tf_op jit(solution)/shard_map/all_to_all | solution.py:267
  12.8 17.9 %copy-start = (f32[8,64,128]{2,1,0:T(8,128)S(1)}, f32[8,64,128]{2,1,0:T(8,128)}, u32[]{:S(2)}) copy-start(f32[8,64,128]{2,1,0:T(8,128)} %param.12) | copy-start | bytes 786436
  12.8 11.2 %collective-permute-start.3 = (s32[2,8]{1,0:T(2,128)S(1)}, s32[2,8]{1,0:T(2,128)S(1)}, u32[]{:S(2)}, u32[]{:S(2)}) collective-permute-start(s32[2,8]{1,0:T(2,128)S(1)} %copy-done.1), channel_id=1, source_target_pairs={{0,4},{4,0},{1,5},{5,1},{2,6},{6,2},{3,7},{7,3},{8,12},{12,8},{9,1... | collective-permute-start | bytes 200 | tf_op jit(solution)/shard_map/ppermute | solution.py:233
  24.0 6.7 %collective-permute-start.6 = (f32[520,128]{1,0:T(8,128)S(1)}, f32[520,128]{1,0:T(8,128)S(1)}, u32[]{:S(2)}, u32[]{:S(2)}) collective-permute-start(f32[520,128]{1,0:T(8,128)S(1)} %append_columns.1.rest_4_), channel_id=1, source_target_pairs={{0,16},{8,24},{16,0},{24,8},{1,17},{9,25},{17,1},{25,9},{2,18},{10... | collective-permute-start | bytes 798728 | tf_op jit(solution)/shard_map/ppermute | solution.py:229
  24.6 8.5 %collective-permute-start.5 = (f32[520,128]{1,0:T(8,128)S(1)}, f32[520,128]{1,0:T(8,128)S(1)}, u32[]{:S(2)}, u32[]{:S(2)}) collective-permute-start(f32[520,128]{1,0:T(8,128)S(1)} %append_columns.1.rest_4_), channel_id=1, source_target_pairs={{0,8},{8,0},{16,24},{24,16},{1,9},{9,1},{17,25},{25,17},{2,10},{10... | collective-permute-start | bytes 798728 | tf_op jit(solution)/shard_map/ppermute | solution.py:229
  30.7 2.3 %collective-permute-start.7 = (f32[520,128]{1,0:T(8,128)S(1)}, f32[520,128]{1,0:T(8,128)S(1)}, u32[]{:S(2)}, u32[]{:S(2)}) collective-permute-start(f32[520,128]{1,0:T(8,128)S(1)} %collective-permute-done.6.rest_6_), channel_id=1, source_target_pairs={{0,8},{8,0},{16,24},{24,16},{1,9},{9,1},{17,25},{25,17},{2,10},{10... | collective-permute-start | bytes 798728 | tf_op jit(solution)/shard_map/ppermute | solution.py:229
  30.7 1.9 %collective-permute-start = (f32[512,128]{1,0:T(8,128)S(1)}, f32[512,128]{1,0:T(8,128)S(1)}, u32[]{:S(2)}, u32[]{:S(2)}) collective-permute-start(f32[512,128]{1,0:T(8,128)S(1)} %bitcast.11), channel_id=1, source_target_pairs={{0,8},{8,0},{16,24},{24,16},{1,9},{9,1},{17,25},{25,17},{2,10},{10... | collective-permute-start | bytes 786440 | tf_op jit(solution)/shard_map/ppermute | solution.py:229
  31.2 1.8 %collective-permute-start.2 = (f32[512,128]{1,0:T(8,128)S(1)}, f32[512,128]{1,0:T(8,128)S(1)}, u32[]{:S(2)}, u32[]{:S(2)}) collective-permute-start(f32[512,128]{1,0:T(8,128)S(1)} %collective-permute-done.1.next_ref.rest_2_), channel_id=1, source_target_pairs={{0,8},{8,0},{16,24},{24,16},{1,9},{9,1},{17,25},{25,17},{2,10},{10... | collective-permute-start | bytes 786440 | tf_op jit(solution)/shard_map/ppermute | solution.py:229

commit v12 on v9

--- a/solution.py
+++ b/solution.py
@@ -24,29 +24,6 @@
 
 def transposed_dot(left, right):
     return lax.dot_general(left, right, (((0,), (0,)), ((), ())), preferred_element_type=jnp.float32)
-
-
-def extend_kernel(columns_ref, blocks_any, out_ref, sem):
-    used = blocks_any.shape[0]
-    entries, fine_rows = columns_ref.shape
-    copy = pltpu.make_async_copy(blocks_any, out_ref.at[pl.ds(0, used)], sem)
-    copy.start()
-    out_ref[used:] = jnp.zeros((EXTRA, out_ref.shape[1]), jnp.float32)
-    out_ref[used : used + entries, :fine_rows] = columns_ref[...].astype(jnp.float32)
-    copy.wait()
-
-
-def extend(columns, blocks):
-    used, width = blocks.shape
-    return pl.pallas_call(
-        extend_kernel,
-        out_shape=jax.ShapeDtypeStruct((used + EXTRA, width), blocks.dtype),
-        in_specs=[pl.BlockSpec(memory_space=pltpu.VMEM), pl.BlockSpec(memory_space=pltpu.HBM)],
-        out_specs=pl.BlockSpec(memory_space=pltpu.VMEM),
-        scratch_shapes=[pltpu.SemaphoreType.DMA],
-        cost_estimate=pl.CostEstimate(flops=0, bytes_accessed=1 << 19, transcendentals=0),
-        name="extend",
-    )(columns, blocks)
 
 
 def hold_kernel(mark_ref, blocks_ref, out_ref):
@@ -223,24 +200,24 @@
     return [pieces[mask] for mask in range(rows)]
 
 
-def place_of_columns(columns):
-    ahead = jnp.arange(columns, dtype=jnp.int32) ^ (lax.axis_index("half") * (columns // 2) + lax.axis_index("near"))
-    place = jnp.zeros_like(ahead)
-    low, high = 1, columns // 2
-    while high:
-        place = place + jnp.where(ahead & low != 0, high, 0)
-        low, high = low * 2, high // 2
-    return place
+def place_of_columns(half):
+    own = lax.axis_index("half") * half + lax.axis_index("near")
+    ahead = jnp.arange(2 * half, dtype=jnp.int32) ^ own
+    return ahead % half * 2 + ahead // half
 
 
 def add_over_columns(sums, half):
-    bit = 1
-    while bit < half:
-        kept, sent = jnp.split(sums, 2)
-        sums = kept + lax.ppermute(sent, "near", [(n, n ^ bit) for n in range(half)])
-        bit *= 2
-    kept, sent = jnp.split(sums, 2)
-    return kept[0] + half_swap(sent)[0]
+    total = sums[:2]
+    for near in range(1, half):
+        total = total + lax.ppermute(sums[2 * near : 2 * near + 2], "near", [(n, n ^ near) for n in range(half)])
+    return total[0] + half_swap(total[1])
+
+
+def with_columns(columns, blocks):
+    entries, fine_rows = columns.shape
+    used, width = blocks.shape
+    rows = jnp.pad(columns.astype(blocks.dtype), ((0, EXTRA - entries), (0, width - fine_rows)))
+    return jnp.concatenate([blocks, rows], axis=0)
 
 
 def local(
@@ -258,9 +235,9 @@
     fine_rows, block_size, width = prolong_blocks.shape
     fetch = fetch_lists.reshape(2 * half, slot_count).T
     own = jnp.stack([lax.axis_index("row"), lax.axis_index("half")])
-    own = jnp.concatenate([own, place_of_columns(2 * half)])
-
-    near_blocks = extend(prolong_cols.T, prolong_blocks.reshape(fine_rows * block_size, width))
+    own = jnp.concatenate([own, place_of_columns(half)])
+
+    near_blocks = with_columns(prolong_cols.T, prolong_blocks.reshape(fine_rows * block_size, width))
     far_blocks = half_swap(near_blocks)
     restricted, mark = restrict_operator(
         operator_count, operator_slot, restrict_rows.T, fetch, operator_blocks, restrict_blocks

time: 48.2 us -> 44.8 us (0.929)
  waiting for transfers between devices: 23.4 us -> 19.1 us
  Pallas kernels: 8.14 us -> 5.78 us
  starting transfers between devices: 15.5 us -> 17.2 us
  other arithmetic: 0.74 us -> 2.38 us
    ppermute x2 -> x3, waiting for transfers between devices: 8.04 us -> 3.78 us  [add_over_columns(): lax.ppermute(sums[2 * near:2 * near + 2], 'near', [(n, n ^ near) for n in...]
    pallas_call x1 -> x0, Pallas kernels: 2.35 us -> none  [extend(): pl.pallas_call(extend_kernel, out_shape=jax.ShapeDtypeStruct((used + EXTR...]
    ppermute x2 -> x3, starting transfers between devices: 1.67 us -> 3.55 us  [add_over_columns(): lax.ppermute(sums[2 * near:2 * near + 2], 'near', [(n, n ^ near) for n in...]
    concatenate x1 -> x2, other arithmetic: 0.08 us -> 1.05 us  [the longest x1 0.97 us: with_columns(): return jnp.concatenate([blocks, rows], axis=0)]
    convert_element_type x0 -> x1, other arithmetic: none -> 0.68 us  [with_columns(): columns.astype(blocks.dtype)]
  transfers between devices with their start and end apart: 11 -> 12, of which waited for: 7 -> 8; matrix products, arithmetic and copies ran while one was open for 0% -> 0% of each run, Pallas kernels for 7% -> 8%
where the time goes in v12:
time: 44.8 us; the launch traced here: 44.6 us
  waiting for transfers between devices  19.1 us (43%)
  starting transfers between devices  17.2 us (38%)
  Pallas kernels  5.78 us (13%)
  other arithmetic  2.38 us (5%)
    ppermute x6, waiting for transfers between devices, row_swap(): lax.ppermute(x, 'row', [(r, r ^ bit) for r in range(lax.axis_size('row'))])  6.83 us
    ppermute x2, waiting for transfers between devices, half_swap(): return lax.ppermute(x, 'half', [(0, 1), (1, 0)])  6.26 us
    ppermute x2, starting transfers between devices, half_swap(): return lax.ppermute(x, 'half', [(0, 1), (1, 0)])  6.19 us
    all_to_all x1, starting transfers between devices, local(): lax.all_to_all(restricted, 'near', split_axis=0, concat_axis=0, tiled=True)  3.78 us
    ppermute x3, waiting for transfers between devices, add_over_columns(): lax.ppermute(sums[2 * near:2 * near + 2], 'near', [(n, n ^ near) for n in...  3.78 us
    ppermute x6, starting transfers between devices, row_swap(): lax.ppermute(x, 'row', [(r, r ^ bit) for r in range(lax.axis_size('row'))])  3.67 us
    ppermute x3, starting transfers between devices, add_over_columns(): lax.ppermute(sums[2 * near:2 * near + 2], 'near', [(n, n ^ near) for n in...  3.55 us
    pallas_call x1, Pallas kernels, restrict_operator(): pl.pallas_call(restrict_kernel, out_shape=(jax.ShapeDtypeStruct((columns...  3.4 us
  transfers between devices with their start and end apart: 12, of which 8 were waited for; matrix products, arithmetic and copies ran while one was open for 0% of the time, Pallas kernels for 8%

profile of v12, /device:TPU:0, one launch (start us, length us, event | category | flops | bytes accessed | tf_op | source)
XLA Modules:
  0.0 44.6 jit_solution(9750278152531292603)
XLA Ops:
  0.0 0.7 %convert_bitcast_fusion = f32[2,8]{1,0:T(2,128)S(1)} fusion(s32[8,2]{0,1:T(2,128)} %param.13), kind=kLoop, calls=%fused_computation.14 | loop fusion | flops 16 | bytes 128 | tf_op jit(solution)/shard_map/convert_element_type | solution.py:219
  0.7 1.0 %select_maximum_fusion.rest_0_ = f32[520,128]{1,0:T(8,128)S(1)} fusion(f32[2,8]{1,0:T(2,128)S(1)} %convert_bitcast_fusion, f32[512,128]{1,0:T(8,128)} %bitcast.19), kind=kLoop, calls=%fused_computation | loop fusion | flops 199680 | bytes 528448 | tf_op jit(solution)/shard_map/concatenate | solution.py:220
  1.7 4.1 %collective-permute-start.3 = (f32[520,128]{1,0:T(8,128)S(1)}, f32[520,128]{1,0:T(8,128)S(1)}, u32[]{:S(2)}, u32[]{:S(2)}) collective-permute-start(f32[520,128]{1,0:T(8,128)S(1)} %select_maximum_fusion.rest_0_), channel_id=1, source_target_pairs={{0,4},{4,0},{1,5},{5,1},{2,6},{6,2},{3,7},{7,3},{8,12},{12,8},{9,1... | collective-permute-start | bytes 798728 | tf_op jit(solution)/shard_map/ppermute | solution.py:190
  5.8 1.5 %collective-permute-start.1 = (f32[520,128]{1,0:T(8,128)S(1)}, f32[520,128]{1,0:T(8,128)S(1)}, u32[]{:S(2)}, u32[]{:S(2)}) collective-permute-start(f32[520,128]{1,0:T(8,128)S(1)} %select_maximum_fusion.rest_0_), channel_id=1, source_target_pairs={{0,16},{8,24},{16,0},{24,8},{1,17},{9,25},{17,1},{25,9},{2,18},{10... | collective-permute-start | bytes 798728 | tf_op jit(solution)/shard_map/ppermute | solution.py:186
  7.3 3.4 %restrict_operator.1 = (f32[4,520,128]{2,1,0:T(8,128)}, f32[8,128]{1,0:T(8,128)}) custom-call(s32[8]{0:T(128)} %count_any.1, s32[8,8]{1,0:T(8,128)} %slot_any.1, s32[2,8]{1,0:T(2,128)} %bitcast.21, s32[4,8]{1,0:T(4,128)} %bitcast.20, f32[8,64,128]{2,1,0:T(8,128)} %restrict_any.1, f32[8,64,512]{2,1,0:T(8,128)} %operator_any.1), custom_call_target="tpu_custom_call" | custom-call | flops 201326592 | bytes 4194304 | tf_op jit(solution)/shard_map/restrict_operator/pallas_call | solution.py:105
  10.7 0.0 copy-start
  10.7 3.8 %all-to-all-start = ((f32[4,520,128]{2,1,0:T(8,128)}), f32[4,520,128]{2,1,0:T(8,128)S(1)}, u32[]{:S(2)}, u32[]{:S(2)}) async-start(f32[4,520,128]{2,1,0:T(8,128)} %get-tuple-element.7), calls=%async_computation | async-start | bytes 2129920 | tf_op jit(solution)/shard_map/all_to_all | solution.py:245
  14.5 3.5 %collective-permute-done.3.blocks_ref = f32[520,128]{1,0:T(8,128)S(1)} collective-permute-done((f32[520,128]{1,0:T(8,128)S(1)}, f32[520,128]{1,0:T(8,128)S(1)}, u32[]{:S(2)}, u32[]{:S(2)}) %collective-permute-start.3) | collective-permute-done | bytes 266272 | tf_op jit(solution)/shard_map/ppermute | solution.py:190
  18.0 1.6 %collective-permute-start.5 = (f32[520,128]{1,0:T(8,128)S(1)}, f32[520,128]{1,0:T(8,128)S(1)}, u32[]{:S(2)}, u32[]{:S(2)}) collective-permute-start(f32[520,128]{1,0:T(8,128)S(1)} %hold_until.1.rest_4_), channel_id=1, source_target_pairs={{0,16},{8,24},{16,0},{24,8},{1,17},{9,25},{17,1},{25,9},{2,18},{10... | collective-permute-start | bytes 798728 | tf_op jit(solution)/shard_map/ppermute | solution.py:186
  19.6 0.5 %collective-permute-start.4 = (f32[520,128]{1,0:T(8,128)S(1)}, f32[520,128]{1,0:T(8,128)S(1)}, u32[]{:S(2)}, u32[]{:S(2)}) collective-permute-start(f32[520,128]{1,0:T(8,128)S(1)} %hold_until.1.rest_4_), channel_id=1, source_target_pairs={{0,8},{8,0},{16,24},{24,16},{1,9},{9,1},{17,25},{25,17},{2,10},{10... | collective-permute-start | bytes 798728 | tf_op jit(solution)/shard_map/ppermute | solution.py:186
  20.1 5.4 %collective-permute-done.5.rest_6_ = f32[520,128]{1,0:T(8,128)S(1)} collective-permute-done((f32[520,128]{1,0:T(8,128)S(1)}, f32[520,128]{1,0:T(8,128)S(1)}, u32[]{:S(2)}, u32[]{:S(2)}) %collective-permute-start.5) | collective-permute-done | bytes 266272 | tf_op jit(solution)/shard_map/ppermute | solution.py:186
  25.5 0.1 pad_add_fusion.own_ref
  25.6 1.4 %collective-permute-done.6.rest_7_ = f32[520,128]{1,0:T(8,128)S(1)} collective-permute-done((f32[520,128]{1,0:T(8,128)S(1)}, f32[520,128]{1,0:T(8,128)S(1)}, u32[]{:S(2)}, u32[]{:S(2)}) %collective-permute-start.6) | collective-permute-done | bytes 266272 | tf_op jit(solution)/shard_map/ppermute | solution.py:186
  27.1 2.2 %all-to-all-done.restricted_ref = f32[4,520,128]{2,1,0:T(8,128)S(1)} async-done(((f32[4,520,128]{2,1,0:T(8,128)}), f32[4,520,128]{2,1,0:T(8,128)S(1)}, u32[]{:S(2)}, u32[]{:S(2)}) %all-to-all-start) | async-done | bytes 1064992 | tf_op jit(solution)/shard_map/all_to_all | solution.py:245
  29.3 2.4 %combine.1 = f32[8,64,128]{2,1,0:T(8,128)S(1)} custom-call(s32[10]{0:T(128)S(1)} %pad_add_fusion.own_ref, f32[4,520,128]{2,1,0:T(8,128)S(1)} %all-to-all-done.restricted_ref, f32[520,128]{1,0:T(8,128)S(1)} %select_maximum_fusion.rest_0_, f32[520,128]{1,0:T(8,128)S(1)} %collective-permute-done.rest_1_, f32[520,128]{1,0:T(8,128)S(1)} %collective-permute-done.1.rest_2_, ...), custom_call_target="tpu_custom_call" | custom-call | flops 268435456 | bytes 4194304 | tf_op jit(solution)/shard_map/combine/pallas_call | solution.py:167
  31.7 0.7 %collective-permute-start.9 = (f32[2,64,128]{2,1,0:T(8,128)S(1)}, f32[2,64,128]{2,1,0:T(8,128)S(1)}, u32[]{:S(2)}, u32[]{:S(2)}) collective-permute-start(f32[2,64,128]{2,1,0:T(8,128)S(1)} %get-tuple-element.10), channel_id=1, source_target_pairs={{0,3},{1,2},{2,1},{3,0},{4,7},{5,6},{6,5},{7,4},{8,11},{9,10},{10,... | collective-permute-start | bytes 196616 | tf_op jit(solution)/shard_map/ppermute | solution.py:212
  32.4 2.4 %collective-permute-start.8 = (f32[2,64,128]{2,1,0:T(8,128)S(1)}, f32[2,64,128]{2,1,0:T(8,128)S(1)}, u32[]{:S(2)}, u32[]{:S(2)}) collective-permute-start(f32[2,64,128]{2,1,0:T(8,128)S(1)} %get-tuple-element.11), channel_id=1, source_target_pairs={{0,2},{1,3},{2,0},{3,1},{4,6},{5,7},{6,4},{7,5},{8,10},{9,11},{10,... | collective-permute-start | bytes 196616 | tf_op jit(solution)/shard_map/ppermute | solution.py:212
  34.8 0.5 %collective-permute-start.7 = (f32[2,64,128]{2,1,0:T(8,128)S(1)}, f32[2,64,128]{2,1,0:T(8,128)S(1)}, u32[]{:S(2)}, u32[]{:S(2)}) collective-permute-start(f32[2,64,128]{2,1,0:T(8,128)S(1)} %get-tuple-element.9), channel_id=1, source_target_pairs={{0,1},{1,0},{2,3},{3,2},{4,5},{5,4},{6,7},{7,6},{8,9},{9,8},{10,11... | collective-permute-start | bytes 196616 | tf_op jit(solution)/shard_map/ppermute | solution.py:212
  35.3 1.8 %collective-permute-done.9 = f32[2,64,128]{2,1,0:T(8,128)S(1)} collective-permute-done((f32[2,64,128]{2,1,0:T(8,128)S(1)}, f32[2,64,128]{2,1,0:T(8,128)S(1)}, u32[]{:S(2)}, u32[]{:S(2)}) %collective-permute-start.9) | collective-permute-done | bytes 65568 | tf_op jit(solution)/shard_map/ppermute | solution.py:212
  37.1 0.9 %collective-permute-done.8 = f32[2,64,128]{2,1,0:T(8,128)S(1)} collective-permute-done((f32[2,64,128]{2,1,0:T(8,128)S(1)}, f32[2,64,128]{2,1,0:T(8,128)S(1)}, u32[]{:S(2)}, u32[]{:S(2)}) %collective-permute-start.8) | collective-permute-done | bytes 65568 | tf_op jit(solution)/shard_map/ppermute | solution.py:212
  37.9 1.1 %collective-permute-done.7 = f32[2,64,128]{2,1,0:T(8,128)S(1)} collective-permute-done((f32[2,64,128]{2,1,0:T(8,128)S(1)}, f32[2,64,128]{2,1,0:T(8,128)S(1)}, u32[]{:S(2)}, u32[]{:S(2)}) %collective-permute-start.7) | collective-permute-done | bytes 65568 | tf_op jit(solution)/shard_map/ppermute | solution.py:212
  39.1 2.1 %collective-permute-start.10 = (f32[64,128]{1,0:T(8,128)S(1)}, f32[64,128]{1,0:T(8,128)S(1)}, u32[]{:S(2)}, u32[]{:S(2)}) collective-permute-start(f32[64,128]{1,0:T(8,128)S(1)} %slice_bitcast_fusion), channel_id=1, source_target_pairs={{0,4},{4,0},{1,5},{5,1},{2,6},{6,2},{3,7},{7,3},{8,12},{12,8},{9,1... | collective-permute-start | bytes 98312 | tf_op jit(solution)/shard_map/ppermute | solution.py:190
  41.2 2.8 %collective-permute-done.10 = f32[64,128]{1,0:T(8,128)S(1)} collective-permute-done((f32[64,128]{1,0:T(8,128)S(1)}, f32[64,128]{1,0:T(8,128)S(1)}, u32[]{:S(2)}, u32[]{:S(2)}) %collective-permute-start.10) | collective-permute-done | bytes 32800 | tf_op jit(solution)/shard_map/ppermute | solution.py:190
  44.0 0.6 %fusion.3 = f32[128,64]{0,1:T(8,128)} fusion(f32[64,128]{1,0:T(8,128)S(1)} %collective-permute-done.10, f32[2,64,128]{2,1,0:T(8,128)S(1)} %fusion.1), kind=kLoop, calls=%fused_computation.8 | loop fusion | flops 8192 | bytes 98304 | tf_op jit(solution)/shard_map/transpose | solution.py:249
  (13 shorter events, 0.1 us)
Async XLA Ops:
  1.7 16.3 %collective-permute-start.3 = (f32[520,128]{1,0:T(8,128)S(1)}, f32[520,128]{1,0:T(8,128)S(1)}, u32[]{:S(2)}, u32[]{:S(2)}) collective-permute-start(f32[520,128]{1,0:T(8,128)S(1)} %select_maximum_fusion.rest_0_), channel_id=1, source_target_pairs={{0,4},{4,0},{1,5},{5,1},{2,6},{6,2},{3,7},{7,3},{8,12},{12,8},{9,1... | collective-permute-start | bytes 798728 | tf_op jit(solution)/shard_map/ppermute | solution.py:190
  5.8 14.4 %collective-permute-start.1 = (f32[520,128]{1,0:T(8,128)S(1)}, f32[520,128]{1,0:T(8,128)S(1)}, u32[]{:S(2)}, u32[]{:S(2)}) collective-permute-start(f32[520,128]{1,0:T(8,128)S(1)} %select_maximum_fusion.rest_0_), channel_id=1, source_target_pairs={{0,16},{8,24},{16,0},{24,8},{1,17},{9,25},{17,1},{25,9},{2,18},{10... | collective-permute-start | bytes 798728 | tf_op jit(solution)/shard_map/ppermute | solution.py:186
  10.7 7.3 %copy-start = (f32[8,128]{1,0:T(8,128)S(1)}, f32[8,128]{1,0:T(8,128)}, u32[]{:S(2)}) copy-start(f32[8,128]{1,0:T(8,128)} %get-tuple-element.8.mark_ref) | copy-start | bytes 12292
  10.7 18.6 %all-to-all-start = ((f32[4,520,128]{2,1,0:T(8,128)}), f32[4,520,128]{2,1,0:T(8,128)S(1)}, u32[]{:S(2)}, u32[]{:S(2)}) async-start(f32[4,520,128]{2,1,0:T(8,128)} %get-tuple-element.7), calls=%async_computation | async-start | bytes 2129920 | tf_op jit(solution)/shard_map/all_to_all | solution.py:245
  18.0 7.5 %collective-permute-start.5 = (f32[520,128]{1,0:T(8,128)S(1)}, f32[520,128]{1,0:T(8,128)S(1)}, u32[]{:S(2)}, u32[]{:S(2)}) collective-permute-start(f32[520,128]{1,0:T(8,128)S(1)} %hold_until.1.rest_4_), channel_id=1, source_target_pairs={{0,16},{8,24},{16,0},{24,8},{1,17},{9,25},{17,1},{25,9},{2,18},{10... | collective-permute-start | bytes 798728 | tf_op jit(solution)/shard_map/ppermute | solution.py:186
  19.6 6.0 %collective-permute-start = (f32[520,128]{1,0:T(8,128)S(1)}, f32[520,128]{1,0:T(8,128)S(1)}, u32[]{:S(2)}, u32[]{:S(2)}) collective-permute-start(f32[520,128]{1,0:T(8,128)S(1)} %select_maximum_fusion.rest_0_), channel_id=1, source_target_pairs={{0,8},{8,0},{16,24},{24,16},{1,9},{9,1},{17,25},{25,17},{2,10},{10... | collective-permute-start | bytes 798728 | tf_op jit(solution)/shard_map/ppermute | solution.py:186
  19.6 6.0 %collective-permute-start.4 = (f32[520,128]{1,0:T(8,128)S(1)}, f32[520,128]{1,0:T(8,128)S(1)}, u32[]{:S(2)}, u32[]{:S(2)}) collective-permute-start(f32[520,128]{1,0:T(8,128)S(1)} %hold_until.1.rest_4_), channel_id=1, source_target_pairs={{0,8},{8,0},{16,24},{24,16},{1,9},{9,1},{17,25},{25,17},{2,10},{10... | collective-permute-start | bytes 798728 | tf_op jit(solution)/shard_map/ppermute | solution.py:186
  20.1 5.5 %collective-permute-start.2 = (f32[520,128]{1,0:T(8,128)S(1)}, f32[520,128]{1,0:T(8,128)S(1)}, u32[]{:S(2)}, u32[]{:S(2)}) collective-permute-start(f32[520,128]{1,0:T(8,128)S(1)} %collective-permute-done.1.rest_2_), channel_id=1, source_target_pairs={{0,8},{8,0},{16,24},{24,16},{1,9},{9,1},{17,25},{25,17},{2,10},{10... | collective-permute-start | bytes 798728 | tf_op jit(solution)/shard_map/ppermute | solution.py:186
  25.5 1.5 %collective-permute-start.6 = (f32[520,128]{1,0:T(8,128)S(1)}, f32[520,128]{1,0:T(8,128)S(1)}, u32[]{:S(2)}, u32[]{:S(2)}) collective-permute-start(f32[520,128]{1,0:T(8,128)S(1)} %collective-permute-done.5.rest_6_), channel_id=1, source_target_pairs={{0,8},{8,0},{16,24},{24,16},{1,9},{9,1},{17,25},{25,17},{2,10},{10... | collective-permute-start | bytes 798728 | tf_op jit(solution)/shard_map/ppermute | solution.py:186
  31.7 5.4 %collective-permute-start.9 = (f32[2,64,128]{2,1,0:T(8,128)S(1)}, f32[2,64,128]{2,1,0:T(8,128)S(1)}, u32[]{:S(2)}, u32[]{:S(2)}) collective-permute-start(f32[2,64,128]{2,1,0:T(8,128)S(1)} %get-tuple-element.10), channel_id=1, source_target_pairs={{0,3},{1,2},{2,1},{3,0},{4,7},{5,6},{6,5},{7,4},{8,11},{9,10},{10,... | collective-permute-start | bytes 196616 | tf_op jit(solution)/shard_map/ppermute | solution.py:212
  32.4 5.5 %collective-permute-start.8 = (f32[2,64,128]{2,1,0:T(8,128)S(1)}, f32[2,64,128]{2,1,0:T(8,128)S(1)}, u32[]{:S(2)}, u32[]{:S(2)}) collective-permute-start(f32[2,64,128]{2,1,0:T(8,128)S(1)} %get-tuple-element.11), channel_id=1, source_target_pairs={{0,2},{1,3},{2,0},{3,1},{4,6},{5,7},{6,4},{7,5},{8,10},{9,11},{10,... | collective-permute-start | bytes 196616 | tf_op jit(solution)/shard_map/ppermute | solution.py:212
  34.8 4.3 %collective-permute-start.7 = (f32[2,64,128]{2,1,0:T(8,128)S(1)}, f32[2,64,128]{2,1,0:T(8,128)S(1)}, u32[]{:S(2)}, u32[]{:S(2)}) collective-permute-start(f32[2,64,128]{2,1,0:T(8,128)S(1)} %get-tuple-element.9), channel_id=1, source_target_pairs={{0,1},{1,0},{2,3},{3,2},{4,5},{5,4},{6,7},{7,6},{8,9},{9,8},{10,11... | collective-permute-start | bytes 196616 | tf_op jit(solution)/shard_map/ppermute | solution.py:212
  39.1 4.9 %collective-permute-start.10 = (f32[64,128]{1,0:T(8,128)S(1)}, f32[64,128]{1,0:T(8,128)S(1)}, u32[]{:S(2)}, u32[]{:S(2)}) collective-permute-start(f32[64,128]{1,0:T(8,128)S(1)} %slice_bitcast_fusion), channel_id=1, source_target_pairs={{0,4},{4,0},{1,5},{5,1},{2,6},{6,2},{3,7},{7,3},{8,12},{12,8},{9,1... | collective-permute-start | bytes 98312 | tf_op jit(solution)/shard_map/ppermute | solution.py:190

commit v13 on v12

--- a/solution.py
+++ b/solution.py
@@ -43,8 +43,8 @@
 
 
 def restrict_kernel(
-    count_any, slot_any, rows_any, fetch_any, restrict_any, operator_any, out_ref, mark_ref,
-    count_ref, slot_ref, rows_ref, fetch_ref, restrict_ref, operator_ref, sems, operator_sems,
+    count_any, slot_any, rows_any, fetch_any, restrict_ref, operator_ref, out_ref, mark_ref,
+    count_ref, slot_ref, rows_ref, fetch_ref, sems,
 ):
     fine_rows, block_size, _ = operator_ref.shape
     entries = slot_ref.shape[1]
@@ -53,15 +53,9 @@
     used = 2 * slot_count * block_size
     wide = NCR * block_size
 
-    pairs = [
-        (count_any, count_ref), (slot_any, slot_ref), (rows_any, rows_ref),
-        (fetch_any, fetch_ref), (restrict_any, restrict_ref),
-    ]
+    pairs = [(count_any, count_ref), (slot_any, slot_ref), (rows_any, rows_ref), (fetch_any, fetch_ref)]
     copies = [pltpu.make_async_copy(a, b, sems.at[i]) for i, (a, b) in enumerate(pairs)]
-    operators = [
-        pltpu.make_async_copy(operator_any.at[i], operator_ref.at[i], operator_sems.at[i]) for i in range(fine_rows)
-    ]
-    for copy in copies + operators:
+    for copy in copies:
         copy.start()
 
     lane = lax.broadcasted_iota(jnp.int32, (block_size, wide), 1)
@@ -69,7 +63,7 @@
     short_lane = lax.broadcasted_iota(jnp.int32, (EXTRA, wide), 1)
     for near in range(half):
         out_ref[near, :used] = jnp.zeros((used, wide), jnp.float32)
-    for copy in copies + operators:
+    for copy in copies:
         copy.wait()
 
     for near in range(half):
@@ -108,11 +102,10 @@
             jax.ShapeDtypeStruct((columns // 2, rows, wide), jnp.float32),
             jax.ShapeDtypeStruct((EXTRA, wide), jnp.float32),
         ),
-        in_specs=[pl.BlockSpec(memory_space=pltpu.HBM)] * 6,
+        in_specs=[pl.BlockSpec(memory_space=pltpu.HBM)] * 4 + [pl.BlockSpec(memory_space=pltpu.VMEM)] * 2,
         out_specs=[pl.BlockSpec(memory_space=pltpu.VMEM)] * 2,
-        scratch_shapes=[pltpu.SMEM(x.shape, x.dtype) for x in small]
-        + [pltpu.VMEM(x.shape, x.dtype) for x in (restrict_blocks, operator_blocks)]
-        + [pltpu.SemaphoreType.DMA((5,)), pltpu.SemaphoreType.DMA((fine_rows,))],
+        scratch_shapes=[pltpu.SMEM(x.shape, x.dtype) for x in small] + [pltpu.SemaphoreType.DMA((4,))],
+        compiler_params=pltpu.CompilerParams(vmem_limit_bytes=VMEM_LIMIT),
         cost_estimate=pl.CostEstimate(
             flops=6 * fine_rows * block_size * width * wide, bytes_accessed=4 << 20, transcendentals=0
         ),

time: 44.8 us -> 47.7 us (1.065)
  local copies, waits for them, and re-layouts: 0.03 us -> 4.89 us
  starting transfers between devices: 17.2 us -> 14.8 us
  waiting for transfers between devices: 19.1 us -> 20.2 us
  Pallas kernels: 5.78 us -> 5 us
    unnamed x2 -> x12, local copies, waits for them, and re-layouts: 0.01 us -> 4.87 us
    all_to_all x1, waiting for transfers between devices: 2.24 us -> 4.29 us  [local(): lax.all_to_all(restricted, 'near', split_axis=0, concat_axis=0, tiled=True)]
    ppermute x2, starting transfers between devices: 6.19 us -> 4.52 us  [half_swap(): return lax.ppermute(x, 'half', [(0, 1), (1, 0)])]
    ppermute x2, waiting for transfers between devices: 6.26 us -> 4.81 us  [half_swap(): return lax.ppermute(x, 'half', [(0, 1), (1, 0)])]
    pallas_call x1, Pallas kernels: 3.4 us -> 2.62 us  [restrict_operator(): pl.pallas_call(restrict_kernel, out_shape=(jax.ShapeDtypeStruct((columns...]
    ppermute x6, starting transfers between devices: 3.67 us -> 2.95 us  [row_swap(): lax.ppermute(x, 'row', [(r, r ^ bit) for r in range(lax.axis_size('row'))])]
    ppermute x6, waiting for transfers between devices: 6.83 us -> 7.41 us  [row_swap(): lax.ppermute(x, 'row', [(r, r ^ bit) for r in range(lax.axis_size('row'))])]
  transfers between devices with their start and end apart: 12 -> 12, of which waited for: 8 -> 7; matrix products, arithmetic and copies ran while one was open for 0% -> 0% of each run, Pallas kernels for 8% -> 6%
where the time goes in v13:
time: 47.7 us; the launch traced here: 47.4 us
  waiting for transfers between devices  20.2 us (42%)
  starting transfers between devices  14.8 us (31%)
  Pallas kernels  5 us (10%)
  local copies, waits for them, and re-layouts  4.89 us (10%)
  other arithmetic  2.38 us (5%)
    ppermute x6, waiting for transfers between devices, row_swap(): lax.ppermute(x, 'row', [(r, r ^ bit) for r in range(lax.axis_size('row'))])  7.41 us
    unnamed x12, local copies, waits for them, and re-layouts  4.87 us
    ppermute x2, waiting for transfers between devices, half_swap(): return lax.ppermute(x, 'half', [(0, 1), (1, 0)])  4.81 us
    ppermute x2, starting transfers between devices, half_swap(): return lax.ppermute(x, 'half', [(0, 1), (1, 0)])  4.52 us
    all_to_all x1, waiting for transfers between devices, local(): lax.all_to_all(restricted, 'near', split_axis=0, concat_axis=0, tiled=True)  4.29 us
    all_to_all x1, starting transfers between devices, local(): lax.all_to_all(restricted, 'near', split_axis=0, concat_axis=0, tiled=True)  3.79 us
    ppermute x3, waiting for transfers between devices, add_over_columns(): lax.ppermute(sums[2 * near:2 * near + 2], 'near', [(n, n ^ near) for n in...  3.7 us
    ppermute x3, starting transfers between devices, add_over_columns(): lax.ppermute(sums[2 * near:2 * near + 2], 'near', [(n, n ^ near) for n in...  3.55 us
  transfers between devices with their start and end apart: 12, of which 7 were waited for; matrix products, arithmetic and copies ran while one was open for 0% of the time, Pallas kernels for 6%

profile of v13, /device:TPU:0, one launch (start us, length us, event | category | flops | bytes accessed | tf_op | source)
XLA Modules:
  0.0 47.4 jit_solution(10247364815499708760)
XLA Ops:
  0.0 0.7 %convert_bitcast_fusion = f32[2,8]{1,0:T(2,128)S(1)} fusion(s32[8,2]{0,1:T(2,128)} %param.13), kind=kLoop, calls=%fused_computation.14 | loop fusion | flops 16 | bytes 128 | tf_op jit(solution)/shard_map/convert_element_type | solution.py:212
  0.7 1.0 %select_maximum_fusion.rest_0_ = f32[520,128]{1,0:T(8,128)S(1)} fusion(f32[2,8]{1,0:T(2,128)S(1)} %convert_bitcast_fusion, f32[512,128]{1,0:T(8,128)} %bitcast.21), kind=kLoop, calls=%fused_computation | loop fusion | flops 199680 | bytes 528448 | tf_op jit(solution)/shard_map/concatenate | solution.py:213
  1.7 4.1 %collective-permute-start.3 = (f32[520,128]{1,0:T(8,128)S(1)}, f32[520,128]{1,0:T(8,128)S(1)}, u32[]{:S(2)}, u32[]{:S(2)}) collective-permute-start(f32[520,128]{1,0:T(8,128)S(1)} %select_maximum_fusion.rest_0_), channel_id=1, source_target_pairs={{0,4},{4,0},{1,5},{5,1},{2,6},{6,2},{3,7},{7,3},{8,12},{12,8},{9,1... | collective-permute-start | bytes 798728 | tf_op jit(solution)/shard_map/ppermute | solution.py:183
  5.8 1.5 %collective-permute-start.1 = (f32[520,128]{1,0:T(8,128)S(1)}, f32[520,128]{1,0:T(8,128)S(1)}, u32[]{:S(2)}, u32[]{:S(2)}) collective-permute-start(f32[520,128]{1,0:T(8,128)S(1)} %select_maximum_fusion.rest_0_), channel_id=1, source_target_pairs={{0,16},{8,24},{16,0},{24,8},{1,17},{9,25},{17,1},{25,9},{2,18},{10... | collective-permute-start | bytes 798728 | tf_op jit(solution)/shard_map/ppermute | solution.py:179
  7.3 1.2 %copy-done = f32[8,64,512]{2,1,0:T(8,128)S(1)} copy-done((f32[8,64,512]{2,1,0:T(8,128)S(1)}, f32[8,64,512]{2,1,0:T(8,128)}, u32[]{:S(2)}) %copy-start) | copy-done | bytes 1048600
  8.5 0.9 %copy-done.1 = f32[8,64,128]{2,1,0:T(8,128)S(1)} copy-done((f32[8,64,128]{2,1,0:T(8,128)S(1)}, f32[8,64,128]{2,1,0:T(8,128)}, u32[]{:S(2)}) %copy-start.1) | copy-done | bytes 262168
  9.5 0.7 %copy-done.2 = s32[8,8]{1,0:T(8,128)S(1)} copy-done((s32[8,8]{1,0:T(8,128)S(1)}, s32[8,8]{1,0:T(8,128)}, u32[]{:S(2)}) %copy-start.2) | copy-done | bytes 280
  10.1 0.7 %copy-done.3 = s32[1,1,8,4]{2,3,1,0:T(4,128)S(1)} copy-done((s32[1,1,8,4]{2,3,1,0:T(4,128)S(1)}, s32[1,1,8,4]{2,3,1,0:T(4,128)}, u32[]{:S(2)}) %copy-start.3) | copy-done | bytes 152
  10.8 0.7 %copy-done.4 = s32[8,2]{0,1:T(2,128)S(1)} copy-done((s32[8,2]{0,1:T(2,128)S(1)}, s32[8,2]{0,1:T(2,128)}, u32[]{:S(2)}) %copy-start.4) | copy-done | bytes 88
  11.5 0.7 %copy-done.5 = s32[8]{0:T(128)S(1)} copy-done((s32[8]{0:T(128)S(1)}, s32[8]{0:T(128)}, u32[]{:S(2)}) %copy-start.5) | copy-done | bytes 56
  12.2 2.6 %restrict_operator.1 = (f32[4,520,128]{2,1,0:T(8,128)}, f32[8,128]{1,0:T(8,128)S(1)}) custom-call(s32[8]{0:T(128)S(1)} %copy-done.5, s32[8,8]{1,0:T(8,128)S(1)} %copy-done.2, s32[2,8]{1,0:T(2,128)S(1)} %bitcast.20, s32[4,8]{1,0:T(4,128)S(1)} %bitcast.19, f32[8,64,128]{2,1,0:T(8,128)S(1)} %copy-done.1, f32[8,64,512]{2,1,0:T(8,128)S(1)} %copy-done), custom_call_target="tpu_custom_call" | custom-call | flops 201326592 | bytes 4194304 | tf_op jit(solution)/shard_map/restrict_operator/pallas_call | solution.py:99
  14.8 3.8 %all-to-all-start = ((f32[4,520,128]{2,1,0:T(8,128)}), f32[4,520,128]{2,1,0:T(8,128)S(1)}, u32[]{:S(2)}, u32[]{:S(2)}) async-start(f32[4,520,128]{2,1,0:T(8,128)} %get-tuple-element.7), calls=%async_computation | async-start | bytes 2129920 | tf_op jit(solution)/shard_map/all_to_all | solution.py:238
  18.6 0.9 %collective-permute-start.5 = (f32[520,128]{1,0:T(8,128)S(1)}, f32[520,128]{1,0:T(8,128)S(1)}, u32[]{:S(2)}, u32[]{:S(2)}) collective-permute-start(f32[520,128]{1,0:T(8,128)S(1)} %hold_until.1.rest_4_), channel_id=1, source_target_pairs={{0,16},{8,24},{16,0},{24,8},{1,17},{9,25},{17,1},{25,9},{2,18},{10... | collective-permute-start | bytes 798728 | tf_op jit(solution)/shard_map/ppermute | solution.py:179
  20.0 6.0 %collective-permute-done.5.rest_6_ = f32[520,128]{1,0:T(8,128)S(1)} collective-permute-done((f32[520,128]{1,0:T(8,128)S(1)}, f32[520,128]{1,0:T(8,128)S(1)}, u32[]{:S(2)}, u32[]{:S(2)}) %collective-permute-start.5) | collective-permute-done | bytes 266272 | tf_op jit(solution)/shard_map/ppermute | solution.py:179
  26.1 1.4 %collective-permute-done.6.rest_7_ = f32[520,128]{1,0:T(8,128)S(1)} collective-permute-done((f32[520,128]{1,0:T(8,128)S(1)}, f32[520,128]{1,0:T(8,128)S(1)}, u32[]{:S(2)}, u32[]{:S(2)}) %collective-permute-start.6) | collective-permute-done | bytes 266272 | tf_op jit(solution)/shard_map/ppermute | solution.py:179
  27.5 4.3 %all-to-all-done.restricted_ref = f32[4,520,128]{2,1,0:T(8,128)S(1)} async-done(((f32[4,520,128]{2,1,0:T(8,128)}), f32[4,520,128]{2,1,0:T(8,128)S(1)}, u32[]{:S(2)}, u32[]{:S(2)}) %all-to-all-start) | async-done | bytes 1064992 | tf_op jit(solution)/shard_map/all_to_all | solution.py:238
  31.8 2.4 %combine.1 = f32[8,64,128]{2,1,0:T(8,128)S(1)} custom-call(s32[10]{0:T(128)S(1)} %pad_add_fusion.own_ref, f32[4,520,128]{2,1,0:T(8,128)S(1)} %all-to-all-done.restricted_ref, f32[520,128]{1,0:T(8,128)S(1)} %select_maximum_fusion.rest_0_, f32[520,128]{1,0:T(8,128)S(1)} %collective-permute-done.rest_1_, f32[520,128]{1,0:T(8,128)S(1)} %collective-permute-done.1.rest_2_, ...), custom_call_target="tpu_custom_call" | custom-call | flops 268435456 | bytes 4194304 | tf_op jit(solution)/shard_map/combine/pallas_call | solution.py:160
  34.2 1.5 %collective-permute-start.9 = (f32[2,64,128]{2,1,0:T(8,128)S(1)}, f32[2,64,128]{2,1,0:T(8,128)S(1)}, u32[]{:S(2)}, u32[]{:S(2)}) collective-permute-start(f32[2,64,128]{2,1,0:T(8,128)S(1)} %get-tuple-element.10), channel_id=1, source_target_pairs={{0,3},{1,2},{2,1},{3,0},{4,7},{5,6},{6,5},{7,4},{8,11},{9,10},{10,... | collective-permute-start | bytes 196616 | tf_op jit(solution)/shard_map/ppermute | solution.py:205
  35.7 1.5 %collective-permute-start.8 = (f32[2,64,128]{2,1,0:T(8,128)S(1)}, f32[2,64,128]{2,1,0:T(8,128)S(1)}, u32[]{:S(2)}, u32[]{:S(2)}) collective-permute-start(f32[2,64,128]{2,1,0:T(8,128)S(1)} %get-tuple-element.11), channel_id=1, source_target_pairs={{0,2},{1,3},{2,0},{3,1},{4,6},{5,7},{6,4},{7,5},{8,10},{9,11},{10,... | collective-permute-start | bytes 196616 | tf_op jit(solution)/shard_map/ppermute | solution.py:205
  37.2 0.6 %collective-permute-start.7 = (f32[2,64,128]{2,1,0:T(8,128)S(1)}, f32[2,64,128]{2,1,0:T(8,128)S(1)}, u32[]{:S(2)}, u32[]{:S(2)}) collective-permute-start(f32[2,64,128]{2,1,0:T(8,128)S(1)} %get-tuple-element.9), channel_id=1, source_target_pairs={{0,1},{1,0},{2,3},{3,2},{4,5},{5,4},{6,7},{7,6},{8,9},{9,8},{10,11... | collective-permute-start | bytes 196616 | tf_op jit(solution)/shard_map/ppermute | solution.py:205
  37.8 2.2 %collective-permute-done.9 = f32[2,64,128]{2,1,0:T(8,128)S(1)} collective-permute-done((f32[2,64,128]{2,1,0:T(8,128)S(1)}, f32[2,64,128]{2,1,0:T(8,128)S(1)}, u32[]{:S(2)}, u32[]{:S(2)}) %collective-permute-start.9) | collective-permute-done | bytes 65568 | tf_op jit(solution)/shard_map/ppermute | solution.py:205
  40.2 1.3 %collective-permute-done.7 = f32[2,64,128]{2,1,0:T(8,128)S(1)} collective-permute-done((f32[2,64,128]{2,1,0:T(8,128)S(1)}, f32[2,64,128]{2,1,0:T(8,128)S(1)}, u32[]{:S(2)}, u32[]{:S(2)}) %collective-permute-start.7) | collective-permute-done | bytes 65568 | tf_op jit(solution)/shard_map/ppermute | solution.py:205
  41.9 4.8 %collective-permute-done.10 = f32[64,128]{1,0:T(8,128)S(1)} collective-permute-done((f32[64,128]{1,0:T(8,128)S(1)}, f32[64,128]{1,0:T(8,128)S(1)}, u32[]{:S(2)}, u32[]{:S(2)}) %collective-permute-start.10) | collective-permute-done | bytes 32800 | tf_op jit(solution)/shard_map/ppermute | solution.py:183
  46.7 0.6 %fusion.3 = f32[128,64]{0,1:T(8,128)} fusion(f32[64,128]{1,0:T(8,128)S(1)} %collective-permute-done.10, f32[2,64,128]{2,1,0:T(8,128)S(1)} %fusion.1), kind=kLoop, calls=%fused_computation.8 | loop fusion | flops 8192 | bytes 98304 | tf_op jit(solution)/shard_map/transpose | solution.py:242
  (23 shorter events, 1.3 us)
Async XLA Ops:
  1.7 16.9 %collective-permute-start.3 = (f32[520,128]{1,0:T(8,128)S(1)}, f32[520,128]{1,0:T(8,128)S(1)}, u32[]{:S(2)}, u32[]{:S(2)}) collective-permute-start(f32[520,128]{1,0:T(8,128)S(1)} %select_maximum_fusion.rest_0_), channel_id=1, source_target_pairs={{0,4},{4,0},{1,5},{5,1},{2,6},{6,2},{3,7},{7,3},{8,12},{12,8},{9,1... | collective-permute-start | bytes 798728 | tf_op jit(solution)/shard_map/ppermute | solution.py:183
  5.8 14.3 %collective-permute-start.1 = (f32[520,128]{1,0:T(8,128)S(1)}, f32[520,128]{1,0:T(8,128)S(1)}, u32[]{:S(2)}, u32[]{:S(2)}) collective-permute-start(f32[520,128]{1,0:T(8,128)S(1)} %select_maximum_fusion.rest_0_), channel_id=1, source_target_pairs={{0,16},{8,24},{16,0},{24,8},{1,17},{9,25},{17,1},{25,9},{2,18},{10... | collective-permute-start | bytes 798728 | tf_op jit(solution)/shard_map/ppermute | solution.py:179
  7.3 1.2 %copy-start = (f32[8,64,512]{2,1,0:T(8,128)S(1)}, f32[8,64,512]{2,1,0:T(8,128)}, u32[]{:S(2)}) copy-start(f32[8,64,512]{2,1,0:T(8,128)} %operator_ref.1) | copy-start | bytes 3145732
  8.5 0.9 %copy-start.1 = (f32[8,64,128]{2,1,0:T(8,128)S(1)}, f32[8,64,128]{2,1,0:T(8,128)}, u32[]{:S(2)}) copy-start(f32[8,64,128]{2,1,0:T(8,128)} %restrict_ref.1) | copy-start | bytes 786436
  9.4 0.7 %copy-start.2 = (s32[8,8]{1,0:T(8,128)S(1)}, s32[8,8]{1,0:T(8,128)}, u32[]{:S(2)}) copy-start(s32[8,8]{1,0:T(8,128)} %slot_any.1) | copy-start | bytes 772
  10.1 0.7 %copy-start.3 = (s32[1,1,8,4]{2,3,1,0:T(4,128)S(1)}, s32[1,1,8,4]{2,3,1,0:T(4,128)}, u32[]{:S(2)}) copy-start(s32[1,1,8,4]{2,3,1,0:T(4,128)} %param.11) | copy-start | bytes 388
  10.8 0.7 %copy-start.4 = (s32[8,2]{0,1:T(2,128)S(1)}, s32[8,2]{0,1:T(2,128)}, u32[]{:S(2)}) copy-start(s32[8,2]{0,1:T(2,128)} %param.15) | copy-start | bytes 196
  11.5 0.7 %copy-start.5 = (s32[8]{0:T(128)S(1)}, s32[8]{0:T(128)}, u32[]{:S(2)}) copy-start(s32[8]{0:T(128)} %count_any.1) | copy-start | bytes 100
  14.8 17.0 %all-to-all-start = ((f32[4,520,128]{2,1,0:T(8,128)}), f32[4,520,128]{2,1,0:T(8,128)S(1)}, u32[]{:S(2)}, u32[]{:S(2)}) async-start(f32[4,520,128]{2,1,0:T(8,128)} %get-tuple-element.7), calls=%async_computation | async-start | bytes 2129920 | tf_op jit(solution)/shard_map/all_to_all | solution.py:238
  18.6 7.4 %collective-permute-start.5 = (f32[520,128]{1,0:T(8,128)S(1)}, f32[520,128]{1,0:T(8,128)S(1)}, u32[]{:S(2)}, u32[]{:S(2)}) collective-permute-start(f32[520,128]{1,0:T(8,128)S(1)} %hold_until.1.rest_4_), channel_id=1, source_target_pairs={{0,16},{8,24},{16,0},{24,8},{1,17},{9,25},{17,1},{25,9},{2,18},{10... | collective-permute-start | bytes 798728 | tf_op jit(solution)/shard_map/ppermute | solution.py:179
  19.5 6.6 %collective-permute-start = (f32[520,128]{1,0:T(8,128)S(1)}, f32[520,128]{1,0:T(8,128)S(1)}, u32[]{:S(2)}, u32[]{:S(2)}) collective-permute-start(f32[520,128]{1,0:T(8,128)S(1)} %select_maximum_fusion.rest_0_), channel_id=1, source_target_pairs={{0,8},{8,0},{16,24},{24,16},{1,9},{9,1},{17,25},{25,17},{2,10},{10... | collective-permute-start | bytes 798728 | tf_op jit(solution)/shard_map/ppermute | solution.py:179
  19.5 6.6 %collective-permute-start.4 = (f32[520,128]{1,0:T(8,128)S(1)}, f32[520,128]{1,0:T(8,128)S(1)}, u32[]{:S(2)}, u32[]{:S(2)}) collective-permute-start(f32[520,128]{1,0:T(8,128)S(1)} %hold_until.1.rest_4_), channel_id=1, source_target_pairs={{0,8},{8,0},{16,24},{24,16},{1,9},{9,1},{17,25},{25,17},{2,10},{10... | collective-permute-start | bytes 798728 | tf_op jit(solution)/shard_map/ppermute | solution.py:179
  20.0 6.1 %collective-permute-start.2 = (f32[520,128]{1,0:T(8,128)S(1)}, f32[520,128]{1,0:T(8,128)S(1)}, u32[]{:S(2)}, u32[]{:S(2)}) collective-permute-start(f32[520,128]{1,0:T(8,128)S(1)} %collective-permute-done.1.rest_2_), channel_id=1, source_target_pairs={{0,8},{8,0},{16,24},{24,16},{1,9},{9,1},{17,25},{25,17},{2,10},{10... | collective-permute-start | bytes 798728 | tf_op jit(solution)/shard_map/ppermute | solution.py:179
  26.0 1.5 %collective-permute-start.6 = (f32[520,128]{1,0:T(8,128)S(1)}, f32[520,128]{1,0:T(8,128)S(1)}, u32[]{:S(2)}, u32[]{:S(2)}) collective-permute-start(f32[520,128]{1,0:T(8,128)S(1)} %collective-permute-done.5.rest_6_), channel_id=1, source_target_pairs={{0,8},{8,0},{16,24},{24,16},{1,9},{9,1},{17,25},{25,17},{2,10},{10... | collective-permute-start | bytes 798728 | tf_op jit(solution)/shard_map/ppermute | solution.py:179
  34.2 5.8 %collective-permute-start.9 = (f32[2,64,128]{2,1,0:T(8,128)S(1)}, f32[2,64,128]{2,1,0:T(8,128)S(1)}, u32[]{:S(2)}, u32[]{:S(2)}) collective-permute-start(f32[2,64,128]{2,1,0:T(8,128)S(1)} %get-tuple-element.10), channel_id=1, source_target_pairs={{0,3},{1,2},{2,1},{3,0},{4,7},{5,6},{6,5},{7,4},{8,11},{9,10},{10,... | collective-permute-start | bytes 196616 | tf_op jit(solution)/shard_map/ppermute | solution.py:205
  35.7 4.4 %collective-permute-start.8 = (f32[2,64,128]{2,1,0:T(8,128)S(1)}, f32[2,64,128]{2,1,0:T(8,128)S(1)}, u32[]{:S(2)}, u32[]{:S(2)}) collective-permute-start(f32[2,64,128]{2,1,0:T(8,128)S(1)} %get-tuple-element.11), channel_id=1, source_target_pairs={{0,2},{1,3},{2,0},{3,1},{4,6},{5,7},{6,4},{7,5},{8,10},{9,11},{10,... | collective-permute-start | bytes 196616 | tf_op jit(solution)/shard_map/ppermute | solution.py:205
  37.2 4.3 %collective-permute-start.7 = (f32[2,64,128]{2,1,0:T(8,128)S(1)}, f32[2,64,128]{2,1,0:T(8,128)S(1)}, u32[]{:S(2)}, u32[]{:S(2)}) collective-permute-start(f32[2,64,128]{2,1,0:T(8,128)S(1)} %get-tuple-element.9), channel_id=1, source_target_pairs={{0,1},{1,0},{2,3},{3,2},{4,5},{5,4},{6,7},{7,6},{8,9},{9,8},{10,11... | collective-permute-start | bytes 196616 | tf_op jit(solution)/shard_map/ppermute | solution.py:205
  41.5 5.2 %collective-permute-start.10 = (f32[64,128]{1,0:T(8,128)S(1)}, f32[64,128]{1,0:T(8,128)S(1)}, u32[]{:S(2)}, u32[]{:S(2)}) collective-permute-start(f32[64,128]{1,0:T(8,128)S(1)} %slice_bitcast_fusion), channel_id=1, source_target_pairs={{0,4},{4,0},{1,5},{5,1},{2,6},{6,2},{3,7},{7,3},{8,12},{12,8},{9,1... | collective-permute-start | bytes 98312 | tf_op jit(solution)/shard_map/ppermute | solution.py:183

commit v14 on v10

--- a/solution.py
+++ b/solution.py
@@ -26,7 +26,7 @@
     return lax.dot_general(left, right, (((0,), (0,)), ((), ())), preferred_element_type=jnp.float32)
 
 
-def append_kernel(mark_ref, far_columns_ref, own_columns_ref, blocks_ref, out_ref):
+def append_kernel(mark_ref, next_ref, far_columns_ref, own_columns_ref, blocks_ref, out_ref):
     used = blocks_ref.shape[0]
     entries, fine_rows = own_columns_ref.shape
     out_ref[:used] = blocks_ref[...]
@@ -35,17 +35,17 @@
     out_ref[used + entries : used + 2 * entries, :fine_rows] = own_columns_ref[...].astype(jnp.float32)
 
 
-def append_columns(mark, far_columns, own_columns, blocks):
+def append_columns(mark, next_blocks, far_columns, own_columns, blocks):
     used, width = blocks.shape
     return pl.pallas_call(
         append_kernel,
         out_shape=jax.ShapeDtypeStruct((used + EXTRA, width), blocks.dtype),
-        in_specs=[pl.BlockSpec(memory_space=pltpu.VMEM)] * 4,
+        in_specs=[pl.BlockSpec(memory_space=pltpu.VMEM)] * 5,
         out_specs=pl.BlockSpec(memory_space=pltpu.VMEM),
         compiler_params=pltpu.CompilerParams(vmem_limit_bytes=VMEM_LIMIT),
         cost_estimate=pl.CostEstimate(flops=HOLD_FLOPS, bytes_accessed=HOLD_FLOPS >> 8, transcendentals=0),
         name="append_columns",
-    )(mark, far_columns, own_columns, blocks)
+    )(mark, next_blocks, far_columns, own_columns, blocks)
 
 
 def restrict_kernel(
@@ -127,7 +127,8 @@
 
 
 def combine_kernel(own_ref, restricted_ref, *rest, slot_count, fine_rows, entries):
-    pieces, (out_ref, held_ref, table_ref, index_ref, sem) = rest[:-5], rest[-5:]
+    pieces, (out_ref, held_ref, table_ref, index_ref, sem) = rest[:-9], rest[-9:-4]
+    sums = rest[-4:]
     half = restricted_ref.shape[0]
     rows = len(pieces) // 2
     block_size = out_ref.shape[1]
@@ -146,10 +147,11 @@
     copy.start()
     for i, piece in enumerate(pieces):
         held_ref[i] = piece[...] if i < rows else piece[:held]
-    out_ref[...] = jnp.zeros_like(out_ref)
+    for total in sums:
+        total[...] = jnp.zeros_like(total)
     copy.wait()
 
-    def step(i, carry):
+    def add_product(i, total):
         near = lax.div(i, 2 * slot_count)
         place = lax.rem(i, 2 * slot_count)
         wanted = index_ref[near, place]
@@ -160,11 +162,16 @@
         restricted = restricted_ref[near, pl.ds(pl.multiple_of(place * block_size, block_size), block_size)]
         product = transposed_dot(split3(block, "left"), split3(restricted, "right"))
         for m in range(entries):
-            column = index_ref[half + entries * piece + m, inside]
-            out_ref[column] += product[m * block_size : (m + 1) * block_size]
+            column = own_ref[2 + index_ref[half + entries * piece + m, inside]]
+            total[m % len(total)][column] += product[m * block_size : (m + 1) * block_size]
+
+    def step(i, carry):
+        add_product(2 * i, sums[:2])
+        add_product(2 * i + 1, sums[2:])
         return carry
 
-    lax.fori_loop(0, half * 2 * slot_count, step, 0, unroll=16)
+    lax.fori_loop(0, half * slot_count, step, 0, unroll=8)
+    out_ref[...] = (sums[0][...] + sums[1][...]) + (sums[2][...] + sums[3][...])
 
 
 def combine(own, restricted, pieces, coarse_all, slot_count, fine_rows, block_size):
@@ -183,29 +190,12 @@
             pltpu.VMEM((table_rows, LANES), jnp.int32),
             pltpu.SMEM((table_rows, LANES), jnp.int32),
             pltpu.SemaphoreType.DMA,
-        ],
+        ]
+        + [pltpu.VMEM((coarse_all, block_size, wide), jnp.float32)] * 4,
         compiler_params=pltpu.CompilerParams(vmem_limit_bytes=VMEM_LIMIT),
         cost_estimate=pl.CostEstimate(flops=1 << 28, bytes_accessed=4 << 20, transcendentals=0),
         name="combine",
     )(own, restricted, *pieces)
-
-
-def add_kernel(parts_ref, out_ref):
-    total = parts_ref[0]
-    for i in range(1, parts_ref.shape[0]):
-        total = total + parts_ref[i]
-    out_ref[...] = total
-
-
-def add_up(parts):
-    return pl.pallas_call(
-        add_kernel,
-        out_shape=jax.ShapeDtypeStruct(parts.shape[1:], parts.dtype),
-        in_specs=[pl.BlockSpec(memory_space=pltpu.VMEM)],
-        out_specs=pl.BlockSpec(memory_space=pltpu.VMEM),
-        compiler_params=pltpu.CompilerParams(vmem_limit_bytes=VMEM_LIMIT),
-        name="add_up",
-    )(parts)
 
 
 def row_swap(x, bit):
@@ -224,6 +214,19 @@
             pieces[mask ^ bit] = row_swap(pieces[mask], bit)
         bit //= 2
     return [pieces[mask] for mask in range(rows)]
+
+
+def place_of_columns(half):
+    own = lax.axis_index("half") * half + lax.axis_index("near")
+    ahead = jnp.arange(2 * half, dtype=jnp.int32) ^ own
+    return ahead % half * 2 + ahead // half
+
+
+def add_over_columns(sums, half):
+    total = sums[:2]
+    for near in range(1, half):
+        total = total + lax.ppermute(sums[2 * near : 2 * near + 2], "near", [(n, n ^ near) for n in range(half)])
+    return total[0] + half_swap(total[1])
 
 
 def local(
@@ -241,8 +244,9 @@
     fine_rows, block_size, width = prolong_blocks.shape
     fetch = fetch_lists.reshape(2 * half, slot_count).T
     own = jnp.stack([lax.axis_index("row"), lax.axis_index("half")])
+    own = jnp.concatenate([own, place_of_columns(half)])
+
     own_columns = prolong_cols.T
-
     near_blocks = prolong_blocks.reshape(fine_rows * block_size, width)
     far_blocks = half_swap(near_blocks)
     far_columns = half_swap(own_columns)
@@ -250,11 +254,11 @@
         operator_count, operator_slot, restrict_rows.T, fetch, operator_blocks, restrict_blocks
     )
     restricted = lax.all_to_all(restricted, "near", split_axis=0, concat_axis=0, tiled=True)
-    far_blocks = append_columns(mark, far_columns, own_columns, far_blocks)
-    pieces = spread_over_rows(near_blocks, rows) + spread_over_rows(far_blocks, rows)
+    near_pieces = spread_over_rows(near_blocks, rows)
+    far_blocks = append_columns(mark, near_pieces[rows // 2], far_columns, own_columns, far_blocks)
+    pieces = near_pieces + spread_over_rows(far_blocks, rows)
     sums = combine(own, restricted, pieces, NCR * rows, slot_count, fine_rows, block_size)
-    parts = lax.all_to_all(sums, ("half", "near"), split_axis=0, concat_axis=0, tiled=True)
-    return add_up(parts).T
+    return add_over_columns(sums, half).T
 
 
 def solution(mesh):

time: 49.9 us -> 44.4 us (0.89)
  blocking collectives: 15.5 us -> 0 us
  starting transfers between devices: 11.2 us -> 16.4 us
  waiting for transfers between devices: 16.4 us -> 21.2 us
  other arithmetic: 0.07 us -> 0.73 us
  Pallas kernels: 6.41 us -> 5.81 us
    all_to_all x1 -> x0, blocking collectives: 15.5 us -> none  [local(): lax.all_to_all(sums, ('half', 'near'), split_axis=0, concat_axis=0, tiled...]
    ppermute x0 -> x3, waiting for transfers between devices: none -> 3.73 us  [add_over_columns(): lax.ppermute(sums[2 * near:2 * near + 2], 'near', [(n, n ^ near) for n in...]
    ppermute x0 -> x3, starting transfers between devices: none -> 3.55 us  [add_over_columns(): lax.ppermute(sums[2 * near:2 * near + 2], 'near', [(n, n ^ near) for n in...]
    ppermute x6, waiting for transfers between devices: 11.6 us -> 8.35 us  [row_swap(): lax.ppermute(x, 'row', [(r, r ^ bit) for r in range(lax.axis_size('row'))])]
    ppermute x2 -> x3, waiting for transfers between devices: 4.75 us -> 7.35 us  [half_swap(): return lax.ppermute(x, 'half', [(0, 1), (1, 0)])]
    all_to_all x1, waiting for transfers between devices: 0.01 us -> 1.76 us  [local(): lax.all_to_all(restricted, 'near', split_axis=0, concat_axis=0, tiled=True)]
    ppermute x6, starting transfers between devices: 3 us -> 4.02 us  [row_swap(): lax.ppermute(x, 'row', [(r, r ^ bit) for r in range(lax.axis_size('row'))])]
    ppermute x2 -> x3, starting transfers between devices: 4.07 us -> 5 us  [half_swap(): return lax.ppermute(x, 'half', [(0, 1), (1, 0)])]
  transfers between devices with their start and end apart: 9 -> 13, of which waited for: 4 -> 9; matrix products, arithmetic and copies ran while one was open for 0% -> 0% of each run, Pallas kernels for 7% -> 8%
where the time goes in v14:
time: 44.4 us; the launch traced here: 44.2 us
  waiting for transfers between devices  21.2 us (48%)
  starting transfers between devices  16.4 us (37%)
  Pallas kernels  5.81 us (13%)
  other arithmetic  0.73 us (2%)
    ppermute x6, waiting for transfers between devices, row_swap(): lax.ppermute(x, 'row', [(r, r ^ bit) for r in range(lax.axis_size('row'))])  8.35 us
    ppermute x3, waiting for transfers between devices, half_swap(): return lax.ppermute(x, 'half', [(0, 1), (1, 0)])  7.35 us
    ppermute x3, starting transfers between devices, half_swap(): return lax.ppermute(x, 'half', [(0, 1), (1, 0)])  5 us
    ppermute x6, starting transfers between devices, row_swap(): lax.ppermute(x, 'row', [(r, r ^ bit) for r in range(lax.axis_size('row'))])  4.02 us
    all_to_all x1, starting transfers between devices, local(): lax.all_to_all(restricted, 'near', split_axis=0, concat_axis=0, tiled=True)  3.78 us
    ppermute x3, waiting for transfers between devices, add_over_columns(): lax.ppermute(sums[2 * near:2 * near + 2], 'near', [(n, n ^ near) for n in...  3.73 us
    ppermute x3, starting transfers between devices, add_over_columns(): lax.ppermute(sums[2 * near:2 * near + 2], 'near', [(n, n ^ near) for n in...  3.55 us
    pallas_call x1, Pallas kernels, restrict_operator(): pl.pallas_call(restrict_kernel, out_shape=(jax.ShapeDtypeStruct((columns...  3.4 us
  transfers between devices with their start and end apart: 13, of which 9 were waited for; matrix products, arithmetic and copies ran while one was open for 0% of the time, Pallas kernels for 8%

profile of v14, /device:TPU:0, one launch (start us, length us, event | category | flops | bytes accessed | tf_op | source)
XLA Modules:
  0.0 44.2 jit_solution(15310456610074168504)
XLA Ops:
  0.0 3.0 %collective-permute-start.1 = (f32[512,128]{1,0:T(8,128)}, f32[512,128]{1,0:T(8,128)S(1)}, u32[]{:S(2)}, u32[]{:S(2)}) collective-permute-start(f32[512,128]{1,0:T(8,128)} %bitcast.18), channel_id=1, source_target_pairs={{0,16},{8,24},{16,0},{24,8},{1,17},{9,25},{17,1},{25,9},{2,18},{10... | collective-permute-start | bytes 786440 | tf_op jit(solution)/shard_map/ppermute | solution.py:202
  3.0 2.6 %collective-permute-start.4 = (f32[512,128]{1,0:T(8,128)}, f32[512,128]{1,0:T(8,128)S(1)}, u32[]{:S(2)}, u32[]{:S(2)}) collective-permute-start(f32[512,128]{1,0:T(8,128)} %bitcast.19), channel_id=1, source_target_pairs={{0,4},{4,0},{1,5},{5,1},{2,6},{6,2},{3,7},{7,3},{8,12},{12,8},{9,1... | collective-permute-start | bytes 786440 | tf_op jit(solution)/shard_map/ppermute | solution.py:206
  5.6 0.3 collective-permute-start.3
  5.9 3.4 %restrict_operator.1 = (f32[4,520,128]{2,1,0:T(8,128)}, f32[8,128]{1,0:T(8,128)}) custom-call(s32[8]{0:T(128)} %count_any.1, s32[8,8]{1,0:T(8,128)} %slot_any.1, s32[2,8]{1,0:T(2,128)} %bitcast.25, s32[4,8]{1,0:T(4,128)} %bitcast.24, f32[8,64,128]{2,1,0:T(8,128)} %restrict_any.1, f32[8,64,512]{2,1,0:T(8,128)} %operator_any.1), custom_call_target="tpu_custom_call" | custom-call | flops 201326592 | bytes 4194304 | tf_op jit(solution)/shard_map/restrict_operator/pallas_call | solution.py:111
  9.3 0.0 copy-start.1
  9.3 3.8 %all-to-all-start = ((f32[4,520,128]{2,1,0:T(8,128)}), f32[4,520,128]{2,1,0:T(8,128)S(1)}, u32[]{:S(2)}, u32[]{:S(2)}) async-start(f32[4,520,128]{2,1,0:T(8,128)} %get-tuple-element.7), calls=%async_computation | async-start | bytes 2129920 | tf_op jit(solution)/shard_map/all_to_all | solution.py:256
  13.1 4.5 %collective-permute-done.3.far_columns_ref = s32[2,8]{1,0:T(2,128)S(1)} collective-permute-done((s32[2,8]{1,0:T(2,128)}, s32[2,8]{1,0:T(2,128)S(1)}, u32[]{:S(2)}, u32[]{:S(2)}) %collective-permute-start.3) | collective-permute-done | bytes 96 | tf_op jit(solution)/shard_map/ppermute | solution.py:206
  17.7 0.5 %collective-permute-start.6 = (f32[520,128]{1,0:T(8,128)S(1)}, f32[520,128]{1,0:T(8,128)S(1)}, u32[]{:S(2)}, u32[]{:S(2)}) collective-permute-start(f32[520,128]{1,0:T(8,128)S(1)} %append_columns.1.rest_4_), channel_id=1, source_target_pairs={{0,16},{8,24},{16,0},{24,8},{1,17},{9,25},{17,1},{25,9},{2,18},{10... | collective-permute-start | bytes 798728 | tf_op jit(solution)/shard_map/ppermute | solution.py:202
  18.3 6.7 %collective-permute-done.6.rest_6_ = f32[520,128]{1,0:T(8,128)S(1)} collective-permute-done((f32[520,128]{1,0:T(8,128)S(1)}, f32[520,128]{1,0:T(8,128)S(1)}, u32[]{:S(2)}, u32[]{:S(2)}) %collective-permute-start.6) | collective-permute-done | bytes 266272 | tf_op jit(solution)/shard_map/ppermute | solution.py:202
  24.9 0.5 %collective-permute-start = (f32[512,128]{1,0:T(8,128)S(1)}, f32[512,128]{1,0:T(8,128)S(1)}, u32[]{:S(2)}, u32[]{:S(2)}) collective-permute-start(f32[512,128]{1,0:T(8,128)S(1)} %bitcast.20), channel_id=1, source_target_pairs={{0,8},{8,0},{16,24},{24,16},{1,9},{9,1},{17,25},{25,17},{2,10},{10... | collective-permute-start | bytes 786440 | tf_op jit(solution)/shard_map/ppermute | solution.py:202
  25.5 0.1 pad_add_fusion.own_ref
  25.5 1.3 %collective-permute-done.rest_1_ = f32[512,128]{1,0:T(8,128)S(1)} collective-permute-done((f32[512,128]{1,0:T(8,128)S(1)}, f32[512,128]{1,0:T(8,128)S(1)}, u32[]{:S(2)}, u32[]{:S(2)}) %collective-permute-start) | collective-permute-done | bytes 262176 | tf_op jit(solution)/shard_map/ppermute | solution.py:202
  26.8 0.4 collective-permute-done.2.rest_3_
  27.2 1.8 %all-to-all-done.restricted_ref = f32[4,520,128]{2,1,0:T(8,128)S(1)} async-done(((f32[4,520,128]{2,1,0:T(8,128)}), f32[4,520,128]{2,1,0:T(8,128)S(1)}, u32[]{:S(2)}, u32[]{:S(2)}) %all-to-all-start) | async-done | bytes 1064992 | tf_op jit(solution)/shard_map/all_to_all | solution.py:256
  29.0 2.4 %combine.1 = f32[8,64,128]{2,1,0:T(8,128)S(1)} custom-call(s32[10]{0:T(128)S(1)} %pad_add_fusion.own_ref, f32[4,520,128]{2,1,0:T(8,128)S(1)} %all-to-all-done.restricted_ref, f32[512,128]{1,0:T(8,128)S(1)} %bitcast.21, f32[512,128]{1,0:T(8,128)S(1)} %collective-permute-done.rest_1_, f32[512,128]{1,0:T(8,128)S(1)} %collective-permute-done.1.next_ref.rest_2_, ...), custom_call_target="tpu_custom_call" | custom-call | flops 268435456 | bytes 4194304 | tf_op jit(solution)/shard_map/combine/pallas_call | solution.py:182
  31.4 1.1 %collective-permute-start.10 = (f32[2,64,128]{2,1,0:T(8,128)S(1)}, f32[2,64,128]{2,1,0:T(8,128)S(1)}, u32[]{:S(2)}, u32[]{:S(2)}) collective-permute-start(f32[2,64,128]{2,1,0:T(8,128)S(1)} %get-tuple-element.10), channel_id=1, source_target_pairs={{0,3},{1,2},{2,1},{3,0},{4,7},{5,6},{6,5},{7,4},{8,11},{9,10},{10,... | collective-permute-start | bytes 196616 | tf_op jit(solution)/shard_map/ppermute | solution.py:228
  32.5 2.0 %collective-permute-start.9 = (f32[2,64,128]{2,1,0:T(8,128)S(1)}, f32[2,64,128]{2,1,0:T(8,128)S(1)}, u32[]{:S(2)}, u32[]{:S(2)}) collective-permute-start(f32[2,64,128]{2,1,0:T(8,128)S(1)} %get-tuple-element.11), channel_id=1, source_target_pairs={{0,2},{1,3},{2,0},{3,1},{4,6},{5,7},{6,4},{7,5},{8,10},{9,11},{10,... | collective-permute-start | bytes 196616 | tf_op jit(solution)/shard_map/ppermute | solution.py:228
  34.4 0.5 %collective-permute-start.8 = (f32[2,64,128]{2,1,0:T(8,128)S(1)}, f32[2,64,128]{2,1,0:T(8,128)S(1)}, u32[]{:S(2)}, u32[]{:S(2)}) collective-permute-start(f32[2,64,128]{2,1,0:T(8,128)S(1)} %get-tuple-element.9), channel_id=1, source_target_pairs={{0,1},{1,0},{2,3},{3,2},{4,5},{5,4},{6,7},{7,6},{8,9},{9,8},{10,11... | collective-permute-start | bytes 196616 | tf_op jit(solution)/shard_map/ppermute | solution.py:228
  35.0 2.2 %collective-permute-done.10 = f32[2,64,128]{2,1,0:T(8,128)S(1)} collective-permute-done((f32[2,64,128]{2,1,0:T(8,128)S(1)}, f32[2,64,128]{2,1,0:T(8,128)S(1)}, u32[]{:S(2)}, u32[]{:S(2)}) %collective-permute-start.10) | collective-permute-done | bytes 65568 | tf_op jit(solution)/shard_map/ppermute | solution.py:228
  37.2 0.6 %collective-permute-done.9 = f32[2,64,128]{2,1,0:T(8,128)S(1)} collective-permute-done((f32[2,64,128]{2,1,0:T(8,128)S(1)}, f32[2,64,128]{2,1,0:T(8,128)S(1)}, u32[]{:S(2)}, u32[]{:S(2)}) %collective-permute-start.9) | collective-permute-done | bytes 65568 | tf_op jit(solution)/shard_map/ppermute | solution.py:228
  37.8 0.9 %collective-permute-done.8 = f32[2,64,128]{2,1,0:T(8,128)S(1)} collective-permute-done((f32[2,64,128]{2,1,0:T(8,128)S(1)}, f32[2,64,128]{2,1,0:T(8,128)S(1)}, u32[]{:S(2)}, u32[]{:S(2)}) %collective-permute-start.8) | collective-permute-done | bytes 65568 | tf_op jit(solution)/shard_map/ppermute | solution.py:228
  38.7 2.1 %collective-permute-start.11 = (f32[64,128]{1,0:T(8,128)S(1)}, f32[64,128]{1,0:T(8,128)S(1)}, u32[]{:S(2)}, u32[]{:S(2)}) collective-permute-start(f32[64,128]{1,0:T(8,128)S(1)} %slice_bitcast_fusion), channel_id=1, source_target_pairs={{0,4},{4,0},{1,5},{5,1},{2,6},{6,2},{3,7},{7,3},{8,12},{12,8},{9,1... | collective-permute-start | bytes 98312 | tf_op jit(solution)/shard_map/ppermute | solution.py:206
  40.8 2.8 %collective-permute-done.11 = f32[64,128]{1,0:T(8,128)S(1)} collective-permute-done((f32[64,128]{1,0:T(8,128)S(1)}, f32[64,128]{1,0:T(8,128)S(1)}, u32[]{:S(2)}, u32[]{:S(2)}) %collective-permute-start.11) | collective-permute-done | bytes 32800 | tf_op jit(solution)/shard_map/ppermute | solution.py:206
  43.6 0.6 %fusion.3 = f32[128,64]{0,1:T(8,128)} fusion(f32[64,128]{1,0:T(8,128)S(1)} %collective-permute-done.11, f32[2,64,128]{2,1,0:T(8,128)S(1)} %fusion.1), kind=kLoop, calls=%fused_computation.6 | loop fusion | flops 8192 | bytes 98304 | tf_op jit(solution)/shard_map/transpose | solution.py:261
  (17 shorter events, 0.1 us)
Async XLA Ops:
  0.0 17.7 %collective-permute-start.1 = (f32[512,128]{1,0:T(8,128)}, f32[512,128]{1,0:T(8,128)S(1)}, u32[]{:S(2)}, u32[]{:S(2)}) collective-permute-start(f32[512,128]{1,0:T(8,128)} %bitcast.18), channel_id=1, source_target_pairs={{0,16},{8,24},{16,0},{24,8},{1,17},{9,25},{17,1},{25,9},{2,18},{10... | collective-permute-start | bytes 786440 | tf_op jit(solution)/shard_map/ppermute | solution.py:202
  3.0 14.7 %collective-permute-start.4 = (f32[512,128]{1,0:T(8,128)}, f32[512,128]{1,0:T(8,128)S(1)}, u32[]{:S(2)}, u32[]{:S(2)}) collective-permute-start(f32[512,128]{1,0:T(8,128)} %bitcast.19), channel_id=1, source_target_pairs={{0,4},{4,0},{1,5},{5,1},{2,6},{6,2},{3,7},{7,3},{8,12},{12,8},{9,1... | collective-permute-start | bytes 786440 | tf_op jit(solution)/shard_map/ppermute | solution.py:206
  5.6 12.1 %collective-permute-start.3 = (s32[2,8]{1,0:T(2,128)}, s32[2,8]{1,0:T(2,128)S(1)}, u32[]{:S(2)}, u32[]{:S(2)}) collective-permute-start(s32[2,8]{1,0:T(2,128)} %bitcast.22), channel_id=1, source_target_pairs={{0,4},{4,0},{1,5},{5,1},{2,6},{6,2},{3,7},{7,3},{8,12},{12,8},{9,1... | collective-permute-start | bytes 200 | tf_op jit(solution)/shard_map/ppermute | solution.py:206
  9.3 8.4 %copy-start.1 = (f32[8,128]{1,0:T(8,128)S(1)}, f32[8,128]{1,0:T(8,128)}, u32[]{:S(2)}) copy-start(f32[8,128]{1,0:T(8,128)} %get-tuple-element.8.mark_ref) | copy-start | bytes 12292
  9.3 8.4 %copy-start.2 = (s32[8,2]{0,1:T(2,128)S(1)}, s32[8,2]{0,1:T(2,128)}, u32[]{:S(2)}) copy-start(s32[8,2]{0,1:T(2,128)} %param.13) | copy-start | bytes 196
  9.3 19.7 %all-to-all-start = ((f32[4,520,128]{2,1,0:T(8,128)}), f32[4,520,128]{2,1,0:T(8,128)S(1)}, u32[]{:S(2)}, u32[]{:S(2)}) async-start(f32[4,520,128]{2,1,0:T(8,128)} %get-tuple-element.7), calls=%async_computation | async-start | bytes 2129920 | tf_op jit(solution)/shard_map/all_to_all | solution.py:256
  17.7 7.2 %copy-start = (f32[8,64,128]{2,1,0:T(8,128)S(1)}, f32[8,64,128]{2,1,0:T(8,128)}, u32[]{:S(2)}) copy-start(f32[8,64,128]{2,1,0:T(8,128)} %param.12) | copy-start | bytes 786436
  17.7 7.2 %collective-permute-start.6 = (f32[520,128]{1,0:T(8,128)S(1)}, f32[520,128]{1,0:T(8,128)S(1)}, u32[]{:S(2)}, u32[]{:S(2)}) collective-permute-start(f32[520,128]{1,0:T(8,128)S(1)} %append_columns.1.rest_4_), channel_id=1, source_target_pairs={{0,16},{8,24},{16,0},{24,8},{1,17},{9,25},{17,1},{25,9},{2,18},{10... | collective-permute-start | bytes 798728 | tf_op jit(solution)/shard_map/ppermute | solution.py:202
  18.3 9.0 %collective-permute-start.5 = (f32[520,128]{1,0:T(8,128)S(1)}, f32[520,128]{1,0:T(8,128)S(1)}, u32[]{:S(2)}, u32[]{:S(2)}) collective-permute-start(f32[520,128]{1,0:T(8,128)S(1)} %append_columns.1.rest_4_), channel_id=1, source_target_pairs={{0,8},{8,0},{16,24},{24,16},{1,9},{9,1},{17,25},{25,17},{2,10},{10... | collective-permute-start | bytes 798728 | tf_op jit(solution)/shard_map/ppermute | solution.py:202
  24.9 2.3 %collective-permute-start.7 = (f32[520,128]{1,0:T(8,128)S(1)}, f32[520,128]{1,0:T(8,128)S(1)}, u32[]{:S(2)}, u32[]{:S(2)}) collective-permute-start(f32[520,128]{1,0:T(8,128)S(1)} %collective-permute-done.6.rest_6_), channel_id=1, source_target_pairs={{0,8},{8,0},{16,24},{24,16},{1,9},{9,1},{17,25},{25,17},{2,10},{10... | collective-permute-start | bytes 798728 | tf_op jit(solution)/shard_map/ppermute | solution.py:202
  24.9 1.9 %collective-permute-start = (f32[512,128]{1,0:T(8,128)S(1)}, f32[512,128]{1,0:T(8,128)S(1)}, u32[]{:S(2)}, u32[]{:S(2)}) collective-permute-start(f32[512,128]{1,0:T(8,128)S(1)} %bitcast.20), channel_id=1, source_target_pairs={{0,8},{8,0},{16,24},{24,16},{1,9},{9,1},{17,25},{25,17},{2,10},{10... | collective-permute-start | bytes 786440 | tf_op jit(solution)/shard_map/ppermute | solution.py:202
  25.4 1.8 %collective-permute-start.2 = (f32[512,128]{1,0:T(8,128)S(1)}, f32[512,128]{1,0:T(8,128)S(1)}, u32[]{:S(2)}, u32[]{:S(2)}) collective-permute-start(f32[512,128]{1,0:T(8,128)S(1)} %collective-permute-done.1.next_ref.rest_2_), channel_id=1, source_target_pairs={{0,8},{8,0},{16,24},{24,16},{1,9},{9,1},{17,25},{25,17},{2,10},{10... | collective-permute-start | bytes 786440 | tf_op jit(solution)/shard_map/ppermute | solution.py:202
  31.4 5.8 %collective-permute-start.10 = (f32[2,64,128]{2,1,0:T(8,128)S(1)}, f32[2,64,128]{2,1,0:T(8,128)S(1)}, u32[]{:S(2)}, u32[]{:S(2)}) collective-permute-start(f32[2,64,128]{2,1,0:T(8,128)S(1)} %get-tuple-element.10), channel_id=1, source_target_pairs={{0,3},{1,2},{2,1},{3,0},{4,7},{5,6},{6,5},{7,4},{8,11},{9,10},{10,... | collective-permute-start | bytes 196616 | tf_op jit(solution)/shard_map/ppermute | solution.py:228
  32.5 5.3 %collective-permute-start.9 = (f32[2,64,128]{2,1,0:T(8,128)S(1)}, f32[2,64,128]{2,1,0:T(8,128)S(1)}, u32[]{:S(2)}, u32[]{:S(2)}) collective-permute-start(f32[2,64,128]{2,1,0:T(8,128)S(1)} %get-tuple-element.11), channel_id=1, source_target_pairs={{0,2},{1,3},{2,0},{3,1},{4,6},{5,7},{6,4},{7,5},{8,10},{9,11},{10,... | collective-permute-start | bytes 196616 | tf_op jit(solution)/shard_map/ppermute | solution.py:228
  34.4 4.3 %collective-permute-start.8 = (f32[2,64,128]{2,1,0:T(8,128)S(1)}, f32[2,64,128]{2,1,0:T(8,128)S(1)}, u32[]{:S(2)}, u32[]{:S(2)}) collective-permute-start(f32[2,64,128]{2,1,0:T(8,128)S(1)} %get-tuple-element.9), channel_id=1, source_target_pairs={{0,1},{1,0},{2,3},{3,2},{4,5},{5,4},{6,7},{7,6},{8,9},{9,8},{10,11... | collective-permute-start | bytes 196616 | tf_op jit(solution)/shard_map/ppermute | solution.py:228
  38.7 4.9 %collective-permute-start.11 = (f32[64,128]{1,0:T(8,128)S(1)}, f32[64,128]{1,0:T(8,128)S(1)}, u32[]{:S(2)}, u32[]{:S(2)}) collective-permute-start(f32[64,128]{1,0:T(8,128)S(1)} %slice_bitcast_fusion), channel_id=1, source_target_pairs={{0,4},{4,0},{1,5},{5,1},{2,6},{6,2},{3,7},{7,3},{8,12},{12,8},{9,1... | collective-permute-start | bytes 98312 | tf_op jit(solution)/shard_map/ppermute | solution.py:206

commit v15 on v14

--- a/solution.py
+++ b/solution.py
@@ -15,18 +15,21 @@
 VMEM_LIMIT = 48 * 1024 * 1024
 
 
-def split3(x, order):
+def halves(x):
     high = x.astype(jnp.bfloat16)
-    low = (x - high.astype(jnp.float32)).astype(jnp.bfloat16)
-    parts = {"left": (high, low, high), "right": (high, high, low)}[order]
-    return jnp.concatenate(parts, axis=0)
-
-
-def transposed_dot(left, right):
-    return lax.dot_general(left, right, (((0,), (0,)), ((), ())), preferred_element_type=jnp.float32)
-
-
-def append_kernel(mark_ref, next_ref, far_columns_ref, own_columns_ref, blocks_ref, out_ref):
+    return high, (x - high.astype(jnp.float32)).astype(jnp.bfloat16)
+
+
+def transposed_product(left, right):
+    tall = jnp.concatenate(halves(left), axis=0)
+    wide = jnp.concatenate(halves(right), axis=1)
+    wide = jnp.concatenate([wide, wide], axis=0)
+    both = lax.dot_general(tall, wide, (((0,), (0,)), ((), ())), preferred_element_type=jnp.float32)
+    width = right.shape[1]
+    return both[:, :width] + both[:, width:]
+
+
+def append_kernel(next_ref, far_columns_ref, own_columns_ref, blocks_ref, out_ref):
     used = blocks_ref.shape[0]
     entries, fine_rows = own_columns_ref.shape
     out_ref[:used] = blocks_ref[...]
@@ -35,21 +38,22 @@
     out_ref[used + entries : used + 2 * entries, :fine_rows] = own_columns_ref[...].astype(jnp.float32)
 
 
-def append_columns(mark, next_blocks, far_columns, own_columns, blocks):
+def append_columns(next_blocks, far_columns, own_columns, blocks):
     used, width = blocks.shape
     return pl.pallas_call(
         append_kernel,
         out_shape=jax.ShapeDtypeStruct((used + EXTRA, width), blocks.dtype),
-        in_specs=[pl.BlockSpec(memory_space=pltpu.VMEM)] * 5,
+        in_specs=[pl.BlockSpec(memory_space=pltpu.VMEM)] * 4,
         out_specs=pl.BlockSpec(memory_space=pltpu.VMEM),
         compiler_params=pltpu.CompilerParams(vmem_limit_bytes=VMEM_LIMIT),
         cost_estimate=pl.CostEstimate(flops=HOLD_FLOPS, bytes_accessed=HOLD_FLOPS >> 8, transcendentals=0),
         name="append_columns",
-    )(mark, next_blocks, far_columns, own_columns, blocks)
+    )(next_blocks, far_columns, own_columns, blocks)
 
 
 def restrict_kernel(
-    count_any, slot_any, rows_any, fetch_any, restrict_any, operator_any, out_ref, mark_ref,
+    count_any, slot_any, rows_any, fetch_any, restrict_any, operator_any, columns_any, blocks_any,
+    out_ref, own_columns_ref, own_blocks_ref,
     count_ref, slot_ref, rows_ref, fetch_ref, restrict_ref, operator_ref, sems, operator_sems,
 ):
     fine_rows, block_size, _ = operator_ref.shape
@@ -62,6 +66,7 @@
     pairs = [
         (count_any, count_ref), (slot_any, slot_ref), (rows_any, rows_ref),
         (fetch_any, fetch_ref), (restrict_any, restrict_ref),
+        (columns_any, own_columns_ref), (blocks_any, own_blocks_ref),
     ]
     copies = [pltpu.make_async_copy(a, b, sems.at[i]) for i, (a, b) in enumerate(pairs)]
     operators = [
@@ -85,7 +90,6 @@
                 wanted = fetch_ref[s, side * half + near]
                 value = jnp.where(short_lane == side * slot_count + s, wanted, value)
         out_ref[near, used:] = value.astype(jnp.float32)
-    mark_ref[...] = out_ref[0, used:]
 
     for i in range(fine_rows):
         value = restrict_ref[i]
@@ -93,7 +97,7 @@
         own_row = jnp.where(second == 0, rows_ref[0, i], rows_ref[1, i])
         other_row = jnp.where(second == 0, rows_ref[1, i], rows_ref[0, i])
         dense = jnp.where(own_row == second, value, 0.0) + jnp.where(other_row == second, swapped, 0.0)
-        product = transposed_dot(split3(operator_ref[i], "left"), split3(dense, "right"))
+        product = transposed_product(operator_ref[i], dense)
         for k in range(entries):
             part = jnp.where(k < count_ref[i], product[k * block_size : (k + 1) * block_size], 0.0)
             peer = lax.div(slot_ref[i, k], slot_count)
@@ -102,7 +106,9 @@
             out_ref[lax.rem(peer, half), pl.ds(start, block_size)] += part
 
 
-def restrict_operator(operator_count, operator_slot, restrict_rows, fetch, operator_blocks, restrict_blocks):
+def restrict_operator(
+    operator_count, operator_slot, restrict_rows, fetch, operator_blocks, restrict_blocks, own_columns, own_blocks
+):
     fine_rows, block_size, width = operator_blocks.shape
     slot_count, columns = fetch.shape
     wide = NCR * block_size
@@ -112,18 +118,19 @@
         restrict_kernel,
         out_shape=(
             jax.ShapeDtypeStruct((columns // 2, rows, wide), jnp.float32),
-            jax.ShapeDtypeStruct((EXTRA, wide), jnp.float32),
+            jax.ShapeDtypeStruct(own_columns.shape, own_columns.dtype),
+            jax.ShapeDtypeStruct(own_blocks.shape, own_blocks.dtype),
         ),
-        in_specs=[pl.BlockSpec(memory_space=pltpu.HBM)] * 6,
-        out_specs=[pl.BlockSpec(memory_space=pltpu.VMEM)] * 2,
+        in_specs=[pl.BlockSpec(memory_space=pltpu.HBM)] * 8,
+        out_specs=[pl.BlockSpec(memory_space=pltpu.VMEM)] * 3,
         scratch_shapes=[pltpu.SMEM(x.shape, x.dtype) for x in small]
         + [pltpu.VMEM(x.shape, x.dtype) for x in (restrict_blocks, operator_blocks)]
-        + [pltpu.SemaphoreType.DMA((5,)), pltpu.SemaphoreType.DMA((fine_rows,))],
+        + [pltpu.SemaphoreType.DMA((7,)), pltpu.SemaphoreType.DMA((fine_rows,))],
         cost_estimate=pl.CostEstimate(
             flops=6 * fine_rows * block_size * width * wide, bytes_accessed=4 << 20, transcendentals=0
         ),
         name="restrict_operator",
-    )(*small, restrict_blocks, operator_blocks)
+    )(*small, restrict_blocks, operator_blocks, own_columns, own_blocks)
 
 
 def combine_kernel(own_ref, restricted_ref, *rest, slot_count, fine_rows, entries):
@@ -160,7 +167,7 @@
         piece = far * rows + (lax.div(wanted, fine_rows * columns) ^ own_ref[0])
         block = held_ref[piece, pl.ds(pl.multiple_of(inside * block_size, block_size), block_size)]
         restricted = restricted_ref[near, pl.ds(pl.multiple_of(place * block_size, block_size), block_size)]
-        product = transposed_dot(split3(block, "left"), split3(restricted, "right"))
+        product = transposed_product(block, restricted)
         for m in range(entries):
             column = own_ref[2 + index_ref[half + entries * piece + m, inside]]
             total[m % len(total)][column] += product[m * block_size : (m + 1) * block_size]
@@ -246,16 +253,22 @@
     own = jnp.stack([lax.axis_index("row"), lax.axis_index("half")])
     own = jnp.concatenate([own, place_of_columns(half)])
 
-    own_columns = prolong_cols.T
     near_blocks = prolong_blocks.reshape(fine_rows * block_size, width)
     far_blocks = half_swap(near_blocks)
-    far_columns = half_swap(own_columns)
-    restricted, mark = restrict_operator(
-        operator_count, operator_slot, restrict_rows.T, fetch, operator_blocks, restrict_blocks
+    restricted, own_columns, near_blocks = restrict_operator(
+        operator_count,
+        operator_slot,
+        restrict_rows.T,
+        fetch,
+        operator_blocks,
+        restrict_blocks,
+        prolong_cols.T,
+        near_blocks,
     )
     restricted = lax.all_to_all(restricted, "near", split_axis=0, concat_axis=0, tiled=True)
+    far_columns = half_swap(own_columns)
     near_pieces = spread_over_rows(near_blocks, rows)
-    far_blocks = append_columns(mark, near_pieces[rows // 2], far_columns, own_columns, far_blocks)
+    far_blocks = append_columns(near_pieces[rows // 2], far_columns, own_columns, far_blocks)
     pieces = near_pieces + spread_over_rows(far_blocks, rows)
     sums = combine(own, restricted, pieces, NCR * rows, slot_count, fine_rows, block_size)
     return add_over_columns(sums, half).T

time: 44.4 us -> 42.8 us (0.964)
  waiting for transfers between devices: 21.2 us -> 17.2 us
  starting transfers between devices: 16.4 us -> 18.8 us
    ppermute x3, starting transfers between devices: 5 us -> 7.56 us  [half_swap(): return lax.ppermute(x, 'half', [(0, 1), (1, 0)])]
    ppermute x3, waiting for transfers between devices: 7.35 us -> 4.94 us  [half_swap(): return lax.ppermute(x, 'half', [(0, 1), (1, 0)])]
    ppermute x6, waiting for transfers between devices: 8.35 us -> 7.55 us  [row_swap(): lax.ppermute(x, 'row', [(r, r ^ bit) for r in range(lax.axis_size('row'))])]
    ppermute x3, waiting for transfers between devices: 3.73 us -> 3.22 us  [add_over_columns(): lax.ppermute(sums[2 * near:2 * near + 2], 'near', [(n, n ^ near) for n in...]
  transfers between devices with their start and end apart: 13 -> 13, of which waited for: 9 -> 8; matrix products, arithmetic and copies ran while one was open for 0% -> 0% of each run, Pallas kernels for 8% -> 8%
where the time goes in v15:
time: 42.8 us; the launch traced here: 42.5 us
  starting transfers between devices  18.8 us (44%)
  waiting for transfers between devices  17.2 us (40%)
  Pallas kernels  5.79 us (14%)
  other arithmetic  0.73 us (2%)
    ppermute x3, starting transfers between devices, half_swap(): return lax.ppermute(x, 'half', [(0, 1), (1, 0)])  7.56 us
    ppermute x6, waiting for transfers between devices, row_swap(): lax.ppermute(x, 'row', [(r, r ^ bit) for r in range(lax.axis_size('row'))])  7.55 us
    ppermute x3, waiting for transfers between devices, half_swap(): return lax.ppermute(x, 'half', [(0, 1), (1, 0)])  4.94 us
    all_to_all x1, starting transfers between devices, local(): lax.all_to_all(restricted, 'near', split_axis=0, concat_axis=0, tiled=True)  3.9 us
    ppermute x6, starting transfers between devices, row_swap(): lax.ppermute(x, 'row', [(r, r ^ bit) for r in range(lax.axis_size('row'))])  3.74 us
    ppermute x3, starting transfers between devices, add_over_columns(): lax.ppermute(sums[2 * near:2 * near + 2], 'near', [(n, n ^ near) for n in...  3.55 us
    pallas_call x1, Pallas kernels, restrict_operator(): pl.pallas_call(restrict_kernel, out_shape=(jax.ShapeDtypeStruct((columns...  3.43 us
    ppermute x3, waiting for transfers between devices, add_over_columns(): lax.ppermute(sums[2 * near:2 * near + 2], 'near', [(n, n ^ near) for n in...  3.22 us
  transfers between devices with their start and end apart: 13, of which 8 were waited for; matrix products, arithmetic and copies ran while one was open for 0% of the time, Pallas kernels for 8%

profile of v15, /device:TPU:0, one launch (start us, length us, event | category | flops | bytes accessed | tf_op | source)
XLA Modules:
  0.0 42.5 jit_solution(10869861301793426226)
XLA Ops:
  0.0 4.0 %collective-permute-start.4 = (f32[512,128]{1,0:T(8,128)}, f32[512,128]{1,0:T(8,128)S(1)}, u32[]{:S(2)}, u32[]{:S(2)}) collective-permute-start(f32[512,128]{1,0:T(8,128)} %bitcast.18), channel_id=1, source_target_pairs={{0,4},{4,0},{1,5},{5,1},{2,6},{6,2},{3,7},{7,3},{8,12},{12,8},{9,1... | collective-permute-start | bytes 786440 | tf_op jit(solution)/shard_map/ppermute | solution.py:213
  4.0 3.4 %restrict_operator.1 = (f32[4,520,128]{2,1,0:T(8,128)}, s32[2,8]{1,0:T(2,128)}, f32[512,128]{1,0:T(8,128)}) custom-call(s32[8]{0:T(128)} %count_any.1, s32[8,8]{1,0:T(8,128)} %slot_any.1, s32[2,8]{1,0:T(2,128)} %bitcast.21, s32[4,8]{1,0:T(4,128)} %bitcast.20, f32[8,64,128]{2,1,0:T(8,128)} %restrict_any.1, f32[8,64,512]{2,1,0:T(8,128)} %operator_any.1, ...), custom_call_target="tpu_custom_call" | custom-call | flops 201326592 | bytes 4194304 | tf_op jit(solution)/shard_map/restrict_operator/pallas_call | solution.py:117
  7.5 1.6 %collective-permute-start.1 = (f32[512,128]{1,0:T(8,128)}, f32[512,128]{1,0:T(8,128)S(1)}, u32[]{:S(2)}, u32[]{:S(2)}) collective-permute-start(f32[512,128]{1,0:T(8,128)} %get-tuple-element.9.rest_0_), channel_id=1, source_target_pairs={{0,16},{8,24},{16,0},{24,8},{1,17},{9,25},{17,1},{25,9},{2,18},{10... | collective-permute-start | bytes 786440 | tf_op jit(solution)/shard_map/ppermute | solution.py:209
  9.1 0.3 collective-permute-start.3
  9.4 3.9 %all-to-all-start = ((f32[4,520,128]{2,1,0:T(8,128)}), f32[4,520,128]{2,1,0:T(8,128)S(1)}, u32[]{:S(2)}, u32[]{:S(2)}) async-start(f32[4,520,128]{2,1,0:T(8,128)} %get-tuple-element.8), calls=%async_computation | async-start | bytes 2129920 | tf_op jit(solution)/shard_map/all_to_all | solution.py:268
  13.3 3.0 %collective-permute-done.3.far_columns_ref = s32[2,8]{1,0:T(2,128)S(1)} collective-permute-done((s32[2,8]{1,0:T(2,128)}, s32[2,8]{1,0:T(2,128)S(1)}, u32[]{:S(2)}, u32[]{:S(2)}) %collective-permute-start.3) | collective-permute-done | bytes 96 | tf_op jit(solution)/shard_map/ppermute | solution.py:213
  16.4 1.6 %collective-permute-start.6 = (f32[520,128]{1,0:T(8,128)S(1)}, f32[520,128]{1,0:T(8,128)S(1)}, u32[]{:S(2)}, u32[]{:S(2)}) collective-permute-start(f32[520,128]{1,0:T(8,128)S(1)} %append_columns.1.rest_4_), channel_id=1, source_target_pairs={{0,16},{8,24},{16,0},{24,8},{1,17},{9,25},{17,1},{25,9},{2,18},{10... | collective-permute-start | bytes 798728 | tf_op jit(solution)/shard_map/ppermute | solution.py:209
  18.0 5.9 %collective-permute-done.6.rest_6_ = f32[520,128]{1,0:T(8,128)S(1)} collective-permute-done((f32[520,128]{1,0:T(8,128)S(1)}, f32[520,128]{1,0:T(8,128)S(1)}, u32[]{:S(2)}, u32[]{:S(2)}) %collective-permute-start.6) | collective-permute-done | bytes 266272 | tf_op jit(solution)/shard_map/ppermute | solution.py:209
  23.9 0.5 %collective-permute-start = (f32[512,128]{1,0:T(8,128)S(1)}, f32[512,128]{1,0:T(8,128)S(1)}, u32[]{:S(2)}, u32[]{:S(2)}) collective-permute-start(f32[512,128]{1,0:T(8,128)S(1)} %copy-done), channel_id=1, source_target_pairs={{0,8},{8,0},{16,24},{24,16},{1,9},{9,1},{17,25},{25,17},{2,10},{10... | collective-permute-start | bytes 786440 | tf_op jit(solution)/shard_map/ppermute | solution.py:209
  24.4 0.0 collective-permute-start.2
  24.4 0.1 pad_add_fusion.own_ref
  24.5 1.3 %collective-permute-done.rest_1_ = f32[512,128]{1,0:T(8,128)S(1)} collective-permute-done((f32[512,128]{1,0:T(8,128)S(1)}, f32[512,128]{1,0:T(8,128)S(1)}, u32[]{:S(2)}, u32[]{:S(2)}) %collective-permute-start) | collective-permute-done | bytes 262176 | tf_op jit(solution)/shard_map/ppermute | solution.py:209
  25.8 0.4 collective-permute-done.2.rest_3_
  26.2 0.0 collective-permute-done.5.rest_5_
  26.2 1.5 %all-to-all-done.restricted_ref = f32[4,520,128]{2,1,0:T(8,128)S(1)} async-done(((f32[4,520,128]{2,1,0:T(8,128)}), f32[4,520,128]{2,1,0:T(8,128)S(1)}, u32[]{:S(2)}, u32[]{:S(2)}) %all-to-all-start) | async-done | bytes 1064992 | tf_op jit(solution)/shard_map/all_to_all | solution.py:268
  27.7 2.3 %combine.1 = f32[8,64,128]{2,1,0:T(8,128)S(1)} custom-call(s32[10]{0:T(128)S(1)} %pad_add_fusion.own_ref, f32[4,520,128]{2,1,0:T(8,128)S(1)} %all-to-all-done.restricted_ref, f32[512,128]{1,0:T(8,128)S(1)} %copy-done, f32[512,128]{1,0:T(8,128)S(1)} %collective-permute-done.rest_1_, f32[512,128]{1,0:T(8,128)S(1)} %collective-permute-done.1.next_ref.rest_2_, ...), custom_call_target="tpu_custom_call" | custom-call | flops 268435456 | bytes 4194304 | tf_op jit(solution)/shard_map/combine/pallas_call | solution.py:189
  30.0 1.6 %collective-permute-start.8 = (f32[2,64,128]{2,1,0:T(8,128)S(1)}, f32[2,64,128]{2,1,0:T(8,128)S(1)}, u32[]{:S(2)}, u32[]{:S(2)}) collective-permute-start(f32[2,64,128]{2,1,0:T(8,128)S(1)} %get-tuple-element.11), channel_id=1, source_target_pairs={{0,1},{1,0},{2,3},{3,2},{4,5},{5,4},{6,7},{7,6},{8,9},{9,8},{10,11... | collective-permute-start | bytes 196616 | tf_op jit(solution)/shard_map/ppermute | solution.py:235
  31.6 0.0 collective-permute-start.10
  31.7 1.9 %collective-permute-start.9 = (f32[2,64,128]{2,1,0:T(8,128)S(1)}, f32[2,64,128]{2,1,0:T(8,128)S(1)}, u32[]{:S(2)}, u32[]{:S(2)}) collective-permute-start(f32[2,64,128]{2,1,0:T(8,128)S(1)} %get-tuple-element.13), channel_id=1, source_target_pairs={{0,2},{1,3},{2,0},{3,1},{4,6},{5,7},{6,4},{7,5},{8,10},{9,11},{10,... | collective-permute-start | bytes 196616 | tf_op jit(solution)/shard_map/ppermute | solution.py:235
  33.6 1.5 %collective-permute-done.8 = f32[2,64,128]{2,1,0:T(8,128)S(1)} collective-permute-done((f32[2,64,128]{2,1,0:T(8,128)S(1)}, f32[2,64,128]{2,1,0:T(8,128)S(1)}, u32[]{:S(2)}, u32[]{:S(2)}) %collective-permute-start.8) | collective-permute-done | bytes 65568 | tf_op jit(solution)/shard_map/ppermute | solution.py:235
  35.1 1.7 %collective-permute-done.10 = f32[2,64,128]{2,1,0:T(8,128)S(1)} collective-permute-done((f32[2,64,128]{2,1,0:T(8,128)S(1)}, f32[2,64,128]{2,1,0:T(8,128)S(1)}, u32[]{:S(2)}, u32[]{:S(2)}) %collective-permute-start.10) | collective-permute-done | bytes 65568 | tf_op jit(solution)/shard_map/ppermute | solution.py:235
  36.8 3.2 %collective-permute-start.11 = (f32[64,128]{1,0:T(8,128)S(1)}, f32[64,128]{1,0:T(8,128)S(1)}, u32[]{:S(2)}, u32[]{:S(2)}) collective-permute-start(f32[64,128]{1,0:T(8,128)S(1)} %slice_bitcast_fusion), channel_id=1, source_target_pairs={{0,4},{4,0},{1,5},{5,1},{2,6},{6,2},{3,7},{7,3},{8,12},{12,8},{9,1... | collective-permute-start | bytes 98312 | tf_op jit(solution)/shard_map/ppermute | solution.py:213
  40.0 1.9 %collective-permute-done.11 = f32[64,128]{1,0:T(8,128)S(1)} collective-permute-done((f32[64,128]{1,0:T(8,128)S(1)}, f32[64,128]{1,0:T(8,128)S(1)}, u32[]{:S(2)}, u32[]{:S(2)}) %collective-permute-start.11) | collective-permute-done | bytes 32800 | tf_op jit(solution)/shard_map/ppermute | solution.py:213
  41.9 0.6 %fusion.3 = f32[128,64]{0,1:T(8,128)} fusion(f32[64,128]{1,0:T(8,128)S(1)} %collective-permute-done.11, f32[2,64,128]{2,1,0:T(8,128)S(1)} %fusion.1), kind=kLoop, calls=%fused_computation.6 | loop fusion | flops 8192 | bytes 98304 | tf_op jit(solution)/shard_map/transpose | solution.py:274
  (15 shorter events, 0.1 us)
Async XLA Ops:
  0.0 16.4 %collective-permute-start.4 = (f32[512,128]{1,0:T(8,128)}, f32[512,128]{1,0:T(8,128)S(1)}, u32[]{:S(2)}, u32[]{:S(2)}) collective-permute-start(f32[512,128]{1,0:T(8,128)} %bitcast.18), channel_id=1, source_target_pairs={{0,4},{4,0},{1,5},{5,1},{2,6},{6,2},{3,7},{7,3},{8,12},{12,8},{9,1... | collective-permute-start | bytes 786440 | tf_op jit(solution)/shard_map/ppermute | solution.py:213
  7.5 8.9 %collective-permute-start.1 = (f32[512,128]{1,0:T(8,128)}, f32[512,128]{1,0:T(8,128)S(1)}, u32[]{:S(2)}, u32[]{:S(2)}) collective-permute-start(f32[512,128]{1,0:T(8,128)} %get-tuple-element.9.rest_0_), channel_id=1, source_target_pairs={{0,16},{8,24},{16,0},{24,8},{1,17},{9,25},{17,1},{25,9},{2,18},{10... | collective-permute-start | bytes 786440 | tf_op jit(solution)/shard_map/ppermute | solution.py:209
  9.1 7.3 %collective-permute-start.3 = (s32[2,8]{1,0:T(2,128)}, s32[2,8]{1,0:T(2,128)S(1)}, u32[]{:S(2)}, u32[]{:S(2)}) collective-permute-start(s32[2,8]{1,0:T(2,128)} %get-tuple-element.10.own_columns_ref), channel_id=1, source_target_pairs={{0,4},{4,0},{1,5},{5,1},{2,6},{6,2},{3,7},{7,3},{8,12},{12,8},{9,1... | collective-permute-start | bytes 200 | tf_op jit(solution)/shard_map/ppermute | solution.py:213
  9.4 7.0 %copy-start.1 = (s32[2,8]{1,0:T(2,128)S(1)}, s32[2,8]{1,0:T(2,128)}, u32[]{:S(2)}) copy-start(s32[2,8]{1,0:T(2,128)} %get-tuple-element.10.own_columns_ref) | copy-start | bytes 196
  9.4 18.3 %all-to-all-start = ((f32[4,520,128]{2,1,0:T(8,128)}), f32[4,520,128]{2,1,0:T(8,128)S(1)}, u32[]{:S(2)}, u32[]{:S(2)}) async-start(f32[4,520,128]{2,1,0:T(8,128)} %get-tuple-element.8), calls=%async_computation | async-start | bytes 2129920 | tf_op jit(solution)/shard_map/all_to_all | solution.py:268
  13.3 10.6 %copy-start = (f32[512,128]{1,0:T(8,128)S(1)}, f32[512,128]{1,0:T(8,128)}, u32[]{:S(2)}) copy-start(f32[512,128]{1,0:T(8,128)} %get-tuple-element.9.rest_0_) | copy-start | bytes 786436
  16.4 7.5 %collective-permute-start.6 = (f32[520,128]{1,0:T(8,128)S(1)}, f32[520,128]{1,0:T(8,128)S(1)}, u32[]{:S(2)}, u32[]{:S(2)}) collective-permute-start(f32[520,128]{1,0:T(8,128)S(1)} %append_columns.1.rest_4_), channel_id=1, source_target_pairs={{0,16},{8,24},{16,0},{24,8},{1,17},{9,25},{17,1},{25,9},{2,18},{10... | collective-permute-start | bytes 798728 | tf_op jit(solution)/shard_map/ppermute | solution.py:209
  18.0 8.2 %collective-permute-start.5 = (f32[520,128]{1,0:T(8,128)S(1)}, f32[520,128]{1,0:T(8,128)S(1)}, u32[]{:S(2)}, u32[]{:S(2)}) collective-permute-start(f32[520,128]{1,0:T(8,128)S(1)} %append_columns.1.rest_4_), channel_id=1, source_target_pairs={{0,8},{8,0},{16,24},{24,16},{1,9},{9,1},{17,25},{25,17},{2,10},{10... | collective-permute-start | bytes 798728 | tf_op jit(solution)/shard_map/ppermute | solution.py:209
  23.9 2.3 %collective-permute-start.7 = (f32[520,128]{1,0:T(8,128)S(1)}, f32[520,128]{1,0:T(8,128)S(1)}, u32[]{:S(2)}, u32[]{:S(2)}) collective-permute-start(f32[520,128]{1,0:T(8,128)S(1)} %collective-permute-done.6.rest_6_), channel_id=1, source_target_pairs={{0,8},{8,0},{16,24},{24,16},{1,9},{9,1},{17,25},{25,17},{2,10},{10... | collective-permute-start | bytes 798728 | tf_op jit(solution)/shard_map/ppermute | solution.py:209
  23.9 1.9 %collective-permute-start = (f32[512,128]{1,0:T(8,128)S(1)}, f32[512,128]{1,0:T(8,128)S(1)}, u32[]{:S(2)}, u32[]{:S(2)}) collective-permute-start(f32[512,128]{1,0:T(8,128)S(1)} %copy-done), channel_id=1, source_target_pairs={{0,8},{8,0},{16,24},{24,16},{1,9},{9,1},{17,25},{25,17},{2,10},{10... | collective-permute-start | bytes 786440 | tf_op jit(solution)/shard_map/ppermute | solution.py:209
  24.4 1.8 %collective-permute-start.2 = (f32[512,128]{1,0:T(8,128)S(1)}, f32[512,128]{1,0:T(8,128)S(1)}, u32[]{:S(2)}, u32[]{:S(2)}) collective-permute-start(f32[512,128]{1,0:T(8,128)S(1)} %collective-permute-done.1.next_ref.rest_2_), channel_id=1, source_target_pairs={{0,8},{8,0},{16,24},{24,16},{1,9},{9,1},{17,25},{25,17},{2,10},{10... | collective-permute-start | bytes 786440 | tf_op jit(solution)/shard_map/ppermute | solution.py:209
  30.0 5.0 %collective-permute-start.8 = (f32[2,64,128]{2,1,0:T(8,128)S(1)}, f32[2,64,128]{2,1,0:T(8,128)S(1)}, u32[]{:S(2)}, u32[]{:S(2)}) collective-permute-start(f32[2,64,128]{2,1,0:T(8,128)S(1)} %get-tuple-element.11), channel_id=1, source_target_pairs={{0,1},{1,0},{2,3},{3,2},{4,5},{5,4},{6,7},{7,6},{8,9},{9,8},{10,11... | collective-permute-start | bytes 196616 | tf_op jit(solution)/shard_map/ppermute | solution.py:235
  31.6 5.2 %collective-permute-start.10 = (f32[2,64,128]{2,1,0:T(8,128)S(1)}, f32[2,64,128]{2,1,0:T(8,128)S(1)}, u32[]{:S(2)}, u32[]{:S(2)}) collective-permute-start(f32[2,64,128]{2,1,0:T(8,128)S(1)} %get-tuple-element.12), channel_id=1, source_target_pairs={{0,3},{1,2},{2,1},{3,0},{4,7},{5,6},{6,5},{7,4},{8,11},{9,10},{10,... | collective-permute-start | bytes 196616 | tf_op jit(solution)/shard_map/ppermute | solution.py:235
  31.7 5.1 %collective-permute-start.9 = (f32[2,64,128]{2,1,0:T(8,128)S(1)}, f32[2,64,128]{2,1,0:T(8,128)S(1)}, u32[]{:S(2)}, u32[]{:S(2)}) collective-permute-start(f32[2,64,128]{2,1,0:T(8,128)S(1)} %get-tuple-element.13), channel_id=1, source_target_pairs={{0,2},{1,3},{2,0},{3,1},{4,6},{5,7},{6,4},{7,5},{8,10},{9,11},{10,... | collective-permute-start | bytes 196616 | tf_op jit(solution)/shard_map/ppermute | solution.py:235
  36.8 5.1 %collective-permute-start.11 = (f32[64,128]{1,0:T(8,128)S(1)}, f32[64,128]{1,0:T(8,128)S(1)}, u32[]{:S(2)}, u32[]{:S(2)}) collective-permute-start(f32[64,128]{1,0:T(8,128)S(1)} %slice_bitcast_fusion), channel_id=1, source_target_pairs={{0,4},{4,0},{1,5},{5,1},{2,6},{6,2},{3,7},{7,3},{8,12},{12,8},{9,1... | collective-permute-start | bytes 98312 | tf_op jit(solution)/shard_map/ppermute | solution.py:213

commit v16 on v15

v16 whole, which is shorter than its diff:
```python
import functools

import jax
import jax.numpy as jnp
from jax import lax
from jax.experimental import pallas as pl
from jax.experimental.pallas import tpu as pltpu
from jax.sharding import Mesh
from jax.sharding import PartitionSpec as P

NCR = 2
LANES = 128
EXTRA = 8
HOLD_FLOPS = 16 << 30
VMEM_LIMIT = 48 * 1024 * 1024


def halves(x):
    high = x.astype(jnp.bfloat16)
    return high, (x - high.astype(jnp.float32)).astype(jnp.bfloat16)


def transposed_product(left, right):
    tall = jnp.concatenate(halves(left), axis=0)
    wide = jnp.concatenate(halves(right), axis=1)
    wide = jnp.concatenate([wide, wide], axis=0)
    both = lax.dot_general(tall, wide, (((0,), (0,)), ((), ())), preferred_element_type=jnp.float32)
    width = right.shape[1]
    return both[:, :width] + both[:, width:]


def append_kernel(next_ref, far_columns_ref, own_columns_ref, blocks_ref, out_ref):
    used = blocks_ref.shape[0]
    entries, fine_rows = own_columns_ref.shape
    out_ref[:used] = blocks_ref[...]
    out_ref[used:] = jnp.zeros((EXTRA, out_ref.shape[1]), jnp.float32)
    out_ref[used : used + entries, :fine_rows] = far_columns_ref[...].astype(jnp.float32)
    out_ref[used + entries : used + 2 * entries, :fine_rows] = own_columns_ref[...].astype(jnp.float32)


def append_columns(next_blocks, far_columns, own_columns, blocks):
    used, width = blocks.shape
    return pl.pallas_call(
        append_kernel,
        out_shape=jax.ShapeDtypeStruct((used + EXTRA, width), blocks.dtype),
        in_specs=[pl.BlockSpec(memory_space=pltpu.VMEM)] * 4,
        out_specs=pl.BlockSpec(memory_space=pltpu.VMEM),
        compiler_params=pltpu.CompilerParams(vmem_limit_bytes=VMEM_LIMIT),
        cost_estimate=pl.CostEstimate(flops=HOLD_FLOPS, bytes_accessed=HOLD_FLOPS >> 8, transcendentals=0),
        name="append_columns",
    )(next_blocks, far_columns, own_columns, blocks)


def restrict_kernel(own_ref, *refs):
    count_any, slot_any, rows_any, fetch_any, restrict_any, operator_any, columns_any, blocks_any = refs[:8]
    own_columns_ref, own_blocks_any = refs[8:10]
    count_ref, slot_ref, rows_ref, fetch_ref, restrict_ref, operator_ref, blocks_ref, sums_ref = refs[-12:-4]
    sems, operator_sems, blocks_sem, out_sems = refs[-4:]
    outs = refs[10:-12]
    fine_rows, block_size, _ = operator_ref.shape
    entries = slot_ref.shape[1]
    slot_count, columns = fetch_ref.shape
    half = columns // 2
    used = 2 * slot_count * block_size
    wide = NCR * block_size
    own_near = own_ref[2]

    pairs = [
        (count_any, count_ref), (slot_any, slot_ref), (rows_any, rows_ref),
        (fetch_any, fetch_ref), (restrict_any, restrict_ref),
        (columns_any, own_columns_ref), (blocks_any, blocks_ref),
    ]
    copies = [pltpu.make_async_copy(a, b, sems.at[i]) for i, (a, b) in enumerate(pairs)]
    operators = [
        pltpu.make_async_copy(operator_any.at[i], operator_ref.at[i], operator_sems.at[i]) for i in range(fine_rows)
    ]
    for copy in copies + operators:
        copy.start()

    lane = lax.broadcasted_iota(jnp.int32, (block_size, wide), 1)
    second = (lane >= block_size).astype(jnp.int32)
    short_lane = lax.broadcasted_iota(jnp.int32, (EXTRA, wide), 1)
    for ahead in range(half):
        sums_ref[ahead, :used] = jnp.zeros((used, wide), jnp.float32)
    for copy in copies:
        copy.wait()
    pass_on = pltpu.make_async_copy(blocks_ref, own_blocks_any, blocks_sem)
    pass_on.start()

    for near in range(half):
        value = jnp.zeros((EXTRA, wide), jnp.int32)
        for side in range(2):
            for s in range(slot_count):
                wanted = fetch_ref[s, side * half + near]
                value = jnp.where(short_lane == side * slot_count + s, wanted, value)
        sums_ref[near ^ own_near, used:] = value.astype(jnp.float32)
    for copy in operators:
        copy.wait()

    for i in range(fine_rows):
        value = restrict_ref[i]
        swapped = pltpu.roll(value, block_size, 1)
        own_row = jnp.where(second == 0, rows_ref[0, i], rows_ref[1, i])
        other_row = jnp.where(second == 0, rows_ref[1, i], rows_ref[0, i])
        dense = jnp.where(own_row == second, value, 0.0) + jnp.where(other_row == second, swapped, 0.0)
        product = transposed_product(operator_ref[i], dense)
        for k in range(entries):
            part = jnp.where(k < count_ref[i], product[k * block_size : (k + 1) * block_size], 0.0)
            peer = lax.div(slot_ref[i, k], slot_count)
            place = lax.div(peer, half) * slot_count + lax.rem(slot_ref[i, k], slot_count)
            start = pl.multiple_of(place * block_size, block_size)
            sums_ref[lax.rem(peer, half) ^ own_near, pl.ds(start, block_size)] += part

    writes = [pltpu.make_async_copy(sums_ref.at[ahead], out, out_sems.at[ahead]) for ahead, out in enumerate(outs)]
    for copy in writes:
        copy.start()
    for copy in writes:
        copy.wait()
    pass_on.wait()


def restrict_operator(
    own, operator_count, operator_slot, restrict_rows, fetch, operator_blocks, restrict_blocks, own_columns, own_blocks
):
    fine_rows, block_size, width = operator_blocks.shape
    slot_count, columns = fetch.shape
    wide = NCR * block_size
    rows = 2 * slot_count * block_size + EXTRA
    small = (operator_count, operator_slot, restrict_rows, fetch)
    hbm = pl.BlockSpec(memory_space=pltpu.HBM)
    results = pl.pallas_call(
        restrict_kernel,
        out_shape=(
            jax.ShapeDtypeStruct(own_columns.shape, own_columns.dtype),
            jax.ShapeDtypeStruct(own_blocks.shape, own_blocks.dtype),
        )
        + (jax.ShapeDtypeStruct((rows, wide), jnp.float32),) * (columns // 2),
        in_specs=[pl.BlockSpec(memory_space=pltpu.SMEM)] + [hbm] * 8,
        out_specs=[pl.BlockSpec(memory_space=pltpu.VMEM)] + [hbm] * (1 + columns // 2),
        scratch_shapes=[pltpu.SMEM(x.shape, x.dtype) for x in small]
        + [pltpu.VMEM(x.shape, x.dtype) for x in (restrict_blocks, operator_blocks, own_blocks)]
        + [pltpu.VMEM((columns // 2, rows, wide), jnp.float32)]
        + [pltpu.SemaphoreType.DMA((7,)), pltpu.SemaphoreType.DMA((fine_rows,))]
        + [pltpu.SemaphoreType.DMA, pltpu.SemaphoreType.DMA((columns // 2,))],
        cost_estimate=pl.CostEstimate(
            flops=6 * fine_rows * block_size * width * wide, bytes_accessed=4 << 20, transcendentals=0
        ),
        name="restrict_operator",
    )(own, *small, restrict_blocks, operator_blocks, own_columns, own_blocks)
    return results[0], results[1], results[2:]


def index_kernel(*refs):
    out_ref = refs[-1]
    out_ref[...] = jnp.zeros_like(out_ref)
    for i, part in enumerate(refs[:-1]):
        out_ref[i : i + 1] = part[part.shape[0] - EXTRA : part.shape[0] - EXTRA + 1].astype(jnp.int32)


def index_table(parts):
    rows = -(-len(parts) // 8) * 8
    return pl.pallas_call(
        index_kernel,
        out_shape=jax.ShapeDtypeStruct((rows, LANES), jnp.int32),
        in_specs=[pl.BlockSpec(memory_space=pltpu.VMEM)] * len(parts),
        out_specs=pl.BlockSpec(memory_space=pltpu.VMEM),
        compiler_params=pltpu.CompilerParams(vmem_limit_bytes=VMEM_LIMIT),
        cost_estimate=pl.CostEstimate(flops=HOLD_FLOPS, bytes_accessed=HOLD_FLOPS >> 8, transcendentals=0),
        name="index_table",
    )(*parts)


def combine_kernel(own_ref, wanted_ref, *rest, half, split, slot_count, fine_rows, entries):
    parts, chunks = rest[:half], list(rest[half:-5])
    out_ref, held_ref, table_ref, index_ref, sem = rest[-5:]
    rows = len(split) // 2
    block_size = out_ref.shape[1]
    columns = 2 * half
    held = fine_rows * block_size
    pieces = [[chunks.pop(0) for _ in range(count)] for count in split]

    table_ref[:half] = wanted_ref[:half]
    for i, piece in enumerate(pieces[rows:]):
        last = piece[-1]
        for far in range(2):
            first = half + entries * (far * rows + i)
            row = last.shape[0] - EXTRA + entries * (1 - far)
            table_ref[first : first + entries] = last[row : row + entries].astype(jnp.int32)
    copy = pltpu.make_async_copy(table_ref, index_ref, sem)
    copy.start()
    for i, piece in enumerate(pieces):
        start = 0
        for chunk in piece:
            size = min(chunk.shape[0], held - start)
            held_ref[i, start : start + size] = chunk[:size]
            start += size
    out_ref[...] = jnp.zeros_like(out_ref)
    copy.wait()

    for ahead, part in enumerate(parts):

        def step(place, carry, ahead=ahead, part=part):
            wanted = index_ref[ahead, place]
            inside = lax.rem(wanted, fine_rows)
            far = lax.div(place, slot_count) ^ own_ref[1]
            piece = far * rows + (lax.div(wanted, fine_rows * columns) ^ own_ref[0])
            block = held_ref[piece, pl.ds(pl.multiple_of(inside * block_size, block_size), block_size)]
            restricted = part[pl.ds(pl.multiple_of(place * block_size, block_size), block_size)]
            product = transposed_product(block, restricted)
            for m in range(entries):
                column = own_ref[3 + index_ref[half + entries * piece + m, inside]]
                out_ref[column] += product[m * block_size : (m + 1) * block_size]
            return carry

        lax.fori_loop(0, 2 * slot_count, step, 0, unroll=half <= 4)


def combine(own, wanted, parts, pieces, coarse_all, slot_count, fine_rows, block_size):
    half = len(parts)
    wide = parts[0].shape[1]
    width = pieces[0][0].shape[1]
    entries = width // block_size
    split = tuple(len(piece) for piece in pieces)
    chunks = [chunk for piece in pieces for chunk in piece]
    table_rows = -(-(half + entries * len(pieces)) // 8) * 8
    return pl.pallas_call(
        functools.partial(
            combine_kernel, half=half, split=split, slot_count=slot_count, fine_rows=fine_rows, entries=entries
        ),
        out_shape=jax.ShapeDtypeStruct((coarse_all, block_size, wide), jnp.float32),
        in_specs=[pl.BlockSpec(memory_space=pltpu.SMEM)]
        + [pl.BlockSpec(memory_space=pltpu.VMEM)] * (1 + half + len(chunks)),
        out_specs=pl.BlockSpec(memory_space=pltpu.VMEM),
        scratch_shapes=[
            pltpu.VMEM((len(pieces), fine_rows * block_size, width), jnp.float32),
            pltpu.VMEM((table_rows, LANES), jnp.int32),
            pltpu.SMEM((table_rows, LANES), jnp.int32),
            pltpu.SemaphoreType.DMA,
        ],
        compiler_params=pltpu.CompilerParams(vmem_limit_bytes=VMEM_LIMIT),
        cost_estimate=pl.CostEstimate(flops=1 << 28, bytes_accessed=4 << 20, transcendentals=0),
        name="combine",
    )(own, wanted, *parts, *chunks)


def row_swap(x, bit):
    return lax.ppermute(x, "row", [(r, r ^ bit) for r in range(lax.axis_size("row"))])


def half_swap(x):
    return lax.ppermute(x, "half", [(0, 1), (1, 0)])


def spread_over_rows(blocks, rows, cut):
    pieces = {0: [blocks]}
    bit = rows // 2
    while bit:
        for mask in list(pieces):
            chunks = pieces[mask]
            if cut and bit == rows // 2:
                chunks = [blocks[:cut], blocks[cut:]]
            pieces[mask ^ bit] = [row_swap(chunk, bit) for chunk in chunks]
        bit //= 2
    return [pieces[mask] for mask in range(rows)]


def place_of_columns(half):
    own = lax.axis_index("half") * half + lax.axis_index("near")
    ahead = jnp.arange(2 * half, dtype=jnp.int32) ^ own
    return ahead % half * 2 + ahead // half


def add_over_columns(sums, half):
    total = sums[:2]
    for near in range(1, half):
        total = total + lax.ppermute(sums[2 * near : 2 * near + 2], "near", [(n, n ^ near) for n in range(half)])
    return total[0] + half_swap(total[1])


def local(
    operator_blocks,
    operator_count,
    operator_slot,
    fetch_lists,
    prolong_blocks,
    prolong_cols,
    restrict_blocks,
    restrict_rows,
):
    rows, half = lax.axis_size("row"), lax.axis_size("near")
    slot_count = fetch_lists.shape[3]
    fine_rows, block_size, width = prolong_blocks.shape
    fetch = fetch_lists.reshape(2 * half, slot_count).T
    own = jnp.stack([lax.axis_index("row"), lax.axis_index("half"), lax.axis_index("near")])
    own = jnp.concatenate([own, place_of_columns(half)])

    near_blocks = prolong_blocks.reshape(fine_rows * block_size, width)
    far_blocks = half_swap(near_blocks)
    own_columns, near_blocks, parts = restrict_operator(
        own,
        operator_count,
        operator_slot,
        restrict_rows.T,
        fetch,
        operator_blocks,
        restrict_blocks,
        prolong_cols.T,
        near_blocks,
    )
    parts = [parts[0]] + [
        lax.ppermute(parts[ahead], "near", [(n, n ^ ahead) for n in range(half)]) for ahead in range(1, half)
    ]
    wanted = index_table(parts)
    far_columns = half_swap(own_columns)
    near_pieces = spread_over_rows(near_blocks, rows, 0)
    far_blocks = append_columns(near_pieces[rows // 2][0], far_columns, own_columns, far_blocks)
    pieces = near_pieces + spread_over_rows(far_blocks, rows, fine_rows * block_size // 2)
    sums = combine(own, wanted, parts, pieces, NCR * rows, slot_count, fine_rows, block_size)
    return add_over_columns(sums, half).T


def solution(mesh):
    rows, columns = mesh.shape["row"], mesh.shape["col"]
    split = Mesh(mesh.devices.reshape(rows, 2, columns // 2), ("row", "half", "near"))
    flat = ("row", "half", "near")
    return jax.shard_map(
        local,
        mesh=split,
        in_specs=(
            P(flat, None, None),
            P(flat),
            P(flat, None),
            P("row", ("half", "near"), None, None),
            P(flat, None, None),
            P(flat, None),
            P(flat, None, None),
            P(flat, None),
        ),
        out_specs=P("row", ("half", "near")),
        check_vma=False,
    )
```

time: 42.8 us -> 50.1 us (1.17)
  waiting for transfers between devices: 17.2 us -> 20.9 us
  starting transfers between devices: 18.8 us -> 20.7 us
  Pallas kernels: 5.79 us -> 6.92 us
  other arithmetic: 0.73 us -> 1.27 us
    ppermute x3, waiting for transfers between devices: 4.94 us -> 10.6 us  [half_swap(): return lax.ppermute(x, 'half', [(0, 1), (1, 0)])]
    ppermute x6 -> x8, waiting for transfers between devices: 7.55 us -> 2.39 us  [row_swap(): lax.ppermute(x, 'row', [(r, r ^ bit) for r in range(lax.axis_size('row'))])]
    ppermute x0 -> x3, starting transfers between devices: none -> 4.58 us  [local(): lax.ppermute(parts[ahead], 'near', [(n, n ^ ahead) for n in range(half)])]
    ppermute x0 -> x3, waiting for transfers between devices: none -> 4.01 us  [local(): lax.ppermute(parts[ahead], 'near', [(n, n ^ ahead) for n in range(half)])]
    all_to_all x1 -> x0, starting transfers between devices: 3.9 us -> none  [local(): lax.all_to_all(restricted, 'near', split_axis=0, concat_axis=0, tiled=True)]
    ppermute x6 -> x8, starting transfers between devices: 3.74 us -> 6.2 us  [row_swap(): lax.ppermute(x, 'row', [(r, r ^ bit) for r in range(lax.axis_size('row'))])]
    all_to_all x1 -> x0, waiting for transfers between devices: 1.47 us -> none  [local(): lax.all_to_all(restricted, 'near', split_axis=0, concat_axis=0, tiled=True)]
    ppermute x3, starting transfers between devices: 7.56 us -> 6.37 us  [half_swap(): return lax.ppermute(x, 'half', [(0, 1), (1, 0)])]
  transfers between devices with their start and end apart: 13 -> 17, of which waited for: 8 -> 9; matrix products, arithmetic and copies ran while one was open for 0% -> 0% of each run, Pallas kernels for 8% -> 0%
where the time goes in v16:
time: 50.1 us; the launch traced here: 50 us
  waiting for transfers between devices  20.9 us (42%)
  starting transfers between devices  20.7 us (41%)
  Pallas kernels  6.92 us (14%)
  other arithmetic  1.27 us (3%)
    ppermute x3, waiting for transfers between devices, half_swap(): return lax.ppermute(x, 'half', [(0, 1), (1, 0)])  10.6 us
    ppermute x3, starting transfers between devices, half_swap(): return lax.ppermute(x, 'half', [(0, 1), (1, 0)])  6.37 us
    ppermute x8, starting transfers between devices, row_swap(): lax.ppermute(x, 'row', [(r, r ^ bit) for r in range(lax.axis_size('row'))])  6.2 us
    pallas_call x1, Pallas kernels, restrict_operator(): pl.pallas_call(restrict_kernel, out_shape=(jax.ShapeDtypeStruct(own_colum...  4.84 us
    ppermute x3, starting transfers between devices, local(): lax.ppermute(parts[ahead], 'near', [(n, n ^ ahead) for n in range(half)])  4.58 us
    ppermute x3, waiting for transfers between devices, local(): lax.ppermute(parts[ahead], 'near', [(n, n ^ ahead) for n in range(half)])  4.01 us
    ppermute x3, waiting for transfers between devices, add_over_columns(): lax.ppermute(sums[2 * near:2 * near + 2], 'near', [(n, n ^ near) for n in...  3.86 us
    ppermute x3, starting transfers between devices, add_over_columns(): lax.ppermute(sums[2 * near:2 * near + 2], 'near', [(n, n ^ near) for n in...  3.55 us
  transfers between devices with their start and end apart: 17, of which 9 were waited for; matrix products, arithmetic and copies ran while one was open for 0% of the time, Pallas kernels for 0%

profile of v16, /device:TPU:0, one launch (start us, length us, event | category | flops | bytes accessed | tf_op | source)
XLA Modules:
  0.0 50.0 jit_solution(704620712807438811)
XLA Ops:
  0.0 0.6 %pad_add_fusion.own_ref = s32[11]{0:T(128)} fusion(s32[8]{0:T(128)S(1)} %fusion.5, s32[1]{0:T(128)} %bitcast.2, s32[1]{0:T(128)} %bitcast.1, s32[1]{0:T(128)} %bitcast), kind=kLoop, calls=%fused_computation.14 | loop fusion | flops 33 | bytes 88 | tf_op jit(solution)/shard_map/concatenate | solution.py:295
  0.6 4.8 %restrict_operator.1 = (s32[2,8]{1,0:T(2,128)}, f32[512,128]{1,0:T(8,128)}, f32[520,128]{1,0:T(8,128)}, f32[520,128]{1,0:T(8,128)}, f32[520,128]{1,0:T(8,128)}, /*index=5*/f32[520,128]{1,0:T(8,128)}) custom-call(s32[11]{0:T(128)} %pad_add_fusion.own_ref, s32[8]{0:T(128)} %refs_0_.1, s32[8,8]{1,0:T(8,128)} %refs_1_.1, s32[2,8]{1,0:T(2,128)} %bitcast.22, ...), custom_call_target="tpu_custom_call" | custom-call | flops 201326592 | bytes 4194304 | tf_op jit(solution)/shard_map/restrict_operator/pallas_call | solution.py:131
  5.5 3.0 %collective-permute-start.4 = (f32[512,128]{1,0:T(8,128)}, f32[512,128]{1,0:T(8,128)S(1)}, u32[]{:S(2)}, u32[]{:S(2)}) collective-permute-start(f32[512,128]{1,0:T(8,128)} %get-tuple-element.15.rest_4_), channel_id=1, source_target_pairs={{0,16},{8,24},{16,0},{24,8},{1,17},{9,25},{17,1},{25,9},{2,18},{10... | collective-permute-start | bytes 786440 | tf_op jit(solution)/shard_map/ppermute | solution.py:247
  8.5 2.6 %collective-permute-start.7 = (f32[512,128]{1,0:T(8,128)S(1)}, f32[512,128]{1,0:T(8,128)S(1)}, u32[]{:S(2)}, u32[]{:S(2)}) collective-permute-start(f32[512,128]{1,0:T(8,128)S(1)} %bitcast.20), channel_id=1, source_target_pairs={{0,4},{4,0},{1,5},{5,1},{2,6},{6,2},{3,7},{7,3},{8,12},{12,8},{9,1... | collective-permute-start | bytes 786440 | tf_op jit(solution)/shard_map/ppermute | solution.py:251
  11.1 1.5 %collective-permute-start = (f32[520,128]{1,0:T(8,128)}, f32[520,128]{1,0:T(8,128)S(1)}, u32[]{:S(2)}, u32[]{:S(2)}) collective-permute-start(f32[520,128]{1,0:T(8,128)} %get-tuple-element.12), channel_id=1, source_target_pairs={{0,1},{1,0},{2,3},{3,2},{4,5},{5,4},{6,7},{7,6},{8,9},{9,8},{10,11... | collective-permute-start | bytes 798728 | tf_op jit(solution)/shard_map/ppermute | solution.py:311
  12.9 1.6 %collective-permute-start.1 = (f32[520,128]{1,0:T(8,128)}, f32[520,128]{1,0:T(8,128)S(1)}, u32[]{:S(2)}, u32[]{:S(2)}) collective-permute-start(f32[520,128]{1,0:T(8,128)} %get-tuple-element.13), channel_id=1, source_target_pairs={{0,2},{1,3},{2,0},{3,1},{4,6},{5,7},{6,4},{7,5},{8,10},{9,11},{10,... | collective-permute-start | bytes 798728 | tf_op jit(solution)/shard_map/ppermute | solution.py:311
  14.5 8.5 %collective-permute-done.6.far_columns_ref = s32[2,8]{1,0:T(2,128)S(1)} collective-permute-done((s32[2,8]{1,0:T(2,128)S(1)}, s32[2,8]{1,0:T(2,128)S(1)}, u32[]{:S(2)}, u32[]{:S(2)}) %collective-permute-start.6) | collective-permute-done | bytes 96 | tf_op jit(solution)/shard_map/ppermute | solution.py:251
  23.0 1.5 %collective-permute-start.2 = (f32[520,128]{1,0:T(8,128)}, f32[520,128]{1,0:T(8,128)S(1)}, u32[]{:S(2)}, u32[]{:S(2)}) collective-permute-start(f32[520,128]{1,0:T(8,128)} %get-tuple-element.14), channel_id=1, source_target_pairs={{0,3},{1,2},{2,1},{3,0},{4,7},{5,6},{6,5},{7,4},{8,11},{9,10},{10,... | collective-permute-start | bytes 798728 | tf_op jit(solution)/shard_map/ppermute | solution.py:311
  24.6 0.6 %collective-permute-start.10 = (f32[264,128]{1,0:T(8,128)S(1)}, f32[264,128]{1,0:T(8,128)S(1)}, u32[]{:S(2)}, u32[]{:S(2)}) collective-permute-start(f32[264,128]{1,0:T(8,128)S(1)} %slice.33), channel_id=1, source_target_pairs={{0,16},{8,24},{16,0},{24,8},{1,17},{9,25},{17,1},{25,9},{2,18},{10... | collective-permute-start | bytes 405512 | tf_op jit(solution)/shard_map/ppermute | solution.py:247
  25.2 1.6 %collective-permute-start.9 = (f32[256,128]{1,0:T(8,128)S(1)}, f32[256,128]{1,0:T(8,128)S(1)}, u32[]{:S(2)}, u32[]{:S(2)}) collective-permute-start(f32[256,128]{1,0:T(8,128)S(1)} %slice.32), channel_id=1, source_target_pairs={{0,16},{8,24},{16,0},{24,8},{1,17},{9,25},{17,1},{25,9},{2,18},{10... | collective-permute-start | bytes 393224 | tf_op jit(solution)/shard_map/ppermute | solution.py:247
  27.3 4.0 %collective-permute-done.2.refs_3_.rest_3_ = f32[520,128]{1,0:T(8,128)S(1)} collective-permute-done((f32[520,128]{1,0:T(8,128)}, f32[520,128]{1,0:T(8,128)S(1)}, u32[]{:S(2)}, u32[]{:S(2)}) %collective-permute-start.2) | collective-permute-done | bytes 266272 | tf_op jit(solution)/shard_map/ppermute | solution.py:311
  31.3 1.4 %collective-permute-done.9.rest_10_ = f32[256,128]{1,0:T(8,128)S(1)} collective-permute-done((f32[256,128]{1,0:T(8,128)S(1)}, f32[256,128]{1,0:T(8,128)S(1)}, u32[]{:S(2)}, u32[]{:S(2)}) %collective-permute-start.9) | collective-permute-done | bytes 131104 | tf_op jit(solution)/shard_map/ppermute | solution.py:247
  32.7 0.5 %collective-permute-start.12 = (f32[264,128]{1,0:T(8,128)S(1)}, f32[264,128]{1,0:T(8,128)S(1)}, u32[]{:S(2)}, u32[]{:S(2)}) collective-permute-start(f32[264,128]{1,0:T(8,128)S(1)} %collective-permute-done.10.rest_11_), channel_id=1, source_target_pairs={{0,8},{8,0},{16,24},{24,16},{1,9},{9,1},{17,25},{25,17},{2,10},{10... | collective-permute-start | bytes 405512 | tf_op jit(solution)/shard_map/ppermute | solution.py:247
  33.2 0.8 %collective-permute-done.11.rest_12_ = f32[256,128]{1,0:T(8,128)S(1)} collective-permute-done((f32[256,128]{1,0:T(8,128)S(1)}, f32[256,128]{1,0:T(8,128)S(1)}, u32[]{:S(2)}, u32[]{:S(2)}) %collective-permute-start.11) | collective-permute-done | bytes 131104 | tf_op jit(solution)/shard_map/ppermute | solution.py:247
  34.2 2.1 %combine.1 = f32[8,64,128]{2,1,0:T(8,128)S(1)} custom-call(s32[11]{0:T(128)S(1)} %copy-done.2, s32[8,128]{1,0:T(8,128)S(1)} %index_table.1.wanted_ref, f32[520,128]{1,0:T(8,128)S(1)} %copy-done, f32[520,128]{1,0:T(8,128)S(1)} %collective-permute-done.refs_1_.rest_1_, f32[520,128]{1,0:T(8,128)S(1)} %collective-permute-done.1.refs_2_.rest_2_, ...), custom_call_target="tpu_custom_call" | custom-call | flops 268435456 | bytes 4194304 | tf_op jit(solution)/shard_map/combine/pallas_call | solution.py:226
  36.3 0.6 %collective-permute-start.13 = (f32[2,64,128]{2,1,0:T(8,128)S(1)}, f32[2,64,128]{2,1,0:T(8,128)S(1)}, u32[]{:S(2)}, u32[]{:S(2)}) collective-permute-start(f32[2,64,128]{2,1,0:T(8,128)S(1)} %get-tuple-element.17), channel_id=1, source_target_pairs={{0,1},{1,0},{2,3},{3,2},{4,5},{5,4},{6,7},{7,6},{8,9},{9,8},{10,11... | collective-permute-start | bytes 196616 | tf_op jit(solution)/shard_map/ppermute | solution.py:276
  36.9 1.6 %collective-permute-start.14 = (f32[2,64,128]{2,1,0:T(8,128)S(1)}, f32[2,64,128]{2,1,0:T(8,128)S(1)}, u32[]{:S(2)}, u32[]{:S(2)}) collective-permute-start(f32[2,64,128]{2,1,0:T(8,128)S(1)} %get-tuple-element.19), channel_id=1, source_target_pairs={{0,2},{1,3},{2,0},{3,1},{4,6},{5,7},{6,4},{7,5},{8,10},{9,11},{10,... | collective-permute-start | bytes 196616 | tf_op jit(solution)/shard_map/ppermute | solution.py:276
  38.6 1.3 %collective-permute-start.15 = (f32[2,64,128]{2,1,0:T(8,128)S(1)}, f32[2,64,128]{2,1,0:T(8,128)S(1)}, u32[]{:S(2)}, u32[]{:S(2)}) collective-permute-start(f32[2,64,128]{2,1,0:T(8,128)S(1)} %get-tuple-element.18), channel_id=1, source_target_pairs={{0,3},{1,2},{2,1},{3,0},{4,7},{5,6},{6,5},{7,4},{8,11},{9,10},{10,... | collective-permute-start | bytes 196616 | tf_op jit(solution)/shard_map/ppermute | solution.py:276
  39.9 0.8 %collective-permute-done.13 = f32[2,64,128]{2,1,0:T(8,128)S(1)} collective-permute-done((f32[2,64,128]{2,1,0:T(8,128)S(1)}, f32[2,64,128]{2,1,0:T(8,128)S(1)}, u32[]{:S(2)}, u32[]{:S(2)}) %collective-permute-start.13) | collective-permute-done | bytes 65568 | tf_op jit(solution)/shard_map/ppermute | solution.py:276
  40.7 0.9 %collective-permute-done.14 = f32[2,64,128]{2,1,0:T(8,128)S(1)} collective-permute-done((f32[2,64,128]{2,1,0:T(8,128)S(1)}, f32[2,64,128]{2,1,0:T(8,128)S(1)}, u32[]{:S(2)}, u32[]{:S(2)}) %collective-permute-start.14) | collective-permute-done | bytes 65568 | tf_op jit(solution)/shard_map/ppermute | solution.py:276
  41.6 2.1 %collective-permute-done.15 = f32[2,64,128]{2,1,0:T(8,128)S(1)} collective-permute-done((f32[2,64,128]{2,1,0:T(8,128)S(1)}, f32[2,64,128]{2,1,0:T(8,128)S(1)}, u32[]{:S(2)}, u32[]{:S(2)}) %collective-permute-start.15) | collective-permute-done | bytes 65568 | tf_op jit(solution)/shard_map/ppermute | solution.py:276
  43.8 3.4 %collective-permute-start.16 = (f32[64,128]{1,0:T(8,128)S(1)}, f32[64,128]{1,0:T(8,128)S(1)}, u32[]{:S(2)}, u32[]{:S(2)}) collective-permute-start(f32[64,128]{1,0:T(8,128)S(1)} %slice_bitcast_fusion), channel_id=1, source_target_pairs={{0,4},{4,0},{1,5},{5,1},{2,6},{6,2},{3,7},{7,3},{8,12},{12,8},{9,1... | collective-permute-start | bytes 98312 | tf_op jit(solution)/shard_map/ppermute | solution.py:251
  47.2 2.2 %collective-permute-done.16 = f32[64,128]{1,0:T(8,128)S(1)} collective-permute-done((f32[64,128]{1,0:T(8,128)S(1)}, f32[64,128]{1,0:T(8,128)S(1)}, u32[]{:S(2)}, u32[]{:S(2)}) %collective-permute-start.16) | collective-permute-done | bytes 32800 | tf_op jit(solution)/shard_map/ppermute | solution.py:251
  49.4 0.6 %fusion.3 = f32[128,64]{0,1:T(8,128)} fusion(f32[64,128]{1,0:T(8,128)S(1)} %collective-permute-done.16, f32[2,64,128]{2,1,0:T(8,128)S(1)} %fusion.1), kind=kLoop, calls=%fused_computation.6 | loop fusion | flops 8192 | bytes 98304 | tf_op jit(solution)/shard_map/transpose | solution.py:319
  (32 shorter events, 1.2 us)
Async XLA Ops:
  0.6 7.9 %copy-start.4 = (f32[8,64,128]{2,1,0:T(8,128)S(1)}, f32[8,64,128]{2,1,0:T(8,128)}, u32[]{:S(2)}) copy-start(f32[8,64,128]{2,1,0:T(8,128)} %param.12) | copy-start | bytes 786436
  5.5 19.0 %collective-permute-start.4 = (f32[512,128]{1,0:T(8,128)}, f32[512,128]{1,0:T(8,128)S(1)}, u32[]{:S(2)}, u32[]{:S(2)}) collective-permute-start(f32[512,128]{1,0:T(8,128)} %get-tuple-element.15.rest_4_), channel_id=1, source_target_pairs={{0,16},{8,24},{16,0},{24,8},{1,17},{9,25},{17,1},{25,9},{2,18},{10... | collective-permute-start | bytes 786440 | tf_op jit(solution)/shard_map/ppermute | solution.py:247
  8.5 16.0 %collective-permute-start.7 = (f32[512,128]{1,0:T(8,128)S(1)}, f32[512,128]{1,0:T(8,128)S(1)}, u32[]{:S(2)}, u32[]{:S(2)}) collective-permute-start(f32[512,128]{1,0:T(8,128)S(1)} %bitcast.20), channel_id=1, source_target_pairs={{0,4},{4,0},{1,5},{5,1},{2,6},{6,2},{3,7},{7,3},{8,12},{12,8},{9,1... | collective-permute-start | bytes 786440 | tf_op jit(solution)/shard_map/ppermute | solution.py:251
  11.1 1.5 %copy-start.3 = (s32[2,8]{1,0:T(2,128)S(1)}, s32[2,8]{1,0:T(2,128)}, u32[]{:S(2)}) copy-start(s32[2,8]{1,0:T(2,128)} %get-tuple-element.16.own_columns_ref) | copy-start | bytes 196
  11.1 15.6 %collective-permute-start = (f32[520,128]{1,0:T(8,128)}, f32[520,128]{1,0:T(8,128)S(1)}, u32[]{:S(2)}, u32[]{:S(2)}) collective-permute-start(f32[520,128]{1,0:T(8,128)} %get-tuple-element.12), channel_id=1, source_target_pairs={{0,1},{1,0},{2,3},{3,2},{4,5},{5,4},{6,7},{7,6},{8,9},{9,8},{10,11... | collective-permute-start | bytes 798728 | tf_op jit(solution)/shard_map/ppermute | solution.py:311
  12.6 10.4 %collective-permute-start.6 = (s32[2,8]{1,0:T(2,128)S(1)}, s32[2,8]{1,0:T(2,128)S(1)}, u32[]{:S(2)}, u32[]{:S(2)}) collective-permute-start(s32[2,8]{1,0:T(2,128)S(1)} %copy-done.3), channel_id=1, source_target_pairs={{0,4},{4,0},{1,5},{5,1},{2,6},{6,2},{3,7},{7,3},{8,12},{12,8},{9,1... | collective-permute-start | bytes 200 | tf_op jit(solution)/shard_map/ppermute | solution.py:251
  12.9 13.8 %collective-permute-start.1 = (f32[520,128]{1,0:T(8,128)}, f32[520,128]{1,0:T(8,128)S(1)}, u32[]{:S(2)}, u32[]{:S(2)}) collective-permute-start(f32[520,128]{1,0:T(8,128)} %get-tuple-element.13), channel_id=1, source_target_pairs={{0,2},{1,3},{2,0},{3,1},{4,6},{5,7},{6,4},{7,5},{8,10},{9,11},{10,... | collective-permute-start | bytes 798728 | tf_op jit(solution)/shard_map/ppermute | solution.py:311
  23.0 8.3 %collective-permute-start.2 = (f32[520,128]{1,0:T(8,128)}, f32[520,128]{1,0:T(8,128)S(1)}, u32[]{:S(2)}, u32[]{:S(2)}) collective-permute-start(f32[520,128]{1,0:T(8,128)} %get-tuple-element.14), channel_id=1, source_target_pairs={{0,3},{1,2},{2,1},{3,0},{4,7},{5,6},{6,5},{7,4},{8,11},{9,10},{10,... | collective-permute-start | bytes 798728 | tf_op jit(solution)/shard_map/ppermute | solution.py:311
  24.5 2.2 %copy-start.1 = (f32[512,128]{1,0:T(8,128)S(1)}, f32[512,128]{1,0:T(8,128)}, u32[]{:S(2)}) copy-start(f32[512,128]{1,0:T(8,128)} %get-tuple-element.15.rest_4_) | copy-start | bytes 786436
  24.6 8.6 %copy-start = (f32[520,128]{1,0:T(8,128)S(1)}, f32[520,128]{1,0:T(8,128)}, u32[]{:S(2)}) copy-start(f32[520,128]{1,0:T(8,128)} %get-tuple-element.11.refs_0_.rest_0_) | copy-start | bytes 798724
  24.6 8.1 %collective-permute-start.10 = (f32[264,128]{1,0:T(8,128)S(1)}, f32[264,128]{1,0:T(8,128)S(1)}, u32[]{:S(2)}, u32[]{:S(2)}) collective-permute-start(f32[264,128]{1,0:T(8,128)S(1)} %slice.33), channel_id=1, source_target_pairs={{0,16},{8,24},{16,0},{24,8},{1,17},{9,25},{17,1},{25,9},{2,18},{10... | collective-permute-start | bytes 405512 | tf_op jit(solution)/shard_map/ppermute | solution.py:247
  25.2 7.5 %collective-permute-start.9 = (f32[256,128]{1,0:T(8,128)S(1)}, f32[256,128]{1,0:T(8,128)S(1)}, u32[]{:S(2)}, u32[]{:S(2)}) collective-permute-start(f32[256,128]{1,0:T(8,128)S(1)} %slice.32), channel_id=1, source_target_pairs={{0,16},{8,24},{16,0},{24,8},{1,17},{9,25},{17,1},{25,9},{2,18},{10... | collective-permute-start | bytes 393224 | tf_op jit(solution)/shard_map/ppermute | solution.py:247
  26.8 6.4 %collective-permute-start.3 = (f32[512,128]{1,0:T(8,128)S(1)}, f32[512,128]{1,0:T(8,128)S(1)}, u32[]{:S(2)}, u32[]{:S(2)}) collective-permute-start(f32[512,128]{1,0:T(8,128)S(1)} %copy-done.1), channel_id=1, source_target_pairs={{0,8},{8,0},{16,24},{24,16},{1,9},{9,1},{17,25},{25,17},{2,10},{10... | collective-permute-start | bytes 786440 | tf_op jit(solution)/shard_map/ppermute | solution.py:247
  26.8 7.2 %collective-permute-start.8 = (f32[520,128]{1,0:T(8,128)S(1)}, f32[520,128]{1,0:T(8,128)S(1)}, u32[]{:S(2)}, u32[]{:S(2)}) collective-permute-start(f32[520,128]{1,0:T(8,128)S(1)} %append_columns.1.rest_8_), channel_id=1, source_target_pairs={{0,8},{8,0},{16,24},{24,16},{1,9},{9,1},{17,25},{25,17},{2,10},{10... | collective-permute-start | bytes 798728 | tf_op jit(solution)/shard_map/ppermute | solution.py:247
  31.3 2.7 %collective-permute-start.5 = (f32[512,128]{1,0:T(8,128)S(1)}, f32[512,128]{1,0:T(8,128)S(1)}, u32[]{:S(2)}, u32[]{:S(2)}) collective-permute-start(f32[512,128]{1,0:T(8,128)S(1)} %collective-permute-done.4.next_ref.rest_6_), channel_id=1, source_target_pairs={{0,8},{8,0},{16,24},{24,16},{1,9},{9,1},{17,25},{25,17},{2,10},{10... | collective-permute-start | bytes 786440 | tf_op jit(solution)/shard_map/ppermute | solution.py:247
  32.7 1.3 %collective-permute-start.11 = (f32[256,128]{1,0:T(8,128)S(1)}, f32[256,128]{1,0:T(8,128)S(1)}, u32[]{:S(2)}, u32[]{:S(2)}) collective-permute-start(f32[256,128]{1,0:T(8,128)S(1)} %collective-permute-done.9.rest_10_), channel_id=1, source_target_pairs={{0,8},{8,0},{16,24},{24,16},{1,9},{9,1},{17,25},{25,17},{2,10},{10... | collective-permute-start | bytes 393224 | tf_op jit(solution)/shard_map/ppermute | solution.py:247
  32.7 1.5 %collective-permute-start.12 = (f32[264,128]{1,0:T(8,128)S(1)}, f32[264,128]{1,0:T(8,128)S(1)}, u32[]{:S(2)}, u32[]{:S(2)}) collective-permute-start(f32[264,128]{1,0:T(8,128)S(1)} %collective-permute-done.10.rest_11_), channel_id=1, source_target_pairs={{0,8},{8,0},{16,24},{24,16},{1,9},{9,1},{17,25},{25,17},{2,10},{10... | collective-permute-start | bytes 405512 | tf_op jit(solution)/shard_map/ppermute | solution.py:247
  33.2 1.0 %copy-start.2 = (s32[11]{0:T(128)S(1)}, s32[11]{0:T(128)}, u32[]{:S(2)}) copy-start(s32[11]{0:T(128)} %pad_add_fusion.own_ref) | copy-start | bytes 136
  36.3 4.4 %collective-permute-start.13 = (f32[2,64,128]{2,1,0:T(8,128)S(1)}, f32[2,64,128]{2,1,0:T(8,128)S(1)}, u32[]{:S(2)}, u32[]{:S(2)}) collective-permute-start(f32[2,64,128]{2,1,0:T(8,128)S(1)} %get-tuple-element.17), channel_id=1, source_target_pairs={{0,1},{1,0},{2,3},{3,2},{4,5},{5,4},{6,7},{7,6},{8,9},{9,8},{10,11... | collective-permute-start | bytes 196616 | tf_op jit(solution)/shard_map/ppermute | solution.py:276
  36.9 4.7 %collective-permute-start.14 = (f32[2,64,128]{2,1,0:T(8,128)S(1)}, f32[2,64,128]{2,1,0:T(8,128)S(1)}, u32[]{:S(2)}, u32[]{:S(2)}) collective-permute-start(f32[2,64,128]{2,1,0:T(8,128)S(1)} %get-tuple-element.19), channel_id=1, source_target_pairs={{0,2},{1,3},{2,0},{3,1},{4,6},{5,7},{6,4},{7,5},{8,10},{9,11},{10,... | collective-permute-start | bytes 196616 | tf_op jit(solution)/shard_map/ppermute | solution.py:276
  38.6 5.2 %collective-permute-start.15 = (f32[2,64,128]{2,1,0:T(8,128)S(1)}, f32[2,64,128]{2,1,0:T(8,128)S(1)}, u32[]{:S(2)}, u32[]{:S(2)}) collective-permute-start(f32[2,64,128]{2,1,0:T(8,128)S(1)} %get-tuple-element.18), channel_id=1, source_target_pairs={{0,3},{1,2},{2,1},{3,0},{4,7},{5,6},{6,5},{7,4},{8,11},{9,10},{10,... | collective-permute-start | bytes 196616 | tf_op jit(solution)/shard_map/ppermute | solution.py:276
  43.8 5.6 %collective-permute-start.16 = (f32[64,128]{1,0:T(8,128)S(1)}, f32[64,128]{1,0:T(8,128)S(1)}, u32[]{:S(2)}, u32[]{:S(2)}) collective-permute-start(f32[64,128]{1,0:T(8,128)S(1)} %slice_bitcast_fusion), channel_id=1, source_target_pairs={{0,4},{4,0},{1,5},{5,1},{2,6},{6,2},{3,7},{7,3},{8,12},{12,8},{9,1... | collective-permute-start | bytes 98312 | tf_op jit(solution)/shard_map/ppermute | solution.py:251

commit v17 on v15

--- a/solution.py
+++ b/solution.py
@@ -29,7 +29,23 @@
     return both[:, :width] + both[:, width:]
 
 
-def append_kernel(next_ref, far_columns_ref, own_columns_ref, blocks_ref, out_ref):
+def hold_kernel(mark_ref, blocks_ref, out_ref):
+    out_ref[...] = blocks_ref[...]
+
+
+def hold_until(mark, blocks):
+    return pl.pallas_call(
+        hold_kernel,
+        out_shape=jax.ShapeDtypeStruct(blocks.shape, blocks.dtype),
+        in_specs=[pl.BlockSpec(memory_space=pltpu.VMEM)] * 2,
+        out_specs=pl.BlockSpec(memory_space=pltpu.VMEM),
+        compiler_params=pltpu.CompilerParams(vmem_limit_bytes=VMEM_LIMIT),
+        cost_estimate=pl.CostEstimate(flops=HOLD_FLOPS, bytes_accessed=HOLD_FLOPS >> 8, transcendentals=0),
+        name="hold_until",
+    )(mark, blocks)
+
+
+def append_kernel(far_columns_ref, own_columns_ref, next_ref, blocks_ref, out_ref):
     used = blocks_ref.shape[0]
     entries, fine_rows = own_columns_ref.shape
     out_ref[:used] = blocks_ref[...]
@@ -38,7 +54,7 @@
     out_ref[used + entries : used + 2 * entries, :fine_rows] = own_columns_ref[...].astype(jnp.float32)
 
 
-def append_columns(next_blocks, far_columns, own_columns, blocks):
+def append_columns(far_columns, own_columns, next_blocks, blocks):
     used, width = blocks.shape
     return pl.pallas_call(
         append_kernel,
@@ -46,14 +62,14 @@
         in_specs=[pl.BlockSpec(memory_space=pltpu.VMEM)] * 4,
         out_specs=pl.BlockSpec(memory_space=pltpu.VMEM),
         compiler_params=pltpu.CompilerParams(vmem_limit_bytes=VMEM_LIMIT),
-        cost_estimate=pl.CostEstimate(flops=HOLD_FLOPS, bytes_accessed=HOLD_FLOPS >> 8, transcendentals=0),
+        cost_estimate=pl.CostEstimate(flops=0, bytes_accessed=1 << 19, transcendentals=0),
         name="append_columns",
-    )(next_blocks, far_columns, own_columns, blocks)
+    )(far_columns, own_columns, next_blocks, blocks)
 
 
 def restrict_kernel(
-    count_any, slot_any, rows_any, fetch_any, restrict_any, operator_any, columns_any, blocks_any,
-    out_ref, own_columns_ref, own_blocks_ref,
+    count_any, slot_any, rows_any, fetch_any, restrict_any, operator_any, columns_any,
+    out_ref, own_columns_ref,
     count_ref, slot_ref, rows_ref, fetch_ref, restrict_ref, operator_ref, sems, operator_sems,
 ):
     fine_rows, block_size, _ = operator_ref.shape
@@ -66,7 +82,7 @@
     pairs = [
         (count_any, count_ref), (slot_any, slot_ref), (rows_any, rows_ref),
         (fetch_any, fetch_ref), (restrict_any, restrict_ref),
-        (columns_any, own_columns_ref), (blocks_any, own_blocks_ref),
+        (columns_any, own_columns_ref),
     ]
     copies = [pltpu.make_async_copy(a, b, sems.at[i]) for i, (a, b) in enumerate(pairs)]
     operators = [
@@ -107,7 +123,7 @@
 
 
 def restrict_operator(
-    operator_count, operator_slot, restrict_rows, fetch, operator_blocks, restrict_blocks, own_columns, own_blocks
+    operator_count, operator_slot, restrict_rows, fetch, operator_blocks, restrict_blocks, own_columns
 ):
     fine_rows, block_size, width = operator_blocks.shape
     slot_count, columns = fetch.shape
@@ -119,23 +135,21 @@
         out_shape=(
             jax.ShapeDtypeStruct((columns // 2, rows, wide), jnp.float32),
             jax.ShapeDtypeStruct(own_columns.shape, own_columns.dtype),
-            jax.ShapeDtypeStruct(own_blocks.shape, own_blocks.dtype),
         ),
-        in_specs=[pl.BlockSpec(memory_space=pltpu.HBM)] * 8,
-        out_specs=[pl.BlockSpec(memory_space=pltpu.VMEM)] * 3,
+        in_specs=[pl.BlockSpec(memory_space=pltpu.HBM)] * 7,
+        out_specs=[pl.BlockSpec(memory_space=pltpu.VMEM)] * 2,
         scratch_shapes=[pltpu.SMEM(x.shape, x.dtype) for x in small]
         + [pltpu.VMEM(x.shape, x.dtype) for x in (restrict_blocks, operator_blocks)]
-        + [pltpu.SemaphoreType.DMA((7,)), pltpu.SemaphoreType.DMA((fine_rows,))],
+        + [pltpu.SemaphoreType.DMA((6,)), pltpu.SemaphoreType.DMA((fine_rows,))],
         cost_estimate=pl.CostEstimate(
             flops=6 * fine_rows * block_size * width * wide, bytes_accessed=4 << 20, transcendentals=0
         ),
         name="restrict_operator",
-    )(*small, restrict_blocks, operator_blocks, own_columns, own_blocks)
+    )(*small, restrict_blocks, operator_blocks, own_columns)
 
 
 def combine_kernel(own_ref, restricted_ref, *rest, slot_count, fine_rows, entries):
-    pieces, (out_ref, held_ref, table_ref, index_ref, sem) = rest[:-9], rest[-9:-4]
-    sums = rest[-4:]
+    pieces, (out_ref, held_ref, table_ref, index_ref, sem) = rest[:-5], rest[-5:]
     half = restricted_ref.shape[0]
     rows = len(pieces) // 2
     block_size = out_ref.shape[1]
@@ -154,11 +168,10 @@
     copy.start()
     for i, piece in enumerate(pieces):
         held_ref[i] = piece[...] if i < rows else piece[:held]
-    for total in sums:
-        total[...] = jnp.zeros_like(total)
+    out_ref[...] = jnp.zeros_like(out_ref)
     copy.wait()
 
-    def add_product(i, total):
+    def step(i, carry):
         near = lax.div(i, 2 * slot_count)
         place = lax.rem(i, 2 * slot_count)
         wanted = index_ref[near, place]
@@ -170,15 +183,10 @@
         product = transposed_product(block, restricted)
         for m in range(entries):
             column = own_ref[2 + index_ref[half + entries * piece + m, inside]]
-            total[m % len(total)][column] += product[m * block_size : (m + 1) * block_size]
-
-    def step(i, carry):
-        add_product(2 * i, sums[:2])
-        add_product(2 * i + 1, sums[2:])
+            out_ref[column] += product[m * block_size : (m + 1) * block_size]
         return carry
 
-    lax.fori_loop(0, half * slot_count, step, 0, unroll=8)
-    out_ref[...] = (sums[0][...] + sums[1][...]) + (sums[2][...] + sums[3][...])
+    lax.fori_loop(0, half * 2 * slot_count, step, 0, unroll=16)
 
 
 def combine(own, restricted, pieces, coarse_all, slot_count, fine_rows, block_size):
@@ -197,8 +205,7 @@
             pltpu.VMEM((table_rows, LANES), jnp.int32),
             pltpu.SMEM((table_rows, LANES), jnp.int32),
             pltpu.SemaphoreType.DMA,
-        ]
-        + [pltpu.VMEM((coarse_all, block_size, wide), jnp.float32)] * 4,
+        ],
         compiler_params=pltpu.CompilerParams(vmem_limit_bytes=VMEM_LIMIT),
         cost_estimate=pl.CostEstimate(flops=1 << 28, bytes_accessed=4 << 20, transcendentals=0),
         name="combine",
@@ -255,7 +262,7 @@
 
     near_blocks = prolong_blocks.reshape(fine_rows * block_size, width)
     far_blocks = half_swap(near_blocks)
-    restricted, own_columns, near_blocks = restrict_operator(
+    restricted, own_columns = restrict_operator(
         operator_count,
         operator_slot,
         restrict_rows.T,
@@ -263,12 +270,12 @@
         operator_blocks,
         restrict_blocks,
         prolong_cols.T,
-        near_blocks,
     )
     restricted = lax.all_to_all(restricted, "near", split_axis=0, concat_axis=0, tiled=True)
     far_columns = half_swap(own_columns)
     near_pieces = spread_over_rows(near_blocks, rows)
-    far_blocks = append_columns(near_pieces[rows // 2], far_columns, own_columns, far_blocks)
+    far_blocks = hold_until(far_columns, far_blocks)
+    far_blocks = append_columns(far_columns, own_columns, near_pieces[rows // 2], far_blocks)
     pieces = near_pieces + spread_over_rows(far_blocks, rows)
     sums = combine(own, restricted, pieces, NCR * rows, slot_count, fine_rows, block_size)
     return add_over_columns(sums, half).T

time: 42.8 us -> 43.1 us (level)
  waiting for transfers between devices: 17.2 us -> 18.8 us
  starting transfers between devices: 18.8 us -> 17.5 us
    ppermute x3, waiting for transfers between devices: 4.94 us -> 6.07 us  [half_swap(): return lax.ppermute(x, 'half', [(0, 1), (1, 0)])]
    ppermute x3, starting transfers between devices: 7.56 us -> 6.54 us  [half_swap(): return lax.ppermute(x, 'half', [(0, 1), (1, 0)])]
    ppermute x3, waiting for transfers between devices: 3.22 us -> 3.79 us  [add_over_columns(): lax.ppermute(sums[2 * near:2 * near + 2], 'near', [(n, n ^ near) for n in...]
  transfers between devices with their start and end apart: 13 -> 13, of which waited for: 8 -> 9; matrix products, arithmetic and copies ran while one was open for 0% -> 0% of each run, Pallas kernels for 8% -> 8%
where the time goes in v17:
time: 43.1 us; the launch traced here: 42.9 us
  waiting for transfers between devices  18.8 us (44%)
  starting transfers between devices  17.5 us (41%)
  Pallas kernels  5.63 us (13%)
  other arithmetic  0.73 us (2%)
    ppermute x6, waiting for transfers between devices, row_swap(): lax.ppermute(x, 'row', [(r, r ^ bit) for r in range(lax.axis_size('row'))])  7.56 us
    ppermute x3, starting transfers between devices, half_swap(): return lax.ppermute(x, 'half', [(0, 1), (1, 0)])  6.54 us
    ppermute x3, waiting for transfers between devices, half_swap(): return lax.ppermute(x, 'half', [(0, 1), (1, 0)])  6.07 us
    ppermute x3, waiting for transfers between devices, add_over_columns(): lax.ppermute(sums[2 * near:2 * near + 2], 'near', [(n, n ^ near) for n in...  3.79 us
    all_to_all x1, starting transfers between devices, local(): lax.all_to_all(restricted, 'near', split_axis=0, concat_axis=0, tiled=True)  3.77 us
    ppermute x6, starting transfers between devices, row_swap(): lax.ppermute(x, 'row', [(r, r ^ bit) for r in range(lax.axis_size('row'))])  3.67 us
    ppermute x3, starting transfers between devices, add_over_columns(): lax.ppermute(sums[2 * near:2 * near + 2], 'near', [(n, n ^ near) for n in...  3.55 us
    pallas_call x1, Pallas kernels, restrict_operator(): pl.pallas_call(restrict_kernel, out_shape=(jax.ShapeDtypeStruct((columns...  3.3 us
  transfers between devices with their start and end apart: 13, of which 9 were waited for; matrix products, arithmetic and copies ran while one was open for 0% of the time, Pallas kernels for 8%

profile of v17, /device:TPU:0, one launch (start us, length us, event | category | flops | bytes accessed | tf_op | source)
XLA Modules:
  0.0 42.9 jit_solution(4782319432538197323)
XLA Ops:
  0.0 4.0 %collective-permute-start.4 = (f32[512,128]{1,0:T(8,128)}, f32[512,128]{1,0:T(8,128)S(1)}, u32[]{:S(2)}, u32[]{:S(2)}) collective-permute-start(f32[512,128]{1,0:T(8,128)} %bitcast.18), channel_id=1, source_target_pairs={{0,4},{4,0},{1,5},{5,1},{2,6},{6,2},{3,7},{7,3},{8,12},{12,8},{9,1... | collective-permute-start | bytes 786440 | tf_op jit(solution)/shard_map/ppermute | solution.py:220
  4.0 1.5 %collective-permute-start.1 = (f32[512,128]{1,0:T(8,128)}, f32[512,128]{1,0:T(8,128)S(1)}, u32[]{:S(2)}, u32[]{:S(2)}) collective-permute-start(f32[512,128]{1,0:T(8,128)} %bitcast.19), channel_id=1, source_target_pairs={{0,16},{8,24},{16,0},{24,8},{1,17},{9,25},{17,1},{25,9},{2,18},{10... | collective-permute-start | bytes 786440 | tf_op jit(solution)/shard_map/ppermute | solution.py:216
  5.6 3.3 %restrict_operator.1 = (f32[4,520,128]{2,1,0:T(8,128)}, s32[2,8]{1,0:T(2,128)}) custom-call(s32[8]{0:T(128)} %count_any.1, s32[8,8]{1,0:T(8,128)} %slot_any.1, s32[2,8]{1,0:T(2,128)} %bitcast.23, s32[4,8]{1,0:T(4,128)} %bitcast.22, f32[8,64,128]{2,1,0:T(8,128)} %restrict_any.1, f32[8,64,512]{2,1,0:T(8,128)} %operator_any.1, s32[2,8]{1,0:T(2,128)} %bitcast.24), custom_call_target="tpu_custom_call" | custom-call | flops 201326592 | bytes 4194304 | tf_op jit(solution)/shard_map/restrict_operator/pallas_call | solution.py:133
  8.9 0.4 collective-permute-start.3
  9.3 3.8 %all-to-all-start = ((f32[4,520,128]{2,1,0:T(8,128)}), f32[4,520,128]{2,1,0:T(8,128)S(1)}, u32[]{:S(2)}, u32[]{:S(2)}) async-start(f32[4,520,128]{2,1,0:T(8,128)} %get-tuple-element.7), calls=%async_computation | async-start | bytes 2129920 | tf_op jit(solution)/shard_map/all_to_all | solution.py:274
  13.0 3.3 %collective-permute-done.3.mark_ref.far_columns_ref = s32[2,8]{1,0:T(2,128)S(1)} collective-permute-done((s32[2,8]{1,0:T(2,128)}, s32[2,8]{1,0:T(2,128)S(1)}, u32[]{:S(2)}, u32[]{:S(2)}) %collective-permute-start.3) | collective-permute-done | bytes 96 | tf_op jit(solution)/shard_map/ppermute | solution.py:220
  16.4 1.6 %collective-permute-start.6 = (f32[520,128]{1,0:T(8,128)S(1)}, f32[520,128]{1,0:T(8,128)S(1)}, u32[]{:S(2)}, u32[]{:S(2)}) collective-permute-start(f32[520,128]{1,0:T(8,128)S(1)} %append_columns.1.rest_4_), channel_id=1, source_target_pairs={{0,16},{8,24},{16,0},{24,8},{1,17},{9,25},{17,1},{25,9},{2,18},{10... | collective-permute-start | bytes 798728 | tf_op jit(solution)/shard_map/ppermute | solution.py:216
  18.1 5.9 %collective-permute-done.6.rest_6_ = f32[520,128]{1,0:T(8,128)S(1)} collective-permute-done((f32[520,128]{1,0:T(8,128)S(1)}, f32[520,128]{1,0:T(8,128)S(1)}, u32[]{:S(2)}, u32[]{:S(2)}) %collective-permute-start.6) | collective-permute-done | bytes 266272 | tf_op jit(solution)/shard_map/ppermute | solution.py:216
  23.9 0.5 %collective-permute-start = (f32[512,128]{1,0:T(8,128)S(1)}, f32[512,128]{1,0:T(8,128)S(1)}, u32[]{:S(2)}, u32[]{:S(2)}) collective-permute-start(f32[512,128]{1,0:T(8,128)S(1)} %bitcast.20), channel_id=1, source_target_pairs={{0,8},{8,0},{16,24},{24,16},{1,9},{9,1},{17,25},{25,17},{2,10},{10... | collective-permute-start | bytes 786440 | tf_op jit(solution)/shard_map/ppermute | solution.py:216
  24.4 0.0 collective-permute-start.2
  24.5 0.1 pad_add_fusion.own_ref
  24.5 1.3 %collective-permute-done.rest_1_ = f32[512,128]{1,0:T(8,128)S(1)} collective-permute-done((f32[512,128]{1,0:T(8,128)S(1)}, f32[512,128]{1,0:T(8,128)S(1)}, u32[]{:S(2)}, u32[]{:S(2)}) %collective-permute-start) | collective-permute-done | bytes 262176 | tf_op jit(solution)/shard_map/ppermute | solution.py:216
  25.8 0.4 collective-permute-done.2.rest_3_
  26.2 1.4 %all-to-all-done.restricted_ref = f32[4,520,128]{2,1,0:T(8,128)S(1)} async-done(((f32[4,520,128]{2,1,0:T(8,128)}), f32[4,520,128]{2,1,0:T(8,128)S(1)}, u32[]{:S(2)}, u32[]{:S(2)}) %all-to-all-start) | async-done | bytes 1064992 | tf_op jit(solution)/shard_map/all_to_all | solution.py:274
  27.7 2.3 %combine.1 = f32[8,64,128]{2,1,0:T(8,128)S(1)} custom-call(s32[10]{0:T(128)S(1)} %pad_add_fusion.own_ref, f32[4,520,128]{2,1,0:T(8,128)S(1)} %all-to-all-done.restricted_ref, f32[512,128]{1,0:T(8,128)S(1)} %bitcast.21, f32[512,128]{1,0:T(8,128)S(1)} %collective-permute-done.rest_1_, f32[512,128]{1,0:T(8,128)S(1)} %collective-permute-done.1.next_ref.rest_2_, ...), custom_call_target="tpu_custom_call" | custom-call | flops 268435456 | bytes 4194304 | tf_op jit(solution)/shard_map/combine/pallas_call | solution.py:197
  30.0 1.2 %collective-permute-start.10 = (f32[2,64,128]{2,1,0:T(8,128)S(1)}, f32[2,64,128]{2,1,0:T(8,128)S(1)}, u32[]{:S(2)}, u32[]{:S(2)}) collective-permute-start(f32[2,64,128]{2,1,0:T(8,128)S(1)} %get-tuple-element.10), channel_id=1, source_target_pairs={{0,3},{1,2},{2,1},{3,0},{4,7},{5,6},{6,5},{7,4},{8,11},{9,10},{10,... | collective-permute-start | bytes 196616 | tf_op jit(solution)/shard_map/ppermute | solution.py:242
  31.1 1.9 %collective-permute-start.9 = (f32[2,64,128]{2,1,0:T(8,128)S(1)}, f32[2,64,128]{2,1,0:T(8,128)S(1)}, u32[]{:S(2)}, u32[]{:S(2)}) collective-permute-start(f32[2,64,128]{2,1,0:T(8,128)S(1)} %get-tuple-element.11), channel_id=1, source_target_pairs={{0,2},{1,3},{2,0},{3,1},{4,6},{5,7},{6,4},{7,5},{8,10},{9,11},{10,... | collective-permute-start | bytes 196616 | tf_op jit(solution)/shard_map/ppermute | solution.py:242
  33.1 0.5 %collective-permute-start.8 = (f32[2,64,128]{2,1,0:T(8,128)S(1)}, f32[2,64,128]{2,1,0:T(8,128)S(1)}, u32[]{:S(2)}, u32[]{:S(2)}) collective-permute-start(f32[2,64,128]{2,1,0:T(8,128)S(1)} %get-tuple-element.9), channel_id=1, source_target_pairs={{0,1},{1,0},{2,3},{3,2},{4,5},{5,4},{6,7},{7,6},{8,9},{9,8},{10,11... | collective-permute-start | bytes 196616 | tf_op jit(solution)/shard_map/ppermute | solution.py:242
  33.5 1.7 %collective-permute-done.10 = f32[2,64,128]{2,1,0:T(8,128)S(1)} collective-permute-done((f32[2,64,128]{2,1,0:T(8,128)S(1)}, f32[2,64,128]{2,1,0:T(8,128)S(1)}, u32[]{:S(2)}, u32[]{:S(2)}) %collective-permute-start.10) | collective-permute-done | bytes 65568 | tf_op jit(solution)/shard_map/ppermute | solution.py:242
  35.3 0.7 %collective-permute-done.9 = f32[2,64,128]{2,1,0:T(8,128)S(1)} collective-permute-done((f32[2,64,128]{2,1,0:T(8,128)S(1)}, f32[2,64,128]{2,1,0:T(8,128)S(1)}, u32[]{:S(2)}, u32[]{:S(2)}) %collective-permute-start.9) | collective-permute-done | bytes 65568 | tf_op jit(solution)/shard_map/ppermute | solution.py:242
  36.0 1.3 %collective-permute-done.8 = f32[2,64,128]{2,1,0:T(8,128)S(1)} collective-permute-done((f32[2,64,128]{2,1,0:T(8,128)S(1)}, f32[2,64,128]{2,1,0:T(8,128)S(1)}, u32[]{:S(2)}, u32[]{:S(2)}) %collective-permute-start.8) | collective-permute-done | bytes 65568 | tf_op jit(solution)/shard_map/ppermute | solution.py:242
  37.4 2.1 %collective-permute-start.11 = (f32[64,128]{1,0:T(8,128)S(1)}, f32[64,128]{1,0:T(8,128)S(1)}, u32[]{:S(2)}, u32[]{:S(2)}) collective-permute-start(f32[64,128]{1,0:T(8,128)S(1)} %slice_bitcast_fusion), channel_id=1, source_target_pairs={{0,4},{4,0},{1,5},{5,1},{2,6},{6,2},{3,7},{7,3},{8,12},{12,8},{9,1... | collective-permute-start | bytes 98312 | tf_op jit(solution)/shard_map/ppermute | solution.py:220
  39.5 2.8 %collective-permute-done.11 = f32[64,128]{1,0:T(8,128)S(1)} collective-permute-done((f32[64,128]{1,0:T(8,128)S(1)}, f32[64,128]{1,0:T(8,128)S(1)}, u32[]{:S(2)}, u32[]{:S(2)}) %collective-permute-start.11) | collective-permute-done | bytes 32800 | tf_op jit(solution)/shard_map/ppermute | solution.py:220
  42.2 0.6 %fusion.3 = f32[128,64]{0,1:T(8,128)} fusion(f32[64,128]{1,0:T(8,128)S(1)} %collective-permute-done.11, f32[2,64,128]{2,1,0:T(8,128)S(1)} %fusion.1), kind=kLoop, calls=%fused_computation.6 | loop fusion | flops 8192 | bytes 98304 | tf_op jit(solution)/shard_map/transpose | solution.py:281
  (16 shorter events, 0.1 us)
Async XLA Ops:
  0.0 16.3 %collective-permute-start.4 = (f32[512,128]{1,0:T(8,128)}, f32[512,128]{1,0:T(8,128)S(1)}, u32[]{:S(2)}, u32[]{:S(2)}) collective-permute-start(f32[512,128]{1,0:T(8,128)} %bitcast.18), channel_id=1, source_target_pairs={{0,4},{4,0},{1,5},{5,1},{2,6},{6,2},{3,7},{7,3},{8,12},{12,8},{9,1... | collective-permute-start | bytes 786440 | tf_op jit(solution)/shard_map/ppermute | solution.py:220
  4.0 12.3 %collective-permute-start.1 = (f32[512,128]{1,0:T(8,128)}, f32[512,128]{1,0:T(8,128)S(1)}, u32[]{:S(2)}, u32[]{:S(2)}) collective-permute-start(f32[512,128]{1,0:T(8,128)} %bitcast.19), channel_id=1, source_target_pairs={{0,16},{8,24},{16,0},{24,8},{1,17},{9,25},{17,1},{25,9},{2,18},{10... | collective-permute-start | bytes 786440 | tf_op jit(solution)/shard_map/ppermute | solution.py:216
  8.9 7.5 %collective-permute-start.3 = (s32[2,8]{1,0:T(2,128)}, s32[2,8]{1,0:T(2,128)S(1)}, u32[]{:S(2)}, u32[]{:S(2)}) collective-permute-start(s32[2,8]{1,0:T(2,128)} %get-tuple-element.8.own_columns_ref), channel_id=1, source_target_pairs={{0,4},{4,0},{1,5},{5,1},{2,6},{6,2},{3,7},{7,3},{8,12},{12,8},{9,1... | collective-permute-start | bytes 200 | tf_op jit(solution)/shard_map/ppermute | solution.py:220
  9.3 18.4 %all-to-all-start = ((f32[4,520,128]{2,1,0:T(8,128)}), f32[4,520,128]{2,1,0:T(8,128)S(1)}, u32[]{:S(2)}, u32[]{:S(2)}) async-start(f32[4,520,128]{2,1,0:T(8,128)} %get-tuple-element.7), calls=%async_computation | async-start | bytes 2129920 | tf_op jit(solution)/shard_map/all_to_all | solution.py:274
  13.0 3.3 %copy-start.1 = (s32[2,8]{1,0:T(2,128)S(1)}, s32[2,8]{1,0:T(2,128)}, u32[]{:S(2)}) copy-start(s32[2,8]{1,0:T(2,128)} %get-tuple-element.8.own_columns_ref) | copy-start | bytes 196
  13.0 10.9 %copy-start = (f32[8,64,128]{2,1,0:T(8,128)S(1)}, f32[8,64,128]{2,1,0:T(8,128)}, u32[]{:S(2)}) copy-start(f32[8,64,128]{2,1,0:T(8,128)} %param.12) | copy-start | bytes 786436
  16.4 7.5 %collective-permute-start.6 = (f32[520,128]{1,0:T(8,128)S(1)}, f32[520,128]{1,0:T(8,128)S(1)}, u32[]{:S(2)}, u32[]{:S(2)}) collective-permute-start(f32[520,128]{1,0:T(8,128)S(1)} %append_columns.1.rest_4_), channel_id=1, source_target_pairs={{0,16},{8,24},{16,0},{24,8},{1,17},{9,25},{17,1},{25,9},{2,18},{10... | collective-permute-start | bytes 798728 | tf_op jit(solution)/shard_map/ppermute | solution.py:216
  18.1 8.2 %collective-permute-start.5 = (f32[520,128]{1,0:T(8,128)S(1)}, f32[520,128]{1,0:T(8,128)S(1)}, u32[]{:S(2)}, u32[]{:S(2)}) collective-permute-start(f32[520,128]{1,0:T(8,128)S(1)} %append_columns.1.rest_4_), channel_id=1, source_target_pairs={{0,8},{8,0},{16,24},{24,16},{1,9},{9,1},{17,25},{25,17},{2,10},{10... | collective-permute-start | bytes 798728 | tf_op jit(solution)/shard_map/ppermute | solution.py:216
  23.9 2.3 %collective-permute-start.7 = (f32[520,128]{1,0:T(8,128)S(1)}, f32[520,128]{1,0:T(8,128)S(1)}, u32[]{:S(2)}, u32[]{:S(2)}) collective-permute-start(f32[520,128]{1,0:T(8,128)S(1)} %collective-permute-done.6.rest_6_), channel_id=1, source_target_pairs={{0,8},{8,0},{16,24},{24,16},{1,9},{9,1},{17,25},{25,17},{2,10},{10... | collective-permute-start | bytes 798728 | tf_op jit(solution)/shard_map/ppermute | solution.py:216
  23.9 1.9 %collective-permute-start = (f32[512,128]{1,0:T(8,128)S(1)}, f32[512,128]{1,0:T(8,128)S(1)}, u32[]{:S(2)}, u32[]{:S(2)}) collective-permute-start(f32[512,128]{1,0:T(8,128)S(1)} %bitcast.20), channel_id=1, source_target_pairs={{0,8},{8,0},{16,24},{24,16},{1,9},{9,1},{17,25},{25,17},{2,10},{10... | collective-permute-start | bytes 786440 | tf_op jit(solution)/shard_map/ppermute | solution.py:216
  24.4 1.8 %collective-permute-start.2 = (f32[512,128]{1,0:T(8,128)S(1)}, f32[512,128]{1,0:T(8,128)S(1)}, u32[]{:S(2)}, u32[]{:S(2)}) collective-permute-start(f32[512,128]{1,0:T(8,128)S(1)} %collective-permute-done.1.next_ref.rest_2_), channel_id=1, source_target_pairs={{0,8},{8,0},{16,24},{24,16},{1,9},{9,1},{17,25},{25,17},{2,10},{10... | collective-permute-start | bytes 786440 | tf_op jit(solution)/shard_map/ppermute | solution.py:216
  30.0 5.3 %collective-permute-start.10 = (f32[2,64,128]{2,1,0:T(8,128)S(1)}, f32[2,64,128]{2,1,0:T(8,128)S(1)}, u32[]{:S(2)}, u32[]{:S(2)}) collective-permute-start(f32[2,64,128]{2,1,0:T(8,128)S(1)} %get-tuple-element.10), channel_id=1, source_target_pairs={{0,3},{1,2},{2,1},{3,0},{4,7},{5,6},{6,5},{7,4},{8,11},{9,10},{10,... | collective-permute-start | bytes 196616 | tf_op jit(solution)/shard_map/ppermute | solution.py:242
  31.1 4.9 %collective-permute-start.9 = (f32[2,64,128]{2,1,0:T(8,128)S(1)}, f32[2,64,128]{2,1,0:T(8,128)S(1)}, u32[]{:S(2)}, u32[]{:S(2)}) collective-permute-start(f32[2,64,128]{2,1,0:T(8,128)S(1)} %get-tuple-element.11), channel_id=1, source_target_pairs={{0,2},{1,3},{2,0},{3,1},{4,6},{5,7},{6,4},{7,5},{8,10},{9,11},{10,... | collective-permute-start | bytes 196616 | tf_op jit(solution)/shard_map/ppermute | solution.py:242
  33.1 4.3 %collective-permute-start.8 = (f32[2,64,128]{2,1,0:T(8,128)S(1)}, f32[2,64,128]{2,1,0:T(8,128)S(1)}, u32[]{:S(2)}, u32[]{:S(2)}) collective-permute-start(f32[2,64,128]{2,1,0:T(8,128)S(1)} %get-tuple-element.9), channel_id=1, source_target_pairs={{0,1},{1,0},{2,3},{3,2},{4,5},{5,4},{6,7},{7,6},{8,9},{9,8},{10,11... | collective-permute-start | bytes 196616 | tf_op jit(solution)/shard_map/ppermute | solution.py:242
  37.4 4.9 %collective-permute-start.11 = (f32[64,128]{1,0:T(8,128)S(1)}, f32[64,128]{1,0:T(8,128)S(1)}, u32[]{:S(2)}, u32[]{:S(2)}) collective-permute-start(f32[64,128]{1,0:T(8,128)S(1)} %slice_bitcast_fusion), channel_id=1, source_target_pairs={{0,4},{4,0},{1,5},{5,1},{2,6},{6,2},{3,7},{7,3},{8,12},{12,8},{9,1... | collective-permute-start | bytes 98312 | tf_op jit(solution)/shard_map/ppermute | solution.py:220

commit v18 on v15

--- a/solution.py
+++ b/solution.py
@@ -52,9 +52,9 @@
 
 
 def restrict_kernel(
-    count_any, slot_any, rows_any, fetch_any, restrict_any, operator_any, columns_any, blocks_any,
+    count_any, slot_any, rows_any, fetch_any, restrict_any, operator_any, columns_any, blocks_any, side_any,
     out_ref, own_columns_ref, own_blocks_ref,
-    count_ref, slot_ref, rows_ref, fetch_ref, restrict_ref, operator_ref, sems, operator_sems,
+    count_ref, slot_ref, rows_ref, fetch_ref, side_ref, restrict_ref, operator_ref, sems, operator_sems,
 ):
     fine_rows, block_size, _ = operator_ref.shape
     entries = slot_ref.shape[1]
@@ -66,7 +66,7 @@
     pairs = [
         (count_any, count_ref), (slot_any, slot_ref), (rows_any, rows_ref),
         (fetch_any, fetch_ref), (restrict_any, restrict_ref),
-        (columns_any, own_columns_ref), (blocks_any, own_blocks_ref),
+        (columns_any, own_columns_ref), (blocks_any, own_blocks_ref), (side_any, side_ref),
     ]
     copies = [pltpu.make_async_copy(a, b, sems.at[i]) for i, (a, b) in enumerate(pairs)]
     operators = [
@@ -87,7 +87,8 @@
         value = jnp.zeros((EXTRA, wide), jnp.int32)
         for side in range(2):
             for s in range(slot_count):
-                wanted = fetch_ref[s, side * half + near]
+                turned = near ^ jnp.where(side_ref[0] == side, 0, half // 2)
+                wanted = fetch_ref[s, side * half + turned]
                 value = jnp.where(short_lane == side * slot_count + s, wanted, value)
         out_ref[near, used:] = value.astype(jnp.float32)
 
@@ -101,19 +102,22 @@
         for k in range(entries):
             part = jnp.where(k < count_ref[i], product[k * block_size : (k + 1) * block_size], 0.0)
             peer = lax.div(slot_ref[i, k], slot_count)
-            place = lax.div(peer, half) * slot_count + lax.rem(slot_ref[i, k], slot_count)
+            side = lax.div(peer, half)
+            place = side * slot_count + lax.rem(slot_ref[i, k], slot_count)
+            near = lax.rem(peer, half) ^ jnp.where(side_ref[0] == side, 0, half // 2)
             start = pl.multiple_of(place * block_size, block_size)
-            out_ref[lax.rem(peer, half), pl.ds(start, block_size)] += part
+            out_ref[near, pl.ds(start, block_size)] += part
 
 
 def restrict_operator(
-    operator_count, operator_slot, restrict_rows, fetch, operator_blocks, restrict_blocks, own_columns, own_blocks
+    operator_count, operator_slot, restrict_rows, fetch, operator_blocks, restrict_blocks, own_columns, own_blocks, side
 ):
     fine_rows, block_size, width = operator_blocks.shape
     slot_count, columns = fetch.shape
     wide = NCR * block_size
     rows = 2 * slot_count * block_size + EXTRA
     small = (operator_count, operator_slot, restrict_rows, fetch)
+    kept = small + (side,)
     return pl.pallas_call(
         restrict_kernel,
         out_shape=(
@@ -121,21 +125,20 @@
             jax.ShapeDtypeStruct(own_columns.shape, own_columns.dtype),
             jax.ShapeDtypeStruct(own_blocks.shape, own_blocks.dtype),
         ),
-        in_specs=[pl.BlockSpec(memory_space=pltpu.HBM)] * 8,
+        in_specs=[pl.BlockSpec(memory_space=pltpu.HBM)] * 9,
         out_specs=[pl.BlockSpec(memory_space=pltpu.VMEM)] * 3,
-        scratch_shapes=[pltpu.SMEM(x.shape, x.dtype) for x in small]
+        scratch_shapes=[pltpu.SMEM(x.shape, x.dtype) for x in kept]
         + [pltpu.VMEM(x.shape, x.dtype) for x in (restrict_blocks, operator_blocks)]
-        + [pltpu.SemaphoreType.DMA((7,)), pltpu.SemaphoreType.DMA((fine_rows,))],
+        + [pltpu.SemaphoreType.DMA((8,)), pltpu.SemaphoreType.DMA((fine_rows,))],
         cost_estimate=pl.CostEstimate(
             flops=6 * fine_rows * block_size * width * wide, bytes_accessed=4 << 20, transcendentals=0
         ),
         name="restrict_operator",
-    )(*small, restrict_blocks, operator_blocks, own_columns, own_blocks)
+    )(*small, restrict_blocks, operator_blocks, own_columns, own_blocks, side)
 
 
 def combine_kernel(own_ref, restricted_ref, *rest, slot_count, fine_rows, entries):
-    pieces, (out_ref, held_ref, table_ref, index_ref, sem) = rest[:-9], rest[-9:-4]
-    sums = rest[-4:]
+    pieces, (out_ref, held_ref, table_ref, index_ref, sem) = rest[:-5], rest[-5:]
     half = restricted_ref.shape[0]
     rows = len(pieces) // 2
     block_size = out_ref.shape[1]
@@ -143,62 +146,55 @@
     used = 2 * slot_count * block_size
     held = fine_rows * block_size
 
+    table_ref[:1, : own_ref.shape[1]] = own_ref[...]
     for near in range(half):
-        table_ref[near : near + 1] = restricted_ref[near, used : used + 1].astype(jnp.int32)
+        table_ref[1 + near : 2 + near] = restricted_ref[near, used : used + 1].astype(jnp.int32)
     for i, piece in enumerate(pieces[rows:]):
         for far in range(2):
-            first = half + entries * (far * rows + i)
+            first = 1 + half + entries * (far * rows + i)
             row = held + entries * (1 - far)
             table_ref[first : first + entries] = piece[row : row + entries].astype(jnp.int32)
     copy = pltpu.make_async_copy(table_ref, index_ref, sem)
     copy.start()
     for i, piece in enumerate(pieces):
         held_ref[i] = piece[...] if i < rows else piece[:held]
-    for total in sums:
-        total[...] = jnp.zeros_like(total)
+    out_ref[...] = jnp.zeros_like(out_ref)
     copy.wait()
 
-    def add_product(i, total):
+    def step(i, carry):
         near = lax.div(i, 2 * slot_count)
         place = lax.rem(i, 2 * slot_count)
-        wanted = index_ref[near, place]
+        wanted = index_ref[1 + near, place]
         inside = lax.rem(wanted, fine_rows)
-        far = lax.div(place, slot_count) ^ own_ref[1]
-        piece = far * rows + (lax.div(wanted, fine_rows * columns) ^ own_ref[0])
+        far = lax.div(place, slot_count) ^ index_ref[0, 1]
+        piece = far * rows + (lax.div(wanted, fine_rows * columns) ^ index_ref[0, 0])
         block = held_ref[piece, pl.ds(pl.multiple_of(inside * block_size, block_size), block_size)]
         restricted = restricted_ref[near, pl.ds(pl.multiple_of(place * block_size, block_size), block_size)]
         product = transposed_product(block, restricted)
         for m in range(entries):
-            column = own_ref[2 + index_ref[half + entries * piece + m, inside]]
-            total[m % len(total)][column] += product[m * block_size : (m + 1) * block_size]
-
-    def step(i, carry):
-        add_product(2 * i, sums[:2])
-        add_product(2 * i + 1, sums[2:])
+            column = index_ref[0, 2 + index_ref[1 + half + entries * piece + m, inside]]
+            out_ref[column] += product[m * block_size : (m + 1) * block_size]
         return carry
 
-    lax.fori_loop(0, half * slot_count, step, 0, unroll=8)
-    out_ref[...] = (sums[0][...] + sums[1][...]) + (sums[2][...] + sums[3][...])
+    lax.fori_loop(0, half * 2 * slot_count, step, 0, unroll=16)
 
 
 def combine(own, restricted, pieces, coarse_all, slot_count, fine_rows, block_size):
     half, _, wide = restricted.shape
     width = pieces[0].shape[1]
     entries = width // block_size
-    table_rows = -(-(half + entries * len(pieces)) // 8) * 8
+    table_rows = -(-(1 + half + entries * len(pieces)) // 8) * 8
     return pl.pallas_call(
         functools.partial(combine_kernel, slot_count=slot_count, fine_rows=fine_rows, entries=entries),
         out_shape=jax.ShapeDtypeStruct((coarse_all, block_size, wide), jnp.float32),
-        in_specs=[pl.BlockSpec(memory_space=pltpu.SMEM)]
-        + [pl.BlockSpec(memory_space=pltpu.VMEM)] * (1 + len(pieces)),
+        in_specs=[pl.BlockSpec(memory_space=pltpu.VMEM)] * (2 + len(pieces)),
         out_specs=pl.BlockSpec(memory_space=pltpu.VMEM),
         scratch_shapes=[
             pltpu.VMEM((len(pieces), fine_rows * block_size, width), jnp.float32),
             pltpu.VMEM((table_rows, LANES), jnp.int32),
             pltpu.SMEM((table_rows, LANES), jnp.int32),
             pltpu.SemaphoreType.DMA,
-        ]
-        + [pltpu.VMEM((coarse_all, block_size, wide), jnp.float32)] * 4,
+        ],
         compiler_params=pltpu.CompilerParams(vmem_limit_bytes=VMEM_LIMIT),
         cost_estimate=pl.CostEstimate(flops=1 << 28, bytes_accessed=4 << 20, transcendentals=0),
         name="combine",
@@ -211,6 +207,12 @@
 
 def half_swap(x):
     return lax.ppermute(x, "half", [(0, 1), (1, 0)])
+
+
+def far_swap(x):
+    half = lax.axis_size("near")
+    pairs = [(h * half + n, (1 - h) * half + (n ^ half // 2)) for h in range(2) for n in range(half)]
+    return lax.ppermute(x, ("half", "near"), pairs)
 
 
 def spread_over_rows(blocks, rows):
@@ -251,10 +253,10 @@
     fine_rows, block_size, width = prolong_blocks.shape
     fetch = fetch_lists.reshape(2 * half, slot_count).T
     own = jnp.stack([lax.axis_index("row"), lax.axis_index("half")])
-    own = jnp.concatenate([own, place_of_columns(half)])
+    own = jnp.concatenate([own, place_of_columns(half)])[None]
 
     near_blocks = prolong_blocks.reshape(fine_rows * block_size, width)
-    far_blocks = half_swap(near_blocks)
+    far_blocks = far_swap(near_blocks)
     restricted, own_columns, near_blocks = restrict_operator(
         operator_count,
         operator_slot,
@@ -264,9 +266,10 @@
         restrict_blocks,
         prolong_cols.T,
         near_blocks,
+        lax.axis_index("half").reshape(1),
     )
     restricted = lax.all_to_all(restricted, "near", split_axis=0, concat_axis=0, tiled=True)
-    far_columns = half_swap(own_columns)
+    far_columns = far_swap(own_columns)
     near_pieces = spread_over_rows(near_blocks, rows)
     far_blocks = append_columns(near_pieces[rows // 2], far_columns, own_columns, far_blocks)
     pieces = near_pieces + spread_over_rows(far_blocks, rows)

time: 42.8 us -> 42 us (0.981)
  Pallas kernels: 5.79 us -> 5.27 us
    ppermute x0 -> x2, starting transfers between devices: none -> 5.27 us  [far_swap(): return lax.ppermute(x, ('half', 'near'), pairs)]
    ppermute x3 -> x1, starting transfers between devices: 7.56 us -> 2.6 us  [half_swap(): return lax.ppermute(x, 'half', [(0, 1), (1, 0)])]
    ppermute x3 -> x1, waiting for transfers between devices: 4.94 us -> 2.29 us  [half_swap(): return lax.ppermute(x, 'half', [(0, 1), (1, 0)])]
    ppermute x0 -> x2, waiting for transfers between devices: none -> 1.69 us  [far_swap(): return lax.ppermute(x, ('half', 'near'), pairs)]
    pallas_call x1, Pallas kernels: 2.33 us -> 1.75 us  [combine(): pl.pallas_call(functools.partial(combine_kernel, slot_count=slot_count, f...]
    ppermute x6, waiting for transfers between devices: 7.55 us -> 7.98 us  [row_swap(): lax.ppermute(x, 'row', [(r, r ^ bit) for r in range(lax.axis_size('row'))])]
    ppermute x3, waiting for transfers between devices: 3.22 us -> 3.65 us  [add_over_columns(): lax.ppermute(sums[2 * near:2 * near + 2], 'near', [(n, n ^ near) for n in...]
  transfers between devices with their start and end apart: 13 -> 13, of which waited for: 8 -> 10; matrix products, arithmetic and copies ran while one was open for 0% -> 0% of each run, Pallas kernels for 8% -> 8%
where the time goes in v18:
time: 42 us; the launch traced here: 41.8 us
  starting transfers between devices  18.8 us (45%)
  waiting for transfers between devices  17 us (40%)
  Pallas kernels  5.27 us (13%)
  other arithmetic  0.73 us (2%)
    ppermute x6, waiting for transfers between devices, row_swap(): lax.ppermute(x, 'row', [(r, r ^ bit) for r in range(lax.axis_size('row'))])  7.98 us
    ppermute x2, starting transfers between devices, far_swap(): return lax.ppermute(x, ('half', 'near'), pairs)  5.27 us
    ppermute x6, starting transfers between devices, row_swap(): lax.ppermute(x, 'row', [(r, r ^ bit) for r in range(lax.axis_size('row'))])  3.68 us
    ppermute x3, waiting for transfers between devices, add_over_columns(): lax.ppermute(sums[2 * near:2 * near + 2], 'near', [(n, n ^ near) for n in...  3.65 us
    all_to_all x1, starting transfers between devices, local(): lax.all_to_all(restricted, 'near', split_axis=0, concat_axis=0, tiled=True)  3.65 us
    ppermute x3, starting transfers between devices, add_over_columns(): lax.ppermute(sums[2 * near:2 * near + 2], 'near', [(n, n ^ near) for n in...  3.55 us
    pallas_call x1, Pallas kernels, restrict_operator(): pl.pallas_call(restrict_kernel, out_shape=(jax.ShapeDtypeStruct((columns...  3.49 us
    ppermute x1, starting transfers between devices, half_swap(): return lax.ppermute(x, 'half', [(0, 1), (1, 0)])  2.6 us
  transfers between devices with their start and end apart: 13, of which 10 were waited for; matrix products, arithmetic and copies ran while one was open for 0% of the time, Pallas kernels for 8%

profile of v18, /device:TPU:0, one launch (start us, length us, event | category | flops | bytes accessed | tf_op | source)
XLA Modules:
  0.0 41.8 jit_solution(17009992148963655823)
XLA Ops:
  0.0 5.0 %collective-permute-start.4 = (f32[512,128]{1,0:T(8,128)}, f32[512,128]{1,0:T(8,128)S(1)}, u32[]{:S(2)}, u32[]{:S(2)}) collective-permute-start(f32[512,128]{1,0:T(8,128)} %bitcast.20), channel_id=1, source_target_pairs={{0,6},{1,7},{2,4},{3,5},{4,2},{5,3},{6,0},{7,1},{8,14},{9,15},{10,... | collective-permute-start | bytes 786440 | tf_op jit(solution)/shard_map/ppermute | solution.py:215
  5.0 3.5 %restrict_operator.1 = (f32[4,520,128]{2,1,0:T(8,128)}, s32[2,8]{1,0:T(2,128)}, f32[512,128]{1,0:T(8,128)}) custom-call(s32[8]{0:T(128)} %count_any.1, s32[8,8]{1,0:T(8,128)} %slot_any.1, s32[2,8]{1,0:T(2,128)} %bitcast.23, s32[4,8]{1,0:T(4,128)} %bitcast.22, f32[8,64,128]{2,1,0:T(8,128)} %restrict_any.1, f32[8,64,512]{2,1,0:T(8,128)} %operator_any.1, ...), custom_call_target="tpu_custom_call" | custom-call | flops 201326592 | bytes 4194304 | tf_op jit(solution)/shard_map/restrict_operator/pallas_call | solution.py:121
  8.6 1.6 %collective-permute-start.1 = (f32[512,128]{1,0:T(8,128)}, f32[512,128]{1,0:T(8,128)S(1)}, u32[]{:S(2)}, u32[]{:S(2)}) collective-permute-start(f32[512,128]{1,0:T(8,128)} %get-tuple-element.9.rest_0_), channel_id=1, source_target_pairs={{0,16},{8,24},{16,0},{24,8},{1,17},{9,25},{17,1},{25,9},{2,18},{10... | collective-permute-start | bytes 786440 | tf_op jit(solution)/shard_map/ppermute | solution.py:205
  10.1 0.2 collective-permute-start.3
  10.4 3.6 %all-to-all-start = ((f32[4,520,128]{2,1,0:T(8,128)}), f32[4,520,128]{2,1,0:T(8,128)S(1)}, u32[]{:S(2)}, u32[]{:S(2)}) async-start(f32[4,520,128]{2,1,0:T(8,128)} %get-tuple-element.8), calls=%async_computation | async-start | bytes 2129920 | tf_op jit(solution)/shard_map/all_to_all | solution.py:271
  14.0 1.7 %collective-permute-done.3.far_columns_ref = s32[2,8]{1,0:T(2,128)S(1)} collective-permute-done((s32[2,8]{1,0:T(2,128)}, s32[2,8]{1,0:T(2,128)S(1)}, u32[]{:S(2)}, u32[]{:S(2)}) %collective-permute-start.3) | collective-permute-done | bytes 96 | tf_op jit(solution)/shard_map/ppermute | solution.py:215
  15.7 0.9 %collective-permute-done.1.next_ref.rest_2_ = f32[512,128]{1,0:T(8,128)S(1)} collective-permute-done((f32[512,128]{1,0:T(8,128)}, f32[512,128]{1,0:T(8,128)S(1)}, u32[]{:S(2)}, u32[]{:S(2)}) %collective-permute-start.1) | collective-permute-done | bytes 262176 | tf_op jit(solution)/shard_map/ppermute | solution.py:205
  16.6 1.6 %collective-permute-start.6 = (f32[520,128]{1,0:T(8,128)S(1)}, f32[520,128]{1,0:T(8,128)S(1)}, u32[]{:S(2)}, u32[]{:S(2)}) collective-permute-start(f32[520,128]{1,0:T(8,128)S(1)} %append_columns.1.rest_4_), channel_id=1, source_target_pairs={{0,16},{8,24},{16,0},{24,8},{1,17},{9,25},{17,1},{25,9},{2,18},{10... | collective-permute-start | bytes 798728 | tf_op jit(solution)/shard_map/ppermute | solution.py:205
  18.2 5.4 %collective-permute-done.6.rest_6_ = f32[520,128]{1,0:T(8,128)S(1)} collective-permute-done((f32[520,128]{1,0:T(8,128)S(1)}, f32[520,128]{1,0:T(8,128)S(1)}, u32[]{:S(2)}, u32[]{:S(2)}) %collective-permute-start.6) | collective-permute-done | bytes 266272 | tf_op jit(solution)/shard_map/ppermute | solution.py:205
  23.6 0.5 %collective-permute-start = (f32[512,128]{1,0:T(8,128)S(1)}, f32[512,128]{1,0:T(8,128)S(1)}, u32[]{:S(2)}, u32[]{:S(2)}) collective-permute-start(f32[512,128]{1,0:T(8,128)S(1)} %copy-done), channel_id=1, source_target_pairs={{0,8},{8,0},{16,24},{24,16},{1,9},{9,1},{17,25},{25,17},{2,10},{10... | collective-permute-start | bytes 786440 | tf_op jit(solution)/shard_map/ppermute | solution.py:205
  24.2 0.1 add_bitcast_fusion.own_ref
  24.2 1.3 %collective-permute-done.rest_1_ = f32[512,128]{1,0:T(8,128)S(1)} collective-permute-done((f32[512,128]{1,0:T(8,128)S(1)}, f32[512,128]{1,0:T(8,128)S(1)}, u32[]{:S(2)}, u32[]{:S(2)}) %collective-permute-start) | collective-permute-done | bytes 262176 | tf_op jit(solution)/shard_map/ppermute | solution.py:205
  25.5 0.4 collective-permute-done.2.rest_3_
  25.9 1.4 %all-to-all-done.restricted_ref = f32[4,520,128]{2,1,0:T(8,128)S(1)} async-done(((f32[4,520,128]{2,1,0:T(8,128)}), f32[4,520,128]{2,1,0:T(8,128)S(1)}, u32[]{:S(2)}, u32[]{:S(2)}) %all-to-all-start) | async-done | bytes 1064992 | tf_op jit(solution)/shard_map/all_to_all | solution.py:271
  27.3 1.8 %combine.1 = f32[8,64,128]{2,1,0:T(8,128)S(1)} custom-call(s32[1,10]{1,0:T(1,128)S(1)} %add_bitcast_fusion.own_ref, f32[4,520,128]{2,1,0:T(8,128)S(1)} %all-to-all-done.restricted_ref, f32[512,128]{1,0:T(8,128)S(1)} %copy-done, f32[512,128]{1,0:T(8,128)S(1)} %collective-permute-done.rest_1_, f32[512,128]{1,0:T(8,128)S(1)} %collective-permute-done.1.next_ref.rest_2_, ...), custom_call_target="tpu_custom_call" | custom-call | flops 268435456 | bytes 4194304 | tf_op jit(solution)/shard_map/combine/pallas_call | solution.py:187
  29.1 1.5 %collective-permute-start.8 = (f32[2,64,128]{2,1,0:T(8,128)S(1)}, f32[2,64,128]{2,1,0:T(8,128)S(1)}, u32[]{:S(2)}, u32[]{:S(2)}) collective-permute-start(f32[2,64,128]{2,1,0:T(8,128)S(1)} %get-tuple-element.11), channel_id=1, source_target_pairs={{0,1},{1,0},{2,3},{3,2},{4,5},{5,4},{6,7},{7,6},{8,9},{9,8},{10,11... | collective-permute-start | bytes 196616 | tf_op jit(solution)/shard_map/ppermute | solution.py:237
  30.6 1.4 %collective-permute-start.10 = (f32[2,64,128]{2,1,0:T(8,128)S(1)}, f32[2,64,128]{2,1,0:T(8,128)S(1)}, u32[]{:S(2)}, u32[]{:S(2)}) collective-permute-start(f32[2,64,128]{2,1,0:T(8,128)S(1)} %get-tuple-element.12), channel_id=1, source_target_pairs={{0,3},{1,2},{2,1},{3,0},{4,7},{5,6},{6,5},{7,4},{8,11},{9,10},{10,... | collective-permute-start | bytes 196616 | tf_op jit(solution)/shard_map/ppermute | solution.py:237
  32.0 0.6 %collective-permute-start.9 = (f32[2,64,128]{2,1,0:T(8,128)S(1)}, f32[2,64,128]{2,1,0:T(8,128)S(1)}, u32[]{:S(2)}, u32[]{:S(2)}) collective-permute-start(f32[2,64,128]{2,1,0:T(8,128)S(1)} %get-tuple-element.13), channel_id=1, source_target_pairs={{0,2},{1,3},{2,0},{3,1},{4,6},{5,7},{6,4},{7,5},{8,10},{9,11},{10,... | collective-permute-start | bytes 196616 | tf_op jit(solution)/shard_map/ppermute | solution.py:237
  32.6 1.4 %collective-permute-done.8 = f32[2,64,128]{2,1,0:T(8,128)S(1)} collective-permute-done((f32[2,64,128]{2,1,0:T(8,128)S(1)}, f32[2,64,128]{2,1,0:T(8,128)S(1)}, u32[]{:S(2)}, u32[]{:S(2)}) %collective-permute-start.8) | collective-permute-done | bytes 65568 | tf_op jit(solution)/shard_map/ppermute | solution.py:237
  34.0 1.7 %collective-permute-done.10 = f32[2,64,128]{2,1,0:T(8,128)S(1)} collective-permute-done((f32[2,64,128]{2,1,0:T(8,128)S(1)}, f32[2,64,128]{2,1,0:T(8,128)S(1)}, u32[]{:S(2)}, u32[]{:S(2)}) %collective-permute-start.10) | collective-permute-done | bytes 65568 | tf_op jit(solution)/shard_map/ppermute | solution.py:237
  35.8 0.5 %collective-permute-done.9 = f32[2,64,128]{2,1,0:T(8,128)S(1)} collective-permute-done((f32[2,64,128]{2,1,0:T(8,128)S(1)}, f32[2,64,128]{2,1,0:T(8,128)S(1)}, u32[]{:S(2)}, u32[]{:S(2)}) %collective-permute-start.9) | collective-permute-done | bytes 65568 | tf_op jit(solution)/shard_map/ppermute | solution.py:237
  36.3 2.6 %collective-permute-start.11 = (f32[64,128]{1,0:T(8,128)S(1)}, f32[64,128]{1,0:T(8,128)S(1)}, u32[]{:S(2)}, u32[]{:S(2)}) collective-permute-start(f32[64,128]{1,0:T(8,128)S(1)} %slice_bitcast_fusion), channel_id=1, source_target_pairs={{0,4},{4,0},{1,5},{5,1},{2,6},{6,2},{3,7},{7,3},{8,12},{12,8},{9,1... | collective-permute-start | bytes 98312 | tf_op jit(solution)/shard_map/ppermute | solution.py:209
  38.9 2.3 %collective-permute-done.11 = f32[64,128]{1,0:T(8,128)S(1)} collective-permute-done((f32[64,128]{1,0:T(8,128)S(1)}, f32[64,128]{1,0:T(8,128)S(1)}, u32[]{:S(2)}, u32[]{:S(2)}) %collective-permute-start.11) | collective-permute-done | bytes 32800 | tf_op jit(solution)/shard_map/ppermute | solution.py:209
  41.2 0.6 %fusion.3 = f32[128,64]{0,1:T(8,128)} fusion(f32[64,128]{1,0:T(8,128)S(1)} %collective-permute-done.11, f32[2,64,128]{2,1,0:T(8,128)S(1)} %fusion.1), kind=kLoop, calls=%fused_computation.6 | loop fusion | flops 8192 | bytes 98304 | tf_op jit(solution)/shard_map/transpose | solution.py:277
  (15 shorter events, 0.1 us)
Async XLA Ops:
  0.0 15.7 %collective-permute-start.4 = (f32[512,128]{1,0:T(8,128)}, f32[512,128]{1,0:T(8,128)S(1)}, u32[]{:S(2)}, u32[]{:S(2)}) collective-permute-start(f32[512,128]{1,0:T(8,128)} %bitcast.20), channel_id=1, source_target_pairs={{0,6},{1,7},{2,4},{3,5},{4,2},{5,3},{6,0},{7,1},{8,14},{9,15},{10,... | collective-permute-start | bytes 786440 | tf_op jit(solution)/shard_map/ppermute | solution.py:215
  8.6 8.0 %collective-permute-start.1 = (f32[512,128]{1,0:T(8,128)}, f32[512,128]{1,0:T(8,128)S(1)}, u32[]{:S(2)}, u32[]{:S(2)}) collective-permute-start(f32[512,128]{1,0:T(8,128)} %get-tuple-element.9.rest_0_), channel_id=1, source_target_pairs={{0,16},{8,24},{16,0},{24,8},{1,17},{9,25},{17,1},{25,9},{2,18},{10... | collective-permute-start | bytes 786440 | tf_op jit(solution)/shard_map/ppermute | solution.py:205
  10.1 5.6 %collective-permute-start.3 = (s32[2,8]{1,0:T(2,128)}, s32[2,8]{1,0:T(2,128)S(1)}, u32[]{:S(2)}, u32[]{:S(2)}) collective-permute-start(s32[2,8]{1,0:T(2,128)} %get-tuple-element.10.own_columns_ref), channel_id=1, source_target_pairs={{0,6},{1,7},{2,4},{3,5},{4,2},{5,3},{6,0},{7,1},{8,14},{9,15},{10,... | collective-permute-start | bytes 200 | tf_op jit(solution)/shard_map/ppermute | solution.py:215
  10.4 6.2 %copy-start.1 = (s32[2,8]{1,0:T(2,128)S(1)}, s32[2,8]{1,0:T(2,128)}, u32[]{:S(2)}) copy-start(s32[2,8]{1,0:T(2,128)} %get-tuple-element.10.own_columns_ref) | copy-start | bytes 196
  10.4 16.9 %all-to-all-start = ((f32[4,520,128]{2,1,0:T(8,128)}), f32[4,520,128]{2,1,0:T(8,128)S(1)}, u32[]{:S(2)}, u32[]{:S(2)}) async-start(f32[4,520,128]{2,1,0:T(8,128)} %get-tuple-element.8), calls=%async_computation | async-start | bytes 2129920 | tf_op jit(solution)/shard_map/all_to_all | solution.py:271
  14.0 9.6 %copy-start = (f32[512,128]{1,0:T(8,128)S(1)}, f32[512,128]{1,0:T(8,128)}, u32[]{:S(2)}) copy-start(f32[512,128]{1,0:T(8,128)} %get-tuple-element.9.rest_0_) | copy-start | bytes 786436
  16.6 7.0 %collective-permute-start.6 = (f32[520,128]{1,0:T(8,128)S(1)}, f32[520,128]{1,0:T(8,128)S(1)}, u32[]{:S(2)}, u32[]{:S(2)}) collective-permute-start(f32[520,128]{1,0:T(8,128)S(1)} %append_columns.1.rest_4_), channel_id=1, source_target_pairs={{0,16},{8,24},{16,0},{24,8},{1,17},{9,25},{17,1},{25,9},{2,18},{10... | collective-permute-start | bytes 798728 | tf_op jit(solution)/shard_map/ppermute | solution.py:205
  18.2 7.7 %collective-permute-start.5 = (f32[520,128]{1,0:T(8,128)S(1)}, f32[520,128]{1,0:T(8,128)S(1)}, u32[]{:S(2)}, u32[]{:S(2)}) collective-permute-start(f32[520,128]{1,0:T(8,128)S(1)} %append_columns.1.rest_4_), channel_id=1, source_target_pairs={{0,8},{8,0},{16,24},{24,16},{1,9},{9,1},{17,25},{25,17},{2,10},{10... | collective-permute-start | bytes 798728 | tf_op jit(solution)/shard_map/ppermute | solution.py:205
  23.6 2.3 %collective-permute-start.7 = (f32[520,128]{1,0:T(8,128)S(1)}, f32[520,128]{1,0:T(8,128)S(1)}, u32[]{:S(2)}, u32[]{:S(2)}) collective-permute-start(f32[520,128]{1,0:T(8,128)S(1)} %collective-permute-done.6.rest_6_), channel_id=1, source_target_pairs={{0,8},{8,0},{16,24},{24,16},{1,9},{9,1},{17,25},{25,17},{2,10},{10... | collective-permute-start | bytes 798728 | tf_op jit(solution)/shard_map/ppermute | solution.py:205
  23.6 1.9 %collective-permute-start = (f32[512,128]{1,0:T(8,128)S(1)}, f32[512,128]{1,0:T(8,128)S(1)}, u32[]{:S(2)}, u32[]{:S(2)}) collective-permute-start(f32[512,128]{1,0:T(8,128)S(1)} %copy-done), channel_id=1, source_target_pairs={{0,8},{8,0},{16,24},{24,16},{1,9},{9,1},{17,25},{25,17},{2,10},{10... | collective-permute-start | bytes 786440 | tf_op jit(solution)/shard_map/ppermute | solution.py:205
  24.1 1.8 %collective-permute-start.2 = (f32[512,128]{1,0:T(8,128)S(1)}, f32[512,128]{1,0:T(8,128)S(1)}, u32[]{:S(2)}, u32[]{:S(2)}) collective-permute-start(f32[512,128]{1,0:T(8,128)S(1)} %collective-permute-done.1.next_ref.rest_2_), channel_id=1, source_target_pairs={{0,8},{8,0},{16,24},{24,16},{1,9},{9,1},{17,25},{25,17},{2,10},{10... | collective-permute-start | bytes 786440 | tf_op jit(solution)/shard_map/ppermute | solution.py:205
  29.1 5.0 %collective-permute-start.8 = (f32[2,64,128]{2,1,0:T(8,128)S(1)}, f32[2,64,128]{2,1,0:T(8,128)S(1)}, u32[]{:S(2)}, u32[]{:S(2)}) collective-permute-start(f32[2,64,128]{2,1,0:T(8,128)S(1)} %get-tuple-element.11), channel_id=1, source_target_pairs={{0,1},{1,0},{2,3},{3,2},{4,5},{5,4},{6,7},{7,6},{8,9},{9,8},{10,11... | collective-permute-start | bytes 196616 | tf_op jit(solution)/shard_map/ppermute | solution.py:237
  30.6 5.2 %collective-permute-start.10 = (f32[2,64,128]{2,1,0:T(8,128)S(1)}, f32[2,64,128]{2,1,0:T(8,128)S(1)}, u32[]{:S(2)}, u32[]{:S(2)}) collective-permute-start(f32[2,64,128]{2,1,0:T(8,128)S(1)} %get-tuple-element.12), channel_id=1, source_target_pairs={{0,3},{1,2},{2,1},{3,0},{4,7},{5,6},{6,5},{7,4},{8,11},{9,10},{10,... | collective-permute-start | bytes 196616 | tf_op jit(solution)/shard_map/ppermute | solution.py:237
  32.0 4.3 %collective-permute-start.9 = (f32[2,64,128]{2,1,0:T(8,128)S(1)}, f32[2,64,128]{2,1,0:T(8,128)S(1)}, u32[]{:S(2)}, u32[]{:S(2)}) collective-permute-start(f32[2,64,128]{2,1,0:T(8,128)S(1)} %get-tuple-element.13), channel_id=1, source_target_pairs={{0,2},{1,3},{2,0},{3,1},{4,6},{5,7},{6,4},{7,5},{8,10},{9,11},{10,... | collective-permute-start | bytes 196616 | tf_op jit(solution)/shard_map/ppermute | solution.py:237
  36.3 4.9 %collective-permute-start.11 = (f32[64,128]{1,0:T(8,128)S(1)}, f32[64,128]{1,0:T(8,128)S(1)}, u32[]{:S(2)}, u32[]{:S(2)}) collective-permute-start(f32[64,128]{1,0:T(8,128)S(1)} %slice_bitcast_fusion), channel_id=1, source_target_pairs={{0,4},{4,0},{1,5},{5,1},{2,6},{6,2},{3,7},{7,3},{8,12},{12,8},{9,1... | collective-permute-start | bytes 98312 | tf_op jit(solution)/shard_map/ppermute | solution.py:209

commit v19 on v18

--- a/solution.py
+++ b/solution.py
@@ -12,6 +12,7 @@
 LANES = 128
 EXTRA = 8
 HOLD_FLOPS = 16 << 30
+COLUMN_FLOPS = 3 << 30
 VMEM_LIMIT = 48 * 1024 * 1024
 
 
@@ -29,26 +30,42 @@
     return both[:, :width] + both[:, width:]
 
 
-def append_kernel(next_ref, far_columns_ref, own_columns_ref, blocks_ref, out_ref):
+def column_kernel(far_columns_ref, own_columns_ref, out_ref):
+    entries, fine_rows = own_columns_ref.shape
+    out_ref[...] = jnp.zeros_like(out_ref)
+    out_ref[:entries, :fine_rows] = far_columns_ref[...].astype(jnp.float32)
+    out_ref[entries : 2 * entries, :fine_rows] = own_columns_ref[...].astype(jnp.float32)
+
+
+def column_rows(far_columns, own_columns):
+    return pl.pallas_call(
+        column_kernel,
+        out_shape=jax.ShapeDtypeStruct((EXTRA, LANES), jnp.float32),
+        in_specs=[pl.BlockSpec(memory_space=pltpu.VMEM)] * 2,
+        out_specs=pl.BlockSpec(memory_space=pltpu.VMEM),
+        compiler_params=pltpu.CompilerParams(vmem_limit_bytes=VMEM_LIMIT),
+        cost_estimate=pl.CostEstimate(flops=COLUMN_FLOPS, bytes_accessed=COLUMN_FLOPS >> 8, transcendentals=0),
+        name="column_rows",
+    )(far_columns, own_columns)
+
+
+def append_kernel(next_ref, extra_ref, blocks_ref, out_ref):
     used = blocks_ref.shape[0]
-    entries, fine_rows = own_columns_ref.shape
     out_ref[:used] = blocks_ref[...]
-    out_ref[used:] = jnp.zeros((EXTRA, out_ref.shape[1]), jnp.float32)
-    out_ref[used : used + entries, :fine_rows] = far_columns_ref[...].astype(jnp.float32)
-    out_ref[used + entries : used + 2 * entries, :fine_rows] = own_columns_ref[...].astype(jnp.float32)
-
-
-def append_columns(next_blocks, far_columns, own_columns, blocks):
+    out_ref[used:] = extra_ref[...]
+
+
+def append_columns(next_blocks, extra, blocks):
     used, width = blocks.shape
     return pl.pallas_call(
         append_kernel,
         out_shape=jax.ShapeDtypeStruct((used + EXTRA, width), blocks.dtype),
-        in_specs=[pl.BlockSpec(memory_space=pltpu.VMEM)] * 4,
+        in_specs=[pl.BlockSpec(memory_space=pltpu.VMEM)] * 3,
         out_specs=pl.BlockSpec(memory_space=pltpu.VMEM),
         compiler_params=pltpu.CompilerParams(vmem_limit_bytes=VMEM_LIMIT),
         cost_estimate=pl.CostEstimate(flops=HOLD_FLOPS, bytes_accessed=HOLD_FLOPS >> 8, transcendentals=0),
         name="append_columns",
-    )(next_blocks, far_columns, own_columns, blocks)
+    )(next_blocks, extra, blocks)
 
 
 def restrict_kernel(
@@ -271,7 +288,7 @@
     restricted = lax.all_to_all(restricted, "near", split_axis=0, concat_axis=0, tiled=True)
     far_columns = far_swap(own_columns)
     near_pieces = spread_over_rows(near_blocks, rows)
-    far_blocks = append_columns(near_pieces[rows // 2], far_columns, own_columns, far_blocks)
+    far_blocks = append_columns(near_pieces[rows // 2], column_rows(far_columns, own_columns), far_blocks)
     pieces = near_pieces + spread_over_rows(far_blocks, rows)
     sums = combine(own, restricted, pieces, NCR * rows, slot_count, fine_rows, block_size)
     return add_over_columns(sums, half).T

time: 42 us -> 48.5 us (1.15)
  waiting for transfers between devices: 17 us -> 22.3 us
  starting transfers between devices: 18.8 us -> 19.8 us
    ppermute x2, waiting for transfers between devices: 1.69 us -> 10.2 us  [far_swap(): return lax.ppermute(x, ('half', 'near'), pairs)]
    all_to_all x1, waiting for transfers between devices: 1.37 us -> 0.01 us  [local(): lax.all_to_all(restricted, 'near', split_axis=0, concat_axis=0, tiled=True)]
    ppermute x6, waiting for transfers between devices: 7.98 us -> 6.79 us  [row_swap(): lax.ppermute(x, 'row', [(r, r ^ bit) for r in range(lax.axis_size('row'))])]
    ppermute x2, starting transfers between devices: 5.27 us -> 5.96 us  [far_swap(): return lax.ppermute(x, ('half', 'near'), pairs)]
  transfers between devices with their start and end apart: 13 -> 13, of which waited for: 10 -> 7; matrix products, arithmetic and copies ran while one was open for 0% -> 0% of each run, Pallas kernels for 8% -> 7%
where the time goes in v19:
time: 48.5 us; the launch traced here: 48.3 us
  waiting for transfers between devices  22.3 us (46%)
  starting transfers between devices  19.8 us (41%)
  Pallas kernels  5.27 us (11%)
  other arithmetic  0.73 us (2%)
    ppermute x2, waiting for transfers between devices, far_swap(): return lax.ppermute(x, ('half', 'near'), pairs)  10.2 us
    ppermute x6, waiting for transfers between devices, row_swap(): lax.ppermute(x, 'row', [(r, r ^ bit) for r in range(lax.axis_size('row'))])  6.79 us
    ppermute x2, starting transfers between devices, far_swap(): return lax.ppermute(x, ('half', 'near'), pairs)  5.96 us
    all_to_all x1, starting transfers between devices, local(): lax.all_to_all(restricted, 'near', split_axis=0, concat_axis=0, tiled=True)  3.66 us
    ppermute x6, starting transfers between devices, row_swap(): lax.ppermute(x, 'row', [(r, r ^ bit) for r in range(lax.axis_size('row'))])  3.62 us
    ppermute x3, starting transfers between devices, add_over_columns(): lax.ppermute(sums[2 * near:2 * near + 2], 'near', [(n, n ^ near) for n in...  3.55 us
    pallas_call x1, Pallas kernels, restrict_operator(): pl.pallas_call(restrict_kernel, out_shape=(jax.ShapeDtypeStruct((columns...  3.49 us
    ppermute x3, waiting for transfers between devices, add_over_columns(): lax.ppermute(sums[2 * near:2 * near + 2], 'near', [(n, n ^ near) for n in...  3.43 us
  transfers between devices with their start and end apart: 13, of which 7 were waited for; matrix products, arithmetic and copies ran while one was open for 0% of the time, Pallas kernels for 7%

profile of v19, /device:TPU:0, one launch (start us, length us, event | category | flops | bytes accessed | tf_op | source)
XLA Modules:
  0.0 48.3 jit_solution(4508473518997856235)
XLA Ops:
  0.0 5.0 %collective-permute-start.4 = (f32[512,128]{1,0:T(8,128)}, f32[512,128]{1,0:T(8,128)S(1)}, u32[]{:S(2)}, u32[]{:S(2)}) collective-permute-start(f32[512,128]{1,0:T(8,128)} %bitcast.20), channel_id=1, source_target_pairs={{0,6},{1,7},{2,4},{3,5},{4,2},{5,3},{6,0},{7,1},{8,14},{9,15},{10,... | collective-permute-start | bytes 786440 | tf_op jit(solution)/shard_map/ppermute | solution.py:232
  5.0 3.5 %restrict_operator.1 = (f32[4,520,128]{2,1,0:T(8,128)}, s32[2,8]{1,0:T(2,128)}, f32[512,128]{1,0:T(8,128)}) custom-call(s32[8]{0:T(128)} %count_any.1, s32[8,8]{1,0:T(8,128)} %slot_any.1, s32[2,8]{1,0:T(2,128)} %bitcast.23, s32[4,8]{1,0:T(4,128)} %bitcast.22, f32[8,64,128]{2,1,0:T(8,128)} %restrict_any.1, f32[8,64,512]{2,1,0:T(8,128)} %operator_any.1, ...), custom_call_target="tpu_custom_call" | custom-call | flops 201326592 | bytes 4194304 | tf_op jit(solution)/shard_map/restrict_operator/pallas_call | solution.py:138
  8.6 0.0 copy-start.1
  8.6 3.7 %all-to-all-start = ((f32[4,520,128]{2,1,0:T(8,128)}), f32[4,520,128]{2,1,0:T(8,128)S(1)}, u32[]{:S(2)}, u32[]{:S(2)}) async-start(f32[4,520,128]{2,1,0:T(8,128)} %get-tuple-element.8), calls=%async_computation | async-start | bytes 2129920 | tf_op jit(solution)/shard_map/all_to_all | solution.py:288
  12.3 0.9 %collective-permute-start.3 = (s32[2,8]{1,0:T(2,128)S(1)}, s32[2,8]{1,0:T(2,128)S(1)}, u32[]{:S(2)}, u32[]{:S(2)}) collective-permute-start(s32[2,8]{1,0:T(2,128)S(1)} %copy-done.1), channel_id=1, source_target_pairs={{0,6},{1,7},{2,4},{3,5},{4,2},{5,3},{6,0},{7,1},{8,14},{9,15},{10,... | collective-permute-start | bytes 200 | tf_op jit(solution)/shard_map/ppermute | solution.py:232
  13.2 1.5 %collective-permute-start.1 = (f32[512,128]{1,0:T(8,128)S(1)}, f32[512,128]{1,0:T(8,128)S(1)}, u32[]{:S(2)}, u32[]{:S(2)}) collective-permute-start(f32[512,128]{1,0:T(8,128)S(1)} %copy-done), channel_id=1, source_target_pairs={{0,16},{8,24},{16,0},{24,8},{1,17},{9,25},{17,1},{25,9},{2,18},{10... | collective-permute-start | bytes 786440 | tf_op jit(solution)/shard_map/ppermute | solution.py:222
  14.7 10.2 %collective-permute-done.3.far_columns_ref = s32[2,8]{1,0:T(2,128)S(1)} collective-permute-done((s32[2,8]{1,0:T(2,128)S(1)}, s32[2,8]{1,0:T(2,128)S(1)}, u32[]{:S(2)}, u32[]{:S(2)}) %collective-permute-start.3) | collective-permute-done | bytes 96 | tf_op jit(solution)/shard_map/ppermute | solution.py:232
  24.9 0.0 collective-permute-done.1.next_ref.rest_2_
  25.0 1.6 %collective-permute-start.6 = (f32[520,128]{1,0:T(8,128)S(1)}, f32[520,128]{1,0:T(8,128)S(1)}, u32[]{:S(2)}, u32[]{:S(2)}) collective-permute-start(f32[520,128]{1,0:T(8,128)S(1)} %append_columns.1.rest_4_), channel_id=1, source_target_pairs={{0,16},{8,24},{16,0},{24,8},{1,17},{9,25},{17,1},{25,9},{2,18},{10... | collective-permute-start | bytes 798728 | tf_op jit(solution)/shard_map/ppermute | solution.py:222
  26.5 5.1 %collective-permute-done.6.rest_6_ = f32[520,128]{1,0:T(8,128)S(1)} collective-permute-done((f32[520,128]{1,0:T(8,128)S(1)}, f32[520,128]{1,0:T(8,128)S(1)}, u32[]{:S(2)}, u32[]{:S(2)}) %collective-permute-start.6) | collective-permute-done | bytes 266272 | tf_op jit(solution)/shard_map/ppermute | solution.py:222
  31.6 0.5 %collective-permute-start = (f32[512,128]{1,0:T(8,128)S(1)}, f32[512,128]{1,0:T(8,128)S(1)}, u32[]{:S(2)}, u32[]{:S(2)}) collective-permute-start(f32[512,128]{1,0:T(8,128)S(1)} %copy-done), channel_id=1, source_target_pairs={{0,8},{8,0},{16,24},{24,16},{1,9},{9,1},{17,25},{25,17},{2,10},{10... | collective-permute-start | bytes 786440 | tf_op jit(solution)/shard_map/ppermute | solution.py:222
  32.2 0.0 collective-permute-start.2
  32.2 0.1 add_bitcast_fusion.own_ref
  32.2 1.3 %collective-permute-done.rest_1_ = f32[512,128]{1,0:T(8,128)S(1)} collective-permute-done((f32[512,128]{1,0:T(8,128)S(1)}, f32[512,128]{1,0:T(8,128)S(1)}, u32[]{:S(2)}, u32[]{:S(2)}) %collective-permute-start) | collective-permute-done | bytes 262176 | tf_op jit(solution)/shard_map/ppermute | solution.py:222
  33.6 0.4 collective-permute-done.2.rest_3_
  33.9 0.0 collective-permute-done.5.rest_5_
  33.9 1.8 %combine.1 = f32[8,64,128]{2,1,0:T(8,128)S(1)} custom-call(s32[1,10]{1,0:T(1,128)S(1)} %add_bitcast_fusion.own_ref, f32[4,520,128]{2,1,0:T(8,128)S(1)} %all-to-all-done.restricted_ref, f32[512,128]{1,0:T(8,128)S(1)} %copy-done, f32[512,128]{1,0:T(8,128)S(1)} %collective-permute-done.rest_1_, f32[512,128]{1,0:T(8,128)S(1)} %collective-permute-done.1.next_ref.rest_2_, ...), custom_call_target="tpu_custom_call" | custom-call | flops 268435456 | bytes 4194304 | tf_op jit(solution)/shard_map/combine/pallas_call | solution.py:204
  35.7 1.5 %collective-permute-start.8 = (f32[2,64,128]{2,1,0:T(8,128)S(1)}, f32[2,64,128]{2,1,0:T(8,128)S(1)}, u32[]{:S(2)}, u32[]{:S(2)}) collective-permute-start(f32[2,64,128]{2,1,0:T(8,128)S(1)} %get-tuple-element.11), channel_id=1, source_target_pairs={{0,1},{1,0},{2,3},{3,2},{4,5},{5,4},{6,7},{7,6},{8,9},{9,8},{10,11... | collective-permute-start | bytes 196616 | tf_op jit(solution)/shard_map/ppermute | solution.py:254
  37.3 2.0 %collective-permute-start.9 = (f32[2,64,128]{2,1,0:T(8,128)S(1)}, f32[2,64,128]{2,1,0:T(8,128)S(1)}, u32[]{:S(2)}, u32[]{:S(2)}) collective-permute-start(f32[2,64,128]{2,1,0:T(8,128)S(1)} %get-tuple-element.13), channel_id=1, source_target_pairs={{0,2},{1,3},{2,0},{3,1},{4,6},{5,7},{6,4},{7,5},{8,10},{9,11},{10,... | collective-permute-start | bytes 196616 | tf_op jit(solution)/shard_map/ppermute | solution.py:254
  39.3 0.8 %collective-permute-done.8 = f32[2,64,128]{2,1,0:T(8,128)S(1)} collective-permute-done((f32[2,64,128]{2,1,0:T(8,128)S(1)}, f32[2,64,128]{2,1,0:T(8,128)S(1)}, u32[]{:S(2)}, u32[]{:S(2)}) %collective-permute-start.8) | collective-permute-done | bytes 65568 | tf_op jit(solution)/shard_map/ppermute | solution.py:254
  40.1 2.7 %collective-permute-done.10 = f32[2,64,128]{2,1,0:T(8,128)S(1)} collective-permute-done((f32[2,64,128]{2,1,0:T(8,128)S(1)}, f32[2,64,128]{2,1,0:T(8,128)S(1)}, u32[]{:S(2)}, u32[]{:S(2)}) %collective-permute-start.10) | collective-permute-done | bytes 65568 | tf_op jit(solution)/shard_map/ppermute | solution.py:254
  42.8 3.0 %collective-permute-start.11 = (f32[64,128]{1,0:T(8,128)S(1)}, f32[64,128]{1,0:T(8,128)S(1)}, u32[]{:S(2)}, u32[]{:S(2)}) collective-permute-start(f32[64,128]{1,0:T(8,128)S(1)} %slice_bitcast_fusion), channel_id=1, source_target_pairs={{0,4},{4,0},{1,5},{5,1},{2,6},{6,2},{3,7},{7,3},{8,12},{12,8},{9,1... | collective-permute-start | bytes 98312 | tf_op jit(solution)/shard_map/ppermute | solution.py:226
  45.8 1.9 %collective-permute-done.11 = f32[64,128]{1,0:T(8,128)S(1)} collective-permute-done((f32[64,128]{1,0:T(8,128)S(1)}, f32[64,128]{1,0:T(8,128)S(1)}, u32[]{:S(2)}, u32[]{:S(2)}) %collective-permute-start.11) | collective-permute-done | bytes 32800 | tf_op jit(solution)/shard_map/ppermute | solution.py:226
  47.6 0.6 %fusion.3 = f32[128,64]{0,1:T(8,128)} fusion(f32[64,128]{1,0:T(8,128)S(1)} %collective-permute-done.11, f32[2,64,128]{2,1,0:T(8,128)S(1)} %fusion.1), kind=kLoop, calls=%fused_computation.6 | loop fusion | flops 8192 | bytes 98304 | tf_op jit(solution)/shard_map/transpose | solution.py:294
  (16 shorter events, 0.1 us)
Async XLA Ops:
  0.0 24.9 %collective-permute-start.4 = (f32[512,128]{1,0:T(8,128)}, f32[512,128]{1,0:T(8,128)S(1)}, u32[]{:S(2)}, u32[]{:S(2)}) collective-permute-start(f32[512,128]{1,0:T(8,128)} %bitcast.20), channel_id=1, source_target_pairs={{0,6},{1,7},{2,4},{3,5},{4,2},{5,3},{6,0},{7,1},{8,14},{9,15},{10,... | collective-permute-start | bytes 786440 | tf_op jit(solution)/shard_map/ppermute | solution.py:232
  8.6 3.7 %copy-start.1 = (s32[2,8]{1,0:T(2,128)S(1)}, s32[2,8]{1,0:T(2,128)}, u32[]{:S(2)}) copy-start(s32[2,8]{1,0:T(2,128)} %get-tuple-element.10.own_columns_ref) | copy-start | bytes 196
  8.6 4.6 %copy-start = (f32[512,128]{1,0:T(8,128)S(1)}, f32[512,128]{1,0:T(8,128)}, u32[]{:S(2)}) copy-start(f32[512,128]{1,0:T(8,128)} %get-tuple-element.9.rest_0_) | copy-start | bytes 786436
  8.6 25.4 %all-to-all-start = ((f32[4,520,128]{2,1,0:T(8,128)}), f32[4,520,128]{2,1,0:T(8,128)S(1)}, u32[]{:S(2)}, u32[]{:S(2)}) async-start(f32[4,520,128]{2,1,0:T(8,128)} %get-tuple-element.8), calls=%async_computation | async-start | bytes 2129920 | tf_op jit(solution)/shard_map/all_to_all | solution.py:288
  12.3 12.7 %collective-permute-start.3 = (s32[2,8]{1,0:T(2,128)S(1)}, s32[2,8]{1,0:T(2,128)S(1)}, u32[]{:S(2)}, u32[]{:S(2)}) collective-permute-start(s32[2,8]{1,0:T(2,128)S(1)} %copy-done.1), channel_id=1, source_target_pairs={{0,6},{1,7},{2,4},{3,5},{4,2},{5,3},{6,0},{7,1},{8,14},{9,15},{10,... | collective-permute-start | bytes 200 | tf_op jit(solution)/shard_map/ppermute | solution.py:232
  13.2 11.8 %collective-permute-start.1 = (f32[512,128]{1,0:T(8,128)S(1)}, f32[512,128]{1,0:T(8,128)S(1)}, u32[]{:S(2)}, u32[]{:S(2)}) collective-permute-start(f32[512,128]{1,0:T(8,128)S(1)} %copy-done), channel_id=1, source_target_pairs={{0,16},{8,24},{16,0},{24,8},{1,17},{9,25},{17,1},{25,9},{2,18},{10... | collective-permute-start | bytes 786440 | tf_op jit(solution)/shard_map/ppermute | solution.py:222
  25.0 6.7 %collective-permute-start.6 = (f32[520,128]{1,0:T(8,128)S(1)}, f32[520,128]{1,0:T(8,128)S(1)}, u32[]{:S(2)}, u32[]{:S(2)}) collective-permute-start(f32[520,128]{1,0:T(8,128)S(1)} %append_columns.1.rest_4_), channel_id=1, source_target_pairs={{0,16},{8,24},{16,0},{24,8},{1,17},{9,25},{17,1},{25,9},{2,18},{10... | collective-permute-start | bytes 798728 | tf_op jit(solution)/shard_map/ppermute | solution.py:222
  26.5 7.4 %collective-permute-start.5 = (f32[520,128]{1,0:T(8,128)S(1)}, f32[520,128]{1,0:T(8,128)S(1)}, u32[]{:S(2)}, u32[]{:S(2)}) collective-permute-start(f32[520,128]{1,0:T(8,128)S(1)} %append_columns.1.rest_4_), channel_id=1, source_target_pairs={{0,8},{8,0},{16,24},{24,16},{1,9},{9,1},{17,25},{25,17},{2,10},{10... | collective-permute-start | bytes 798728 | tf_op jit(solution)/shard_map/ppermute | solution.py:222
  31.6 2.3 %collective-permute-start.7 = (f32[520,128]{1,0:T(8,128)S(1)}, f32[520,128]{1,0:T(8,128)S(1)}, u32[]{:S(2)}, u32[]{:S(2)}) collective-permute-start(f32[520,128]{1,0:T(8,128)S(1)} %collective-permute-done.6.rest_6_), channel_id=1, source_target_pairs={{0,8},{8,0},{16,24},{24,16},{1,9},{9,1},{17,25},{25,17},{2,10},{10... | collective-permute-start | bytes 798728 | tf_op jit(solution)/shard_map/ppermute | solution.py:222
  31.6 1.9 %collective-permute-start = (f32[512,128]{1,0:T(8,128)S(1)}, f32[512,128]{1,0:T(8,128)S(1)}, u32[]{:S(2)}, u32[]{:S(2)}) collective-permute-start(f32[512,128]{1,0:T(8,128)S(1)} %copy-done), channel_id=1, source_target_pairs={{0,8},{8,0},{16,24},{24,16},{1,9},{9,1},{17,25},{25,17},{2,10},{10... | collective-permute-start | bytes 786440 | tf_op jit(solution)/shard_map/ppermute | solution.py:222
  32.2 1.8 %collective-permute-start.2 = (f32[512,128]{1,0:T(8,128)S(1)}, f32[512,128]{1,0:T(8,128)S(1)}, u32[]{:S(2)}, u32[]{:S(2)}) collective-permute-start(f32[512,128]{1,0:T(8,128)S(1)} %collective-permute-done.1.next_ref.rest_2_), channel_id=1, source_target_pairs={{0,8},{8,0},{16,24},{24,16},{1,9},{9,1},{17,25},{25,17},{2,10},{10... | collective-permute-start | bytes 786440 | tf_op jit(solution)/shard_map/ppermute | solution.py:222
  35.7 4.3 %collective-permute-start.8 = (f32[2,64,128]{2,1,0:T(8,128)S(1)}, f32[2,64,128]{2,1,0:T(8,128)S(1)}, u32[]{:S(2)}, u32[]{:S(2)}) collective-permute-start(f32[2,64,128]{2,1,0:T(8,128)S(1)} %get-tuple-element.11), channel_id=1, source_target_pairs={{0,1},{1,0},{2,3},{3,2},{4,5},{5,4},{6,7},{7,6},{8,9},{9,8},{10,11... | collective-permute-start | bytes 196616 | tf_op jit(solution)/shard_map/ppermute | solution.py:254
  37.3 5.5 %collective-permute-start.10 = (f32[2,64,128]{2,1,0:T(8,128)S(1)}, f32[2,64,128]{2,1,0:T(8,128)S(1)}, u32[]{:S(2)}, u32[]{:S(2)}) collective-permute-start(f32[2,64,128]{2,1,0:T(8,128)S(1)} %get-tuple-element.12), channel_id=1, source_target_pairs={{0,3},{1,2},{2,1},{3,0},{4,7},{5,6},{6,5},{7,4},{8,11},{9,10},{10,... | collective-permute-start | bytes 196616 | tf_op jit(solution)/shard_map/ppermute | solution.py:254
  37.3 5.5 %collective-permute-start.9 = (f32[2,64,128]{2,1,0:T(8,128)S(1)}, f32[2,64,128]{2,1,0:T(8,128)S(1)}, u32[]{:S(2)}, u32[]{:S(2)}) collective-permute-start(f32[2,64,128]{2,1,0:T(8,128)S(1)} %get-tuple-element.13), channel_id=1, source_target_pairs={{0,2},{1,3},{2,0},{3,1},{4,6},{5,7},{6,4},{7,5},{8,10},{9,11},{10,... | collective-permute-start | bytes 196616 | tf_op jit(solution)/shard_map/ppermute | solution.py:254
  42.8 4.9 %collective-permute-start.11 = (f32[64,128]{1,0:T(8,128)S(1)}, f32[64,128]{1,0:T(8,128)S(1)}, u32[]{:S(2)}, u32[]{:S(2)}) collective-permute-start(f32[64,128]{1,0:T(8,128)S(1)} %slice_bitcast_fusion), channel_id=1, source_target_pairs={{0,4},{4,0},{1,5},{5,1},{2,6},{6,2},{3,7},{7,3},{8,12},{12,8},{9,1... | collective-permute-start | bytes 98312 | tf_op jit(solution)/shard_map/ppermute | solution.py:226

commit v20 on v19

--- a/solution.py
+++ b/solution.py
@@ -12,7 +12,7 @@
 LANES = 128
 EXTRA = 8
 HOLD_FLOPS = 16 << 30
-COLUMN_FLOPS = 3 << 30
+COLUMN_FLOPS = 3 << 29
 VMEM_LIMIT = 48 * 1024 * 1024
 
 

time: 48.5 us -> 42 us (0.87)
  waiting for transfers between devices: 22.3 us -> 17 us
  starting transfers between devices: 19.8 us -> 18.8 us
    ppermute x2, waiting for transfers between devices: 10.2 us -> 1.7 us  [far_swap(): return lax.ppermute(x, ('half', 'near'), pairs)]
    all_to_all x1, waiting for transfers between devices: 0.01 us -> 1.38 us  [local(): lax.all_to_all(restricted, 'near', split_axis=0, concat_axis=0, tiled=True)]
    ppermute x6, waiting for transfers between devices: 6.79 us -> 7.95 us  [row_swap(): lax.ppermute(x, 'row', [(r, r ^ bit) for r in range(lax.axis_size('row'))])]
    ppermute x2, starting transfers between devices: 5.96 us -> 5.27 us  [far_swap(): return lax.ppermute(x, ('half', 'near'), pairs)]
  transfers between devices with their start and end apart: 13 -> 13, of which waited for: 7 -> 10; matrix products, arithmetic and copies ran while one was open for 0% -> 0% of each run, Pallas kernels for 7% -> 8%
where the time goes in v20:
time: 42 us; the launch traced here: 41.8 us
  starting transfers between devices  18.8 us (45%)
  waiting for transfers between devices  17 us (40%)
  Pallas kernels  5.27 us (13%)
  other arithmetic  0.73 us (2%)
    ppermute x6, waiting for transfers between devices, row_swap(): lax.ppermute(x, 'row', [(r, r ^ bit) for r in range(lax.axis_size('row'))])  7.95 us
    ppermute x2, starting transfers between devices, far_swap(): return lax.ppermute(x, ('half', 'near'), pairs)  5.27 us
    ppermute x6, starting transfers between devices, row_swap(): lax.ppermute(x, 'row', [(r, r ^ bit) for r in range(lax.axis_size('row'))])  3.69 us
    ppermute x3, waiting for transfers between devices, add_over_columns(): lax.ppermute(sums[2 * near:2 * near + 2], 'near', [(n, n ^ near) for n in...  3.66 us
    all_to_all x1, starting transfers between devices, local(): lax.all_to_all(restricted, 'near', split_axis=0, concat_axis=0, tiled=True)  3.65 us
    ppermute x3, starting transfers between devices, add_over_columns(): lax.ppermute(sums[2 * near:2 * near + 2], 'near', [(n, n ^ near) for n in...  3.55 us
    pallas_call x1, Pallas kernels, restrict_operator(): pl.pallas_call(restrict_kernel, out_shape=(jax.ShapeDtypeStruct((columns...  3.5 us
    ppermute x1, starting transfers between devices, half_swap(): return lax.ppermute(x, 'half', [(0, 1), (1, 0)])  2.59 us
  transfers between devices with their start and end apart: 13, of which 10 were waited for; matrix products, arithmetic and copies ran while one was open for 0% of the time, Pallas kernels for 8%

profile of v20, /device:TPU:0, one launch (start us, length us, event | category | flops | bytes accessed | tf_op | source)
XLA Modules:
  0.0 41.8 jit_solution(9116719838305381452)
XLA Ops:
  0.0 5.0 %collective-permute-start.4 = (f32[512,128]{1,0:T(8,128)}, f32[512,128]{1,0:T(8,128)S(1)}, u32[]{:S(2)}, u32[]{:S(2)}) collective-permute-start(f32[512,128]{1,0:T(8,128)} %bitcast.20), channel_id=1, source_target_pairs={{0,6},{1,7},{2,4},{3,5},{4,2},{5,3},{6,0},{7,1},{8,14},{9,15},{10,... | collective-permute-start | bytes 786440 | tf_op jit(solution)/shard_map/ppermute | solution.py:232
  5.0 3.5 %restrict_operator.1 = (f32[4,520,128]{2,1,0:T(8,128)}, s32[2,8]{1,0:T(2,128)}, f32[512,128]{1,0:T(8,128)}) custom-call(s32[8]{0:T(128)} %count_any.1, s32[8,8]{1,0:T(8,128)} %slot_any.1, s32[2,8]{1,0:T(2,128)} %bitcast.23, s32[4,8]{1,0:T(4,128)} %bitcast.22, f32[8,64,128]{2,1,0:T(8,128)} %restrict_any.1, f32[8,64,512]{2,1,0:T(8,128)} %operator_any.1, ...), custom_call_target="tpu_custom_call" | custom-call | flops 201326592 | bytes 4194304 | tf_op jit(solution)/shard_map/restrict_operator/pallas_call | solution.py:138
  8.6 1.6 %collective-permute-start.1 = (f32[512,128]{1,0:T(8,128)}, f32[512,128]{1,0:T(8,128)S(1)}, u32[]{:S(2)}, u32[]{:S(2)}) collective-permute-start(f32[512,128]{1,0:T(8,128)} %get-tuple-element.9.rest_0_), channel_id=1, source_target_pairs={{0,16},{8,24},{16,0},{24,8},{1,17},{9,25},{17,1},{25,9},{2,18},{10... | collective-permute-start | bytes 786440 | tf_op jit(solution)/shard_map/ppermute | solution.py:222
  10.1 0.2 collective-permute-start.3
  10.4 3.6 %all-to-all-start = ((f32[4,520,128]{2,1,0:T(8,128)}), f32[4,520,128]{2,1,0:T(8,128)S(1)}, u32[]{:S(2)}, u32[]{:S(2)}) async-start(f32[4,520,128]{2,1,0:T(8,128)} %get-tuple-element.8), calls=%async_computation | async-start | bytes 2129920 | tf_op jit(solution)/shard_map/all_to_all | solution.py:288
  14.0 1.7 %collective-permute-done.3.far_columns_ref = s32[2,8]{1,0:T(2,128)S(1)} collective-permute-done((s32[2,8]{1,0:T(2,128)}, s32[2,8]{1,0:T(2,128)S(1)}, u32[]{:S(2)}, u32[]{:S(2)}) %collective-permute-start.3) | collective-permute-done | bytes 96 | tf_op jit(solution)/shard_map/ppermute | solution.py:232
  15.7 0.8 %collective-permute-done.1.next_ref.rest_2_ = f32[512,128]{1,0:T(8,128)S(1)} collective-permute-done((f32[512,128]{1,0:T(8,128)}, f32[512,128]{1,0:T(8,128)S(1)}, u32[]{:S(2)}, u32[]{:S(2)}) %collective-permute-start.1) | collective-permute-done | bytes 262176 | tf_op jit(solution)/shard_map/ppermute | solution.py:222
  16.6 1.6 %collective-permute-start.6 = (f32[520,128]{1,0:T(8,128)S(1)}, f32[520,128]{1,0:T(8,128)S(1)}, u32[]{:S(2)}, u32[]{:S(2)}) collective-permute-start(f32[520,128]{1,0:T(8,128)S(1)} %append_columns.1.rest_4_), channel_id=1, source_target_pairs={{0,16},{8,24},{16,0},{24,8},{1,17},{9,25},{17,1},{25,9},{2,18},{10... | collective-permute-start | bytes 798728 | tf_op jit(solution)/shard_map/ppermute | solution.py:222
  18.2 5.4 %collective-permute-done.6.rest_6_ = f32[520,128]{1,0:T(8,128)S(1)} collective-permute-done((f32[520,128]{1,0:T(8,128)S(1)}, f32[520,128]{1,0:T(8,128)S(1)}, u32[]{:S(2)}, u32[]{:S(2)}) %collective-permute-start.6) | collective-permute-done | bytes 266272 | tf_op jit(solution)/shard_map/ppermute | solution.py:222
  23.6 0.5 %collective-permute-start = (f32[512,128]{1,0:T(8,128)S(1)}, f32[512,128]{1,0:T(8,128)S(1)}, u32[]{:S(2)}, u32[]{:S(2)}) collective-permute-start(f32[512,128]{1,0:T(8,128)S(1)} %copy-done), channel_id=1, source_target_pairs={{0,8},{8,0},{16,24},{24,16},{1,9},{9,1},{17,25},{25,17},{2,10},{10... | collective-permute-start | bytes 786440 | tf_op jit(solution)/shard_map/ppermute | solution.py:222
  24.2 0.1 add_bitcast_fusion.own_ref
  24.2 1.3 %collective-permute-done.rest_1_ = f32[512,128]{1,0:T(8,128)S(1)} collective-permute-done((f32[512,128]{1,0:T(8,128)S(1)}, f32[512,128]{1,0:T(8,128)S(1)}, u32[]{:S(2)}, u32[]{:S(2)}) %collective-permute-start) | collective-permute-done | bytes 262176 | tf_op jit(solution)/shard_map/ppermute | solution.py:222
  25.5 0.4 collective-permute-done.2.rest_3_
  25.9 1.4 %all-to-all-done.restricted_ref = f32[4,520,128]{2,1,0:T(8,128)S(1)} async-done(((f32[4,520,128]{2,1,0:T(8,128)}), f32[4,520,128]{2,1,0:T(8,128)S(1)}, u32[]{:S(2)}, u32[]{:S(2)}) %all-to-all-start) | async-done | bytes 1064992 | tf_op jit(solution)/shard_map/all_to_all | solution.py:288
  27.3 1.8 %combine.1 = f32[8,64,128]{2,1,0:T(8,128)S(1)} custom-call(s32[1,10]{1,0:T(1,128)S(1)} %add_bitcast_fusion.own_ref, f32[4,520,128]{2,1,0:T(8,128)S(1)} %all-to-all-done.restricted_ref, f32[512,128]{1,0:T(8,128)S(1)} %copy-done, f32[512,128]{1,0:T(8,128)S(1)} %collective-permute-done.rest_1_, f32[512,128]{1,0:T(8,128)S(1)} %collective-permute-done.1.next_ref.rest_2_, ...), custom_call_target="tpu_custom_call" | custom-call | flops 268435456 | bytes 4194304 | tf_op jit(solution)/shard_map/combine/pallas_call | solution.py:204
  29.1 1.5 %collective-permute-start.8 = (f32[2,64,128]{2,1,0:T(8,128)S(1)}, f32[2,64,128]{2,1,0:T(8,128)S(1)}, u32[]{:S(2)}, u32[]{:S(2)}) collective-permute-start(f32[2,64,128]{2,1,0:T(8,128)S(1)} %get-tuple-element.11), channel_id=1, source_target_pairs={{0,1},{1,0},{2,3},{3,2},{4,5},{5,4},{6,7},{7,6},{8,9},{9,8},{10,11... | collective-permute-start | bytes 196616 | tf_op jit(solution)/shard_map/ppermute | solution.py:254
  30.6 1.4 %collective-permute-start.10 = (f32[2,64,128]{2,1,0:T(8,128)S(1)}, f32[2,64,128]{2,1,0:T(8,128)S(1)}, u32[]{:S(2)}, u32[]{:S(2)}) collective-permute-start(f32[2,64,128]{2,1,0:T(8,128)S(1)} %get-tuple-element.12), channel_id=1, source_target_pairs={{0,3},{1,2},{2,1},{3,0},{4,7},{5,6},{6,5},{7,4},{8,11},{9,10},{10,... | collective-permute-start | bytes 196616 | tf_op jit(solution)/shard_map/ppermute | solution.py:254
  32.0 0.6 %collective-permute-start.9 = (f32[2,64,128]{2,1,0:T(8,128)S(1)}, f32[2,64,128]{2,1,0:T(8,128)S(1)}, u32[]{:S(2)}, u32[]{:S(2)}) collective-permute-start(f32[2,64,128]{2,1,0:T(8,128)S(1)} %get-tuple-element.13), channel_id=1, source_target_pairs={{0,2},{1,3},{2,0},{3,1},{4,6},{5,7},{6,4},{7,5},{8,10},{9,11},{10,... | collective-permute-start | bytes 196616 | tf_op jit(solution)/shard_map/ppermute | solution.py:254
  32.6 1.4 %collective-permute-done.8 = f32[2,64,128]{2,1,0:T(8,128)S(1)} collective-permute-done((f32[2,64,128]{2,1,0:T(8,128)S(1)}, f32[2,64,128]{2,1,0:T(8,128)S(1)}, u32[]{:S(2)}, u32[]{:S(2)}) %collective-permute-start.8) | collective-permute-done | bytes 65568 | tf_op jit(solution)/shard_map/ppermute | solution.py:254
  34.0 1.8 %collective-permute-done.10 = f32[2,64,128]{2,1,0:T(8,128)S(1)} collective-permute-done((f32[2,64,128]{2,1,0:T(8,128)S(1)}, f32[2,64,128]{2,1,0:T(8,128)S(1)}, u32[]{:S(2)}, u32[]{:S(2)}) %collective-permute-start.10) | collective-permute-done | bytes 65568 | tf_op jit(solution)/shard_map/ppermute | solution.py:254
  35.8 0.5 %collective-permute-done.9 = f32[2,64,128]{2,1,0:T(8,128)S(1)} collective-permute-done((f32[2,64,128]{2,1,0:T(8,128)S(1)}, f32[2,64,128]{2,1,0:T(8,128)S(1)}, u32[]{:S(2)}, u32[]{:S(2)}) %collective-permute-start.9) | collective-permute-done | bytes 65568 | tf_op jit(solution)/shard_map/ppermute | solution.py:254
  36.3 2.6 %collective-permute-start.11 = (f32[64,128]{1,0:T(8,128)S(1)}, f32[64,128]{1,0:T(8,128)S(1)}, u32[]{:S(2)}, u32[]{:S(2)}) collective-permute-start(f32[64,128]{1,0:T(8,128)S(1)} %slice_bitcast_fusion), channel_id=1, source_target_pairs={{0,4},{4,0},{1,5},{5,1},{2,6},{6,2},{3,7},{7,3},{8,12},{12,8},{9,1... | collective-permute-start | bytes 98312 | tf_op jit(solution)/shard_map/ppermute | solution.py:226
  38.9 2.3 %collective-permute-done.11 = f32[64,128]{1,0:T(8,128)S(1)} collective-permute-done((f32[64,128]{1,0:T(8,128)S(1)}, f32[64,128]{1,0:T(8,128)S(1)}, u32[]{:S(2)}, u32[]{:S(2)}) %collective-permute-start.11) | collective-permute-done | bytes 32800 | tf_op jit(solution)/shard_map/ppermute | solution.py:226
  41.2 0.6 %fusion.3 = f32[128,64]{0,1:T(8,128)} fusion(f32[64,128]{1,0:T(8,128)S(1)} %collective-permute-done.11, f32[2,64,128]{2,1,0:T(8,128)S(1)} %fusion.1), kind=kLoop, calls=%fused_computation.6 | loop fusion | flops 8192 | bytes 98304 | tf_op jit(solution)/shard_map/transpose | solution.py:294
  (16 shorter events, 0.1 us)
Async XLA Ops:
  0.0 15.7 %collective-permute-start.4 = (f32[512,128]{1,0:T(8,128)}, f32[512,128]{1,0:T(8,128)S(1)}, u32[]{:S(2)}, u32[]{:S(2)}) collective-permute-start(f32[512,128]{1,0:T(8,128)} %bitcast.20), channel_id=1, source_target_pairs={{0,6},{1,7},{2,4},{3,5},{4,2},{5,3},{6,0},{7,1},{8,14},{9,15},{10,... | collective-permute-start | bytes 786440 | tf_op jit(solution)/shard_map/ppermute | solution.py:232
  8.6 8.0 %collective-permute-start.1 = (f32[512,128]{1,0:T(8,128)}, f32[512,128]{1,0:T(8,128)S(1)}, u32[]{:S(2)}, u32[]{:S(2)}) collective-permute-start(f32[512,128]{1,0:T(8,128)} %get-tuple-element.9.rest_0_), channel_id=1, source_target_pairs={{0,16},{8,24},{16,0},{24,8},{1,17},{9,25},{17,1},{25,9},{2,18},{10... | collective-permute-start | bytes 786440 | tf_op jit(solution)/shard_map/ppermute | solution.py:222
  10.1 5.6 %collective-permute-start.3 = (s32[2,8]{1,0:T(2,128)}, s32[2,8]{1,0:T(2,128)S(1)}, u32[]{:S(2)}, u32[]{:S(2)}) collective-permute-start(s32[2,8]{1,0:T(2,128)} %get-tuple-element.10.own_columns_ref), channel_id=1, source_target_pairs={{0,6},{1,7},{2,4},{3,5},{4,2},{5,3},{6,0},{7,1},{8,14},{9,15},{10,... | collective-permute-start | bytes 200 | tf_op jit(solution)/shard_map/ppermute | solution.py:232
  10.4 5.4 %copy-start.1 = (s32[2,8]{1,0:T(2,128)S(1)}, s32[2,8]{1,0:T(2,128)}, u32[]{:S(2)}) copy-start(s32[2,8]{1,0:T(2,128)} %get-tuple-element.10.own_columns_ref) | copy-start | bytes 196
  10.4 16.9 %all-to-all-start = ((f32[4,520,128]{2,1,0:T(8,128)}), f32[4,520,128]{2,1,0:T(8,128)S(1)}, u32[]{:S(2)}, u32[]{:S(2)}) async-start(f32[4,520,128]{2,1,0:T(8,128)} %get-tuple-element.8), calls=%async_computation | async-start | bytes 2129920 | tf_op jit(solution)/shard_map/all_to_all | solution.py:288
  15.7 7.9 %copy-start = (f32[512,128]{1,0:T(8,128)S(1)}, f32[512,128]{1,0:T(8,128)}, u32[]{:S(2)}) copy-start(f32[512,128]{1,0:T(8,128)} %get-tuple-element.9.rest_0_) | copy-start | bytes 786436
  16.6 7.0 %collective-permute-start.6 = (f32[520,128]{1,0:T(8,128)S(1)}, f32[520,128]{1,0:T(8,128)S(1)}, u32[]{:S(2)}, u32[]{:S(2)}) collective-permute-start(f32[520,128]{1,0:T(8,128)S(1)} %append_columns.1.rest_4_), channel_id=1, source_target_pairs={{0,16},{8,24},{16,0},{24,8},{1,17},{9,25},{17,1},{25,9},{2,18},{10... | collective-permute-start | bytes 798728 | tf_op jit(solution)/shard_map/ppermute | solution.py:222
  18.2 7.7 %collective-permute-start.5 = (f32[520,128]{1,0:T(8,128)S(1)}, f32[520,128]{1,0:T(8,128)S(1)}, u32[]{:S(2)}, u32[]{:S(2)}) collective-permute-start(f32[520,128]{1,0:T(8,128)S(1)} %append_columns.1.rest_4_), channel_id=1, source_target_pairs={{0,8},{8,0},{16,24},{24,16},{1,9},{9,1},{17,25},{25,17},{2,10},{10... | collective-permute-start | bytes 798728 | tf_op jit(solution)/shard_map/ppermute | solution.py:222
  23.6 2.3 %collective-permute-start.7 = (f32[520,128]{1,0:T(8,128)S(1)}, f32[520,128]{1,0:T(8,128)S(1)}, u32[]{:S(2)}, u32[]{:S(2)}) collective-permute-start(f32[520,128]{1,0:T(8,128)S(1)} %collective-permute-done.6.rest_6_), channel_id=1, source_target_pairs={{0,8},{8,0},{16,24},{24,16},{1,9},{9,1},{17,25},{25,17},{2,10},{10... | collective-permute-start | bytes 798728 | tf_op jit(solution)/shard_map/ppermute | solution.py:222
  23.6 1.9 %collective-permute-start = (f32[512,128]{1,0:T(8,128)S(1)}, f32[512,128]{1,0:T(8,128)S(1)}, u32[]{:S(2)}, u32[]{:S(2)}) collective-permute-start(f32[512,128]{1,0:T(8,128)S(1)} %copy-done), channel_id=1, source_target_pairs={{0,8},{8,0},{16,24},{24,16},{1,9},{9,1},{17,25},{25,17},{2,10},{10... | collective-permute-start | bytes 786440 | tf_op jit(solution)/shard_map/ppermute | solution.py:222
  24.1 1.8 %collective-permute-start.2 = (f32[512,128]{1,0:T(8,128)S(1)}, f32[512,128]{1,0:T(8,128)S(1)}, u32[]{:S(2)}, u32[]{:S(2)}) collective-permute-start(f32[512,128]{1,0:T(8,128)S(1)} %collective-permute-done.1.next_ref.rest_2_), channel_id=1, source_target_pairs={{0,8},{8,0},{16,24},{24,16},{1,9},{9,1},{17,25},{25,17},{2,10},{10... | collective-permute-start | bytes 786440 | tf_op jit(solution)/shard_map/ppermute | solution.py:222
  29.1 4.9 %collective-permute-start.8 = (f32[2,64,128]{2,1,0:T(8,128)S(1)}, f32[2,64,128]{2,1,0:T(8,128)S(1)}, u32[]{:S(2)}, u32[]{:S(2)}) collective-permute-start(f32[2,64,128]{2,1,0:T(8,128)S(1)} %get-tuple-element.11), channel_id=1, source_target_pairs={{0,1},{1,0},{2,3},{3,2},{4,5},{5,4},{6,7},{7,6},{8,9},{9,8},{10,11... | collective-permute-start | bytes 196616 | tf_op jit(solution)/shard_map/ppermute | solution.py:254
  30.6 5.2 %collective-permute-start.10 = (f32[2,64,128]{2,1,0:T(8,128)S(1)}, f32[2,64,128]{2,1,0:T(8,128)S(1)}, u32[]{:S(2)}, u32[]{:S(2)}) collective-permute-start(f32[2,64,128]{2,1,0:T(8,128)S(1)} %get-tuple-element.12), channel_id=1, source_target_pairs={{0,3},{1,2},{2,1},{3,0},{4,7},{5,6},{6,5},{7,4},{8,11},{9,10},{10,... | collective-permute-start | bytes 196616 | tf_op jit(solution)/shard_map/ppermute | solution.py:254
  32.0 4.3 %collective-permute-start.9 = (f32[2,64,128]{2,1,0:T(8,128)S(1)}, f32[2,64,128]{2,1,0:T(8,128)S(1)}, u32[]{:S(2)}, u32[]{:S(2)}) collective-permute-start(f32[2,64,128]{2,1,0:T(8,128)S(1)} %get-tuple-element.13), channel_id=1, source_target_pairs={{0,2},{1,3},{2,0},{3,1},{4,6},{5,7},{6,4},{7,5},{8,10},{9,11},{10,... | collective-permute-start | bytes 196616 | tf_op jit(solution)/shard_map/ppermute | solution.py:254
  36.3 4.9 %collective-permute-start.11 = (f32[64,128]{1,0:T(8,128)S(1)}, f32[64,128]{1,0:T(8,128)S(1)}, u32[]{:S(2)}, u32[]{:S(2)}) collective-permute-start(f32[64,128]{1,0:T(8,128)S(1)} %slice_bitcast_fusion), channel_id=1, source_target_pairs={{0,4},{4,0},{1,5},{5,1},{2,6},{6,2},{3,7},{7,3},{8,12},{12,8},{9,1... | collective-permute-start | bytes 98312 | tf_op jit(solution)/shard_map/ppermute | solution.py:226

commit v21 on v20

--- a/solution.py
+++ b/solution.py
@@ -12,7 +12,7 @@
 LANES = 128
 EXTRA = 8
 HOLD_FLOPS = 16 << 30
-COLUMN_FLOPS = 3 << 29
+COLUMN_FLOPS = 9 << 28
 VMEM_LIMIT = 48 * 1024 * 1024
 
 

time: 42 us -> 42 us (level)
  no operation moved by 1% of the time
where the time goes in v21:
time: 42 us; the launch traced here: 41.8 us
  starting transfers between devices  18.8 us (45%)
  waiting for transfers between devices  17 us (40%)
  Pallas kernels  5.27 us (13%)
  other arithmetic  0.73 us (2%)
    ppermute x6, waiting for transfers between devices, row_swap(): lax.ppermute(x, 'row', [(r, r ^ bit) for r in range(lax.axis_size('row'))])  7.97 us
    ppermute x2, starting transfers between devices, far_swap(): return lax.ppermute(x, ('half', 'near'), pairs)  5.28 us
    ppermute x6, starting transfers between devices, row_swap(): lax.ppermute(x, 'row', [(r, r ^ bit) for r in range(lax.axis_size('row'))])  3.68 us
    ppermute x3, waiting for transfers between devices, add_over_columns(): lax.ppermute(sums[2 * near:2 * near + 2], 'near', [(n, n ^ near) for n in...  3.65 us
    all_to_all x1, starting transfers between devices, local(): lax.all_to_all(restricted, 'near', split_axis=0, concat_axis=0, tiled=True)  3.65 us
    ppermute x3, starting transfers between devices, add_over_columns(): lax.ppermute(sums[2 * near:2 * near + 2], 'near', [(n, n ^ near) for n in...  3.55 us
    pallas_call x1, Pallas kernels, restrict_operator(): pl.pallas_call(restrict_kernel, out_shape=(jax.ShapeDtypeStruct((columns...  3.49 us
    ppermute x1, starting transfers between devices, half_swap(): return lax.ppermute(x, 'half', [(0, 1), (1, 0)])  2.6 us
  transfers between devices with their start and end apart: 13, of which 10 were waited for; matrix products, arithmetic and copies ran while one was open for 0% of the time, Pallas kernels for 8%

profile of v21, /device:TPU:0, one launch (start us, length us, event | category | flops | bytes accessed | tf_op | source)
XLA Modules:
  0.0 41.8 jit_solution(9116719838305381452)
XLA Ops:
  0.0 5.0 %collective-permute-start.4 = (f32[512,128]{1,0:T(8,128)}, f32[512,128]{1,0:T(8,128)S(1)}, u32[]{:S(2)}, u32[]{:S(2)}) collective-permute-start(f32[512,128]{1,0:T(8,128)} %bitcast.20), channel_id=1, source_target_pairs={{0,6},{1,7},{2,4},{3,5},{4,2},{5,3},{6,0},{7,1},{8,14},{9,15},{10,... | collective-permute-start | bytes 786440 | tf_op jit(solution)/shard_map/ppermute | solution.py:232
  5.0 3.5 %restrict_operator.1 = (f32[4,520,128]{2,1,0:T(8,128)}, s32[2,8]{1,0:T(2,128)}, f32[512,128]{1,0:T(8,128)}) custom-call(s32[8]{0:T(128)} %count_any.1, s32[8,8]{1,0:T(8,128)} %slot_any.1, s32[2,8]{1,0:T(2,128)} %bitcast.23, s32[4,8]{1,0:T(4,128)} %bitcast.22, f32[8,64,128]{2,1,0:T(8,128)} %restrict_any.1, f32[8,64,512]{2,1,0:T(8,128)} %operator_any.1, ...), custom_call_target="tpu_custom_call" | custom-call | flops 201326592 | bytes 4194304 | tf_op jit(solution)/shard_map/restrict_operator/pallas_call | solution.py:138
  8.6 1.6 %collective-permute-start.1 = (f32[512,128]{1,0:T(8,128)}, f32[512,128]{1,0:T(8,128)S(1)}, u32[]{:S(2)}, u32[]{:S(2)}) collective-permute-start(f32[512,128]{1,0:T(8,128)} %get-tuple-element.9.rest_0_), channel_id=1, source_target_pairs={{0,16},{8,24},{16,0},{24,8},{1,17},{9,25},{17,1},{25,9},{2,18},{10... | collective-permute-start | bytes 786440 | tf_op jit(solution)/shard_map/ppermute | solution.py:222
  10.1 0.2 collective-permute-start.3
  10.4 3.6 %all-to-all-start = ((f32[4,520,128]{2,1,0:T(8,128)}), f32[4,520,128]{2,1,0:T(8,128)S(1)}, u32[]{:S(2)}, u32[]{:S(2)}) async-start(f32[4,520,128]{2,1,0:T(8,128)} %get-tuple-element.8), calls=%async_computation | async-start | bytes 2129920 | tf_op jit(solution)/shard_map/all_to_all | solution.py:288
  14.0 1.7 %collective-permute-done.3.far_columns_ref = s32[2,8]{1,0:T(2,128)S(1)} collective-permute-done((s32[2,8]{1,0:T(2,128)}, s32[2,8]{1,0:T(2,128)S(1)}, u32[]{:S(2)}, u32[]{:S(2)}) %collective-permute-start.3) | collective-permute-done | bytes 96 | tf_op jit(solution)/shard_map/ppermute | solution.py:232
  15.7 0.9 %collective-permute-done.1.next_ref.rest_2_ = f32[512,128]{1,0:T(8,128)S(1)} collective-permute-done((f32[512,128]{1,0:T(8,128)}, f32[512,128]{1,0:T(8,128)S(1)}, u32[]{:S(2)}, u32[]{:S(2)}) %collective-permute-start.1) | collective-permute-done | bytes 262176 | tf_op jit(solution)/shard_map/ppermute | solution.py:222
  16.6 1.6 %collective-permute-start.6 = (f32[520,128]{1,0:T(8,128)S(1)}, f32[520,128]{1,0:T(8,128)S(1)}, u32[]{:S(2)}, u32[]{:S(2)}) collective-permute-start(f32[520,128]{1,0:T(8,128)S(1)} %append_columns.1.rest_4_), channel_id=1, source_target_pairs={{0,16},{8,24},{16,0},{24,8},{1,17},{9,25},{17,1},{25,9},{2,18},{10... | collective-permute-start | bytes 798728 | tf_op jit(solution)/shard_map/ppermute | solution.py:222
  18.2 5.4 %collective-permute-done.6.rest_6_ = f32[520,128]{1,0:T(8,128)S(1)} collective-permute-done((f32[520,128]{1,0:T(8,128)S(1)}, f32[520,128]{1,0:T(8,128)S(1)}, u32[]{:S(2)}, u32[]{:S(2)}) %collective-permute-start.6) | collective-permute-done | bytes 266272 | tf_op jit(solution)/shard_map/ppermute | solution.py:222
  23.6 0.5 %collective-permute-start = (f32[512,128]{1,0:T(8,128)S(1)}, f32[512,128]{1,0:T(8,128)S(1)}, u32[]{:S(2)}, u32[]{:S(2)}) collective-permute-start(f32[512,128]{1,0:T(8,128)S(1)} %copy-done), channel_id=1, source_target_pairs={{0,8},{8,0},{16,24},{24,16},{1,9},{9,1},{17,25},{25,17},{2,10},{10... | collective-permute-start | bytes 786440 | tf_op jit(solution)/shard_map/ppermute | solution.py:222
  24.2 0.1 add_bitcast_fusion.own_ref
  24.2 1.3 %collective-permute-done.rest_1_ = f32[512,128]{1,0:T(8,128)S(1)} collective-permute-done((f32[512,128]{1,0:T(8,128)S(1)}, f32[512,128]{1,0:T(8,128)S(1)}, u32[]{:S(2)}, u32[]{:S(2)}) %collective-permute-start) | collective-permute-done | bytes 262176 | tf_op jit(solution)/shard_map/ppermute | solution.py:222
  25.5 0.4 collective-permute-done.2.rest_3_
  25.9 1.4 %all-to-all-done.restricted_ref = f32[4,520,128]{2,1,0:T(8,128)S(1)} async-done(((f32[4,520,128]{2,1,0:T(8,128)}), f32[4,520,128]{2,1,0:T(8,128)S(1)}, u32[]{:S(2)}, u32[]{:S(2)}) %all-to-all-start) | async-done | bytes 1064992 | tf_op jit(solution)/shard_map/all_to_all | solution.py:288
  27.3 1.8 %combine.1 = f32[8,64,128]{2,1,0:T(8,128)S(1)} custom-call(s32[1,10]{1,0:T(1,128)S(1)} %add_bitcast_fusion.own_ref, f32[4,520,128]{2,1,0:T(8,128)S(1)} %all-to-all-done.restricted_ref, f32[512,128]{1,0:T(8,128)S(1)} %copy-done, f32[512,128]{1,0:T(8,128)S(1)} %collective-permute-done.rest_1_, f32[512,128]{1,0:T(8,128)S(1)} %collective-permute-done.1.next_ref.rest_2_, ...), custom_call_target="tpu_custom_call" | custom-call | flops 268435456 | bytes 4194304 | tf_op jit(solution)/shard_map/combine/pallas_call | solution.py:204
  29.1 1.5 %collective-permute-start.8 = (f32[2,64,128]{2,1,0:T(8,128)S(1)}, f32[2,64,128]{2,1,0:T(8,128)S(1)}, u32[]{:S(2)}, u32[]{:S(2)}) collective-permute-start(f32[2,64,128]{2,1,0:T(8,128)S(1)} %get-tuple-element.11), channel_id=1, source_target_pairs={{0,1},{1,0},{2,3},{3,2},{4,5},{5,4},{6,7},{7,6},{8,9},{9,8},{10,11... | collective-permute-start | bytes 196616 | tf_op jit(solution)/shard_map/ppermute | solution.py:254
  30.6 1.4 %collective-permute-start.10 = (f32[2,64,128]{2,1,0:T(8,128)S(1)}, f32[2,64,128]{2,1,0:T(8,128)S(1)}, u32[]{:S(2)}, u32[]{:S(2)}) collective-permute-start(f32[2,64,128]{2,1,0:T(8,128)S(1)} %get-tuple-element.12), channel_id=1, source_target_pairs={{0,3},{1,2},{2,1},{3,0},{4,7},{5,6},{6,5},{7,4},{8,11},{9,10},{10,... | collective-permute-start | bytes 196616 | tf_op jit(solution)/shard_map/ppermute | solution.py:254
  32.0 0.6 %collective-permute-start.9 = (f32[2,64,128]{2,1,0:T(8,128)S(1)}, f32[2,64,128]{2,1,0:T(8,128)S(1)}, u32[]{:S(2)}, u32[]{:S(2)}) collective-permute-start(f32[2,64,128]{2,1,0:T(8,128)S(1)} %get-tuple-element.13), channel_id=1, source_target_pairs={{0,2},{1,3},{2,0},{3,1},{4,6},{5,7},{6,4},{7,5},{8,10},{9,11},{10,... | collective-permute-start | bytes 196616 | tf_op jit(solution)/shard_map/ppermute | solution.py:254
  32.6 1.4 %collective-permute-done.8 = f32[2,64,128]{2,1,0:T(8,128)S(1)} collective-permute-done((f32[2,64,128]{2,1,0:T(8,128)S(1)}, f32[2,64,128]{2,1,0:T(8,128)S(1)}, u32[]{:S(2)}, u32[]{:S(2)}) %collective-permute-start.8) | collective-permute-done | bytes 65568 | tf_op jit(solution)/shard_map/ppermute | solution.py:254
  34.0 1.7 %collective-permute-done.10 = f32[2,64,128]{2,1,0:T(8,128)S(1)} collective-permute-done((f32[2,64,128]{2,1,0:T(8,128)S(1)}, f32[2,64,128]{2,1,0:T(8,128)S(1)}, u32[]{:S(2)}, u32[]{:S(2)}) %collective-permute-start.10) | collective-permute-done | bytes 65568 | tf_op jit(solution)/shard_map/ppermute | solution.py:254
  35.8 0.5 %collective-permute-done.9 = f32[2,64,128]{2,1,0:T(8,128)S(1)} collective-permute-done((f32[2,64,128]{2,1,0:T(8,128)S(1)}, f32[2,64,128]{2,1,0:T(8,128)S(1)}, u32[]{:S(2)}, u32[]{:S(2)}) %collective-permute-start.9) | collective-permute-done | bytes 65568 | tf_op jit(solution)/shard_map/ppermute | solution.py:254
  36.3 2.6 %collective-permute-start.11 = (f32[64,128]{1,0:T(8,128)S(1)}, f32[64,128]{1,0:T(8,128)S(1)}, u32[]{:S(2)}, u32[]{:S(2)}) collective-permute-start(f32[64,128]{1,0:T(8,128)S(1)} %slice_bitcast_fusion), channel_id=1, source_target_pairs={{0,4},{4,0},{1,5},{5,1},{2,6},{6,2},{3,7},{7,3},{8,12},{12,8},{9,1... | collective-permute-start | bytes 98312 | tf_op jit(solution)/shard_map/ppermute | solution.py:226
  38.9 2.3 %collective-permute-done.11 = f32[64,128]{1,0:T(8,128)S(1)} collective-permute-done((f32[64,128]{1,0:T(8,128)S(1)}, f32[64,128]{1,0:T(8,128)S(1)}, u32[]{:S(2)}, u32[]{:S(2)}) %collective-permute-start.11) | collective-permute-done | bytes 32800 | tf_op jit(solution)/shard_map/ppermute | solution.py:226
  41.2 0.6 %fusion.3 = f32[128,64]{0,1:T(8,128)} fusion(f32[64,128]{1,0:T(8,128)S(1)} %collective-permute-done.11, f32[2,64,128]{2,1,0:T(8,128)S(1)} %fusion.1), kind=kLoop, calls=%fused_computation.6 | loop fusion | flops 8192 | bytes 98304 | tf_op jit(solution)/shard_map/transpose | solution.py:294
  (16 shorter events, 0.1 us)
Async XLA Ops:
  0.0 15.7 %collective-permute-start.4 = (f32[512,128]{1,0:T(8,128)}, f32[512,128]{1,0:T(8,128)S(1)}, u32[]{:S(2)}, u32[]{:S(2)}) collective-permute-start(f32[512,128]{1,0:T(8,128)} %bitcast.20), channel_id=1, source_target_pairs={{0,6},{1,7},{2,4},{3,5},{4,2},{5,3},{6,0},{7,1},{8,14},{9,15},{10,... | collective-permute-start | bytes 786440 | tf_op jit(solution)/shard_map/ppermute | solution.py:232
  8.6 8.0 %collective-permute-start.1 = (f32[512,128]{1,0:T(8,128)}, f32[512,128]{1,0:T(8,128)S(1)}, u32[]{:S(2)}, u32[]{:S(2)}) collective-permute-start(f32[512,128]{1,0:T(8,128)} %get-tuple-element.9.rest_0_), channel_id=1, source_target_pairs={{0,16},{8,24},{16,0},{24,8},{1,17},{9,25},{17,1},{25,9},{2,18},{10... | collective-permute-start | bytes 786440 | tf_op jit(solution)/shard_map/ppermute | solution.py:222
  10.1 5.6 %collective-permute-start.3 = (s32[2,8]{1,0:T(2,128)}, s32[2,8]{1,0:T(2,128)S(1)}, u32[]{:S(2)}, u32[]{:S(2)}) collective-permute-start(s32[2,8]{1,0:T(2,128)} %get-tuple-element.10.own_columns_ref), channel_id=1, source_target_pairs={{0,6},{1,7},{2,4},{3,5},{4,2},{5,3},{6,0},{7,1},{8,14},{9,15},{10,... | collective-permute-start | bytes 200 | tf_op jit(solution)/shard_map/ppermute | solution.py:232
  10.4 5.4 %copy-start.1 = (s32[2,8]{1,0:T(2,128)S(1)}, s32[2,8]{1,0:T(2,128)}, u32[]{:S(2)}) copy-start(s32[2,8]{1,0:T(2,128)} %get-tuple-element.10.own_columns_ref) | copy-start | bytes 196
  10.4 16.9 %all-to-all-start = ((f32[4,520,128]{2,1,0:T(8,128)}), f32[4,520,128]{2,1,0:T(8,128)S(1)}, u32[]{:S(2)}, u32[]{:S(2)}) async-start(f32[4,520,128]{2,1,0:T(8,128)} %get-tuple-element.8), calls=%async_computation | async-start | bytes 2129920 | tf_op jit(solution)/shard_map/all_to_all | solution.py:288
  15.7 7.9 %copy-start = (f32[512,128]{1,0:T(8,128)S(1)}, f32[512,128]{1,0:T(8,128)}, u32[]{:S(2)}) copy-start(f32[512,128]{1,0:T(8,128)} %get-tuple-element.9.rest_0_) | copy-start | bytes 786436
  16.6 7.0 %collective-permute-start.6 = (f32[520,128]{1,0:T(8,128)S(1)}, f32[520,128]{1,0:T(8,128)S(1)}, u32[]{:S(2)}, u32[]{:S(2)}) collective-permute-start(f32[520,128]{1,0:T(8,128)S(1)} %append_columns.1.rest_4_), channel_id=1, source_target_pairs={{0,16},{8,24},{16,0},{24,8},{1,17},{9,25},{17,1},{25,9},{2,18},{10... | collective-permute-start | bytes 798728 | tf_op jit(solution)/shard_map/ppermute | solution.py:222
  18.2 7.7 %collective-permute-start.5 = (f32[520,128]{1,0:T(8,128)S(1)}, f32[520,128]{1,0:T(8,128)S(1)}, u32[]{:S(2)}, u32[]{:S(2)}) collective-permute-start(f32[520,128]{1,0:T(8,128)S(1)} %append_columns.1.rest_4_), channel_id=1, source_target_pairs={{0,8},{8,0},{16,24},{24,16},{1,9},{9,1},{17,25},{25,17},{2,10},{10... | collective-permute-start | bytes 798728 | tf_op jit(solution)/shard_map/ppermute | solution.py:222
  23.6 2.3 %collective-permute-start.7 = (f32[520,128]{1,0:T(8,128)S(1)}, f32[520,128]{1,0:T(8,128)S(1)}, u32[]{:S(2)}, u32[]{:S(2)}) collective-permute-start(f32[520,128]{1,0:T(8,128)S(1)} %collective-permute-done.6.rest_6_), channel_id=1, source_target_pairs={{0,8},{8,0},{16,24},{24,16},{1,9},{9,1},{17,25},{25,17},{2,10},{10... | collective-permute-start | bytes 798728 | tf_op jit(solution)/shard_map/ppermute | solution.py:222
  23.6 1.9 %collective-permute-start = (f32[512,128]{1,0:T(8,128)S(1)}, f32[512,128]{1,0:T(8,128)S(1)}, u32[]{:S(2)}, u32[]{:S(2)}) collective-permute-start(f32[512,128]{1,0:T(8,128)S(1)} %copy-done), channel_id=1, source_target_pairs={{0,8},{8,0},{16,24},{24,16},{1,9},{9,1},{17,25},{25,17},{2,10},{10... | collective-permute-start | bytes 786440 | tf_op jit(solution)/shard_map/ppermute | solution.py:222
  24.1 1.8 %collective-permute-start.2 = (f32[512,128]{1,0:T(8,128)S(1)}, f32[512,128]{1,0:T(8,128)S(1)}, u32[]{:S(2)}, u32[]{:S(2)}) collective-permute-start(f32[512,128]{1,0:T(8,128)S(1)} %collective-permute-done.1.next_ref.rest_2_), channel_id=1, source_target_pairs={{0,8},{8,0},{16,24},{24,16},{1,9},{9,1},{17,25},{25,17},{2,10},{10... | collective-permute-start | bytes 786440 | tf_op jit(solution)/shard_map/ppermute | solution.py:222
  29.1 5.0 %collective-permute-start.8 = (f32[2,64,128]{2,1,0:T(8,128)S(1)}, f32[2,64,128]{2,1,0:T(8,128)S(1)}, u32[]{:S(2)}, u32[]{:S(2)}) collective-permute-start(f32[2,64,128]{2,1,0:T(8,128)S(1)} %get-tuple-element.11), channel_id=1, source_target_pairs={{0,1},{1,0},{2,3},{3,2},{4,5},{5,4},{6,7},{7,6},{8,9},{9,8},{10,11... | collective-permute-start | bytes 196616 | tf_op jit(solution)/shard_map/ppermute | solution.py:254
  30.6 5.2 %collective-permute-start.10 = (f32[2,64,128]{2,1,0:T(8,128)S(1)}, f32[2,64,128]{2,1,0:T(8,128)S(1)}, u32[]{:S(2)}, u32[]{:S(2)}) collective-permute-start(f32[2,64,128]{2,1,0:T(8,128)S(1)} %get-tuple-element.12), channel_id=1, source_target_pairs={{0,3},{1,2},{2,1},{3,0},{4,7},{5,6},{6,5},{7,4},{8,11},{9,10},{10,... | collective-permute-start | bytes 196616 | tf_op jit(solution)/shard_map/ppermute | solution.py:254
  32.0 4.3 %collective-permute-start.9 = (f32[2,64,128]{2,1,0:T(8,128)S(1)}, f32[2,64,128]{2,1,0:T(8,128)S(1)}, u32[]{:S(2)}, u32[]{:S(2)}) collective-permute-start(f32[2,64,128]{2,1,0:T(8,128)S(1)} %get-tuple-element.13), channel_id=1, source_target_pairs={{0,2},{1,3},{2,0},{3,1},{4,6},{5,7},{6,4},{7,5},{8,10},{9,11},{10,... | collective-permute-start | bytes 196616 | tf_op jit(solution)/shard_map/ppermute | solution.py:254
  36.3 4.9 %collective-permute-start.11 = (f32[64,128]{1,0:T(8,128)S(1)}, f32[64,128]{1,0:T(8,128)S(1)}, u32[]{:S(2)}, u32[]{:S(2)}) collective-permute-start(f32[64,128]{1,0:T(8,128)S(1)} %slice_bitcast_fusion), channel_id=1, source_target_pairs={{0,4},{4,0},{1,5},{5,1},{2,6},{6,2},{3,7},{7,3},{8,12},{12,8},{9,1... | collective-permute-start | bytes 98312 | tf_op jit(solution)/shard_map/ppermute | solution.py:226

commit v22 on v18

--- a/solution.py
+++ b/solution.py
@@ -227,15 +227,19 @@
 
 def place_of_columns(half):
     own = lax.axis_index("half") * half + lax.axis_index("near")
-    ahead = jnp.arange(2 * half, dtype=jnp.int32) ^ own
-    return ahead % half * 2 + ahead // half
+    return jnp.arange(2 * half, dtype=jnp.int32) ^ own
+
+
+def add_over_near(sums, half):
+    total = sums[0]
+    for near in range(1, half):
+        total = total + lax.ppermute(sums[near], "near", [(n, n ^ near) for n in range(half)])
+    return total
 
 
 def add_over_columns(sums, half):
-    total = sums[:2]
-    for near in range(1, half):
-        total = total + lax.ppermute(sums[2 * near : 2 * near + 2], "near", [(n, n ^ near) for n in range(half)])
-    return total[0] + half_swap(total[1])
+    crossing = half_swap(add_over_near(sums[half:], half))
+    return add_over_near(sums[:half], half) + crossing
 
 
 def local(

time: 42 us -> 41.9 us (level)
  waiting for transfers between devices: 17 us -> 13.3 us
  starting transfers between devices: 18.8 us -> 22.2 us
    ppermute x3 -> x6, starting transfers between devices: 3.55 us -> 7.04 us  [add_over_near(): lax.ppermute(sums[near], 'near', [(n, n ^ near) for n in range(half)])]
    ppermute x3 -> x6, waiting for transfers between devices: 3.65 us -> 0.69 us  [add_over_near(): lax.ppermute(sums[near], 'near', [(n, n ^ near) for n in range(half)])]
    ppermute x1, waiting for transfers between devices: 2.29 us -> 1.6 us  [half_swap(): return lax.ppermute(x, 'half', [(0, 1), (1, 0)])]
  transfers between devices with their start and end apart: 13 -> 16, of which waited for: 10 -> 9; matrix products, arithmetic and copies ran while one was open for 0% -> 0% of each run, Pallas kernels for 8% -> 8%
where the time goes in v22:
time: 41.9 us; the launch traced here: 41.7 us
  starting transfers between devices  22.2 us (53%)
  waiting for transfers between devices  13.3 us (32%)
  Pallas kernels  5.26 us (13%)
  other arithmetic  0.72 us (2%)
    ppermute x6, waiting for transfers between devices, row_swap(): lax.ppermute(x, 'row', [(r, r ^ bit) for r in range(lax.axis_size('row'))])  7.99 us
    ppermute x6, starting transfers between devices, add_over_near(): lax.ppermute(sums[near], 'near', [(n, n ^ near) for n in range(half)])  7.04 us
    ppermute x2, starting transfers between devices, far_swap(): return lax.ppermute(x, ('half', 'near'), pairs)  5.27 us
    ppermute x6, starting transfers between devices, row_swap(): lax.ppermute(x, 'row', [(r, r ^ bit) for r in range(lax.axis_size('row'))])  3.68 us
    all_to_all x1, starting transfers between devices, local(): lax.all_to_all(restricted, 'near', split_axis=0, concat_axis=0, tiled=True)  3.65 us
    pallas_call x1, Pallas kernels, restrict_operator(): pl.pallas_call(restrict_kernel, out_shape=(jax.ShapeDtypeStruct((columns...  3.49 us
    ppermute x1, starting transfers between devices, half_swap(): return lax.ppermute(x, 'half', [(0, 1), (1, 0)])  2.6 us
    pallas_call x1, Pallas kernels, combine(): pl.pallas_call(functools.partial(combine_kernel, slot_count=slot_count, f...  1.76 us
  transfers between devices with their start and end apart: 16, of which 9 were waited for; matrix products, arithmetic and copies ran while one was open for 0% of the time, Pallas kernels for 8%

profile of v22, /device:TPU:0, one launch (start us, length us, event | category | flops | bytes accessed | tf_op | source)
XLA Modules:
  0.0 41.7 jit_solution(4445727217173617667)
XLA Ops:
  0.0 5.0 %collective-permute-start.4 = (f32[512,128]{1,0:T(8,128)}, f32[512,128]{1,0:T(8,128)S(1)}, u32[]{:S(2)}, u32[]{:S(2)}) collective-permute-start(f32[512,128]{1,0:T(8,128)} %bitcast.44), channel_id=1, source_target_pairs={{0,6},{1,7},{2,4},{3,5},{4,2},{5,3},{6,0},{7,1},{8,14},{9,15},{10,... | collective-permute-start | bytes 786440 | tf_op jit(solution)/shard_map/ppermute | solution.py:215
  5.0 3.5 %restrict_operator.1 = (f32[4,520,128]{2,1,0:T(8,128)}, s32[2,8]{1,0:T(2,128)}, f32[512,128]{1,0:T(8,128)}) custom-call(s32[8]{0:T(128)} %count_any.1, s32[8,8]{1,0:T(8,128)} %slot_any.1, s32[2,8]{1,0:T(2,128)} %bitcast.47, s32[4,8]{1,0:T(4,128)} %bitcast.46, f32[8,64,128]{2,1,0:T(8,128)} %restrict_any.1, f32[8,64,512]{2,1,0:T(8,128)} %operator_any.1, ...), custom_call_target="tpu_custom_call" | custom-call | flops 201326592 | bytes 4194304 | tf_op jit(solution)/shard_map/restrict_operator/pallas_call | solution.py:121
  8.5 1.6 %collective-permute-start.1 = (f32[512,128]{1,0:T(8,128)}, f32[512,128]{1,0:T(8,128)S(1)}, u32[]{:S(2)}, u32[]{:S(2)}) collective-permute-start(f32[512,128]{1,0:T(8,128)} %get-tuple-element.9.rest_0_), channel_id=1, source_target_pairs={{0,16},{8,24},{16,0},{24,8},{1,17},{9,25},{17,1},{25,9},{2,18},{10... | collective-permute-start | bytes 786440 | tf_op jit(solution)/shard_map/ppermute | solution.py:205
  10.1 0.2 collective-permute-start.3
  10.4 3.6 %all-to-all-start = ((f32[4,520,128]{2,1,0:T(8,128)}), f32[4,520,128]{2,1,0:T(8,128)S(1)}, u32[]{:S(2)}, u32[]{:S(2)}) async-start(f32[4,520,128]{2,1,0:T(8,128)} %get-tuple-element.8), calls=%async_computation | async-start | bytes 2129920 | tf_op jit(solution)/shard_map/all_to_all | solution.py:275
  14.0 1.7 %collective-permute-done.3.far_columns_ref = s32[2,8]{1,0:T(2,128)S(1)} collective-permute-done((s32[2,8]{1,0:T(2,128)}, s32[2,8]{1,0:T(2,128)S(1)}, u32[]{:S(2)}, u32[]{:S(2)}) %collective-permute-start.3) | collective-permute-done | bytes 96 | tf_op jit(solution)/shard_map/ppermute | solution.py:215
  15.7 0.9 %collective-permute-done.1.next_ref.rest_2_ = f32[512,128]{1,0:T(8,128)S(1)} collective-permute-done((f32[512,128]{1,0:T(8,128)}, f32[512,128]{1,0:T(8,128)S(1)}, u32[]{:S(2)}, u32[]{:S(2)}) %collective-permute-start.1) | collective-permute-done | bytes 262176 | tf_op jit(solution)/shard_map/ppermute | solution.py:205
  16.6 1.6 %collective-permute-start.6 = (f32[520,128]{1,0:T(8,128)S(1)}, f32[520,128]{1,0:T(8,128)S(1)}, u32[]{:S(2)}, u32[]{:S(2)}) collective-permute-start(f32[520,128]{1,0:T(8,128)S(1)} %append_columns.1.rest_4_), channel_id=1, source_target_pairs={{0,16},{8,24},{16,0},{24,8},{1,17},{9,25},{17,1},{25,9},{2,18},{10... | collective-permute-start | bytes 798728 | tf_op jit(solution)/shard_map/ppermute | solution.py:205
  18.2 5.4 %collective-permute-done.6.rest_6_ = f32[520,128]{1,0:T(8,128)S(1)} collective-permute-done((f32[520,128]{1,0:T(8,128)S(1)}, f32[520,128]{1,0:T(8,128)S(1)}, u32[]{:S(2)}, u32[]{:S(2)}) %collective-permute-start.6) | collective-permute-done | bytes 266272 | tf_op jit(solution)/shard_map/ppermute | solution.py:205
  23.6 0.5 %collective-permute-start = (f32[512,128]{1,0:T(8,128)S(1)}, f32[512,128]{1,0:T(8,128)S(1)}, u32[]{:S(2)}, u32[]{:S(2)}) collective-permute-start(f32[512,128]{1,0:T(8,128)S(1)} %copy-done), channel_id=1, source_target_pairs={{0,8},{8,0},{16,24},{24,16},{1,9},{9,1},{17,25},{25,17},{2,10},{10... | collective-permute-start | bytes 786440 | tf_op jit(solution)/shard_map/ppermute | solution.py:205
  24.2 1.3 %collective-permute-done.rest_1_ = f32[512,128]{1,0:T(8,128)S(1)} collective-permute-done((f32[512,128]{1,0:T(8,128)S(1)}, f32[512,128]{1,0:T(8,128)S(1)}, u32[]{:S(2)}, u32[]{:S(2)}) %collective-permute-start) | collective-permute-done | bytes 262176 | tf_op jit(solution)/shard_map/ppermute | solution.py:205
  25.5 0.4 collective-permute-done.2.rest_3_
  25.9 1.4 %all-to-all-done.restricted_ref = f32[4,520,128]{2,1,0:T(8,128)S(1)} async-done(((f32[4,520,128]{2,1,0:T(8,128)}), f32[4,520,128]{2,1,0:T(8,128)S(1)}, u32[]{:S(2)}, u32[]{:S(2)}) %all-to-all-start) | async-done | bytes 1064992 | tf_op jit(solution)/shard_map/all_to_all | solution.py:275
  27.3 1.8 %combine.1 = f32[8,64,128]{2,1,0:T(8,128)S(1)} custom-call(s32[1,10]{1,0:T(1,128)S(1)} %add_bitcast_fusion.own_ref, f32[4,520,128]{2,1,0:T(8,128)S(1)} %all-to-all-done.restricted_ref, f32[512,128]{1,0:T(8,128)S(1)} %copy-done, f32[512,128]{1,0:T(8,128)S(1)} %collective-permute-done.rest_1_, f32[512,128]{1,0:T(8,128)S(1)} %collective-permute-done.1.next_ref.rest_2_, ...), custom_call_target="tpu_custom_call" | custom-call | flops 268435456 | bytes 4194304 | tf_op jit(solution)/shard_map/combine/pallas_call | solution.py:187
  29.1 1.5 %collective-permute-start.13 = (f32[64,128]{1,0:T(8,128)S(1)}, f32[64,128]{1,0:T(8,128)S(1)}, u32[]{:S(2)}, u32[]{:S(2)}) collective-permute-start(f32[64,128]{1,0:T(8,128)S(1)} %get-tuple-element.12), channel_id=1, source_target_pairs={{0,3},{1,2},{2,1},{3,0},{4,7},{5,6},{6,5},{7,4},{8,11},{9,10},{10,... | collective-permute-start | bytes 98312 | tf_op jit(solution)/shard_map/ppermute | solution.py:236
  30.6 1.5 %collective-permute-start.12 = (f32[64,128]{1,0:T(8,128)S(1)}, f32[64,128]{1,0:T(8,128)S(1)}, u32[]{:S(2)}, u32[]{:S(2)}) collective-permute-start(f32[64,128]{1,0:T(8,128)S(1)} %get-tuple-element.13), channel_id=1, source_target_pairs={{0,2},{1,3},{2,0},{3,1},{4,6},{5,7},{6,4},{7,5},{8,10},{9,11},{10,... | collective-permute-start | bytes 98312 | tf_op jit(solution)/shard_map/ppermute | solution.py:236
  32.1 0.6 %collective-permute-start.11 = (f32[64,128]{1,0:T(8,128)S(1)}, f32[64,128]{1,0:T(8,128)S(1)}, u32[]{:S(2)}, u32[]{:S(2)}) collective-permute-start(f32[64,128]{1,0:T(8,128)S(1)} %get-tuple-element.14), channel_id=1, source_target_pairs={{0,1},{1,0},{2,3},{3,2},{4,5},{5,4},{6,7},{7,6},{8,9},{9,8},{10,11... | collective-permute-start | bytes 98312 | tf_op jit(solution)/shard_map/ppermute | solution.py:236
  32.6 1.5 %collective-permute-start.8 = (f32[64,128]{1,0:T(8,128)S(1)}, f32[64,128]{1,0:T(8,128)S(1)}, u32[]{:S(2)}, u32[]{:S(2)}) collective-permute-start(f32[64,128]{1,0:T(8,128)S(1)} %get-tuple-element.11), channel_id=1, source_target_pairs={{0,1},{1,0},{2,3},{3,2},{4,5},{5,4},{6,7},{7,6},{8,9},{9,8},{10,11... | collective-permute-start | bytes 98312 | tf_op jit(solution)/shard_map/ppermute | solution.py:236
  34.1 1.4 %collective-permute-start.10 = (f32[64,128]{1,0:T(8,128)S(1)}, f32[64,128]{1,0:T(8,128)S(1)}, u32[]{:S(2)}, u32[]{:S(2)}) collective-permute-start(f32[64,128]{1,0:T(8,128)S(1)} %get-tuple-element.15), channel_id=1, source_target_pairs={{0,3},{1,2},{2,1},{3,0},{4,7},{5,6},{6,5},{7,4},{8,11},{9,10},{10,... | collective-permute-start | bytes 98312 | tf_op jit(solution)/shard_map/ppermute | solution.py:236
  35.5 0.6 %collective-permute-start.9 = (f32[64,128]{1,0:T(8,128)S(1)}, f32[64,128]{1,0:T(8,128)S(1)}, u32[]{:S(2)}, u32[]{:S(2)}) collective-permute-start(f32[64,128]{1,0:T(8,128)S(1)} %get-tuple-element.16), channel_id=1, source_target_pairs={{0,2},{1,3},{2,0},{3,1},{4,6},{5,7},{6,4},{7,5},{8,10},{9,11},{10,... | collective-permute-start | bytes 98312 | tf_op jit(solution)/shard_map/ppermute | solution.py:236
  36.1 2.6 %collective-permute-start.14 = (f32[64,128]{1,0:T(8,128)S(1)}, f32[64,128]{1,0:T(8,128)S(1)}, u32[]{:S(2)}, u32[]{:S(2)}) collective-permute-start(f32[64,128]{1,0:T(8,128)S(1)} %fusion.2), channel_id=1, source_target_pairs={{0,4},{4,0},{1,5},{5,1},{2,6},{6,2},{3,7},{7,3},{8,12},{12,8},{9,1... | collective-permute-start | bytes 98312 | tf_op jit(solution)/shard_map/ppermute | solution.py:209
  38.9 0.5 %collective-permute-done.9 = f32[64,128]{1,0:T(8,128)S(1)} collective-permute-done((f32[64,128]{1,0:T(8,128)S(1)}, f32[64,128]{1,0:T(8,128)S(1)}, u32[]{:S(2)}, u32[]{:S(2)}) %collective-permute-start.9) | collective-permute-done | bytes 32800 | tf_op jit(solution)/shard_map/ppermute | solution.py:236
  39.4 1.6 %collective-permute-done.14 = f32[64,128]{1,0:T(8,128)S(1)} collective-permute-done((f32[64,128]{1,0:T(8,128)S(1)}, f32[64,128]{1,0:T(8,128)S(1)}, u32[]{:S(2)}, u32[]{:S(2)}) %collective-permute-start.14) | collective-permute-done | bytes 32800 | tf_op jit(solution)/shard_map/ppermute | solution.py:209
  41.0 0.6 %fusion.7 = f32[128,64]{0,1:T(8,128)} fusion(f32[64,128]{1,0:T(8,128)S(1)} %collective-permute-done.14, f32[64,128]{1,0:T(8,128)S(1)} %collective-permute-done.10, f32[64,128]{1,0:T(8,128)S(1)} %collective-permute-done.9, f32[64,128]{1,0:T(8,128)S(1)} %collective-permute-done.8, f32[8,64,128]{2,1,0:T(8,128)S(1)} %combine.1), kind=kLoop, calls=%fused_computation.15 | loop fusion | flops 32768 | bytes 196608 | tf_op jit(solution)/shard_map/transpose | solution.py:281
  (20 shorter events, 0.3 us)
Async XLA Ops:
  0.0 15.7 %collective-permute-start.4 = (f32[512,128]{1,0:T(8,128)}, f32[512,128]{1,0:T(8,128)S(1)}, u32[]{:S(2)}, u32[]{:S(2)}) collective-permute-start(f32[512,128]{1,0:T(8,128)} %bitcast.44), channel_id=1, source_target_pairs={{0,6},{1,7},{2,4},{3,5},{4,2},{5,3},{6,0},{7,1},{8,14},{9,15},{10,... | collective-permute-start | bytes 786440 | tf_op jit(solution)/shard_map/ppermute | solution.py:215
  8.5 8.0 %collective-permute-start.1 = (f32[512,128]{1,0:T(8,128)}, f32[512,128]{1,0:T(8,128)S(1)}, u32[]{:S(2)}, u32[]{:S(2)}) collective-permute-start(f32[512,128]{1,0:T(8,128)} %get-tuple-element.9.rest_0_), channel_id=1, source_target_pairs={{0,16},{8,24},{16,0},{24,8},{1,17},{9,25},{17,1},{25,9},{2,18},{10... | collective-permute-start | bytes 786440 | tf_op jit(solution)/shard_map/ppermute | solution.py:205
  10.1 5.6 %collective-permute-start.3 = (s32[2,8]{1,0:T(2,128)}, s32[2,8]{1,0:T(2,128)S(1)}, u32[]{:S(2)}, u32[]{:S(2)}) collective-permute-start(s32[2,8]{1,0:T(2,128)} %get-tuple-element.10.own_columns_ref), channel_id=1, source_target_pairs={{0,6},{1,7},{2,4},{3,5},{4,2},{5,3},{6,0},{7,1},{8,14},{9,15},{10,... | collective-permute-start | bytes 200 | tf_op jit(solution)/shard_map/ppermute | solution.py:215
  10.4 6.2 %copy-start.1 = (s32[2,8]{1,0:T(2,128)S(1)}, s32[2,8]{1,0:T(2,128)}, u32[]{:S(2)}) copy-start(s32[2,8]{1,0:T(2,128)} %get-tuple-element.10.own_columns_ref) | copy-start | bytes 196
  10.4 16.9 %all-to-all-start = ((f32[4,520,128]{2,1,0:T(8,128)}), f32[4,520,128]{2,1,0:T(8,128)S(1)}, u32[]{:S(2)}, u32[]{:S(2)}) async-start(f32[4,520,128]{2,1,0:T(8,128)} %get-tuple-element.8), calls=%async_computation | async-start | bytes 2129920 | tf_op jit(solution)/shard_map/all_to_all | solution.py:275
  14.0 9.6 %copy-start = (f32[512,128]{1,0:T(8,128)S(1)}, f32[512,128]{1,0:T(8,128)}, u32[]{:S(2)}) copy-start(f32[512,128]{1,0:T(8,128)} %get-tuple-element.9.rest_0_) | copy-start | bytes 786436
  16.6 7.0 %collective-permute-start.6 = (f32[520,128]{1,0:T(8,128)S(1)}, f32[520,128]{1,0:T(8,128)S(1)}, u32[]{:S(2)}, u32[]{:S(2)}) collective-permute-start(f32[520,128]{1,0:T(8,128)S(1)} %append_columns.1.rest_4_), channel_id=1, source_target_pairs={{0,16},{8,24},{16,0},{24,8},{1,17},{9,25},{17,1},{25,9},{2,18},{10... | collective-permute-start | bytes 798728 | tf_op jit(solution)/shard_map/ppermute | solution.py:205
  18.2 7.7 %collective-permute-start.5 = (f32[520,128]{1,0:T(8,128)S(1)}, f32[520,128]{1,0:T(8,128)S(1)}, u32[]{:S(2)}, u32[]{:S(2)}) collective-permute-start(f32[520,128]{1,0:T(8,128)S(1)} %append_columns.1.rest_4_), channel_id=1, source_target_pairs={{0,8},{8,0},{16,24},{24,16},{1,9},{9,1},{17,25},{25,17},{2,10},{10... | collective-permute-start | bytes 798728 | tf_op jit(solution)/shard_map/ppermute | solution.py:205
  23.6 2.3 %collective-permute-start.7 = (f32[520,128]{1,0:T(8,128)S(1)}, f32[520,128]{1,0:T(8,128)S(1)}, u32[]{:S(2)}, u32[]{:S(2)}) collective-permute-start(f32[520,128]{1,0:T(8,128)S(1)} %collective-permute-done.6.rest_6_), channel_id=1, source_target_pairs={{0,8},{8,0},{16,24},{24,16},{1,9},{9,1},{17,25},{25,17},{2,10},{10... | collective-permute-start | bytes 798728 | tf_op jit(solution)/shard_map/ppermute | solution.py:205
  23.6 1.9 %collective-permute-start = (f32[512,128]{1,0:T(8,128)S(1)}, f32[512,128]{1,0:T(8,128)S(1)}, u32[]{:S(2)}, u32[]{:S(2)}) collective-permute-start(f32[512,128]{1,0:T(8,128)S(1)} %copy-done), channel_id=1, source_target_pairs={{0,8},{8,0},{16,24},{24,16},{1,9},{9,1},{17,25},{25,17},{2,10},{10... | collective-permute-start | bytes 786440 | tf_op jit(solution)/shard_map/ppermute | solution.py:205
  24.1 1.8 %collective-permute-start.2 = (f32[512,128]{1,0:T(8,128)S(1)}, f32[512,128]{1,0:T(8,128)S(1)}, u32[]{:S(2)}, u32[]{:S(2)}) collective-permute-start(f32[512,128]{1,0:T(8,128)S(1)} %collective-permute-done.1.next_ref.rest_2_), channel_id=1, source_target_pairs={{0,8},{8,0},{16,24},{24,16},{1,9},{9,1},{17,25},{25,17},{2,10},{10... | collective-permute-start | bytes 786440 | tf_op jit(solution)/shard_map/ppermute | solution.py:205
  29.1 6.4 %collective-permute-start.13 = (f32[64,128]{1,0:T(8,128)S(1)}, f32[64,128]{1,0:T(8,128)S(1)}, u32[]{:S(2)}, u32[]{:S(2)}) collective-permute-start(f32[64,128]{1,0:T(8,128)S(1)} %get-tuple-element.12), channel_id=1, source_target_pairs={{0,3},{1,2},{2,1},{3,0},{4,7},{5,6},{6,5},{7,4},{8,11},{9,10},{10,... | collective-permute-start | bytes 98312 | tf_op jit(solution)/shard_map/ppermute | solution.py:236
  30.6 5.5 %collective-permute-start.12 = (f32[64,128]{1,0:T(8,128)S(1)}, f32[64,128]{1,0:T(8,128)S(1)}, u32[]{:S(2)}, u32[]{:S(2)}) collective-permute-start(f32[64,128]{1,0:T(8,128)S(1)} %get-tuple-element.13), channel_id=1, source_target_pairs={{0,2},{1,3},{2,0},{3,1},{4,6},{5,7},{6,4},{7,5},{8,10},{9,11},{10,... | collective-permute-start | bytes 98312 | tf_op jit(solution)/shard_map/ppermute | solution.py:236
  32.1 4.1 %collective-permute-start.11 = (f32[64,128]{1,0:T(8,128)S(1)}, f32[64,128]{1,0:T(8,128)S(1)}, u32[]{:S(2)}, u32[]{:S(2)}) collective-permute-start(f32[64,128]{1,0:T(8,128)S(1)} %get-tuple-element.14), channel_id=1, source_target_pairs={{0,1},{1,0},{2,3},{3,2},{4,5},{5,4},{6,7},{7,6},{8,9},{9,8},{10,11... | collective-permute-start | bytes 98312 | tf_op jit(solution)/shard_map/ppermute | solution.py:236
  32.6 6.1 %collective-permute-start.8 = (f32[64,128]{1,0:T(8,128)S(1)}, f32[64,128]{1,0:T(8,128)S(1)}, u32[]{:S(2)}, u32[]{:S(2)}) collective-permute-start(f32[64,128]{1,0:T(8,128)S(1)} %get-tuple-element.11), channel_id=1, source_target_pairs={{0,1},{1,0},{2,3},{3,2},{4,5},{5,4},{6,7},{7,6},{8,9},{9,8},{10,11... | collective-permute-start | bytes 98312 | tf_op jit(solution)/shard_map/ppermute | solution.py:236
  34.1 4.8 %collective-permute-start.10 = (f32[64,128]{1,0:T(8,128)S(1)}, f32[64,128]{1,0:T(8,128)S(1)}, u32[]{:S(2)}, u32[]{:S(2)}) collective-permute-start(f32[64,128]{1,0:T(8,128)S(1)} %get-tuple-element.15), channel_id=1, source_target_pairs={{0,3},{1,2},{2,1},{3,0},{4,7},{5,6},{6,5},{7,4},{8,11},{9,10},{10,... | collective-permute-start | bytes 98312 | tf_op jit(solution)/shard_map/ppermute | solution.py:236
  35.5 3.9 %collective-permute-start.9 = (f32[64,128]{1,0:T(8,128)S(1)}, f32[64,128]{1,0:T(8,128)S(1)}, u32[]{:S(2)}, u32[]{:S(2)}) collective-permute-start(f32[64,128]{1,0:T(8,128)S(1)} %get-tuple-element.16), channel_id=1, source_target_pairs={{0,2},{1,3},{2,0},{3,1},{4,6},{5,7},{6,4},{7,5},{8,10},{9,11},{10,... | collective-permute-start | bytes 98312 | tf_op jit(solution)/shard_map/ppermute | solution.py:236
  36.1 4.9 %collective-permute-start.14 = (f32[64,128]{1,0:T(8,128)S(1)}, f32[64,128]{1,0:T(8,128)S(1)}, u32[]{:S(2)}, u32[]{:S(2)}) collective-permute-start(f32[64,128]{1,0:T(8,128)S(1)} %fusion.2), channel_id=1, source_target_pairs={{0,4},{4,0},{1,5},{5,1},{2,6},{6,2},{3,7},{7,3},{8,12},{12,8},{9,1... | collective-permute-start | bytes 98312 | tf_op jit(solution)/shard_map/ppermute | solution.py:209

commit v23 on v22

--- a/solution.py
+++ b/solution.py
@@ -29,7 +29,23 @@
     return both[:, :width] + both[:, width:]
 
 
-def append_kernel(next_ref, far_columns_ref, own_columns_ref, blocks_ref, out_ref):
+def hold_kernel(mark_ref, blocks_ref, out_ref):
+    out_ref[...] = blocks_ref[...]
+
+
+def hold_until(mark, blocks):
+    return pl.pallas_call(
+        hold_kernel,
+        out_shape=jax.ShapeDtypeStruct(blocks.shape, blocks.dtype),
+        in_specs=[pl.BlockSpec(memory_space=pltpu.VMEM)] * 2,
+        out_specs=pl.BlockSpec(memory_space=pltpu.VMEM),
+        compiler_params=pltpu.CompilerParams(vmem_limit_bytes=VMEM_LIMIT),
+        cost_estimate=pl.CostEstimate(flops=HOLD_FLOPS, bytes_accessed=HOLD_FLOPS >> 8, transcendentals=0),
+        name="hold_until",
+    )(mark, blocks)
+
+
+def append_kernel(far_columns_ref, own_columns_ref, next_ref, blocks_ref, out_ref):
     used = blocks_ref.shape[0]
     entries, fine_rows = own_columns_ref.shape
     out_ref[:used] = blocks_ref[...]
@@ -38,7 +54,7 @@
     out_ref[used + entries : used + 2 * entries, :fine_rows] = own_columns_ref[...].astype(jnp.float32)
 
 
-def append_columns(next_blocks, far_columns, own_columns, blocks):
+def append_columns(far_columns, own_columns, next_blocks, blocks):
     used, width = blocks.shape
     return pl.pallas_call(
         append_kernel,
@@ -46,14 +62,14 @@
         in_specs=[pl.BlockSpec(memory_space=pltpu.VMEM)] * 4,
         out_specs=pl.BlockSpec(memory_space=pltpu.VMEM),
         compiler_params=pltpu.CompilerParams(vmem_limit_bytes=VMEM_LIMIT),
-        cost_estimate=pl.CostEstimate(flops=HOLD_FLOPS, bytes_accessed=HOLD_FLOPS >> 8, transcendentals=0),
+        cost_estimate=pl.CostEstimate(flops=0, bytes_accessed=1 << 19, transcendentals=0),
         name="append_columns",
-    )(next_blocks, far_columns, own_columns, blocks)
+    )(far_columns, own_columns, next_blocks, blocks)
 
 
 def restrict_kernel(
-    count_any, slot_any, rows_any, fetch_any, restrict_any, operator_any, columns_any, blocks_any, side_any,
-    out_ref, own_columns_ref, own_blocks_ref,
+    count_any, slot_any, rows_any, fetch_any, restrict_any, operator_any, columns_any, side_any,
+    out_ref, own_columns_ref,
     count_ref, slot_ref, rows_ref, fetch_ref, side_ref, restrict_ref, operator_ref, sems, operator_sems,
 ):
     fine_rows, block_size, _ = operator_ref.shape
@@ -66,7 +82,7 @@
     pairs = [
         (count_any, count_ref), (slot_any, slot_ref), (rows_any, rows_ref),
         (fetch_any, fetch_ref), (restrict_any, restrict_ref),
-        (columns_any, own_columns_ref), (blocks_any, own_blocks_ref), (side_any, side_ref),
+        (columns_any, own_columns_ref), (side_any, side_ref),
     ]
     copies = [pltpu.make_async_copy(a, b, sems.at[i]) for i, (a, b) in enumerate(pairs)]
     operators = [
@@ -110,7 +126,7 @@
 
 
 def restrict_operator(
-    operator_count, operator_slot, restrict_rows, fetch, operator_blocks, restrict_blocks, own_columns, own_blocks, side
+    operator_count, operator_slot, restrict_rows, fetch, operator_blocks, restrict_blocks, own_columns, side
 ):
     fine_rows, block_size, width = operator_blocks.shape
     slot_count, columns = fetch.shape
@@ -123,18 +139,17 @@
         out_shape=(
             jax.ShapeDtypeStruct((columns // 2, rows, wide), jnp.float32),
             jax.ShapeDtypeStruct(own_columns.shape, own_columns.dtype),
-            jax.ShapeDtypeStruct(own_blocks.shape, own_blocks.dtype),
         ),
-        in_specs=[pl.BlockSpec(memory_space=pltpu.HBM)] * 9,
-        out_specs=[pl.BlockSpec(memory_space=pltpu.VMEM)] * 3,
+        in_specs=[pl.BlockSpec(memory_space=pltpu.HBM)] * 8,
+        out_specs=[pl.BlockSpec(memory_space=pltpu.VMEM)] * 2,
         scratch_shapes=[pltpu.SMEM(x.shape, x.dtype) for x in kept]
         + [pltpu.VMEM(x.shape, x.dtype) for x in (restrict_blocks, operator_blocks)]
-        + [pltpu.SemaphoreType.DMA((8,)), pltpu.SemaphoreType.DMA((fine_rows,))],
+        + [pltpu.SemaphoreType.DMA((7,)), pltpu.SemaphoreType.DMA((fine_rows,))],
         cost_estimate=pl.CostEstimate(
             flops=6 * fine_rows * block_size * width * wide, bytes_accessed=4 << 20, transcendentals=0
         ),
         name="restrict_operator",
-    )(*small, restrict_blocks, operator_blocks, own_columns, own_blocks, side)
+    )(*small, restrict_blocks, operator_blocks, own_columns, side)
 
 
 def combine_kernel(own_ref, restricted_ref, *rest, slot_count, fine_rows, entries):
@@ -151,7 +166,7 @@
         table_ref[1 + near : 2 + near] = restricted_ref[near, used : used + 1].astype(jnp.int32)
     for i, piece in enumerate(pieces[rows:]):
         for far in range(2):
-            first = 1 + half + entries * (far * rows + i)
+            first = 1 + half + entries * (far * rows + (i ^ (far * rows // 2)))
             row = held + entries * (1 - far)
             table_ref[first : first + entries] = piece[row : row + entries].astype(jnp.int32)
     copy = pltpu.make_async_copy(table_ref, index_ref, sem)
@@ -215,6 +230,17 @@
     return lax.ppermute(x, ("half", "near"), pairs)
 
 
+def far_turn(x):
+    rows, half = lax.axis_size("row"), lax.axis_size("near")
+    pairs = [
+        ((r * 2 + h) * half + n, ((r ^ rows // 2) * 2 + 1 - h) * half + (n ^ half // 2))
+        for r in range(rows)
+        for h in range(2)
+        for n in range(half)
+    ]
+    return lax.ppermute(x, ("row", "half", "near"), pairs)
+
+
 def spread_over_rows(blocks, rows):
     pieces = {0: blocks}
     bit = rows // 2
@@ -261,7 +287,7 @@
 
     near_blocks = prolong_blocks.reshape(fine_rows * block_size, width)
     far_blocks = far_swap(near_blocks)
-    restricted, own_columns, near_blocks = restrict_operator(
+    restricted, own_columns = restrict_operator(
         operator_count,
         operator_slot,
         restrict_rows.T,
@@ -269,13 +295,13 @@
         operator_blocks,
         restrict_blocks,
         prolong_cols.T,
-        near_blocks,
         lax.axis_index("half").reshape(1),
     )
     restricted = lax.all_to_all(restricted, "near", split_axis=0, concat_axis=0, tiled=True)
-    far_columns = far_swap(own_columns)
+    far_columns = far_turn(own_columns)
     near_pieces = spread_over_rows(near_blocks, rows)
-    far_blocks = append_columns(near_pieces[rows // 2], far_columns, own_columns, far_blocks)
+    far_blocks = hold_until(own_columns, far_blocks)
+    far_blocks = append_columns(far_columns, own_columns, near_pieces[rows // 2], far_blocks)
     pieces = near_pieces + spread_over_rows(far_blocks, rows)
     sums = combine(own, restricted, pieces, NCR * rows, slot_count, fine_rows, block_size)
     return add_over_columns(sums, half).T

time: 41.9 us -> 49.2 us (1.17)
  waiting for transfers between devices: 13.3 us -> 20.7 us
    ppermute x0 -> x1, waiting for transfers between devices: none -> 11.4 us  [far_turn(): return lax.ppermute(x, ('row', 'half', 'near'), pairs)]
    ppermute x2 -> x1, waiting for transfers between devices: 1.69 us -> 0.01 us  [far_swap(): return lax.ppermute(x, ('half', 'near'), pairs)]
    ppermute x6, waiting for transfers between devices: 7.99 us -> 6.59 us  [row_swap(): lax.ppermute(x, 'row', [(r, r ^ bit) for r in range(lax.axis_size('row'))])]
    all_to_all x1, waiting for transfers between devices: 1.37 us -> 0.01 us  [local(): lax.all_to_all(restricted, 'near', split_axis=0, concat_axis=0, tiled=True)]
    ppermute x0 -> x1, starting transfers between devices: none -> 0.84 us  [far_turn(): return lax.ppermute(x, ('row', 'half', 'near'), pairs)]
    ppermute x2 -> x1, starting transfers between devices: 5.27 us -> 5.05 us  [far_swap(): return lax.ppermute(x, ('half', 'near'), pairs)]
  transfers between devices with their start and end apart: 16 -> 16, of which waited for: 9 -> 6; matrix products, arithmetic and copies ran while one was open for 0% -> 0% of each run, Pallas kernels for 8% -> 7%
where the time goes in v23:
time: 49.2 us; the launch traced here: 49 us
  starting transfers between devices  22.3 us (45%)
  waiting for transfers between devices  20.7 us (42%)
  Pallas kernels  5.12 us (10%)
  other arithmetic  0.72 us (1%)
    ppermute x1, waiting for transfers between devices, far_turn(): return lax.ppermute(x, ('row', 'half', 'near'), pairs)  11.4 us
    ppermute x6, starting transfers between devices, add_over_near(): lax.ppermute(sums[near], 'near', [(n, n ^ near) for n in range(half)])  7.04 us
    ppermute x6, waiting for transfers between devices, row_swap(): lax.ppermute(x, 'row', [(r, r ^ bit) for r in range(lax.axis_size('row'))])  6.59 us
    ppermute x1, starting transfers between devices, far_swap(): return lax.ppermute(x, ('half', 'near'), pairs)  5.05 us
    ppermute x6, starting transfers between devices, row_swap(): lax.ppermute(x, 'row', [(r, r ^ bit) for r in range(lax.axis_size('row'))])  3.62 us
    all_to_all x1, starting transfers between devices, local(): lax.all_to_all(restricted, 'near', split_axis=0, concat_axis=0, tiled=True)  3.53 us
    pallas_call x1, Pallas kernels, restrict_operator(): pl.pallas_call(restrict_kernel, out_shape=(jax.ShapeDtypeStruct((columns...  3.33 us
    ppermute x1, starting transfers between devices, half_swap(): return lax.ppermute(x, 'half', [(0, 1), (1, 0)])  2.21 us
  transfers between devices with their start and end apart: 16, of which 6 were waited for; matrix products, arithmetic and copies ran while one was open for 0% of the time, Pallas kernels for 7%

profile of v23, /device:TPU:0, one launch (start us, length us, event | category | flops | bytes accessed | tf_op | source)
XLA Modules:
  0.0 49.0 jit_solution(3791687332729978741)
XLA Ops:
  0.0 5.0 %collective-permute-start.4 = (f32[512,128]{1,0:T(8,128)}, f32[512,128]{1,0:T(8,128)S(1)}, u32[]{:S(2)}, u32[]{:S(2)}) collective-permute-start(f32[512,128]{1,0:T(8,128)} %bitcast.44), channel_id=1, source_target_pairs={{0,6},{1,7},{2,4},{3,5},{4,2},{5,3},{6,0},{7,1},{8,14},{9,15},{10,... | collective-permute-start | bytes 786440 | tf_op jit(solution)/shard_map/ppermute | solution.py:230
  5.0 1.5 %collective-permute-start.1 = (f32[512,128]{1,0:T(8,128)}, f32[512,128]{1,0:T(8,128)S(1)}, u32[]{:S(2)}, u32[]{:S(2)}) collective-permute-start(f32[512,128]{1,0:T(8,128)} %bitcast.45), channel_id=1, source_target_pairs={{0,16},{8,24},{16,0},{24,8},{1,17},{9,25},{17,1},{25,9},{2,18},{10... | collective-permute-start | bytes 786440 | tf_op jit(solution)/shard_map/ppermute | solution.py:220
  6.6 3.3 %restrict_operator.1 = (f32[4,520,128]{2,1,0:T(8,128)}, s32[2,8]{1,0:T(2,128)}) custom-call(s32[8]{0:T(128)} %count_any.1, s32[8,8]{1,0:T(8,128)} %slot_any.1, s32[2,8]{1,0:T(2,128)} %bitcast.49, s32[4,8]{1,0:T(4,128)} %bitcast.48, f32[8,64,128]{2,1,0:T(8,128)} %restrict_any.1, f32[8,64,512]{2,1,0:T(8,128)} %operator_any.1, s32[2,8]{1,0:T(2,128)} %bitcast.50, ...), custom_call_target="tpu_custom_call" | custom-call | flops 201326592 | bytes 4194304 | tf_op jit(solution)/shard_map/restrict_operator/pallas_call | solution.py:137
  9.9 3.5 %all-to-all-start = ((f32[4,520,128]{2,1,0:T(8,128)}), f32[4,520,128]{2,1,0:T(8,128)S(1)}, u32[]{:S(2)}, u32[]{:S(2)}) async-start(f32[4,520,128]{2,1,0:T(8,128)} %get-tuple-element.7), calls=%async_computation | async-start | bytes 2129920 | tf_op jit(solution)/shard_map/all_to_all | solution.py:300
  13.5 0.0 copy-start
  13.5 0.8 %collective-permute-start.3 = (s32[2,8]{1,0:T(2,128)S(1)}, s32[2,8]{1,0:T(2,128)S(1)}, u32[]{:S(2)}, u32[]{:S(2)}) collective-permute-start(s32[2,8]{1,0:T(2,128)S(1)} %copy-done.1), channel_id=1, source_target_pairs={{0,22},{1,23},{2,20},{3,21},{4,18},{5,19},{6,16},{7,17},{8,30},{9,... | collective-permute-start | bytes 200 | tf_op jit(solution)/shard_map/ppermute | solution.py:241
  14.3 11.4 %collective-permute-done.3.far_columns_ref = s32[2,8]{1,0:T(2,128)S(1)} collective-permute-done((s32[2,8]{1,0:T(2,128)S(1)}, s32[2,8]{1,0:T(2,128)S(1)}, u32[]{:S(2)}, u32[]{:S(2)}) %collective-permute-start.3) | collective-permute-done | bytes 96 | tf_op jit(solution)/shard_map/ppermute | solution.py:241
  25.8 1.6 %collective-permute-start.6 = (f32[520,128]{1,0:T(8,128)S(1)}, f32[520,128]{1,0:T(8,128)S(1)}, u32[]{:S(2)}, u32[]{:S(2)}) collective-permute-start(f32[520,128]{1,0:T(8,128)S(1)} %append_columns.1.rest_4_), channel_id=1, source_target_pairs={{0,16},{8,24},{16,0},{24,8},{1,17},{9,25},{17,1},{25,9},{2,18},{10... | collective-permute-start | bytes 798728 | tf_op jit(solution)/shard_map/ppermute | solution.py:220
  27.4 4.9 %collective-permute-done.6.rest_6_ = f32[520,128]{1,0:T(8,128)S(1)} collective-permute-done((f32[520,128]{1,0:T(8,128)S(1)}, f32[520,128]{1,0:T(8,128)S(1)}, u32[]{:S(2)}, u32[]{:S(2)}) %collective-permute-start.6) | collective-permute-done | bytes 266272 | tf_op jit(solution)/shard_map/ppermute | solution.py:220
  32.3 0.5 %collective-permute-start = (f32[512,128]{1,0:T(8,128)S(1)}, f32[512,128]{1,0:T(8,128)S(1)}, u32[]{:S(2)}, u32[]{:S(2)}) collective-permute-start(f32[512,128]{1,0:T(8,128)S(1)} %bitcast.46), channel_id=1, source_target_pairs={{0,8},{8,0},{16,24},{24,16},{1,9},{9,1},{17,25},{25,17},{2,10},{10... | collective-permute-start | bytes 786440 | tf_op jit(solution)/shard_map/ppermute | solution.py:220
  32.8 0.1 add_bitcast_fusion.own_ref
  32.9 1.3 %collective-permute-done.rest_1_ = f32[512,128]{1,0:T(8,128)S(1)} collective-permute-done((f32[512,128]{1,0:T(8,128)S(1)}, f32[512,128]{1,0:T(8,128)S(1)}, u32[]{:S(2)}, u32[]{:S(2)}) %collective-permute-start) | collective-permute-done | bytes 262176 | tf_op jit(solution)/shard_map/ppermute | solution.py:220
  34.2 0.4 collective-permute-done.2.rest_3_
  34.6 1.8 %combine.1 = f32[8,64,128]{2,1,0:T(8,128)S(1)} custom-call(s32[1,10]{1,0:T(1,128)S(1)} %add_bitcast_fusion.own_ref, f32[4,520,128]{2,1,0:T(8,128)S(1)} %all-to-all-done.restricted_ref, f32[512,128]{1,0:T(8,128)S(1)} %bitcast.47, f32[512,128]{1,0:T(8,128)S(1)} %collective-permute-done.rest_1_, f32[512,128]{1,0:T(8,128)S(1)} %collective-permute-done.1.next_ref.rest_2_, ...), custom_call_target="tpu_custom_call" | custom-call | flops 268435456 | bytes 4194304 | tf_op jit(solution)/shard_map/combine/pallas_call | solution.py:202
  36.4 0.1 collective-permute-start.13
  36.5 2.9 %collective-permute-start.12 = (f32[64,128]{1,0:T(8,128)S(1)}, f32[64,128]{1,0:T(8,128)S(1)}, u32[]{:S(2)}, u32[]{:S(2)}) collective-permute-start(f32[64,128]{1,0:T(8,128)S(1)} %get-tuple-element.11), channel_id=1, source_target_pairs={{0,2},{1,3},{2,0},{3,1},{4,6},{5,7},{6,4},{7,5},{8,10},{9,11},{10,... | collective-permute-start | bytes 98312 | tf_op jit(solution)/shard_map/ppermute | solution.py:262
  39.4 0.6 %collective-permute-start.11 = (f32[64,128]{1,0:T(8,128)S(1)}, f32[64,128]{1,0:T(8,128)S(1)}, u32[]{:S(2)}, u32[]{:S(2)}) collective-permute-start(f32[64,128]{1,0:T(8,128)S(1)} %get-tuple-element.12), channel_id=1, source_target_pairs={{0,1},{1,0},{2,3},{3,2},{4,5},{5,4},{6,7},{7,6},{8,9},{9,8},{10,11... | collective-permute-start | bytes 98312 | tf_op jit(solution)/shard_map/ppermute | solution.py:262
  39.9 0.9 %collective-permute-start.10 = (f32[64,128]{1,0:T(8,128)S(1)}, f32[64,128]{1,0:T(8,128)S(1)}, u32[]{:S(2)}, u32[]{:S(2)}) collective-permute-start(f32[64,128]{1,0:T(8,128)S(1)} %get-tuple-element.13), channel_id=1, source_target_pairs={{0,3},{1,2},{2,1},{3,0},{4,7},{5,6},{6,5},{7,4},{8,11},{9,10},{10,... | collective-permute-start | bytes 98312 | tf_op jit(solution)/shard_map/ppermute | solution.py:262
  40.8 2.0 %collective-permute-start.9 = (f32[64,128]{1,0:T(8,128)S(1)}, f32[64,128]{1,0:T(8,128)S(1)}, u32[]{:S(2)}, u32[]{:S(2)}) collective-permute-start(f32[64,128]{1,0:T(8,128)S(1)} %get-tuple-element.14), channel_id=1, source_target_pairs={{0,2},{1,3},{2,0},{3,1},{4,6},{5,7},{6,4},{7,5},{8,10},{9,11},{10,... | collective-permute-start | bytes 98312 | tf_op jit(solution)/shard_map/ppermute | solution.py:262
  42.9 0.6 %collective-permute-start.8 = (f32[64,128]{1,0:T(8,128)S(1)}, f32[64,128]{1,0:T(8,128)S(1)}, u32[]{:S(2)}, u32[]{:S(2)}) collective-permute-start(f32[64,128]{1,0:T(8,128)S(1)} %get-tuple-element.9), channel_id=1, source_target_pairs={{0,1},{1,0},{2,3},{3,2},{4,5},{5,4},{6,7},{7,6},{8,9},{9,8},{10,11... | collective-permute-start | bytes 98312 | tf_op jit(solution)/shard_map/ppermute | solution.py:262
  43.5 2.2 %collective-permute-start.14 = (f32[64,128]{1,0:T(8,128)S(1)}, f32[64,128]{1,0:T(8,128)S(1)}, u32[]{:S(2)}, u32[]{:S(2)}) collective-permute-start(f32[64,128]{1,0:T(8,128)S(1)} %fusion.2), channel_id=1, source_target_pairs={{0,4},{4,0},{1,5},{5,1},{2,6},{6,2},{3,7},{7,3},{8,12},{12,8},{9,1... | collective-permute-start | bytes 98312 | tf_op jit(solution)/shard_map/ppermute | solution.py:224
  45.7 1.1 %collective-permute-done.8 = f32[64,128]{1,0:T(8,128)S(1)} collective-permute-done((f32[64,128]{1,0:T(8,128)S(1)}, f32[64,128]{1,0:T(8,128)S(1)}, u32[]{:S(2)}, u32[]{:S(2)}) %collective-permute-start.8) | collective-permute-done | bytes 32800 | tf_op jit(solution)/shard_map/ppermute | solution.py:262
  46.8 1.5 %collective-permute-done.14 = f32[64,128]{1,0:T(8,128)S(1)} collective-permute-done((f32[64,128]{1,0:T(8,128)S(1)}, f32[64,128]{1,0:T(8,128)S(1)}, u32[]{:S(2)}, u32[]{:S(2)}) %collective-permute-start.14) | collective-permute-done | bytes 32800 | tf_op jit(solution)/shard_map/ppermute | solution.py:224
  48.3 0.6 %fusion.7 = f32[128,64]{0,1:T(8,128)} fusion(f32[64,128]{1,0:T(8,128)S(1)} %collective-permute-done.14, f32[64,128]{1,0:T(8,128)S(1)} %collective-permute-done.10, f32[64,128]{1,0:T(8,128)S(1)} %collective-permute-done.9, f32[64,128]{1,0:T(8,128)S(1)} %collective-permute-done.8, f32[8,64,128]{2,1,0:T(8,128)S(1)} %combine.1), kind=kLoop, calls=%fused_computation.15 | loop fusion | flops 32768 | bytes 196608 | tf_op jit(solution)/shard_map/transpose | solution.py:307
  (21 shorter events, 0.1 us)
Async XLA Ops:
  0.0 14.3 %collective-permute-start.4 = (f32[512,128]{1,0:T(8,128)}, f32[512,128]{1,0:T(8,128)S(1)}, u32[]{:S(2)}, u32[]{:S(2)}) collective-permute-start(f32[512,128]{1,0:T(8,128)} %bitcast.44), channel_id=1, source_target_pairs={{0,6},{1,7},{2,4},{3,5},{4,2},{5,3},{6,0},{7,1},{8,14},{9,15},{10,... | collective-permute-start | bytes 786440 | tf_op jit(solution)/shard_map/ppermute | solution.py:230
  5.0 20.7 %collective-permute-start.1 = (f32[512,128]{1,0:T(8,128)}, f32[512,128]{1,0:T(8,128)S(1)}, u32[]{:S(2)}, u32[]{:S(2)}) collective-permute-start(f32[512,128]{1,0:T(8,128)} %bitcast.45), channel_id=1, source_target_pairs={{0,16},{8,24},{16,0},{24,8},{1,17},{9,25},{17,1},{25,9},{2,18},{10... | collective-permute-start | bytes 786440 | tf_op jit(solution)/shard_map/ppermute | solution.py:220
  9.9 3.6 %copy-start.1 = (s32[2,8]{1,0:T(2,128)S(1)}, s32[2,8]{1,0:T(2,128)}, u32[]{:S(2)}) copy-start(s32[2,8]{1,0:T(2,128)} %get-tuple-element.8.mark_ref.own_columns_ref) | copy-start | bytes 196
  9.9 24.7 %all-to-all-start = ((f32[4,520,128]{2,1,0:T(8,128)}), f32[4,520,128]{2,1,0:T(8,128)S(1)}, u32[]{:S(2)}, u32[]{:S(2)}) async-start(f32[4,520,128]{2,1,0:T(8,128)} %get-tuple-element.7), calls=%async_computation | async-start | bytes 2129920 | tf_op jit(solution)/shard_map/all_to_all | solution.py:300
  13.5 18.8 %copy-start = (f32[8,64,128]{2,1,0:T(8,128)S(1)}, f32[8,64,128]{2,1,0:T(8,128)}, u32[]{:S(2)}) copy-start(f32[8,64,128]{2,1,0:T(8,128)} %param.12) | copy-start | bytes 786436
  13.5 12.3 %collective-permute-start.3 = (s32[2,8]{1,0:T(2,128)S(1)}, s32[2,8]{1,0:T(2,128)S(1)}, u32[]{:S(2)}, u32[]{:S(2)}) collective-permute-start(s32[2,8]{1,0:T(2,128)S(1)} %copy-done.1), channel_id=1, source_target_pairs={{0,22},{1,23},{2,20},{3,21},{4,18},{5,19},{6,16},{7,17},{8,30},{9,... | collective-permute-start | bytes 200 | tf_op jit(solution)/shard_map/ppermute | solution.py:241
  25.8 6.5 %collective-permute-start.6 = (f32[520,128]{1,0:T(8,128)S(1)}, f32[520,128]{1,0:T(8,128)S(1)}, u32[]{:S(2)}, u32[]{:S(2)}) collective-permute-start(f32[520,128]{1,0:T(8,128)S(1)} %append_columns.1.rest_4_), channel_id=1, source_target_pairs={{0,16},{8,24},{16,0},{24,8},{1,17},{9,25},{17,1},{25,9},{2,18},{10... | collective-permute-start | bytes 798728 | tf_op jit(solution)/shard_map/ppermute | solution.py:220
  27.4 7.2 %collective-permute-start.5 = (f32[520,128]{1,0:T(8,128)S(1)}, f32[520,128]{1,0:T(8,128)S(1)}, u32[]{:S(2)}, u32[]{:S(2)}) collective-permute-start(f32[520,128]{1,0:T(8,128)S(1)} %append_columns.1.rest_4_), channel_id=1, source_target_pairs={{0,8},{8,0},{16,24},{24,16},{1,9},{9,1},{17,25},{25,17},{2,10},{10... | collective-permute-start | bytes 798728 | tf_op jit(solution)/shard_map/ppermute | solution.py:220
  32.3 2.3 %collective-permute-start.7 = (f32[520,128]{1,0:T(8,128)S(1)}, f32[520,128]{1,0:T(8,128)S(1)}, u32[]{:S(2)}, u32[]{:S(2)}) collective-permute-start(f32[520,128]{1,0:T(8,128)S(1)} %collective-permute-done.6.rest_6_), channel_id=1, source_target_pairs={{0,8},{8,0},{16,24},{24,16},{1,9},{9,1},{17,25},{25,17},{2,10},{10... | collective-permute-start | bytes 798728 | tf_op jit(solution)/shard_map/ppermute | solution.py:220
  32.3 1.9 %collective-permute-start = (f32[512,128]{1,0:T(8,128)S(1)}, f32[512,128]{1,0:T(8,128)S(1)}, u32[]{:S(2)}, u32[]{:S(2)}) collective-permute-start(f32[512,128]{1,0:T(8,128)S(1)} %bitcast.46), channel_id=1, source_target_pairs={{0,8},{8,0},{16,24},{24,16},{1,9},{9,1},{17,25},{25,17},{2,10},{10... | collective-permute-start | bytes 786440 | tf_op jit(solution)/shard_map/ppermute | solution.py:220
  32.8 1.8 %collective-permute-start.2 = (f32[512,128]{1,0:T(8,128)S(1)}, f32[512,128]{1,0:T(8,128)S(1)}, u32[]{:S(2)}, u32[]{:S(2)}) collective-permute-start(f32[512,128]{1,0:T(8,128)S(1)} %collective-permute-done.1.next_ref.rest_2_), channel_id=1, source_target_pairs={{0,8},{8,0},{16,24},{24,16},{1,9},{9,1},{17,25},{25,17},{2,10},{10... | collective-permute-start | bytes 786440 | tf_op jit(solution)/shard_map/ppermute | solution.py:220
  36.4 6.5 %collective-permute-start.13 = (f32[64,128]{1,0:T(8,128)S(1)}, f32[64,128]{1,0:T(8,128)S(1)}, u32[]{:S(2)}, u32[]{:S(2)}) collective-permute-start(f32[64,128]{1,0:T(8,128)S(1)} %get-tuple-element.10), channel_id=1, source_target_pairs={{0,3},{1,2},{2,1},{3,0},{4,7},{5,6},{6,5},{7,4},{8,11},{9,10},{10,... | collective-permute-start | bytes 98312 | tf_op jit(solution)/shard_map/ppermute | solution.py:262
  36.5 7.0 %collective-permute-start.12 = (f32[64,128]{1,0:T(8,128)S(1)}, f32[64,128]{1,0:T(8,128)S(1)}, u32[]{:S(2)}, u32[]{:S(2)}) collective-permute-start(f32[64,128]{1,0:T(8,128)S(1)} %get-tuple-element.11), channel_id=1, source_target_pairs={{0,2},{1,3},{2,0},{3,1},{4,6},{5,7},{6,4},{7,5},{8,10},{9,11},{10,... | collective-permute-start | bytes 98312 | tf_op jit(solution)/shard_map/ppermute | solution.py:262
  39.4 4.1 %collective-permute-start.11 = (f32[64,128]{1,0:T(8,128)S(1)}, f32[64,128]{1,0:T(8,128)S(1)}, u32[]{:S(2)}, u32[]{:S(2)}) collective-permute-start(f32[64,128]{1,0:T(8,128)S(1)} %get-tuple-element.12), channel_id=1, source_target_pairs={{0,1},{1,0},{2,3},{3,2},{4,5},{5,4},{6,7},{7,6},{8,9},{9,8},{10,11... | collective-permute-start | bytes 98312 | tf_op jit(solution)/shard_map/ppermute | solution.py:262
  39.9 5.7 %collective-permute-start.10 = (f32[64,128]{1,0:T(8,128)S(1)}, f32[64,128]{1,0:T(8,128)S(1)}, u32[]{:S(2)}, u32[]{:S(2)}) collective-permute-start(f32[64,128]{1,0:T(8,128)S(1)} %get-tuple-element.13), channel_id=1, source_target_pairs={{0,3},{1,2},{2,1},{3,0},{4,7},{5,6},{6,5},{7,4},{8,11},{9,10},{10,... | collective-permute-start | bytes 98312 | tf_op jit(solution)/shard_map/ppermute | solution.py:262
  40.8 4.8 %collective-permute-start.9 = (f32[64,128]{1,0:T(8,128)S(1)}, f32[64,128]{1,0:T(8,128)S(1)}, u32[]{:S(2)}, u32[]{:S(2)}) collective-permute-start(f32[64,128]{1,0:T(8,128)S(1)} %get-tuple-element.14), channel_id=1, source_target_pairs={{0,2},{1,3},{2,0},{3,1},{4,6},{5,7},{6,4},{7,5},{8,10},{9,11},{10,... | collective-permute-start | bytes 98312 | tf_op jit(solution)/shard_map/ppermute | solution.py:262
  42.9 3.9 %collective-permute-start.8 = (f32[64,128]{1,0:T(8,128)S(1)}, f32[64,128]{1,0:T(8,128)S(1)}, u32[]{:S(2)}, u32[]{:S(2)}) collective-permute-start(f32[64,128]{1,0:T(8,128)S(1)} %get-tuple-element.9), channel_id=1, source_target_pairs={{0,1},{1,0},{2,3},{3,2},{4,5},{5,4},{6,7},{7,6},{8,9},{9,8},{10,11... | collective-permute-start | bytes 98312 | tf_op jit(solution)/shard_map/ppermute | solution.py:262
  43.5 4.9 %collective-permute-start.14 = (f32[64,128]{1,0:T(8,128)S(1)}, f32[64,128]{1,0:T(8,128)S(1)}, u32[]{:S(2)}, u32[]{:S(2)}) collective-permute-start(f32[64,128]{1,0:T(8,128)S(1)} %fusion.2), channel_id=1, source_target_pairs={{0,4},{4,0},{1,5},{5,1},{2,6},{6,2},{3,7},{7,3},{8,12},{12,8},{9,1... | collective-permute-start | bytes 98312 | tf_op jit(solution)/shard_map/ppermute | solution.py:224

commit v24 on v22

--- a/solution.py
+++ b/solution.py
@@ -53,8 +53,9 @@
 
 def restrict_kernel(
     count_any, slot_any, rows_any, fetch_any, restrict_any, operator_any, columns_any, blocks_any, side_any,
-    out_ref, own_columns_ref, own_blocks_ref,
-    count_ref, slot_ref, rows_ref, fetch_ref, side_ref, restrict_ref, operator_ref, sems, operator_sems,
+    out_ref, own_columns_ref, own_blocks_any,
+    count_ref, slot_ref, rows_ref, fetch_ref, side_ref, restrict_ref, operator_ref, blocks_ref,
+    sems, operator_sems, blocks_sems,
 ):
     fine_rows, block_size, _ = operator_ref.shape
     entries = slot_ref.shape[1]
@@ -66,13 +67,15 @@
     pairs = [
         (count_any, count_ref), (slot_any, slot_ref), (rows_any, rows_ref),
         (fetch_any, fetch_ref), (restrict_any, restrict_ref),
-        (columns_any, own_columns_ref), (blocks_any, own_blocks_ref), (side_any, side_ref),
+        (columns_any, own_columns_ref), (side_any, side_ref),
     ]
     copies = [pltpu.make_async_copy(a, b, sems.at[i]) for i, (a, b) in enumerate(pairs)]
     operators = [
         pltpu.make_async_copy(operator_any.at[i], operator_ref.at[i], operator_sems.at[i]) for i in range(fine_rows)
     ]
-    for copy in copies + operators:
+    blocks_in = pltpu.make_async_copy(blocks_any, blocks_ref, blocks_sems.at[0])
+    blocks_out = pltpu.make_async_copy(blocks_ref, own_blocks_any, blocks_sems.at[1])
+    for copy in copies + operators + [blocks_in]:
         copy.start()
 
     lane = lax.broadcasted_iota(jnp.int32, (block_size, wide), 1)
@@ -80,7 +83,7 @@
     short_lane = lax.broadcasted_iota(jnp.int32, (EXTRA, wide), 1)
     for near in range(half):
         out_ref[near, :used] = jnp.zeros((used, wide), jnp.float32)
-    for copy in copies + operators:
+    for copy in copies:
         copy.wait()
 
     for near in range(half):
@@ -93,6 +96,12 @@
         out_ref[near, used:] = value.astype(jnp.float32)
 
     for i in range(fine_rows):
+        if i % (fine_rows // 2) == 0:
+            for copy in operators[i : i + fine_rows // 2]:
+                copy.wait()
+        if i == fine_rows // 2:
+            blocks_in.wait()
+            blocks_out.start()
         value = restrict_ref[i]
         swapped = pltpu.roll(value, block_size, 1)
         own_row = jnp.where(second == 0, rows_ref[0, i], rows_ref[1, i])
@@ -107,6 +116,7 @@
             near = lax.rem(peer, half) ^ jnp.where(side_ref[0] == side, 0, half // 2)
             start = pl.multiple_of(place * block_size, block_size)
             out_ref[near, pl.ds(start, block_size)] += part
+    blocks_out.wait()
 
 
 def restrict_operator(
@@ -126,10 +136,10 @@
             jax.ShapeDtypeStruct(own_blocks.shape, own_blocks.dtype),
         ),
         in_specs=[pl.BlockSpec(memory_space=pltpu.HBM)] * 9,
-        out_specs=[pl.BlockSpec(memory_space=pltpu.VMEM)] * 3,
+        out_specs=[pl.BlockSpec(memory_space=pltpu.VMEM)] * 2 + [pl.BlockSpec(memory_space=pltpu.HBM)],
         scratch_shapes=[pltpu.SMEM(x.shape, x.dtype) for x in kept]
-        + [pltpu.VMEM(x.shape, x.dtype) for x in (restrict_blocks, operator_blocks)]
-        + [pltpu.SemaphoreType.DMA((8,)), pltpu.SemaphoreType.DMA((fine_rows,))],
+        + [pltpu.VMEM(x.shape, x.dtype) for x in (restrict_blocks, operator_blocks, own_blocks)]
+        + [pltpu.SemaphoreType.DMA((7,)), pltpu.SemaphoreType.DMA((fine_rows,)), pltpu.SemaphoreType.DMA((2,))],
         cost_estimate=pl.CostEstimate(
             flops=6 * fine_rows * block_size * width * wide, bytes_accessed=4 << 20, transcendentals=0
         ),

time: 41.9 us -> 42.1 us (level)
  transfers between devices with their start and end apart: 16 -> 16, of which waited for: 9 -> 9; matrix products, arithmetic and copies ran while one was open for 0% -> 0% of each run, Pallas kernels for 8% -> 9%
where the time goes in v24:
time: 42.1 us; the launch traced here: 41.9 us
  starting transfers between devices  22.2 us (53%)
  waiting for transfers between devices  13.3 us (32%)
  Pallas kernels  5.5 us (13%)
  other arithmetic  0.72 us (2%)
    ppermute x6, waiting for transfers between devices, row_swap(): lax.ppermute(x, 'row', [(r, r ^ bit) for r in range(lax.axis_size('row'))])  7.99 us
    ppermute x6, starting transfers between devices, add_over_near(): lax.ppermute(sums[near], 'near', [(n, n ^ near) for n in range(half)])  7.04 us
    ppermute x2, starting transfers between devices, far_swap(): return lax.ppermute(x, ('half', 'near'), pairs)  5.27 us
    pallas_call x1, Pallas kernels, restrict_operator(): pl.pallas_call(restrict_kernel, out_shape=(jax.ShapeDtypeStruct((columns...  3.72 us
    ppermute x6, starting transfers between devices, row_swap(): lax.ppermute(x, 'row', [(r, r ^ bit) for r in range(lax.axis_size('row'))])  3.69 us
    all_to_all x1, starting transfers between devices, local(): lax.all_to_all(restricted, 'near', split_axis=0, concat_axis=0, tiled=True)  3.65 us
    ppermute x1, starting transfers between devices, half_swap(): return lax.ppermute(x, 'half', [(0, 1), (1, 0)])  2.6 us
    pallas_call x1, Pallas kernels, combine(): pl.pallas_call(functools.partial(combine_kernel, slot_count=slot_count, f...  1.75 us
  transfers between devices with their start and end apart: 16, of which 9 were waited for; matrix products, arithmetic and copies ran while one was open for 0% of the time, Pallas kernels for 9%

profile of v24, /device:TPU:0, one launch (start us, length us, event | category | flops | bytes accessed | tf_op | source)
XLA Modules:
  0.0 41.9 jit_solution(8526247730224709512)
XLA Ops:
  0.0 5.0 %collective-permute-start.4 = (f32[512,128]{1,0:T(8,128)}, f32[512,128]{1,0:T(8,128)S(1)}, u32[]{:S(2)}, u32[]{:S(2)}) collective-permute-start(f32[512,128]{1,0:T(8,128)} %bitcast.44), channel_id=1, source_target_pairs={{0,6},{1,7},{2,4},{3,5},{4,2},{5,3},{6,0},{7,1},{8,14},{9,15},{10,... | collective-permute-start | bytes 786440 | tf_op jit(solution)/shard_map/ppermute | solution.py:225
  5.0 3.7 %restrict_operator.1 = (f32[4,520,128]{2,1,0:T(8,128)}, s32[2,8]{1,0:T(2,128)}, f32[512,128]{1,0:T(8,128)}) custom-call(s32[8]{0:T(128)} %count_any.1, s32[8,8]{1,0:T(8,128)} %slot_any.1, s32[2,8]{1,0:T(2,128)} %bitcast.47, s32[4,8]{1,0:T(4,128)} %bitcast.46, f32[8,64,128]{2,1,0:T(8,128)} %restrict_any.1, f32[8,64,512]{2,1,0:T(8,128)} %operator_any.1, ...), custom_call_target="tpu_custom_call" | custom-call | flops 201326592 | bytes 4194304 | tf_op jit(solution)/shard_map/restrict_operator/pallas_call | solution.py:131
  8.8 1.6 %collective-permute-start.1 = (f32[512,128]{1,0:T(8,128)}, f32[512,128]{1,0:T(8,128)S(1)}, u32[]{:S(2)}, u32[]{:S(2)}) collective-permute-start(f32[512,128]{1,0:T(8,128)} %get-tuple-element.9.rest_0_), channel_id=1, source_target_pairs={{0,16},{8,24},{16,0},{24,8},{1,17},{9,25},{17,1},{25,9},{2,18},{10... | collective-permute-start | bytes 786440 | tf_op jit(solution)/shard_map/ppermute | solution.py:215
  10.4 0.2 collective-permute-start.3
  10.6 3.6 %all-to-all-start = ((f32[4,520,128]{2,1,0:T(8,128)}), f32[4,520,128]{2,1,0:T(8,128)S(1)}, u32[]{:S(2)}, u32[]{:S(2)}) async-start(f32[4,520,128]{2,1,0:T(8,128)} %get-tuple-element.8), calls=%async_computation | async-start | bytes 2129920 | tf_op jit(solution)/shard_map/all_to_all | solution.py:285
  14.3 1.7 %collective-permute-done.3.far_columns_ref = s32[2,8]{1,0:T(2,128)S(1)} collective-permute-done((s32[2,8]{1,0:T(2,128)}, s32[2,8]{1,0:T(2,128)S(1)}, u32[]{:S(2)}, u32[]{:S(2)}) %collective-permute-start.3) | collective-permute-done | bytes 96 | tf_op jit(solution)/shard_map/ppermute | solution.py:225
  16.0 0.9 %collective-permute-done.1.next_ref.rest_2_ = f32[512,128]{1,0:T(8,128)S(1)} collective-permute-done((f32[512,128]{1,0:T(8,128)}, f32[512,128]{1,0:T(8,128)S(1)}, u32[]{:S(2)}, u32[]{:S(2)}) %collective-permute-start.1) | collective-permute-done | bytes 262176 | tf_op jit(solution)/shard_map/ppermute | solution.py:215
  16.9 1.6 %collective-permute-start.6 = (f32[520,128]{1,0:T(8,128)S(1)}, f32[520,128]{1,0:T(8,128)S(1)}, u32[]{:S(2)}, u32[]{:S(2)}) collective-permute-start(f32[520,128]{1,0:T(8,128)S(1)} %append_columns.1.rest_4_), channel_id=1, source_target_pairs={{0,16},{8,24},{16,0},{24,8},{1,17},{9,25},{17,1},{25,9},{2,18},{10... | collective-permute-start | bytes 798728 | tf_op jit(solution)/shard_map/ppermute | solution.py:215
  18.4 5.4 %collective-permute-done.6.rest_6_ = f32[520,128]{1,0:T(8,128)S(1)} collective-permute-done((f32[520,128]{1,0:T(8,128)S(1)}, f32[520,128]{1,0:T(8,128)S(1)}, u32[]{:S(2)}, u32[]{:S(2)}) %collective-permute-start.6) | collective-permute-done | bytes 266272 | tf_op jit(solution)/shard_map/ppermute | solution.py:215
  23.9 0.5 %collective-permute-start = (f32[512,128]{1,0:T(8,128)S(1)}, f32[512,128]{1,0:T(8,128)S(1)}, u32[]{:S(2)}, u32[]{:S(2)}) collective-permute-start(f32[512,128]{1,0:T(8,128)S(1)} %copy-done), channel_id=1, source_target_pairs={{0,8},{8,0},{16,24},{24,16},{1,9},{9,1},{17,25},{25,17},{2,10},{10... | collective-permute-start | bytes 786440 | tf_op jit(solution)/shard_map/ppermute | solution.py:215
  24.5 1.3 %collective-permute-done.rest_1_ = f32[512,128]{1,0:T(8,128)S(1)} collective-permute-done((f32[512,128]{1,0:T(8,128)S(1)}, f32[512,128]{1,0:T(8,128)S(1)}, u32[]{:S(2)}, u32[]{:S(2)}) %collective-permute-start) | collective-permute-done | bytes 262176 | tf_op jit(solution)/shard_map/ppermute | solution.py:215
  25.8 0.4 collective-permute-done.2.rest_3_
  26.2 1.4 %all-to-all-done.restricted_ref = f32[4,520,128]{2,1,0:T(8,128)S(1)} async-done(((f32[4,520,128]{2,1,0:T(8,128)}), f32[4,520,128]{2,1,0:T(8,128)S(1)}, u32[]{:S(2)}, u32[]{:S(2)}) %all-to-all-start) | async-done | bytes 1064992 | tf_op jit(solution)/shard_map/all_to_all | solution.py:285
  27.5 1.8 %combine.1 = f32[8,64,128]{2,1,0:T(8,128)S(1)} custom-call(s32[1,10]{1,0:T(1,128)S(1)} %add_bitcast_fusion.own_ref, f32[4,520,128]{2,1,0:T(8,128)S(1)} %all-to-all-done.restricted_ref, f32[512,128]{1,0:T(8,128)S(1)} %copy-done, f32[512,128]{1,0:T(8,128)S(1)} %collective-permute-done.rest_1_, f32[512,128]{1,0:T(8,128)S(1)} %collective-permute-done.1.next_ref.rest_2_, ...), custom_call_target="tpu_custom_call" | custom-call | flops 268435456 | bytes 4194304 | tf_op jit(solution)/shard_map/combine/pallas_call | solution.py:197
  29.3 1.5 %collective-permute-start.13 = (f32[64,128]{1,0:T(8,128)S(1)}, f32[64,128]{1,0:T(8,128)S(1)}, u32[]{:S(2)}, u32[]{:S(2)}) collective-permute-start(f32[64,128]{1,0:T(8,128)S(1)} %get-tuple-element.12), channel_id=1, source_target_pairs={{0,3},{1,2},{2,1},{3,0},{4,7},{5,6},{6,5},{7,4},{8,11},{9,10},{10,... | collective-permute-start | bytes 98312 | tf_op jit(solution)/shard_map/ppermute | solution.py:246
  30.8 1.5 %collective-permute-start.12 = (f32[64,128]{1,0:T(8,128)S(1)}, f32[64,128]{1,0:T(8,128)S(1)}, u32[]{:S(2)}, u32[]{:S(2)}) collective-permute-start(f32[64,128]{1,0:T(8,128)S(1)} %get-tuple-element.13), channel_id=1, source_target_pairs={{0,2},{1,3},{2,0},{3,1},{4,6},{5,7},{6,4},{7,5},{8,10},{9,11},{10,... | collective-permute-start | bytes 98312 | tf_op jit(solution)/shard_map/ppermute | solution.py:246
  32.3 0.6 %collective-permute-start.11 = (f32[64,128]{1,0:T(8,128)S(1)}, f32[64,128]{1,0:T(8,128)S(1)}, u32[]{:S(2)}, u32[]{:S(2)}) collective-permute-start(f32[64,128]{1,0:T(8,128)S(1)} %get-tuple-element.14), channel_id=1, source_target_pairs={{0,1},{1,0},{2,3},{3,2},{4,5},{5,4},{6,7},{7,6},{8,9},{9,8},{10,11... | collective-permute-start | bytes 98312 | tf_op jit(solution)/shard_map/ppermute | solution.py:246
  32.9 1.5 %collective-permute-start.8 = (f32[64,128]{1,0:T(8,128)S(1)}, f32[64,128]{1,0:T(8,128)S(1)}, u32[]{:S(2)}, u32[]{:S(2)}) collective-permute-start(f32[64,128]{1,0:T(8,128)S(1)} %get-tuple-element.11), channel_id=1, source_target_pairs={{0,1},{1,0},{2,3},{3,2},{4,5},{5,4},{6,7},{7,6},{8,9},{9,8},{10,11... | collective-permute-start | bytes 98312 | tf_op jit(solution)/shard_map/ppermute | solution.py:246
  34.3 1.4 %collective-permute-start.10 = (f32[64,128]{1,0:T(8,128)S(1)}, f32[64,128]{1,0:T(8,128)S(1)}, u32[]{:S(2)}, u32[]{:S(2)}) collective-permute-start(f32[64,128]{1,0:T(8,128)S(1)} %get-tuple-element.15), channel_id=1, source_target_pairs={{0,3},{1,2},{2,1},{3,0},{4,7},{5,6},{6,5},{7,4},{8,11},{9,10},{10,... | collective-permute-start | bytes 98312 | tf_op jit(solution)/shard_map/ppermute | solution.py:246
  35.7 0.6 %collective-permute-start.9 = (f32[64,128]{1,0:T(8,128)S(1)}, f32[64,128]{1,0:T(8,128)S(1)}, u32[]{:S(2)}, u32[]{:S(2)}) collective-permute-start(f32[64,128]{1,0:T(8,128)S(1)} %get-tuple-element.16), channel_id=1, source_target_pairs={{0,2},{1,3},{2,0},{3,1},{4,6},{5,7},{6,4},{7,5},{8,10},{9,11},{10,... | collective-permute-start | bytes 98312 | tf_op jit(solution)/shard_map/ppermute | solution.py:246
  36.4 2.6 %collective-permute-start.14 = (f32[64,128]{1,0:T(8,128)S(1)}, f32[64,128]{1,0:T(8,128)S(1)}, u32[]{:S(2)}, u32[]{:S(2)}) collective-permute-start(f32[64,128]{1,0:T(8,128)S(1)} %fusion.2), channel_id=1, source_target_pairs={{0,4},{4,0},{1,5},{5,1},{2,6},{6,2},{3,7},{7,3},{8,12},{12,8},{9,1... | collective-permute-start | bytes 98312 | tf_op jit(solution)/shard_map/ppermute | solution.py:219
  39.1 0.5 %collective-permute-done.9 = f32[64,128]{1,0:T(8,128)S(1)} collective-permute-done((f32[64,128]{1,0:T(8,128)S(1)}, f32[64,128]{1,0:T(8,128)S(1)}, u32[]{:S(2)}, u32[]{:S(2)}) %collective-permute-start.9) | collective-permute-done | bytes 32800 | tf_op jit(solution)/shard_map/ppermute | solution.py:246
  39.7 1.6 %collective-permute-done.14 = f32[64,128]{1,0:T(8,128)S(1)} collective-permute-done((f32[64,128]{1,0:T(8,128)S(1)}, f32[64,128]{1,0:T(8,128)S(1)}, u32[]{:S(2)}, u32[]{:S(2)}) %collective-permute-start.14) | collective-permute-done | bytes 32800 | tf_op jit(solution)/shard_map/ppermute | solution.py:219
  41.3 0.6 %fusion.7 = f32[128,64]{0,1:T(8,128)} fusion(f32[64,128]{1,0:T(8,128)S(1)} %collective-permute-done.14, f32[64,128]{1,0:T(8,128)S(1)} %collective-permute-done.10, f32[64,128]{1,0:T(8,128)S(1)} %collective-permute-done.9, f32[64,128]{1,0:T(8,128)S(1)} %collective-permute-done.8, f32[8,64,128]{2,1,0:T(8,128)S(1)} %combine.1), kind=kLoop, calls=%fused_computation.15 | loop fusion | flops 32768 | bytes 196608 | tf_op jit(solution)/shard_map/transpose | solution.py:291
  (20 shorter events, 0.3 us)
Async XLA Ops:
  0.0 16.0 %collective-permute-start.4 = (f32[512,128]{1,0:T(8,128)}, f32[512,128]{1,0:T(8,128)S(1)}, u32[]{:S(2)}, u32[]{:S(2)}) collective-permute-start(f32[512,128]{1,0:T(8,128)} %bitcast.44), channel_id=1, source_target_pairs={{0,6},{1,7},{2,4},{3,5},{4,2},{5,3},{6,0},{7,1},{8,14},{9,15},{10,... | collective-permute-start | bytes 786440 | tf_op jit(solution)/shard_map/ppermute | solution.py:225
  8.8 8.0 %collective-permute-start.1 = (f32[512,128]{1,0:T(8,128)}, f32[512,128]{1,0:T(8,128)S(1)}, u32[]{:S(2)}, u32[]{:S(2)}) collective-permute-start(f32[512,128]{1,0:T(8,128)} %get-tuple-element.9.rest_0_), channel_id=1, source_target_pairs={{0,16},{8,24},{16,0},{24,8},{1,17},{9,25},{17,1},{25,9},{2,18},{10... | collective-permute-start | bytes 786440 | tf_op jit(solution)/shard_map/ppermute | solution.py:215
  10.4 5.6 %collective-permute-start.3 = (s32[2,8]{1,0:T(2,128)}, s32[2,8]{1,0:T(2,128)S(1)}, u32[]{:S(2)}, u32[]{:S(2)}) collective-permute-start(s32[2,8]{1,0:T(2,128)} %get-tuple-element.10.own_columns_ref), channel_id=1, source_target_pairs={{0,6},{1,7},{2,4},{3,5},{4,2},{5,3},{6,0},{7,1},{8,14},{9,15},{10,... | collective-permute-start | bytes 200 | tf_op jit(solution)/shard_map/ppermute | solution.py:225
  10.6 6.2 %copy-start.1 = (s32[2,8]{1,0:T(2,128)S(1)}, s32[2,8]{1,0:T(2,128)}, u32[]{:S(2)}) copy-start(s32[2,8]{1,0:T(2,128)} %get-tuple-element.10.own_columns_ref) | copy-start | bytes 196
  10.6 16.9 %all-to-all-start = ((f32[4,520,128]{2,1,0:T(8,128)}), f32[4,520,128]{2,1,0:T(8,128)S(1)}, u32[]{:S(2)}, u32[]{:S(2)}) async-start(f32[4,520,128]{2,1,0:T(8,128)} %get-tuple-element.8), calls=%async_computation | async-start | bytes 2129920 | tf_op jit(solution)/shard_map/all_to_all | solution.py:285
  14.2 9.6 %copy-start = (f32[512,128]{1,0:T(8,128)S(1)}, f32[512,128]{1,0:T(8,128)}, u32[]{:S(2)}) copy-start(f32[512,128]{1,0:T(8,128)} %get-tuple-element.9.rest_0_) | copy-start | bytes 786436
  16.9 7.0 %collective-permute-start.6 = (f32[520,128]{1,0:T(8,128)S(1)}, f32[520,128]{1,0:T(8,128)S(1)}, u32[]{:S(2)}, u32[]{:S(2)}) collective-permute-start(f32[520,128]{1,0:T(8,128)S(1)} %append_columns.1.rest_4_), channel_id=1, source_target_pairs={{0,16},{8,24},{16,0},{24,8},{1,17},{9,25},{17,1},{25,9},{2,18},{10... | collective-permute-start | bytes 798728 | tf_op jit(solution)/shard_map/ppermute | solution.py:215
  18.4 7.7 %collective-permute-start.5 = (f32[520,128]{1,0:T(8,128)S(1)}, f32[520,128]{1,0:T(8,128)S(1)}, u32[]{:S(2)}, u32[]{:S(2)}) collective-permute-start(f32[520,128]{1,0:T(8,128)S(1)} %append_columns.1.rest_4_), channel_id=1, source_target_pairs={{0,8},{8,0},{16,24},{24,16},{1,9},{9,1},{17,25},{25,17},{2,10},{10... | collective-permute-start | bytes 798728 | tf_op jit(solution)/shard_map/ppermute | solution.py:215
  23.9 2.3 %collective-permute-start.7 = (f32[520,128]{1,0:T(8,128)S(1)}, f32[520,128]{1,0:T(8,128)S(1)}, u32[]{:S(2)}, u32[]{:S(2)}) collective-permute-start(f32[520,128]{1,0:T(8,128)S(1)} %collective-permute-done.6.rest_6_), channel_id=1, source_target_pairs={{0,8},{8,0},{16,24},{24,16},{1,9},{9,1},{17,25},{25,17},{2,10},{10... | collective-permute-start | bytes 798728 | tf_op jit(solution)/shard_map/ppermute | solution.py:215
  23.9 1.9 %collective-permute-start = (f32[512,128]{1,0:T(8,128)S(1)}, f32[512,128]{1,0:T(8,128)S(1)}, u32[]{:S(2)}, u32[]{:S(2)}) collective-permute-start(f32[512,128]{1,0:T(8,128)S(1)} %copy-done), channel_id=1, source_target_pairs={{0,8},{8,0},{16,24},{24,16},{1,9},{9,1},{17,25},{25,17},{2,10},{10... | collective-permute-start | bytes 786440 | tf_op jit(solution)/shard_map/ppermute | solution.py:215
  24.4 1.8 %collective-permute-start.2 = (f32[512,128]{1,0:T(8,128)S(1)}, f32[512,128]{1,0:T(8,128)S(1)}, u32[]{:S(2)}, u32[]{:S(2)}) collective-permute-start(f32[512,128]{1,0:T(8,128)S(1)} %collective-permute-done.1.next_ref.rest_2_), channel_id=1, source_target_pairs={{0,8},{8,0},{16,24},{24,16},{1,9},{9,1},{17,25},{25,17},{2,10},{10... | collective-permute-start | bytes 786440 | tf_op jit(solution)/shard_map/ppermute | solution.py:215
  29.3 6.4 %collective-permute-start.13 = (f32[64,128]{1,0:T(8,128)S(1)}, f32[64,128]{1,0:T(8,128)S(1)}, u32[]{:S(2)}, u32[]{:S(2)}) collective-permute-start(f32[64,128]{1,0:T(8,128)S(1)} %get-tuple-element.12), channel_id=1, source_target_pairs={{0,3},{1,2},{2,1},{3,0},{4,7},{5,6},{6,5},{7,4},{8,11},{9,10},{10,... | collective-permute-start | bytes 98312 | tf_op jit(solution)/shard_map/ppermute | solution.py:246
  30.8 5.5 %collective-permute-start.12 = (f32[64,128]{1,0:T(8,128)S(1)}, f32[64,128]{1,0:T(8,128)S(1)}, u32[]{:S(2)}, u32[]{:S(2)}) collective-permute-start(f32[64,128]{1,0:T(8,128)S(1)} %get-tuple-element.13), channel_id=1, source_target_pairs={{0,2},{1,3},{2,0},{3,1},{4,6},{5,7},{6,4},{7,5},{8,10},{9,11},{10,... | collective-permute-start | bytes 98312 | tf_op jit(solution)/shard_map/ppermute | solution.py:246
  32.3 4.1 %collective-permute-start.11 = (f32[64,128]{1,0:T(8,128)S(1)}, f32[64,128]{1,0:T(8,128)S(1)}, u32[]{:S(2)}, u32[]{:S(2)}) collective-permute-start(f32[64,128]{1,0:T(8,128)S(1)} %get-tuple-element.14), channel_id=1, source_target_pairs={{0,1},{1,0},{2,3},{3,2},{4,5},{5,4},{6,7},{7,6},{8,9},{9,8},{10,11... | collective-permute-start | bytes 98312 | tf_op jit(solution)/shard_map/ppermute | solution.py:246
  32.9 6.1 %collective-permute-start.8 = (f32[64,128]{1,0:T(8,128)S(1)}, f32[64,128]{1,0:T(8,128)S(1)}, u32[]{:S(2)}, u32[]{:S(2)}) collective-permute-start(f32[64,128]{1,0:T(8,128)S(1)} %get-tuple-element.11), channel_id=1, source_target_pairs={{0,1},{1,0},{2,3},{3,2},{4,5},{5,4},{6,7},{7,6},{8,9},{9,8},{10,11... | collective-permute-start | bytes 98312 | tf_op jit(solution)/shard_map/ppermute | solution.py:246
  34.3 4.8 %collective-permute-start.10 = (f32[64,128]{1,0:T(8,128)S(1)}, f32[64,128]{1,0:T(8,128)S(1)}, u32[]{:S(2)}, u32[]{:S(2)}) collective-permute-start(f32[64,128]{1,0:T(8,128)S(1)} %get-tuple-element.15), channel_id=1, source_target_pairs={{0,3},{1,2},{2,1},{3,0},{4,7},{5,6},{6,5},{7,4},{8,11},{9,10},{10,... | collective-permute-start | bytes 98312 | tf_op jit(solution)/shard_map/ppermute | solution.py:246
  35.7 3.9 %collective-permute-start.9 = (f32[64,128]{1,0:T(8,128)S(1)}, f32[64,128]{1,0:T(8,128)S(1)}, u32[]{:S(2)}, u32[]{:S(2)}) collective-permute-start(f32[64,128]{1,0:T(8,128)S(1)} %get-tuple-element.16), channel_id=1, source_target_pairs={{0,2},{1,3},{2,0},{3,1},{4,6},{5,7},{6,4},{7,5},{8,10},{9,11},{10,... | collective-permute-start | bytes 98312 | tf_op jit(solution)/shard_map/ppermute | solution.py:246
  36.4 4.9 %collective-permute-start.14 = (f32[64,128]{1,0:T(8,128)S(1)}, f32[64,128]{1,0:T(8,128)S(1)}, u32[]{:S(2)}, u32[]{:S(2)}) collective-permute-start(f32[64,128]{1,0:T(8,128)S(1)} %fusion.2), channel_id=1, source_target_pairs={{0,4},{4,0},{1,5},{5,1},{2,6},{6,2},{3,7},{7,3},{8,12},{12,8},{9,1... | collective-permute-start | bytes 98312 | tf_op jit(solution)/shard_map/ppermute | solution.py:219

commit v25 on v22

--- a/solution.py
+++ b/solution.py
@@ -20,8 +20,11 @@
     return high, (x - high.astype(jnp.float32)).astype(jnp.bfloat16)
 
 
-def transposed_product(left, right):
-    tall = jnp.concatenate(halves(left), axis=0)
+def tall_halves(left):
+    return jnp.concatenate(halves(left), axis=0)
+
+
+def transposed_product(tall, right):
     wide = jnp.concatenate(halves(right), axis=1)
     wide = jnp.concatenate([wide, wide], axis=0)
     both = lax.dot_general(tall, wide, (((0,), (0,)), ((), ())), preferred_element_type=jnp.float32)
@@ -98,7 +101,7 @@
         own_row = jnp.where(second == 0, rows_ref[0, i], rows_ref[1, i])
         other_row = jnp.where(second == 0, rows_ref[1, i], rows_ref[0, i])
         dense = jnp.where(own_row == second, value, 0.0) + jnp.where(other_row == second, swapped, 0.0)
-        product = transposed_product(operator_ref[i], dense)
+        product = transposed_product(tall_halves(operator_ref[i]), dense)
         for k in range(entries):
             part = jnp.where(k < count_ref[i], product[k * block_size : (k + 1) * block_size], 0.0)
             peer = lax.div(slot_ref[i, k], slot_count)
@@ -137,27 +140,54 @@
     )(*small, restrict_blocks, operator_blocks, own_columns, own_blocks, side)
 
 
-def combine_kernel(own_ref, restricted_ref, *rest, slot_count, fine_rows, entries):
-    pieces, (out_ref, held_ref, table_ref, index_ref, sem) = rest[:-5], rest[-5:]
+def prepare_kernel(*refs, fine_rows, entries):
+    pieces, (held_ref, columns_ref) = refs[:-2], refs[-2:]
+    rows = len(pieces) // 2
+    block_size = held_ref.shape[2] // 2
+    held = fine_rows * block_size
+    for i, piece in enumerate(pieces):
+        for inside in range(fine_rows):
+            held_ref[i, inside] = tall_halves(piece[inside * block_size : (inside + 1) * block_size])
+    for i, piece in enumerate(pieces[rows:]):
+        for far in range(2):
+            first = entries * (far * rows + i)
+            row = held + entries * (1 - far)
+            columns_ref[first : first + entries] = piece[row : row + entries].astype(jnp.int32)
+
+
+def prepare(pieces, fine_rows, block_size):
+    width = pieces[0].shape[1]
+    entries = width // block_size
+    return pl.pallas_call(
+        functools.partial(prepare_kernel, fine_rows=fine_rows, entries=entries),
+        out_shape=(
+            jax.ShapeDtypeStruct((len(pieces), fine_rows, 2 * block_size, width), jnp.bfloat16),
+            jax.ShapeDtypeStruct((entries * len(pieces), LANES), jnp.int32),
+        ),
+        in_specs=[pl.BlockSpec(memory_space=pltpu.VMEM)] * len(pieces),
+        out_specs=[pl.BlockSpec(memory_space=pltpu.VMEM)] * 2,
+        compiler_params=pltpu.CompilerParams(vmem_limit_bytes=VMEM_LIMIT),
+        cost_estimate=pl.CostEstimate(flops=1 << 20, bytes_accessed=4 << 20, transcendentals=0),
+        name="prepare",
+    )(*pieces)
+
+
+def combine_kernel(
+    own_ref, columns_ref, restricted_ref, held_ref, out_ref, table_ref, index_ref, sem, *, slot_count, entries
+):
     half = restricted_ref.shape[0]
-    rows = len(pieces) // 2
+    rows = held_ref.shape[0] // 2
+    fine_rows = held_ref.shape[1]
     block_size = out_ref.shape[1]
     columns = 2 * half
     used = 2 * slot_count * block_size
-    held = fine_rows * block_size
 
     table_ref[:1, : own_ref.shape[1]] = own_ref[...]
     for near in range(half):
         table_ref[1 + near : 2 + near] = restricted_ref[near, used : used + 1].astype(jnp.int32)
-    for i, piece in enumerate(pieces[rows:]):
-        for far in range(2):
-            first = 1 + half + entries * (far * rows + i)
-            row = held + entries * (1 - far)
-            table_ref[first : first + entries] = piece[row : row + entries].astype(jnp.int32)
+    table_ref[1 + half : 1 + half + columns_ref.shape[0]] = columns_ref[...]
     copy = pltpu.make_async_copy(table_ref, index_ref, sem)
     copy.start()
-    for i, piece in enumerate(pieces):
-        held_ref[i] = piece[...] if i < rows else piece[:held]
     out_ref[...] = jnp.zeros_like(out_ref)
     copy.wait()
 
@@ -168,9 +198,8 @@
         inside = lax.rem(wanted, fine_rows)
         far = lax.div(place, slot_count) ^ index_ref[0, 1]
         piece = far * rows + (lax.div(wanted, fine_rows * columns) ^ index_ref[0, 0])
-        block = held_ref[piece, pl.ds(pl.multiple_of(inside * block_size, block_size), block_size)]
         restricted = restricted_ref[near, pl.ds(pl.multiple_of(place * block_size, block_size), block_size)]
-        product = transposed_product(block, restricted)
+        product = transposed_product(held_ref[piece, inside], restricted)
         for m in range(entries):
             column = index_ref[0, 2 + index_ref[1 + half + entries * piece + m, inside]]
             out_ref[column] += product[m * block_size : (m + 1) * block_size]
@@ -179,18 +208,16 @@
     lax.fori_loop(0, half * 2 * slot_count, step, 0, unroll=16)
 
 
-def combine(own, restricted, pieces, coarse_all, slot_count, fine_rows, block_size):
+def combine(own, columns, restricted, held, coarse_all, slot_count, block_size):
     half, _, wide = restricted.shape
-    width = pieces[0].shape[1]
-    entries = width // block_size
-    table_rows = -(-(1 + half + entries * len(pieces)) // 8) * 8
+    entries = held.shape[3] // block_size
+    table_rows = -(-(1 + half + columns.shape[0]) // 8) * 8
     return pl.pallas_call(
-        functools.partial(combine_kernel, slot_count=slot_count, fine_rows=fine_rows, entries=entries),
+        functools.partial(combine_kernel, slot_count=slot_count, entries=entries),
         out_shape=jax.ShapeDtypeStruct((coarse_all, block_size, wide), jnp.float32),
-        in_specs=[pl.BlockSpec(memory_space=pltpu.VMEM)] * (2 + len(pieces)),
+        in_specs=[pl.BlockSpec(memory_space=pltpu.VMEM)] * 4,
         out_specs=pl.BlockSpec(memory_space=pltpu.VMEM),
         scratch_shapes=[
-            pltpu.VMEM((len(pieces), fine_rows * block_size, width), jnp.float32),
             pltpu.VMEM((table_rows, LANES), jnp.int32),
             pltpu.SMEM((table_rows, LANES), jnp.int32),
             pltpu.SemaphoreType.DMA,
@@ -198,7 +225,7 @@
         compiler_params=pltpu.CompilerParams(vmem_limit_bytes=VMEM_LIMIT),
         cost_estimate=pl.CostEstimate(flops=1 << 28, bytes_accessed=4 << 20, transcendentals=0),
         name="combine",
-    )(own, restricted, *pieces)
+    )(own, columns, restricted, held)
 
 
 def row_swap(x, bit):
@@ -277,7 +304,8 @@
     near_pieces = spread_over_rows(near_blocks, rows)
     far_blocks = append_columns(near_pieces[rows // 2], far_columns, own_columns, far_blocks)
     pieces = near_pieces + spread_over_rows(far_blocks, rows)
-    sums = combine(own, restricted, pieces, NCR * rows, slot_count, fine_rows, block_size)
+    held, columns = prepare(pieces, fine_rows, block_size)
+    sums = combine(own, columns, restricted, held, NCR * rows, slot_count, block_size)
     return add_over_columns(sums, half).T
 
 

time: 41.9 us -> 50.6 us (1.21)
  local copies, waits for them, and re-layouts: 0.02 us -> 10.2 us
  waiting for transfers between devices: 13.3 us -> 12.1 us
  starting transfers between devices: 22.2 us -> 21.5 us
    unnamed x4 -> x30, local copies, waits for them, and re-layouts: 0.01 us -> 10.2 us
    all_to_all x1, waiting for transfers between devices: 1.37 us -> 0.01 us  [local(): lax.all_to_all(restricted, 'near', split_axis=0, concat_axis=0, tiled=True)]
    ppermute x1, starting transfers between devices: 2.6 us -> 1.76 us  [half_swap(): return lax.ppermute(x, 'half', [(0, 1), (1, 0)])]
    ppermute x6, waiting for transfers between devices: 7.99 us -> 7.3 us  [row_swap(): lax.ppermute(x, 'row', [(r, r ^ bit) for r in range(lax.axis_size('row'))])]
    ppermute x6, waiting for transfers between devices: 0.69 us -> 1.32 us  [add_over_near(): lax.ppermute(sums[near], 'near', [(n, n ^ near) for n in range(half)])]
    pallas_call x1 -> x2, Pallas kernels: 1.76 us -> 2 us  [the longest x1 1.79 us: combine(): pl.pallas_call(functools.partial(combine_kernel, slot_count=slot_count, e...]
  transfers between devices with their start and end apart: 16 -> 16, of which waited for: 9 -> 7; matrix products, arithmetic and copies ran while one was open for 0% -> 0% of each run, Pallas kernels for 8% -> 7%
where the time goes in v25:
time: 50.6 us; the launch traced here: 50.2 us
  starting transfers between devices  21.5 us (42%)
  waiting for transfers between devices  12.1 us (24%)
  local copies, waits for them, and re-layouts  10.2 us (20%)
  Pallas kernels  5.53 us (11%)
  other arithmetic  0.72 us (1%)
    unnamed x30, local copies, waits for them, and re-layouts  10.2 us
    ppermute x6, waiting for transfers between devices, row_swap(): lax.ppermute(x, 'row', [(r, r ^ bit) for r in range(lax.axis_size('row'))])  7.3 us
    ppermute x6, starting transfers between devices, add_over_near(): lax.ppermute(sums[near], 'near', [(n, n ^ near) for n in range(half)])  7.06 us
    ppermute x2, starting transfers between devices, far_swap(): return lax.ppermute(x, ('half', 'near'), pairs)  5.27 us
    ppermute x6, starting transfers between devices, row_swap(): lax.ppermute(x, 'row', [(r, r ^ bit) for r in range(lax.axis_size('row'))])  3.75 us
    all_to_all x1, starting transfers between devices, local(): lax.all_to_all(restricted, 'near', split_axis=0, concat_axis=0, tiled=True)  3.65 us
    pallas_call x1, Pallas kernels, restrict_operator(): pl.pallas_call(restrict_kernel, out_shape=(jax.ShapeDtypeStruct((columns...  3.51 us
    ppermute x1, waiting for transfers between devices, half_swap(): return lax.ppermute(x, 'half', [(0, 1), (1, 0)])  1.81 us
  transfers between devices with their start and end apart: 16, of which 7 were waited for; matrix products, arithmetic and copies ran while one was open for 0% of the time, Pallas kernels for 7%

profile of v25, /device:TPU:0, one launch (start us, length us, event | category | flops | bytes accessed | tf_op | source)
XLA Modules:
  0.0 50.2 jit_solution(8371728839214677366)
XLA Ops:
  0.0 5.0 %collective-permute-start.4 = (f32[512,128]{1,0:T(8,128)}, f32[512,128]{1,0:T(8,128)S(1)}, u32[]{:S(2)}, u32[]{:S(2)}) collective-permute-start(f32[512,128]{1,0:T(8,128)} %bitcast.44), channel_id=1, source_target_pairs={{0,6},{1,7},{2,4},{3,5},{4,2},{5,3},{6,0},{7,1},{8,14},{9,15},{10,... | collective-permute-start | bytes 786440 | tf_op jit(solution)/shard_map/ppermute | solution.py:242
  5.0 3.5 %restrict_operator.1 = (f32[4,520,128]{2,1,0:T(8,128)}, s32[2,8]{1,0:T(2,128)}, f32[512,128]{1,0:T(8,128)}) custom-call(s32[8]{0:T(128)} %count_any.1, s32[8,8]{1,0:T(8,128)} %slot_any.1, s32[2,8]{1,0:T(2,128)} %bitcast.47, s32[4,8]{1,0:T(4,128)} %bitcast.46, f32[8,64,128]{2,1,0:T(8,128)} %restrict_any.1, f32[8,64,512]{2,1,0:T(8,128)} %operator_any.1, ...), custom_call_target="tpu_custom_call" | custom-call | flops 201326592 | bytes 4194304 | tf_op jit(solution)/shard_map/restrict_operator/pallas_call | solution.py:124
  8.6 1.6 %collective-permute-start.1 = (f32[512,128]{1,0:T(8,128)}, f32[512,128]{1,0:T(8,128)S(1)}, u32[]{:S(2)}, u32[]{:S(2)}) collective-permute-start(f32[512,128]{1,0:T(8,128)} %get-tuple-element.10.refs_0_), channel_id=1, source_target_pairs={{0,16},{8,24},{16,0},{24,8},{1,17},{9,25},{17,1},{25,9},{2,18},{10... | collective-permute-start | bytes 786440 | tf_op jit(solution)/shard_map/ppermute | solution.py:232
  10.4 3.6 %all-to-all-start = ((f32[4,520,128]{2,1,0:T(8,128)}), f32[4,520,128]{2,1,0:T(8,128)S(1)}, u32[]{:S(2)}, u32[]{:S(2)}) async-start(f32[4,520,128]{2,1,0:T(8,128)} %get-tuple-element.13), calls=%async_computation | async-start | bytes 2129920 | tf_op jit(solution)/shard_map/all_to_all | solution.py:302
  14.0 1.7 %collective-permute-done.3.far_columns_ref = s32[2,8]{1,0:T(2,128)S(1)} collective-permute-done((s32[2,8]{1,0:T(2,128)}, s32[2,8]{1,0:T(2,128)S(1)}, u32[]{:S(2)}, u32[]{:S(2)}) %collective-permute-start.3) | collective-permute-done | bytes 96 | tf_op jit(solution)/shard_map/ppermute | solution.py:242
  15.7 0.9 %collective-permute-done.1.next_ref.refs_2_ = f32[512,128]{1,0:T(8,128)S(1)} collective-permute-done((f32[512,128]{1,0:T(8,128)}, f32[512,128]{1,0:T(8,128)S(1)}, u32[]{:S(2)}, u32[]{:S(2)}) %collective-permute-start.1) | collective-permute-done | bytes 262176 | tf_op jit(solution)/shard_map/ppermute | solution.py:232
  16.6 1.6 %collective-permute-start.6 = (f32[520,128]{1,0:T(8,128)S(1)}, f32[520,128]{1,0:T(8,128)S(1)}, u32[]{:S(2)}, u32[]{:S(2)}) collective-permute-start(f32[520,128]{1,0:T(8,128)S(1)} %append_columns.1.refs_4_), channel_id=1, source_target_pairs={{0,16},{8,24},{16,0},{24,8},{1,17},{9,25},{17,1},{25,9},{2,18},{10... | collective-permute-start | bytes 798728 | tf_op jit(solution)/shard_map/ppermute | solution.py:232
  18.2 5.4 %collective-permute-done.6.refs_6_ = f32[520,128]{1,0:T(8,128)S(1)} collective-permute-done((f32[520,128]{1,0:T(8,128)S(1)}, f32[520,128]{1,0:T(8,128)S(1)}, u32[]{:S(2)}, u32[]{:S(2)}) %collective-permute-start.6) | collective-permute-done | bytes 266272 | tf_op jit(solution)/shard_map/ppermute | solution.py:232
  25.0 1.0 %collective-permute-done.refs_1_ = f32[512,128]{1,0:T(8,128)S(1)} collective-permute-done((f32[512,128]{1,0:T(8,128)S(1)}, f32[512,128]{1,0:T(8,128)S(1)}, u32[]{:S(2)}, u32[]{:S(2)}) %collective-permute-start) | collective-permute-done | bytes 262176 | tf_op jit(solution)/shard_map/ppermute | solution.py:232
  28.9 0.9 %copy-done.1 = f32[520,128]{1,0:T(8,128)S(1)} copy-done((f32[520,128]{1,0:T(8,128)S(1)}, f32[520,128]{1,0:T(8,128)}, u32[]{:S(2)}) %copy-start.1) | copy-done | bytes 266264
  29.8 0.9 %copy-done.3 = f32[520,128]{1,0:T(8,128)S(1)} copy-done((f32[520,128]{1,0:T(8,128)S(1)}, f32[520,128]{1,0:T(8,128)}, u32[]{:S(2)}) %copy-start.3) | copy-done | bytes 266264
  30.8 0.9 %copy-done.5 = f32[520,128]{1,0:T(8,128)S(1)} copy-done((f32[520,128]{1,0:T(8,128)S(1)}, f32[520,128]{1,0:T(8,128)}, u32[]{:S(2)}) %copy-start.5) | copy-done | bytes 266264
  31.7 0.9 %copy-done.7 = f32[512,128]{1,0:T(8,128)S(1)} copy-done((f32[512,128]{1,0:T(8,128)S(1)}, f32[512,128]{1,0:T(8,128)}, u32[]{:S(2)}) %copy-start.7) | copy-done | bytes 262168
  32.7 0.9 %copy-done.9 = f32[512,128]{1,0:T(8,128)S(1)} copy-done((f32[512,128]{1,0:T(8,128)S(1)}, f32[512,128]{1,0:T(8,128)}, u32[]{:S(2)}) %copy-start.9) | copy-done | bytes 262168
  33.6 0.9 %copy-done.11 = f32[512,128]{1,0:T(8,128)S(1)} copy-done((f32[512,128]{1,0:T(8,128)S(1)}, f32[512,128]{1,0:T(8,128)}, u32[]{:S(2)}) %copy-start.11) | copy-done | bytes 262168
  34.6 0.9 %copy-done.13 = f32[512,128]{1,0:T(8,128)S(1)} copy-done((f32[512,128]{1,0:T(8,128)S(1)}, f32[512,128]{1,0:T(8,128)}, u32[]{:S(2)}) %copy-start.13) | copy-done | bytes 262168
  35.7 1.8 %combine.1 = f32[8,64,128]{2,1,0:T(8,128)S(1)} custom-call(s32[1,10]{1,0:T(1,128)S(1)} %add_bitcast_fusion.own_ref, s32[16,128]{1,0:T(8,128)S(1)} %get-tuple-element.12.columns_ref, f32[4,520,128]{2,1,0:T(8,128)S(1)} %all-to-all-done.restricted_ref, bf16[8,8,128,128]{3,2,1,0:T(8,128)(2,1)S(1)} %get-tuple-element.14.held_ref), custom_call_target="tpu_custom_call" | custom-call | flops 268435456 | bytes 4194304 | tf_op jit(solution)/shard_map/combine/pallas_call | solution.py:215
  37.6 1.9 %collective-permute-start.13 = (f32[64,128]{1,0:T(8,128)S(1)}, f32[64,128]{1,0:T(8,128)S(1)}, u32[]{:S(2)}, u32[]{:S(2)}) collective-permute-start(f32[64,128]{1,0:T(8,128)S(1)} %get-tuple-element.16), channel_id=1, source_target_pairs={{0,3},{1,2},{2,1},{3,0},{4,7},{5,6},{6,5},{7,4},{8,11},{9,10},{10,... | collective-permute-start | bytes 98312 | tf_op jit(solution)/shard_map/ppermute | solution.py:263
  39.4 1.2 %collective-permute-start.12 = (f32[64,128]{1,0:T(8,128)S(1)}, f32[64,128]{1,0:T(8,128)S(1)}, u32[]{:S(2)}, u32[]{:S(2)}) collective-permute-start(f32[64,128]{1,0:T(8,128)S(1)} %get-tuple-element.17), channel_id=1, source_target_pairs={{0,2},{1,3},{2,0},{3,1},{4,6},{5,7},{6,4},{7,5},{8,10},{9,11},{10,... | collective-permute-start | bytes 98312 | tf_op jit(solution)/shard_map/ppermute | solution.py:263
  41.1 1.5 %collective-permute-start.8 = (f32[64,128]{1,0:T(8,128)S(1)}, f32[64,128]{1,0:T(8,128)S(1)}, u32[]{:S(2)}, u32[]{:S(2)}) collective-permute-start(f32[64,128]{1,0:T(8,128)S(1)} %get-tuple-element.15), channel_id=1, source_target_pairs={{0,1},{1,0},{2,3},{3,2},{4,5},{5,4},{6,7},{7,6},{8,9},{9,8},{10,11... | collective-permute-start | bytes 98312 | tf_op jit(solution)/shard_map/ppermute | solution.py:263
  43.5 1.2 %collective-permute-start.9 = (f32[64,128]{1,0:T(8,128)S(1)}, f32[64,128]{1,0:T(8,128)S(1)}, u32[]{:S(2)}, u32[]{:S(2)}) collective-permute-start(f32[64,128]{1,0:T(8,128)S(1)} %get-tuple-element.20), channel_id=1, source_target_pairs={{0,2},{1,3},{2,0},{3,1},{4,6},{5,7},{6,4},{7,5},{8,10},{9,11},{10,... | collective-permute-start | bytes 98312 | tf_op jit(solution)/shard_map/ppermute | solution.py:263
  44.6 1.8 %collective-permute-start.14 = (f32[64,128]{1,0:T(8,128)S(1)}, f32[64,128]{1,0:T(8,128)S(1)}, u32[]{:S(2)}, u32[]{:S(2)}) collective-permute-start(f32[64,128]{1,0:T(8,128)S(1)} %fusion.2), channel_id=1, source_target_pairs={{0,4},{4,0},{1,5},{5,1},{2,6},{6,2},{3,7},{7,3},{8,12},{12,8},{9,1... | collective-permute-start | bytes 98312 | tf_op jit(solution)/shard_map/ppermute | solution.py:236
  46.4 1.0 %collective-permute-done.10 = f32[64,128]{1,0:T(8,128)S(1)} collective-permute-done((f32[64,128]{1,0:T(8,128)S(1)}, f32[64,128]{1,0:T(8,128)S(1)}, u32[]{:S(2)}, u32[]{:S(2)}) %collective-permute-start.10) | collective-permute-done | bytes 32800 | tf_op jit(solution)/shard_map/ppermute | solution.py:263
  47.7 1.8 %collective-permute-done.14 = f32[64,128]{1,0:T(8,128)S(1)} collective-permute-done((f32[64,128]{1,0:T(8,128)S(1)}, f32[64,128]{1,0:T(8,128)S(1)}, u32[]{:S(2)}, u32[]{:S(2)}) %collective-permute-start.14) | collective-permute-done | bytes 32800 | tf_op jit(solution)/shard_map/ppermute | solution.py:236
  (47 shorter events, 7.0 us)
Async XLA Ops:
  0.0 15.7 %collective-permute-start.4 = (f32[512,128]{1,0:T(8,128)}, f32[512,128]{1,0:T(8,128)S(1)}, u32[]{:S(2)}, u32[]{:S(2)}) collective-permute-start(f32[512,128]{1,0:T(8,128)} %bitcast.44), channel_id=1, source_target_pairs={{0,6},{1,7},{2,4},{3,5},{4,2},{5,3},{6,0},{7,1},{8,14},{9,15},{10,... | collective-permute-start | bytes 786440 | tf_op jit(solution)/shard_map/ppermute | solution.py:242
  8.6 8.0 %collective-permute-start.1 = (f32[512,128]{1,0:T(8,128)}, f32[512,128]{1,0:T(8,128)S(1)}, u32[]{:S(2)}, u32[]{:S(2)}) collective-permute-start(f32[512,128]{1,0:T(8,128)} %get-tuple-element.10.refs_0_), channel_id=1, source_target_pairs={{0,16},{8,24},{16,0},{24,8},{1,17},{9,25},{17,1},{25,9},{2,18},{10... | collective-permute-start | bytes 786440 | tf_op jit(solution)/shard_map/ppermute | solution.py:232
  10.1 5.6 %collective-permute-start.3 = (s32[2,8]{1,0:T(2,128)}, s32[2,8]{1,0:T(2,128)S(1)}, u32[]{:S(2)}, u32[]{:S(2)}) collective-permute-start(s32[2,8]{1,0:T(2,128)} %get-tuple-element.11.own_columns_ref), channel_id=1, source_target_pairs={{0,6},{1,7},{2,4},{3,5},{4,2},{5,3},{6,0},{7,1},{8,14},{9,15},{10,... | collective-permute-start | bytes 200 | tf_op jit(solution)/shard_map/ppermute | solution.py:242
  10.4 6.2 %copy-start.14 = (s32[2,8]{1,0:T(2,128)S(1)}, s32[2,8]{1,0:T(2,128)}, u32[]{:S(2)}) copy-start(s32[2,8]{1,0:T(2,128)} %get-tuple-element.11.own_columns_ref) | copy-start | bytes 196
  10.4 25.4 %all-to-all-start = ((f32[4,520,128]{2,1,0:T(8,128)}), f32[4,520,128]{2,1,0:T(8,128)S(1)}, u32[]{:S(2)}, u32[]{:S(2)}) async-start(f32[4,520,128]{2,1,0:T(8,128)} %get-tuple-element.13), calls=%async_computation | async-start | bytes 2129920 | tf_op jit(solution)/shard_map/all_to_all | solution.py:302
  14.0 10.3 %copy-start.6 = (f32[512,128]{1,0:T(8,128)S(1)}, f32[512,128]{1,0:T(8,128)}, u32[]{:S(2)}) copy-start(f32[512,128]{1,0:T(8,128)} %get-tuple-element.10.refs_0_) | copy-start | bytes 786436
  16.6 8.2 %copy-start.8 = (f32[512,128]{1,0:T(8,128)}, f32[512,128]{1,0:T(8,128)S(1)}, u32[]{:S(2)}) copy-start(f32[512,128]{1,0:T(8,128)S(1)} %collective-permute-done.1.next_ref.refs_2_) | copy-start | bytes 786436
  16.6 7.0 %collective-permute-start.6 = (f32[520,128]{1,0:T(8,128)S(1)}, f32[520,128]{1,0:T(8,128)S(1)}, u32[]{:S(2)}, u32[]{:S(2)}) collective-permute-start(f32[520,128]{1,0:T(8,128)S(1)} %append_columns.1.refs_4_), channel_id=1, source_target_pairs={{0,16},{8,24},{16,0},{24,8},{1,17},{9,25},{17,1},{25,9},{2,18},{10... | collective-permute-start | bytes 798728 | tf_op jit(solution)/shard_map/ppermute | solution.py:232
  18.2 9.2 %collective-permute-start.5 = (f32[520,128]{1,0:T(8,128)S(1)}, f32[520,128]{1,0:T(8,128)S(1)}, u32[]{:S(2)}, u32[]{:S(2)}) collective-permute-start(f32[520,128]{1,0:T(8,128)S(1)} %append_columns.1.refs_4_), channel_id=1, source_target_pairs={{0,8},{8,0},{16,24},{24,16},{1,9},{9,1},{17,25},{25,17},{2,10},{10... | collective-permute-start | bytes 798728 | tf_op jit(solution)/shard_map/ppermute | solution.py:232
  23.6 4.5 %collective-permute-start.7 = (f32[520,128]{1,0:T(8,128)S(1)}, f32[520,128]{1,0:T(8,128)S(1)}, u32[]{:S(2)}, u32[]{:S(2)}) collective-permute-start(f32[520,128]{1,0:T(8,128)S(1)} %collective-permute-done.6.refs_6_), channel_id=1, source_target_pairs={{0,8},{8,0},{16,24},{24,16},{1,9},{9,1},{17,25},{25,17},{2,10},{10... | collective-permute-start | bytes 798728 | tf_op jit(solution)/shard_map/ppermute | solution.py:232
  24.3 1.7 %collective-permute-start = (f32[512,128]{1,0:T(8,128)S(1)}, f32[512,128]{1,0:T(8,128)S(1)}, u32[]{:S(2)}, u32[]{:S(2)}) collective-permute-start(f32[512,128]{1,0:T(8,128)S(1)} %copy-done.6), channel_id=1, source_target_pairs={{0,8},{8,0},{16,24},{24,16},{1,9},{9,1},{17,25},{25,17},{2,10},{10... | collective-permute-start | bytes 786440 | tf_op jit(solution)/shard_map/ppermute | solution.py:232
  24.9 1.9 %collective-permute-start.2 = (f32[512,128]{1,0:T(8,128)S(1)}, f32[512,128]{1,0:T(8,128)S(1)}, u32[]{:S(2)}, u32[]{:S(2)}) collective-permute-start(f32[512,128]{1,0:T(8,128)S(1)} %collective-permute-done.1.next_ref.refs_2_), channel_id=1, source_target_pairs={{0,8},{8,0},{16,24},{24,16},{1,9},{9,1},{17,25},{25,17},{2,10},{10... | collective-permute-start | bytes 786440 | tf_op jit(solution)/shard_map/ppermute | solution.py:232
  28.9 1.0 %copy-start.1 = (f32[520,128]{1,0:T(8,128)S(1)}, f32[520,128]{1,0:T(8,128)}, u32[]{:S(2)}) copy-start(f32[520,128]{1,0:T(8,128)} %copy-done) | copy-start | bytes 798724
  29.8 1.0 %copy-start.3 = (f32[520,128]{1,0:T(8,128)S(1)}, f32[520,128]{1,0:T(8,128)}, u32[]{:S(2)}) copy-start(f32[520,128]{1,0:T(8,128)} %copy-done.2) | copy-start | bytes 798724
  30.8 1.0 %copy-start.5 = (f32[520,128]{1,0:T(8,128)S(1)}, f32[520,128]{1,0:T(8,128)}, u32[]{:S(2)}) copy-start(f32[520,128]{1,0:T(8,128)} %copy-done.4) | copy-start | bytes 798724
  31.7 0.9 %copy-start.7 = (f32[512,128]{1,0:T(8,128)S(1)}, f32[512,128]{1,0:T(8,128)}, u32[]{:S(2)}) copy-start(f32[512,128]{1,0:T(8,128)} %get-tuple-element.10.refs_0_) | copy-start | bytes 786436
  32.7 0.9 %copy-start.9 = (f32[512,128]{1,0:T(8,128)S(1)}, f32[512,128]{1,0:T(8,128)}, u32[]{:S(2)}) copy-start(f32[512,128]{1,0:T(8,128)} %copy-done.8) | copy-start | bytes 786436
  37.6 5.9 %collective-permute-start.13 = (f32[64,128]{1,0:T(8,128)S(1)}, f32[64,128]{1,0:T(8,128)S(1)}, u32[]{:S(2)}, u32[]{:S(2)}) collective-permute-start(f32[64,128]{1,0:T(8,128)S(1)} %get-tuple-element.16), channel_id=1, source_target_pairs={{0,3},{1,2},{2,1},{3,0},{4,7},{5,6},{6,5},{7,4},{8,11},{9,10},{10,... | collective-permute-start | bytes 98312 | tf_op jit(solution)/shard_map/ppermute | solution.py:263
  39.4 5.2 %collective-permute-start.12 = (f32[64,128]{1,0:T(8,128)S(1)}, f32[64,128]{1,0:T(8,128)S(1)}, u32[]{:S(2)}, u32[]{:S(2)}) collective-permute-start(f32[64,128]{1,0:T(8,128)S(1)} %get-tuple-element.17), channel_id=1, source_target_pairs={{0,2},{1,3},{2,0},{3,1},{4,6},{5,7},{6,4},{7,5},{8,10},{9,11},{10,... | collective-permute-start | bytes 98312 | tf_op jit(solution)/shard_map/ppermute | solution.py:263
  40.6 4.0 %collective-permute-start.11 = (f32[64,128]{1,0:T(8,128)S(1)}, f32[64,128]{1,0:T(8,128)S(1)}, u32[]{:S(2)}, u32[]{:S(2)}) collective-permute-start(f32[64,128]{1,0:T(8,128)S(1)} %get-tuple-element.18), channel_id=1, source_target_pairs={{0,1},{1,0},{2,3},{3,2},{4,5},{5,4},{6,7},{7,6},{8,9},{9,8},{10,11... | collective-permute-start | bytes 98312 | tf_op jit(solution)/shard_map/ppermute | solution.py:263
  41.1 5.3 %collective-permute-start.8 = (f32[64,128]{1,0:T(8,128)S(1)}, f32[64,128]{1,0:T(8,128)S(1)}, u32[]{:S(2)}, u32[]{:S(2)}) collective-permute-start(f32[64,128]{1,0:T(8,128)S(1)} %get-tuple-element.15), channel_id=1, source_target_pairs={{0,1},{1,0},{2,3},{3,2},{4,5},{5,4},{6,7},{7,6},{8,9},{9,8},{10,11... | collective-permute-start | bytes 98312 | tf_op jit(solution)/shard_map/ppermute | solution.py:263
  42.6 4.8 %collective-permute-start.10 = (f32[64,128]{1,0:T(8,128)S(1)}, f32[64,128]{1,0:T(8,128)S(1)}, u32[]{:S(2)}, u32[]{:S(2)}) collective-permute-start(f32[64,128]{1,0:T(8,128)S(1)} %get-tuple-element.19), channel_id=1, source_target_pairs={{0,3},{1,2},{2,1},{3,0},{4,7},{5,6},{6,5},{7,4},{8,11},{9,10},{10,... | collective-permute-start | bytes 98312 | tf_op jit(solution)/shard_map/ppermute | solution.py:263
  43.5 4.3 %collective-permute-start.9 = (f32[64,128]{1,0:T(8,128)S(1)}, f32[64,128]{1,0:T(8,128)S(1)}, u32[]{:S(2)}, u32[]{:S(2)}) collective-permute-start(f32[64,128]{1,0:T(8,128)S(1)} %get-tuple-element.20), channel_id=1, source_target_pairs={{0,2},{1,3},{2,0},{3,1},{4,6},{5,7},{6,4},{7,5},{8,10},{9,11},{10,... | collective-permute-start | bytes 98312 | tf_op jit(solution)/shard_map/ppermute | solution.py:263
  44.6 4.9 %collective-permute-start.14 = (f32[64,128]{1,0:T(8,128)S(1)}, f32[64,128]{1,0:T(8,128)S(1)}, u32[]{:S(2)}, u32[]{:S(2)}) collective-permute-start(f32[64,128]{1,0:T(8,128)S(1)} %fusion.2), channel_id=1, source_target_pairs={{0,4},{4,0},{1,5},{5,1},{2,6},{6,2},{3,7},{7,3},{8,12},{12,8},{9,1... | collective-permute-start | bytes 98312 | tf_op jit(solution)/shard_map/ppermute | solution.py:236
  (7 other events, 5.4 us)

commit v26 on v18

--- a/solution.py
+++ b/solution.py
@@ -226,15 +226,15 @@
 
 
 def place_of_columns(half):
-    own = lax.axis_index("half") * half + lax.axis_index("near")
-    ahead = jnp.arange(2 * half, dtype=jnp.int32) ^ own
-    return ahead % half * 2 + ahead // half
+    column = jnp.arange(2 * half, dtype=jnp.int32)
+    return column % half * 2 + (column // half ^ lax.axis_index("half"))
 
 
 def add_over_columns(sums, half):
-    total = sums[:2]
+    parts = lax.all_to_all(sums.reshape((half, 2) + sums.shape[1:]), "near", split_axis=0, concat_axis=0, tiled=True)
+    total = parts[0]
     for near in range(1, half):
-        total = total + lax.ppermute(sums[2 * near : 2 * near + 2], "near", [(n, n ^ near) for n in range(half)])
+        total = total + parts[near]
     return total[0] + half_swap(total[1])
 
 

time: 42 us -> 43.2 us (1.029)
  blocking collectives: 0 us -> 8.38 us
  waiting for transfers between devices: 17 us -> 13.3 us
  starting transfers between devices: 18.8 us -> 15.2 us
    all_to_all x0 -> x1, blocking collectives: none -> 8.38 us  [add_over_columns(): lax.all_to_all(sums.reshape((half, 2) + sums.shape[1:]), 'near', split_ax...]
    ppermute x3 -> x0, waiting for transfers between devices: 3.65 us -> none  [add_over_columns(): lax.ppermute(sums[2 * near:2 * near + 2], 'near', [(n, n ^ near) for n in...]
    ppermute x3 -> x0, starting transfers between devices: 3.55 us -> none  [add_over_columns(): lax.ppermute(sums[2 * near:2 * near + 2], 'near', [(n, n ^ near) for n in...]
  transfers between devices with their start and end apart: 13 -> 10, of which waited for: 10 -> 7; matrix products, arithmetic and copies ran while one was open for 0% -> 0% of each run, Pallas kernels for 8% -> 8%
where the time goes in v26:
time: 43.2 us; the launch traced here: 43 us
  starting transfers between devices  15.2 us (35%)
  waiting for transfers between devices  13.3 us (31%)
  blocking collectives  8.38 us (19%)
  Pallas kernels  5.26 us (12%)
  other arithmetic  0.72 us (2%)
    all_to_all x1, blocking collectives, add_over_columns(): lax.all_to_all(sums.reshape((half, 2) + sums.shape[1:]), 'near', split_ax...  8.38 us
    ppermute x6, waiting for transfers between devices, row_swap(): lax.ppermute(x, 'row', [(r, r ^ bit) for r in range(lax.axis_size('row'))])  7.98 us
    ppermute x2, starting transfers between devices, far_swap(): return lax.ppermute(x, ('half', 'near'), pairs)  5.27 us
    ppermute x6, starting transfers between devices, row_swap(): lax.ppermute(x, 'row', [(r, r ^ bit) for r in range(lax.axis_size('row'))])  3.68 us
    all_to_all x1, starting transfers between devices, local(): lax.all_to_all(restricted, 'near', split_axis=0, concat_axis=0, tiled=True)  3.65 us
    pallas_call x1, Pallas kernels, restrict_operator(): pl.pallas_call(restrict_kernel, out_shape=(jax.ShapeDtypeStruct((columns...  3.48 us
    ppermute x1, starting transfers between devices, half_swap(): return lax.ppermute(x, 'half', [(0, 1), (1, 0)])  2.6 us
    ppermute x1, waiting for transfers between devices, half_swap(): return lax.ppermute(x, 'half', [(0, 1), (1, 0)])  2.28 us
  transfers between devices with their start and end apart: 10, of which 7 were waited for; matrix products, arithmetic and copies ran while one was open for 0% of the time, Pallas kernels for 8%

profile of v26, /device:TPU:0, one launch (start us, length us, event | category | flops | bytes accessed | tf_op | source)
XLA Modules:
  0.0 43.0 jit_solution(9081498508528383595)
XLA Ops:
  0.0 5.0 %collective-permute-start.4 = (f32[512,128]{1,0:T(8,128)}, f32[512,128]{1,0:T(8,128)S(1)}, u32[]{:S(2)}, u32[]{:S(2)}) collective-permute-start(f32[512,128]{1,0:T(8,128)} %bitcast.22), channel_id=1, source_target_pairs={{0,6},{1,7},{2,4},{3,5},{4,2},{5,3},{6,0},{7,1},{8,14},{9,15},{10,... | collective-permute-start | bytes 786440 | tf_op jit(solution)/shard_map/ppermute | solution.py:215
  5.0 3.5 %restrict_operator.1 = (f32[4,520,128]{2,1,0:T(8,128)}, s32[2,8]{1,0:T(2,128)}, f32[512,128]{1,0:T(8,128)}) custom-call(s32[8]{0:T(128)} %count_any.1, s32[8,8]{1,0:T(8,128)} %slot_any.1, s32[2,8]{1,0:T(2,128)} %bitcast.25, s32[4,8]{1,0:T(4,128)} %bitcast.24, f32[8,64,128]{2,1,0:T(8,128)} %restrict_any.1, f32[8,64,512]{2,1,0:T(8,128)} %operator_any.1, ...), custom_call_target="tpu_custom_call" | custom-call | flops 201326592 | bytes 4194304 | tf_op jit(solution)/shard_map/restrict_operator/pallas_call | solution.py:121
  8.5 1.6 %collective-permute-start.1 = (f32[512,128]{1,0:T(8,128)}, f32[512,128]{1,0:T(8,128)S(1)}, u32[]{:S(2)}, u32[]{:S(2)}) collective-permute-start(f32[512,128]{1,0:T(8,128)} %get-tuple-element.9.rest_0_), channel_id=1, source_target_pairs={{0,16},{8,24},{16,0},{24,8},{1,17},{9,25},{17,1},{25,9},{2,18},{10... | collective-permute-start | bytes 786440 | tf_op jit(solution)/shard_map/ppermute | solution.py:205
  10.1 0.2 collective-permute-start.3
  10.3 3.6 %all-to-all-start = ((f32[4,520,128]{2,1,0:T(8,128)}), f32[4,520,128]{2,1,0:T(8,128)S(1)}, u32[]{:S(2)}, u32[]{:S(2)}) async-start(f32[4,520,128]{2,1,0:T(8,128)} %get-tuple-element.8), calls=%async_computation | async-start | bytes 2129920 | tf_op jit(solution)/shard_map/all_to_all | solution.py:271
  14.0 1.7 %collective-permute-done.3.far_columns_ref = s32[2,8]{1,0:T(2,128)S(1)} collective-permute-done((s32[2,8]{1,0:T(2,128)}, s32[2,8]{1,0:T(2,128)S(1)}, u32[]{:S(2)}, u32[]{:S(2)}) %collective-permute-start.3) | collective-permute-done | bytes 96 | tf_op jit(solution)/shard_map/ppermute | solution.py:215
  15.7 0.0 collective-permute-done.4.blocks_ref
  15.7 0.9 %collective-permute-done.1.next_ref.rest_2_ = f32[512,128]{1,0:T(8,128)S(1)} collective-permute-done((f32[512,128]{1,0:T(8,128)}, f32[512,128]{1,0:T(8,128)S(1)}, u32[]{:S(2)}, u32[]{:S(2)}) %collective-permute-start.1) | collective-permute-done | bytes 262176 | tf_op jit(solution)/shard_map/ppermute | solution.py:205
  16.6 1.6 %collective-permute-start.6 = (f32[520,128]{1,0:T(8,128)S(1)}, f32[520,128]{1,0:T(8,128)S(1)}, u32[]{:S(2)}, u32[]{:S(2)}) collective-permute-start(f32[520,128]{1,0:T(8,128)S(1)} %append_columns.1.rest_4_), channel_id=1, source_target_pairs={{0,16},{8,24},{16,0},{24,8},{1,17},{9,25},{17,1},{25,9},{2,18},{10... | collective-permute-start | bytes 798728 | tf_op jit(solution)/shard_map/ppermute | solution.py:205
  18.2 0.0 collective-permute-start.5
  18.2 5.4 %collective-permute-done.6.rest_6_ = f32[520,128]{1,0:T(8,128)S(1)} collective-permute-done((f32[520,128]{1,0:T(8,128)S(1)}, f32[520,128]{1,0:T(8,128)S(1)}, u32[]{:S(2)}, u32[]{:S(2)}) %collective-permute-start.6) | collective-permute-done | bytes 266272 | tf_op jit(solution)/shard_map/ppermute | solution.py:205
  23.6 0.0 collective-permute-start.7
  23.6 0.5 %collective-permute-start = (f32[512,128]{1,0:T(8,128)S(1)}, f32[512,128]{1,0:T(8,128)S(1)}, u32[]{:S(2)}, u32[]{:S(2)}) collective-permute-start(f32[512,128]{1,0:T(8,128)S(1)} %copy-done), channel_id=1, source_target_pairs={{0,8},{8,0},{16,24},{24,16},{1,9},{9,1},{17,25},{25,17},{2,10},{10... | collective-permute-start | bytes 786440 | tf_op jit(solution)/shard_map/ppermute | solution.py:205
  24.1 0.0 collective-permute-start.2
  24.1 0.1 add_bitcast_fusion.own_ref
  24.2 1.3 %collective-permute-done.rest_1_ = f32[512,128]{1,0:T(8,128)S(1)} collective-permute-done((f32[512,128]{1,0:T(8,128)S(1)}, f32[512,128]{1,0:T(8,128)S(1)}, u32[]{:S(2)}, u32[]{:S(2)}) %collective-permute-start) | collective-permute-done | bytes 262176 | tf_op jit(solution)/shard_map/ppermute | solution.py:205
  25.5 0.4 collective-permute-done.2.rest_3_
  25.9 0.0 collective-permute-done.5.rest_5_
  25.9 1.4 %all-to-all-done.restricted_ref = f32[4,520,128]{2,1,0:T(8,128)S(1)} async-done(((f32[4,520,128]{2,1,0:T(8,128)}), f32[4,520,128]{2,1,0:T(8,128)S(1)}, u32[]{:S(2)}, u32[]{:S(2)}) %all-to-all-start) | async-done | bytes 1064992 | tf_op jit(solution)/shard_map/all_to_all | solution.py:271
  27.3 1.8 %combine.1 = f32[8,64,128]{2,1,0:T(8,128)S(1)} custom-call(s32[1,10]{1,0:T(1,128)S(1)} %add_bitcast_fusion.own_ref, f32[4,520,128]{2,1,0:T(8,128)S(1)} %all-to-all-done.restricted_ref, f32[512,128]{1,0:T(8,128)S(1)} %copy-done, f32[512,128]{1,0:T(8,128)S(1)} %collective-permute-done.rest_1_, f32[512,128]{1,0:T(8,128)S(1)} %collective-permute-done.1.next_ref.rest_2_, ...), custom_call_target="tpu_custom_call" | custom-call | flops 268435456 | bytes 4194304 | tf_op jit(solution)/shard_map/combine/pallas_call | solution.py:187
  29.0 8.4 %all_to_all.10 = f32[4,2,64,128]{3,2,1,0:T(8,128)S(1)} all-to-all(f32[4,2,64,128]{3,2,1,0:T(8,128)S(1)} %bitcast.21), channel_id=1, replica_groups=mesh['row'=4,'half'=2,'near'=4] {'near'}, dimensions={0} | all-to-all | bytes 524288 | tf_op jit(solution)/shard_map/all_to_all | solution.py:234
  37.5 2.6 %collective-permute-start.8 = (f32[64,128]{1,0:T(8,128)S(1)}, f32[64,128]{1,0:T(8,128)S(1)}, u32[]{:S(2)}, u32[]{:S(2)}) collective-permute-start(f32[64,128]{1,0:T(8,128)S(1)} %slice_bitcast_fusion), channel_id=1, source_target_pairs={{0,4},{4,0},{1,5},{5,1},{2,6},{6,2},{3,7},{7,3},{8,12},{12,8},{9,1... | collective-permute-start | bytes 98312 | tf_op jit(solution)/shard_map/ppermute | solution.py:209
  40.1 2.3 %collective-permute-done.8 = f32[64,128]{1,0:T(8,128)S(1)} collective-permute-done((f32[64,128]{1,0:T(8,128)S(1)}, f32[64,128]{1,0:T(8,128)S(1)}, u32[]{:S(2)}, u32[]{:S(2)}) %collective-permute-start.8) | collective-permute-done | bytes 32800 | tf_op jit(solution)/shard_map/ppermute | solution.py:209
  42.3 0.6 %fusion.1 = f32[128,64]{0,1:T(8,128)} fusion(f32[64,128]{1,0:T(8,128)S(1)} %collective-permute-done.8, f32[1,2,64,128]{3,2,1,0:T(8,128)S(1)} %slice_add_fusion), kind=kLoop, calls=%fused_computation.6 | loop fusion | flops 8192 | bytes 98304 | tf_op jit(solution)/shard_map/transpose | solution.py:277
  (9 shorter events, 0.1 us)
Async XLA Ops:
  0.0 15.7 %collective-permute-start.4 = (f32[512,128]{1,0:T(8,128)}, f32[512,128]{1,0:T(8,128)S(1)}, u32[]{:S(2)}, u32[]{:S(2)}) collective-permute-start(f32[512,128]{1,0:T(8,128)} %bitcast.22), channel_id=1, source_target_pairs={{0,6},{1,7},{2,4},{3,5},{4,2},{5,3},{6,0},{7,1},{8,14},{9,15},{10,... | collective-permute-start | bytes 786440 | tf_op jit(solution)/shard_map/ppermute | solution.py:215
  8.5 8.0 %collective-permute-start.1 = (f32[512,128]{1,0:T(8,128)}, f32[512,128]{1,0:T(8,128)S(1)}, u32[]{:S(2)}, u32[]{:S(2)}) collective-permute-start(f32[512,128]{1,0:T(8,128)} %get-tuple-element.9.rest_0_), channel_id=1, source_target_pairs={{0,16},{8,24},{16,0},{24,8},{1,17},{9,25},{17,1},{25,9},{2,18},{10... | collective-permute-start | bytes 786440 | tf_op jit(solution)/shard_map/ppermute | solution.py:205
  10.1 5.6 %collective-permute-start.3 = (s32[2,8]{1,0:T(2,128)}, s32[2,8]{1,0:T(2,128)S(1)}, u32[]{:S(2)}, u32[]{:S(2)}) collective-permute-start(s32[2,8]{1,0:T(2,128)} %get-tuple-element.10.own_columns_ref), channel_id=1, source_target_pairs={{0,6},{1,7},{2,4},{3,5},{4,2},{5,3},{6,0},{7,1},{8,14},{9,15},{10,... | collective-permute-start | bytes 200 | tf_op jit(solution)/shard_map/ppermute | solution.py:215
  10.3 6.2 %copy-start.1 = (s32[2,8]{1,0:T(2,128)S(1)}, s32[2,8]{1,0:T(2,128)}, u32[]{:S(2)}) copy-start(s32[2,8]{1,0:T(2,128)} %get-tuple-element.10.own_columns_ref) | copy-start | bytes 196
  10.3 16.9 %all-to-all-start = ((f32[4,520,128]{2,1,0:T(8,128)}), f32[4,520,128]{2,1,0:T(8,128)S(1)}, u32[]{:S(2)}, u32[]{:S(2)}) async-start(f32[4,520,128]{2,1,0:T(8,128)} %get-tuple-element.8), calls=%async_computation | async-start | bytes 2129920 | tf_op jit(solution)/shard_map/all_to_all | solution.py:271
  14.0 9.6 %copy-start = (f32[512,128]{1,0:T(8,128)S(1)}, f32[512,128]{1,0:T(8,128)}, u32[]{:S(2)}) copy-start(f32[512,128]{1,0:T(8,128)} %get-tuple-element.9.rest_0_) | copy-start | bytes 786436
  16.6 7.0 %collective-permute-start.6 = (f32[520,128]{1,0:T(8,128)S(1)}, f32[520,128]{1,0:T(8,128)S(1)}, u32[]{:S(2)}, u32[]{:S(2)}) collective-permute-start(f32[520,128]{1,0:T(8,128)S(1)} %append_columns.1.rest_4_), channel_id=1, source_target_pairs={{0,16},{8,24},{16,0},{24,8},{1,17},{9,25},{17,1},{25,9},{2,18},{10... | collective-permute-start | bytes 798728 | tf_op jit(solution)/shard_map/ppermute | solution.py:205
  18.2 7.7 %collective-permute-start.5 = (f32[520,128]{1,0:T(8,128)S(1)}, f32[520,128]{1,0:T(8,128)S(1)}, u32[]{:S(2)}, u32[]{:S(2)}) collective-permute-start(f32[520,128]{1,0:T(8,128)S(1)} %append_columns.1.rest_4_), channel_id=1, source_target_pairs={{0,8},{8,0},{16,24},{24,16},{1,9},{9,1},{17,25},{25,17},{2,10},{10... | collective-permute-start | bytes 798728 | tf_op jit(solution)/shard_map/ppermute | solution.py:205
  23.6 2.3 %collective-permute-start.7 = (f32[520,128]{1,0:T(8,128)S(1)}, f32[520,128]{1,0:T(8,128)S(1)}, u32[]{:S(2)}, u32[]{:S(2)}) collective-permute-start(f32[520,128]{1,0:T(8,128)S(1)} %collective-permute-done.6.rest_6_), channel_id=1, source_target_pairs={{0,8},{8,0},{16,24},{24,16},{1,9},{9,1},{17,25},{25,17},{2,10},{10... | collective-permute-start | bytes 798728 | tf_op jit(solution)/shard_map/ppermute | solution.py:205
  23.6 1.9 %collective-permute-start = (f32[512,128]{1,0:T(8,128)S(1)}, f32[512,128]{1,0:T(8,128)S(1)}, u32[]{:S(2)}, u32[]{:S(2)}) collective-permute-start(f32[512,128]{1,0:T(8,128)S(1)} %copy-done), channel_id=1, source_target_pairs={{0,8},{8,0},{16,24},{24,16},{1,9},{9,1},{17,25},{25,17},{2,10},{10... | collective-permute-start | bytes 786440 | tf_op jit(solution)/shard_map/ppermute | solution.py:205
  24.1 1.8 %collective-permute-start.2 = (f32[512,128]{1,0:T(8,128)S(1)}, f32[512,128]{1,0:T(8,128)S(1)}, u32[]{:S(2)}, u32[]{:S(2)}) collective-permute-start(f32[512,128]{1,0:T(8,128)S(1)} %collective-permute-done.1.next_ref.rest_2_), channel_id=1, source_target_pairs={{0,8},{8,0},{16,24},{24,16},{1,9},{9,1},{17,25},{25,17},{2,10},{10... | collective-permute-start | bytes 786440 | tf_op jit(solution)/shard_map/ppermute | solution.py:205
  37.5 4.9 %collective-permute-start.8 = (f32[64,128]{1,0:T(8,128)S(1)}, f32[64,128]{1,0:T(8,128)S(1)}, u32[]{:S(2)}, u32[]{:S(2)}) collective-permute-start(f32[64,128]{1,0:T(8,128)S(1)} %slice_bitcast_fusion), channel_id=1, source_target_pairs={{0,4},{4,0},{1,5},{5,1},{2,6},{6,2},{3,7},{7,3},{8,12},{12,8},{9,1... | collective-permute-start | bytes 98312 | tf_op jit(solution)/shard_map/ppermute | solution.py:209

commit v27 on v16

v27 whole, which is shorter than its diff:
```python
import functools

import jax
import jax.numpy as jnp
from jax import lax
from jax.experimental import pallas as pl
from jax.experimental.pallas import tpu as pltpu
from jax.sharding import Mesh
from jax.sharding import PartitionSpec as P

NCR = 2
LANES = 128
EXTRA = 8
HOLD_FLOPS = 16 << 30
VMEM_LIMIT = 48 * 1024 * 1024


def halves(x):
    high = x.astype(jnp.bfloat16)
    return high, (x - high.astype(jnp.float32)).astype(jnp.bfloat16)


def transposed_product(left, right):
    tall = jnp.concatenate(halves(left), axis=0)
    wide = jnp.concatenate(halves(right), axis=1)
    wide = jnp.concatenate([wide, wide], axis=0)
    both = lax.dot_general(tall, wide, (((0,), (0,)), ((), ())), preferred_element_type=jnp.float32)
    width = right.shape[1]
    return both[:, :width] + both[:, width:]


def hold_kernel(mark_ref, next_ref, blocks_ref, out_ref):
    out_ref[...] = blocks_ref[...]


def hold_until(mark, next_blocks, blocks):
    return pl.pallas_call(
        hold_kernel,
        out_shape=jax.ShapeDtypeStruct(blocks.shape, blocks.dtype),
        in_specs=[pl.BlockSpec(memory_space=pltpu.VMEM)] * 3,
        out_specs=pl.BlockSpec(memory_space=pltpu.VMEM),
        compiler_params=pltpu.CompilerParams(vmem_limit_bytes=VMEM_LIMIT),
        cost_estimate=pl.CostEstimate(flops=HOLD_FLOPS, bytes_accessed=HOLD_FLOPS >> 8, transcendentals=0),
        name="hold_until",
    )(mark, next_blocks, blocks)


def restrict_kernel(
    count_any, slot_any, rows_any, fetch_any, restrict_any, operator_any, side_any, near_any,
    mark_ref, *refs,
):
    outs = refs[:-11]
    count_ref, slot_ref, rows_ref, fetch_ref, side_ref, near_ref, restrict_ref, operator_ref = refs[-11:-3]
    sems, operator_sems, out_sems = refs[-3:]
    out_ref = outs[-1]
    outs = outs[:-1]
    fine_rows, block_size, _ = operator_ref.shape
    entries = slot_ref.shape[1]
    slot_count, columns = fetch_ref.shape
    half = columns // 2
    used = 2 * slot_count * block_size
    wide = NCR * block_size

    pairs = [
        (count_any, count_ref), (slot_any, slot_ref), (rows_any, rows_ref),
        (fetch_any, fetch_ref), (restrict_any, restrict_ref),
        (side_any, side_ref), (near_any, near_ref),
    ]
    copies = [pltpu.make_async_copy(a, b, sems.at[i]) for i, (a, b) in enumerate(pairs)]
    operators = [
        pltpu.make_async_copy(operator_any.at[i], operator_ref.at[i], operator_sems.at[i]) for i in range(fine_rows)
    ]
    for copy in copies + operators:
        copy.start()

    lane = lax.broadcasted_iota(jnp.int32, (block_size, wide), 1)
    second = (lane >= block_size).astype(jnp.int32)
    short_lane = lax.broadcasted_iota(jnp.int32, (EXTRA, wide), 1)
    for near in range(half):
        out_ref[near, :used] = jnp.zeros((used, wide), jnp.float32)
    for copy in copies + operators:
        copy.wait()

    for near in range(half):
        value = jnp.zeros((EXTRA, wide), jnp.int32)
        for side in range(2):
            for s in range(slot_count):
                turned = near ^ jnp.where(side_ref[0] == side, 0, half // 2)
                wanted = fetch_ref[s, side * half + turned]
                value = jnp.where(short_lane == side * slot_count + s, wanted, value)
        out_ref[near ^ near_ref[0], used:] = value.astype(jnp.float32)
        mark_ref[...] = value.astype(jnp.float32)

    for i in range(fine_rows):
        value = restrict_ref[i]
        swapped = pltpu.roll(value, block_size, 1)
        own_row = jnp.where(second == 0, rows_ref[0, i], rows_ref[1, i])
        other_row = jnp.where(second == 0, rows_ref[1, i], rows_ref[0, i])
        dense = jnp.where(own_row == second, value, 0.0) + jnp.where(other_row == second, swapped, 0.0)
        product = transposed_product(operator_ref[i], dense)
        for k in range(entries):
            part = jnp.where(k < count_ref[i], product[k * block_size : (k + 1) * block_size], 0.0)
            peer = lax.div(slot_ref[i, k], slot_count)
            side = lax.div(peer, half)
            place = side * slot_count + lax.rem(slot_ref[i, k], slot_count)
            near = lax.rem(peer, half) ^ jnp.where(side_ref[0] == side, 0, half // 2) ^ near_ref[0]
            start = pl.multiple_of(place * block_size, block_size)
            out_ref[near, pl.ds(start, block_size)] += part

    writes = [pltpu.make_async_copy(out_ref.at[ahead], out, out_sems.at[ahead]) for ahead, out in enumerate(outs)]
    for copy in writes:
        copy.start()
    for copy in writes:
        copy.wait()


def restrict_operator(
    operator_count, operator_slot, restrict_rows, fetch, operator_blocks, restrict_blocks, side, near
):
    fine_rows, block_size, width = operator_blocks.shape
    slot_count, columns = fetch.shape
    half = columns // 2
    wide = NCR * block_size
    rows = 2 * slot_count * block_size + EXTRA
    small = (operator_count, operator_slot, restrict_rows, fetch)
    kept = small + (side, near)
    hbm = pl.BlockSpec(memory_space=pltpu.HBM)
    results = pl.pallas_call(
        restrict_kernel,
        out_shape=(jax.ShapeDtypeStruct((EXTRA, wide), jnp.float32),)
        + (jax.ShapeDtypeStruct((rows, wide), jnp.float32),) * half,
        in_specs=[hbm] * 8,
        out_specs=[pl.BlockSpec(memory_space=pltpu.VMEM)] + [hbm] * half,
        scratch_shapes=[pltpu.VMEM((half, rows, wide), jnp.float32)]
        + [pltpu.SMEM(x.shape, x.dtype) for x in kept]
        + [pltpu.VMEM(x.shape, x.dtype) for x in (restrict_blocks, operator_blocks)]
        + [pltpu.SemaphoreType.DMA((7,)), pltpu.SemaphoreType.DMA((fine_rows,)), pltpu.SemaphoreType.DMA((half,))],
        cost_estimate=pl.CostEstimate(
            flops=6 * fine_rows * block_size * width * wide, bytes_accessed=4 << 20, transcendentals=0
        ),
        name="restrict_operator",
    )(*small, restrict_blocks, operator_blocks, side, near)
    return results[0], results[1:]


def index_kernel(*refs):
    out_ref = refs[-1]
    out_ref[...] = jnp.zeros_like(out_ref)
    for i, part in enumerate(refs[:-1]):
        out_ref[i : i + 1] = part[part.shape[0] - EXTRA : part.shape[0] - EXTRA + 1].astype(jnp.int32)


def index_table(parts):
    rows = -(-len(parts) // 8) * 8
    return pl.pallas_call(
        index_kernel,
        out_shape=jax.ShapeDtypeStruct((rows, LANES), jnp.int32),
        in_specs=[pl.BlockSpec(memory_space=pltpu.VMEM)] * len(parts),
        out_specs=pl.BlockSpec(memory_space=pltpu.VMEM),
        compiler_params=pltpu.CompilerParams(vmem_limit_bytes=VMEM_LIMIT),
        cost_estimate=pl.CostEstimate(flops=HOLD_FLOPS, bytes_accessed=HOLD_FLOPS >> 8, transcendentals=0),
        name="index_table",
    )(*parts)


def combine_kernel(own_ref, wanted_ref, *rest, half, split, slot_count, fine_rows, entries):
    parts, chunks = rest[:half], list(rest[half:-5])
    out_ref, held_ref, table_ref, index_ref, sem = rest[-5:]
    rows = len(split) // 2
    block_size = out_ref.shape[1]
    columns = 2 * half
    held = fine_rows * block_size
    pieces = [[chunks.pop(0) for _ in range(count)] for count in split]

    table_ref[:1, : own_ref.shape[1]] = own_ref[...]
    table_ref[1 : 1 + half] = wanted_ref[:half]
    for i, piece in enumerate(pieces):
        first = 1 + half + entries * i
        row = piece[-1].shape[0] - EXTRA
        table_ref[first : first + entries] = piece[-1][row : row + entries].astype(jnp.int32)
    copy = pltpu.make_async_copy(table_ref, index_ref, sem)
    copy.start()
    for i, piece in enumerate(pieces):
        start = 0
        for chunk in piece:
            size = min(chunk.shape[0], held - start)
            held_ref[i, start : start + size] = chunk[:size]
            start += size
    out_ref[...] = jnp.zeros_like(out_ref)
    copy.wait()

    for ahead, part in enumerate(parts):

        def step(place, carry, ahead=ahead, part=part):
            wanted = index_ref[1 + ahead, place]
            inside = lax.rem(wanted, fine_rows)
            far = lax.div(place, slot_count) ^ index_ref[0, 1]
            piece = far * rows + (lax.div(wanted, fine_rows * columns) ^ index_ref[0, 0])
            block = held_ref[piece, pl.ds(pl.multiple_of(inside * block_size, block_size), block_size)]
            restricted = part[pl.ds(pl.multiple_of(place * block_size, block_size), block_size)]
            product = transposed_product(block, restricted)
            for m in range(entries):
                column = index_ref[0, 2 + index_ref[1 + half + entries * piece + m, inside]]
                out_ref[column] += product[m * block_size : (m + 1) * block_size]
            return carry

        lax.fori_loop(0, 2 * slot_count, step, 0, unroll=half <= 4)


def combine(own, wanted, parts, pieces, coarse_all, slot_count, fine_rows, block_size):
    half = len(parts)
    wide = parts[0].shape[1]
    width = pieces[0][0].shape[1]
    entries = width // block_size
    split = tuple(len(piece) for piece in pieces)
    chunks = [chunk for piece in pieces for chunk in piece]
    table_rows = -(-(1 + half + entries * len(pieces)) // 8) * 8
    return pl.pallas_call(
        functools.partial(
            combine_kernel, half=half, split=split, slot_count=slot_count, fine_rows=fine_rows, entries=entries
        ),
        out_shape=jax.ShapeDtypeStruct((coarse_all, block_size, wide), jnp.float32),
        in_specs=[pl.BlockSpec(memory_space=pltpu.VMEM)] * (2 + half + len(chunks)),
        out_specs=pl.BlockSpec(memory_space=pltpu.VMEM),
        scratch_shapes=[
            pltpu.VMEM((len(pieces), fine_rows * block_size, width), jnp.float32),
            pltpu.VMEM((table_rows, LANES), jnp.int32),
            pltpu.SMEM((table_rows, LANES), jnp.int32),
            pltpu.SemaphoreType.DMA,
        ],
        compiler_params=pltpu.CompilerParams(vmem_limit_bytes=VMEM_LIMIT),
        cost_estimate=pl.CostEstimate(flops=1 << 28, bytes_accessed=4 << 20, transcendentals=0),
        name="combine",
    )(own, wanted, *parts, *chunks)


def row_swap(x, bit):
    return lax.ppermute(x, "row", [(r, r ^ bit) for r in range(lax.axis_size("row"))])


def half_swap(x):
    return lax.ppermute(x, "half", [(0, 1), (1, 0)])


def far_swap(x):
    half = lax.axis_size("near")
    pairs = [(h * half + n, (1 - h) * half + (n ^ half // 2)) for h in range(2) for n in range(half)]
    return lax.ppermute(x, ("half", "near"), pairs)


def spread_over_rows(blocks, rows, cut):
    pieces = {0: [blocks]}
    bit = rows // 2
    while bit:
        for mask in list(pieces):
            chunks = pieces[mask]
            if cut and bit == rows // 2:
                chunks = [blocks[:cut], blocks[cut:]]
            pieces[mask ^ bit] = [row_swap(chunk, bit) for chunk in chunks]
        bit //= 2
    return [pieces[mask] for mask in range(rows)]


def place_of_columns(half):
    own = lax.axis_index("half") * half + lax.axis_index("near")
    return jnp.arange(2 * half, dtype=jnp.int32) ^ own


def add_over_near(sums, half):
    total = sums[0]
    for near in range(1, half):
        total = total + lax.ppermute(sums[near], "near", [(n, n ^ near) for n in range(half)])
    return total


def add_over_columns(sums, half):
    crossing = half_swap(add_over_near(sums[half:], half))
    return add_over_near(sums[:half], half) + crossing


def with_columns(columns, blocks):
    entries, fine_rows = columns.shape
    used, width = blocks.shape
    rows = jnp.pad(columns.astype(blocks.dtype), ((0, EXTRA - entries), (0, width - fine_rows)))
    return jnp.concatenate([blocks, rows], axis=0)


def local(
    operator_blocks,
    operator_count,
    operator_slot,
    fetch_lists,
    prolong_blocks,
    prolong_cols,
    restrict_blocks,
    restrict_rows,
):
    rows, half = lax.axis_size("row"), lax.axis_size("near")
    slot_count = fetch_lists.shape[3]
    fine_rows, block_size, width = prolong_blocks.shape
    fetch = fetch_lists.reshape(2 * half, slot_count).T
    own = jnp.stack([lax.axis_index("row"), lax.axis_index("half")])
    own = jnp.concatenate([own, place_of_columns(half)])[None]

    near_blocks = with_columns(prolong_cols.T, prolong_blocks.reshape(fine_rows * block_size, width))
    far_blocks = far_swap(near_blocks)
    mark, parts = restrict_operator(
        operator_count,
        operator_slot,
        restrict_rows.T,
        fetch,
        operator_blocks,
        restrict_blocks,
        lax.axis_index("half").reshape(1),
        lax.axis_index("near").reshape(1),
    )
    parts = [parts[0]] + [
        lax.ppermute(parts[ahead], "near", [(n, n ^ ahead) for n in range(half)]) for ahead in range(1, half)
    ]
    wanted = index_table(parts)
    near_pieces = spread_over_rows(near_blocks, rows, 0)
    far_blocks = hold_until(mark, near_pieces[rows // 2][0], far_blocks)
    pieces = near_pieces + spread_over_rows(far_blocks, rows, fine_rows * block_size // 2)
    sums = combine(own, wanted, parts, pieces, NCR * rows, slot_count, fine_rows, block_size)
    return add_over_columns(sums, half).T


def solution(mesh):
    rows, columns = mesh.shape["row"], mesh.shape["col"]
    split = Mesh(mesh.devices.reshape(rows, 2, columns // 2), ("row", "half", "near"))
    flat = ("row", "half", "near")
    return jax.shard_map(
        local,
        mesh=split,
        in_specs=(
            P(flat, None, None),
            P(flat),
            P(flat, None),
            P("row", ("half", "near"), None, None),
            P(flat, None, None),
            P(flat, None),
            P(flat, None, None),
            P(flat, None),
        ),
        out_specs=P("row", ("half", "near")),
        check_vma=False,
    )
```

time: 50.1 us -> 43.3 us (0.86)
  waiting for transfers between devices: 20.9 us -> 14.5 us
  Pallas kernels: 6.92 us -> 5.52 us
  other arithmetic: 1.27 us -> 2.37 us
    ppermute x3 -> x7, starting transfers between devices: 3.55 us -> 12.2 us  [the longest x6 7.04 us: add_over_near(): lax.ppermute(sums[near], 'near', [(n, n ^ near) for n in range(half)])]
    ppermute x3 -> x1, waiting for transfers between devices: 10.6 us -> 2.16 us  [half_swap(): return lax.ppermute(x, 'half', [(0, 1), (1, 0)])]
    ppermute x3 -> x1, starting transfers between devices: 6.37 us -> 0.74 us  [half_swap(): return lax.ppermute(x, 'half', [(0, 1), (1, 0)])]
    ppermute x3, waiting for transfers between devices: 4.01 us -> 8.92 us  [local(): lax.ppermute(parts[ahead], 'near', [(n, n ^ ahead) for n in range(half)])]
    ppermute x8, starting transfers between devices: 6.2 us -> 4.2 us  [row_swap(): lax.ppermute(x, 'row', [(r, r ^ bit) for r in range(lax.axis_size('row'))])]
    ppermute x3 -> x7, waiting for transfers between devices: 3.86 us -> 2.06 us  [the longest x6 2.06 us: add_over_near(): lax.ppermute(sums[near], 'near', [(n, n ^ near) for n in range(half)])]
    ppermute x8, waiting for transfers between devices: 2.39 us -> 1.32 us  [row_swap(): lax.ppermute(x, 'row', [(r, r ^ bit) for r in range(lax.axis_size('row'))])]
    ppermute x3, starting transfers between devices: 4.58 us -> 3.55 us  [local(): lax.ppermute(parts[ahead], 'near', [(n, n ^ ahead) for n in range(half)])]
  transfers between devices with their start and end apart: 17 -> 19, of which waited for: 9 -> 7; matrix products, arithmetic and copies ran while one was open for 0% -> 0% of each run, Pallas kernels for 0% -> 9%
where the time goes in v27:
time: 43.3 us; the launch traced here: 43.1 us
  starting transfers between devices  20.6 us (48%)
  waiting for transfers between devices  14.5 us (33%)
  Pallas kernels  5.52 us (13%)
  other arithmetic  2.37 us (5%)
    ppermute x3, waiting for transfers between devices, local(): lax.ppermute(parts[ahead], 'near', [(n, n ^ ahead) for n in range(half)])  8.92 us
    ppermute x6, starting transfers between devices, add_over_near(): lax.ppermute(sums[near], 'near', [(n, n ^ near) for n in range(half)])  7.04 us
    ppermute x1, starting transfers between devices, far_swap(): return lax.ppermute(x, ('half', 'near'), pairs)  5.11 us
    ppermute x8, starting transfers between devices, row_swap(): lax.ppermute(x, 'row', [(r, r ^ bit) for r in range(lax.axis_size('row'))])  4.2 us
    pallas_call x1, Pallas kernels, restrict_operator(): pl.pallas_call(restrict_kernel, out_shape=(jax.ShapeDtypeStruct((EXTRA, w...  3.97 us
    ppermute x3, starting transfers between devices, local(): lax.ppermute(parts[ahead], 'near', [(n, n ^ ahead) for n in range(half)])  3.55 us
    ppermute x1, waiting for transfers between devices, half_swap(): return lax.ppermute(x, 'half', [(0, 1), (1, 0)])  2.16 us
    ppermute x6, waiting for transfers between devices, add_over_near(): lax.ppermute(sums[near], 'near', [(n, n ^ near) for n in range(half)])  2.06 us
  transfers between devices with their start and end apart: 19, of which 7 were waited for; matrix products, arithmetic and copies ran while one was open for 0% of the time, Pallas kernels for 9%

profile of v27, /device:TPU:0, one launch (start us, length us, event | category | flops | bytes accessed | tf_op | source)
XLA Modules:
  0.0 43.1 jit_solution(16839703376207608242)
XLA Ops:
  0.0 0.7 %convert_bitcast_fusion = f32[2,8]{1,0:T(2,128)S(1)} fusion(s32[8,2]{0,1:T(2,128)} %param.13), kind=kLoop, calls=%fused_computation.18 | loop fusion | flops 16 | bytes 128 | tf_op jit(solution)/shard_map/convert_element_type | solution.py:284
  0.7 1.0 %select_maximum_fusion.rest_4_ = f32[520,128]{1,0:T(8,128)S(1)} fusion(f32[2,8]{1,0:T(2,128)S(1)} %convert_bitcast_fusion, f32[512,128]{1,0:T(8,128)} %bitcast.46), kind=kLoop, calls=%fused_computation | loop fusion | flops 199680 | bytes 528448 | tf_op jit(solution)/shard_map/concatenate | solution.py:285
  1.7 5.1 %collective-permute-start.6 = (f32[520,128]{1,0:T(8,128)S(1)}, f32[520,128]{1,0:T(8,128)S(1)}, u32[]{:S(2)}, u32[]{:S(2)}) collective-permute-start(f32[520,128]{1,0:T(8,128)S(1)} %select_maximum_fusion.rest_4_), channel_id=1, source_target_pairs={{0,6},{1,7},{2,4},{3,5},{4,2},{5,3},{6,0},{7,1},{8,14},{9,15},{10,... | collective-permute-start | bytes 798728 | tf_op jit(solution)/shard_map/ppermute | solution.py:248
  6.8 1.5 %collective-permute-start.4 = (f32[520,128]{1,0:T(8,128)S(1)}, f32[520,128]{1,0:T(8,128)S(1)}, u32[]{:S(2)}, u32[]{:S(2)}) collective-permute-start(f32[520,128]{1,0:T(8,128)S(1)} %select_maximum_fusion.rest_4_), channel_id=1, source_target_pairs={{0,16},{8,24},{16,0},{24,8},{1,17},{9,25},{17,1},{25,9},{2,18},{10... | collective-permute-start | bytes 798728 | tf_op jit(solution)/shard_map/ppermute | solution.py:238
  8.3 4.0 %restrict_operator.1 = (f32[8,128]{1,0:T(8,128)}, f32[520,128]{1,0:T(8,128)}, f32[520,128]{1,0:T(8,128)}, f32[520,128]{1,0:T(8,128)}, f32[520,128]{1,0:T(8,128)}) custom-call(s32[8]{0:T(128)} %count_any.1, s32[8,8]{1,0:T(8,128)} %slot_any.1, s32[2,8]{1,0:T(2,128)} %bitcast.48, s32[4,8]{1,0:T(4,128)} %bitcast.47, f32[8,64,128]{2,1,0:T(8,128)} %restrict_any.1, ...), custom_call_target="tpu_custom_call" | custom-call | flops 201326592 | bytes 4194304 | tf_op jit(solution)/shard_map/restrict_operator/pallas_call | solution.py:128
  12.3 1.6 %collective-permute-start = (f32[520,128]{1,0:T(8,128)}, f32[520,128]{1,0:T(8,128)S(1)}, u32[]{:S(2)}, u32[]{:S(2)}) collective-permute-start(f32[520,128]{1,0:T(8,128)} %get-tuple-element.11), channel_id=1, source_target_pairs={{0,1},{1,0},{2,3},{3,2},{4,5},{5,4},{6,7},{7,6},{8,9},{9,8},{10,11... | collective-permute-start | bytes 798728 | tf_op jit(solution)/shard_map/ppermute | solution.py:318
  13.8 2.0 %collective-permute-start.2 = (f32[520,128]{1,0:T(8,128)}, f32[520,128]{1,0:T(8,128)S(1)}, u32[]{:S(2)}, u32[]{:S(2)}) collective-permute-start(f32[520,128]{1,0:T(8,128)} %get-tuple-element.13), channel_id=1, source_target_pairs={{0,3},{1,2},{2,1},{3,0},{4,7},{5,6},{6,5},{7,4},{8,11},{9,10},{10,... | collective-permute-start | bytes 798728 | tf_op jit(solution)/shard_map/ppermute | solution.py:318
  15.9 0.6 %collective-permute-start.8 = (f32[256,128]{1,0:T(8,128)S(1)}, f32[256,128]{1,0:T(8,128)S(1)}, u32[]{:S(2)}, u32[]{:S(2)}) collective-permute-start(f32[256,128]{1,0:T(8,128)S(1)} %slice.50), channel_id=1, source_target_pairs={{0,16},{8,24},{16,0},{24,8},{1,17},{9,25},{17,1},{25,9},{2,18},{10... | collective-permute-start | bytes 393224 | tf_op jit(solution)/shard_map/ppermute | solution.py:238
  16.5 1.5 %collective-permute-start.9 = (f32[264,128]{1,0:T(8,128)S(1)}, f32[264,128]{1,0:T(8,128)S(1)}, u32[]{:S(2)}, u32[]{:S(2)}) collective-permute-start(f32[264,128]{1,0:T(8,128)S(1)} %slice.51), channel_id=1, source_target_pairs={{0,16},{8,24},{16,0},{24,8},{1,17},{9,25},{17,1},{25,9},{2,18},{10... | collective-permute-start | bytes 405512 | tf_op jit(solution)/shard_map/ppermute | solution.py:238
  18.1 2.9 %collective-permute-done.refs_1_.rest_1_ = f32[520,128]{1,0:T(8,128)S(1)} collective-permute-done((f32[520,128]{1,0:T(8,128)}, f32[520,128]{1,0:T(8,128)S(1)}, u32[]{:S(2)}, u32[]{:S(2)}) %collective-permute-start) | collective-permute-done | bytes 266272 | tf_op jit(solution)/shard_map/ppermute | solution.py:318
  21.0 2.4 %collective-permute-done.1.refs_2_.rest_2_ = f32[520,128]{1,0:T(8,128)S(1)} collective-permute-done((f32[520,128]{1,0:T(8,128)}, f32[520,128]{1,0:T(8,128)S(1)}, u32[]{:S(2)}, u32[]{:S(2)}) %collective-permute-start.1) | collective-permute-done | bytes 266272 | tf_op jit(solution)/shard_map/ppermute | solution.py:318
  23.4 3.6 %collective-permute-done.2.refs_3_.rest_3_ = f32[520,128]{1,0:T(8,128)S(1)} collective-permute-done((f32[520,128]{1,0:T(8,128)}, f32[520,128]{1,0:T(8,128)S(1)}, u32[]{:S(2)}, u32[]{:S(2)}) %collective-permute-start.2) | collective-permute-done | bytes 266272 | tf_op jit(solution)/shard_map/ppermute | solution.py:318
  27.0 0.5 %collective-permute-start.10 = (f32[256,128]{1,0:T(8,128)S(1)}, f32[256,128]{1,0:T(8,128)S(1)}, u32[]{:S(2)}, u32[]{:S(2)}) collective-permute-start(f32[256,128]{1,0:T(8,128)S(1)} %collective-permute-done.8.rest_10_), channel_id=1, source_target_pairs={{0,8},{8,0},{16,24},{24,16},{1,9},{9,1},{17,25},{25,17},{2,10},{10... | collective-permute-start | bytes 393224 | tf_op jit(solution)/shard_map/ppermute | solution.py:238
  27.6 1.1 %collective-permute-done.10.rest_12_ = f32[256,128]{1,0:T(8,128)S(1)} collective-permute-done((f32[256,128]{1,0:T(8,128)S(1)}, f32[256,128]{1,0:T(8,128)S(1)}, u32[]{:S(2)}, u32[]{:S(2)}) %collective-permute-start.10) | collective-permute-done | bytes 131104 | tf_op jit(solution)/shard_map/ppermute | solution.py:238
  28.9 1.5 %combine.1 = f32[8,64,128]{2,1,0:T(8,128)S(1)} custom-call(s32[1,10]{1,0:T(1,128)S(1)} %add_bitcast_fusion.own_ref, s32[8,128]{1,0:T(8,128)S(1)} %index_table.1.wanted_ref, f32[520,128]{1,0:T(8,128)S(1)} %copy-done, f32[520,128]{1,0:T(8,128)S(1)} %collective-permute-done.refs_1_.rest_1_, f32[520,128]{1,0:T(8,128)S(1)} %collective-permute-done.1.refs_2_.rest_2_, ...), custom_call_target="tpu_custom_call" | custom-call | flops 268435456 | bytes 4194304 | tf_op jit(solution)/shard_map/combine/pallas_call | solution.py:218
  30.5 1.3 %collective-permute-start.17 = (f32[64,128]{1,0:T(8,128)S(1)}, f32[64,128]{1,0:T(8,128)S(1)}, u32[]{:S(2)}, u32[]{:S(2)}) collective-permute-start(f32[64,128]{1,0:T(8,128)S(1)} %get-tuple-element.16), channel_id=1, source_target_pairs={{0,3},{1,2},{2,1},{3,0},{4,7},{5,6},{6,5},{7,4},{8,11},{9,10},{10,... | collective-permute-start | bytes 98312 | tf_op jit(solution)/shard_map/ppermute | solution.py:272
  31.8 1.7 %collective-permute-start.16 = (f32[64,128]{1,0:T(8,128)S(1)}, f32[64,128]{1,0:T(8,128)S(1)}, u32[]{:S(2)}, u32[]{:S(2)}) collective-permute-start(f32[64,128]{1,0:T(8,128)S(1)} %get-tuple-element.17), channel_id=1, source_target_pairs={{0,2},{1,3},{2,0},{3,1},{4,6},{5,7},{6,4},{7,5},{8,10},{9,11},{10,... | collective-permute-start | bytes 98312 | tf_op jit(solution)/shard_map/ppermute | solution.py:272
  33.5 0.5 %collective-permute-start.15 = (f32[64,128]{1,0:T(8,128)S(1)}, f32[64,128]{1,0:T(8,128)S(1)}, u32[]{:S(2)}, u32[]{:S(2)}) collective-permute-start(f32[64,128]{1,0:T(8,128)S(1)} %get-tuple-element.18), channel_id=1, source_target_pairs={{0,1},{1,0},{2,3},{3,2},{4,5},{5,4},{6,7},{7,6},{8,9},{9,8},{10,11... | collective-permute-start | bytes 98312 | tf_op jit(solution)/shard_map/ppermute | solution.py:272
  34.0 1.5 %collective-permute-start.12 = (f32[64,128]{1,0:T(8,128)S(1)}, f32[64,128]{1,0:T(8,128)S(1)}, u32[]{:S(2)}, u32[]{:S(2)}) collective-permute-start(f32[64,128]{1,0:T(8,128)S(1)} %get-tuple-element.15), channel_id=1, source_target_pairs={{0,1},{1,0},{2,3},{3,2},{4,5},{5,4},{6,7},{7,6},{8,9},{9,8},{10,11... | collective-permute-start | bytes 98312 | tf_op jit(solution)/shard_map/ppermute | solution.py:272
  35.8 1.7 %collective-permute-start.13 = (f32[64,128]{1,0:T(8,128)S(1)}, f32[64,128]{1,0:T(8,128)S(1)}, u32[]{:S(2)}, u32[]{:S(2)}) collective-permute-start(f32[64,128]{1,0:T(8,128)S(1)} %get-tuple-element.20), channel_id=1, source_target_pairs={{0,2},{1,3},{2,0},{3,1},{4,6},{5,7},{6,4},{7,5},{8,10},{9,11},{10,... | collective-permute-start | bytes 98312 | tf_op jit(solution)/shard_map/ppermute | solution.py:272
  37.6 0.7 %collective-permute-start.18 = (f32[64,128]{1,0:T(8,128)S(1)}, f32[64,128]{1,0:T(8,128)S(1)}, u32[]{:S(2)}, u32[]{:S(2)}) collective-permute-start(f32[64,128]{1,0:T(8,128)S(1)} %fusion.2), channel_id=1, source_target_pairs={{0,4},{4,0},{1,5},{5,1},{2,6},{6,2},{3,7},{7,3},{8,12},{12,8},{9,1... | collective-permute-start | bytes 98312 | tf_op jit(solution)/shard_map/ppermute | solution.py:242
  38.3 2.0 %collective-permute-done.14 = f32[64,128]{1,0:T(8,128)S(1)} collective-permute-done((f32[64,128]{1,0:T(8,128)S(1)}, f32[64,128]{1,0:T(8,128)S(1)}, u32[]{:S(2)}, u32[]{:S(2)}) %collective-permute-start.14) | collective-permute-done | bytes 32800 | tf_op jit(solution)/shard_map/ppermute | solution.py:272
  40.3 2.2 %collective-permute-done.18 = f32[64,128]{1,0:T(8,128)S(1)} collective-permute-done((f32[64,128]{1,0:T(8,128)S(1)}, f32[64,128]{1,0:T(8,128)S(1)}, u32[]{:S(2)}, u32[]{:S(2)}) %collective-permute-start.18) | collective-permute-done | bytes 32800 | tf_op jit(solution)/shard_map/ppermute | solution.py:242
  42.5 0.6 %fusion.7 = f32[128,64]{0,1:T(8,128)} fusion(f32[64,128]{1,0:T(8,128)S(1)} %collective-permute-done.18, f32[64,128]{1,0:T(8,128)S(1)} %collective-permute-done.14, f32[64,128]{1,0:T(8,128)S(1)} %collective-permute-done.13, f32[64,128]{1,0:T(8,128)S(1)} %collective-permute-done.12, f32[8,64,128]{2,1,0:T(8,128)S(1)} %combine.1), kind=kLoop, calls=%fused_computation.17 | loop fusion | flops 32768 | bytes 196608 | tf_op jit(solution)/shard_map/transpose | solution.py:325
  (31 shorter events, 0.7 us)
Async XLA Ops:
  1.7 14.2 %collective-permute-start.6 = (f32[520,128]{1,0:T(8,128)S(1)}, f32[520,128]{1,0:T(8,128)S(1)}, u32[]{:S(2)}, u32[]{:S(2)}) collective-permute-start(f32[520,128]{1,0:T(8,128)S(1)} %select_maximum_fusion.rest_4_), channel_id=1, source_target_pairs={{0,6},{1,7},{2,4},{3,5},{4,2},{5,3},{6,0},{7,1},{8,14},{9,15},{10,... | collective-permute-start | bytes 798728 | tf_op jit(solution)/shard_map/ppermute | solution.py:248
  6.8 9.1 %collective-permute-start.4 = (f32[520,128]{1,0:T(8,128)S(1)}, f32[520,128]{1,0:T(8,128)S(1)}, u32[]{:S(2)}, u32[]{:S(2)}) collective-permute-start(f32[520,128]{1,0:T(8,128)S(1)} %select_maximum_fusion.rest_4_), channel_id=1, source_target_pairs={{0,16},{8,24},{16,0},{24,8},{1,17},{9,25},{17,1},{25,9},{2,18},{10... | collective-permute-start | bytes 798728 | tf_op jit(solution)/shard_map/ppermute | solution.py:238
  12.3 8.7 %collective-permute-start = (f32[520,128]{1,0:T(8,128)}, f32[520,128]{1,0:T(8,128)S(1)}, u32[]{:S(2)}, u32[]{:S(2)}) collective-permute-start(f32[520,128]{1,0:T(8,128)} %get-tuple-element.11), channel_id=1, source_target_pairs={{0,1},{1,0},{2,3},{3,2},{4,5},{5,4},{6,7},{7,6},{8,9},{9,8},{10,11... | collective-permute-start | bytes 798728 | tf_op jit(solution)/shard_map/ppermute | solution.py:318
  13.8 2.0 %copy-start.1 = (f32[8,128]{1,0:T(8,128)S(1)}, f32[8,128]{1,0:T(8,128)}, u32[]{:S(2)}) copy-start(f32[8,128]{1,0:T(8,128)} %get-tuple-element.14.mark_ref) | copy-start | bytes 12292
  13.8 9.5 %collective-permute-start.1 = (f32[520,128]{1,0:T(8,128)}, f32[520,128]{1,0:T(8,128)S(1)}, u32[]{:S(2)}, u32[]{:S(2)}) collective-permute-start(f32[520,128]{1,0:T(8,128)} %get-tuple-element.12), channel_id=1, source_target_pairs={{0,2},{1,3},{2,0},{3,1},{4,6},{5,7},{6,4},{7,5},{8,10},{9,11},{10,... | collective-permute-start | bytes 798728 | tf_op jit(solution)/shard_map/ppermute | solution.py:318
  13.8 13.2 %collective-permute-start.2 = (f32[520,128]{1,0:T(8,128)}, f32[520,128]{1,0:T(8,128)S(1)}, u32[]{:S(2)}, u32[]{:S(2)}) collective-permute-start(f32[520,128]{1,0:T(8,128)} %get-tuple-element.13), channel_id=1, source_target_pairs={{0,3},{1,2},{2,1},{3,0},{4,7},{5,6},{6,5},{7,4},{8,11},{9,10},{10,... | collective-permute-start | bytes 798728 | tf_op jit(solution)/shard_map/ppermute | solution.py:318
  15.9 11.7 %copy-start = (f32[520,128]{1,0:T(8,128)S(1)}, f32[520,128]{1,0:T(8,128)}, u32[]{:S(2)}) copy-start(f32[520,128]{1,0:T(8,128)} %get-tuple-element.10.refs_0_.rest_0_) | copy-start | bytes 798724
  15.9 11.1 %collective-permute-start.8 = (f32[256,128]{1,0:T(8,128)S(1)}, f32[256,128]{1,0:T(8,128)S(1)}, u32[]{:S(2)}, u32[]{:S(2)}) collective-permute-start(f32[256,128]{1,0:T(8,128)S(1)} %slice.50), channel_id=1, source_target_pairs={{0,16},{8,24},{16,0},{24,8},{1,17},{9,25},{17,1},{25,9},{2,18},{10... | collective-permute-start | bytes 393224 | tf_op jit(solution)/shard_map/ppermute | solution.py:238
  16.5 11.0 %collective-permute-start.9 = (f32[264,128]{1,0:T(8,128)S(1)}, f32[264,128]{1,0:T(8,128)S(1)}, u32[]{:S(2)}, u32[]{:S(2)}) collective-permute-start(f32[264,128]{1,0:T(8,128)S(1)} %slice.51), channel_id=1, source_target_pairs={{0,16},{8,24},{16,0},{24,8},{1,17},{9,25},{17,1},{25,9},{2,18},{10... | collective-permute-start | bytes 405512 | tf_op jit(solution)/shard_map/ppermute | solution.py:238
  21.0 6.6 %collective-permute-start.3 = (f32[520,128]{1,0:T(8,128)S(1)}, f32[520,128]{1,0:T(8,128)S(1)}, u32[]{:S(2)}, u32[]{:S(2)}) collective-permute-start(f32[520,128]{1,0:T(8,128)S(1)} %select_maximum_fusion.rest_4_), channel_id=1, source_target_pairs={{0,8},{8,0},{16,24},{24,16},{1,9},{9,1},{17,25},{25,17},{2,10},{10... | collective-permute-start | bytes 798728 | tf_op jit(solution)/shard_map/ppermute | solution.py:238
  23.4 5.4 %collective-permute-start.7 = (f32[520,128]{1,0:T(8,128)S(1)}, f32[520,128]{1,0:T(8,128)S(1)}, u32[]{:S(2)}, u32[]{:S(2)}) collective-permute-start(f32[520,128]{1,0:T(8,128)S(1)} %hold_until.1.rest_8_), channel_id=1, source_target_pairs={{0,8},{8,0},{16,24},{24,16},{1,9},{9,1},{17,25},{25,17},{2,10},{10... | collective-permute-start | bytes 798728 | tf_op jit(solution)/shard_map/ppermute | solution.py:238
  27.0 1.7 %collective-permute-start.5 = (f32[520,128]{1,0:T(8,128)S(1)}, f32[520,128]{1,0:T(8,128)S(1)}, u32[]{:S(2)}, u32[]{:S(2)}) collective-permute-start(f32[520,128]{1,0:T(8,128)S(1)} %collective-permute-done.4.next_ref.rest_6_), channel_id=1, source_target_pairs={{0,8},{8,0},{16,24},{24,16},{1,9},{9,1},{17,25},{25,17},{2,10},{10... | collective-permute-start | bytes 798728 | tf_op jit(solution)/shard_map/ppermute | solution.py:238
  27.0 1.7 %collective-permute-start.10 = (f32[256,128]{1,0:T(8,128)S(1)}, f32[256,128]{1,0:T(8,128)S(1)}, u32[]{:S(2)}, u32[]{:S(2)}) collective-permute-start(f32[256,128]{1,0:T(8,128)S(1)} %collective-permute-done.8.rest_10_), channel_id=1, source_target_pairs={{0,8},{8,0},{16,24},{24,16},{1,9},{9,1},{17,25},{25,17},{2,10},{10... | collective-permute-start | bytes 393224 | tf_op jit(solution)/shard_map/ppermute | solution.py:238
  27.5 1.4 %collective-permute-start.11 = (f32[264,128]{1,0:T(8,128)S(1)}, f32[264,128]{1,0:T(8,128)S(1)}, u32[]{:S(2)}, u32[]{:S(2)}) collective-permute-start(f32[264,128]{1,0:T(8,128)S(1)} %collective-permute-done.9.rest_11_), channel_id=1, source_target_pairs={{0,8},{8,0},{16,24},{24,16},{1,9},{9,1},{17,25},{25,17},{2,10},{10... | collective-permute-start | bytes 405512 | tf_op jit(solution)/shard_map/ppermute | solution.py:238
  30.5 5.3 %collective-permute-start.17 = (f32[64,128]{1,0:T(8,128)S(1)}, f32[64,128]{1,0:T(8,128)S(1)}, u32[]{:S(2)}, u32[]{:S(2)}) collective-permute-start(f32[64,128]{1,0:T(8,128)S(1)} %get-tuple-element.16), channel_id=1, source_target_pairs={{0,3},{1,2},{2,1},{3,0},{4,7},{5,6},{6,5},{7,4},{8,11},{9,10},{10,... | collective-permute-start | bytes 98312 | tf_op jit(solution)/shard_map/ppermute | solution.py:272
  31.8 5.8 %collective-permute-start.16 = (f32[64,128]{1,0:T(8,128)S(1)}, f32[64,128]{1,0:T(8,128)S(1)}, u32[]{:S(2)}, u32[]{:S(2)}) collective-permute-start(f32[64,128]{1,0:T(8,128)S(1)} %get-tuple-element.17), channel_id=1, source_target_pairs={{0,2},{1,3},{2,0},{3,1},{4,6},{5,7},{6,4},{7,5},{8,10},{9,11},{10,... | collective-permute-start | bytes 98312 | tf_op jit(solution)/shard_map/ppermute | solution.py:272
  33.5 4.0 %collective-permute-start.15 = (f32[64,128]{1,0:T(8,128)S(1)}, f32[64,128]{1,0:T(8,128)S(1)}, u32[]{:S(2)}, u32[]{:S(2)}) collective-permute-start(f32[64,128]{1,0:T(8,128)S(1)} %get-tuple-element.18), channel_id=1, source_target_pairs={{0,1},{1,0},{2,3},{3,2},{4,5},{5,4},{6,7},{7,6},{8,9},{9,8},{10,11... | collective-permute-start | bytes 98312 | tf_op jit(solution)/shard_map/ppermute | solution.py:272
  34.0 4.3 %collective-permute-start.12 = (f32[64,128]{1,0:T(8,128)S(1)}, f32[64,128]{1,0:T(8,128)S(1)}, u32[]{:S(2)}, u32[]{:S(2)}) collective-permute-start(f32[64,128]{1,0:T(8,128)S(1)} %get-tuple-element.15), channel_id=1, source_target_pairs={{0,1},{1,0},{2,3},{3,2},{4,5},{5,4},{6,7},{7,6},{8,9},{9,8},{10,11... | collective-permute-start | bytes 98312 | tf_op jit(solution)/shard_map/ppermute | solution.py:272
  35.5 4.8 %collective-permute-start.14 = (f32[64,128]{1,0:T(8,128)S(1)}, f32[64,128]{1,0:T(8,128)S(1)}, u32[]{:S(2)}, u32[]{:S(2)}) collective-permute-start(f32[64,128]{1,0:T(8,128)S(1)} %get-tuple-element.19), channel_id=1, source_target_pairs={{0,3},{1,2},{2,1},{3,0},{4,7},{5,6},{6,5},{7,4},{8,11},{9,10},{10,... | collective-permute-start | bytes 98312 | tf_op jit(solution)/shard_map/ppermute | solution.py:272
  35.8 4.6 %collective-permute-start.13 = (f32[64,128]{1,0:T(8,128)S(1)}, f32[64,128]{1,0:T(8,128)S(1)}, u32[]{:S(2)}, u32[]{:S(2)}) collective-permute-start(f32[64,128]{1,0:T(8,128)S(1)} %get-tuple-element.20), channel_id=1, source_target_pairs={{0,2},{1,3},{2,0},{3,1},{4,6},{5,7},{6,4},{7,5},{8,10},{9,11},{10,... | collective-permute-start | bytes 98312 | tf_op jit(solution)/shard_map/ppermute | solution.py:272
  37.6 4.9 %collective-permute-start.18 = (f32[64,128]{1,0:T(8,128)S(1)}, f32[64,128]{1,0:T(8,128)S(1)}, u32[]{:S(2)}, u32[]{:S(2)}) collective-permute-start(f32[64,128]{1,0:T(8,128)S(1)} %fusion.2), channel_id=1, source_target_pairs={{0,4},{4,0},{1,5},{5,1},{2,6},{6,2},{3,7},{7,3},{8,12},{12,8},{9,1... | collective-permute-start | bytes 98312 | tf_op jit(solution)/shard_map/ppermute | solution.py:242

commit v28 on v27

--- a/solution.py
+++ b/solution.py
@@ -12,6 +12,7 @@
 LANES = 128
 EXTRA = 8
 HOLD_FLOPS = 16 << 30
+INDEX_FLOPS = 1 << 30
 VMEM_LIMIT = 48 * 1024 * 1024
 
 
@@ -158,7 +159,7 @@
         in_specs=[pl.BlockSpec(memory_space=pltpu.VMEM)] * len(parts),
         out_specs=pl.BlockSpec(memory_space=pltpu.VMEM),
         compiler_params=pltpu.CompilerParams(vmem_limit_bytes=VMEM_LIMIT),
-        cost_estimate=pl.CostEstimate(flops=HOLD_FLOPS, bytes_accessed=HOLD_FLOPS >> 8, transcendentals=0),
+        cost_estimate=pl.CostEstimate(flops=INDEX_FLOPS, bytes_accessed=INDEX_FLOPS >> 8, transcendentals=0),
         name="index_table",
     )(*parts)
 

time: 43.3 us -> 43.3 us (level)
  no operation moved by 1% of the time
where the time goes in v28:
time: 43.3 us; the launch traced here: 43.1 us
  starting transfers between devices  20.7 us (48%)
  waiting for transfers between devices  14.4 us (33%)
  Pallas kernels  5.52 us (13%)
  other arithmetic  2.36 us (5%)
    ppermute x3, waiting for transfers between devices, local(): lax.ppermute(parts[ahead], 'near', [(n, n ^ ahead) for n in range(half)])  8.94 us
    ppermute x6, starting transfers between devices, add_over_near(): lax.ppermute(sums[near], 'near', [(n, n ^ near) for n in range(half)])  7.04 us
    ppermute x1, starting transfers between devices, far_swap(): return lax.ppermute(x, ('half', 'near'), pairs)  5.11 us
    ppermute x8, starting transfers between devices, row_swap(): lax.ppermute(x, 'row', [(r, r ^ bit) for r in range(lax.axis_size('row'))])  4.27 us
    pallas_call x1, Pallas kernels, restrict_operator(): pl.pallas_call(restrict_kernel, out_shape=(jax.ShapeDtypeStruct((EXTRA, w...  3.98 us
    ppermute x3, starting transfers between devices, local(): lax.ppermute(parts[ahead], 'near', [(n, n ^ ahead) for n in range(half)])  3.55 us
    ppermute x1, waiting for transfers between devices, half_swap(): return lax.ppermute(x, 'half', [(0, 1), (1, 0)])  2.16 us
    ppermute x6, waiting for transfers between devices, add_over_near(): lax.ppermute(sums[near], 'near', [(n, n ^ near) for n in range(half)])  2.06 us
  transfers between devices with their start and end apart: 19, of which 7 were waited for; matrix products, arithmetic and copies ran while one was open for 0% of the time, Pallas kernels for 9%

profile of v28, /device:TPU:0, one launch (start us, length us, event | category | flops | bytes accessed | tf_op | source)
XLA Modules:
  0.0 43.1 jit_solution(3002227991472015418)
XLA Ops:
  0.0 0.7 %convert_bitcast_fusion = f32[2,8]{1,0:T(2,128)S(1)} fusion(s32[8,2]{0,1:T(2,128)} %param.13), kind=kLoop, calls=%fused_computation.18 | loop fusion | flops 16 | bytes 128 | tf_op jit(solution)/shard_map/convert_element_type | solution.py:285
  0.7 1.0 %select_maximum_fusion.rest_4_ = f32[520,128]{1,0:T(8,128)S(1)} fusion(f32[2,8]{1,0:T(2,128)S(1)} %convert_bitcast_fusion, f32[512,128]{1,0:T(8,128)} %bitcast.46), kind=kLoop, calls=%fused_computation | loop fusion | flops 199680 | bytes 528448 | tf_op jit(solution)/shard_map/concatenate | solution.py:286
  1.7 5.1 %collective-permute-start.6 = (f32[520,128]{1,0:T(8,128)S(1)}, f32[520,128]{1,0:T(8,128)S(1)}, u32[]{:S(2)}, u32[]{:S(2)}) collective-permute-start(f32[520,128]{1,0:T(8,128)S(1)} %select_maximum_fusion.rest_4_), channel_id=1, source_target_pairs={{0,6},{1,7},{2,4},{3,5},{4,2},{5,3},{6,0},{7,1},{8,14},{9,15},{10,... | collective-permute-start | bytes 798728 | tf_op jit(solution)/shard_map/ppermute | solution.py:249
  6.8 1.5 %collective-permute-start.4 = (f32[520,128]{1,0:T(8,128)S(1)}, f32[520,128]{1,0:T(8,128)S(1)}, u32[]{:S(2)}, u32[]{:S(2)}) collective-permute-start(f32[520,128]{1,0:T(8,128)S(1)} %select_maximum_fusion.rest_4_), channel_id=1, source_target_pairs={{0,16},{8,24},{16,0},{24,8},{1,17},{9,25},{17,1},{25,9},{2,18},{10... | collective-permute-start | bytes 798728 | tf_op jit(solution)/shard_map/ppermute | solution.py:239
  8.3 4.0 %restrict_operator.1 = (f32[8,128]{1,0:T(8,128)}, f32[520,128]{1,0:T(8,128)}, f32[520,128]{1,0:T(8,128)}, f32[520,128]{1,0:T(8,128)}, f32[520,128]{1,0:T(8,128)}) custom-call(s32[8]{0:T(128)} %count_any.1, s32[8,8]{1,0:T(8,128)} %slot_any.1, s32[2,8]{1,0:T(2,128)} %bitcast.48, s32[4,8]{1,0:T(4,128)} %bitcast.47, f32[8,64,128]{2,1,0:T(8,128)} %restrict_any.1, ...), custom_call_target="tpu_custom_call" | custom-call | flops 201326592 | bytes 4194304 | tf_op jit(solution)/shard_map/restrict_operator/pallas_call | solution.py:129
  12.3 1.6 %collective-permute-start = (f32[520,128]{1,0:T(8,128)}, f32[520,128]{1,0:T(8,128)S(1)}, u32[]{:S(2)}, u32[]{:S(2)}) collective-permute-start(f32[520,128]{1,0:T(8,128)} %get-tuple-element.11), channel_id=1, source_target_pairs={{0,1},{1,0},{2,3},{3,2},{4,5},{5,4},{6,7},{7,6},{8,9},{9,8},{10,11... | collective-permute-start | bytes 798728 | tf_op jit(solution)/shard_map/ppermute | solution.py:319
  13.8 2.0 %collective-permute-start.2 = (f32[520,128]{1,0:T(8,128)}, f32[520,128]{1,0:T(8,128)S(1)}, u32[]{:S(2)}, u32[]{:S(2)}) collective-permute-start(f32[520,128]{1,0:T(8,128)} %get-tuple-element.13), channel_id=1, source_target_pairs={{0,3},{1,2},{2,1},{3,0},{4,7},{5,6},{6,5},{7,4},{8,11},{9,10},{10,... | collective-permute-start | bytes 798728 | tf_op jit(solution)/shard_map/ppermute | solution.py:319
  15.9 0.6 %collective-permute-start.9 = (f32[264,128]{1,0:T(8,128)S(1)}, f32[264,128]{1,0:T(8,128)S(1)}, u32[]{:S(2)}, u32[]{:S(2)}) collective-permute-start(f32[264,128]{1,0:T(8,128)S(1)} %slice.51), channel_id=1, source_target_pairs={{0,16},{8,24},{16,0},{24,8},{1,17},{9,25},{17,1},{25,9},{2,18},{10... | collective-permute-start | bytes 405512 | tf_op jit(solution)/shard_map/ppermute | solution.py:239
  16.5 1.6 %collective-permute-start.8 = (f32[256,128]{1,0:T(8,128)S(1)}, f32[256,128]{1,0:T(8,128)S(1)}, u32[]{:S(2)}, u32[]{:S(2)}) collective-permute-start(f32[256,128]{1,0:T(8,128)S(1)} %slice.50), channel_id=1, source_target_pairs={{0,16},{8,24},{16,0},{24,8},{1,17},{9,25},{17,1},{25,9},{2,18},{10... | collective-permute-start | bytes 393224 | tf_op jit(solution)/shard_map/ppermute | solution.py:239
  18.1 2.9 %collective-permute-done.refs_1_.rest_1_ = f32[520,128]{1,0:T(8,128)S(1)} collective-permute-done((f32[520,128]{1,0:T(8,128)}, f32[520,128]{1,0:T(8,128)S(1)}, u32[]{:S(2)}, u32[]{:S(2)}) %collective-permute-start) | collective-permute-done | bytes 266272 | tf_op jit(solution)/shard_map/ppermute | solution.py:319
  21.0 2.4 %collective-permute-done.1.refs_2_.rest_2_ = f32[520,128]{1,0:T(8,128)S(1)} collective-permute-done((f32[520,128]{1,0:T(8,128)}, f32[520,128]{1,0:T(8,128)S(1)}, u32[]{:S(2)}, u32[]{:S(2)}) %collective-permute-start.1) | collective-permute-done | bytes 266272 | tf_op jit(solution)/shard_map/ppermute | solution.py:319
  23.4 3.6 %collective-permute-done.2.refs_3_.rest_3_ = f32[520,128]{1,0:T(8,128)S(1)} collective-permute-done((f32[520,128]{1,0:T(8,128)}, f32[520,128]{1,0:T(8,128)S(1)}, u32[]{:S(2)}, u32[]{:S(2)}) %collective-permute-start.2) | collective-permute-done | bytes 266272 | tf_op jit(solution)/shard_map/ppermute | solution.py:319
  27.0 0.5 %collective-permute-start.10 = (f32[256,128]{1,0:T(8,128)S(1)}, f32[256,128]{1,0:T(8,128)S(1)}, u32[]{:S(2)}, u32[]{:S(2)}) collective-permute-start(f32[256,128]{1,0:T(8,128)S(1)} %collective-permute-done.8.rest_10_), channel_id=1, source_target_pairs={{0,8},{8,0},{16,24},{24,16},{1,9},{9,1},{17,25},{25,17},{2,10},{10... | collective-permute-start | bytes 393224 | tf_op jit(solution)/shard_map/ppermute | solution.py:239
  27.7 1.0 %collective-permute-done.10.rest_12_ = f32[256,128]{1,0:T(8,128)S(1)} collective-permute-done((f32[256,128]{1,0:T(8,128)S(1)}, f32[256,128]{1,0:T(8,128)S(1)}, u32[]{:S(2)}, u32[]{:S(2)}) %collective-permute-start.10) | collective-permute-done | bytes 131104 | tf_op jit(solution)/shard_map/ppermute | solution.py:239
  28.9 1.5 %combine.1 = f32[8,64,128]{2,1,0:T(8,128)S(1)} custom-call(s32[1,10]{1,0:T(1,128)S(1)} %add_bitcast_fusion.own_ref, s32[8,128]{1,0:T(8,128)S(1)} %index_table.1.wanted_ref, f32[520,128]{1,0:T(8,128)S(1)} %copy-done, f32[520,128]{1,0:T(8,128)S(1)} %collective-permute-done.refs_1_.rest_1_, f32[520,128]{1,0:T(8,128)S(1)} %collective-permute-done.1.refs_2_.rest_2_, ...), custom_call_target="tpu_custom_call" | custom-call | flops 268435456 | bytes 4194304 | tf_op jit(solution)/shard_map/combine/pallas_call | solution.py:219
  30.5 1.3 %collective-permute-start.17 = (f32[64,128]{1,0:T(8,128)S(1)}, f32[64,128]{1,0:T(8,128)S(1)}, u32[]{:S(2)}, u32[]{:S(2)}) collective-permute-start(f32[64,128]{1,0:T(8,128)S(1)} %get-tuple-element.16), channel_id=1, source_target_pairs={{0,3},{1,2},{2,1},{3,0},{4,7},{5,6},{6,5},{7,4},{8,11},{9,10},{10,... | collective-permute-start | bytes 98312 | tf_op jit(solution)/shard_map/ppermute | solution.py:273
  31.8 1.7 %collective-permute-start.16 = (f32[64,128]{1,0:T(8,128)S(1)}, f32[64,128]{1,0:T(8,128)S(1)}, u32[]{:S(2)}, u32[]{:S(2)}) collective-permute-start(f32[64,128]{1,0:T(8,128)S(1)} %get-tuple-element.17), channel_id=1, source_target_pairs={{0,2},{1,3},{2,0},{3,1},{4,6},{5,7},{6,4},{7,5},{8,10},{9,11},{10,... | collective-permute-start | bytes 98312 | tf_op jit(solution)/shard_map/ppermute | solution.py:273
  33.5 0.5 %collective-permute-start.15 = (f32[64,128]{1,0:T(8,128)S(1)}, f32[64,128]{1,0:T(8,128)S(1)}, u32[]{:S(2)}, u32[]{:S(2)}) collective-permute-start(f32[64,128]{1,0:T(8,128)S(1)} %get-tuple-element.18), channel_id=1, source_target_pairs={{0,1},{1,0},{2,3},{3,2},{4,5},{5,4},{6,7},{7,6},{8,9},{9,8},{10,11... | collective-permute-start | bytes 98312 | tf_op jit(solution)/shard_map/ppermute | solution.py:273
  34.0 1.5 %collective-permute-start.12 = (f32[64,128]{1,0:T(8,128)S(1)}, f32[64,128]{1,0:T(8,128)S(1)}, u32[]{:S(2)}, u32[]{:S(2)}) collective-permute-start(f32[64,128]{1,0:T(8,128)S(1)} %get-tuple-element.15), channel_id=1, source_target_pairs={{0,1},{1,0},{2,3},{3,2},{4,5},{5,4},{6,7},{7,6},{8,9},{9,8},{10,11... | collective-permute-start | bytes 98312 | tf_op jit(solution)/shard_map/ppermute | solution.py:273
  35.8 1.7 %collective-permute-start.13 = (f32[64,128]{1,0:T(8,128)S(1)}, f32[64,128]{1,0:T(8,128)S(1)}, u32[]{:S(2)}, u32[]{:S(2)}) collective-permute-start(f32[64,128]{1,0:T(8,128)S(1)} %get-tuple-element.20), channel_id=1, source_target_pairs={{0,2},{1,3},{2,0},{3,1},{4,6},{5,7},{6,4},{7,5},{8,10},{9,11},{10,... | collective-permute-start | bytes 98312 | tf_op jit(solution)/shard_map/ppermute | solution.py:273
  37.6 0.7 %collective-permute-start.18 = (f32[64,128]{1,0:T(8,128)S(1)}, f32[64,128]{1,0:T(8,128)S(1)}, u32[]{:S(2)}, u32[]{:S(2)}) collective-permute-start(f32[64,128]{1,0:T(8,128)S(1)} %fusion.2), channel_id=1, source_target_pairs={{0,4},{4,0},{1,5},{5,1},{2,6},{6,2},{3,7},{7,3},{8,12},{12,8},{9,1... | collective-permute-start | bytes 98312 | tf_op jit(solution)/shard_map/ppermute | solution.py:243
  38.3 2.0 %collective-permute-done.14 = f32[64,128]{1,0:T(8,128)S(1)} collective-permute-done((f32[64,128]{1,0:T(8,128)S(1)}, f32[64,128]{1,0:T(8,128)S(1)}, u32[]{:S(2)}, u32[]{:S(2)}) %collective-permute-start.14) | collective-permute-done | bytes 32800 | tf_op jit(solution)/shard_map/ppermute | solution.py:273
  40.4 2.2 %collective-permute-done.18 = f32[64,128]{1,0:T(8,128)S(1)} collective-permute-done((f32[64,128]{1,0:T(8,128)S(1)}, f32[64,128]{1,0:T(8,128)S(1)}, u32[]{:S(2)}, u32[]{:S(2)}) %collective-permute-start.18) | collective-permute-done | bytes 32800 | tf_op jit(solution)/shard_map/ppermute | solution.py:243
  42.5 0.6 %fusion.7 = f32[128,64]{0,1:T(8,128)} fusion(f32[64,128]{1,0:T(8,128)S(1)} %collective-permute-done.18, f32[64,128]{1,0:T(8,128)S(1)} %collective-permute-done.14, f32[64,128]{1,0:T(8,128)S(1)} %collective-permute-done.13, f32[64,128]{1,0:T(8,128)S(1)} %collective-permute-done.12, f32[8,64,128]{2,1,0:T(8,128)S(1)} %combine.1), kind=kLoop, calls=%fused_computation.17 | loop fusion | flops 32768 | bytes 196608 | tf_op jit(solution)/shard_map/transpose | solution.py:326
  (31 shorter events, 0.7 us)
Async XLA Ops:
  1.7 14.2 %collective-permute-start.6 = (f32[520,128]{1,0:T(8,128)S(1)}, f32[520,128]{1,0:T(8,128)S(1)}, u32[]{:S(2)}, u32[]{:S(2)}) collective-permute-start(f32[520,128]{1,0:T(8,128)S(1)} %select_maximum_fusion.rest_4_), channel_id=1, source_target_pairs={{0,6},{1,7},{2,4},{3,5},{4,2},{5,3},{6,0},{7,1},{8,14},{9,15},{10,... | collective-permute-start | bytes 798728 | tf_op jit(solution)/shard_map/ppermute | solution.py:249
  6.8 9.1 %collective-permute-start.4 = (f32[520,128]{1,0:T(8,128)S(1)}, f32[520,128]{1,0:T(8,128)S(1)}, u32[]{:S(2)}, u32[]{:S(2)}) collective-permute-start(f32[520,128]{1,0:T(8,128)S(1)} %select_maximum_fusion.rest_4_), channel_id=1, source_target_pairs={{0,16},{8,24},{16,0},{24,8},{1,17},{9,25},{17,1},{25,9},{2,18},{10... | collective-permute-start | bytes 798728 | tf_op jit(solution)/shard_map/ppermute | solution.py:239
  12.3 3.6 %copy-start.1 = (f32[8,128]{1,0:T(8,128)S(1)}, f32[8,128]{1,0:T(8,128)}, u32[]{:S(2)}) copy-start(f32[8,128]{1,0:T(8,128)} %get-tuple-element.14.mark_ref) | copy-start | bytes 12292
  12.3 8.7 %collective-permute-start = (f32[520,128]{1,0:T(8,128)}, f32[520,128]{1,0:T(8,128)S(1)}, u32[]{:S(2)}, u32[]{:S(2)}) collective-permute-start(f32[520,128]{1,0:T(8,128)} %get-tuple-element.11), channel_id=1, source_target_pairs={{0,1},{1,0},{2,3},{3,2},{4,5},{5,4},{6,7},{7,6},{8,9},{9,8},{10,11... | collective-permute-start | bytes 798728 | tf_op jit(solution)/shard_map/ppermute | solution.py:319
  13.8 9.5 %collective-permute-start.1 = (f32[520,128]{1,0:T(8,128)}, f32[520,128]{1,0:T(8,128)S(1)}, u32[]{:S(2)}, u32[]{:S(2)}) collective-permute-start(f32[520,128]{1,0:T(8,128)} %get-tuple-element.12), channel_id=1, source_target_pairs={{0,2},{1,3},{2,0},{3,1},{4,6},{5,7},{6,4},{7,5},{8,10},{9,11},{10,... | collective-permute-start | bytes 798728 | tf_op jit(solution)/shard_map/ppermute | solution.py:319
  13.8 13.2 %collective-permute-start.2 = (f32[520,128]{1,0:T(8,128)}, f32[520,128]{1,0:T(8,128)S(1)}, u32[]{:S(2)}, u32[]{:S(2)}) collective-permute-start(f32[520,128]{1,0:T(8,128)} %get-tuple-element.13), channel_id=1, source_target_pairs={{0,3},{1,2},{2,1},{3,0},{4,7},{5,6},{6,5},{7,4},{8,11},{9,10},{10,... | collective-permute-start | bytes 798728 | tf_op jit(solution)/shard_map/ppermute | solution.py:319
  15.9 11.8 %copy-start = (f32[520,128]{1,0:T(8,128)S(1)}, f32[520,128]{1,0:T(8,128)}, u32[]{:S(2)}) copy-start(f32[520,128]{1,0:T(8,128)} %get-tuple-element.10.refs_0_.rest_0_) | copy-start | bytes 798724
  15.9 11.6 %collective-permute-start.9 = (f32[264,128]{1,0:T(8,128)S(1)}, f32[264,128]{1,0:T(8,128)S(1)}, u32[]{:S(2)}, u32[]{:S(2)}) collective-permute-start(f32[264,128]{1,0:T(8,128)S(1)} %slice.51), channel_id=1, source_target_pairs={{0,16},{8,24},{16,0},{24,8},{1,17},{9,25},{17,1},{25,9},{2,18},{10... | collective-permute-start | bytes 405512 | tf_op jit(solution)/shard_map/ppermute | solution.py:239
  16.5 10.5 %collective-permute-start.8 = (f32[256,128]{1,0:T(8,128)S(1)}, f32[256,128]{1,0:T(8,128)S(1)}, u32[]{:S(2)}, u32[]{:S(2)}) collective-permute-start(f32[256,128]{1,0:T(8,128)S(1)} %slice.50), channel_id=1, source_target_pairs={{0,16},{8,24},{16,0},{24,8},{1,17},{9,25},{17,1},{25,9},{2,18},{10... | collective-permute-start | bytes 393224 | tf_op jit(solution)/shard_map/ppermute | solution.py:239
  21.0 6.7 %collective-permute-start.3 = (f32[520,128]{1,0:T(8,128)S(1)}, f32[520,128]{1,0:T(8,128)S(1)}, u32[]{:S(2)}, u32[]{:S(2)}) collective-permute-start(f32[520,128]{1,0:T(8,128)S(1)} %select_maximum_fusion.rest_4_), channel_id=1, source_target_pairs={{0,8},{8,0},{16,24},{24,16},{1,9},{9,1},{17,25},{25,17},{2,10},{10... | collective-permute-start | bytes 798728 | tf_op jit(solution)/shard_map/ppermute | solution.py:239
  23.4 5.4 %collective-permute-start.7 = (f32[520,128]{1,0:T(8,128)S(1)}, f32[520,128]{1,0:T(8,128)S(1)}, u32[]{:S(2)}, u32[]{:S(2)}) collective-permute-start(f32[520,128]{1,0:T(8,128)S(1)} %hold_until.1.rest_8_), channel_id=1, source_target_pairs={{0,8},{8,0},{16,24},{24,16},{1,9},{9,1},{17,25},{25,17},{2,10},{10... | collective-permute-start | bytes 798728 | tf_op jit(solution)/shard_map/ppermute | solution.py:239
  27.0 1.7 %collective-permute-start.5 = (f32[520,128]{1,0:T(8,128)S(1)}, f32[520,128]{1,0:T(8,128)S(1)}, u32[]{:S(2)}, u32[]{:S(2)}) collective-permute-start(f32[520,128]{1,0:T(8,128)S(1)} %collective-permute-done.4.next_ref.rest_6_), channel_id=1, source_target_pairs={{0,8},{8,0},{16,24},{24,16},{1,9},{9,1},{17,25},{25,17},{2,10},{10... | collective-permute-start | bytes 798728 | tf_op jit(solution)/shard_map/ppermute | solution.py:239
  27.0 1.7 %collective-permute-start.10 = (f32[256,128]{1,0:T(8,128)S(1)}, f32[256,128]{1,0:T(8,128)S(1)}, u32[]{:S(2)}, u32[]{:S(2)}) collective-permute-start(f32[256,128]{1,0:T(8,128)S(1)} %collective-permute-done.8.rest_10_), channel_id=1, source_target_pairs={{0,8},{8,0},{16,24},{24,16},{1,9},{9,1},{17,25},{25,17},{2,10},{10... | collective-permute-start | bytes 393224 | tf_op jit(solution)/shard_map/ppermute | solution.py:239
  27.5 1.4 %collective-permute-start.11 = (f32[264,128]{1,0:T(8,128)S(1)}, f32[264,128]{1,0:T(8,128)S(1)}, u32[]{:S(2)}, u32[]{:S(2)}) collective-permute-start(f32[264,128]{1,0:T(8,128)S(1)} %collective-permute-done.9.rest_11_), channel_id=1, source_target_pairs={{0,8},{8,0},{16,24},{24,16},{1,9},{9,1},{17,25},{25,17},{2,10},{10... | collective-permute-start | bytes 405512 | tf_op jit(solution)/shard_map/ppermute | solution.py:239
  30.5 5.3 %collective-permute-start.17 = (f32[64,128]{1,0:T(8,128)S(1)}, f32[64,128]{1,0:T(8,128)S(1)}, u32[]{:S(2)}, u32[]{:S(2)}) collective-permute-start(f32[64,128]{1,0:T(8,128)S(1)} %get-tuple-element.16), channel_id=1, source_target_pairs={{0,3},{1,2},{2,1},{3,0},{4,7},{5,6},{6,5},{7,4},{8,11},{9,10},{10,... | collective-permute-start | bytes 98312 | tf_op jit(solution)/shard_map/ppermute | solution.py:273
  31.8 5.8 %collective-permute-start.16 = (f32[64,128]{1,0:T(8,128)S(1)}, f32[64,128]{1,0:T(8,128)S(1)}, u32[]{:S(2)}, u32[]{:S(2)}) collective-permute-start(f32[64,128]{1,0:T(8,128)S(1)} %get-tuple-element.17), channel_id=1, source_target_pairs={{0,2},{1,3},{2,0},{3,1},{4,6},{5,7},{6,4},{7,5},{8,10},{9,11},{10,... | collective-permute-start | bytes 98312 | tf_op jit(solution)/shard_map/ppermute | solution.py:273
  33.5 4.0 %collective-permute-start.15 = (f32[64,128]{1,0:T(8,128)S(1)}, f32[64,128]{1,0:T(8,128)S(1)}, u32[]{:S(2)}, u32[]{:S(2)}) collective-permute-start(f32[64,128]{1,0:T(8,128)S(1)} %get-tuple-element.18), channel_id=1, source_target_pairs={{0,1},{1,0},{2,3},{3,2},{4,5},{5,4},{6,7},{7,6},{8,9},{9,8},{10,11... | collective-permute-start | bytes 98312 | tf_op jit(solution)/shard_map/ppermute | solution.py:273
  34.0 4.3 %collective-permute-start.12 = (f32[64,128]{1,0:T(8,128)S(1)}, f32[64,128]{1,0:T(8,128)S(1)}, u32[]{:S(2)}, u32[]{:S(2)}) collective-permute-start(f32[64,128]{1,0:T(8,128)S(1)} %get-tuple-element.15), channel_id=1, source_target_pairs={{0,1},{1,0},{2,3},{3,2},{4,5},{5,4},{6,7},{7,6},{8,9},{9,8},{10,11... | collective-permute-start | bytes 98312 | tf_op jit(solution)/shard_map/ppermute | solution.py:273
  35.5 4.8 %collective-permute-start.14 = (f32[64,128]{1,0:T(8,128)S(1)}, f32[64,128]{1,0:T(8,128)S(1)}, u32[]{:S(2)}, u32[]{:S(2)}) collective-permute-start(f32[64,128]{1,0:T(8,128)S(1)} %get-tuple-element.19), channel_id=1, source_target_pairs={{0,3},{1,2},{2,1},{3,0},{4,7},{5,6},{6,5},{7,4},{8,11},{9,10},{10,... | collective-permute-start | bytes 98312 | tf_op jit(solution)/shard_map/ppermute | solution.py:273
  35.8 4.6 %collective-permute-start.13 = (f32[64,128]{1,0:T(8,128)S(1)}, f32[64,128]{1,0:T(8,128)S(1)}, u32[]{:S(2)}, u32[]{:S(2)}) collective-permute-start(f32[64,128]{1,0:T(8,128)S(1)} %get-tuple-element.20), channel_id=1, source_target_pairs={{0,2},{1,3},{2,0},{3,1},{4,6},{5,7},{6,4},{7,5},{8,10},{9,11},{10,... | collective-permute-start | bytes 98312 | tf_op jit(solution)/shard_map/ppermute | solution.py:273
  37.6 5.0 %collective-permute-start.18 = (f32[64,128]{1,0:T(8,128)S(1)}, f32[64,128]{1,0:T(8,128)S(1)}, u32[]{:S(2)}, u32[]{:S(2)}) collective-permute-start(f32[64,128]{1,0:T(8,128)S(1)} %fusion.2), channel_id=1, source_target_pairs={{0,4},{4,0},{1,5},{5,1},{2,6},{6,2},{3,7},{7,3},{8,12},{12,8},{9,1... | collective-permute-start | bytes 98312 | tf_op jit(solution)/shard_map/ppermute | solution.py:243

commit v29 on v28

--- a/solution.py
+++ b/solution.py
@@ -12,7 +12,7 @@
 LANES = 128
 EXTRA = 8
 HOLD_FLOPS = 16 << 30
-INDEX_FLOPS = 1 << 30
+INDEX_FLOPS = 1 << 20
 VMEM_LIMIT = 48 * 1024 * 1024
 
 
@@ -250,14 +250,11 @@
 
 
 def spread_over_rows(blocks, rows, cut):
-    pieces = {0: [blocks]}
+    pieces = {0: [blocks[:cut], blocks[cut:]] if cut else [blocks]}
     bit = rows // 2
     while bit:
         for mask in list(pieces):
-            chunks = pieces[mask]
-            if cut and bit == rows // 2:
-                chunks = [blocks[:cut], blocks[cut:]]
-            pieces[mask ^ bit] = [row_swap(chunk, bit) for chunk in chunks]
+            pieces[mask ^ bit] = [row_swap(chunk, bit) for chunk in pieces[mask]]
         bit //= 2
     return [pieces[mask] for mask in range(rows)]
 

time: 43.3 us -> 44.6 us (1.030)
  waiting for transfers between devices: 14.4 us -> 15.6 us
    ppermute x3, waiting for transfers between devices: 8.94 us -> 11.3 us  [local(): lax.ppermute(parts[ahead], 'near', [(n, n ^ ahead) for n in range(half)])]
    ppermute x1, starting transfers between devices: 5.11 us -> 3.6 us  [far_swap(): return lax.ppermute(x, ('half', 'near'), pairs)]
    ppermute x8 -> x9, starting transfers between devices: 4.27 us -> 5.14 us  [row_swap(): lax.ppermute(x, 'row', [(r, r ^ bit) for r in range(lax.axis_size('row'))])]
    ppermute x1, starting transfers between devices: 0.74 us -> 1.43 us  [half_swap(): return lax.ppermute(x, 'half', [(0, 1), (1, 0)])]
    ppermute x8 -> x9, waiting for transfers between devices: 1.23 us -> 0.94 us  [row_swap(): lax.ppermute(x, 'row', [(r, r ^ bit) for r in range(lax.axis_size('row'))])]
  transfers between devices with their start and end apart: 19 -> 20, of which waited for: 7 -> 9; matrix products, arithmetic and copies ran while one was open for 0% -> 0% of each run, Pallas kernels for 9% -> 9%
where the time goes in v29:
time: 44.6 us; the launch traced here: 44.5 us
  starting transfers between devices  20.8 us (47%)
  waiting for transfers between devices  15.6 us (35%)
  Pallas kernels  5.53 us (12%)
  other arithmetic  2.37 us (5%)
    ppermute x3, waiting for transfers between devices, local(): lax.ppermute(parts[ahead], 'near', [(n, n ^ ahead) for n in range(half)])  11.3 us
    ppermute x6, starting transfers between devices, add_over_near(): lax.ppermute(sums[near], 'near', [(n, n ^ near) for n in range(half)])  7.04 us
    ppermute x9, starting transfers between devices, row_swap(): lax.ppermute(x, 'row', [(r, r ^ bit) for r in range(lax.axis_size('row'))])  5.14 us
    pallas_call x1, Pallas kernels, restrict_operator(): pl.pallas_call(restrict_kernel, out_shape=(jax.ShapeDtypeStruct((EXTRA, w...  3.99 us
    ppermute x1, starting transfers between devices, far_swap(): return lax.ppermute(x, ('half', 'near'), pairs)  3.6 us
    ppermute x3, starting transfers between devices, local(): lax.ppermute(parts[ahead], 'near', [(n, n ^ ahead) for n in range(half)])  3.55 us
    ppermute x1, waiting for transfers between devices, half_swap(): return lax.ppermute(x, 'half', [(0, 1), (1, 0)])  1.8 us
    ppermute x6, waiting for transfers between devices, add_over_near(): lax.ppermute(sums[near], 'near', [(n, n ^ near) for n in range(half)])  1.65 us
  transfers between devices with their start and end apart: 20, of which 9 were waited for; matrix products, arithmetic and copies ran while one was open for 0% of the time, Pallas kernels for 9%

profile of v29, /device:TPU:0, one launch (start us, length us, event | category | flops | bytes accessed | tf_op | source)
XLA Modules:
  0.0 44.5 jit_solution(13550050604838315020)
XLA Ops:
  0.0 0.7 %convert_bitcast_fusion = f32[2,8]{1,0:T(2,128)S(1)} fusion(s32[8,2]{0,1:T(2,128)} %param.13), kind=kLoop, calls=%fused_computation.18 | loop fusion | flops 16 | bytes 128 | tf_op jit(solution)/shard_map/convert_element_type | solution.py:282
  0.7 1.0 %select_maximum_fusion.rest_4_ = f32[520,128]{1,0:T(8,128)S(1)} fusion(f32[2,8]{1,0:T(2,128)S(1)} %convert_bitcast_fusion, f32[512,128]{1,0:T(8,128)} %bitcast.46), kind=kLoop, calls=%fused_computation | loop fusion | flops 199680 | bytes 528448 | tf_op jit(solution)/shard_map/concatenate | solution.py:283
  1.7 3.0 %collective-permute-start.4 = (f32[520,128]{1,0:T(8,128)S(1)}, f32[520,128]{1,0:T(8,128)S(1)}, u32[]{:S(2)}, u32[]{:S(2)}) collective-permute-start(f32[520,128]{1,0:T(8,128)S(1)} %select_maximum_fusion.rest_4_), channel_id=1, source_target_pairs={{0,16},{8,24},{16,0},{24,8},{1,17},{9,25},{17,1},{25,9},{2,18},{10... | collective-permute-start | bytes 798728 | tf_op jit(solution)/shard_map/ppermute | solution.py:239
  4.7 3.6 %collective-permute-start.6 = (f32[520,128]{1,0:T(8,128)S(1)}, f32[520,128]{1,0:T(8,128)S(1)}, u32[]{:S(2)}, u32[]{:S(2)}) collective-permute-start(f32[520,128]{1,0:T(8,128)S(1)} %select_maximum_fusion.rest_4_), channel_id=1, source_target_pairs={{0,6},{1,7},{2,4},{3,5},{4,2},{5,3},{6,0},{7,1},{8,14},{9,15},{10,... | collective-permute-start | bytes 798728 | tf_op jit(solution)/shard_map/ppermute | solution.py:249
  8.3 4.0 %restrict_operator.1 = (f32[8,128]{1,0:T(8,128)}, f32[520,128]{1,0:T(8,128)}, f32[520,128]{1,0:T(8,128)}, f32[520,128]{1,0:T(8,128)}, f32[520,128]{1,0:T(8,128)}) custom-call(s32[8]{0:T(128)} %count_any.1, s32[8,8]{1,0:T(8,128)} %slot_any.1, s32[2,8]{1,0:T(2,128)} %bitcast.48, s32[4,8]{1,0:T(4,128)} %bitcast.47, f32[8,64,128]{2,1,0:T(8,128)} %restrict_any.1, ...), custom_call_target="tpu_custom_call" | custom-call | flops 201326592 | bytes 4194304 | tf_op jit(solution)/shard_map/restrict_operator/pallas_call | solution.py:129
  12.3 1.6 %collective-permute-start = (f32[520,128]{1,0:T(8,128)}, f32[520,128]{1,0:T(8,128)S(1)}, u32[]{:S(2)}, u32[]{:S(2)}) collective-permute-start(f32[520,128]{1,0:T(8,128)} %get-tuple-element.11), channel_id=1, source_target_pairs={{0,1},{1,0},{2,3},{3,2},{4,5},{5,4},{6,7},{7,6},{8,9},{9,8},{10,11... | collective-permute-start | bytes 798728 | tf_op jit(solution)/shard_map/ppermute | solution.py:316
  13.9 2.0 %collective-permute-start.2 = (f32[520,128]{1,0:T(8,128)}, f32[520,128]{1,0:T(8,128)S(1)}, u32[]{:S(2)}, u32[]{:S(2)}) collective-permute-start(f32[520,128]{1,0:T(8,128)} %get-tuple-element.13), channel_id=1, source_target_pairs={{0,3},{1,2},{2,1},{3,0},{4,7},{5,6},{6,5},{7,4},{8,11},{9,10},{10,... | collective-permute-start | bytes 798728 | tf_op jit(solution)/shard_map/ppermute | solution.py:316
  15.9 0.6 %collective-permute-start.10 = (f32[264,128]{1,0:T(8,128)S(1)}, f32[264,128]{1,0:T(8,128)S(1)}, u32[]{:S(2)}, u32[]{:S(2)}) collective-permute-start(f32[264,128]{1,0:T(8,128)S(1)} %slice.51.rest_9_), channel_id=1, source_target_pairs={{0,16},{8,24},{16,0},{24,8},{1,17},{9,25},{17,1},{25,9},{2,18},{10... | collective-permute-start | bytes 405512 | tf_op jit(solution)/shard_map/ppermute | solution.py:239
  16.5 4.9 %collective-permute-done.refs_1_.rest_1_ = f32[520,128]{1,0:T(8,128)S(1)} collective-permute-done((f32[520,128]{1,0:T(8,128)}, f32[520,128]{1,0:T(8,128)S(1)}, u32[]{:S(2)}, u32[]{:S(2)}) %collective-permute-start) | collective-permute-done | bytes 266272 | tf_op jit(solution)/shard_map/ppermute | solution.py:316
  21.4 0.5 %collective-permute-start.9 = (f32[256,128]{1,0:T(8,128)S(1)}, f32[256,128]{1,0:T(8,128)S(1)}, u32[]{:S(2)}, u32[]{:S(2)}) collective-permute-start(f32[256,128]{1,0:T(8,128)S(1)} %slice.50.rest_8_), channel_id=1, source_target_pairs={{0,16},{8,24},{16,0},{24,8},{1,17},{9,25},{17,1},{25,9},{2,18},{10... | collective-permute-start | bytes 393224 | tf_op jit(solution)/shard_map/ppermute | solution.py:239
  21.9 1.4 %collective-permute-done.1.refs_2_.rest_2_ = f32[520,128]{1,0:T(8,128)S(1)} collective-permute-done((f32[520,128]{1,0:T(8,128)}, f32[520,128]{1,0:T(8,128)S(1)}, u32[]{:S(2)}, u32[]{:S(2)}) %collective-permute-start.1) | collective-permute-done | bytes 266272 | tf_op jit(solution)/shard_map/ppermute | solution.py:316
  23.3 5.0 %collective-permute-done.2.refs_3_.rest_3_ = f32[520,128]{1,0:T(8,128)S(1)} collective-permute-done((f32[520,128]{1,0:T(8,128)}, f32[520,128]{1,0:T(8,128)S(1)}, u32[]{:S(2)}, u32[]{:S(2)}) %collective-permute-start.2) | collective-permute-done | bytes 266272 | tf_op jit(solution)/shard_map/ppermute | solution.py:316
  28.3 0.5 %collective-permute-start.7 = (f32[256,128]{1,0:T(8,128)S(1)}, f32[256,128]{1,0:T(8,128)S(1)}, u32[]{:S(2)}, u32[]{:S(2)}) collective-permute-start(f32[256,128]{1,0:T(8,128)S(1)} %slice.50.rest_8_), channel_id=1, source_target_pairs={{0,8},{8,0},{16,24},{24,16},{1,9},{9,1},{17,25},{25,17},{2,10},{10... | collective-permute-start | bytes 393224 | tf_op jit(solution)/shard_map/ppermute | solution.py:239
  28.9 0.4 collective-permute-start.12
  30.3 1.5 %combine.1 = f32[8,64,128]{2,1,0:T(8,128)S(1)} custom-call(s32[1,10]{1,0:T(1,128)S(1)} %add_bitcast_fusion.own_ref, s32[8,128]{1,0:T(8,128)S(1)} %index_table.1.wanted_ref, f32[520,128]{1,0:T(8,128)S(1)} %copy-done, f32[520,128]{1,0:T(8,128)S(1)} %collective-permute-done.refs_1_.rest_1_, f32[520,128]{1,0:T(8,128)S(1)} %collective-permute-done.1.refs_2_.rest_2_, ...), custom_call_target="tpu_custom_call" | custom-call | flops 268435456 | bytes 4194304 | tf_op jit(solution)/shard_map/combine/pallas_call | solution.py:219
  31.9 1.6 %collective-permute-start.16 = (f32[64,128]{1,0:T(8,128)S(1)}, f32[64,128]{1,0:T(8,128)S(1)}, u32[]{:S(2)}, u32[]{:S(2)}) collective-permute-start(f32[64,128]{1,0:T(8,128)S(1)} %get-tuple-element.18), channel_id=1, source_target_pairs={{0,1},{1,0},{2,3},{3,2},{4,5},{5,4},{6,7},{7,6},{8,9},{9,8},{10,11... | collective-permute-start | bytes 98312 | tf_op jit(solution)/shard_map/ppermute | solution.py:270
  33.7 1.7 %collective-permute-start.18 = (f32[64,128]{1,0:T(8,128)S(1)}, f32[64,128]{1,0:T(8,128)S(1)}, u32[]{:S(2)}, u32[]{:S(2)}) collective-permute-start(f32[64,128]{1,0:T(8,128)S(1)} %get-tuple-element.16), channel_id=1, source_target_pairs={{0,3},{1,2},{2,1},{3,0},{4,7},{5,6},{6,5},{7,4},{8,11},{9,10},{10,... | collective-permute-start | bytes 98312 | tf_op jit(solution)/shard_map/ppermute | solution.py:270
  35.4 1.5 %collective-permute-start.13 = (f32[64,128]{1,0:T(8,128)S(1)}, f32[64,128]{1,0:T(8,128)S(1)}, u32[]{:S(2)}, u32[]{:S(2)}) collective-permute-start(f32[64,128]{1,0:T(8,128)S(1)} %get-tuple-element.15), channel_id=1, source_target_pairs={{0,1},{1,0},{2,3},{3,2},{4,5},{5,4},{6,7},{7,6},{8,9},{9,8},{10,11... | collective-permute-start | bytes 98312 | tf_op jit(solution)/shard_map/ppermute | solution.py:270
  37.2 1.7 %collective-permute-start.15 = (f32[64,128]{1,0:T(8,128)S(1)}, f32[64,128]{1,0:T(8,128)S(1)}, u32[]{:S(2)}, u32[]{:S(2)}) collective-permute-start(f32[64,128]{1,0:T(8,128)S(1)} %get-tuple-element.19), channel_id=1, source_target_pairs={{0,3},{1,2},{2,1},{3,0},{4,7},{5,6},{6,5},{7,4},{8,11},{9,10},{10,... | collective-permute-start | bytes 98312 | tf_op jit(solution)/shard_map/ppermute | solution.py:270
  38.9 1.4 %collective-permute-start.19 = (f32[64,128]{1,0:T(8,128)S(1)}, f32[64,128]{1,0:T(8,128)S(1)}, u32[]{:S(2)}, u32[]{:S(2)}) collective-permute-start(f32[64,128]{1,0:T(8,128)S(1)} %fusion.2), channel_id=1, source_target_pairs={{0,4},{4,0},{1,5},{5,1},{2,6},{6,2},{3,7},{7,3},{8,12},{12,8},{9,1... | collective-permute-start | bytes 98312 | tf_op jit(solution)/shard_map/ppermute | solution.py:243
  40.4 0.5 %collective-permute-done.14 = f32[64,128]{1,0:T(8,128)S(1)} collective-permute-done((f32[64,128]{1,0:T(8,128)S(1)}, f32[64,128]{1,0:T(8,128)S(1)}, u32[]{:S(2)}, u32[]{:S(2)}) %collective-permute-start.14) | collective-permute-done | bytes 32800 | tf_op jit(solution)/shard_map/ppermute | solution.py:270
  40.8 1.2 %collective-permute-done.15 = f32[64,128]{1,0:T(8,128)S(1)} collective-permute-done((f32[64,128]{1,0:T(8,128)S(1)}, f32[64,128]{1,0:T(8,128)S(1)}, u32[]{:S(2)}, u32[]{:S(2)}) %collective-permute-start.15) | collective-permute-done | bytes 32800 | tf_op jit(solution)/shard_map/ppermute | solution.py:270
  42.0 1.8 %collective-permute-done.19 = f32[64,128]{1,0:T(8,128)S(1)} collective-permute-done((f32[64,128]{1,0:T(8,128)S(1)}, f32[64,128]{1,0:T(8,128)S(1)}, u32[]{:S(2)}, u32[]{:S(2)}) %collective-permute-start.19) | collective-permute-done | bytes 32800 | tf_op jit(solution)/shard_map/ppermute | solution.py:243
  43.8 0.6 %fusion.7 = f32[128,64]{0,1:T(8,128)} fusion(f32[64,128]{1,0:T(8,128)S(1)} %collective-permute-done.19, f32[64,128]{1,0:T(8,128)S(1)} %collective-permute-done.15, f32[64,128]{1,0:T(8,128)S(1)} %collective-permute-done.14, f32[64,128]{1,0:T(8,128)S(1)} %collective-permute-done.13, f32[8,64,128]{2,1,0:T(8,128)S(1)} %combine.1), kind=kLoop, calls=%fused_computation.17 | loop fusion | flops 32768 | bytes 196608 | tf_op jit(solution)/shard_map/transpose | solution.py:323
  (33 shorter events, 1.8 us)
Async XLA Ops:
  1.7 12.2 %collective-permute-start.4 = (f32[520,128]{1,0:T(8,128)S(1)}, f32[520,128]{1,0:T(8,128)S(1)}, u32[]{:S(2)}, u32[]{:S(2)}) collective-permute-start(f32[520,128]{1,0:T(8,128)S(1)} %select_maximum_fusion.rest_4_), channel_id=1, source_target_pairs={{0,16},{8,24},{16,0},{24,8},{1,17},{9,25},{17,1},{25,9},{2,18},{10... | collective-permute-start | bytes 798728 | tf_op jit(solution)/shard_map/ppermute | solution.py:239
  4.7 11.2 %collective-permute-start.6 = (f32[520,128]{1,0:T(8,128)S(1)}, f32[520,128]{1,0:T(8,128)S(1)}, u32[]{:S(2)}, u32[]{:S(2)}) collective-permute-start(f32[520,128]{1,0:T(8,128)S(1)} %select_maximum_fusion.rest_4_), channel_id=1, source_target_pairs={{0,6},{1,7},{2,4},{3,5},{4,2},{5,3},{6,0},{7,1},{8,14},{9,15},{10,... | collective-permute-start | bytes 798728 | tf_op jit(solution)/shard_map/ppermute | solution.py:249
  8.3 20.0 %collective-permute-start.3 = (f32[520,128]{1,0:T(8,128)S(1)}, f32[520,128]{1,0:T(8,128)S(1)}, u32[]{:S(2)}, u32[]{:S(2)}) collective-permute-start(f32[520,128]{1,0:T(8,128)S(1)} %select_maximum_fusion.rest_4_), channel_id=1, source_target_pairs={{0,8},{8,0},{16,24},{24,16},{1,9},{9,1},{17,25},{25,17},{2,10},{10... | collective-permute-start | bytes 798728 | tf_op jit(solution)/shard_map/ppermute | solution.py:239
  12.3 3.6 %copy-start.1 = (f32[8,128]{1,0:T(8,128)S(1)}, f32[8,128]{1,0:T(8,128)}, u32[]{:S(2)}) copy-start(f32[8,128]{1,0:T(8,128)} %get-tuple-element.14.mark_ref) | copy-start | bytes 12292
  12.3 9.1 %collective-permute-start = (f32[520,128]{1,0:T(8,128)}, f32[520,128]{1,0:T(8,128)S(1)}, u32[]{:S(2)}, u32[]{:S(2)}) collective-permute-start(f32[520,128]{1,0:T(8,128)} %get-tuple-element.11), channel_id=1, source_target_pairs={{0,1},{1,0},{2,3},{3,2},{4,5},{5,4},{6,7},{7,6},{8,9},{9,8},{10,11... | collective-permute-start | bytes 798728 | tf_op jit(solution)/shard_map/ppermute | solution.py:316
  13.9 9.4 %collective-permute-start.1 = (f32[520,128]{1,0:T(8,128)}, f32[520,128]{1,0:T(8,128)S(1)}, u32[]{:S(2)}, u32[]{:S(2)}) collective-permute-start(f32[520,128]{1,0:T(8,128)} %get-tuple-element.12), channel_id=1, source_target_pairs={{0,2},{1,3},{2,0},{3,1},{4,6},{5,7},{6,4},{7,5},{8,10},{9,11},{10,... | collective-permute-start | bytes 798728 | tf_op jit(solution)/shard_map/ppermute | solution.py:316
  13.9 14.4 %collective-permute-start.2 = (f32[520,128]{1,0:T(8,128)}, f32[520,128]{1,0:T(8,128)S(1)}, u32[]{:S(2)}, u32[]{:S(2)}) collective-permute-start(f32[520,128]{1,0:T(8,128)} %get-tuple-element.13), channel_id=1, source_target_pairs={{0,3},{1,2},{2,1},{3,0},{4,7},{5,6},{6,5},{7,4},{8,11},{9,10},{10,... | collective-permute-start | bytes 798728 | tf_op jit(solution)/shard_map/ppermute | solution.py:316
  15.9 13.5 %copy-start = (f32[520,128]{1,0:T(8,128)S(1)}, f32[520,128]{1,0:T(8,128)}, u32[]{:S(2)}) copy-start(f32[520,128]{1,0:T(8,128)} %get-tuple-element.10.refs_0_.rest_0_) | copy-start | bytes 798724
  15.9 12.9 %collective-permute-start.10 = (f32[264,128]{1,0:T(8,128)S(1)}, f32[264,128]{1,0:T(8,128)S(1)}, u32[]{:S(2)}, u32[]{:S(2)}) collective-permute-start(f32[264,128]{1,0:T(8,128)S(1)} %slice.51.rest_9_), channel_id=1, source_target_pairs={{0,16},{8,24},{16,0},{24,8},{1,17},{9,25},{17,1},{25,9},{2,18},{10... | collective-permute-start | bytes 405512 | tf_op jit(solution)/shard_map/ppermute | solution.py:239
  21.4 7.4 %collective-permute-start.9 = (f32[256,128]{1,0:T(8,128)S(1)}, f32[256,128]{1,0:T(8,128)S(1)}, u32[]{:S(2)}, u32[]{:S(2)}) collective-permute-start(f32[256,128]{1,0:T(8,128)S(1)} %slice.50.rest_8_), channel_id=1, source_target_pairs={{0,16},{8,24},{16,0},{24,8},{1,17},{9,25},{17,1},{25,9},{2,18},{10... | collective-permute-start | bytes 393224 | tf_op jit(solution)/shard_map/ppermute | solution.py:239
  23.3 6.8 %collective-permute-start.5 = (f32[520,128]{1,0:T(8,128)S(1)}, f32[520,128]{1,0:T(8,128)S(1)}, u32[]{:S(2)}, u32[]{:S(2)}) collective-permute-start(f32[520,128]{1,0:T(8,128)S(1)} %collective-permute-done.4.next_ref.rest_6_), channel_id=1, source_target_pairs={{0,8},{8,0},{16,24},{24,16},{1,9},{9,1},{17,25},{25,17},{2,10},{10... | collective-permute-start | bytes 798728 | tf_op jit(solution)/shard_map/ppermute | solution.py:239
  28.3 1.5 %collective-permute-start.8 = (f32[264,128]{1,0:T(8,128)S(1)}, f32[264,128]{1,0:T(8,128)S(1)}, u32[]{:S(2)}, u32[]{:S(2)}) collective-permute-start(f32[264,128]{1,0:T(8,128)S(1)} %slice.51.rest_9_), channel_id=1, source_target_pairs={{0,8},{8,0},{16,24},{24,16},{1,9},{9,1},{17,25},{25,17},{2,10},{10... | collective-permute-start | bytes 405512 | tf_op jit(solution)/shard_map/ppermute | solution.py:239
  28.3 1.5 %collective-permute-start.7 = (f32[256,128]{1,0:T(8,128)S(1)}, f32[256,128]{1,0:T(8,128)S(1)}, u32[]{:S(2)}, u32[]{:S(2)}) collective-permute-start(f32[256,128]{1,0:T(8,128)S(1)} %slice.50.rest_8_), channel_id=1, source_target_pairs={{0,8},{8,0},{16,24},{24,16},{1,9},{9,1},{17,25},{25,17},{2,10},{10... | collective-permute-start | bytes 393224 | tf_op jit(solution)/shard_map/ppermute | solution.py:239
  28.8 1.3 %collective-permute-start.11 = (f32[256,128]{1,0:T(8,128)S(1)}, f32[256,128]{1,0:T(8,128)S(1)}, u32[]{:S(2)}, u32[]{:S(2)}) collective-permute-start(f32[256,128]{1,0:T(8,128)S(1)} %collective-permute-done.9.rest_12_), channel_id=1, source_target_pairs={{0,8},{8,0},{16,24},{24,16},{1,9},{9,1},{17,25},{25,17},{2,10},{10... | collective-permute-start | bytes 393224 | tf_op jit(solution)/shard_map/ppermute | solution.py:239
  28.9 1.5 %collective-permute-start.12 = (f32[264,128]{1,0:T(8,128)S(1)}, f32[264,128]{1,0:T(8,128)S(1)}, u32[]{:S(2)}, u32[]{:S(2)}) collective-permute-start(f32[264,128]{1,0:T(8,128)S(1)} %collective-permute-done.10.rest_13_), channel_id=1, source_target_pairs={{0,8},{8,0},{16,24},{24,16},{1,9},{9,1},{17,25},{25,17},{2,10},{10... | collective-permute-start | bytes 405512 | tf_op jit(solution)/shard_map/ppermute | solution.py:239
  31.9 5.3 %collective-permute-start.16 = (f32[64,128]{1,0:T(8,128)S(1)}, f32[64,128]{1,0:T(8,128)S(1)}, u32[]{:S(2)}, u32[]{:S(2)}) collective-permute-start(f32[64,128]{1,0:T(8,128)S(1)} %get-tuple-element.18), channel_id=1, source_target_pairs={{0,1},{1,0},{2,3},{3,2},{4,5},{5,4},{6,7},{7,6},{8,9},{9,8},{10,11... | collective-permute-start | bytes 98312 | tf_op jit(solution)/shard_map/ppermute | solution.py:270
  33.4 5.5 %collective-permute-start.17 = (f32[64,128]{1,0:T(8,128)S(1)}, f32[64,128]{1,0:T(8,128)S(1)}, u32[]{:S(2)}, u32[]{:S(2)}) collective-permute-start(f32[64,128]{1,0:T(8,128)S(1)} %get-tuple-element.17), channel_id=1, source_target_pairs={{0,2},{1,3},{2,0},{3,1},{4,6},{5,7},{6,4},{7,5},{8,10},{9,11},{10,... | collective-permute-start | bytes 98312 | tf_op jit(solution)/shard_map/ppermute | solution.py:270
  33.7 5.2 %collective-permute-start.18 = (f32[64,128]{1,0:T(8,128)S(1)}, f32[64,128]{1,0:T(8,128)S(1)}, u32[]{:S(2)}, u32[]{:S(2)}) collective-permute-start(f32[64,128]{1,0:T(8,128)S(1)} %get-tuple-element.16), channel_id=1, source_target_pairs={{0,3},{1,2},{2,1},{3,0},{4,7},{5,6},{6,5},{7,4},{8,11},{9,10},{10,... | collective-permute-start | bytes 98312 | tf_op jit(solution)/shard_map/ppermute | solution.py:270
  35.4 5.0 %collective-permute-start.13 = (f32[64,128]{1,0:T(8,128)S(1)}, f32[64,128]{1,0:T(8,128)S(1)}, u32[]{:S(2)}, u32[]{:S(2)}) collective-permute-start(f32[64,128]{1,0:T(8,128)S(1)} %get-tuple-element.15), channel_id=1, source_target_pairs={{0,1},{1,0},{2,3},{3,2},{4,5},{5,4},{6,7},{7,6},{8,9},{9,8},{10,11... | collective-permute-start | bytes 98312 | tf_op jit(solution)/shard_map/ppermute | solution.py:270
  36.9 3.9 %collective-permute-start.14 = (f32[64,128]{1,0:T(8,128)S(1)}, f32[64,128]{1,0:T(8,128)S(1)}, u32[]{:S(2)}, u32[]{:S(2)}) collective-permute-start(f32[64,128]{1,0:T(8,128)S(1)} %get-tuple-element.20), channel_id=1, source_target_pairs={{0,2},{1,3},{2,0},{3,1},{4,6},{5,7},{6,4},{7,5},{8,10},{9,11},{10,... | collective-permute-start | bytes 98312 | tf_op jit(solution)/shard_map/ppermute | solution.py:270
  37.2 4.8 %collective-permute-start.15 = (f32[64,128]{1,0:T(8,128)S(1)}, f32[64,128]{1,0:T(8,128)S(1)}, u32[]{:S(2)}, u32[]{:S(2)}) collective-permute-start(f32[64,128]{1,0:T(8,128)S(1)} %get-tuple-element.19), channel_id=1, source_target_pairs={{0,3},{1,2},{2,1},{3,0},{4,7},{5,6},{6,5},{7,4},{8,11},{9,10},{10,... | collective-permute-start | bytes 98312 | tf_op jit(solution)/shard_map/ppermute | solution.py:270
  38.9 4.9 %collective-permute-start.19 = (f32[64,128]{1,0:T(8,128)S(1)}, f32[64,128]{1,0:T(8,128)S(1)}, u32[]{:S(2)}, u32[]{:S(2)}) collective-permute-start(f32[64,128]{1,0:T(8,128)S(1)} %fusion.2), channel_id=1, source_target_pairs={{0,4},{4,0},{1,5},{5,1},{2,6},{6,2},{3,7},{7,3},{8,12},{12,8},{9,1... | collective-permute-start | bytes 98312 | tf_op jit(solution)/shard_map/ppermute | solution.py:243

commit v30 on v22

--- a/solution.py
+++ b/solution.py
@@ -29,7 +29,7 @@
     return both[:, :width] + both[:, width:]
 
 
-def append_kernel(next_ref, far_columns_ref, own_columns_ref, blocks_ref, out_ref):
+def append_kernel(far_columns_ref, own_columns_ref, blocks_ref, out_ref):
     used = blocks_ref.shape[0]
     entries, fine_rows = own_columns_ref.shape
     out_ref[:used] = blocks_ref[...]
@@ -38,17 +38,33 @@
     out_ref[used + entries : used + 2 * entries, :fine_rows] = own_columns_ref[...].astype(jnp.float32)
 
 
-def append_columns(next_blocks, far_columns, own_columns, blocks):
+def append_columns(far_columns, own_columns, blocks):
     used, width = blocks.shape
     return pl.pallas_call(
         append_kernel,
         out_shape=jax.ShapeDtypeStruct((used + EXTRA, width), blocks.dtype),
-        in_specs=[pl.BlockSpec(memory_space=pltpu.VMEM)] * 4,
+        in_specs=[pl.BlockSpec(memory_space=pltpu.VMEM)] * 3,
         out_specs=pl.BlockSpec(memory_space=pltpu.VMEM),
         compiler_params=pltpu.CompilerParams(vmem_limit_bytes=VMEM_LIMIT),
         cost_estimate=pl.CostEstimate(flops=HOLD_FLOPS, bytes_accessed=HOLD_FLOPS >> 8, transcendentals=0),
         name="append_columns",
-    )(next_blocks, far_columns, own_columns, blocks)
+    )(far_columns, own_columns, blocks)
+
+
+def hold_kernel(next_ref, blocks_ref, out_ref):
+    out_ref[...] = blocks_ref[...]
+
+
+def hold_until(next_blocks, blocks):
+    return pl.pallas_call(
+        hold_kernel,
+        out_shape=jax.ShapeDtypeStruct(blocks.shape, blocks.dtype),
+        in_specs=[pl.BlockSpec(memory_space=pltpu.VMEM)] * 2,
+        out_specs=pl.BlockSpec(memory_space=pltpu.VMEM),
+        compiler_params=pltpu.CompilerParams(vmem_limit_bytes=VMEM_LIMIT),
+        cost_estimate=pl.CostEstimate(flops=0, bytes_accessed=1 << 19, transcendentals=0),
+        name="hold_until",
+    )(next_blocks, blocks)
 
 
 def restrict_kernel(
@@ -275,7 +291,8 @@
     restricted = lax.all_to_all(restricted, "near", split_axis=0, concat_axis=0, tiled=True)
     far_columns = far_swap(own_columns)
     near_pieces = spread_over_rows(near_blocks, rows)
-    far_blocks = append_columns(near_pieces[rows // 2], far_columns, own_columns, far_blocks)
+    far_blocks = append_columns(far_columns, own_columns, far_blocks)
+    far_blocks = hold_until(near_pieces[rows // 2], far_blocks)
     pieces = near_pieces + spread_over_rows(far_blocks, rows)
     sums = combine(own, restricted, pieces, NCR * rows, slot_count, fine_rows, block_size)
     return add_over_columns(sums, half).T

time: 41.9 us -> 48.5 us (1.16)
  waiting for transfers between devices: 13.3 us -> 19.7 us
    ppermute x2, waiting for transfers between devices: 1.69 us -> 10.2 us  [far_swap(): return lax.ppermute(x, ('half', 'near'), pairs)]
    all_to_all x1, waiting for transfers between devices: 1.37 us -> 0.01 us  [local(): lax.all_to_all(restricted, 'near', split_axis=0, concat_axis=0, tiled=True)]
    ppermute x6, waiting for transfers between devices: 7.99 us -> 6.8 us  [row_swap(): lax.ppermute(x, 'row', [(r, r ^ bit) for r in range(lax.axis_size('row'))])]
    ppermute x2, starting transfers between devices: 5.27 us -> 5.96 us  [far_swap(): return lax.ppermute(x, ('half', 'near'), pairs)]
    ppermute x1, waiting for transfers between devices: 1.6 us -> 2.1 us  [half_swap(): return lax.ppermute(x, 'half', [(0, 1), (1, 0)])]
  transfers between devices with their start and end apart: 16 -> 16, of which waited for: 9 -> 6; matrix products, arithmetic and copies ran while one was open for 0% -> 0% of each run, Pallas kernels for 8% -> 7%
where the time goes in v30:
time: 48.5 us; the launch traced here: 48.3 us
  starting transfers between devices  22.5 us (46%)
  waiting for transfers between devices  19.7 us (41%)
  Pallas kernels  5.28 us (11%)
  other arithmetic  0.72 us (1%)
    ppermute x2, waiting for transfers between devices, far_swap(): return lax.ppermute(x, ('half', 'near'), pairs)  10.2 us
    ppermute x6, starting transfers between devices, add_over_near(): lax.ppermute(sums[near], 'near', [(n, n ^ near) for n in range(half)])  7.03 us
    ppermute x6, waiting for transfers between devices, row_swap(): lax.ppermute(x, 'row', [(r, r ^ bit) for r in range(lax.axis_size('row'))])  6.8 us
    ppermute x2, starting transfers between devices, far_swap(): return lax.ppermute(x, ('half', 'near'), pairs)  5.96 us
    all_to_all x1, starting transfers between devices, local(): lax.all_to_all(restricted, 'near', split_axis=0, concat_axis=0, tiled=True)  3.66 us
    ppermute x6, starting transfers between devices, row_swap(): lax.ppermute(x, 'row', [(r, r ^ bit) for r in range(lax.axis_size('row'))])  3.62 us
    pallas_call x1, Pallas kernels, restrict_operator(): pl.pallas_call(restrict_kernel, out_shape=(jax.ShapeDtypeStruct((columns...  3.49 us
    ppermute x1, starting transfers between devices, half_swap(): return lax.ppermute(x, 'half', [(0, 1), (1, 0)])  2.19 us
  transfers between devices with their start and end apart: 16, of which 6 were waited for; matrix products, arithmetic and copies ran while one was open for 0% of the time, Pallas kernels for 7%

profile of v30, /device:TPU:0, one launch (start us, length us, event | category | flops | bytes accessed | tf_op | source)
XLA Modules:
  0.0 48.3 jit_solution(12738910702962245534)
XLA Ops:
  0.0 5.0 %collective-permute-start.4 = (f32[512,128]{1,0:T(8,128)}, f32[512,128]{1,0:T(8,128)S(1)}, u32[]{:S(2)}, u32[]{:S(2)}) collective-permute-start(f32[512,128]{1,0:T(8,128)} %bitcast.44), channel_id=1, source_target_pairs={{0,6},{1,7},{2,4},{3,5},{4,2},{5,3},{6,0},{7,1},{8,14},{9,15},{10,... | collective-permute-start | bytes 786440 | tf_op jit(solution)/shard_map/ppermute | solution.py:231
  5.0 3.5 %restrict_operator.1 = (f32[4,520,128]{2,1,0:T(8,128)}, s32[2,8]{1,0:T(2,128)}, f32[512,128]{1,0:T(8,128)}) custom-call(s32[8]{0:T(128)} %count_any.1, s32[8,8]{1,0:T(8,128)} %slot_any.1, s32[2,8]{1,0:T(2,128)} %bitcast.47, s32[4,8]{1,0:T(4,128)} %bitcast.46, f32[8,64,128]{2,1,0:T(8,128)} %restrict_any.1, f32[8,64,512]{2,1,0:T(8,128)} %operator_any.1, ...), custom_call_target="tpu_custom_call" | custom-call | flops 201326592 | bytes 4194304 | tf_op jit(solution)/shard_map/restrict_operator/pallas_call | solution.py:137
  8.5 0.0 copy-start.1
  8.6 3.7 %all-to-all-start = ((f32[4,520,128]{2,1,0:T(8,128)}), f32[4,520,128]{2,1,0:T(8,128)S(1)}, u32[]{:S(2)}, u32[]{:S(2)}) async-start(f32[4,520,128]{2,1,0:T(8,128)} %get-tuple-element.8), calls=%async_computation | async-start | bytes 2129920 | tf_op jit(solution)/shard_map/all_to_all | solution.py:291
  12.2 0.9 %collective-permute-start.3 = (s32[2,8]{1,0:T(2,128)S(1)}, s32[2,8]{1,0:T(2,128)S(1)}, u32[]{:S(2)}, u32[]{:S(2)}) collective-permute-start(s32[2,8]{1,0:T(2,128)S(1)} %copy-done.1), channel_id=1, source_target_pairs={{0,6},{1,7},{2,4},{3,5},{4,2},{5,3},{6,0},{7,1},{8,14},{9,15},{10,... | collective-permute-start | bytes 200 | tf_op jit(solution)/shard_map/ppermute | solution.py:231
  13.2 1.5 %collective-permute-start.1 = (f32[512,128]{1,0:T(8,128)S(1)}, f32[512,128]{1,0:T(8,128)S(1)}, u32[]{:S(2)}, u32[]{:S(2)}) collective-permute-start(f32[512,128]{1,0:T(8,128)S(1)} %copy-done), channel_id=1, source_target_pairs={{0,16},{8,24},{16,0},{24,8},{1,17},{9,25},{17,1},{25,9},{2,18},{10... | collective-permute-start | bytes 786440 | tf_op jit(solution)/shard_map/ppermute | solution.py:221
  14.7 10.2 %collective-permute-done.3.far_columns_ref = s32[2,8]{1,0:T(2,128)S(1)} collective-permute-done((s32[2,8]{1,0:T(2,128)S(1)}, s32[2,8]{1,0:T(2,128)S(1)}, u32[]{:S(2)}, u32[]{:S(2)}) %collective-permute-start.3) | collective-permute-done | bytes 96 | tf_op jit(solution)/shard_map/ppermute | solution.py:231
  25.0 1.6 %collective-permute-start.6 = (f32[520,128]{1,0:T(8,128)S(1)}, f32[520,128]{1,0:T(8,128)S(1)}, u32[]{:S(2)}, u32[]{:S(2)}) collective-permute-start(f32[520,128]{1,0:T(8,128)S(1)} %hold_until.1.rest_4_), channel_id=1, source_target_pairs={{0,16},{8,24},{16,0},{24,8},{1,17},{9,25},{17,1},{25,9},{2,18},{10... | collective-permute-start | bytes 798728 | tf_op jit(solution)/shard_map/ppermute | solution.py:221
  26.6 5.1 %collective-permute-done.6.rest_6_ = f32[520,128]{1,0:T(8,128)S(1)} collective-permute-done((f32[520,128]{1,0:T(8,128)S(1)}, f32[520,128]{1,0:T(8,128)S(1)}, u32[]{:S(2)}, u32[]{:S(2)}) %collective-permute-start.6) | collective-permute-done | bytes 266272 | tf_op jit(solution)/shard_map/ppermute | solution.py:221
  31.7 0.5 %collective-permute-start = (f32[512,128]{1,0:T(8,128)S(1)}, f32[512,128]{1,0:T(8,128)S(1)}, u32[]{:S(2)}, u32[]{:S(2)}) collective-permute-start(f32[512,128]{1,0:T(8,128)S(1)} %copy-done), channel_id=1, source_target_pairs={{0,8},{8,0},{16,24},{24,16},{1,9},{9,1},{17,25},{25,17},{2,10},{10... | collective-permute-start | bytes 786440 | tf_op jit(solution)/shard_map/ppermute | solution.py:221
  32.2 0.1 add_bitcast_fusion.own_ref
  32.3 1.3 %collective-permute-done.rest_1_ = f32[512,128]{1,0:T(8,128)S(1)} collective-permute-done((f32[512,128]{1,0:T(8,128)S(1)}, f32[512,128]{1,0:T(8,128)S(1)}, u32[]{:S(2)}, u32[]{:S(2)}) %collective-permute-start) | collective-permute-done | bytes 262176 | tf_op jit(solution)/shard_map/ppermute | solution.py:221
  33.6 0.4 collective-permute-done.2.rest_3_
  34.0 1.8 %combine.1 = f32[8,64,128]{2,1,0:T(8,128)S(1)} custom-call(s32[1,10]{1,0:T(1,128)S(1)} %add_bitcast_fusion.own_ref, f32[4,520,128]{2,1,0:T(8,128)S(1)} %all-to-all-done.restricted_ref, f32[512,128]{1,0:T(8,128)S(1)} %copy-done, f32[512,128]{1,0:T(8,128)S(1)} %collective-permute-done.rest_1_, f32[512,128]{1,0:T(8,128)S(1)} %collective-permute-done.1.next_ref.rest_2_, ...), custom_call_target="tpu_custom_call" | custom-call | flops 268435456 | bytes 4194304 | tf_op jit(solution)/shard_map/combine/pallas_call | solution.py:203
  35.7 0.1 collective-permute-start.13
  35.8 2.9 %collective-permute-start.12 = (f32[64,128]{1,0:T(8,128)S(1)}, f32[64,128]{1,0:T(8,128)S(1)}, u32[]{:S(2)}, u32[]{:S(2)}) collective-permute-start(f32[64,128]{1,0:T(8,128)S(1)} %get-tuple-element.13), channel_id=1, source_target_pairs={{0,2},{1,3},{2,0},{3,1},{4,6},{5,7},{6,4},{7,5},{8,10},{9,11},{10,... | collective-permute-start | bytes 98312 | tf_op jit(solution)/shard_map/ppermute | solution.py:252
  38.7 0.6 %collective-permute-start.11 = (f32[64,128]{1,0:T(8,128)S(1)}, f32[64,128]{1,0:T(8,128)S(1)}, u32[]{:S(2)}, u32[]{:S(2)}) collective-permute-start(f32[64,128]{1,0:T(8,128)S(1)} %get-tuple-element.14), channel_id=1, source_target_pairs={{0,1},{1,0},{2,3},{3,2},{4,5},{5,4},{6,7},{7,6},{8,9},{9,8},{10,11... | collective-permute-start | bytes 98312 | tf_op jit(solution)/shard_map/ppermute | solution.py:252
  39.3 1.5 %collective-permute-start.8 = (f32[64,128]{1,0:T(8,128)S(1)}, f32[64,128]{1,0:T(8,128)S(1)}, u32[]{:S(2)}, u32[]{:S(2)}) collective-permute-start(f32[64,128]{1,0:T(8,128)S(1)} %get-tuple-element.11), channel_id=1, source_target_pairs={{0,1},{1,0},{2,3},{3,2},{4,5},{5,4},{6,7},{7,6},{8,9},{9,8},{10,11... | collective-permute-start | bytes 98312 | tf_op jit(solution)/shard_map/ppermute | solution.py:252
  40.8 0.1 collective-permute-start.10
  40.9 1.9 %collective-permute-start.9 = (f32[64,128]{1,0:T(8,128)S(1)}, f32[64,128]{1,0:T(8,128)S(1)}, u32[]{:S(2)}, u32[]{:S(2)}) collective-permute-start(f32[64,128]{1,0:T(8,128)S(1)} %get-tuple-element.16), channel_id=1, source_target_pairs={{0,2},{1,3},{2,0},{3,1},{4,6},{5,7},{6,4},{7,5},{8,10},{9,11},{10,... | collective-permute-start | bytes 98312 | tf_op jit(solution)/shard_map/ppermute | solution.py:252
  42.8 2.2 %collective-permute-start.14 = (f32[64,128]{1,0:T(8,128)S(1)}, f32[64,128]{1,0:T(8,128)S(1)}, u32[]{:S(2)}, u32[]{:S(2)}) collective-permute-start(f32[64,128]{1,0:T(8,128)S(1)} %fusion.2), channel_id=1, source_target_pairs={{0,4},{4,0},{1,5},{5,1},{2,6},{6,2},{3,7},{7,3},{8,12},{12,8},{9,1... | collective-permute-start | bytes 98312 | tf_op jit(solution)/shard_map/ppermute | solution.py:225
  45.0 0.6 %collective-permute-done.10 = f32[64,128]{1,0:T(8,128)S(1)} collective-permute-done((f32[64,128]{1,0:T(8,128)S(1)}, f32[64,128]{1,0:T(8,128)S(1)}, u32[]{:S(2)}, u32[]{:S(2)}) %collective-permute-start.10) | collective-permute-done | bytes 32800 | tf_op jit(solution)/shard_map/ppermute | solution.py:252
  45.6 2.1 %collective-permute-done.14 = f32[64,128]{1,0:T(8,128)S(1)} collective-permute-done((f32[64,128]{1,0:T(8,128)S(1)}, f32[64,128]{1,0:T(8,128)S(1)}, u32[]{:S(2)}, u32[]{:S(2)}) %collective-permute-start.14) | collective-permute-done | bytes 32800 | tf_op jit(solution)/shard_map/ppermute | solution.py:225
  47.7 0.6 %fusion.7 = f32[128,64]{0,1:T(8,128)} fusion(f32[64,128]{1,0:T(8,128)S(1)} %collective-permute-done.14, f32[64,128]{1,0:T(8,128)S(1)} %collective-permute-done.10, f32[64,128]{1,0:T(8,128)S(1)} %collective-permute-done.9, f32[64,128]{1,0:T(8,128)S(1)} %collective-permute-done.8, f32[8,64,128]{2,1,0:T(8,128)S(1)} %combine.1), kind=kLoop, calls=%fused_computation.15 | loop fusion | flops 32768 | bytes 196608 | tf_op jit(solution)/shard_map/transpose | solution.py:298
  (21 shorter events, 0.1 us)
Async XLA Ops:
  0.0 24.9 %collective-permute-start.4 = (f32[512,128]{1,0:T(8,128)}, f32[512,128]{1,0:T(8,128)S(1)}, u32[]{:S(2)}, u32[]{:S(2)}) collective-permute-start(f32[512,128]{1,0:T(8,128)} %bitcast.44), channel_id=1, source_target_pairs={{0,6},{1,7},{2,4},{3,5},{4,2},{5,3},{6,0},{7,1},{8,14},{9,15},{10,... | collective-permute-start | bytes 786440 | tf_op jit(solution)/shard_map/ppermute | solution.py:231
  8.5 3.7 %copy-start.1 = (s32[2,8]{1,0:T(2,128)S(1)}, s32[2,8]{1,0:T(2,128)}, u32[]{:S(2)}) copy-start(s32[2,8]{1,0:T(2,128)} %get-tuple-element.10.own_columns_ref) | copy-start | bytes 196
  8.6 4.6 %copy-start = (f32[512,128]{1,0:T(8,128)S(1)}, f32[512,128]{1,0:T(8,128)}, u32[]{:S(2)}) copy-start(f32[512,128]{1,0:T(8,128)} %get-tuple-element.9.rest_0_) | copy-start | bytes 786436
  8.6 25.4 %all-to-all-start = ((f32[4,520,128]{2,1,0:T(8,128)}), f32[4,520,128]{2,1,0:T(8,128)S(1)}, u32[]{:S(2)}, u32[]{:S(2)}) async-start(f32[4,520,128]{2,1,0:T(8,128)} %get-tuple-element.8), calls=%async_computation | async-start | bytes 2129920 | tf_op jit(solution)/shard_map/all_to_all | solution.py:291
  12.2 12.7 %collective-permute-start.3 = (s32[2,8]{1,0:T(2,128)S(1)}, s32[2,8]{1,0:T(2,128)S(1)}, u32[]{:S(2)}, u32[]{:S(2)}) collective-permute-start(s32[2,8]{1,0:T(2,128)S(1)} %copy-done.1), channel_id=1, source_target_pairs={{0,6},{1,7},{2,4},{3,5},{4,2},{5,3},{6,0},{7,1},{8,14},{9,15},{10,... | collective-permute-start | bytes 200 | tf_op jit(solution)/shard_map/ppermute | solution.py:231
  13.2 11.8 %collective-permute-start.1 = (f32[512,128]{1,0:T(8,128)S(1)}, f32[512,128]{1,0:T(8,128)S(1)}, u32[]{:S(2)}, u32[]{:S(2)}) collective-permute-start(f32[512,128]{1,0:T(8,128)S(1)} %copy-done), channel_id=1, source_target_pairs={{0,16},{8,24},{16,0},{24,8},{1,17},{9,25},{17,1},{25,9},{2,18},{10... | collective-permute-start | bytes 786440 | tf_op jit(solution)/shard_map/ppermute | solution.py:221
  25.0 6.7 %collective-permute-start.6 = (f32[520,128]{1,0:T(8,128)S(1)}, f32[520,128]{1,0:T(8,128)S(1)}, u32[]{:S(2)}, u32[]{:S(2)}) collective-permute-start(f32[520,128]{1,0:T(8,128)S(1)} %hold_until.1.rest_4_), channel_id=1, source_target_pairs={{0,16},{8,24},{16,0},{24,8},{1,17},{9,25},{17,1},{25,9},{2,18},{10... | collective-permute-start | bytes 798728 | tf_op jit(solution)/shard_map/ppermute | solution.py:221
  26.6 7.4 %collective-permute-start.5 = (f32[520,128]{1,0:T(8,128)S(1)}, f32[520,128]{1,0:T(8,128)S(1)}, u32[]{:S(2)}, u32[]{:S(2)}) collective-permute-start(f32[520,128]{1,0:T(8,128)S(1)} %hold_until.1.rest_4_), channel_id=1, source_target_pairs={{0,8},{8,0},{16,24},{24,16},{1,9},{9,1},{17,25},{25,17},{2,10},{10... | collective-permute-start | bytes 798728 | tf_op jit(solution)/shard_map/ppermute | solution.py:221
  31.7 2.3 %collective-permute-start.7 = (f32[520,128]{1,0:T(8,128)S(1)}, f32[520,128]{1,0:T(8,128)S(1)}, u32[]{:S(2)}, u32[]{:S(2)}) collective-permute-start(f32[520,128]{1,0:T(8,128)S(1)} %collective-permute-done.6.rest_6_), channel_id=1, source_target_pairs={{0,8},{8,0},{16,24},{24,16},{1,9},{9,1},{17,25},{25,17},{2,10},{10... | collective-permute-start | bytes 798728 | tf_op jit(solution)/shard_map/ppermute | solution.py:221
  31.7 1.9 %collective-permute-start = (f32[512,128]{1,0:T(8,128)S(1)}, f32[512,128]{1,0:T(8,128)S(1)}, u32[]{:S(2)}, u32[]{:S(2)}) collective-permute-start(f32[512,128]{1,0:T(8,128)S(1)} %copy-done), channel_id=1, source_target_pairs={{0,8},{8,0},{16,24},{24,16},{1,9},{9,1},{17,25},{25,17},{2,10},{10... | collective-permute-start | bytes 786440 | tf_op jit(solution)/shard_map/ppermute | solution.py:221
  32.2 1.8 %collective-permute-start.2 = (f32[512,128]{1,0:T(8,128)S(1)}, f32[512,128]{1,0:T(8,128)S(1)}, u32[]{:S(2)}, u32[]{:S(2)}) collective-permute-start(f32[512,128]{1,0:T(8,128)S(1)} %collective-permute-done.1.next_ref.rest_2_), channel_id=1, source_target_pairs={{0,8},{8,0},{16,24},{24,16},{1,9},{9,1},{17,25},{25,17},{2,10},{10... | collective-permute-start | bytes 786440 | tf_op jit(solution)/shard_map/ppermute | solution.py:221
  35.7 5.1 %collective-permute-start.13 = (f32[64,128]{1,0:T(8,128)S(1)}, f32[64,128]{1,0:T(8,128)S(1)}, u32[]{:S(2)}, u32[]{:S(2)}) collective-permute-start(f32[64,128]{1,0:T(8,128)S(1)} %get-tuple-element.12), channel_id=1, source_target_pairs={{0,3},{1,2},{2,1},{3,0},{4,7},{5,6},{6,5},{7,4},{8,11},{9,10},{10,... | collective-permute-start | bytes 98312 | tf_op jit(solution)/shard_map/ppermute | solution.py:252
  35.8 7.0 %collective-permute-start.12 = (f32[64,128]{1,0:T(8,128)S(1)}, f32[64,128]{1,0:T(8,128)S(1)}, u32[]{:S(2)}, u32[]{:S(2)}) collective-permute-start(f32[64,128]{1,0:T(8,128)S(1)} %get-tuple-element.13), channel_id=1, source_target_pairs={{0,2},{1,3},{2,0},{3,1},{4,6},{5,7},{6,4},{7,5},{8,10},{9,11},{10,... | collective-permute-start | bytes 98312 | tf_op jit(solution)/shard_map/ppermute | solution.py:252
  38.7 4.1 %collective-permute-start.11 = (f32[64,128]{1,0:T(8,128)S(1)}, f32[64,128]{1,0:T(8,128)S(1)}, u32[]{:S(2)}, u32[]{:S(2)}) collective-permute-start(f32[64,128]{1,0:T(8,128)S(1)} %get-tuple-element.14), channel_id=1, source_target_pairs={{0,1},{1,0},{2,3},{3,2},{4,5},{5,4},{6,7},{7,6},{8,9},{9,8},{10,11... | collective-permute-start | bytes 98312 | tf_op jit(solution)/shard_map/ppermute | solution.py:252
  39.3 5.7 %collective-permute-start.8 = (f32[64,128]{1,0:T(8,128)S(1)}, f32[64,128]{1,0:T(8,128)S(1)}, u32[]{:S(2)}, u32[]{:S(2)}) collective-permute-start(f32[64,128]{1,0:T(8,128)S(1)} %get-tuple-element.11), channel_id=1, source_target_pairs={{0,1},{1,0},{2,3},{3,2},{4,5},{5,4},{6,7},{7,6},{8,9},{9,8},{10,11... | collective-permute-start | bytes 98312 | tf_op jit(solution)/shard_map/ppermute | solution.py:252
  40.8 4.8 %collective-permute-start.10 = (f32[64,128]{1,0:T(8,128)S(1)}, f32[64,128]{1,0:T(8,128)S(1)}, u32[]{:S(2)}, u32[]{:S(2)}) collective-permute-start(f32[64,128]{1,0:T(8,128)S(1)} %get-tuple-element.15), channel_id=1, source_target_pairs={{0,3},{1,2},{2,1},{3,0},{4,7},{5,6},{6,5},{7,4},{8,11},{9,10},{10,... | collective-permute-start | bytes 98312 | tf_op jit(solution)/shard_map/ppermute | solution.py:252
  40.9 4.7 %collective-permute-start.9 = (f32[64,128]{1,0:T(8,128)S(1)}, f32[64,128]{1,0:T(8,128)S(1)}, u32[]{:S(2)}, u32[]{:S(2)}) collective-permute-start(f32[64,128]{1,0:T(8,128)S(1)} %get-tuple-element.16), channel_id=1, source_target_pairs={{0,2},{1,3},{2,0},{3,1},{4,6},{5,7},{6,4},{7,5},{8,10},{9,11},{10,... | collective-permute-start | bytes 98312 | tf_op jit(solution)/shard_map/ppermute | solution.py:252
  42.8 4.9 %collective-permute-start.14 = (f32[64,128]{1,0:T(8,128)S(1)}, f32[64,128]{1,0:T(8,128)S(1)}, u32[]{:S(2)}, u32[]{:S(2)}) collective-permute-start(f32[64,128]{1,0:T(8,128)S(1)} %fusion.2), channel_id=1, source_target_pairs={{0,4},{4,0},{1,5},{5,1},{2,6},{6,2},{3,7},{7,3},{8,12},{12,8},{9,1... | collective-permute-start | bytes 98312 | tf_op jit(solution)/shard_map/ppermute | solution.py:225

commit v31 on v22

--- a/solution.py
+++ b/solution.py
@@ -29,31 +29,25 @@
     return both[:, :width] + both[:, width:]
 
 
-def append_kernel(next_ref, far_columns_ref, own_columns_ref, blocks_ref, out_ref):
-    used = blocks_ref.shape[0]
-    entries, fine_rows = own_columns_ref.shape
-    out_ref[:used] = blocks_ref[...]
-    out_ref[used:] = jnp.zeros((EXTRA, out_ref.shape[1]), jnp.float32)
-    out_ref[used : used + entries, :fine_rows] = far_columns_ref[...].astype(jnp.float32)
-    out_ref[used + entries : used + 2 * entries, :fine_rows] = own_columns_ref[...].astype(jnp.float32)
-
-
-def append_columns(next_blocks, far_columns, own_columns, blocks):
-    used, width = blocks.shape
+def hold_kernel(mark_ref, next_ref, blocks_ref, out_ref):
+    out_ref[...] = blocks_ref[...]
+
+
+def hold_until(mark, next_blocks, blocks):
     return pl.pallas_call(
-        append_kernel,
-        out_shape=jax.ShapeDtypeStruct((used + EXTRA, width), blocks.dtype),
-        in_specs=[pl.BlockSpec(memory_space=pltpu.VMEM)] * 4,
+        hold_kernel,
+        out_shape=jax.ShapeDtypeStruct(blocks.shape, blocks.dtype),
+        in_specs=[pl.BlockSpec(memory_space=pltpu.VMEM)] * 3,
         out_specs=pl.BlockSpec(memory_space=pltpu.VMEM),
         compiler_params=pltpu.CompilerParams(vmem_limit_bytes=VMEM_LIMIT),
         cost_estimate=pl.CostEstimate(flops=HOLD_FLOPS, bytes_accessed=HOLD_FLOPS >> 8, transcendentals=0),
-        name="append_columns",
-    )(next_blocks, far_columns, own_columns, blocks)
+        name="hold_until",
+    )(mark, next_blocks, blocks)
 
 
 def restrict_kernel(
-    count_any, slot_any, rows_any, fetch_any, restrict_any, operator_any, columns_any, blocks_any, side_any,
-    out_ref, own_columns_ref, own_blocks_ref,
+    count_any, slot_any, rows_any, fetch_any, restrict_any, operator_any, side_any,
+    out_ref, mark_ref,
     count_ref, slot_ref, rows_ref, fetch_ref, side_ref, restrict_ref, operator_ref, sems, operator_sems,
 ):
     fine_rows, block_size, _ = operator_ref.shape
@@ -66,7 +60,7 @@
     pairs = [
         (count_any, count_ref), (slot_any, slot_ref), (rows_any, rows_ref),
         (fetch_any, fetch_ref), (restrict_any, restrict_ref),
-        (columns_any, own_columns_ref), (blocks_any, own_blocks_ref), (side_any, side_ref),
+        (side_any, side_ref),
     ]
     copies = [pltpu.make_async_copy(a, b, sems.at[i]) for i, (a, b) in enumerate(pairs)]
     operators = [
@@ -91,6 +85,7 @@
                 wanted = fetch_ref[s, side * half + turned]
                 value = jnp.where(short_lane == side * slot_count + s, wanted, value)
         out_ref[near, used:] = value.astype(jnp.float32)
+    mark_ref[...] = out_ref[0, used:]
 
     for i in range(fine_rows):
         value = restrict_ref[i]
@@ -110,7 +105,7 @@
 
 
 def restrict_operator(
-    operator_count, operator_slot, restrict_rows, fetch, operator_blocks, restrict_blocks, own_columns, own_blocks, side
+    operator_count, operator_slot, restrict_rows, fetch, operator_blocks, restrict_blocks, side
 ):
     fine_rows, block_size, width = operator_blocks.shape
     slot_count, columns = fetch.shape
@@ -122,19 +117,18 @@
         restrict_kernel,
         out_shape=(
             jax.ShapeDtypeStruct((columns // 2, rows, wide), jnp.float32),
-            jax.ShapeDtypeStruct(own_columns.shape, own_columns.dtype),
-            jax.ShapeDtypeStruct(own_blocks.shape, own_blocks.dtype),
+            jax.ShapeDtypeStruct((EXTRA, wide), jnp.float32),
         ),
-        in_specs=[pl.BlockSpec(memory_space=pltpu.HBM)] * 9,
-        out_specs=[pl.BlockSpec(memory_space=pltpu.VMEM)] * 3,
+        in_specs=[pl.BlockSpec(memory_space=pltpu.HBM)] * 7,
+        out_specs=[pl.BlockSpec(memory_space=pltpu.VMEM)] * 2,
         scratch_shapes=[pltpu.SMEM(x.shape, x.dtype) for x in kept]
         + [pltpu.VMEM(x.shape, x.dtype) for x in (restrict_blocks, operator_blocks)]
-        + [pltpu.SemaphoreType.DMA((8,)), pltpu.SemaphoreType.DMA((fine_rows,))],
+        + [pltpu.SemaphoreType.DMA((6,)), pltpu.SemaphoreType.DMA((fine_rows,))],
         cost_estimate=pl.CostEstimate(
             flops=6 * fine_rows * block_size * width * wide, bytes_accessed=4 << 20, transcendentals=0
         ),
         name="restrict_operator",
-    )(*small, restrict_blocks, operator_blocks, own_columns, own_blocks, side)
+    )(*small, restrict_blocks, operator_blocks, side)
 
 
 def combine_kernel(own_ref, restricted_ref, *rest, slot_count, fine_rows, entries):
@@ -149,15 +143,13 @@
     table_ref[:1, : own_ref.shape[1]] = own_ref[...]
     for near in range(half):
         table_ref[1 + near : 2 + near] = restricted_ref[near, used : used + 1].astype(jnp.int32)
-    for i, piece in enumerate(pieces[rows:]):
-        for far in range(2):
-            first = 1 + half + entries * (far * rows + i)
-            row = held + entries * (1 - far)
-            table_ref[first : first + entries] = piece[row : row + entries].astype(jnp.int32)
+    for i, piece in enumerate(pieces):
+        first = 1 + half + entries * i
+        table_ref[first : first + entries] = piece[held : held + entries].astype(jnp.int32)
     copy = pltpu.make_async_copy(table_ref, index_ref, sem)
     copy.start()
     for i, piece in enumerate(pieces):
-        held_ref[i] = piece[...] if i < rows else piece[:held]
+        held_ref[i] = piece[:held]
     out_ref[...] = jnp.zeros_like(out_ref)
     copy.wait()
 
@@ -242,6 +234,13 @@
     return add_over_near(sums[:half], half) + crossing
 
 
+def with_columns(columns, blocks):
+    entries, fine_rows = columns.shape
+    used, width = blocks.shape
+    rows = jnp.pad(columns.astype(blocks.dtype), ((0, EXTRA - entries), (0, width - fine_rows)))
+    return jnp.concatenate([blocks, rows], axis=0)
+
+
 def local(
     operator_blocks,
     operator_count,
@@ -259,23 +258,20 @@
     own = jnp.stack([lax.axis_index("row"), lax.axis_index("half")])
     own = jnp.concatenate([own, place_of_columns(half)])[None]
 
-    near_blocks = prolong_blocks.reshape(fine_rows * block_size, width)
+    near_blocks = with_columns(prolong_cols.T, prolong_blocks.reshape(fine_rows * block_size, width))
     far_blocks = far_swap(near_blocks)
-    restricted, own_columns, near_blocks = restrict_operator(
+    restricted, mark = restrict_operator(
         operator_count,
         operator_slot,
         restrict_rows.T,
         fetch,
         operator_blocks,
         restrict_blocks,
-        prolong_cols.T,
-        near_blocks,
         lax.axis_index("half").reshape(1),
     )
     restricted = lax.all_to_all(restricted, "near", split_axis=0, concat_axis=0, tiled=True)
-    far_columns = far_swap(own_columns)
     near_pieces = spread_over_rows(near_blocks, rows)
-    far_blocks = append_columns(near_pieces[rows // 2], far_columns, own_columns, far_blocks)
+    far_blocks = hold_until(mark, near_pieces[rows // 2], far_blocks)
     pieces = near_pieces + spread_over_rows(far_blocks, rows)
     sums = combine(own, restricted, pieces, NCR * rows, slot_count, fine_rows, block_size)
     return add_over_columns(sums, half).T

time: 41.9 us -> 43.5 us (1.038)
  waiting for transfers between devices: 13.3 us -> 16.7 us
  starting transfers between devices: 22.2 us -> 18.9 us
  other arithmetic: 0.72 us -> 2.37 us
    all_to_all x1, waiting for transfers between devices: 1.37 us -> 4.25 us  [local(): lax.all_to_all(restricted, 'near', split_axis=0, concat_axis=0, tiled=True)]
    ppermute x6, waiting for transfers between devices: 0.69 us -> 2.69 us  [add_over_near(): lax.ppermute(sums[near], 'near', [(n, n ^ near) for n in range(half)])]
    ppermute x1, starting transfers between devices: 2.6 us -> 0.65 us  [half_swap(): return lax.ppermute(x, 'half', [(0, 1), (1, 0)])]
    ppermute x2 -> x1, waiting for transfers between devices: 1.69 us -> 0.01 us  [far_swap(): return lax.ppermute(x, ('half', 'near'), pairs)]
    ppermute x2 -> x1, starting transfers between devices: 5.27 us -> 3.6 us  [far_swap(): return lax.ppermute(x, ('half', 'near'), pairs)]
    concatenate x0 -> x1, other arithmetic: none -> 0.97 us  [with_columns(): return jnp.concatenate([blocks, rows], axis=0)]
    convert_element_type x0 -> x1, other arithmetic: none -> 0.68 us  [with_columns(): columns.astype(blocks.dtype)]
  transfers between devices with their start and end apart: 16 -> 15, of which waited for: 9 -> 8; matrix products, arithmetic and copies ran while one was open for 0% -> 0% of each run, Pallas kernels for 8% -> 8%
where the time goes in v31:
time: 43.5 us; the launch traced here: 43.2 us
  starting transfers between devices  18.9 us (43%)
  waiting for transfers between devices  16.7 us (38%)
  Pallas kernels  5.07 us (12%)
  other arithmetic  2.37 us (5%)
    ppermute x6, waiting for transfers between devices, row_swap(): lax.ppermute(x, 'row', [(r, r ^ bit) for r in range(lax.axis_size('row'))])  8.01 us
    ppermute x6, starting transfers between devices, add_over_near(): lax.ppermute(sums[near], 'near', [(n, n ^ near) for n in range(half)])  7.04 us
    all_to_all x1, waiting for transfers between devices, local(): lax.all_to_all(restricted, 'near', split_axis=0, concat_axis=0, tiled=True)  4.25 us
    ppermute x6, starting transfers between devices, row_swap(): lax.ppermute(x, 'row', [(r, r ^ bit) for r in range(lax.axis_size('row'))])  4.12 us
    ppermute x1, starting transfers between devices, far_swap(): return lax.ppermute(x, ('half', 'near'), pairs)  3.6 us
    all_to_all x1, starting transfers between devices, local(): lax.all_to_all(restricted, 'near', split_axis=0, concat_axis=0, tiled=True)  3.53 us
    pallas_call x1, Pallas kernels, restrict_operator(): pl.pallas_call(restrict_kernel, out_shape=(jax.ShapeDtypeStruct((columns...  3.29 us
    ppermute x6, waiting for transfers between devices, add_over_near(): lax.ppermute(sums[near], 'near', [(n, n ^ near) for n in range(half)])  2.69 us
  transfers between devices with their start and end apart: 15, of which 8 were waited for; matrix products, arithmetic and copies ran while one was open for 0% of the time, Pallas kernels for 8%

profile of v31, /device:TPU:0, one launch (start us, length us, event | category | flops | bytes accessed | tf_op | source)
XLA Modules:
  0.0 43.2 jit_solution(12576382927519642742)
XLA Ops:
  0.0 0.7 %convert_bitcast_fusion = f32[2,8]{1,0:T(2,128)S(1)} fusion(s32[8,2]{0,1:T(2,128)} %param.13), kind=kLoop, calls=%fused_computation.18 | loop fusion | flops 16 | bytes 128 | tf_op jit(solution)/shard_map/convert_element_type | solution.py:240
  0.7 1.0 %select_maximum_fusion.rest_0_ = f32[520,128]{1,0:T(8,128)S(1)} fusion(f32[2,8]{1,0:T(2,128)S(1)} %convert_bitcast_fusion, f32[512,128]{1,0:T(8,128)} %bitcast.45), kind=kLoop, calls=%fused_computation | loop fusion | flops 199680 | bytes 528448 | tf_op jit(solution)/shard_map/concatenate | solution.py:241
  1.7 3.0 %collective-permute-start.1 = (f32[520,128]{1,0:T(8,128)S(1)}, f32[520,128]{1,0:T(8,128)S(1)}, u32[]{:S(2)}, u32[]{:S(2)}) collective-permute-start(f32[520,128]{1,0:T(8,128)S(1)} %select_maximum_fusion.rest_0_), channel_id=1, source_target_pairs={{0,16},{8,24},{16,0},{24,8},{1,17},{9,25},{17,1},{25,9},{2,18},{10... | collective-permute-start | bytes 798728 | tf_op jit(solution)/shard_map/ppermute | solution.py:197
  4.7 3.6 %collective-permute-start.3 = (f32[520,128]{1,0:T(8,128)S(1)}, f32[520,128]{1,0:T(8,128)S(1)}, u32[]{:S(2)}, u32[]{:S(2)}) collective-permute-start(f32[520,128]{1,0:T(8,128)S(1)} %select_maximum_fusion.rest_0_), channel_id=1, source_target_pairs={{0,6},{1,7},{2,4},{3,5},{4,2},{5,3},{6,0},{7,1},{8,14},{9,15},{10,... | collective-permute-start | bytes 798728 | tf_op jit(solution)/shard_map/ppermute | solution.py:207
  8.3 3.3 %restrict_operator.1 = (f32[4,520,128]{2,1,0:T(8,128)}, f32[8,128]{1,0:T(8,128)}) custom-call(s32[8]{0:T(128)} %count_any.1, s32[8,8]{1,0:T(8,128)} %slot_any.1, s32[2,8]{1,0:T(2,128)} %bitcast.47, s32[4,8]{1,0:T(4,128)} %bitcast.46, f32[8,64,128]{2,1,0:T(8,128)} %restrict_any.1, f32[8,64,512]{2,1,0:T(8,128)} %operator_any.1, s32[1]{0:T(128)} %bitcast.1.side_any), custom_call_target="tpu_custom_call" | custom-call | flops 201326592 | bytes 4194304 | tf_op jit(solution)/shard_map/restrict_operator/pallas_call | solution.py:116
  11.6 3.5 %all-to-all-start = ((f32[4,520,128]{2,1,0:T(8,128)}), f32[4,520,128]{2,1,0:T(8,128)S(1)}, u32[]{:S(2)}, u32[]{:S(2)}) async-start(f32[4,520,128]{2,1,0:T(8,128)} %get-tuple-element.7), calls=%async_computation | async-start | bytes 2129920 | tf_op jit(solution)/shard_map/all_to_all | solution.py:272
  15.2 0.6 %collective-permute-start.5 = (f32[520,128]{1,0:T(8,128)S(1)}, f32[520,128]{1,0:T(8,128)S(1)}, u32[]{:S(2)}, u32[]{:S(2)}) collective-permute-start(f32[520,128]{1,0:T(8,128)S(1)} %hold_until.1.rest_4_), channel_id=1, source_target_pairs={{0,16},{8,24},{16,0},{24,8},{1,17},{9,25},{17,1},{25,9},{2,18},{10... | collective-permute-start | bytes 798728 | tf_op jit(solution)/shard_map/ppermute | solution.py:197
  15.8 0.5 %collective-permute-start.4 = (f32[520,128]{1,0:T(8,128)S(1)}, f32[520,128]{1,0:T(8,128)S(1)}, u32[]{:S(2)}, u32[]{:S(2)}) collective-permute-start(f32[520,128]{1,0:T(8,128)S(1)} %hold_until.1.rest_4_), channel_id=1, source_target_pairs={{0,8},{8,0},{16,24},{24,16},{1,9},{9,1},{17,25},{25,17},{2,10},{10... | collective-permute-start | bytes 798728 | tf_op jit(solution)/shard_map/ppermute | solution.py:197
  16.3 6.6 %collective-permute-done.5.rest_6_ = f32[520,128]{1,0:T(8,128)S(1)} collective-permute-done((f32[520,128]{1,0:T(8,128)S(1)}, f32[520,128]{1,0:T(8,128)S(1)}, u32[]{:S(2)}, u32[]{:S(2)}) %collective-permute-start.5) | collective-permute-done | bytes 266272 | tf_op jit(solution)/shard_map/ppermute | solution.py:197
  22.9 1.4 %collective-permute-done.6.rest_7_ = f32[520,128]{1,0:T(8,128)S(1)} collective-permute-done((f32[520,128]{1,0:T(8,128)S(1)}, f32[520,128]{1,0:T(8,128)S(1)}, u32[]{:S(2)}, u32[]{:S(2)}) %collective-permute-start.6) | collective-permute-done | bytes 266272 | tf_op jit(solution)/shard_map/ppermute | solution.py:197
  24.4 4.3 %all-to-all-done.restricted_ref = f32[4,520,128]{2,1,0:T(8,128)S(1)} async-done(((f32[4,520,128]{2,1,0:T(8,128)}), f32[4,520,128]{2,1,0:T(8,128)S(1)}, u32[]{:S(2)}, u32[]{:S(2)}) %all-to-all-start) | async-done | bytes 1064992 | tf_op jit(solution)/shard_map/all_to_all | solution.py:272
  28.6 1.8 %combine.1 = f32[8,64,128]{2,1,0:T(8,128)S(1)} custom-call(s32[1,10]{1,0:T(1,128)S(1)} %add_bitcast_fusion.own_ref, f32[4,520,128]{2,1,0:T(8,128)S(1)} %all-to-all-done.restricted_ref, f32[520,128]{1,0:T(8,128)S(1)} %select_maximum_fusion.rest_0_, f32[520,128]{1,0:T(8,128)S(1)} %collective-permute-done.rest_1_, ...), custom_call_target="tpu_custom_call" | custom-call | flops 268435456 | bytes 4194304 | tf_op jit(solution)/shard_map/combine/pallas_call | solution.py:179
  30.4 1.5 %collective-permute-start.12 = (f32[64,128]{1,0:T(8,128)S(1)}, f32[64,128]{1,0:T(8,128)S(1)}, u32[]{:S(2)}, u32[]{:S(2)}) collective-permute-start(f32[64,128]{1,0:T(8,128)S(1)} %get-tuple-element.10), channel_id=1, source_target_pairs={{0,3},{1,2},{2,1},{3,0},{4,7},{5,6},{6,5},{7,4},{8,11},{9,10},{10,... | collective-permute-start | bytes 98312 | tf_op jit(solution)/shard_map/ppermute | solution.py:228
  31.9 1.5 %collective-permute-start.11 = (f32[64,128]{1,0:T(8,128)S(1)}, f32[64,128]{1,0:T(8,128)S(1)}, u32[]{:S(2)}, u32[]{:S(2)}) collective-permute-start(f32[64,128]{1,0:T(8,128)S(1)} %get-tuple-element.11), channel_id=1, source_target_pairs={{0,2},{1,3},{2,0},{3,1},{4,6},{5,7},{6,4},{7,5},{8,10},{9,11},{10,... | collective-permute-start | bytes 98312 | tf_op jit(solution)/shard_map/ppermute | solution.py:228
  33.4 0.6 %collective-permute-start.10 = (f32[64,128]{1,0:T(8,128)S(1)}, f32[64,128]{1,0:T(8,128)S(1)}, u32[]{:S(2)}, u32[]{:S(2)}) collective-permute-start(f32[64,128]{1,0:T(8,128)S(1)} %get-tuple-element.12), channel_id=1, source_target_pairs={{0,1},{1,0},{2,3},{3,2},{4,5},{5,4},{6,7},{7,6},{8,9},{9,8},{10,11... | collective-permute-start | bytes 98312 | tf_op jit(solution)/shard_map/ppermute | solution.py:228
  34.0 1.5 %collective-permute-start.9 = (f32[64,128]{1,0:T(8,128)S(1)}, f32[64,128]{1,0:T(8,128)S(1)}, u32[]{:S(2)}, u32[]{:S(2)}) collective-permute-start(f32[64,128]{1,0:T(8,128)S(1)} %get-tuple-element.13), channel_id=1, source_target_pairs={{0,3},{1,2},{2,1},{3,0},{4,7},{5,6},{6,5},{7,4},{8,11},{9,10},{10,... | collective-permute-start | bytes 98312 | tf_op jit(solution)/shard_map/ppermute | solution.py:228
  35.4 1.5 %collective-permute-start.8 = (f32[64,128]{1,0:T(8,128)S(1)}, f32[64,128]{1,0:T(8,128)S(1)}, u32[]{:S(2)}, u32[]{:S(2)}) collective-permute-start(f32[64,128]{1,0:T(8,128)S(1)} %get-tuple-element.14), channel_id=1, source_target_pairs={{0,2},{1,3},{2,0},{3,1},{4,6},{5,7},{6,4},{7,5},{8,10},{9,11},{10,... | collective-permute-start | bytes 98312 | tf_op jit(solution)/shard_map/ppermute | solution.py:228
  36.9 0.6 %collective-permute-start.7 = (f32[64,128]{1,0:T(8,128)S(1)}, f32[64,128]{1,0:T(8,128)S(1)}, u32[]{:S(2)}, u32[]{:S(2)}) collective-permute-start(f32[64,128]{1,0:T(8,128)S(1)} %get-tuple-element.9), channel_id=1, source_target_pairs={{0,1},{1,0},{2,3},{3,2},{4,5},{5,4},{6,7},{7,6},{8,9},{9,8},{10,11... | collective-permute-start | bytes 98312 | tf_op jit(solution)/shard_map/ppermute | solution.py:228
  37.7 0.6 %collective-permute-start.13 = (f32[64,128]{1,0:T(8,128)S(1)}, f32[64,128]{1,0:T(8,128)S(1)}, u32[]{:S(2)}, u32[]{:S(2)}) collective-permute-start(f32[64,128]{1,0:T(8,128)S(1)} %fusion.2), channel_id=1, source_target_pairs={{0,4},{4,0},{1,5},{5,1},{2,6},{6,2},{3,7},{7,3},{8,12},{12,8},{9,1... | collective-permute-start | bytes 98312 | tf_op jit(solution)/shard_map/ppermute | solution.py:201
  38.3 0.5 %collective-permute-done.9 = f32[64,128]{1,0:T(8,128)S(1)} collective-permute-done((f32[64,128]{1,0:T(8,128)S(1)}, f32[64,128]{1,0:T(8,128)S(1)}, u32[]{:S(2)}, u32[]{:S(2)}) %collective-permute-start.9) | collective-permute-done | bytes 32800 | tf_op jit(solution)/shard_map/ppermute | solution.py:228
  38.8 0.9 %collective-permute-done.8 = f32[64,128]{1,0:T(8,128)S(1)} collective-permute-done((f32[64,128]{1,0:T(8,128)S(1)}, f32[64,128]{1,0:T(8,128)S(1)}, u32[]{:S(2)}, u32[]{:S(2)}) %collective-permute-start.8) | collective-permute-done | bytes 32800 | tf_op jit(solution)/shard_map/ppermute | solution.py:228
  39.7 1.1 %collective-permute-done.7 = f32[64,128]{1,0:T(8,128)S(1)} collective-permute-done((f32[64,128]{1,0:T(8,128)S(1)}, f32[64,128]{1,0:T(8,128)S(1)}, u32[]{:S(2)}, u32[]{:S(2)}) %collective-permute-start.7) | collective-permute-done | bytes 32800 | tf_op jit(solution)/shard_map/ppermute | solution.py:228
  40.8 1.7 %collective-permute-done.13 = f32[64,128]{1,0:T(8,128)S(1)} collective-permute-done((f32[64,128]{1,0:T(8,128)S(1)}, f32[64,128]{1,0:T(8,128)S(1)}, u32[]{:S(2)}, u32[]{:S(2)}) %collective-permute-start.13) | collective-permute-done | bytes 32800 | tf_op jit(solution)/shard_map/ppermute | solution.py:201
  42.6 0.6 %fusion.7 = f32[128,64]{0,1:T(8,128)} fusion(f32[64,128]{1,0:T(8,128)S(1)} %collective-permute-done.13, f32[64,128]{1,0:T(8,128)S(1)} %collective-permute-done.9, f32[64,128]{1,0:T(8,128)S(1)} %collective-permute-done.8, f32[64,128]{1,0:T(8,128)S(1)} %collective-permute-done.7, f32[8,64,128]{2,1,0:T(8,128)S(1)} %combine.1), kind=kLoop, calls=%fused_computation.17 | loop fusion | flops 32768 | bytes 196608 | tf_op jit(solution)/shard_map/transpose | solution.py:277
  (18 shorter events, 0.4 us)
Async XLA Ops:
  1.7 13.5 %collective-permute-start.1 = (f32[520,128]{1,0:T(8,128)S(1)}, f32[520,128]{1,0:T(8,128)S(1)}, u32[]{:S(2)}, u32[]{:S(2)}) collective-permute-start(f32[520,128]{1,0:T(8,128)S(1)} %select_maximum_fusion.rest_0_), channel_id=1, source_target_pairs={{0,16},{8,24},{16,0},{24,8},{1,17},{9,25},{17,1},{25,9},{2,18},{10... | collective-permute-start | bytes 798728 | tf_op jit(solution)/shard_map/ppermute | solution.py:197
  4.7 10.5 %collective-permute-start.3 = (f32[520,128]{1,0:T(8,128)S(1)}, f32[520,128]{1,0:T(8,128)S(1)}, u32[]{:S(2)}, u32[]{:S(2)}) collective-permute-start(f32[520,128]{1,0:T(8,128)S(1)} %select_maximum_fusion.rest_0_), channel_id=1, source_target_pairs={{0,6},{1,7},{2,4},{3,5},{4,2},{5,3},{6,0},{7,1},{8,14},{9,15},{10,... | collective-permute-start | bytes 798728 | tf_op jit(solution)/shard_map/ppermute | solution.py:207
  11.6 3.6 %copy-start = (f32[8,128]{1,0:T(8,128)S(1)}, f32[8,128]{1,0:T(8,128)}, u32[]{:S(2)}) copy-start(f32[8,128]{1,0:T(8,128)} %get-tuple-element.8.mark_ref) | copy-start | bytes 12292
  11.6 17.0 %all-to-all-start = ((f32[4,520,128]{2,1,0:T(8,128)}), f32[4,520,128]{2,1,0:T(8,128)S(1)}, u32[]{:S(2)}, u32[]{:S(2)}) async-start(f32[4,520,128]{2,1,0:T(8,128)} %get-tuple-element.7), calls=%async_computation | async-start | bytes 2129920 | tf_op jit(solution)/shard_map/all_to_all | solution.py:272
  15.2 7.6 %collective-permute-start.5 = (f32[520,128]{1,0:T(8,128)S(1)}, f32[520,128]{1,0:T(8,128)S(1)}, u32[]{:S(2)}, u32[]{:S(2)}) collective-permute-start(f32[520,128]{1,0:T(8,128)S(1)} %hold_until.1.rest_4_), channel_id=1, source_target_pairs={{0,16},{8,24},{16,0},{24,8},{1,17},{9,25},{17,1},{25,9},{2,18},{10... | collective-permute-start | bytes 798728 | tf_op jit(solution)/shard_map/ppermute | solution.py:197
  15.8 7.2 %collective-permute-start = (f32[520,128]{1,0:T(8,128)S(1)}, f32[520,128]{1,0:T(8,128)S(1)}, u32[]{:S(2)}, u32[]{:S(2)}) collective-permute-start(f32[520,128]{1,0:T(8,128)S(1)} %select_maximum_fusion.rest_0_), channel_id=1, source_target_pairs={{0,8},{8,0},{16,24},{24,16},{1,9},{9,1},{17,25},{25,17},{2,10},{10... | collective-permute-start | bytes 798728 | tf_op jit(solution)/shard_map/ppermute | solution.py:197
  15.8 7.2 %collective-permute-start.4 = (f32[520,128]{1,0:T(8,128)S(1)}, f32[520,128]{1,0:T(8,128)S(1)}, u32[]{:S(2)}, u32[]{:S(2)}) collective-permute-start(f32[520,128]{1,0:T(8,128)S(1)} %hold_until.1.rest_4_), channel_id=1, source_target_pairs={{0,8},{8,0},{16,24},{24,16},{1,9},{9,1},{17,25},{25,17},{2,10},{10... | collective-permute-start | bytes 798728 | tf_op jit(solution)/shard_map/ppermute | solution.py:197
  16.3 6.7 %collective-permute-start.2 = (f32[520,128]{1,0:T(8,128)S(1)}, f32[520,128]{1,0:T(8,128)S(1)}, u32[]{:S(2)}, u32[]{:S(2)}) collective-permute-start(f32[520,128]{1,0:T(8,128)S(1)} %collective-permute-done.1.next_ref.rest_2_), channel_id=1, source_target_pairs={{0,8},{8,0},{16,24},{24,16},{1,9},{9,1},{17,25},{25,17},{2,10},{10... | collective-permute-start | bytes 798728 | tf_op jit(solution)/shard_map/ppermute | solution.py:197
  22.8 1.5 %collective-permute-start.6 = (f32[520,128]{1,0:T(8,128)S(1)}, f32[520,128]{1,0:T(8,128)S(1)}, u32[]{:S(2)}, u32[]{:S(2)}) collective-permute-start(f32[520,128]{1,0:T(8,128)S(1)} %collective-permute-done.5.rest_6_), channel_id=1, source_target_pairs={{0,8},{8,0},{16,24},{24,16},{1,9},{9,1},{17,25},{25,17},{2,10},{10... | collective-permute-start | bytes 798728 | tf_op jit(solution)/shard_map/ppermute | solution.py:197
  30.4 6.5 %collective-permute-start.12 = (f32[64,128]{1,0:T(8,128)S(1)}, f32[64,128]{1,0:T(8,128)S(1)}, u32[]{:S(2)}, u32[]{:S(2)}) collective-permute-start(f32[64,128]{1,0:T(8,128)S(1)} %get-tuple-element.10), channel_id=1, source_target_pairs={{0,3},{1,2},{2,1},{3,0},{4,7},{5,6},{6,5},{7,4},{8,11},{9,10},{10,... | collective-permute-start | bytes 98312 | tf_op jit(solution)/shard_map/ppermute | solution.py:228
  31.9 5.5 %collective-permute-start.11 = (f32[64,128]{1,0:T(8,128)S(1)}, f32[64,128]{1,0:T(8,128)S(1)}, u32[]{:S(2)}, u32[]{:S(2)}) collective-permute-start(f32[64,128]{1,0:T(8,128)S(1)} %get-tuple-element.11), channel_id=1, source_target_pairs={{0,2},{1,3},{2,0},{3,1},{4,6},{5,7},{6,4},{7,5},{8,10},{9,11},{10,... | collective-permute-start | bytes 98312 | tf_op jit(solution)/shard_map/ppermute | solution.py:228
  33.4 4.3 %collective-permute-start.10 = (f32[64,128]{1,0:T(8,128)S(1)}, f32[64,128]{1,0:T(8,128)S(1)}, u32[]{:S(2)}, u32[]{:S(2)}) collective-permute-start(f32[64,128]{1,0:T(8,128)S(1)} %get-tuple-element.12), channel_id=1, source_target_pairs={{0,1},{1,0},{2,3},{3,2},{4,5},{5,4},{6,7},{7,6},{8,9},{9,8},{10,11... | collective-permute-start | bytes 98312 | tf_op jit(solution)/shard_map/ppermute | solution.py:228
  34.0 4.8 %collective-permute-start.9 = (f32[64,128]{1,0:T(8,128)S(1)}, f32[64,128]{1,0:T(8,128)S(1)}, u32[]{:S(2)}, u32[]{:S(2)}) collective-permute-start(f32[64,128]{1,0:T(8,128)S(1)} %get-tuple-element.13), channel_id=1, source_target_pairs={{0,3},{1,2},{2,1},{3,0},{4,7},{5,6},{6,5},{7,4},{8,11},{9,10},{10,... | collective-permute-start | bytes 98312 | tf_op jit(solution)/shard_map/ppermute | solution.py:228
  35.4 4.3 %collective-permute-start.8 = (f32[64,128]{1,0:T(8,128)S(1)}, f32[64,128]{1,0:T(8,128)S(1)}, u32[]{:S(2)}, u32[]{:S(2)}) collective-permute-start(f32[64,128]{1,0:T(8,128)S(1)} %get-tuple-element.14), channel_id=1, source_target_pairs={{0,2},{1,3},{2,0},{3,1},{4,6},{5,7},{6,4},{7,5},{8,10},{9,11},{10,... | collective-permute-start | bytes 98312 | tf_op jit(solution)/shard_map/ppermute | solution.py:228
  36.9 3.9 %collective-permute-start.7 = (f32[64,128]{1,0:T(8,128)S(1)}, f32[64,128]{1,0:T(8,128)S(1)}, u32[]{:S(2)}, u32[]{:S(2)}) collective-permute-start(f32[64,128]{1,0:T(8,128)S(1)} %get-tuple-element.9), channel_id=1, source_target_pairs={{0,1},{1,0},{2,3},{3,2},{4,5},{5,4},{6,7},{7,6},{8,9},{9,8},{10,11... | collective-permute-start | bytes 98312 | tf_op jit(solution)/shard_map/ppermute | solution.py:228
  37.7 4.9 %collective-permute-start.13 = (f32[64,128]{1,0:T(8,128)S(1)}, f32[64,128]{1,0:T(8,128)S(1)}, u32[]{:S(2)}, u32[]{:S(2)}) collective-permute-start(f32[64,128]{1,0:T(8,128)S(1)} %fusion.2), channel_id=1, source_target_pairs={{0,4},{4,0},{1,5},{5,1},{2,6},{6,2},{3,7},{7,3},{8,12},{12,8},{9,1... | collective-permute-start | bytes 98312 | tf_op jit(solution)/shard_map/ppermute | solution.py:201

commit v32 on v22

--- a/solution.py
+++ b/solution.py
@@ -98,9 +98,11 @@
         own_row = jnp.where(second == 0, rows_ref[0, i], rows_ref[1, i])
         other_row = jnp.where(second == 0, rows_ref[1, i], rows_ref[0, i])
         dense = jnp.where(own_row == second, value, 0.0) + jnp.where(other_row == second, swapped, 0.0)
-        product = transposed_product(operator_ref[i], dense)
         for k in range(entries):
-            part = jnp.where(k < count_ref[i], product[k * block_size : (k + 1) * block_size], 0.0)
+            first = k % 2 * block_size
+            if first == 0:
+                product = transposed_product(operator_ref[i, :, k * block_size : (k + 2) * block_size], dense)
+            part = jnp.where(k < count_ref[i], product[first : first + block_size], 0.0)
             peer = lax.div(slot_ref[i, k], slot_count)
             side = lax.div(peer, half)
             place = side * slot_count + lax.rem(slot_ref[i, k], slot_count)

time: 41.9 us -> 41.9 us (level)
  no operation moved by 1% of the time
where the time goes in v32:
time: 41.9 us; the launch traced here: 41.7 us
  starting transfers between devices  22.2 us (53%)
  waiting for transfers between devices  13.3 us (32%)
  Pallas kernels  5.26 us (13%)
  other arithmetic  0.72 us (2%)
    ppermute x6, waiting for transfers between devices, row_swap(): lax.ppermute(x, 'row', [(r, r ^ bit) for r in range(lax.axis_size('row'))])  8 us
    ppermute x6, starting transfers between devices, add_over_near(): lax.ppermute(sums[near], 'near', [(n, n ^ near) for n in range(half)])  7.04 us
    ppermute x2, starting transfers between devices, far_swap(): return lax.ppermute(x, ('half', 'near'), pairs)  5.28 us
    ppermute x6, starting transfers between devices, row_swap(): lax.ppermute(x, 'row', [(r, r ^ bit) for r in range(lax.axis_size('row'))])  3.68 us
    all_to_all x1, starting transfers between devices, local(): lax.all_to_all(restricted, 'near', split_axis=0, concat_axis=0, tiled=True)  3.65 us
    pallas_call x1, Pallas kernels, restrict_operator(): pl.pallas_call(restrict_kernel, out_shape=(jax.ShapeDtypeStruct((columns...  3.49 us
    ppermute x1, starting transfers between devices, half_swap(): return lax.ppermute(x, 'half', [(0, 1), (1, 0)])  2.59 us
    pallas_call x1, Pallas kernels, combine(): pl.pallas_call(functools.partial(combine_kernel, slot_count=slot_count, f...  1.75 us
  transfers between devices with their start and end apart: 16, of which 9 were waited for; matrix products, arithmetic and copies ran while one was open for 0% of the time, Pallas kernels for 8%

profile of v32, /device:TPU:0, one launch (start us, length us, event | category | flops | bytes accessed | tf_op | source)
XLA Modules:
  0.0 41.7 jit_solution(13823213112268851197)
XLA Ops:
  0.0 5.0 %collective-permute-start.4 = (f32[512,128]{1,0:T(8,128)}, f32[512,128]{1,0:T(8,128)S(1)}, u32[]{:S(2)}, u32[]{:S(2)}) collective-permute-start(f32[512,128]{1,0:T(8,128)} %bitcast.44), channel_id=1, source_target_pairs={{0,6},{1,7},{2,4},{3,5},{4,2},{5,3},{6,0},{7,1},{8,14},{9,15},{10,... | collective-permute-start | bytes 786440 | tf_op jit(solution)/shard_map/ppermute | solution.py:217
  5.0 3.5 %restrict_operator.1 = (f32[4,520,128]{2,1,0:T(8,128)}, s32[2,8]{1,0:T(2,128)}, f32[512,128]{1,0:T(8,128)}) custom-call(s32[8]{0:T(128)} %count_any.1, s32[8,8]{1,0:T(8,128)} %slot_any.1, s32[2,8]{1,0:T(2,128)} %bitcast.47, s32[4,8]{1,0:T(4,128)} %bitcast.46, f32[8,64,128]{2,1,0:T(8,128)} %restrict_any.1, f32[8,64,512]{2,1,0:T(8,128)} %operator_any.1, ...), custom_call_target="tpu_custom_call" | custom-call | flops 201326592 | bytes 4194304 | tf_op jit(solution)/shard_map/restrict_operator/pallas_call | solution.py:123
  8.5 1.6 %collective-permute-start.1 = (f32[512,128]{1,0:T(8,128)}, f32[512,128]{1,0:T(8,128)S(1)}, u32[]{:S(2)}, u32[]{:S(2)}) collective-permute-start(f32[512,128]{1,0:T(8,128)} %get-tuple-element.9.rest_0_), channel_id=1, source_target_pairs={{0,16},{8,24},{16,0},{24,8},{1,17},{9,25},{17,1},{25,9},{2,18},{10... | collective-permute-start | bytes 786440 | tf_op jit(solution)/shard_map/ppermute | solution.py:207
  10.1 0.2 collective-permute-start.3
  10.4 3.6 %all-to-all-start = ((f32[4,520,128]{2,1,0:T(8,128)}), f32[4,520,128]{2,1,0:T(8,128)S(1)}, u32[]{:S(2)}, u32[]{:S(2)}) async-start(f32[4,520,128]{2,1,0:T(8,128)} %get-tuple-element.8), calls=%async_computation | async-start | bytes 2129920 | tf_op jit(solution)/shard_map/all_to_all | solution.py:277
  14.0 1.7 %collective-permute-done.3.far_columns_ref = s32[2,8]{1,0:T(2,128)S(1)} collective-permute-done((s32[2,8]{1,0:T(2,128)}, s32[2,8]{1,0:T(2,128)S(1)}, u32[]{:S(2)}, u32[]{:S(2)}) %collective-permute-start.3) | collective-permute-done | bytes 96 | tf_op jit(solution)/shard_map/ppermute | solution.py:217
  15.7 0.9 %collective-permute-done.1.next_ref.rest_2_ = f32[512,128]{1,0:T(8,128)S(1)} collective-permute-done((f32[512,128]{1,0:T(8,128)}, f32[512,128]{1,0:T(8,128)S(1)}, u32[]{:S(2)}, u32[]{:S(2)}) %collective-permute-start.1) | collective-permute-done | bytes 262176 | tf_op jit(solution)/shard_map/ppermute | solution.py:207
  16.6 1.6 %collective-permute-start.6 = (f32[520,128]{1,0:T(8,128)S(1)}, f32[520,128]{1,0:T(8,128)S(1)}, u32[]{:S(2)}, u32[]{:S(2)}) collective-permute-start(f32[520,128]{1,0:T(8,128)S(1)} %append_columns.1.rest_4_), channel_id=1, source_target_pairs={{0,16},{8,24},{16,0},{24,8},{1,17},{9,25},{17,1},{25,9},{2,18},{10... | collective-permute-start | bytes 798728 | tf_op jit(solution)/shard_map/ppermute | solution.py:207
  18.2 5.4 %collective-permute-done.6.rest_6_ = f32[520,128]{1,0:T(8,128)S(1)} collective-permute-done((f32[520,128]{1,0:T(8,128)S(1)}, f32[520,128]{1,0:T(8,128)S(1)}, u32[]{:S(2)}, u32[]{:S(2)}) %collective-permute-start.6) | collective-permute-done | bytes 266272 | tf_op jit(solution)/shard_map/ppermute | solution.py:207
  23.6 0.5 %collective-permute-start = (f32[512,128]{1,0:T(8,128)S(1)}, f32[512,128]{1,0:T(8,128)S(1)}, u32[]{:S(2)}, u32[]{:S(2)}) collective-permute-start(f32[512,128]{1,0:T(8,128)S(1)} %copy-done), channel_id=1, source_target_pairs={{0,8},{8,0},{16,24},{24,16},{1,9},{9,1},{17,25},{25,17},{2,10},{10... | collective-permute-start | bytes 786440 | tf_op jit(solution)/shard_map/ppermute | solution.py:207
  24.2 1.3 %collective-permute-done.rest_1_ = f32[512,128]{1,0:T(8,128)S(1)} collective-permute-done((f32[512,128]{1,0:T(8,128)S(1)}, f32[512,128]{1,0:T(8,128)S(1)}, u32[]{:S(2)}, u32[]{:S(2)}) %collective-permute-start) | collective-permute-done | bytes 262176 | tf_op jit(solution)/shard_map/ppermute | solution.py:207
  25.5 0.4 collective-permute-done.2.rest_3_
  25.9 1.4 %all-to-all-done.restricted_ref = f32[4,520,128]{2,1,0:T(8,128)S(1)} async-done(((f32[4,520,128]{2,1,0:T(8,128)}), f32[4,520,128]{2,1,0:T(8,128)S(1)}, u32[]{:S(2)}, u32[]{:S(2)}) %all-to-all-start) | async-done | bytes 1064992 | tf_op jit(solution)/shard_map/all_to_all | solution.py:277
  27.3 1.8 %combine.1 = f32[8,64,128]{2,1,0:T(8,128)S(1)} custom-call(s32[1,10]{1,0:T(1,128)S(1)} %add_bitcast_fusion.own_ref, f32[4,520,128]{2,1,0:T(8,128)S(1)} %all-to-all-done.restricted_ref, f32[512,128]{1,0:T(8,128)S(1)} %copy-done, f32[512,128]{1,0:T(8,128)S(1)} %collective-permute-done.rest_1_, f32[512,128]{1,0:T(8,128)S(1)} %collective-permute-done.1.next_ref.rest_2_, ...), custom_call_target="tpu_custom_call" | custom-call | flops 268435456 | bytes 4194304 | tf_op jit(solution)/shard_map/combine/pallas_call | solution.py:189
  29.1 1.5 %collective-permute-start.13 = (f32[64,128]{1,0:T(8,128)S(1)}, f32[64,128]{1,0:T(8,128)S(1)}, u32[]{:S(2)}, u32[]{:S(2)}) collective-permute-start(f32[64,128]{1,0:T(8,128)S(1)} %get-tuple-element.12), channel_id=1, source_target_pairs={{0,3},{1,2},{2,1},{3,0},{4,7},{5,6},{6,5},{7,4},{8,11},{9,10},{10,... | collective-permute-start | bytes 98312 | tf_op jit(solution)/shard_map/ppermute | solution.py:238
  30.6 1.5 %collective-permute-start.12 = (f32[64,128]{1,0:T(8,128)S(1)}, f32[64,128]{1,0:T(8,128)S(1)}, u32[]{:S(2)}, u32[]{:S(2)}) collective-permute-start(f32[64,128]{1,0:T(8,128)S(1)} %get-tuple-element.13), channel_id=1, source_target_pairs={{0,2},{1,3},{2,0},{3,1},{4,6},{5,7},{6,4},{7,5},{8,10},{9,11},{10,... | collective-permute-start | bytes 98312 | tf_op jit(solution)/shard_map/ppermute | solution.py:238
  32.1 0.6 %collective-permute-start.11 = (f32[64,128]{1,0:T(8,128)S(1)}, f32[64,128]{1,0:T(8,128)S(1)}, u32[]{:S(2)}, u32[]{:S(2)}) collective-permute-start(f32[64,128]{1,0:T(8,128)S(1)} %get-tuple-element.14), channel_id=1, source_target_pairs={{0,1},{1,0},{2,3},{3,2},{4,5},{5,4},{6,7},{7,6},{8,9},{9,8},{10,11... | collective-permute-start | bytes 98312 | tf_op jit(solution)/shard_map/ppermute | solution.py:238
  32.6 1.5 %collective-permute-start.8 = (f32[64,128]{1,0:T(8,128)S(1)}, f32[64,128]{1,0:T(8,128)S(1)}, u32[]{:S(2)}, u32[]{:S(2)}) collective-permute-start(f32[64,128]{1,0:T(8,128)S(1)} %get-tuple-element.11), channel_id=1, source_target_pairs={{0,1},{1,0},{2,3},{3,2},{4,5},{5,4},{6,7},{7,6},{8,9},{9,8},{10,11... | collective-permute-start | bytes 98312 | tf_op jit(solution)/shard_map/ppermute | solution.py:238
  34.1 1.4 %collective-permute-start.10 = (f32[64,128]{1,0:T(8,128)S(1)}, f32[64,128]{1,0:T(8,128)S(1)}, u32[]{:S(2)}, u32[]{:S(2)}) collective-permute-start(f32[64,128]{1,0:T(8,128)S(1)} %get-tuple-element.15), channel_id=1, source_target_pairs={{0,3},{1,2},{2,1},{3,0},{4,7},{5,6},{6,5},{7,4},{8,11},{9,10},{10,... | collective-permute-start | bytes 98312 | tf_op jit(solution)/shard_map/ppermute | solution.py:238
  35.5 0.6 %collective-permute-start.9 = (f32[64,128]{1,0:T(8,128)S(1)}, f32[64,128]{1,0:T(8,128)S(1)}, u32[]{:S(2)}, u32[]{:S(2)}) collective-permute-start(f32[64,128]{1,0:T(8,128)S(1)} %get-tuple-element.16), channel_id=1, source_target_pairs={{0,2},{1,3},{2,0},{3,1},{4,6},{5,7},{6,4},{7,5},{8,10},{9,11},{10,... | collective-permute-start | bytes 98312 | tf_op jit(solution)/shard_map/ppermute | solution.py:238
  36.1 2.6 %collective-permute-start.14 = (f32[64,128]{1,0:T(8,128)S(1)}, f32[64,128]{1,0:T(8,128)S(1)}, u32[]{:S(2)}, u32[]{:S(2)}) collective-permute-start(f32[64,128]{1,0:T(8,128)S(1)} %fusion.2), channel_id=1, source_target_pairs={{0,4},{4,0},{1,5},{5,1},{2,6},{6,2},{3,7},{7,3},{8,12},{12,8},{9,1... | collective-permute-start | bytes 98312 | tf_op jit(solution)/shard_map/ppermute | solution.py:211
  38.9 0.5 %collective-permute-done.9 = f32[64,128]{1,0:T(8,128)S(1)} collective-permute-done((f32[64,128]{1,0:T(8,128)S(1)}, f32[64,128]{1,0:T(8,128)S(1)}, u32[]{:S(2)}, u32[]{:S(2)}) %collective-permute-start.9) | collective-permute-done | bytes 32800 | tf_op jit(solution)/shard_map/ppermute | solution.py:238
  39.4 1.6 %collective-permute-done.14 = f32[64,128]{1,0:T(8,128)S(1)} collective-permute-done((f32[64,128]{1,0:T(8,128)S(1)}, f32[64,128]{1,0:T(8,128)S(1)}, u32[]{:S(2)}, u32[]{:S(2)}) %collective-permute-start.14) | collective-permute-done | bytes 32800 | tf_op jit(solution)/shard_map/ppermute | solution.py:211
  41.0 0.6 %fusion.7 = f32[128,64]{0,1:T(8,128)} fusion(f32[64,128]{1,0:T(8,128)S(1)} %collective-permute-done.14, f32[64,128]{1,0:T(8,128)S(1)} %collective-permute-done.10, f32[64,128]{1,0:T(8,128)S(1)} %collective-permute-done.9, f32[64,128]{1,0:T(8,128)S(1)} %collective-permute-done.8, f32[8,64,128]{2,1,0:T(8,128)S(1)} %combine.1), kind=kLoop, calls=%fused_computation.15 | loop fusion | flops 32768 | bytes 196608 | tf_op jit(solution)/shard_map/transpose | solution.py:283
  (20 shorter events, 0.3 us)
Async XLA Ops:
  0.0 15.7 %collective-permute-start.4 = (f32[512,128]{1,0:T(8,128)}, f32[512,128]{1,0:T(8,128)S(1)}, u32[]{:S(2)}, u32[]{:S(2)}) collective-permute-start(f32[512,128]{1,0:T(8,128)} %bitcast.44), channel_id=1, source_target_pairs={{0,6},{1,7},{2,4},{3,5},{4,2},{5,3},{6,0},{7,1},{8,14},{9,15},{10,... | collective-permute-start | bytes 786440 | tf_op jit(solution)/shard_map/ppermute | solution.py:217
  8.5 8.0 %collective-permute-start.1 = (f32[512,128]{1,0:T(8,128)}, f32[512,128]{1,0:T(8,128)S(1)}, u32[]{:S(2)}, u32[]{:S(2)}) collective-permute-start(f32[512,128]{1,0:T(8,128)} %get-tuple-element.9.rest_0_), channel_id=1, source_target_pairs={{0,16},{8,24},{16,0},{24,8},{1,17},{9,25},{17,1},{25,9},{2,18},{10... | collective-permute-start | bytes 786440 | tf_op jit(solution)/shard_map/ppermute | solution.py:207
  10.1 5.6 %collective-permute-start.3 = (s32[2,8]{1,0:T(2,128)}, s32[2,8]{1,0:T(2,128)S(1)}, u32[]{:S(2)}, u32[]{:S(2)}) collective-permute-start(s32[2,8]{1,0:T(2,128)} %get-tuple-element.10.own_columns_ref), channel_id=1, source_target_pairs={{0,6},{1,7},{2,4},{3,5},{4,2},{5,3},{6,0},{7,1},{8,14},{9,15},{10,... | collective-permute-start | bytes 200 | tf_op jit(solution)/shard_map/ppermute | solution.py:217
  10.4 6.2 %copy-start.1 = (s32[2,8]{1,0:T(2,128)S(1)}, s32[2,8]{1,0:T(2,128)}, u32[]{:S(2)}) copy-start(s32[2,8]{1,0:T(2,128)} %get-tuple-element.10.own_columns_ref) | copy-start | bytes 196
  10.4 16.9 %all-to-all-start = ((f32[4,520,128]{2,1,0:T(8,128)}), f32[4,520,128]{2,1,0:T(8,128)S(1)}, u32[]{:S(2)}, u32[]{:S(2)}) async-start(f32[4,520,128]{2,1,0:T(8,128)} %get-tuple-element.8), calls=%async_computation | async-start | bytes 2129920 | tf_op jit(solution)/shard_map/all_to_all | solution.py:277
  14.0 9.6 %copy-start = (f32[512,128]{1,0:T(8,128)S(1)}, f32[512,128]{1,0:T(8,128)}, u32[]{:S(2)}) copy-start(f32[512,128]{1,0:T(8,128)} %get-tuple-element.9.rest_0_) | copy-start | bytes 786436
  16.6 7.0 %collective-permute-start.6 = (f32[520,128]{1,0:T(8,128)S(1)}, f32[520,128]{1,0:T(8,128)S(1)}, u32[]{:S(2)}, u32[]{:S(2)}) collective-permute-start(f32[520,128]{1,0:T(8,128)S(1)} %append_columns.1.rest_4_), channel_id=1, source_target_pairs={{0,16},{8,24},{16,0},{24,8},{1,17},{9,25},{17,1},{25,9},{2,18},{10... | collective-permute-start | bytes 798728 | tf_op jit(solution)/shard_map/ppermute | solution.py:207
  18.2 7.7 %collective-permute-start.5 = (f32[520,128]{1,0:T(8,128)S(1)}, f32[520,128]{1,0:T(8,128)S(1)}, u32[]{:S(2)}, u32[]{:S(2)}) collective-permute-start(f32[520,128]{1,0:T(8,128)S(1)} %append_columns.1.rest_4_), channel_id=1, source_target_pairs={{0,8},{8,0},{16,24},{24,16},{1,9},{9,1},{17,25},{25,17},{2,10},{10... | collective-permute-start | bytes 798728 | tf_op jit(solution)/shard_map/ppermute | solution.py:207
  23.6 2.3 %collective-permute-start.7 = (f32[520,128]{1,0:T(8,128)S(1)}, f32[520,128]{1,0:T(8,128)S(1)}, u32[]{:S(2)}, u32[]{:S(2)}) collective-permute-start(f32[520,128]{1,0:T(8,128)S(1)} %collective-permute-done.6.rest_6_), channel_id=1, source_target_pairs={{0,8},{8,0},{16,24},{24,16},{1,9},{9,1},{17,25},{25,17},{2,10},{10... | collective-permute-start | bytes 798728 | tf_op jit(solution)/shard_map/ppermute | solution.py:207
  23.6 1.9 %collective-permute-start = (f32[512,128]{1,0:T(8,128)S(1)}, f32[512,128]{1,0:T(8,128)S(1)}, u32[]{:S(2)}, u32[]{:S(2)}) collective-permute-start(f32[512,128]{1,0:T(8,128)S(1)} %copy-done), channel_id=1, source_target_pairs={{0,8},{8,0},{16,24},{24,16},{1,9},{9,1},{17,25},{25,17},{2,10},{10... | collective-permute-start | bytes 786440 | tf_op jit(solution)/shard_map/ppermute | solution.py:207
  24.1 1.8 %collective-permute-start.2 = (f32[512,128]{1,0:T(8,128)S(1)}, f32[512,128]{1,0:T(8,128)S(1)}, u32[]{:S(2)}, u32[]{:S(2)}) collective-permute-start(f32[512,128]{1,0:T(8,128)S(1)} %collective-permute-done.1.next_ref.rest_2_), channel_id=1, source_target_pairs={{0,8},{8,0},{16,24},{24,16},{1,9},{9,1},{17,25},{25,17},{2,10},{10... | collective-permute-start | bytes 786440 | tf_op jit(solution)/shard_map/ppermute | solution.py:207
  29.1 6.4 %collective-permute-start.13 = (f32[64,128]{1,0:T(8,128)S(1)}, f32[64,128]{1,0:T(8,128)S(1)}, u32[]{:S(2)}, u32[]{:S(2)}) collective-permute-start(f32[64,128]{1,0:T(8,128)S(1)} %get-tuple-element.12), channel_id=1, source_target_pairs={{0,3},{1,2},{2,1},{3,0},{4,7},{5,6},{6,5},{7,4},{8,11},{9,10},{10,... | collective-permute-start | bytes 98312 | tf_op jit(solution)/shard_map/ppermute | solution.py:238
  30.6 5.5 %collective-permute-start.12 = (f32[64,128]{1,0:T(8,128)S(1)}, f32[64,128]{1,0:T(8,128)S(1)}, u32[]{:S(2)}, u32[]{:S(2)}) collective-permute-start(f32[64,128]{1,0:T(8,128)S(1)} %get-tuple-element.13), channel_id=1, source_target_pairs={{0,2},{1,3},{2,0},{3,1},{4,6},{5,7},{6,4},{7,5},{8,10},{9,11},{10,... | collective-permute-start | bytes 98312 | tf_op jit(solution)/shard_map/ppermute | solution.py:238
  32.1 4.1 %collective-permute-start.11 = (f32[64,128]{1,0:T(8,128)S(1)}, f32[64,128]{1,0:T(8,128)S(1)}, u32[]{:S(2)}, u32[]{:S(2)}) collective-permute-start(f32[64,128]{1,0:T(8,128)S(1)} %get-tuple-element.14), channel_id=1, source_target_pairs={{0,1},{1,0},{2,3},{3,2},{4,5},{5,4},{6,7},{7,6},{8,9},{9,8},{10,11... | collective-permute-start | bytes 98312 | tf_op jit(solution)/shard_map/ppermute | solution.py:238
  32.6 6.1 %collective-permute-start.8 = (f32[64,128]{1,0:T(8,128)S(1)}, f32[64,128]{1,0:T(8,128)S(1)}, u32[]{:S(2)}, u32[]{:S(2)}) collective-permute-start(f32[64,128]{1,0:T(8,128)S(1)} %get-tuple-element.11), channel_id=1, source_target_pairs={{0,1},{1,0},{2,3},{3,2},{4,5},{5,4},{6,7},{7,6},{8,9},{9,8},{10,11... | collective-permute-start | bytes 98312 | tf_op jit(solution)/shard_map/ppermute | solution.py:238
  34.1 4.8 %collective-permute-start.10 = (f32[64,128]{1,0:T(8,128)S(1)}, f32[64,128]{1,0:T(8,128)S(1)}, u32[]{:S(2)}, u32[]{:S(2)}) collective-permute-start(f32[64,128]{1,0:T(8,128)S(1)} %get-tuple-element.15), channel_id=1, source_target_pairs={{0,3},{1,2},{2,1},{3,0},{4,7},{5,6},{6,5},{7,4},{8,11},{9,10},{10,... | collective-permute-start | bytes 98312 | tf_op jit(solution)/shard_map/ppermute | solution.py:238
  35.5 3.9 %collective-permute-start.9 = (f32[64,128]{1,0:T(8,128)S(1)}, f32[64,128]{1,0:T(8,128)S(1)}, u32[]{:S(2)}, u32[]{:S(2)}) collective-permute-start(f32[64,128]{1,0:T(8,128)S(1)} %get-tuple-element.16), channel_id=1, source_target_pairs={{0,2},{1,3},{2,0},{3,1},{4,6},{5,7},{6,4},{7,5},{8,10},{9,11},{10,... | collective-permute-start | bytes 98312 | tf_op jit(solution)/shard_map/ppermute | solution.py:238
  36.1 4.9 %collective-permute-start.14 = (f32[64,128]{1,0:T(8,128)S(1)}, f32[64,128]{1,0:T(8,128)S(1)}, u32[]{:S(2)}, u32[]{:S(2)}) collective-permute-start(f32[64,128]{1,0:T(8,128)S(1)} %fusion.2), channel_id=1, source_target_pairs={{0,4},{4,0},{1,5},{5,1},{2,6},{6,2},{3,7},{7,3},{8,12},{12,8},{9,1... | collective-permute-start | bytes 98312 | tf_op jit(solution)/shard_map/ppermute | solution.py:211

commit v33 on v22

--- a/solution.py
+++ b/solution.py
@@ -87,8 +87,7 @@
         value = jnp.zeros((EXTRA, wide), jnp.int32)
         for side in range(2):
             for s in range(slot_count):
-                turned = near ^ jnp.where(side_ref[0] == side, 0, half // 2)
-                wanted = fetch_ref[s, side * half + turned]
+                wanted = fetch_ref[s, side * half + near]
                 value = jnp.where(short_lane == side * slot_count + s, wanted, value)
         out_ref[near, used:] = value.astype(jnp.float32)
 
@@ -104,7 +103,7 @@
             peer = lax.div(slot_ref[i, k], slot_count)
             side = lax.div(peer, half)
             place = side * slot_count + lax.rem(slot_ref[i, k], slot_count)
-            near = lax.rem(peer, half) ^ jnp.where(side_ref[0] == side, 0, half // 2)
+            near = lax.rem(peer, half)
             start = pl.multiple_of(place * block_size, block_size)
             out_ref[near, pl.ds(start, block_size)] += part
 
@@ -209,12 +208,6 @@
     return lax.ppermute(x, "half", [(0, 1), (1, 0)])
 
 
-def far_swap(x):
-    half = lax.axis_size("near")
-    pairs = [(h * half + n, (1 - h) * half + (n ^ half // 2)) for h in range(2) for n in range(half)]
-    return lax.ppermute(x, ("half", "near"), pairs)
-
-
 def spread_over_rows(blocks, rows):
     pieces = {0: blocks}
     bit = rows // 2
@@ -260,7 +253,7 @@
     own = jnp.concatenate([own, place_of_columns(half)])[None]
 
     near_blocks = prolong_blocks.reshape(fine_rows * block_size, width)
-    far_blocks = far_swap(near_blocks)
+    far_blocks = half_swap(near_blocks)
     restricted, own_columns, near_blocks = restrict_operator(
         operator_count,
         operator_slot,
@@ -273,7 +266,7 @@
         lax.axis_index("half").reshape(1),
     )
     restricted = lax.all_to_all(restricted, "near", split_axis=0, concat_axis=0, tiled=True)
-    far_columns = far_swap(own_columns)
+    far_columns = half_swap(own_columns)
     near_pieces = spread_over_rows(near_blocks, rows)
     far_blocks = append_columns(near_pieces[rows // 2], far_columns, own_columns, far_blocks)
     pieces = near_pieces + spread_over_rows(far_blocks, rows)

time: 41.9 us -> 42.5 us (1.014)
  waiting for transfers between devices: 13.3 us -> 15.3 us
  starting transfers between devices: 22.2 us -> 21 us
    ppermute x2 -> x0, starting transfers between devices: 5.27 us -> none  [far_swap(): return lax.ppermute(x, ('half', 'near'), pairs)]
    ppermute x1 -> x3, starting transfers between devices: 2.6 us -> 6.34 us  [half_swap(): return lax.ppermute(x, 'half', [(0, 1), (1, 0)])]
    ppermute x1 -> x3, waiting for transfers between devices: 1.6 us -> 5 us  [half_swap(): return lax.ppermute(x, 'half', [(0, 1), (1, 0)])]
    ppermute x2 -> x0, waiting for transfers between devices: 1.69 us -> none  [far_swap(): return lax.ppermute(x, ('half', 'near'), pairs)]
    ppermute x6, waiting for transfers between devices: 0.69 us -> 1.24 us  [add_over_near(): lax.ppermute(sums[near], 'near', [(n, n ^ near) for n in range(half)])]
    ppermute x6, waiting for transfers between devices: 7.99 us -> 7.56 us  [row_swap(): lax.ppermute(x, 'row', [(r, r ^ bit) for r in range(lax.axis_size('row'))])]
  transfers between devices with their start and end apart: 16 -> 16, of which waited for: 9 -> 8; matrix products, arithmetic and copies ran while one was open for 0% -> 0% of each run, Pallas kernels for 8% -> 8%
where the time goes in v33:
time: 42.5 us; the launch traced here: 42.3 us
  starting transfers between devices  21 us (49%)
  waiting for transfers between devices  15.3 us (36%)
  Pallas kernels  5.22 us (12%)
  other arithmetic  0.72 us (2%)
    ppermute x6, waiting for transfers between devices, row_swap(): lax.ppermute(x, 'row', [(r, r ^ bit) for r in range(lax.axis_size('row'))])  7.56 us
    ppermute x6, starting transfers between devices, add_over_near(): lax.ppermute(sums[near], 'near', [(n, n ^ near) for n in range(half)])  7.04 us
    ppermute x3, starting transfers between devices, half_swap(): return lax.ppermute(x, 'half', [(0, 1), (1, 0)])  6.34 us
    ppermute x3, waiting for transfers between devices, half_swap(): return lax.ppermute(x, 'half', [(0, 1), (1, 0)])  5 us
    all_to_all x1, starting transfers between devices, local(): lax.all_to_all(restricted, 'near', split_axis=0, concat_axis=0, tiled=True)  3.9 us
    ppermute x6, starting transfers between devices, row_swap(): lax.ppermute(x, 'row', [(r, r ^ bit) for r in range(lax.axis_size('row'))])  3.74 us
    pallas_call x1, Pallas kernels, restrict_operator(): pl.pallas_call(restrict_kernel, out_shape=(jax.ShapeDtypeStruct((columns...  3.44 us
    pallas_call x1, Pallas kernels, combine(): pl.pallas_call(functools.partial(combine_kernel, slot_count=slot_count, f...  1.75 us
  transfers between devices with their start and end apart: 16, of which 8 were waited for; matrix products, arithmetic and copies ran while one was open for 0% of the time, Pallas kernels for 8%

profile of v33, /device:TPU:0, one launch (start us, length us, event | category | flops | bytes accessed | tf_op | source)
XLA Modules:
  0.0 42.3 jit_solution(18007215262220702760)
XLA Ops:
  0.0 4.0 %collective-permute-start.4 = (f32[512,128]{1,0:T(8,128)}, f32[512,128]{1,0:T(8,128)S(1)}, u32[]{:S(2)}, u32[]{:S(2)}) collective-permute-start(f32[512,128]{1,0:T(8,128)} %bitcast.44), channel_id=1, source_target_pairs={{0,4},{4,0},{1,5},{5,1},{2,6},{6,2},{3,7},{7,3},{8,12},{12,8},{9,1... | collective-permute-start | bytes 786440 | tf_op jit(solution)/shard_map/ppermute | solution.py:208
  4.0 3.4 %restrict_operator.1 = (f32[4,520,128]{2,1,0:T(8,128)}, s32[2,8]{1,0:T(2,128)}, f32[512,128]{1,0:T(8,128)}) custom-call(s32[8]{0:T(128)} %count_any.1, s32[8,8]{1,0:T(8,128)} %slot_any.1, s32[2,8]{1,0:T(2,128)} %bitcast.47, s32[4,8]{1,0:T(4,128)} %bitcast.46, f32[8,64,128]{2,1,0:T(8,128)} %restrict_any.1, f32[8,64,512]{2,1,0:T(8,128)} %operator_any.1, ...), custom_call_target="tpu_custom_call" | custom-call | flops 201326592 | bytes 4194304 | tf_op jit(solution)/shard_map/restrict_operator/pallas_call | solution.py:120
  7.5 1.6 %collective-permute-start.1 = (f32[512,128]{1,0:T(8,128)}, f32[512,128]{1,0:T(8,128)S(1)}, u32[]{:S(2)}, u32[]{:S(2)}) collective-permute-start(f32[512,128]{1,0:T(8,128)} %get-tuple-element.9.rest_0_), channel_id=1, source_target_pairs={{0,16},{8,24},{16,0},{24,8},{1,17},{9,25},{17,1},{25,9},{2,18},{10... | collective-permute-start | bytes 786440 | tf_op jit(solution)/shard_map/ppermute | solution.py:204
  9.1 0.3 collective-permute-start.3
  9.4 3.9 %all-to-all-start = ((f32[4,520,128]{2,1,0:T(8,128)}), f32[4,520,128]{2,1,0:T(8,128)S(1)}, u32[]{:S(2)}, u32[]{:S(2)}) async-start(f32[4,520,128]{2,1,0:T(8,128)} %get-tuple-element.8), calls=%async_computation | async-start | bytes 2129920 | tf_op jit(solution)/shard_map/all_to_all | solution.py:268
  13.3 3.0 %collective-permute-done.3.far_columns_ref = s32[2,8]{1,0:T(2,128)S(1)} collective-permute-done((s32[2,8]{1,0:T(2,128)}, s32[2,8]{1,0:T(2,128)S(1)}, u32[]{:S(2)}, u32[]{:S(2)}) %collective-permute-start.3) | collective-permute-done | bytes 96 | tf_op jit(solution)/shard_map/ppermute | solution.py:208
  16.4 1.6 %collective-permute-start.6 = (f32[520,128]{1,0:T(8,128)S(1)}, f32[520,128]{1,0:T(8,128)S(1)}, u32[]{:S(2)}, u32[]{:S(2)}) collective-permute-start(f32[520,128]{1,0:T(8,128)S(1)} %append_columns.1.rest_4_), channel_id=1, source_target_pairs={{0,16},{8,24},{16,0},{24,8},{1,17},{9,25},{17,1},{25,9},{2,18},{10... | collective-permute-start | bytes 798728 | tf_op jit(solution)/shard_map/ppermute | solution.py:204
  18.0 5.9 %collective-permute-done.6.rest_6_ = f32[520,128]{1,0:T(8,128)S(1)} collective-permute-done((f32[520,128]{1,0:T(8,128)S(1)}, f32[520,128]{1,0:T(8,128)S(1)}, u32[]{:S(2)}, u32[]{:S(2)}) %collective-permute-start.6) | collective-permute-done | bytes 266272 | tf_op jit(solution)/shard_map/ppermute | solution.py:204
  23.9 0.5 %collective-permute-start = (f32[512,128]{1,0:T(8,128)S(1)}, f32[512,128]{1,0:T(8,128)S(1)}, u32[]{:S(2)}, u32[]{:S(2)}) collective-permute-start(f32[512,128]{1,0:T(8,128)S(1)} %copy-done), channel_id=1, source_target_pairs={{0,8},{8,0},{16,24},{24,16},{1,9},{9,1},{17,25},{25,17},{2,10},{10... | collective-permute-start | bytes 786440 | tf_op jit(solution)/shard_map/ppermute | solution.py:204
  24.4 0.1 add_bitcast_fusion.own_ref
  24.5 1.3 %collective-permute-done.rest_1_ = f32[512,128]{1,0:T(8,128)S(1)} collective-permute-done((f32[512,128]{1,0:T(8,128)S(1)}, f32[512,128]{1,0:T(8,128)S(1)}, u32[]{:S(2)}, u32[]{:S(2)}) %collective-permute-start) | collective-permute-done | bytes 262176 | tf_op jit(solution)/shard_map/ppermute | solution.py:204
  25.8 0.4 collective-permute-done.2.rest_3_
  26.2 1.5 %all-to-all-done.restricted_ref = f32[4,520,128]{2,1,0:T(8,128)S(1)} async-done(((f32[4,520,128]{2,1,0:T(8,128)}), f32[4,520,128]{2,1,0:T(8,128)S(1)}, u32[]{:S(2)}, u32[]{:S(2)}) %all-to-all-start) | async-done | bytes 1064992 | tf_op jit(solution)/shard_map/all_to_all | solution.py:268
  27.7 1.8 %combine.1 = f32[8,64,128]{2,1,0:T(8,128)S(1)} custom-call(s32[1,10]{1,0:T(1,128)S(1)} %add_bitcast_fusion.own_ref, f32[4,520,128]{2,1,0:T(8,128)S(1)} %all-to-all-done.restricted_ref, f32[512,128]{1,0:T(8,128)S(1)} %copy-done, f32[512,128]{1,0:T(8,128)S(1)} %collective-permute-done.rest_1_, f32[512,128]{1,0:T(8,128)S(1)} %collective-permute-done.1.next_ref.rest_2_, ...), custom_call_target="tpu_custom_call" | custom-call | flops 268435456 | bytes 4194304 | tf_op jit(solution)/shard_map/combine/pallas_call | solution.py:186
  29.5 1.1 %collective-permute-start.13 = (f32[64,128]{1,0:T(8,128)S(1)}, f32[64,128]{1,0:T(8,128)S(1)}, u32[]{:S(2)}, u32[]{:S(2)}) collective-permute-start(f32[64,128]{1,0:T(8,128)S(1)} %get-tuple-element.12), channel_id=1, source_target_pairs={{0,3},{1,2},{2,1},{3,0},{4,7},{5,6},{6,5},{7,4},{8,11},{9,10},{10,... | collective-permute-start | bytes 98312 | tf_op jit(solution)/shard_map/ppermute | solution.py:229
  30.6 2.0 %collective-permute-start.12 = (f32[64,128]{1,0:T(8,128)S(1)}, f32[64,128]{1,0:T(8,128)S(1)}, u32[]{:S(2)}, u32[]{:S(2)}) collective-permute-start(f32[64,128]{1,0:T(8,128)S(1)} %get-tuple-element.13), channel_id=1, source_target_pairs={{0,2},{1,3},{2,0},{3,1},{4,6},{5,7},{6,4},{7,5},{8,10},{9,11},{10,... | collective-permute-start | bytes 98312 | tf_op jit(solution)/shard_map/ppermute | solution.py:229
  32.5 0.5 %collective-permute-start.11 = (f32[64,128]{1,0:T(8,128)S(1)}, f32[64,128]{1,0:T(8,128)S(1)}, u32[]{:S(2)}, u32[]{:S(2)}) collective-permute-start(f32[64,128]{1,0:T(8,128)S(1)} %get-tuple-element.14), channel_id=1, source_target_pairs={{0,1},{1,0},{2,3},{3,2},{4,5},{5,4},{6,7},{7,6},{8,9},{9,8},{10,11... | collective-permute-start | bytes 98312 | tf_op jit(solution)/shard_map/ppermute | solution.py:229
  33.0 1.5 %collective-permute-start.8 = (f32[64,128]{1,0:T(8,128)S(1)}, f32[64,128]{1,0:T(8,128)S(1)}, u32[]{:S(2)}, u32[]{:S(2)}) collective-permute-start(f32[64,128]{1,0:T(8,128)S(1)} %get-tuple-element.11), channel_id=1, source_target_pairs={{0,1},{1,0},{2,3},{3,2},{4,5},{5,4},{6,7},{7,6},{8,9},{9,8},{10,11... | collective-permute-start | bytes 98312 | tf_op jit(solution)/shard_map/ppermute | solution.py:229
  34.6 1.9 %collective-permute-start.9 = (f32[64,128]{1,0:T(8,128)S(1)}, f32[64,128]{1,0:T(8,128)S(1)}, u32[]{:S(2)}, u32[]{:S(2)}) collective-permute-start(f32[64,128]{1,0:T(8,128)S(1)} %get-tuple-element.16), channel_id=1, source_target_pairs={{0,2},{1,3},{2,0},{3,1},{4,6},{5,7},{6,4},{7,5},{8,10},{9,11},{10,... | collective-permute-start | bytes 98312 | tf_op jit(solution)/shard_map/ppermute | solution.py:229
  36.5 0.3 collective-permute-done.11
  36.8 2.0 %collective-permute-start.14 = (f32[64,128]{1,0:T(8,128)S(1)}, f32[64,128]{1,0:T(8,128)S(1)}, u32[]{:S(2)}, u32[]{:S(2)}) collective-permute-start(f32[64,128]{1,0:T(8,128)S(1)} %fusion.2), channel_id=1, source_target_pairs={{0,4},{4,0},{1,5},{5,1},{2,6},{6,2},{3,7},{7,3},{8,12},{12,8},{9,1... | collective-permute-start | bytes 98312 | tf_op jit(solution)/shard_map/ppermute | solution.py:208
  38.8 0.9 %collective-permute-done.10 = f32[64,128]{1,0:T(8,128)S(1)} collective-permute-done((f32[64,128]{1,0:T(8,128)S(1)}, f32[64,128]{1,0:T(8,128)S(1)}, u32[]{:S(2)}, u32[]{:S(2)}) %collective-permute-start.10) | collective-permute-done | bytes 32800 | tf_op jit(solution)/shard_map/ppermute | solution.py:229
  39.7 2.0 %collective-permute-done.14 = f32[64,128]{1,0:T(8,128)S(1)} collective-permute-done((f32[64,128]{1,0:T(8,128)S(1)}, f32[64,128]{1,0:T(8,128)S(1)}, u32[]{:S(2)}, u32[]{:S(2)}) %collective-permute-start.14) | collective-permute-done | bytes 32800 | tf_op jit(solution)/shard_map/ppermute | solution.py:208
  41.7 0.6 %fusion.7 = f32[128,64]{0,1:T(8,128)} fusion(f32[64,128]{1,0:T(8,128)S(1)} %collective-permute-done.14, f32[64,128]{1,0:T(8,128)S(1)} %collective-permute-done.10, f32[64,128]{1,0:T(8,128)S(1)} %collective-permute-done.9, f32[64,128]{1,0:T(8,128)S(1)} %collective-permute-done.8, f32[8,64,128]{2,1,0:T(8,128)S(1)} %combine.1), kind=kLoop, calls=%fused_computation.15 | loop fusion | flops 32768 | bytes 196608 | tf_op jit(solution)/shard_map/transpose | solution.py:274
  (20 shorter events, 0.2 us)
Async XLA Ops:
  0.0 16.4 %collective-permute-start.4 = (f32[512,128]{1,0:T(8,128)}, f32[512,128]{1,0:T(8,128)S(1)}, u32[]{:S(2)}, u32[]{:S(2)}) collective-permute-start(f32[512,128]{1,0:T(8,128)} %bitcast.44), channel_id=1, source_target_pairs={{0,4},{4,0},{1,5},{5,1},{2,6},{6,2},{3,7},{7,3},{8,12},{12,8},{9,1... | collective-permute-start | bytes 786440 | tf_op jit(solution)/shard_map/ppermute | solution.py:208
  7.5 8.9 %collective-permute-start.1 = (f32[512,128]{1,0:T(8,128)}, f32[512,128]{1,0:T(8,128)S(1)}, u32[]{:S(2)}, u32[]{:S(2)}) collective-permute-start(f32[512,128]{1,0:T(8,128)} %get-tuple-element.9.rest_0_), channel_id=1, source_target_pairs={{0,16},{8,24},{16,0},{24,8},{1,17},{9,25},{17,1},{25,9},{2,18},{10... | collective-permute-start | bytes 786440 | tf_op jit(solution)/shard_map/ppermute | solution.py:204
  9.1 7.3 %collective-permute-start.3 = (s32[2,8]{1,0:T(2,128)}, s32[2,8]{1,0:T(2,128)S(1)}, u32[]{:S(2)}, u32[]{:S(2)}) collective-permute-start(s32[2,8]{1,0:T(2,128)} %get-tuple-element.10.own_columns_ref), channel_id=1, source_target_pairs={{0,4},{4,0},{1,5},{5,1},{2,6},{6,2},{3,7},{7,3},{8,12},{12,8},{9,1... | collective-permute-start | bytes 200 | tf_op jit(solution)/shard_map/ppermute | solution.py:208
  9.4 6.9 %copy-start.1 = (s32[2,8]{1,0:T(2,128)S(1)}, s32[2,8]{1,0:T(2,128)}, u32[]{:S(2)}) copy-start(s32[2,8]{1,0:T(2,128)} %get-tuple-element.10.own_columns_ref) | copy-start | bytes 196
  9.4 18.3 %all-to-all-start = ((f32[4,520,128]{2,1,0:T(8,128)}), f32[4,520,128]{2,1,0:T(8,128)S(1)}, u32[]{:S(2)}, u32[]{:S(2)}) async-start(f32[4,520,128]{2,1,0:T(8,128)} %get-tuple-element.8), calls=%async_computation | async-start | bytes 2129920 | tf_op jit(solution)/shard_map/all_to_all | solution.py:268
  13.3 10.6 %copy-start = (f32[512,128]{1,0:T(8,128)S(1)}, f32[512,128]{1,0:T(8,128)}, u32[]{:S(2)}) copy-start(f32[512,128]{1,0:T(8,128)} %get-tuple-element.9.rest_0_) | copy-start | bytes 786436
  16.4 7.5 %collective-permute-start.6 = (f32[520,128]{1,0:T(8,128)S(1)}, f32[520,128]{1,0:T(8,128)S(1)}, u32[]{:S(2)}, u32[]{:S(2)}) collective-permute-start(f32[520,128]{1,0:T(8,128)S(1)} %append_columns.1.rest_4_), channel_id=1, source_target_pairs={{0,16},{8,24},{16,0},{24,8},{1,17},{9,25},{17,1},{25,9},{2,18},{10... | collective-permute-start | bytes 798728 | tf_op jit(solution)/shard_map/ppermute | solution.py:204
  18.0 8.2 %collective-permute-start.5 = (f32[520,128]{1,0:T(8,128)S(1)}, f32[520,128]{1,0:T(8,128)S(1)}, u32[]{:S(2)}, u32[]{:S(2)}) collective-permute-start(f32[520,128]{1,0:T(8,128)S(1)} %append_columns.1.rest_4_), channel_id=1, source_target_pairs={{0,8},{8,0},{16,24},{24,16},{1,9},{9,1},{17,25},{25,17},{2,10},{10... | collective-permute-start | bytes 798728 | tf_op jit(solution)/shard_map/ppermute | solution.py:204
  23.9 2.3 %collective-permute-start.7 = (f32[520,128]{1,0:T(8,128)S(1)}, f32[520,128]{1,0:T(8,128)S(1)}, u32[]{:S(2)}, u32[]{:S(2)}) collective-permute-start(f32[520,128]{1,0:T(8,128)S(1)} %collective-permute-done.6.rest_6_), channel_id=1, source_target_pairs={{0,8},{8,0},{16,24},{24,16},{1,9},{9,1},{17,25},{25,17},{2,10},{10... | collective-permute-start | bytes 798728 | tf_op jit(solution)/shard_map/ppermute | solution.py:204
  23.9 1.9 %collective-permute-start = (f32[512,128]{1,0:T(8,128)S(1)}, f32[512,128]{1,0:T(8,128)S(1)}, u32[]{:S(2)}, u32[]{:S(2)}) collective-permute-start(f32[512,128]{1,0:T(8,128)S(1)} %copy-done), channel_id=1, source_target_pairs={{0,8},{8,0},{16,24},{24,16},{1,9},{9,1},{17,25},{25,17},{2,10},{10... | collective-permute-start | bytes 786440 | tf_op jit(solution)/shard_map/ppermute | solution.py:204
  24.4 1.8 %collective-permute-start.2 = (f32[512,128]{1,0:T(8,128)S(1)}, f32[512,128]{1,0:T(8,128)S(1)}, u32[]{:S(2)}, u32[]{:S(2)}) collective-permute-start(f32[512,128]{1,0:T(8,128)S(1)} %collective-permute-done.1.next_ref.rest_2_), channel_id=1, source_target_pairs={{0,8},{8,0},{16,24},{24,16},{1,9},{9,1},{17,25},{25,17},{2,10},{10... | collective-permute-start | bytes 786440 | tf_op jit(solution)/shard_map/ppermute | solution.py:204
  29.5 5.2 %collective-permute-start.13 = (f32[64,128]{1,0:T(8,128)S(1)}, f32[64,128]{1,0:T(8,128)S(1)}, u32[]{:S(2)}, u32[]{:S(2)}) collective-permute-start(f32[64,128]{1,0:T(8,128)S(1)} %get-tuple-element.12), channel_id=1, source_target_pairs={{0,3},{1,2},{2,1},{3,0},{4,7},{5,6},{6,5},{7,4},{8,11},{9,10},{10,... | collective-permute-start | bytes 98312 | tf_op jit(solution)/shard_map/ppermute | solution.py:229
  30.6 5.9 %collective-permute-start.12 = (f32[64,128]{1,0:T(8,128)S(1)}, f32[64,128]{1,0:T(8,128)S(1)}, u32[]{:S(2)}, u32[]{:S(2)}) collective-permute-start(f32[64,128]{1,0:T(8,128)S(1)} %get-tuple-element.13), channel_id=1, source_target_pairs={{0,2},{1,3},{2,0},{3,1},{4,6},{5,7},{6,4},{7,5},{8,10},{9,11},{10,... | collective-permute-start | bytes 98312 | tf_op jit(solution)/shard_map/ppermute | solution.py:229
  32.5 4.3 %collective-permute-start.11 = (f32[64,128]{1,0:T(8,128)S(1)}, f32[64,128]{1,0:T(8,128)S(1)}, u32[]{:S(2)}, u32[]{:S(2)}) collective-permute-start(f32[64,128]{1,0:T(8,128)S(1)} %get-tuple-element.14), channel_id=1, source_target_pairs={{0,1},{1,0},{2,3},{3,2},{4,5},{5,4},{6,7},{7,6},{8,9},{9,8},{10,11... | collective-permute-start | bytes 98312 | tf_op jit(solution)/shard_map/ppermute | solution.py:229
  33.0 5.8 %collective-permute-start.8 = (f32[64,128]{1,0:T(8,128)S(1)}, f32[64,128]{1,0:T(8,128)S(1)}, u32[]{:S(2)}, u32[]{:S(2)}) collective-permute-start(f32[64,128]{1,0:T(8,128)S(1)} %get-tuple-element.11), channel_id=1, source_target_pairs={{0,1},{1,0},{2,3},{3,2},{4,5},{5,4},{6,7},{7,6},{8,9},{9,8},{10,11... | collective-permute-start | bytes 98312 | tf_op jit(solution)/shard_map/ppermute | solution.py:229
  34.6 5.2 %collective-permute-start.10 = (f32[64,128]{1,0:T(8,128)S(1)}, f32[64,128]{1,0:T(8,128)S(1)}, u32[]{:S(2)}, u32[]{:S(2)}) collective-permute-start(f32[64,128]{1,0:T(8,128)S(1)} %get-tuple-element.15), channel_id=1, source_target_pairs={{0,3},{1,2},{2,1},{3,0},{4,7},{5,6},{6,5},{7,4},{8,11},{9,10},{10,... | collective-permute-start | bytes 98312 | tf_op jit(solution)/shard_map/ppermute | solution.py:229
  34.6 5.1 %collective-permute-start.9 = (f32[64,128]{1,0:T(8,128)S(1)}, f32[64,128]{1,0:T(8,128)S(1)}, u32[]{:S(2)}, u32[]{:S(2)}) collective-permute-start(f32[64,128]{1,0:T(8,128)S(1)} %get-tuple-element.16), channel_id=1, source_target_pairs={{0,2},{1,3},{2,0},{3,1},{4,6},{5,7},{6,4},{7,5},{8,10},{9,11},{10,... | collective-permute-start | bytes 98312 | tf_op jit(solution)/shard_map/ppermute | solution.py:229
  36.8 4.9 %collective-permute-start.14 = (f32[64,128]{1,0:T(8,128)S(1)}, f32[64,128]{1,0:T(8,128)S(1)}, u32[]{:S(2)}, u32[]{:S(2)}) collective-permute-start(f32[64,128]{1,0:T(8,128)S(1)} %fusion.2), channel_id=1, source_target_pairs={{0,4},{4,0},{1,5},{5,1},{2,6},{6,2},{3,7},{7,3},{8,12},{12,8},{9,1... | collective-permute-start | bytes 98312 | tf_op jit(solution)/shard_map/ppermute | solution.py:208

commit v34 on v22

--- a/solution.py
+++ b/solution.py
@@ -230,16 +230,18 @@
     return jnp.arange(2 * half, dtype=jnp.int32) ^ own
 
 
-def add_over_near(sums, half):
-    total = sums[0]
-    for near in range(1, half):
+def add_over_near(sums, first, half):
+    total = sums[0] + first
+    for near in range(2, half):
         total = total + lax.ppermute(sums[near], "near", [(n, n ^ near) for n in range(half)])
     return total
 
 
 def add_over_columns(sums, half):
-    crossing = half_swap(add_over_near(sums[half:], half))
-    return add_over_near(sums[:half], half) + crossing
+    pair = jnp.stack([sums[1], sums[half + 1]])
+    pair = lax.ppermute(pair, "near", [(n, n ^ 1) for n in range(half)])
+    crossing = half_swap(add_over_near(sums[half:], pair[1], half))
+    return add_over_near(sums[:half], pair[0], half) + crossing
 
 
 def local(

time: 41.9 us -> 41.8 us (level)
  starting transfers between devices: 22.2 us -> 21.7 us
  waiting for transfers between devices: 13.3 us -> 13.8 us
    ppermute x6 -> x4, starting transfers between devices: 7.04 us -> 4.95 us  [add_over_near(): lax.ppermute(sums[near], 'near', [(n, n ^ near) for n in range(half)])]
    ppermute x0 -> x1, starting transfers between devices: none -> 1.53 us  [add_over_columns(): pair = lax.ppermute(pair, 'near', [(n, n ^ 1) for n in range(half)])]
    ppermute x1, waiting for transfers between devices: 1.6 us -> 2.08 us  [half_swap(): return lax.ppermute(x, 'half', [(0, 1), (1, 0)])]
  transfers between devices with their start and end apart: 16 -> 15, of which waited for: 9 -> 9; matrix products, arithmetic and copies ran while one was open for 0% -> 0% of each run, Pallas kernels for 8% -> 8%
where the time goes in v34:
time: 41.8 us; the launch traced here: 41.6 us
  starting transfers between devices  21.7 us (52%)
  waiting for transfers between devices  13.8 us (33%)
  Pallas kernels  5.26 us (13%)
  other arithmetic  0.73 us (2%)
    ppermute x6, waiting for transfers between devices, row_swap(): lax.ppermute(x, 'row', [(r, r ^ bit) for r in range(lax.axis_size('row'))])  7.99 us
    ppermute x2, starting transfers between devices, far_swap(): return lax.ppermute(x, ('half', 'near'), pairs)  5.27 us
    ppermute x4, starting transfers between devices, add_over_near(): lax.ppermute(sums[near], 'near', [(n, n ^ near) for n in range(half)])  4.95 us
    ppermute x6, starting transfers between devices, row_swap(): lax.ppermute(x, 'row', [(r, r ^ bit) for r in range(lax.axis_size('row'))])  3.69 us
    all_to_all x1, starting transfers between devices, local(): lax.all_to_all(restricted, 'near', split_axis=0, concat_axis=0, tiled=True)  3.65 us
    pallas_call x1, Pallas kernels, restrict_operator(): pl.pallas_call(restrict_kernel, out_shape=(jax.ShapeDtypeStruct((columns...  3.49 us
    ppermute x1, starting transfers between devices, half_swap(): return lax.ppermute(x, 'half', [(0, 1), (1, 0)])  2.6 us
    ppermute x1, waiting for transfers between devices, half_swap(): return lax.ppermute(x, 'half', [(0, 1), (1, 0)])  2.08 us
  transfers between devices with their start and end apart: 15, of which 9 were waited for; matrix products, arithmetic and copies ran while one was open for 0% of the time, Pallas kernels for 8%

profile of v34, /device:TPU:0, one launch (start us, length us, event | category | flops | bytes accessed | tf_op | source)
XLA Modules:
  0.0 41.6 jit_solution(6699509240780517879)
XLA Ops:
  0.0 5.0 %collective-permute-start.4 = (f32[512,128]{1,0:T(8,128)}, f32[512,128]{1,0:T(8,128)S(1)}, u32[]{:S(2)}, u32[]{:S(2)}) collective-permute-start(f32[512,128]{1,0:T(8,128)} %bitcast.36), channel_id=1, source_target_pairs={{0,6},{1,7},{2,4},{3,5},{4,2},{5,3},{6,0},{7,1},{8,14},{9,15},{10,... | collective-permute-start | bytes 786440 | tf_op jit(solution)/shard_map/ppermute | solution.py:215
  5.0 3.5 %restrict_operator.1 = (f32[4,520,128]{2,1,0:T(8,128)}, s32[2,8]{1,0:T(2,128)}, f32[512,128]{1,0:T(8,128)}) custom-call(s32[8]{0:T(128)} %count_any.1, s32[8,8]{1,0:T(8,128)} %slot_any.1, s32[2,8]{1,0:T(2,128)} %bitcast.39, s32[4,8]{1,0:T(4,128)} %bitcast.38, f32[8,64,128]{2,1,0:T(8,128)} %restrict_any.1, f32[8,64,512]{2,1,0:T(8,128)} %operator_any.1, ...), custom_call_target="tpu_custom_call" | custom-call | flops 201326592 | bytes 4194304 | tf_op jit(solution)/shard_map/restrict_operator/pallas_call | solution.py:121
  8.5 1.6 %collective-permute-start.1 = (f32[512,128]{1,0:T(8,128)}, f32[512,128]{1,0:T(8,128)S(1)}, u32[]{:S(2)}, u32[]{:S(2)}) collective-permute-start(f32[512,128]{1,0:T(8,128)} %get-tuple-element.9.rest_0_), channel_id=1, source_target_pairs={{0,16},{8,24},{16,0},{24,8},{1,17},{9,25},{17,1},{25,9},{2,18},{10... | collective-permute-start | bytes 786440 | tf_op jit(solution)/shard_map/ppermute | solution.py:205
  10.1 0.2 collective-permute-start.3
  10.4 3.6 %all-to-all-start = ((f32[4,520,128]{2,1,0:T(8,128)}), f32[4,520,128]{2,1,0:T(8,128)S(1)}, u32[]{:S(2)}, u32[]{:S(2)}) async-start(f32[4,520,128]{2,1,0:T(8,128)} %get-tuple-element.8), calls=%async_computation | async-start | bytes 2129920 | tf_op jit(solution)/shard_map/all_to_all | solution.py:277
  14.0 1.7 %collective-permute-done.3.far_columns_ref = s32[2,8]{1,0:T(2,128)S(1)} collective-permute-done((s32[2,8]{1,0:T(2,128)}, s32[2,8]{1,0:T(2,128)S(1)}, u32[]{:S(2)}, u32[]{:S(2)}) %collective-permute-start.3) | collective-permute-done | bytes 96 | tf_op jit(solution)/shard_map/ppermute | solution.py:215
  15.7 0.9 %collective-permute-done.1.next_ref.rest_2_ = f32[512,128]{1,0:T(8,128)S(1)} collective-permute-done((f32[512,128]{1,0:T(8,128)}, f32[512,128]{1,0:T(8,128)S(1)}, u32[]{:S(2)}, u32[]{:S(2)}) %collective-permute-start.1) | collective-permute-done | bytes 262176 | tf_op jit(solution)/shard_map/ppermute | solution.py:205
  16.6 1.6 %collective-permute-start.6 = (f32[520,128]{1,0:T(8,128)S(1)}, f32[520,128]{1,0:T(8,128)S(1)}, u32[]{:S(2)}, u32[]{:S(2)}) collective-permute-start(f32[520,128]{1,0:T(8,128)S(1)} %append_columns.1.rest_4_), channel_id=1, source_target_pairs={{0,16},{8,24},{16,0},{24,8},{1,17},{9,25},{17,1},{25,9},{2,18},{10... | collective-permute-start | bytes 798728 | tf_op jit(solution)/shard_map/ppermute | solution.py:205
  18.2 5.4 %collective-permute-done.6.rest_6_ = f32[520,128]{1,0:T(8,128)S(1)} collective-permute-done((f32[520,128]{1,0:T(8,128)S(1)}, f32[520,128]{1,0:T(8,128)S(1)}, u32[]{:S(2)}, u32[]{:S(2)}) %collective-permute-start.6) | collective-permute-done | bytes 266272 | tf_op jit(solution)/shard_map/ppermute | solution.py:205
  23.6 0.5 %collective-permute-start = (f32[512,128]{1,0:T(8,128)S(1)}, f32[512,128]{1,0:T(8,128)S(1)}, u32[]{:S(2)}, u32[]{:S(2)}) collective-permute-start(f32[512,128]{1,0:T(8,128)S(1)} %copy-done), channel_id=1, source_target_pairs={{0,8},{8,0},{16,24},{24,16},{1,9},{9,1},{17,25},{25,17},{2,10},{10... | collective-permute-start | bytes 786440 | tf_op jit(solution)/shard_map/ppermute | solution.py:205
  24.2 1.3 %collective-permute-done.rest_1_ = f32[512,128]{1,0:T(8,128)S(1)} collective-permute-done((f32[512,128]{1,0:T(8,128)S(1)}, f32[512,128]{1,0:T(8,128)S(1)}, u32[]{:S(2)}, u32[]{:S(2)}) %collective-permute-start) | collective-permute-done | bytes 262176 | tf_op jit(solution)/shard_map/ppermute | solution.py:205
  25.5 0.4 collective-permute-done.2.rest_3_
  25.9 1.4 %all-to-all-done.restricted_ref = f32[4,520,128]{2,1,0:T(8,128)S(1)} async-done(((f32[4,520,128]{2,1,0:T(8,128)}), f32[4,520,128]{2,1,0:T(8,128)S(1)}, u32[]{:S(2)}, u32[]{:S(2)}) %all-to-all-start) | async-done | bytes 1064992 | tf_op jit(solution)/shard_map/all_to_all | solution.py:277
  27.3 1.8 %combine.1 = f32[8,64,128]{2,1,0:T(8,128)S(1)} custom-call(s32[1,10]{1,0:T(1,128)S(1)} %add_bitcast_fusion.own_ref, f32[4,520,128]{2,1,0:T(8,128)S(1)} %all-to-all-done.restricted_ref, f32[512,128]{1,0:T(8,128)S(1)} %copy-done, f32[512,128]{1,0:T(8,128)S(1)} %collective-permute-done.rest_1_, f32[512,128]{1,0:T(8,128)S(1)} %collective-permute-done.1.next_ref.rest_2_, ...), custom_call_target="tpu_custom_call" | custom-call | flops 268435456 | bytes 4194304 | tf_op jit(solution)/shard_map/combine/pallas_call | solution.py:187
  29.1 1.5 %collective-permute-start.8 = (f32[2,64,128]{2,1,0:T(8,128)S(1)}, f32[2,64,128]{2,1,0:T(8,128)S(1)}, u32[]{:S(2)}, u32[]{:S(2)}) collective-permute-start(f32[2,64,128]{2,1,0:T(8,128)S(1)} %pad_maximum_fusion), channel_id=1, source_target_pairs={{0,1},{1,0},{2,3},{3,2},{4,5},{5,4},{6,7},{7,6},{8,9},{9,8},{10,11... | collective-permute-start | bytes 196616 | tf_op jit(solution)/shard_map/ppermute | solution.py:242
  30.6 1.4 %collective-permute-start.12 = (f32[64,128]{1,0:T(8,128)S(1)}, f32[64,128]{1,0:T(8,128)S(1)}, u32[]{:S(2)}, u32[]{:S(2)}) collective-permute-start(f32[64,128]{1,0:T(8,128)S(1)} %get-tuple-element.12), channel_id=1, source_target_pairs={{0,3},{1,2},{2,1},{3,0},{4,7},{5,6},{6,5},{7,4},{8,11},{9,10},{10,... | collective-permute-start | bytes 98312 | tf_op jit(solution)/shard_map/ppermute | solution.py:236
  32.0 0.6 %collective-permute-start.11 = (f32[64,128]{1,0:T(8,128)S(1)}, f32[64,128]{1,0:T(8,128)S(1)}, u32[]{:S(2)}, u32[]{:S(2)}) collective-permute-start(f32[64,128]{1,0:T(8,128)S(1)} %get-tuple-element.13), channel_id=1, source_target_pairs={{0,2},{1,3},{2,0},{3,1},{4,6},{5,7},{6,4},{7,5},{8,10},{9,11},{10,... | collective-permute-start | bytes 98312 | tf_op jit(solution)/shard_map/ppermute | solution.py:236
  32.6 1.4 %collective-permute-start.9 = (f32[64,128]{1,0:T(8,128)S(1)}, f32[64,128]{1,0:T(8,128)S(1)}, u32[]{:S(2)}, u32[]{:S(2)}) collective-permute-start(f32[64,128]{1,0:T(8,128)S(1)} %get-tuple-element.11), channel_id=1, source_target_pairs={{0,2},{1,3},{2,0},{3,1},{4,6},{5,7},{6,4},{7,5},{8,10},{9,11},{10,... | collective-permute-start | bytes 98312 | tf_op jit(solution)/shard_map/ppermute | solution.py:236
  34.1 1.5 %collective-permute-start.10 = (f32[64,128]{1,0:T(8,128)S(1)}, f32[64,128]{1,0:T(8,128)S(1)}, u32[]{:S(2)}, u32[]{:S(2)}) collective-permute-start(f32[64,128]{1,0:T(8,128)S(1)} %get-tuple-element.14), channel_id=1, source_target_pairs={{0,3},{1,2},{2,1},{3,0},{4,7},{5,6},{6,5},{7,4},{8,11},{9,10},{10,... | collective-permute-start | bytes 98312 | tf_op jit(solution)/shard_map/ppermute | solution.py:236
  35.6 0.5 %collective-permute-done.11 = f32[64,128]{1,0:T(8,128)S(1)} collective-permute-done((f32[64,128]{1,0:T(8,128)S(1)}, f32[64,128]{1,0:T(8,128)S(1)}, u32[]{:S(2)}, u32[]{:S(2)}) %collective-permute-start.11) | collective-permute-done | bytes 32800 | tf_op jit(solution)/shard_map/ppermute | solution.py:236
  36.1 2.6 %collective-permute-start.13 = (f32[64,128]{1,0:T(8,128)S(1)}, f32[64,128]{1,0:T(8,128)S(1)}, u32[]{:S(2)}, u32[]{:S(2)}) collective-permute-start(f32[64,128]{1,0:T(8,128)S(1)} %fusion.2), channel_id=1, source_target_pairs={{0,4},{4,0},{1,5},{5,1},{2,6},{6,2},{3,7},{7,3},{8,12},{12,8},{9,1... | collective-permute-start | bytes 98312 | tf_op jit(solution)/shard_map/ppermute | solution.py:209
  38.7 0.2 collective-permute-done.10
  38.9 2.1 %collective-permute-done.13 = f32[64,128]{1,0:T(8,128)S(1)} collective-permute-done((f32[64,128]{1,0:T(8,128)S(1)}, f32[64,128]{1,0:T(8,128)S(1)}, u32[]{:S(2)}, u32[]{:S(2)}) %collective-permute-start.13) | collective-permute-done | bytes 32800 | tf_op jit(solution)/shard_map/ppermute | solution.py:209
  41.0 0.6 %fusion.7 = f32[128,64]{0,1:T(8,128)} fusion(f32[64,128]{1,0:T(8,128)S(1)} %collective-permute-done.13, f32[64,128]{1,0:T(8,128)S(1)} %collective-permute-done.10, f32[64,128]{1,0:T(8,128)S(1)} %collective-permute-done.9, f32[2,64,128]{2,1,0:T(8,128)S(1)} %collective-permute-done.8, f32[8,64,128]{2,1,0:T(8,128)S(1)} %combine.1), kind=kLoop, calls=%fused_computation.14 | loop fusion | flops 32768 | bytes 196608 | tf_op jit(solution)/shard_map/transpose | solution.py:283
  (19 shorter events, 0.2 us)
Async XLA Ops:
  0.0 15.7 %collective-permute-start.4 = (f32[512,128]{1,0:T(8,128)}, f32[512,128]{1,0:T(8,128)S(1)}, u32[]{:S(2)}, u32[]{:S(2)}) collective-permute-start(f32[512,128]{1,0:T(8,128)} %bitcast.36), channel_id=1, source_target_pairs={{0,6},{1,7},{2,4},{3,5},{4,2},{5,3},{6,0},{7,1},{8,14},{9,15},{10,... | collective-permute-start | bytes 786440 | tf_op jit(solution)/shard_map/ppermute | solution.py:215
  8.5 8.0 %collective-permute-start.1 = (f32[512,128]{1,0:T(8,128)}, f32[512,128]{1,0:T(8,128)S(1)}, u32[]{:S(2)}, u32[]{:S(2)}) collective-permute-start(f32[512,128]{1,0:T(8,128)} %get-tuple-element.9.rest_0_), channel_id=1, source_target_pairs={{0,16},{8,24},{16,0},{24,8},{1,17},{9,25},{17,1},{25,9},{2,18},{10... | collective-permute-start | bytes 786440 | tf_op jit(solution)/shard_map/ppermute | solution.py:205
  10.1 5.6 %collective-permute-start.3 = (s32[2,8]{1,0:T(2,128)}, s32[2,8]{1,0:T(2,128)S(1)}, u32[]{:S(2)}, u32[]{:S(2)}) collective-permute-start(s32[2,8]{1,0:T(2,128)} %get-tuple-element.10.own_columns_ref), channel_id=1, source_target_pairs={{0,6},{1,7},{2,4},{3,5},{4,2},{5,3},{6,0},{7,1},{8,14},{9,15},{10,... | collective-permute-start | bytes 200 | tf_op jit(solution)/shard_map/ppermute | solution.py:215
  10.4 6.2 %copy-start.1 = (s32[2,8]{1,0:T(2,128)S(1)}, s32[2,8]{1,0:T(2,128)}, u32[]{:S(2)}) copy-start(s32[2,8]{1,0:T(2,128)} %get-tuple-element.10.own_columns_ref) | copy-start | bytes 196
  10.4 16.9 %all-to-all-start = ((f32[4,520,128]{2,1,0:T(8,128)}), f32[4,520,128]{2,1,0:T(8,128)S(1)}, u32[]{:S(2)}, u32[]{:S(2)}) async-start(f32[4,520,128]{2,1,0:T(8,128)} %get-tuple-element.8), calls=%async_computation | async-start | bytes 2129920 | tf_op jit(solution)/shard_map/all_to_all | solution.py:277
  14.0 9.6 %copy-start = (f32[512,128]{1,0:T(8,128)S(1)}, f32[512,128]{1,0:T(8,128)}, u32[]{:S(2)}) copy-start(f32[512,128]{1,0:T(8,128)} %get-tuple-element.9.rest_0_) | copy-start | bytes 786436
  16.6 7.0 %collective-permute-start.6 = (f32[520,128]{1,0:T(8,128)S(1)}, f32[520,128]{1,0:T(8,128)S(1)}, u32[]{:S(2)}, u32[]{:S(2)}) collective-permute-start(f32[520,128]{1,0:T(8,128)S(1)} %append_columns.1.rest_4_), channel_id=1, source_target_pairs={{0,16},{8,24},{16,0},{24,8},{1,17},{9,25},{17,1},{25,9},{2,18},{10... | collective-permute-start | bytes 798728 | tf_op jit(solution)/shard_map/ppermute | solution.py:205
  18.2 7.7 %collective-permute-start.5 = (f32[520,128]{1,0:T(8,128)S(1)}, f32[520,128]{1,0:T(8,128)S(1)}, u32[]{:S(2)}, u32[]{:S(2)}) collective-permute-start(f32[520,128]{1,0:T(8,128)S(1)} %append_columns.1.rest_4_), channel_id=1, source_target_pairs={{0,8},{8,0},{16,24},{24,16},{1,9},{9,1},{17,25},{25,17},{2,10},{10... | collective-permute-start | bytes 798728 | tf_op jit(solution)/shard_map/ppermute | solution.py:205
  23.6 2.3 %collective-permute-start.7 = (f32[520,128]{1,0:T(8,128)S(1)}, f32[520,128]{1,0:T(8,128)S(1)}, u32[]{:S(2)}, u32[]{:S(2)}) collective-permute-start(f32[520,128]{1,0:T(8,128)S(1)} %collective-permute-done.6.rest_6_), channel_id=1, source_target_pairs={{0,8},{8,0},{16,24},{24,16},{1,9},{9,1},{17,25},{25,17},{2,10},{10... | collective-permute-start | bytes 798728 | tf_op jit(solution)/shard_map/ppermute | solution.py:205
  23.6 1.9 %collective-permute-start = (f32[512,128]{1,0:T(8,128)S(1)}, f32[512,128]{1,0:T(8,128)S(1)}, u32[]{:S(2)}, u32[]{:S(2)}) collective-permute-start(f32[512,128]{1,0:T(8,128)S(1)} %copy-done), channel_id=1, source_target_pairs={{0,8},{8,0},{16,24},{24,16},{1,9},{9,1},{17,25},{25,17},{2,10},{10... | collective-permute-start | bytes 786440 | tf_op jit(solution)/shard_map/ppermute | solution.py:205
  24.1 1.8 %collective-permute-start.2 = (f32[512,128]{1,0:T(8,128)S(1)}, f32[512,128]{1,0:T(8,128)S(1)}, u32[]{:S(2)}, u32[]{:S(2)}) collective-permute-start(f32[512,128]{1,0:T(8,128)S(1)} %collective-permute-done.1.next_ref.rest_2_), channel_id=1, source_target_pairs={{0,8},{8,0},{16,24},{24,16},{1,9},{9,1},{17,25},{25,17},{2,10},{10... | collective-permute-start | bytes 786440 | tf_op jit(solution)/shard_map/ppermute | solution.py:205
  29.1 7.0 %collective-permute-start.8 = (f32[2,64,128]{2,1,0:T(8,128)S(1)}, f32[2,64,128]{2,1,0:T(8,128)S(1)}, u32[]{:S(2)}, u32[]{:S(2)}) collective-permute-start(f32[2,64,128]{2,1,0:T(8,128)S(1)} %pad_maximum_fusion), channel_id=1, source_target_pairs={{0,1},{1,0},{2,3},{3,2},{4,5},{5,4},{6,7},{7,6},{8,9},{9,8},{10,11... | collective-permute-start | bytes 196616 | tf_op jit(solution)/shard_map/ppermute | solution.py:242
  30.6 5.0 %collective-permute-start.12 = (f32[64,128]{1,0:T(8,128)S(1)}, f32[64,128]{1,0:T(8,128)S(1)}, u32[]{:S(2)}, u32[]{:S(2)}) collective-permute-start(f32[64,128]{1,0:T(8,128)S(1)} %get-tuple-element.12), channel_id=1, source_target_pairs={{0,3},{1,2},{2,1},{3,0},{4,7},{5,6},{6,5},{7,4},{8,11},{9,10},{10,... | collective-permute-start | bytes 98312 | tf_op jit(solution)/shard_map/ppermute | solution.py:236
  32.0 4.0 %collective-permute-start.11 = (f32[64,128]{1,0:T(8,128)S(1)}, f32[64,128]{1,0:T(8,128)S(1)}, u32[]{:S(2)}, u32[]{:S(2)}) collective-permute-start(f32[64,128]{1,0:T(8,128)S(1)} %get-tuple-element.13), channel_id=1, source_target_pairs={{0,2},{1,3},{2,0},{3,1},{4,6},{5,7},{6,4},{7,5},{8,10},{9,11},{10,... | collective-permute-start | bytes 98312 | tf_op jit(solution)/shard_map/ppermute | solution.py:236
  32.6 6.0 %collective-permute-start.9 = (f32[64,128]{1,0:T(8,128)S(1)}, f32[64,128]{1,0:T(8,128)S(1)}, u32[]{:S(2)}, u32[]{:S(2)}) collective-permute-start(f32[64,128]{1,0:T(8,128)S(1)} %get-tuple-element.11), channel_id=1, source_target_pairs={{0,2},{1,3},{2,0},{3,1},{4,6},{5,7},{6,4},{7,5},{8,10},{9,11},{10,... | collective-permute-start | bytes 98312 | tf_op jit(solution)/shard_map/ppermute | solution.py:236
  34.1 4.8 %collective-permute-start.10 = (f32[64,128]{1,0:T(8,128)S(1)}, f32[64,128]{1,0:T(8,128)S(1)}, u32[]{:S(2)}, u32[]{:S(2)}) collective-permute-start(f32[64,128]{1,0:T(8,128)S(1)} %get-tuple-element.14), channel_id=1, source_target_pairs={{0,3},{1,2},{2,1},{3,0},{4,7},{5,6},{6,5},{7,4},{8,11},{9,10},{10,... | collective-permute-start | bytes 98312 | tf_op jit(solution)/shard_map/ppermute | solution.py:236
  36.1 4.9 %collective-permute-start.13 = (f32[64,128]{1,0:T(8,128)S(1)}, f32[64,128]{1,0:T(8,128)S(1)}, u32[]{:S(2)}, u32[]{:S(2)}) collective-permute-start(f32[64,128]{1,0:T(8,128)S(1)} %fusion.2), channel_id=1, source_target_pairs={{0,4},{4,0},{1,5},{5,1},{2,6},{6,2},{3,7},{7,3},{8,12},{12,8},{9,1... | collective-permute-start | bytes 98312 | tf_op jit(solution)/shard_map/ppermute | solution.py:209
